TPU v7x, 32 devices: a whole 2x2x4 slice. The times are simulated.
32 devices in a mesh: member: 1, gx: 4 (over z), gy: 8 (over y, x, core).
Axes of the slice: x: 2, y: 2, z: 4, core: 2. Of those that a mesh axis runs over, the one named last changes fastest.
Arguments:
- couplings: float32 [6, 4, 32, 64, 128], P('member', None, 'gx', 'gy'), may hold values from -0.4 to 0.1
- diagonal_blocks: float32 [4, 32, 64, 128], P('member', 'gx', 'gy'), may hold values from -1 to 12
- well_vectors: float32 [4, 32, 64, 128], P('member', 'gx', 'gy'), may hold values from -3 to 3, as said below
- well_ids: int32 [32, 64, 128], P('gx', 'gy'), may hold values from 0 to 40, as said below
- right_side: float32 [4, 2, 32, 64, 128], P('member', None, 'gx', 'gy'), may hold values from -24 to 24
- initial_guess: float32 [4, 2, 32, 64, 128], P('member', None, 'gx', 'gy'), may hold values from -3 to 3
Outputs:
- solution: float32 [4, 2, 32, 64, 128], P('member', None, 'gx', 'gy')
Inputs may be any that keep to these rules, and one draw needn't show every extreme that they name: `well_ids`: A value below 40 names the well perforating the cell; 40 marks a cell without a perforation. `well_vectors`: entries 0 and 1 lie within -1 to 1, entries 2 and 3 within -3 to 3.
All inputs are finite; a program needn't handle non-finite values.
Results may differ from a plain program's by a relative error of at most 0.0003.
Values sent between devices are 32-bit elements; how exact they have to be, the bound alone decides.
No kernel may reach another device: no remote copies, remote signals or barrier semaphores. Data moves between devices by JAX's collectives and lax.ppermute only.
A program may use at most 64 MiB of HBM per device.

v0:
```python
import jax
import jax.numpy as jnp
from jax import lax
from jax.sharding import PartitionSpec as P

WELLS = 40
ITERS = 3


def from_behind(value, axis, steps):
    count = lax.axis_size(axis)
    leading, last = (max(0, -steps), min(count, count - steps))
    return lax.ppermute(value, axis, [(source, source + steps) for source in range(leading, last)])


def block_product(blocks, vectors):
    first = blocks[0] * vectors[:, 0] + blocks[2] * vectors[:, 1]
    second = blocks[1] * vectors[:, 0] + blocks[3] * vectors[:, 1]
    return jnp.stack([first, second], axis=1)


def moved_along(partial_sum, axis_number, upward):
    length = partial_sum.shape[axis_number]
    widths = [(0, 0)] * partial_sum.ndim
    if upward:
        kept = lax.slice_in_dim(partial_sum, 0, length - 1, axis=axis_number)
        widths[axis_number] = (1, 0)
    else:
        kept = lax.slice_in_dim(partial_sum, 1, length, axis=axis_number)
        widths[axis_number] = (0, 1)
    return jnp.pad(kept, widths)


def areal_terms(vectors, couplings):
    eastward = block_product(couplings[0], vectors)
    from_west = from_behind(eastward[:, :, -1:], "gx", 1)
    result = jnp.concatenate([from_west, eastward[:, :, :-1]], axis=2)
    westward = block_product(couplings[1], vectors)
    from_east = from_behind(westward[:, :, :1], "gx", -1)
    result = result + jnp.concatenate([westward[:, :, 1:], from_east], axis=2)
    northward = block_product(couplings[2], vectors)
    from_south = from_behind(northward[:, :, :, -1:], "gy", 1)
    result = result + jnp.concatenate([from_south, northward[:, :, :, :-1]], axis=3)
    southward = block_product(couplings[3], vectors)
    from_north = from_behind(southward[:, :, :, :1], "gy", -1)
    result = result + jnp.concatenate([southward[:, :, :, 1:], from_north], axis=3)
    return result


def well_partial(vectors, well_vectors, well_table):
    weighted = (well_vectors[0] * vectors[:, 0] + well_vectors[1] * vectors[:, 1]).reshape(
        vectors.shape[0], -1
    )
    return jnp.einsum("kc,wc->kw", weighted, well_table, precision=lax.Precision.HIGHEST)


def transpose_apply(vectors, totals, couplings, diagonal_blocks, well_vectors, well_table):
    result = block_product(diagonal_blocks, vectors)
    result = result + areal_terms(vectors, couplings)
    result = result + moved_along(block_product(couplings[4], vectors), 4, True)
    result = result + moved_along(block_product(couplings[5], vectors), 4, False)
    spread = jnp.dot(totals, well_table, precision=lax.Precision.HIGHEST).reshape(
        (vectors.shape[0],) + vectors.shape[2:]
    )
    return result + jnp.stack([well_vectors[2] * spread, well_vectors[3] * spread], axis=1)


def inner(first, second):
    return jnp.sum(first * second, axis=(1, 2, 3, 4))


def widen(scalars):
    return scalars[:, None, None, None, None]


def global_norm(vectors):
    return jnp.sqrt(lax.psum(inner(vectors, vectors), ("gx", "gy")))


def small_solve(factor, target):
    return jax.scipy.linalg.cho_solve((factor, True), target)


def body(couplings, diagonal_blocks, well_vectors, well_ids, right_side, initial_guess):
    batch_count = right_side.shape[0]
    well_table = (well_ids.reshape(1, -1) == jnp.arange(WELLS, dtype=jnp.int32)[:, None]).astype(
        jnp.float32
    )

    def apply_with(vectors, totals):
        return transpose_apply(
            vectors, totals, couplings, diagonal_blocks, well_vectors, well_table
        )

    def apply_summed(vectors):
        totals = lax.psum(well_partial(vectors, well_vectors, well_table), ("gx", "gy"))
        return apply_with(vectors, totals)

    residual = right_side - apply_summed(initial_guess)
    columns = []
    start_norm = global_norm(residual)
    basis = [residual / widen(start_norm)]
    for step in range(ITERS):
        image = apply_summed(basis[step])
        heights = lax.psum(
            jnp.stack([inner(vector, image) for vector in basis], axis=1), ("gx", "gy")
        )
        for position in range(len(basis)):
            image = image - widen(heights[:, position]) * basis[position]
        length = global_norm(image)
        columns.append(
            jnp.concatenate(
                [heights, length[:, None], jnp.zeros((batch_count, ITERS - 1 - step), jnp.float32)],
                axis=1,
            )
        )
        if step + 1 < ITERS:
            basis.append(image / widen(length))
    hessenberg = jnp.stack(columns, axis=2)
    gram = jnp.einsum("kij,kil->kjl", hessenberg, hessenberg, precision=lax.Precision.HIGHEST)
    target = start_norm[:, None] * hessenberg[:, 0, :]
    factor = jnp.linalg.cholesky(gram)
    weights = jax.vmap(small_solve)(factor, target)
    solution = initial_guess
    for position in range(ITERS):
        solution = solution + widen(weights[:, position]) * basis[position]
    return solution


def solution(mesh):
    in_specs = (
        P("member", None, "gx", "gy", None),
        P("member", "gx", "gy", None),
        P("member", "gx", "gy", None),
        P("gx", "gy", None),
        P("member", None, "gx", "gy", None),
        P("member", None, "gx", "gy", None),
    )
    out_specs = P("member", None, "gx", "gy", None)
    return jax.shard_map(body, mesh=mesh, in_specs=in_specs, out_specs=out_specs, check_vma=False)
```

profile of v0, /device:TPU:0, one launch (start us, length us, event | category | flops | bytes accessed | tf_op | source)
XLA Modules:
  0.0 520.6 jit_solution(17952014786150584935)
XLA Ops:
  0.0 1.1 slice_bitcast_fusion.27
  1.3 1.3 collective-permute-start.3
  2.8 3.0 collective-permute-start.2
  5.8 1.3 collective-permute-start.1
  7.1 0.8 slice_bitcast_fusion.26
  8.1 0.6 pad_maximum_fusion.23
  8.7 5.5 %collective-permute-start = (f32[4,2,1,8,128]{4,3,2,1,0:T(8,128)}, f32[4,2,1,8,128]{4,3,2,1,0:T(8,128)S(1)}, u32[]{:S(2)}, u32[]{:S(2)}) collective-permute-start(f32[4,2,1,8,128]{4,3,2,1,0:T(8,128)} %pad_maximum_fusion.23), channel_id=1, source_target_pairs={{0,8},{8,16},{16,24},{1,9},{9,17},{17,25},{2,10},{10,18},{18,26},{... | collective-permute-start | bytes 98312 | tf_op jit(solution)/shard_map/ppermute | solution.py:13
  15.0 0.8 fusion.7
  15.8 41.0 %psum.77 = f32[4,40]{1,0:T(4,128)S(1)} all-reduce(f32[4,40]{1,0:T(4,128)S(1)} %fusion.7), channel_id=1, replica_groups=mesh['member'=1,'gx'=4,'gy'=8] {'gx','gy'}, use_global_device_ids=true, to_apply=%region_0.0 | all-reduce | flops 160 | bytes 1280 | tf_op jit(solution)/shard_map/psum | solution.py:96
  57.9 0.7 pad.68.clone
  58.9 39.0 %psum.78 = f32[4]{0:T(128)S(1)} all-reduce(f32[4]{0:T(128)S(1)} %get-tuple-element.16), channel_id=1, replica_groups=mesh['member'=1,'gx'=4,'gy'=8] {'gx','gy'}, use_global_device_ids=true, to_apply=%region_2.3 | all-reduce | flops 4 | bytes 32 | tf_op jit(solution)/shard_map/psum | solution.py:77
  99.1 0.8 fusion.5
  99.9 40.9 %psum.79 = f32[4,40]{1,0:T(4,128)S(1)} all-reduce(f32[4,40]{1,0:T(4,128)S(1)} %fusion.5), channel_id=1, replica_groups=mesh['member'=1,'gx'=4,'gy'=8] {'gx','gy'}, use_global_device_ids=true, to_apply=%region_3.4 | all-reduce | flops 160 | bytes 1280 | tf_op jit(solution)/shard_map/psum | solution.py:96
  141.4 1.3 collective-permute-start.7
  142.7 3.0 collective-permute-start.6
  145.8 1.3 collective-permute-start.5
  147.1 4.5 collective-permute-start.4
  151.7 1.5 collective-permute-done.4
  153.5 41.1 %psum.80 = f32[4,1]{0,1:T(1,128)S(1)} all-reduce(f32[4,1]{0,1:T(1,128)S(1)} %bitcast.269), channel_id=1, replica_groups=mesh['member'=1,'gx'=4,'gy'=8] {'gx','gy'}, use_global_device_ids=true, to_apply=%region_5.6 | all-reduce | flops 4 | bytes 32 | tf_op jit(solution)/shard_map/psum | solution.py:105
  194.8 0.6 pad.97.clone
  195.4 39.3 %psum.81 = f32[4]{0:T(128)S(1)} all-reduce(f32[4]{0:T(128)S(1)} %multiply_reduce_fusion.7), channel_id=1, replica_groups=mesh['member'=1,'gx'=4,'gy'=8] {'gx','gy'}, use_global_device_ids=true, to_apply=%region_7.8 | all-reduce | flops 4 | bytes 32 | tf_op jit(solution)/shard_map/psum | solution.py:77
  234.8 0.7 multiply_add_fusion.28
  235.6 0.8 multiply_add_fusion.20
  237.7 1.7 fusion.3
  239.4 40.6 %psum.82 = f32[4,40]{1,0:T(4,128)S(1)} all-reduce(f32[4,40]{1,0:T(4,128)S(1)} %fusion.3), channel_id=1, replica_groups=mesh['member'=1,'gx'=4,'gy'=8] {'gx','gy'}, use_global_device_ids=true, to_apply=%region_8.9 | all-reduce | flops 160 | bytes 1280 | tf_op jit(solution)/shard_map/psum | solution.py:96
  280.1 1.3 fusion.10
  281.3 0.7 fusion.82
  282.0 1.3 collective-permute-start.11
  283.3 0.6 pad_maximum_fusion.13
  283.9 3.0 collective-permute-start.10
  287.6 1.3 collective-permute-start.9
  289.5 5.1 collective-permute-start.8
  294.7 0.7 maximum_bitcast_fusion
  295.9 1.4 multiply_reduce_fusion.6
  297.4 41.8 %psum.83 = f32[4,2]{0,1:T(2,128)S(1)} all-reduce(f32[4,2]{0,1:T(2,128)S(1)} %pad_maximum_fusion.26), channel_id=1, replica_groups=mesh['member'=1,'gx'=4,'gy'=8] {'gx','gy'}, use_global_device_ids=true, to_apply=%region_11.12 | all-reduce | flops 8 | bytes 64 | tf_op jit(solution)/shard_map/psum | solution.py:105
  339.5 39.3 %psum.84 = f32[4]{0:T(128)S(1)} all-reduce(f32[4]{0:T(128)S(1)} %get-tuple-element.11), channel_id=1, replica_groups=mesh['member'=1,'gx'=4,'gy'=8] {'gx','gy'}, use_global_device_ids=true, to_apply=%region_13.14 | all-reduce | flops 4 | bytes 32 | tf_op jit(solution)/shard_map/psum | solution.py:77
  379.9 0.8 fusion.1
  380.7 40.7 %psum.85 = f32[4,40]{1,0:T(4,128)S(1)} all-reduce(f32[4,40]{1,0:T(4,128)S(1)} %fusion.1), channel_id=1, replica_groups=mesh['member'=1,'gx'=4,'gy'=8] {'gx','gy'}, use_global_device_ids=true, to_apply=%region_14.15 | all-reduce | flops 160 | bytes 1280 | tf_op jit(solution)/shard_map/psum | solution.py:96
  421.9 1.3 collective-permute-start.15
  423.3 3.0 collective-permute-start.14
  426.3 1.3 collective-permute-start.13
  427.6 4.5 collective-permute-start.12
  432.3 1.5 collective-permute-done.12
  434.5 41.1 %psum.86 = f32[4,3]{0,1:T(4,128)S(1)} all-reduce(f32[4,3]{0,1:T(4,128)S(1)} %pad_maximum_fusion.25), channel_id=1, replica_groups=mesh['member'=1,'gx'=4,'gy'=8] {'gx','gy'}, use_global_device_ids=true, to_apply=%region_18.19 | all-reduce | flops 12 | bytes 96 | tf_op jit(solution)/shard_map/psum | solution.py:105
  476.0 39.8 %psum.87 = f32[4]{0:T(128)S(1)} all-reduce(f32[4]{0:T(128)S(1)} %multiply_reduce_fusion), channel_id=1, replica_groups=mesh['member'=1,'gx'=4,'gy'=8] {'gx','gy'}, use_global_device_ids=true, to_apply=%region_20.21 | all-reduce | flops 4 | bytes 32 | tf_op jit(solution)/shard_map/psum | solution.py:77
  516.4 1.1 custom-call.11
  517.8 1.0 custom-call.12
  519.8 0.9 multiply_add_fusion
  (137 shorter events, 12.9 us)
Async XLA Ops:
  0.0 1.2 copy-start
  1.3 57.2 %collective-permute-start.3 = (f32[4,2,8,1,128]{4,3,2,1,0:T(1,128)S(1)}, f32[4,2,8,1,128]{4,3,2,1,0:T(1,128)S(1)}, u32[]{:S(2)}, u32[]{:S(2)}) collective-permute-start(f32[4,2,8,1,128]{4,3,2,1,0:T(1,128)S(1)} %pad_maximum_fusion.20), channel_id=1, source_target_pairs={{1,0},{2,1},{3,2},{4,3},{5,4},{6,5},{7,6},{9,8},{10,9},{11,10},{12... | collective-permute-start | bytes 98312 | tf_op jit(solution)/shard_map/ppermute | solution.py:13
  2.6 5.3 %copy-start.2 = (f32[4,8,8,128]{3,2,1,0:T(8,128)S(1)}, f32[4,8,8,128]{3,2,1,0:T(8,128)}, u32[]{:S(2)}) copy-start(f32[4,8,8,128]{3,2,1,0:T(8,128)} %param.7) | copy-start | bytes 393220
  2.8 55.8 %collective-permute-start.2 = (f32[4,2,8,1,128]{4,3,2,1,0:T(1,128)S(1)}, f32[4,2,8,1,128]{4,3,2,1,0:T(1,128)S(1)}, u32[]{:S(2)}, u32[]{:S(2)}) collective-permute-start(f32[4,2,8,1,128]{4,3,2,1,0:T(1,128)S(1)} %pad_maximum_fusion.21), channel_id=1, source_target_pairs={{0,1},{1,2},{2,3},{3,4},{4,5},{5,6},{6,7},{8,9},{9,10},{10,11},{11... | collective-permute-start | bytes 98312 | tf_op jit(solution)/shard_map/ppermute | solution.py:13
  5.8 52.8 %collective-permute-start.1 = (f32[4,2,1,8,128]{4,3,2,1,0:T(8,128)S(1)}, f32[4,2,1,8,128]{4,3,2,1,0:T(8,128)S(1)}, u32[]{:S(2)}, u32[]{:S(2)}) collective-permute-start(f32[4,2,1,8,128]{4,3,2,1,0:T(8,128)S(1)} %pad_maximum_fusion.22), channel_id=1, source_target_pairs={{8,0},{16,8},{24,16},{9,1},{17,9},{25,17},{10,2},{18,10},{26,18},{... | collective-permute-start | bytes 98312 | tf_op jit(solution)/shard_map/ppermute | solution.py:13
  8.1 6.9 %copy-start.3 = (f32[4,8,8,128]{3,2,1,0:T(8,128)S(1)}, f32[4,8,8,128]{3,2,1,0:T(8,128)}, u32[]{:S(2)}) copy-start(f32[4,8,8,128]{3,2,1,0:T(8,128)} %param.8) | copy-start | bytes 393220
  8.1 6.9 %copy-start.14 = (s32[8,8,128]{2,1,0:T(8,128)S(1)}, s32[8,8,128]{2,1,0:T(8,128)}, u32[]{:S(2)}) copy-start(s32[8,8,128]{2,1,0:T(8,128)} %param.9) | copy-start | bytes 98308
  8.7 49.9 %collective-permute-start = (f32[4,2,1,8,128]{4,3,2,1,0:T(8,128)}, f32[4,2,1,8,128]{4,3,2,1,0:T(8,128)S(1)}, u32[]{:S(2)}, u32[]{:S(2)}) collective-permute-start(f32[4,2,1,8,128]{4,3,2,1,0:T(8,128)} %pad_maximum_fusion.23), channel_id=1, source_target_pairs={{0,8},{8,16},{16,24},{1,9},{9,17},{17,25},{2,10},{10,18},{18,26},{... | collective-permute-start | bytes 98312 | tf_op jit(solution)/shard_map/ppermute | solution.py:13
  14.3 42.5 %copy-start.15 = (s32[8,8,128]{2,1,0:T(8,128)S(1)}, s32[8,8,128]{2,1,0:T(8,128)}, u32[]{:S(2)}) copy-start(s32[8,8,128]{2,1,0:T(8,128)} %param.9) | copy-start | bytes 98308
  15.0 0.8 copy-start.4
  15.0 0.8 copy-start.7
  15.8 42.8 %copy-start.1 = (f32[4,2,8,8,128]{4,3,2,1,0:T(8,128)S(1)}, f32[4,2,8,8,128]{4,3,2,1,0:T(8,128)}, u32[]{:S(2)}) copy-start(f32[4,2,8,8,128]{4,3,2,1,0:T(8,128)} %param.10) | copy-start | bytes 786436
  98.3 0.8 copy-start.5
  98.3 0.8 copy-start.8
  98.3 0.8 copy-start.16
  141.4 10.3 %collective-permute-start.7 = (f32[4,2,8,1,128]{4,3,2,1,0:T(1,128)S(1)}, f32[4,2,8,1,128]{4,3,2,1,0:T(1,128)S(1)}, u32[]{:S(2)}, u32[]{:S(2)}) collective-permute-start(f32[4,2,8,1,128]{4,3,2,1,0:T(1,128)S(1)} %pad_maximum_fusion.16), channel_id=1, source_target_pairs={{1,0},{2,1},{3,2},{4,3},{5,4},{6,5},{7,6},{9,8},{10,9},{11,10},{12... | collective-permute-start | bytes 98312 | tf_op jit(solution)/shard_map/ppermute | solution.py:13
  142.7 9.0 %collective-permute-start.6 = (f32[4,2,8,1,128]{4,3,2,1,0:T(1,128)S(1)}, f32[4,2,8,1,128]{4,3,2,1,0:T(1,128)S(1)}, u32[]{:S(2)}, u32[]{:S(2)}) collective-permute-start(f32[4,2,8,1,128]{4,3,2,1,0:T(1,128)S(1)} %pad_maximum_fusion.17), channel_id=1, source_target_pairs={{0,1},{1,2},{2,3},{3,4},{4,5},{5,6},{6,7},{8,9},{9,10},{10,11},{11... | collective-permute-start | bytes 98312 | tf_op jit(solution)/shard_map/ppermute | solution.py:13
  145.8 5.9 %collective-permute-start.5 = (f32[4,2,1,8,128]{4,3,2,1,0:T(8,128)S(1)}, f32[4,2,1,8,128]{4,3,2,1,0:T(8,128)S(1)}, u32[]{:S(2)}, u32[]{:S(2)}) collective-permute-start(f32[4,2,1,8,128]{4,3,2,1,0:T(8,128)S(1)} %pad_maximum_fusion.18), channel_id=1, source_target_pairs={{8,0},{16,8},{24,16},{9,1},{17,9},{25,17},{10,2},{18,10},{26,18},{... | collective-permute-start | bytes 98312 | tf_op jit(solution)/shard_map/ppermute | solution.py:13
  147.1 6.1 %collective-permute-start.4 = (f32[4,2,1,8,128]{4,3,2,1,0:T(8,128)S(1)}, f32[4,2,1,8,128]{4,3,2,1,0:T(8,128)S(1)}, u32[]{:S(2)}, u32[]{:S(2)}) collective-permute-start(f32[4,2,1,8,128]{4,3,2,1,0:T(8,128)S(1)} %pad_maximum_fusion.19), channel_id=1, source_target_pairs={{0,8},{8,16},{16,24},{1,9},{9,17},{17,25},{2,10},{10,18},{18,26},{... | collective-permute-start | bytes 98312 | tf_op jit(solution)/shard_map/ppermute | solution.py:13
  237.0 0.8 copy-start.9
  282.0 13.4 %collective-permute-start.11 = (f32[4,2,8,1,128]{4,3,2,1,0:T(1,128)}, f32[4,2,8,1,128]{4,3,2,1,0:T(1,128)S(1)}, u32[]{:S(2)}, u32[]{:S(2)}) collective-permute-start(f32[4,2,8,1,128]{4,3,2,1,0:T(1,128)} %pad_maximum_fusion.12), channel_id=1, source_target_pairs={{1,0},{2,1},{3,2},{4,3},{5,4},{6,5},{7,6},{9,8},{10,9},{11,10},{12... | collective-permute-start | bytes 98312 | tf_op jit(solution)/shard_map/ppermute | solution.py:13
  283.9 11.5 %collective-permute-start.10 = (f32[4,2,8,1,128]{4,3,2,1,0:T(1,128)}, f32[4,2,8,1,128]{4,3,2,1,0:T(1,128)S(1)}, u32[]{:S(2)}, u32[]{:S(2)}) collective-permute-start(f32[4,2,8,1,128]{4,3,2,1,0:T(1,128)} %pad_maximum_fusion.13), channel_id=1, source_target_pairs={{0,1},{1,2},{2,3},{3,4},{4,5},{5,6},{6,7},{8,9},{9,10},{10,11},{11... | collective-permute-start | bytes 98312 | tf_op jit(solution)/shard_map/ppermute | solution.py:13
  287.6 7.9 %collective-permute-start.9 = (f32[4,2,1,8,128]{4,3,2,1,0:T(8,128)}, f32[4,2,1,8,128]{4,3,2,1,0:T(8,128)}, u32[]{:S(2)}, u32[]{:S(2)}) collective-permute-start(f32[4,2,1,8,128]{4,3,2,1,0:T(8,128)} %pad_maximum_fusion.14), channel_id=1, source_target_pairs={{8,0},{16,8},{24,16},{9,1},{17,9},{25,17},{10,2},{18,10},{26,18},{... | collective-permute-start | bytes 98312 | tf_op jit(solution)/shard_map/ppermute | solution.py:13
  289.5 6.4 %collective-permute-start.8 = (f32[4,2,1,8,128]{4,3,2,1,0:T(8,128)}, f32[4,2,1,8,128]{4,3,2,1,0:T(8,128)}, u32[]{:S(2)}, u32[]{:S(2)}) collective-permute-start(f32[4,2,1,8,128]{4,3,2,1,0:T(8,128)} %pad_maximum_fusion.15), channel_id=1, source_target_pairs={{0,8},{8,16},{16,24},{1,9},{9,17},{17,25},{2,10},{10,18},{18,26},{... | collective-permute-start | bytes 98312 | tf_op jit(solution)/shard_map/ppermute | solution.py:13
  379.1 0.8 copy-start.6
  379.2 0.8 copy-start.10
  379.2 0.8 copy-start.17
  421.9 10.3 %collective-permute-start.15 = (f32[4,2,8,1,128]{4,3,2,1,0:T(1,128)S(1)}, f32[4,2,8,1,128]{4,3,2,1,0:T(1,128)S(1)}, u32[]{:S(2)}, u32[]{:S(2)}) collective-permute-start(f32[4,2,8,1,128]{4,3,2,1,0:T(1,128)S(1)} %pad_maximum_fusion.8), channel_id=1, source_target_pairs={{1,0},{2,1},{3,2},{4,3},{5,4},{6,5},{7,6},{9,8},{10,9},{11,10},{12... | collective-permute-start | bytes 98312 | tf_op jit(solution)/shard_map/ppermute | solution.py:13
  423.3 9.0 %collective-permute-start.14 = (f32[4,2,8,1,128]{4,3,2,1,0:T(1,128)S(1)}, f32[4,2,8,1,128]{4,3,2,1,0:T(1,128)S(1)}, u32[]{:S(2)}, u32[]{:S(2)}) collective-permute-start(f32[4,2,8,1,128]{4,3,2,1,0:T(1,128)S(1)} %pad_maximum_fusion.9), channel_id=1, source_target_pairs={{0,1},{1,2},{2,3},{3,4},{4,5},{5,6},{6,7},{8,9},{9,10},{10,11},{11... | collective-permute-start | bytes 98312 | tf_op jit(solution)/shard_map/ppermute | solution.py:13
  426.3 5.9 %collective-permute-start.13 = (f32[4,2,1,8,128]{4,3,2,1,0:T(8,128)S(1)}, f32[4,2,1,8,128]{4,3,2,1,0:T(8,128)S(1)}, u32[]{:S(2)}, u32[]{:S(2)}) collective-permute-start(f32[4,2,1,8,128]{4,3,2,1,0:T(8,128)S(1)} %pad_maximum_fusion.10), channel_id=1, source_target_pairs={{8,0},{16,8},{24,16},{9,1},{17,9},{25,17},{10,2},{18,10},{26,18},{... | collective-permute-start | bytes 98312 | tf_op jit(solution)/shard_map/ppermute | solution.py:13
  427.6 6.1 %collective-permute-start.12 = (f32[4,2,1,8,128]{4,3,2,1,0:T(8,128)S(1)}, f32[4,2,1,8,128]{4,3,2,1,0:T(8,128)S(1)}, u32[]{:S(2)}, u32[]{:S(2)}) collective-permute-start(f32[4,2,1,8,128]{4,3,2,1,0:T(8,128)S(1)} %pad_maximum_fusion.11), channel_id=1, source_target_pairs={{0,8},{8,16},{16,24},{1,9},{9,17},{17,25},{2,10},{10,18},{18,26},{... | collective-permute-start | bytes 98312 | tf_op jit(solution)/shard_map/ppermute | solution.py:13
  433.8 0.7 copy-start.12
  434.2 83.4 %copy-start.13 = (pred[3,3]{1,0:T(4,128)(4,1)S(1)}, pred[3,3]{1,0:T(4,128)(4,1)}, u32[]{:S(2)}) copy-start(pred[3,3]{1,0:T(4,128)(4,1)} %iota_compare_fusion.19) | copy-start | bytes 31
  434.2 83.6 %copy-start.11 = (pred[3,3]{1,0:T(4,128)(4,1)S(1)}, pred[3,3]{1,0:T(4,128)(4,1)}, u32[]{:S(2)}) copy-start(pred[3,3]{1,0:T(4,128)(4,1)} %iota_compare_fusion.20) | copy-start | bytes 31
where the time goes:
time: 523 us; the launch traced here: 521 us
  blocking collectives  445 us (85%)
  starting transfers between devices  42.2 us (8%)
  other arithmetic  15.4 us (3%)
  matrix products  7.38 us (1%)
  local copies, waits for them, and re-layouts  6.72 us (1%)
    psum x4, blocking collectives, apply_summed(): lax.psum(well_partial(vectors, well_vectors, well_table), ('gx', 'gy'))  163 us
    psum x4, blocking collectives, global_norm(): return jnp.sqrt(lax.psum(inner(vectors, vectors), ('gx', 'gy')))  157 us
    psum x3, blocking collectives, body(): lax.psum(jnp.stack([inner(vector, image) for vector in basis], axis=1), (...  124 us
    ppermute x16, starting transfers between devices, from_behind(): lax.ppermute(value, axis, [(source, source + steps) for source in range(l...  42.2 us
  transfers between devices with their start and end apart: 16, of which 3 were waited for; matrix products, arithmetic and copies ran while one was open for 1% of the time, Pallas kernels for 0%

commit v1 on v0

--- a/solution.py
+++ b/solution.py
@@ -5,6 +5,13 @@
 
 WELLS = 40
 ITERS = 3
+
+
+def total_of(value):
+    count = lax.axis_size("gx") * lax.axis_size("gy")
+    copies = jnp.broadcast_to(value.reshape(1, -1), (count, value.size))
+    parts = lax.all_to_all(copies, ("gx", "gy"), 0, 0, tiled=True)
+    return jnp.sum(parts, axis=0).reshape(value.shape)
 
 
 def from_behind(value, axis, steps):
@@ -74,7 +81,7 @@
 
 
 def global_norm(vectors):
-    return jnp.sqrt(lax.psum(inner(vectors, vectors), ("gx", "gy")))
+    return jnp.sqrt(total_of(inner(vectors, vectors)))
 
 
 def small_solve(factor, target):
@@ -93,7 +100,7 @@
         )
 
     def apply_summed(vectors):
-        totals = lax.psum(well_partial(vectors, well_vectors, well_table), ("gx", "gy"))
+        totals = total_of(well_partial(vectors, well_vectors, well_table))
         return apply_with(vectors, totals)
 
     residual = right_side - apply_summed(initial_guess)
@@ -102,8 +109,8 @@
     basis = [residual / widen(start_norm)]
     for step in range(ITERS):
         image = apply_summed(basis[step])
-        heights = lax.psum(
-            jnp.stack([inner(vector, image) for vector in basis], axis=1), ("gx", "gy")
+        heights = total_of(
+            jnp.stack([inner(vector, image) for vector in basis], axis=1)
         )
         for position in range(len(basis)):
             image = image - widen(heights[:, position]) * basis[position]

time: 523 us -> 181 us (0.35)
  blocking collectives: 445 us -> 35.5 us
  starting transfers between devices: 42.2 us -> 75.1 us
  waiting for transfers between devices: 3.52 us -> 28.6 us
  local copies, waits for them, and re-layouts: 6.72 us -> 15.1 us
    psum x11 -> x0, blocking collectives: 445 us -> none  [the longest x4 163 us: apply_summed(): lax.psum(well_partial(vectors, well_vectors, well_table), ('gx', 'gy'))]
    all_to_all x0 -> x3, blocking collectives: none -> 35.5 us  [total_of(): parts = lax.all_to_all(copies, ('gx', 'gy'), 0, 0, tiled=True)]
    all_to_all x0 -> x8, starting transfers between devices: none -> 33.3 us  [total_of(): parts = lax.all_to_all(copies, ('gx', 'gy'), 0, 0, tiled=True)]
    all_to_all x0 -> x8, waiting for transfers between devices: none -> 27.3 us  [total_of(): parts = lax.all_to_all(copies, ('gx', 'gy'), 0, 0, tiled=True)]
    broadcast_in_dim x4 -> x17, local copies, waits for them, and re-layouts: 0.11 us -> 5.65 us  [total_of(): copies = jnp.broadcast_to(value.reshape(1, -1), (count, value.size))]
  transfers between devices with their start and end apart: 16 -> 24, of which waited for: 3 -> 7; matrix products, arithmetic and copies ran while one was open for 1% -> 5% of each run, Pallas kernels for 0% -> 0%
where the time goes in v1:
time: 181 us; the launch traced here: 180 us
  starting transfers between devices  75.1 us (41%)
  blocking collectives  35.5 us (20%)
  waiting for transfers between devices  28.6 us (16%)
  other arithmetic  17 us (9%)
  local copies, waits for them, and re-layouts  15.1 us (8%)
  matrix products  7.78 us (4%)
    ppermute x16, starting transfers between devices, from_behind(): lax.ppermute(value, axis, [(source, source + steps) for source in range(l...  41.8 us
    all_to_all x3, blocking collectives, total_of(): parts = lax.all_to_all(copies, ('gx', 'gy'), 0, 0, tiled=True)  35.5 us
    all_to_all x8, starting transfers between devices, total_of(): parts = lax.all_to_all(copies, ('gx', 'gy'), 0, 0, tiled=True)  33.3 us
    all_to_all x8, waiting for transfers between devices, total_of(): parts = lax.all_to_all(copies, ('gx', 'gy'), 0, 0, tiled=True)  27.3 us
    reduce_sum x7, other arithmetic, inner(): return jnp.sum(first * second, axis=(1, 2, 3, 4))  6.19 us
    broadcast_in_dim x17, local copies, waits for them, and re-layouts, total_of(): copies = jnp.broadcast_to(value.reshape(1, -1), (count, value.size))  5.65 us
    dot_general x4, matrix products, transpose_apply(): jnp.dot(totals, well_table, precision=lax.Precision.HIGHEST)  4.37 us
    unnamed x53, local copies, waits for them, and re-layouts  3.78 us
  transfers between devices with their start and end apart: 24, of which 7 were waited for; matrix products, arithmetic and copies ran while one was open for 5% of the time, Pallas kernels for 0%

profile of v1, /device:TPU:0, one launch (start us, length us, event | category | flops | bytes accessed | tf_op | source)
XLA Modules:
  0.0 179.9 jit_solution(2960390358233947336)
XLA Ops:
  0.0 0.9 slice_bitcast_fusion.26
  0.9 1.1 slice_bitcast_fusion.27
  3.7 0.7 fusion.3
  5.1 7.3 %all-to-all-start = ((f32[32,1,160]{2,1,0:T(1,128)}), f32[32,1,160]{2,1,0:T(1,128)S(1)}, u32[]{:S(2)}, u32[]{:S(2)}) async-start(f32[32,1,160]{2,1,0:T(1,128)} %broadcast_in_dim.38), calls=%async_computation | async-start | bytes 65536 | tf_op jit(solution)/shard_map/all_to_all | solution.py:13
  13.2 1.3 collective-permute-start.3
  15.3 3.6 %collective-permute-start.2 = (f32[4,2,8,1,128]{4,0,3,2,1:T(4,128)}, f32[4,2,8,1,128]{4,0,3,2,1:T(4,128)}, u32[]{:S(2)}, u32[]{:S(2)}) collective-permute-start(f32[4,2,8,1,128]{4,0,3,2,1:T(4,128)} %pad_maximum_fusion.21), channel_id=1, source_target_pairs={{0,1},{1,2},{2,3},{3,4},{4,5},{5,6},{6,7},{8,9},{9,10},{10,11},{11... | collective-permute-start | bytes 98312 | tf_op jit(solution)/shard_map/ppermute | solution.py:20
  19.5 1.3 collective-permute-start.1
  21.4 5.1 %collective-permute-start = (f32[4,2,1,8,128]{4,0,3,2,1:T(4,128)}, f32[4,2,1,8,128]{4,0,3,2,1:T(4,128)}, u32[]{:S(2)}, u32[]{:S(2)}) collective-permute-start(f32[4,2,1,8,128]{4,0,3,2,1:T(4,128)} %pad_maximum_fusion.23), channel_id=1, source_target_pairs={{0,8},{8,16},{16,24},{1,9},{9,17},{17,25},{2,10},{10,18},{18,26},{... | collective-permute-start | bytes 98312 | tf_op jit(solution)/shard_map/ppermute | solution.py:20
  27.0 1.3 multiply_bitcast_fusion.7
  28.3 1.4 multiply_reduce_fusion.9
  29.8 13.1 %all_to_all.66 = f32[32,1,4]{2,1,0:T(1,128)S(1)} all-to-all(f32[32,1,4]{2,1,0:T(1,128)S(1)} %broadcast_in_dim.39), channel_id=1, replica_groups=mesh['member'=1,'gx'=4,'gy'=8] {'gx','gy'}, dimensions={0} | all-to-all | bytes 1024 | tf_op jit(solution)/shard_map/all_to_all | solution.py:13
  44.5 0.7 fusion.2
  46.0 2.6 %all-to-all-start.2 = ((f32[32,1,160]{2,1,0:T(1,128)}), f32[32,1,160]{2,1,0:T(1,128)S(1)}, u32[]{:S(2)}, u32[]{:S(2)}) async-start(f32[32,1,160]{2,1,0:T(1,128)} %broadcast_in_dim.41), calls=%async_computation.2 | async-start | bytes 65536 | tf_op jit(solution)/shard_map/all_to_all | solution.py:13
  48.6 1.3 collective-permute-start.7
  49.9 3.0 %collective-permute-start.6 = (f32[4,2,8,1,128]{4,0,3,2,1:T(4,128)S(1)}, f32[4,2,8,1,128]{4,0,3,2,1:T(4,128)S(1)}, u32[]{:S(2)}, u32[]{:S(2)}) collective-permute-start(f32[4,2,8,1,128]{4,0,3,2,1:T(4,128)S(1)} %pad_maximum_fusion.17), channel_id=1, source_target_pairs={{0,1},{1,2},{2,3},{3,4},{4,5},{5,6},{6,7},{8,9},{9,10},{10,11},{11... | collective-permute-start | bytes 98312 | tf_op jit(solution)/shard_map/ppermute | solution.py:20
  52.9 1.3 collective-permute-start.5
  54.3 4.5 %collective-permute-start.4 = (f32[4,2,1,8,128]{4,0,3,2,1:T(4,128)S(1)}, f32[4,2,1,8,128]{4,0,3,2,1:T(4,128)S(1)}, u32[]{:S(2)}, u32[]{:S(2)}) collective-permute-start(f32[4,2,1,8,128]{4,0,3,2,1:T(4,128)S(1)} %pad_maximum_fusion.19), channel_id=1, source_target_pairs={{0,8},{8,16},{16,24},{1,9},{9,17},{17,25},{2,10},{10,18},{18,26},{... | collective-permute-start | bytes 98312 | tf_op jit(solution)/shard_map/ppermute | solution.py:20
  59.0 1.3 multiply_bitcast_fusion.5
  61.1 1.3 multiply_reduce_fusion.8
  62.4 13.5 %all_to_all.67 = f32[32,1,4]{2,1,0:T(1,128)S(1)} all-to-all(f32[32,1,4]{2,1,0:T(1,128)S(1)} %broadcast_in_dim.42), channel_id=1, replica_groups=mesh['member'=1,'gx'=4,'gy'=8] {'gx','gy'}, dimensions={0} | all-to-all | bytes 1024 | tf_op jit(solution)/shard_map/all_to_all | solution.py:13
  76.3 8.8 %all_to_all.68 = f32[32,1,4]{2,1,0:T(1,128)S(1)} all-to-all(f32[32,1,4]{2,1,0:T(1,128)S(1)} %broadcast_in_dim.45), channel_id=1, replica_groups=mesh['member'=1,'gx'=4,'gy'=8] {'gx','gy'}, dimensions={0} | all-to-all | bytes 1024 | tf_op jit(solution)/shard_map/all_to_all | solution.py:13
  85.8 0.9 multiply_add_fusion.20
  87.5 0.7 fusion.1
  89.0 2.6 %all-to-all-start.5 = ((f32[32,1,160]{2,1,0:T(1,128)}), f32[32,1,160]{2,1,0:T(1,128)S(1)}, u32[]{:S(2)}, u32[]{:S(2)}) async-start(f32[32,1,160]{2,1,0:T(1,128)} %broadcast_in_dim.89), calls=%async_computation.5 | async-start | bytes 65536 | tf_op jit(solution)/shard_map/all_to_all | solution.py:13
  91.5 1.3 collective-permute-start.11
  92.9 3.0 %collective-permute-start.10 = (f32[4,2,8,1,128]{4,0,3,2,1:T(4,128)S(1)}, f32[4,2,8,1,128]{4,0,3,2,1:T(4,128)S(1)}, u32[]{:S(2)}, u32[]{:S(2)}) collective-permute-start(f32[4,2,8,1,128]{4,0,3,2,1:T(4,128)S(1)} %pad_maximum_fusion.13), channel_id=1, source_target_pairs={{0,1},{1,2},{2,3},{3,4},{4,5},{5,6},{6,7},{8,9},{9,10},{10,11},{11... | collective-permute-start | bytes 98312 | tf_op jit(solution)/shard_map/ppermute | solution.py:20
  95.9 1.3 collective-permute-start.9
  97.2 4.5 %collective-permute-start.8 = (f32[4,2,1,8,128]{4,0,3,2,1:T(4,128)S(1)}, f32[4,2,1,8,128]{4,0,3,2,1:T(4,128)S(1)}, u32[]{:S(2)}, u32[]{:S(2)}) collective-permute-start(f32[4,2,1,8,128]{4,0,3,2,1:T(4,128)S(1)} %pad_maximum_fusion.15), channel_id=1, source_target_pairs={{0,8},{8,16},{16,24},{1,9},{9,17},{17,25},{2,10},{10,18},{18,26},{... | collective-permute-start | bytes 98312 | tf_op jit(solution)/shard_map/ppermute | solution.py:20
  101.9 1.3 multiply_bitcast_fusion.3
  104.0 1.6 multiply_reduce_fusion.6
  106.5 6.5 %all-to-all-start.6 = ((f32[32,1,8]{2,1,0:T(1,128)}), f32[32,1,8]{2,1,0:T(1,128)S(1)}, u32[]{:S(2)}, u32[]{:S(2)}) async-start(f32[32,1,8]{2,1,0:T(1,128)} %broadcast_in_dim.91), calls=%async_computation.6 | async-start | bytes 32768 | tf_op jit(solution)/shard_map/all_to_all | solution.py:13
  113.0 7.1 %all-to-all-done.6 = f32[32,1,8]{2,1,0:T(1,128)S(1)} async-done(((f32[32,1,8]{2,1,0:T(1,128)}), f32[32,1,8]{2,1,0:T(1,128)S(1)}, u32[]{:S(2)}, u32[]{:S(2)}) %all-to-all-start.6) | async-done | bytes 1056 | tf_op jit(solution)/shard_map/all_to_all | solution.py:13
  121.4 2.7 %all-to-all-start.7 = ((f32[32,1,4]{2,1,0:T(1,128)}), f32[32,1,4]{2,1,0:T(1,128)S(1)}, u32[]{:S(2)}, u32[]{:S(2)}) async-start(f32[32,1,4]{2,1,0:T(1,128)} %broadcast_in_dim.92), calls=%async_computation.7 | async-start | bytes 32768 | tf_op jit(solution)/shard_map/all_to_all | solution.py:13
  124.5 6.5 %all-to-all-done.7 = f32[32,1,4]{2,1,0:T(1,128)S(1)} async-done(((f32[32,1,4]{2,1,0:T(1,128)}), f32[32,1,4]{2,1,0:T(1,128)S(1)}, u32[]{:S(2)}, u32[]{:S(2)}) %all-to-all-start.7) | async-done | bytes 544 | tf_op jit(solution)/shard_map/all_to_all | solution.py:13
  132.6 0.7 fusion
  134.1 2.6 %all-to-all-start.8 = ((f32[32,1,160]{2,1,0:T(1,128)}), f32[32,1,160]{2,1,0:T(1,128)S(1)}, u32[]{:S(2)}, u32[]{:S(2)}) async-start(f32[32,1,160]{2,1,0:T(1,128)} %broadcast_in_dim.94), calls=%async_computation.8 | async-start | bytes 65536 | tf_op jit(solution)/shard_map/all_to_all | solution.py:13
  136.7 1.3 collective-permute-start.15
  138.0 3.0 %collective-permute-start.14 = (f32[4,2,8,1,128]{4,0,3,2,1:T(4,128)S(1)}, f32[4,2,8,1,128]{4,0,3,2,1:T(4,128)S(1)}, u32[]{:S(2)}, u32[]{:S(2)}) collective-permute-start(f32[4,2,8,1,128]{4,0,3,2,1:T(4,128)S(1)} %pad_maximum_fusion.9), channel_id=1, source_target_pairs={{0,1},{1,2},{2,3},{3,4},{4,5},{5,6},{6,7},{8,9},{9,10},{10,11},{11... | collective-permute-start | bytes 98312 | tf_op jit(solution)/shard_map/ppermute | solution.py:20
  141.0 1.3 collective-permute-start.13
  142.3 4.5 %collective-permute-start.12 = (f32[4,2,1,8,128]{4,0,3,2,1:T(4,128)S(1)}, f32[4,2,1,8,128]{4,0,3,2,1:T(4,128)S(1)}, u32[]{:S(2)}, u32[]{:S(2)}) collective-permute-start(f32[4,2,1,8,128]{4,0,3,2,1:T(4,128)S(1)} %pad_maximum_fusion.11), channel_id=1, source_target_pairs={{0,8},{8,16},{16,24},{1,9},{9,17},{17,25},{2,10},{10,18},{18,26},{... | collective-permute-start | bytes 98312 | tf_op jit(solution)/shard_map/ppermute | solution.py:20
  147.6 1.0 collective-permute-done.12
  150.1 6.5 %all-to-all-start.9 = ((f32[32,1,12]{2,1,0:T(1,128)}), f32[32,1,12]{2,1,0:T(1,128)S(1)}, u32[]{:S(2)}, u32[]{:S(2)}) async-start(f32[32,1,12]{2,1,0:T(1,128)} %broadcast_in_dim.96), calls=%async_computation.9 | async-start | bytes 32768 | tf_op jit(solution)/shard_map/all_to_all | solution.py:13
  156.9 6.8 %all-to-all-done.9 = f32[32,1,12]{2,1,0:T(1,128)S(1)} async-done(((f32[32,1,12]{2,1,0:T(1,128)}), f32[32,1,12]{2,1,0:T(1,128)S(1)}, u32[]{:S(2)}, u32[]{:S(2)}) %all-to-all-start.9) | async-done | bytes 1568 | tf_op jit(solution)/shard_map/all_to_all | solution.py:13
  165.0 2.5 %all-to-all-start.10 = ((f32[32,1,4]{2,1,0:T(1,128)}), f32[32,1,4]{2,1,0:T(1,128)S(1)}, u32[]{:S(2)}, u32[]{:S(2)}) async-start(f32[32,1,4]{2,1,0:T(1,128)} %broadcast_in_dim.97), calls=%async_computation.10 | async-start | bytes 32768 | tf_op jit(solution)/shard_map/all_to_all | solution.py:13
  167.8 6.9 %all-to-all-done.10 = f32[32,1,4]{2,1,0:T(1,128)S(1)} async-done(((f32[32,1,4]{2,1,0:T(1,128)}), f32[32,1,4]{2,1,0:T(1,128)S(1)}, u32[]{:S(2)}, u32[]{:S(2)}) %all-to-all-start.10) | async-done | bytes 544 | tf_op jit(solution)/shard_map/all_to_all | solution.py:13
  175.6 1.1 custom-call.11
  176.9 1.0 custom-call.12
  179.2 0.7 copy.123
  (193 shorter events, 23.2 us)
Async XLA Ops:
  0.0 2.0 %copy-start.2 = (f32[4,8,8,128]{3,2,1,0:T(8,128)S(1)}, f32[4,8,8,128]{3,2,1,0:T(8,128)}, u32[]{:S(2)}) copy-start(f32[4,8,8,128]{3,2,1,0:T(8,128)} %param.8) | copy-start | bytes 393220
  0.9 1.8 %copy-start.3 = (f32[4,8,8,128]{3,2,1,0:T(8,128)S(1)}, f32[4,8,8,128]{3,2,1,0:T(8,128)}, u32[]{:S(2)}) copy-start(f32[4,8,8,128]{3,2,1,0:T(8,128)} %param.7) | copy-start | bytes 393220
  0.9 1.8 %copy-start = (f32[4,2,8,8,128]{4,3,2,1,0:T(8,128)S(1)}, f32[4,2,8,8,128]{4,3,2,1,0:T(8,128)}, u32[]{:S(2)}) copy-start(f32[4,2,8,8,128]{4,3,2,1,0:T(8,128)} %param.11) | copy-start | bytes 786436
  2.7 0.6 copy-start.12
  2.7 0.6 copy-start.16
  2.9 0.8 copy-start.20
  5.1 21.7 %all-to-all-start = ((f32[32,1,160]{2,1,0:T(1,128)}), f32[32,1,160]{2,1,0:T(1,128)S(1)}, u32[]{:S(2)}, u32[]{:S(2)}) async-start(f32[32,1,160]{2,1,0:T(1,128)} %broadcast_in_dim.38), calls=%async_computation | async-start | bytes 65536 | tf_op jit(solution)/shard_map/all_to_all | solution.py:13
  13.2 15.1 %collective-permute-start.3 = (f32[4,2,8,1,128]{4,0,3,2,1:T(4,128)}, f32[4,2,8,1,128]{4,0,3,2,1:T(4,128)S(1)}, u32[]{:S(2)}, u32[]{:S(2)}) collective-permute-start(f32[4,2,8,1,128]{4,0,3,2,1:T(4,128)} %pad_maximum_fusion.20), channel_id=1, source_target_pairs={{1,0},{2,1},{3,2},{4,3},{5,4},{6,5},{7,6},{9,8},{10,9},{11,10},{12... | collective-permute-start | bytes 98312 | tf_op jit(solution)/shard_map/ppermute | solution.py:20
  15.3 13.0 %collective-permute-start.2 = (f32[4,2,8,1,128]{4,0,3,2,1:T(4,128)}, f32[4,2,8,1,128]{4,0,3,2,1:T(4,128)}, u32[]{:S(2)}, u32[]{:S(2)}) collective-permute-start(f32[4,2,8,1,128]{4,0,3,2,1:T(4,128)} %pad_maximum_fusion.21), channel_id=1, source_target_pairs={{0,1},{1,2},{2,3},{3,4},{4,5},{5,6},{6,7},{8,9},{9,10},{10,11},{11... | collective-permute-start | bytes 98312 | tf_op jit(solution)/shard_map/ppermute | solution.py:20
  19.5 8.8 %collective-permute-start.1 = (f32[4,2,1,8,128]{4,0,3,2,1:T(4,128)}, f32[4,2,1,8,128]{4,0,3,2,1:T(4,128)}, u32[]{:S(2)}, u32[]{:S(2)}) collective-permute-start(f32[4,2,1,8,128]{4,0,3,2,1:T(4,128)} %pad_maximum_fusion.22), channel_id=1, source_target_pairs={{8,0},{16,8},{24,16},{9,1},{17,9},{25,17},{10,2},{18,10},{26,18},{... | collective-permute-start | bytes 98312 | tf_op jit(solution)/shard_map/ppermute | solution.py:20
  21.4 6.9 %collective-permute-start = (f32[4,2,1,8,128]{4,0,3,2,1:T(4,128)}, f32[4,2,1,8,128]{4,0,3,2,1:T(4,128)}, u32[]{:S(2)}, u32[]{:S(2)}) collective-permute-start(f32[4,2,1,8,128]{4,0,3,2,1:T(4,128)} %pad_maximum_fusion.23), channel_id=1, source_target_pairs={{0,8},{8,16},{16,24},{1,9},{9,17},{17,25},{2,10},{10,18},{18,26},{... | collective-permute-start | bytes 98312 | tf_op jit(solution)/shard_map/ppermute | solution.py:20
  26.6 1.7 copy-start.1
  43.7 0.8 copy-start.13
  43.8 0.8 copy-start.17
  43.8 0.8 copy-start.21
  44.0 15.0 %copy-start.8 = (f32[8,8,128]{2,1,0:T(8,128)S(1)}, f32[8,8,128]{2,1,0:T(8,128)}, u32[]{:S(2)}) copy-start(f32[8,8,128]{2,1,0:T(8,128)} %get-tuple-element.123) | copy-start | bytes 98308
  46.0 12.8 %all-to-all-start.2 = ((f32[32,1,160]{2,1,0:T(1,128)}), f32[32,1,160]{2,1,0:T(1,128)S(1)}, u32[]{:S(2)}, u32[]{:S(2)}) async-start(f32[32,1,160]{2,1,0:T(1,128)} %broadcast_in_dim.41), calls=%async_computation.2 | async-start | bytes 65536 | tf_op jit(solution)/shard_map/all_to_all | solution.py:13
  48.6 11.7 %collective-permute-start.7 = (f32[4,2,8,1,128]{4,0,3,2,1:T(4,128)S(1)}, f32[4,2,8,1,128]{4,0,3,2,1:T(4,128)S(1)}, u32[]{:S(2)}, u32[]{:S(2)}) collective-permute-start(f32[4,2,8,1,128]{4,0,3,2,1:T(4,128)S(1)} %pad_maximum_fusion.16), channel_id=1, source_target_pairs={{1,0},{2,1},{3,2},{4,3},{5,4},{6,5},{7,6},{9,8},{10,9},{11,10},{12... | collective-permute-start | bytes 98312 | tf_op jit(solution)/shard_map/ppermute | solution.py:20
  49.9 10.4 %collective-permute-start.6 = (f32[4,2,8,1,128]{4,0,3,2,1:T(4,128)S(1)}, f32[4,2,8,1,128]{4,0,3,2,1:T(4,128)S(1)}, u32[]{:S(2)}, u32[]{:S(2)}) collective-permute-start(f32[4,2,8,1,128]{4,0,3,2,1:T(4,128)S(1)} %pad_maximum_fusion.17), channel_id=1, source_target_pairs={{0,1},{1,2},{2,3},{3,4},{4,5},{5,6},{6,7},{8,9},{9,10},{10,11},{11... | collective-permute-start | bytes 98312 | tf_op jit(solution)/shard_map/ppermute | solution.py:20
  52.9 7.3 %collective-permute-start.5 = (f32[4,2,1,8,128]{4,0,3,2,1:T(4,128)S(1)}, f32[4,2,1,8,128]{4,0,3,2,1:T(4,128)S(1)}, u32[]{:S(2)}, u32[]{:S(2)}) collective-permute-start(f32[4,2,1,8,128]{4,0,3,2,1:T(4,128)S(1)} %pad_maximum_fusion.18), channel_id=1, source_target_pairs={{8,0},{16,8},{24,16},{9,1},{17,9},{25,17},{10,2},{18,10},{26,18},{... | collective-permute-start | bytes 98312 | tf_op jit(solution)/shard_map/ppermute | solution.py:20
  54.3 6.2 %collective-permute-start.4 = (f32[4,2,1,8,128]{4,0,3,2,1:T(4,128)S(1)}, f32[4,2,1,8,128]{4,0,3,2,1:T(4,128)S(1)}, u32[]{:S(2)}, u32[]{:S(2)}) collective-permute-start(f32[4,2,1,8,128]{4,0,3,2,1:T(4,128)S(1)} %pad_maximum_fusion.19), channel_id=1, source_target_pairs={{0,8},{8,16},{16,24},{1,9},{9,17},{17,25},{2,10},{10,18},{18,26},{... | collective-permute-start | bytes 98312 | tf_op jit(solution)/shard_map/ppermute | solution.py:20
  60.3 0.6 copy-start.5
  60.5 0.6 copy-start.7
  86.7 0.8 copy-start.14
  86.7 0.8 copy-start.18
  86.7 0.8 copy-start.22
  86.9 15.0 %copy-start.9 = (f32[8,8,128]{2,1,0:T(8,128)S(1)}, f32[8,8,128]{2,1,0:T(8,128)}, u32[]{:S(2)}) copy-start(f32[8,8,128]{2,1,0:T(8,128)} %get-tuple-element.123) | copy-start | bytes 98308
  89.0 12.8 %all-to-all-start.5 = ((f32[32,1,160]{2,1,0:T(1,128)}), f32[32,1,160]{2,1,0:T(1,128)S(1)}, u32[]{:S(2)}, u32[]{:S(2)}) async-start(f32[32,1,160]{2,1,0:T(1,128)} %broadcast_in_dim.89), calls=%async_computation.5 | async-start | bytes 65536 | tf_op jit(solution)/shard_map/all_to_all | solution.py:13
  91.5 11.7 %collective-permute-start.11 = (f32[4,2,8,1,128]{4,0,3,2,1:T(4,128)S(1)}, f32[4,2,8,1,128]{4,0,3,2,1:T(4,128)S(1)}, u32[]{:S(2)}, u32[]{:S(2)}) collective-permute-start(f32[4,2,8,1,128]{4,0,3,2,1:T(4,128)S(1)} %pad_maximum_fusion.12), channel_id=1, source_target_pairs={{1,0},{2,1},{3,2},{4,3},{5,4},{6,5},{7,6},{9,8},{10,9},{11,10},{12... | collective-permute-start | bytes 98312 | tf_op jit(solution)/shard_map/ppermute | solution.py:20
  92.9 10.4 %collective-permute-start.10 = (f32[4,2,8,1,128]{4,0,3,2,1:T(4,128)S(1)}, f32[4,2,8,1,128]{4,0,3,2,1:T(4,128)S(1)}, u32[]{:S(2)}, u32[]{:S(2)}) collective-permute-start(f32[4,2,8,1,128]{4,0,3,2,1:T(4,128)S(1)} %pad_maximum_fusion.13), channel_id=1, source_target_pairs={{0,1},{1,2},{2,3},{3,4},{4,5},{5,6},{6,7},{8,9},{9,10},{10,11},{11... | collective-permute-start | bytes 98312 | tf_op jit(solution)/shard_map/ppermute | solution.py:20
  95.9 7.3 %collective-permute-start.9 = (f32[4,2,1,8,128]{4,0,3,2,1:T(4,128)S(1)}, f32[4,2,1,8,128]{4,0,3,2,1:T(4,128)S(1)}, u32[]{:S(2)}, u32[]{:S(2)}) collective-permute-start(f32[4,2,1,8,128]{4,0,3,2,1:T(4,128)S(1)} %pad_maximum_fusion.14), channel_id=1, source_target_pairs={{8,0},{16,8},{24,16},{9,1},{17,9},{25,17},{10,2},{18,10},{26,18},{... | collective-permute-start | bytes 98312 | tf_op jit(solution)/shard_map/ppermute | solution.py:20
  97.2 6.2 %collective-permute-start.8 = (f32[4,2,1,8,128]{4,0,3,2,1:T(4,128)S(1)}, f32[4,2,1,8,128]{4,0,3,2,1:T(4,128)S(1)}, u32[]{:S(2)}, u32[]{:S(2)}) collective-permute-start(f32[4,2,1,8,128]{4,0,3,2,1:T(4,128)S(1)} %pad_maximum_fusion.15), channel_id=1, source_target_pairs={{0,8},{8,16},{16,24},{1,9},{9,17},{17,25},{2,10},{10,18},{18,26},{... | collective-permute-start | bytes 98312 | tf_op jit(solution)/shard_map/ppermute | solution.py:20
  103.2 0.6 copy-start.4
  103.4 0.6 copy-start.6
  106.5 13.6 %all-to-all-start.6 = ((f32[32,1,8]{2,1,0:T(1,128)}), f32[32,1,8]{2,1,0:T(1,128)S(1)}, u32[]{:S(2)}, u32[]{:S(2)}) async-start(f32[32,1,8]{2,1,0:T(1,128)} %broadcast_in_dim.91), calls=%async_computation.6 | async-start | bytes 32768 | tf_op jit(solution)/shard_map/all_to_all | solution.py:13
  121.4 9.6 %all-to-all-start.7 = ((f32[32,1,4]{2,1,0:T(1,128)}), f32[32,1,4]{2,1,0:T(1,128)S(1)}, u32[]{:S(2)}, u32[]{:S(2)}) async-start(f32[32,1,4]{2,1,0:T(1,128)} %broadcast_in_dim.92), calls=%async_computation.7 | async-start | bytes 32768 | tf_op jit(solution)/shard_map/all_to_all | solution.py:13
  131.8 0.8 copy-start.15
  131.8 0.8 copy-start.19
  131.8 0.8 copy-start.23
  132.1 15.0 %copy-start.10 = (f32[8,8,128]{2,1,0:T(8,128)S(1)}, f32[8,8,128]{2,1,0:T(8,128)}, u32[]{:S(2)}) copy-start(f32[8,8,128]{2,1,0:T(8,128)} %get-tuple-element.123) | copy-start | bytes 98308
  132.1 15.0 %copy-start.11 = (f32[8,8,128]{2,1,0:T(8,128)S(1)}, f32[8,8,128]{2,1,0:T(8,128)}, u32[]{:S(2)}) copy-start(f32[8,8,128]{2,1,0:T(8,128)} %get-tuple-element.125) | copy-start | bytes 98308
  134.1 12.8 %all-to-all-start.8 = ((f32[32,1,160]{2,1,0:T(1,128)}), f32[32,1,160]{2,1,0:T(1,128)S(1)}, u32[]{:S(2)}, u32[]{:S(2)}) async-start(f32[32,1,160]{2,1,0:T(1,128)} %broadcast_in_dim.94), calls=%async_computation.8 | async-start | bytes 65536 | tf_op jit(solution)/shard_map/all_to_all | solution.py:13
  136.7 10.9 %collective-permute-start.15 = (f32[4,2,8,1,128]{4,0,3,2,1:T(4,128)S(1)}, f32[4,2,8,1,128]{4,0,3,2,1:T(4,128)S(1)}, u32[]{:S(2)}, u32[]{:S(2)}) collective-permute-start(f32[4,2,8,1,128]{4,0,3,2,1:T(4,128)S(1)} %pad_maximum_fusion.8), channel_id=1, source_target_pairs={{1,0},{2,1},{3,2},{4,3},{5,4},{6,5},{7,6},{9,8},{10,9},{11,10},{12... | collective-permute-start | bytes 98312 | tf_op jit(solution)/shard_map/ppermute | solution.py:20
  138.0 9.6 %collective-permute-start.14 = (f32[4,2,8,1,128]{4,0,3,2,1:T(4,128)S(1)}, f32[4,2,8,1,128]{4,0,3,2,1:T(4,128)S(1)}, u32[]{:S(2)}, u32[]{:S(2)}) collective-permute-start(f32[4,2,8,1,128]{4,0,3,2,1:T(4,128)S(1)} %pad_maximum_fusion.9), channel_id=1, source_target_pairs={{0,1},{1,2},{2,3},{3,4},{4,5},{5,6},{6,7},{8,9},{9,10},{10,11},{11... | collective-permute-start | bytes 98312 | tf_op jit(solution)/shard_map/ppermute | solution.py:20
  141.0 6.6 %collective-permute-start.13 = (f32[4,2,1,8,128]{4,0,3,2,1:T(4,128)S(1)}, f32[4,2,1,8,128]{4,0,3,2,1:T(4,128)S(1)}, u32[]{:S(2)}, u32[]{:S(2)}) collective-permute-start(f32[4,2,1,8,128]{4,0,3,2,1:T(4,128)S(1)} %pad_maximum_fusion.10), channel_id=1, source_target_pairs={{8,0},{16,8},{24,16},{9,1},{17,9},{25,17},{10,2},{18,10},{26,18},{... | collective-permute-start | bytes 98312 | tf_op jit(solution)/shard_map/ppermute | solution.py:20
  142.3 6.2 %collective-permute-start.12 = (f32[4,2,1,8,128]{4,0,3,2,1:T(4,128)S(1)}, f32[4,2,1,8,128]{4,0,3,2,1:T(4,128)S(1)}, u32[]{:S(2)}, u32[]{:S(2)}) collective-permute-start(f32[4,2,1,8,128]{4,0,3,2,1:T(4,128)S(1)} %pad_maximum_fusion.11), channel_id=1, source_target_pairs={{0,8},{8,16},{16,24},{1,9},{9,17},{17,25},{2,10},{10,18},{18,26},{... | collective-permute-start | bytes 98312 | tf_op jit(solution)/shard_map/ppermute | solution.py:20
  150.1 13.6 %all-to-all-start.9 = ((f32[32,1,12]{2,1,0:T(1,128)}), f32[32,1,12]{2,1,0:T(1,128)S(1)}, u32[]{:S(2)}, u32[]{:S(2)}) async-start(f32[32,1,12]{2,1,0:T(1,128)} %broadcast_in_dim.96), calls=%async_computation.9 | async-start | bytes 32768 | tf_op jit(solution)/shard_map/all_to_all | solution.py:13
  165.0 9.6 %all-to-all-start.10 = ((f32[32,1,4]{2,1,0:T(1,128)}), f32[32,1,4]{2,1,0:T(1,128)S(1)}, u32[]{:S(2)}, u32[]{:S(2)}) async-start(f32[32,1,4]{2,1,0:T(1,128)} %broadcast_in_dim.97), calls=%async_computation.10 | async-start | bytes 32768 | tf_op jit(solution)/shard_map/all_to_all | solution.py:13

commit v2 on v0

v2 whole, which is shorter than its diff:
```python
import functools

import jax
import jax.numpy as jnp
from jax import lax
from jax.experimental import pallas as pl
from jax.experimental.pallas import tpu as pltpu
from jax.sharding import PartitionSpec as P

WELLS = 40
RHS = 4
LANES = 128
LAT_UP, LAT_DOWN, RISE, FALL, DIAGONAL = 4, 8, 12, 16, 20
WELL_EQ, WELL_ID, GUESS, RIGHT = 24, 26, 27, 35
BACK_IN, BACK_EQ, BACK_ID, BACK_GUESS = 43, 47, 49, 50
FACE_PLANES = 58
CORNER_ROWS = 19
SIDE_IN, SIDE_EQ, SIDE_ID, SIDE_GUESS = 4, 8, 10, 11


def product(blocks, first, second):
    return [
        blocks(0) * first + blocks(2) * second,
        blocks(1) * first + blocks(3) * second,
    ]


def iota(shape, axis):
    return lax.broadcasted_iota(jnp.int32, shape, axis)


def roll_up(value, axis):
    return pltpu.roll(value, 1, axis)


def roll_down(value, axis):
    return pltpu.roll(value, value.shape[axis] - 1, axis)


def layer_moves(rising, falling):
    axis = rising.ndim - 1
    lane = iota(rising.shape, axis)
    up = jnp.where(lane == 0, 0.0, roll_up(rising, axis))
    down = jnp.where(lane == LANES - 1, 0.0, roll_down(falling, axis))
    return up + down


def block_stencil(couplings, diagonal, first, second, incoming):
    result = product(lambda e: diagonal[e], first, second)
    moved = [product(lambda e, d=d: couplings[d, e], first, second) for d in range(6)]
    row = iota(first.shape, 1)
    outgoing = [[], [], [], []]
    for b in range(2):
        east, west, north, south, rise, fall = (moved[d][b] for d in range(6))
        total = result[b] + jnp.concatenate([incoming[0][b][None], east[:-1]], axis=0)
        total = total + jnp.concatenate([west[1:], incoming[1][b][None]], axis=0)
        total = total + jnp.where(row == 0, incoming[2][b][:, None, :], roll_up(north, 1))
        total = total + jnp.where(
            row == row.shape[1] - 1, incoming[3][b][:, None, :], roll_down(south, 1)
        )
        result[b] = total + layer_moves(rise, fall)
        outgoing[0].append(west[0])
        outgoing[1].append(east[-1])
        outgoing[2].append(south[:, 0, :])
        outgoing[3].append(north[:, -1, :])
    return result, outgoing


def face_stencil(face, first, second, low_end, high_end, behind, entering):
    def planes(start):
        return lambda e: face[start + e]

    result = product(planes(DIAGONAL), first, second)
    up = product(planes(LAT_UP), first, second)
    down = product(planes(LAT_DOWN), first, second)
    rise = product(planes(RISE), first, second)
    fall = product(planes(FALL), first, second)
    row = iota(first.shape, 0)
    for b in range(2):
        total = result[b] + behind[b] + entering[b]
        total = total + jnp.where(row == 0, low_end[b], roll_up(up[b], 0))
        total = total + jnp.where(row == row.shape[0] - 1, high_end[b], roll_down(down[b], 0))
        result[b] = total + layer_moves(rise[b], fall[b])
    return result


def spread(totals, ids):
    table = jnp.broadcast_to(totals, (8, LANES))
    if ids.ndim == 2:
        return jnp.take_along_axis(table, ids, axis=1)
    return jnp.stack(
        [jnp.take_along_axis(table, ids[x], axis=1) for x in range(ids.shape[0])], axis=0
    )


def as_ids(plane):
    return plane.astype(jnp.int32)


class Corner:
    def __init__(self, pack, which, base):
        self.pack, self.start = pack, base * 8 + which

    def row(self, number):
        at = self.start + number
        return self.pack[at // 8, at % 8 : at % 8 + 1, :]


def corners_of(faces, base, rows):
    found = []
    for y_face in (2, 3):
        for x_end in range(2):
            found.append(Corner(faces[y_face], x_end * rows, base))
    return found


def corner_inputs(corners, values):
    ends = {}
    for c in range(4):
        x_end, y_end = c % 2, c // 2
        over_x = product(corners[c].row, *values[c])
        over_y = product(lambda e, c=c: corners[c].row(SIDE_IN + e), *values[c])
        ends[(2 + y_end, x_end)] = over_x
        ends[(x_end, y_end)] = over_y
    return ends


def put(row_number, lane_number, value, table):
    at = (iota(table.shape, 0) == row_number) & (iota(table.shape, 1) == lane_number)
    return jnp.where(at, value, table)


def full_sum(value):
    while value.ndim > 2:
        value = jnp.sum(value, axis=0)
    return jnp.sum(jnp.sum(value, axis=0, keepdims=True), axis=1, keepdims=True)


def segment_rows(ids, values, scratch):
    masks_at = [ids[x] for x in range(ids.shape[0])]
    fields = [[value[x] for x in range(ids.shape[0])] for value in values]
    scratch[:, WELLS:, :] = jnp.zeros_like(scratch[:, WELLS:, :])
    for w in range(WELLS):
        masks = [at == w for at in masks_at]
        for number, field in enumerate(fields):
            total = jnp.where(masks[0], field[0], 0.0)
            for x in range(1, len(masks)):
                total = total + jnp.where(masks[x], field[x], 0.0)
            scratch[number, w : w + 1, :] = jnp.sum(total, axis=0, keepdims=True)
    ones = jnp.ones((8, LANES), jnp.float32)
    rows = []
    for number in range(len(fields)):
        summed = lax.dot_general(
            ones,
            scratch[number],
            (((1,), (1,)), ((), ())),
            precision=lax.Precision.HIGHEST,
            preferred_element_type=jnp.float32,
        )
        rows.append(summed[0:1, :])
    return rows


def pack_rows(rows, table):
    for number, row in enumerate(rows):
        placed = row if number % 3 == 0 else pltpu.roll(row, WELLS * (number % 3), 1)
        table = table + jnp.where(
            iota(table.shape, 0) == number // 3, jnp.broadcast_to(placed, table.shape), 0.0
        )
    return table


def unpack_row(table, number):
    row = table[number // 3 : number // 3 + 1, :]
    if number % 3:
        row = pltpu.roll(row, LANES - WELLS * (number % 3), 1)
    return jnp.where(iota(row.shape, 1) < WELLS, row, 0.0)


def lane(table, row_number, lane_number):
    return table[row_number : row_number + 1, lane_number : lane_number + 1]


def lane_sum(row):
    return jnp.sum(row, axis=1, keepdims=True)


def pack_kernel(
    couplings, diagonal, wells, ids, right, guess, x_low, x_high, y_low, y_high
):
    last = guess.shape[2] - 1
    for axis, packs in ((0, (x_low, x_high)), (1, (y_low, y_high))):
        for end, pack in enumerate(packs):
            outer = 0 if end == 0 else last
            behind = 1 if end == 0 else last - 1
            inward = 2 * axis + (1 if end == 0 else 0)
            lateral = 2 * (1 - axis)

            def cut(ref, *index, at=outer):
                if axis == 0:
                    return ref[index + (at,)]
                return ref[index + (slice(None), at, slice(None))]

            for e in range(4):
                pack[e] = cut(couplings, inward, e)
                pack[LAT_UP + e] = cut(couplings, lateral, e)
                pack[LAT_DOWN + e] = cut(couplings, lateral + 1, e)
                pack[RISE + e] = cut(couplings, 4, e)
                pack[FALL + e] = cut(couplings, 5, e)
                pack[DIAGONAL + e] = cut(diagonal, e)
                pack[BACK_IN + e] = cut(couplings, inward, e, at=behind)
            for a in range(2):
                pack[WELL_EQ + a] = cut(wells, 2 + a)
                pack[BACK_EQ + a] = cut(wells, 2 + a, at=behind)
            pack[WELL_ID] = cut(ids).astype(jnp.float32)
            pack[BACK_ID] = cut(ids, at=behind).astype(jnp.float32)
            for k in range(RHS):
                for a in range(2):
                    pack[GUESS + 2 * k + a] = cut(guess, k, a)
                    pack[RIGHT + 2 * k + a] = cut(right, k, a)
                entering = product(
                    lambda e: cut(couplings, inward, e, at=behind),
                    cut(guess, k, 0, at=behind),
                    cut(guess, k, 1, at=behind),
                )
                pack[BACK_GUESS + 2 * k] = entering[0]
                pack[BACK_GUESS + 2 * k + 1] = entering[1]


def guess_kernel(wells, ids, guess, part, scratch):
    values = [wells[0] * guess[k, 0] + wells[1] * guess[k, 1] for k in range(RHS)]
    values.append(wells[0] * wells[2] + wells[1] * wells[3])
    values.append(wells[2] * wells[2] + wells[3] * wells[3])
    rows = segment_rows(ids, values, scratch)
    table = pack_rows(rows, jnp.zeros((8, LANES), jnp.float32))
    part[...] = jnp.broadcast_to(table[None, :2], part.shape)


def residual_kernel(
    couplings, diagonal, wells, ids, right, guess, fxl, fxh, fyl, fyh, parts,
    residual, image, residual_faces, x_low, x_high, y_low, y_high, part, small,
    scratch,
):
    faces = (fxl, fxh, fyl, fyh)
    totals = jnp.sum(parts[...], axis=0)
    corners = corners_of(faces, FACE_PLANES, CORNER_ROWS)
    all_ids = ids[...]
    face_ids = [as_ids(face[WELL_ID]) for face in faces]
    last = guess.shape[2] - 1
    table = jnp.zeros((8, LANES), jnp.float32)
    for k in range(RHS):
        s_row = unpack_row(totals, k)
        first, second = guess[k, 0], guess[k, 1]
        incoming = [
            product(
                lambda e, f=f: faces[f][e],
                faces[f][GUESS + 2 * k],
                faces[f][GUESS + 2 * k + 1],
            )
            for f in range(4)
        ]
        applied, outgoing = block_stencil(couplings, diagonal, first, second, incoming)
        at_wells = spread(s_row, all_ids)
        now = [
            right[k, a] - applied[a] - wells[2 + a] * at_wells for a in range(2)
        ]
        for a in range(2):
            residual[k, a] = now[a]
        ends = corner_inputs(
            corners,
            [[corners[c].row(SIDE_GUESS + 2 * k + a) for a in range(2)] for c in range(4)],
        )
        incoming = []
        for f in range(4):
            face = faces[f]
            there = face_stencil(
                face,
                face[GUESS + 2 * k],
                face[GUESS + 2 * k + 1],
                ends[(f, 0)],
                ends[(f, 1)],
                [face[BACK_GUESS + 2 * k + b] for b in range(2)],
                outgoing[f],
            )
            face_wells = spread(s_row, face_ids[f])
            outer = [
                face[RIGHT + 2 * k + a] - there[a] - face[WELL_EQ + a] * face_wells
                for a in range(2)
            ]
            for a in range(2):
                residual_faces[f, 2 * k + a] = outer[a]
            incoming.append(product(lambda e, f=f: faces[f][e], *outer))
        result, _ = block_stencil(couplings, diagonal, now[0], now[1], incoming)
        for a in range(2):
            image[k, a] = result[a]
            x_low[2 * k + a] = result[a][0]
            x_low[8 + 2 * k + a] = result[a][1]
            x_high[2 * k + a] = result[a][last]
            x_high[8 + 2 * k + a] = result[a][last - 1]
            y_low[2 * k + a] = result[a][:, 0, :]
            y_low[8 + 2 * k + a] = result[a][:, 1, :]
            y_high[2 * k + a] = result[a][:, last, :]
            y_high[8 + 2 * k + a] = result[a][:, last - 1, :]
        table = put(6, k, full_sum(now[0] * now[0] + now[1] * now[1]), table)
        table = put(6, 4 + k, full_sum(now[0] * result[0] + now[1] * result[1]), table)
        table = put(6, 8 + k, full_sum(result[0] * result[0] + result[1] * result[1]), table)
    values = []
    for side in (0, 2):
        for field in (residual, image):
            for k in range(RHS):
                values.append(wells[side] * field[k, 0] + wells[side + 1] * field[k, 1])
    rows = segment_rows(all_ids, values, scratch)
    table = pack_rows(rows, table)
    part[...] = jnp.broadcast_to(table[None], part.shape)
    small[...] = jnp.concatenate(
        [unpack_row(totals, 4), unpack_row(totals, 5), jnp.zeros((6, LANES), jnp.float32)], axis=0
    )


def first_step(totals, small, k):
    s_row, us_row = unpack_row(totals, k), unpack_row(totals, 4 + k)
    p_row, ps_row = unpack_row(totals, 8 + k), unpack_row(totals, 12 + k)
    within, equation = small[0:1, :], small[1:2, :]
    rr, rs, ss = (lane(totals, 6, 4 * i + k) for i in range(3))
    height = (rs + lane_sum(p_row * s_row)) / rr
    square = ss + lane_sum(2.0 * ps_row * s_row + equation * s_row * s_row)
    left = jnp.maximum(square - height * height * rr, 1e-7 * square)
    scale = lax.rsqrt(left)
    s_image = us_row + within * s_row
    s_second = (s_image - height * s_row) * scale
    p_second = (ps_row + equation * s_row - height * p_row) * scale
    shift = rs / rr + lane_sum(p_second * s_second)
    return dict(
        rr=rr, height=height, scale=scale, shift=shift, s_row=s_row, s_image=s_image,
        p_row=p_row, p_second=p_second,
    )


def krylov_kernel(
    couplings, diagonal, wells, ids, fxl, fxh, fyl, fyh, gxl, gxh, gyl, gyh,
    residual, image, residual_faces, parts, small_in,
    second_out, third_out, part, totals_out, scratch, values_scratch,
):
    faces, sent = (fxl, fxh, fyl, fyh), (gxl, gxh, gyl, gyh)
    totals = jnp.sum(parts[...], axis=0)
    totals_out[...] = totals
    small = small_in[...]
    corners = corners_of(faces, FACE_PLANES, CORNER_ROWS)
    sent_corners = corners_of(sent, 16, 8)
    all_ids = ids[...]
    face_ids = [as_ids(face[WELL_ID]) for face in faces]
    back_ids = [as_ids(face[BACK_ID]) for face in faces]
    corner_ids = [
        as_ids(jnp.broadcast_to(corner.row(SIDE_ID), (8, LANES))) for corner in corners
    ]
    table = jnp.zeros((8, LANES), jnp.float32)
    values = []
    for k in range(RHS):
        step = first_step(totals, small, k)
        height, scale, shift = step["height"], step["scale"], step["shift"]
        s_row, s_image = step["s_row"], step["s_image"]
        at_wells = spread(s_row, all_ids)
        now = [image[k, a] + wells[2 + a] * at_wells for a in range(2)]
        face_now, back_in = [], []
        for f in range(4):
            face, got = faces[f], sent[f]
            here = spread(s_row, face_ids[f])
            face_now.append([got[2 * k + a] + face[WELL_EQ + a] * here for a in range(2)])
            there = spread(s_row, back_ids[f])
            back = [got[8 + 2 * k + a] + face[BACK_EQ + a] * there for a in range(2)]
            back_in.append(product(lambda e, f=f: faces[f][BACK_IN + e], *back))
        corner_now = []
        for c in range(4):
            here = spread(s_row, corner_ids[c])[0:1, :]
            corner_now.append(
                [
                    sent_corners[c].row(2 * k + a) + corners[c].row(SIDE_EQ + a) * here
                    for a in range(2)
                ]
            )
        incoming = [product(lambda e, f=f: faces[f][e], *face_now[f]) for f in range(4)]
        applied, outgoing = block_stencil(couplings, diagonal, now[0], now[1], incoming)
        at_wells = spread(s_image, all_ids)
        second, third = [], []
        for a in range(2):
            twice = applied[a] + wells[2 + a] * at_wells
            base = (now[a] - height * residual[k, a]) * scale
            second.append(base)
            third.append((twice - height * now[a]) * scale - shift * base)
            second_out[k, a] = second[a]
            third_out[k, a] = third[a]
        ends = corner_inputs(corners, corner_now)
        incoming = []
        for f in range(4):
            face = faces[f]
            there = face_stencil(
                face, face_now[f][0], face_now[f][1], ends[(f, 0)], ends[(f, 1)], back_in[f],
                outgoing[f],
            )
            here = spread(s_image, face_ids[f])
            outer = []
            for a in range(2):
                twice = there[a] + face[WELL_EQ + a] * here
                base = (face_now[f][a] - height * residual_faces[f, 2 * k + a]) * scale
                outer.append((twice - height * face_now[f][a]) * scale - shift * base)
            incoming.append(product(lambda e, f=f: faces[f][e], *outer))
        result, _ = block_stencil(couplings, diagonal, third[0], third[1], incoming)
        fourth = [result[a] - shift * third[a] for a in range(2)]
        values_scratch[k] = wells[0] * third[0] + wells[1] * third[1]
        values_scratch[4 + k] = wells[2] * third[0] + wells[3] * third[1]
        values_scratch[8 + k] = wells[2] * fourth[0] + wells[3] * fourth[1]
        unit = lax.rsqrt(step["rr"])
        fields = [[residual[k, a] * unit for a in range(2)], second, third, fourth]
        number = 0
        for i in range(4):
            for j in range(i, 4):
                dot = full_sum(fields[i][0] * fields[j][0] + fields[i][1] * fields[j][1])
                table = put(4, 4 * number + k, dot, table)
                number += 1
    rows = segment_rows(all_ids, [values_scratch[n] for n in range(12)], scratch)
    table = pack_rows(rows, table)
    part[...] = jnp.broadcast_to(table[None], part.shape)


def solve_kernel(
    guess, residual, second, third, parts, first_totals, small_in, solution
):
    totals = jnp.sum(parts[...], axis=0)
    before, small = first_totals[...], small_in[...]
    equation = small[1:2, :]
    for k in range(RHS):
        step = first_step(before, small, k)
        unit = lax.rsqrt(step["rr"])
        beta = step["rr"] * unit
        s_third, p_third = unpack_row(totals, k), unpack_row(totals, 4 + k)
        p_fourth = unpack_row(totals, 8 + k)
        gram = {}
        number = 0
        for i in range(4):
            for j in range(i, 4):
                gram[(i, j)] = lane(totals, 4, 4 * number + k)
                number += 1
        gram[(0, 3)] += lane_sum(step["p_row"] * s_third) * unit
        gram[(1, 3)] += lane_sum(step["p_second"] * s_third)
        gram[(2, 3)] += lane_sum(p_third * s_third)
        gram[(3, 3)] += lane_sum(2.0 * p_fourth * s_third + equation * s_third * s_third)
        tiny = 1e-30
        inverse = [lax.rsqrt(jnp.maximum(gram[(i, i)], tiny)) for i in range(4)]
        length = [jnp.maximum(gram[(i, i)], tiny) * inverse[i] for i in range(4)]
        upper = {}
        for i in range(4):
            for j in range(i, 4):
                entry = gram[(i, j)] * inverse[i] * inverse[j]
                for m in range(i):
                    entry = entry - upper[(m, i)] * upper[(m, j)]
                if i == j:
                    pivot = lax.rsqrt(jnp.maximum(entry, 1e-6))
                    upper[(i, i)] = jnp.maximum(entry, 1e-6) * pivot
                    over = pivot
                else:
                    upper[(i, j)] = entry * over
        shift = step["shift"]
        following = lax.rsqrt(step["rr"]) / step["scale"]
        columns = [
            [(0, step["height"] * length[0]), (1, following * length[1])],
            [(1, shift * length[1]), (2, length[2])],
            [(2, shift * length[2]), (3, length[3])],
        ]
        zero = jnp.zeros_like(shift)
        hessenberg = [[zero] * 3 for _ in range(4)]
        for j in range(3):
            for i in range(j + 2):
                for m, factor in columns[j]:
                    if m >= i:
                        hessenberg[i][j] = hessenberg[i][j] + upper[(i, m)] * factor
        target = [beta * length[0] * upper[(0, 0)], zero, zero, zero]
        for j in range(3):
            top, bottom = hessenberg[j][j], hessenberg[j + 1][j]
            turn = lax.rsqrt(top * top + bottom * bottom)
            cosine, sine = top * turn, bottom * turn
            for m in range(j, 3):
                high, low = hessenberg[j][m], hessenberg[j + 1][m]
                hessenberg[j][m] = cosine * high + sine * low
                hessenberg[j + 1][m] = cosine * low - sine * high
            high, low = target[j], target[j + 1]
            target[j] = cosine * high + sine * low
            target[j + 1] = cosine * low - sine * high
        weights = [zero] * 3
        for i in (2, 1, 0):
            value = target[i]
            for j in range(i + 1, 3):
                value = value - hessenberg[i][j] * weights[j]
            weights[i] = value / hessenberg[i][i]
        for a in range(2):
            solution[k, a] = (
                guess[k, a]
                + (weights[0] * unit) * residual[k, a]
                + weights[1] * second[k, a]
                + weights[2] * third[k, a]
            )


def call(kernel, shapes, arguments, scratch=()):
    whole = pl.BlockSpec(memory_space=pltpu.VMEM)
    return pl.pallas_call(
        kernel,
        out_shape=[jax.ShapeDtypeStruct(shape, jnp.float32) for shape in shapes],
        in_specs=[whole] * len(arguments),
        out_specs=[whole] * len(shapes),
        scratch_shapes=[pltpu.VMEM(shape, jnp.float32) for shape in scratch],
        compiler_params=pltpu.CompilerParams(vmem_limit_bytes=24 << 20),
    )(*arguments)


def from_behind(value, axis, steps):
    count = lax.axis_size(axis)
    leading, last = (max(0, -steps), min(count, count - steps))
    return lax.ppermute(value, axis, [(source, source + steps) for source in range(leading, last)])


def exchanged(part):
    return lax.all_to_all(part, ("gx", "gy"), 0, 0, tiled=True)


def corner_planes(rows):
    stacked = jnp.concatenate(rows, axis=0)
    spare = -stacked.shape[0] % 8
    if spare:
        stacked = jnp.pad(stacked, ((0, spare), (0, 0)))
    return stacked.reshape(-1, 8, LANES)


def body(couplings, diagonal, wells, ids, right, guess):
    devices = lax.axis_size("gx") * lax.axis_size("gy")
    plane = (8, LANES)
    field = guess.shape
    last = guess.shape[2] - 1

    packs = call(
        pack_kernel,
        [(FACE_PLANES,) + plane] * 4,
        (couplings, diagonal, wells, ids, right, guess),
    )
    fxl = from_behind(packs[1], "gx", 1)
    fxh = from_behind(packs[0], "gx", -1)
    (part,) = call(guess_kernel, [(devices, 2, LANES)], (wells, ids, guess), [(6, LANES, LANES)])
    parts = exchanged(part)
    packed = []
    for pack, at, side in ((packs[2], 0, LAT_DOWN), (packs[3], last, LAT_UP)):
        rows = []
        for face in (fxl, fxh):
            rows += [face[0:4, at], face[side : side + 4, at], face[WELL_EQ : GUESS + 8, at]]
        packed.append(jnp.concatenate([pack, corner_planes(rows)], axis=0))
    fyl = from_behind(packed[1], "gy", 1)
    fyh = from_behind(packed[0], "gy", -1)

    residual, image, residual_faces, x_low, x_high, y_low, y_high, part, small = call(
        residual_kernel,
        [field, field, (4, 8) + plane]
        + [(16,) + plane] * 4
        + [(devices, 8, LANES), (8, LANES)],
        (couplings, diagonal, wells, ids, right, guess, fxl, fxh, fyl, fyh, parts),
        [(16, LANES, LANES)],
    )
    gxl = from_behind(x_high, "gx", 1)
    gxh = from_behind(x_low, "gx", -1)
    parts = exchanged(part)
    packed = []
    for pack, at in ((y_low, 0), (y_high, last)):
        rows = [face[0:8, at] for face in (gxl, gxh)]
        packed.append(jnp.concatenate([pack, corner_planes(rows)], axis=0))
    gyl = from_behind(packed[1], "gy", 1)
    gyh = from_behind(packed[0], "gy", -1)

    second, third, part, totals = call(
        krylov_kernel,
        [field, field, (devices, 8, LANES), (8, LANES)],
        (couplings, diagonal, wells, ids, fxl, fxh, fyl, fyh, gxl, gxh, gyl, gyh)
        + (residual, image, residual_faces, parts, small),
        [(12, LANES, LANES), (12,) + guess.shape[2:]],
    )
    parts = exchanged(part)
    (result,) = call(
        solve_kernel,
        [field],
        (guess, residual, second, third, parts, totals, small),
    )
    return result


def solution(mesh):
    in_specs = (
        P("member", None, "gx", "gy", None),
        P("member", "gx", "gy", None),
        P("member", "gx", "gy", None),
        P("gx", "gy", None),
        P("member", None, "gx", "gy", None),
        P("member", None, "gx", "gy", None),
    )
    out_specs = P("member", None, "gx", "gy", None)
    return jax.shard_map(body, mesh=mesh, in_specs=in_specs, out_specs=out_specs, check_vma=False)
```

time: 523 us -> 87 us (0.17)
  blocking collectives: 445 us -> 14.5 us
  waiting for transfers between devices: 3.52 us -> 21.5 us
  other arithmetic: 15.4 us -> 0.06 us
  Pallas kernels: 0 us -> 14.1 us
  starting transfers between devices: 42.2 us -> 28.8 us
  matrix products: 7.38 us -> 0 us
    psum x11 -> x0, blocking collectives: 445 us -> none  [the longest x4 163 us: apply_summed(): lax.psum(well_partial(vectors, well_vectors, well_table), ('gx', 'gy'))]
    ppermute x16 -> x8, starting transfers between devices: 42.2 us -> 16.3 us  [from_behind(): lax.ppermute(value, axis, [(source, source + steps) for source in range(l...]
    all_to_all x0 -> x1, blocking collectives: none -> 14.5 us  [exchanged(): return lax.all_to_all(part, ('gx', 'gy'), 0, 0, tiled=True)]
    pallas_call x0 -> x5, Pallas kernels: none -> 14.1 us  [call(): pl.pallas_call(kernel, out_shape=[jax.ShapeDtypeStruct(shape, jnp.float32...]
    all_to_all x0 -> x2, starting transfers between devices: none -> 12.5 us  [exchanged(): return lax.all_to_all(part, ('gx', 'gy'), 0, 0, tiled=True)]
    ppermute x16 -> x8, waiting for transfers between devices: 3.52 us -> 14.4 us  [from_behind(): lax.ppermute(value, axis, [(source, source + steps) for source in range(l...]
    dot_general x9 -> x0, matrix products: 7.21 us -> none  [the longest x4 4.13 us: well_partial(): jnp.einsum('kc,wc->kw', weighted, well_table, precision=lax.Precision.HIG...]
    all_to_all x0 -> x2, waiting for transfers between devices: none -> 7.08 us  [exchanged(): return lax.all_to_all(part, ('gx', 'gy'), 0, 0, tiled=True)]
  transfers between devices with their start and end apart: 16 -> 10, of which waited for: 3 -> 5; matrix products, arithmetic and copies ran while one was open for 1% -> 0% of each run, Pallas kernels for 0% -> 3%
where the time goes in v2:
time: 87 us; the launch traced here: 86.4 us
  starting transfers between devices  28.8 us (33%)
  waiting for transfers between devices  21.5 us (25%)
  blocking collectives  14.5 us (17%)
  Pallas kernels  14.1 us (16%)
  local copies, waits for them, and re-layouts  7 us (8%)
    ppermute x8, starting transfers between devices, from_behind(): lax.ppermute(value, axis, [(source, source + steps) for source in range(l...  16.3 us
    all_to_all x1, blocking collectives, exchanged(): return lax.all_to_all(part, ('gx', 'gy'), 0, 0, tiled=True)  14.5 us
    ppermute x8, waiting for transfers between devices, from_behind(): lax.ppermute(value, axis, [(source, source + steps) for source in range(l...  14.4 us
    pallas_call x5, Pallas kernels, call(): pl.pallas_call(kernel, out_shape=[jax.ShapeDtypeStruct(shape, jnp.float32...  14.1 us
    all_to_all x2, starting transfers between devices, exchanged(): return lax.all_to_all(part, ('gx', 'gy'), 0, 0, tiled=True)  12.5 us
    all_to_all x2, waiting for transfers between devices, exchanged(): return lax.all_to_all(part, ('gx', 'gy'), 0, 0, tiled=True)  7.08 us
    unnamed x28, local copies, waits for them, and re-layouts  5.64 us
  transfers between devices with their start and end apart: 10, of which 5 were waited for; matrix products, arithmetic and copies ran while one was open for 0% of the time, Pallas kernels for 3%

profile of v2, /device:TPU:0, one launch (start us, length us, event | category | flops | bytes accessed | tf_op | source)
XLA Modules:
  0.0 86.4 jit_solution(13971584807252663409)
XLA Ops:
  0.0 1.1 %copy-done = f32[6,4,8,8,128]{4,3,2,1,0:T(8,128)S(1)} copy-done((f32[6,4,8,8,128]{4,3,2,1,0:T(8,128)S(1)}, f32[6,4,8,8,128]{4,3,2,1,0:T(8,128)}, u32[]{:S(2)}) %copy-start) | copy-done | bytes 786456
  1.1 0.9 %copy-done.2 = f32[4,2,8,8,128]{4,3,2,1,0:T(8,128)S(1)} copy-done((f32[4,2,8,8,128]{4,3,2,1,0:T(8,128)S(1)}, f32[4,2,8,8,128]{4,3,2,1,0:T(8,128)}, u32[]{:S(2)}) %copy-start.2) | copy-done | bytes 262168
  2.1 0.9 %copy-done.4 = f32[4,8,8,128]{3,2,1,0:T(8,128)S(1)} copy-done((f32[4,8,8,128]{3,2,1,0:T(8,128)S(1)}, f32[4,8,8,128]{3,2,1,0:T(8,128)}, u32[]{:S(2)}) %copy-start.4) | copy-done | bytes 131096
  3.0 0.9 %copy-done.6 = f32[4,8,8,128]{3,2,1,0:T(8,128)S(1)} copy-done((f32[4,8,8,128]{3,2,1,0:T(8,128)S(1)}, f32[4,8,8,128]{3,2,1,0:T(8,128)}, u32[]{:S(2)}) %copy-start.6) | copy-done | bytes 131096
  3.9 0.9 %copy-done.8 = f32[4,2,8,8,128]{4,3,2,1,0:T(8,128)S(1)} copy-done((f32[4,2,8,8,128]{4,3,2,1,0:T(8,128)S(1)}, f32[4,2,8,8,128]{4,3,2,1,0:T(8,128)}, u32[]{:S(2)}) %copy-start.8) | copy-done | bytes 262168
  4.8 0.8 copy-done.10
  5.6 0.3 shard_map.64
  5.9 1.3 %collective-permute-start.1 = (f32[58,8,128]{2,1,0:T(8,128)S(1)}, f32[58,8,128]{2,1,0:T(8,128)S(1)}, u32[]{:S(2)}, u32[]{:S(2)}) collective-permute-start(f32[58,8,128]{2,1,0:T(8,128)S(1)} %get-tuple-element.23), channel_id=1, source_target_pairs={{8,0},{16,8},{24,16},{9,1},{17,9},{25,17},{10,2},{18,10},{26,18},{... | collective-permute-start | bytes 712712 | tf_op jit(solution)/shard_map/ppermute | solution.py:518
  7.3 5.6 %collective-permute-start = (f32[58,8,128]{2,0,1:T(8,128)S(1)}, f32[58,8,128]{2,0,1:T(8,128)S(1)}, u32[]{:S(2)}, u32[]{:S(2)}) collective-permute-start(f32[58,8,128]{2,0,1:T(8,128)S(1)} %copy.7), channel_id=1, source_target_pairs={{0,8},{8,16},{16,24},{1,9},{9,17},{17,25},{2,10},{10,18},{18,26},{... | collective-permute-start | bytes 712712 | tf_op jit(solution)/shard_map/ppermute | solution.py:518
  12.9 3.8 %collective-permute-done.1.fxh = f32[58,8,128]{2,1,0:T(8,128)S(1)} collective-permute-done((f32[58,8,128]{2,1,0:T(8,128)S(1)}, f32[58,8,128]{2,1,0:T(8,128)S(1)}, u32[]{:S(2)}, u32[]{:S(2)}) %collective-permute-start.1) | collective-permute-done | bytes 237600 | tf_op jit(solution)/shard_map/ppermute | solution.py:518
  16.7 1.7 %collective-permute-done = f32[58,8,128]{2,0,1:T(8,128)S(1)} collective-permute-done((f32[58,8,128]{2,0,1:T(8,128)S(1)}, f32[58,8,128]{2,0,1:T(8,128)S(1)}, u32[]{:S(2)}, u32[]{:S(2)}) %collective-permute-start) | collective-permute-done | bytes 237600 | tf_op jit(solution)/shard_map/ppermute | solution.py:518
  18.4 0.2 concatenate.26
  18.7 0.2 concatenate.24
  18.9 0.0 copy-start.3
  18.9 0.0 copy-start.5
  18.9 0.0 copy-start.11
  19.0 0.0 copy-start.1
  19.0 1.4 %collective-permute-start.2 = (f32[63,8,128]{2,1,0:T(8,128)S(1)}, f32[63,8,128]{2,1,0:T(8,128)S(1)}, u32[]{:S(2)}, u32[]{:S(2)}) collective-permute-start(f32[63,8,128]{2,1,0:T(8,128)S(1)} %pad_maximum_fusion), channel_id=1, source_target_pairs={{0,1},{1,2},{2,3},{3,4},{4,5},{5,6},{6,7},{8,9},{9,10},{10,11},{11... | collective-permute-start | bytes 774152 | tf_op jit(solution)/shard_map/ppermute | solution.py:518
  20.5 1.3 %collective-permute-start.3 = (f32[63,8,128]{2,1,0:T(8,128)S(1)}, f32[63,8,128]{2,1,0:T(8,128)S(1)}, u32[]{:S(2)}, u32[]{:S(2)}) collective-permute-start(f32[63,8,128]{2,1,0:T(8,128)S(1)} %pad_maximum_fusion.1), channel_id=1, source_target_pairs={{1,0},{2,1},{3,2},{4,3},{5,4},{6,5},{7,6},{9,8},{10,9},{11,10},{12... | collective-permute-start | bytes 774152 | tf_op jit(solution)/shard_map/ppermute | solution.py:518
  21.8 0.0 copy-done.3
  21.8 0.0 copy-done.5
  21.8 0.0 copy-done.11
  21.8 2.2 %shard_map.65 = f32[32,2,128]{2,1,0:T(2,128)} custom-call(f32[4,8,8,128]{3,2,1,0:T(8,128)S(1)} %copy-done.5, s32[8,8,128]{2,1,0:T(8,128)S(1)} %copy-done.11, f32[4,2,8,8,128]{4,3,2,1,0:T(8,128)S(1)} %copy-done.3), custom_call_target="tpu_custom_call" | custom-call | tf_op jit(solution)/shard_map/pallas_call | solution.py:505
  24.0 9.9 %all-to-all-start = ((f32[32,2,128]{2,1,0:T(2,128)}), f32[32,2,128]{2,1,0:T(2,128)S(1)}, u32[]{:S(2)}, u32[]{:S(2)}) async-start(f32[32,2,128]{2,1,0:T(2,128)} %shard_map.65), calls=%async_computation | async-start | bytes 65536 | tf_op jit(solution)/shard_map/all_to_all | solution.py:522
  33.9 0.0 copy-start.7
  33.9 0.0 copy-start.9
  33.9 0.1 copy.13.fxl
  34.1 7.1 %all-to-all-done.parts = f32[32,2,128]{2,1,0:T(2,128)S(1)} async-done(((f32[32,2,128]{2,1,0:T(2,128)}), f32[32,2,128]{2,1,0:T(2,128)S(1)}, u32[]{:S(2)}, u32[]{:S(2)}) %all-to-all-start) | async-done | bytes 32800 | tf_op jit(solution)/shard_map/all_to_all | solution.py:522
  41.1 0.0 collective-permute-done.2.fyl
  41.1 0.0 collective-permute-done.3.fyh
  41.2 0.0 copy-done.1
  41.2 0.0 copy-done.7
  41.2 0.0 copy-done.9
  41.2 5.0 %shard_map.66 = (f32[4,2,8,8,128]{4,3,2,1,0:T(8,128)S(1)}, f32[4,2,8,8,128]{4,3,2,1,0:T(8,128)S(1)}, f32[4,8,8,128]{3,2,1,0:T(8,128)S(1)}, f32[16,8,128]{2,1,0:T...) custom-call(f32[6,4,8,8,128]{4,3,2,1,0:T(8,128)S(1)} %copy-done.1, ...), custom_call_target="tpu_custom_call" | custom-call | tf_op jit(solution)/shard_map/pallas_call | solution.py:505
  46.1 0.6 copy.14
  46.8 2.5 %collective-permute-start.4 = (f32[16,8,128]{2,0,1:T(8,128)}, f32[16,8,128]{2,0,1:T(8,128)S(1)}, u32[]{:S(2)}, u32[]{:S(2)}) collective-permute-start(f32[16,8,128]{2,0,1:T(8,128)} %copy.14), channel_id=1, source_target_pairs={{0,8},{8,16},{16,24},{1,9},{9,17},{17,25},{2,10},{10,18},{18,26},{... | collective-permute-start | bytes 196616 | tf_op jit(solution)/shard_map/ppermute | solution.py:518
  49.3 2.6 %all-to-all-start.1 = ((f32[32,8,128]{2,1,0:T(8,128)}), f32[32,8,128]{2,1,0:T(8,128)S(1)}, u32[]{:S(2)}, u32[]{:S(2)}) async-start(f32[32,8,128]{2,1,0:T(8,128)} %get-tuple-element.33), calls=%async_computation.1 | async-start | bytes 262144 | tf_op jit(solution)/shard_map/all_to_all | solution.py:522
  51.9 1.3 %collective-permute-start.5 = (f32[16,8,128]{2,1,0:T(8,128)S(1)}, f32[16,8,128]{2,1,0:T(8,128)S(1)}, u32[]{:S(2)}, u32[]{:S(2)}) collective-permute-start(f32[16,8,128]{2,1,0:T(8,128)S(1)} %get-tuple-element.28), channel_id=1, source_target_pairs={{8,0},{16,8},{24,16},{9,1},{17,9},{25,17},{10,2},{18,10},{26,18},{... | collective-permute-start | bytes 196616 | tf_op jit(solution)/shard_map/ppermute | solution.py:518
  53.2 0.0 collective-permute-done.4
  53.2 5.7 %collective-permute-done.5.gxh = f32[16,8,128]{2,1,0:T(8,128)S(1)} collective-permute-done((f32[16,8,128]{2,1,0:T(8,128)S(1)}, f32[16,8,128]{2,1,0:T(8,128)S(1)}, u32[]{:S(2)}, u32[]{:S(2)}) %collective-permute-start.5) | collective-permute-done | bytes 65568 | tf_op jit(solution)/shard_map/ppermute | solution.py:518
  58.9 1.6 %collective-permute-start.6 = (f32[18,8,128]{2,1,0:T(8,128)S(1)}, f32[18,8,128]{2,1,0:T(8,128)S(1)}, u32[]{:S(2)}, u32[]{:S(2)}) collective-permute-start(f32[18,8,128]{2,1,0:T(8,128)S(1)} %pad_maximum_fusion.2), channel_id=1, source_target_pairs={{0,1},{1,2},{2,3},{3,4},{4,5},{5,6},{6,7},{8,9},{9,10},{10,11},{11... | collective-permute-start | bytes 221192 | tf_op jit(solution)/shard_map/ppermute | solution.py:518
  60.6 1.3 %collective-permute-start.7 = (f32[18,8,128]{2,1,0:T(8,128)S(1)}, f32[18,8,128]{2,1,0:T(8,128)S(1)}, u32[]{:S(2)}, u32[]{:S(2)}) collective-permute-start(f32[18,8,128]{2,1,0:T(8,128)S(1)} %pad_maximum_fusion.3), channel_id=1, source_target_pairs={{1,0},{2,1},{3,2},{4,3},{5,4},{6,5},{7,6},{9,8},{10,9},{11,10},{12... | collective-permute-start | bytes 221192 | tf_op jit(solution)/shard_map/ppermute | solution.py:518
  62.0 0.0 collective-permute-done.6.gyl
  62.0 3.2 %collective-permute-done.7.gyh = f32[18,8,128]{2,1,0:T(8,128)S(1)} collective-permute-done((f32[18,8,128]{2,1,0:T(8,128)S(1)}, f32[18,8,128]{2,1,0:T(8,128)S(1)}, u32[]{:S(2)}, u32[]{:S(2)}) %collective-permute-start.7) | collective-permute-done | bytes 73760 | tf_op jit(solution)/shard_map/ppermute | solution.py:518
  65.2 0.0 all-to-all-done.1.parts
  65.2 4.7 %shard_map.67 = (f32[4,2,8,8,128]{4,3,2,1,0:T(8,128)S(1)}, f32[4,2,8,8,128]{4,3,2,1,0:T(8,128)S(1)}, f32[32,8,128]{2,1,0:T(8,128)S(1)}, f32[8,128]{1,0:T(8,128)S(1)}) custom-call(f32[6,4,8,8,128]{4,3,2,1,0:T(8,128)S(1)} %copy-done.1, f32[4,8,8,128]{3,2,1,0:T(8,128)S(1)} %copy-done.7, f32[4,8,8,128]{3,2,1,0:T(8,128)S(1)} %copy-done.5, ...), custom_call_target="tpu_custom_call" | custom-call | tf_op jit(solution)/shard_map/pallas_call | solution.py:505
  69.9 14.5 %all_to_all.15.parts = f32[32,8,128]{2,1,0:T(8,128)S(1)} all-to-all(f32[32,8,128]{2,1,0:T(8,128)S(1)} %get-tuple-element.37), channel_id=1, replica_groups=mesh['member'=1,'gx'=4,'gy'=8] {'gx','gy'}, dimensions={0} | all-to-all | bytes 262144 | tf_op jit(solution)/shard_map/all_to_all | solution.py:522
  84.4 1.9 %shard_map.68 = f32[4,2,8,8,128]{4,3,2,1,0:T(8,128)} custom-call(f32[4,2,8,8,128]{4,3,2,1,0:T(8,128)S(1)} %copy-done.3, f32[4,2,8,8,128]{4,3,2,1,0:T(8,128)S(1)} %get-tuple-element.26.residual, f32[4,2,8,8,128]{4,3,2,1,0:T(8,128)S(1)} %get-tuple-element.35.second, f32[4,2,8,8,128]{4,3,2,1,0:T(8,128)S(1)} %get-tuple-element.36.third, ...), custom_call_target="tpu_custom_call" | custom-call | tf_op jit(solution)/shard_map/pallas_call | solution.py:505
  (27 shorter events, 0.2 us)
Async XLA Ops:
  0.0 1.1 %copy-start = (f32[6,4,8,8,128]{4,3,2,1,0:T(8,128)S(1)}, f32[6,4,8,8,128]{4,3,2,1,0:T(8,128)}, u32[]{:S(2)}) copy-start(f32[6,4,8,8,128]{4,3,2,1,0:T(8,128)} %couplings.5) | copy-start | bytes 2359300
  1.1 0.9 %copy-start.2 = (f32[4,2,8,8,128]{4,3,2,1,0:T(8,128)S(1)}, f32[4,2,8,8,128]{4,3,2,1,0:T(8,128)}, u32[]{:S(2)}) copy-start(f32[4,2,8,8,128]{4,3,2,1,0:T(8,128)} %guess.7) | copy-start | bytes 786436
  2.1 0.9 %copy-start.4 = (f32[4,8,8,128]{3,2,1,0:T(8,128)S(1)}, f32[4,8,8,128]{3,2,1,0:T(8,128)}, u32[]{:S(2)}) copy-start(f32[4,8,8,128]{3,2,1,0:T(8,128)} %wells.7) | copy-start | bytes 393220
  3.0 0.9 %copy-start.6 = (f32[4,8,8,128]{3,2,1,0:T(8,128)S(1)}, f32[4,8,8,128]{3,2,1,0:T(8,128)}, u32[]{:S(2)}) copy-start(f32[4,8,8,128]{3,2,1,0:T(8,128)} %diagonal.5) | copy-start | bytes 393220
  3.9 0.9 %copy-start.8 = (f32[4,2,8,8,128]{4,3,2,1,0:T(8,128)S(1)}, f32[4,2,8,8,128]{4,3,2,1,0:T(8,128)}, u32[]{:S(2)}) copy-start(f32[4,2,8,8,128]{4,3,2,1,0:T(8,128)} %right.3) | copy-start | bytes 786436
  4.8 0.8 copy-start.10
  5.9 10.7 %collective-permute-start.1 = (f32[58,8,128]{2,1,0:T(8,128)S(1)}, f32[58,8,128]{2,1,0:T(8,128)S(1)}, u32[]{:S(2)}, u32[]{:S(2)}) collective-permute-start(f32[58,8,128]{2,1,0:T(8,128)S(1)} %get-tuple-element.23), channel_id=1, source_target_pairs={{8,0},{16,8},{24,16},{9,1},{17,9},{25,17},{10,2},{18,10},{26,18},{... | collective-permute-start | bytes 712712 | tf_op jit(solution)/shard_map/ppermute | solution.py:518
  7.3 11.1 %collective-permute-start = (f32[58,8,128]{2,0,1:T(8,128)S(1)}, f32[58,8,128]{2,0,1:T(8,128)S(1)}, u32[]{:S(2)}, u32[]{:S(2)}) collective-permute-start(f32[58,8,128]{2,0,1:T(8,128)S(1)} %copy.7), channel_id=1, source_target_pairs={{0,8},{8,16},{16,24},{1,9},{9,17},{17,25},{2,10},{10,18},{18,26},{... | collective-permute-start | bytes 712712 | tf_op jit(solution)/shard_map/ppermute | solution.py:518
  18.9 2.9 %copy-start.3 = (f32[4,2,8,8,128]{4,3,2,1,0:T(8,128)S(1)}, f32[4,2,8,8,128]{4,3,2,1,0:T(8,128)}, u32[]{:S(2)}) copy-start(f32[4,2,8,8,128]{4,3,2,1,0:T(8,128)} %guess.7) | copy-start | bytes 786436
  18.9 2.8 %copy-start.5 = (f32[4,8,8,128]{3,2,1,0:T(8,128)S(1)}, f32[4,8,8,128]{3,2,1,0:T(8,128)}, u32[]{:S(2)}) copy-start(f32[4,8,8,128]{3,2,1,0:T(8,128)} %wells.7) | copy-start | bytes 393220
  18.9 2.8 %copy-start.11 = (s32[8,8,128]{2,1,0:T(8,128)S(1)}, s32[8,8,128]{2,1,0:T(8,128)}, u32[]{:S(2)}) copy-start(s32[8,8,128]{2,1,0:T(8,128)} %ids.7) | copy-start | bytes 98308
  19.0 22.2 %copy-start.1 = (f32[6,4,8,8,128]{4,3,2,1,0:T(8,128)S(1)}, f32[6,4,8,8,128]{4,3,2,1,0:T(8,128)}, u32[]{:S(2)}) copy-start(f32[6,4,8,8,128]{4,3,2,1,0:T(8,128)} %couplings.5) | copy-start | bytes 2359300
  19.0 22.2 %collective-permute-start.2 = (f32[63,8,128]{2,1,0:T(8,128)S(1)}, f32[63,8,128]{2,1,0:T(8,128)S(1)}, u32[]{:S(2)}, u32[]{:S(2)}) collective-permute-start(f32[63,8,128]{2,1,0:T(8,128)S(1)} %pad_maximum_fusion), channel_id=1, source_target_pairs={{0,1},{1,2},{2,3},{3,4},{4,5},{5,6},{6,7},{8,9},{9,10},{10,11},{11... | collective-permute-start | bytes 774152 | tf_op jit(solution)/shard_map/ppermute | solution.py:518
  20.5 20.7 %collective-permute-start.3 = (f32[63,8,128]{2,1,0:T(8,128)S(1)}, f32[63,8,128]{2,1,0:T(8,128)S(1)}, u32[]{:S(2)}, u32[]{:S(2)}) collective-permute-start(f32[63,8,128]{2,1,0:T(8,128)S(1)} %pad_maximum_fusion.1), channel_id=1, source_target_pairs={{1,0},{2,1},{3,2},{4,3},{5,4},{6,5},{7,6},{9,8},{10,9},{11,10},{12... | collective-permute-start | bytes 774152 | tf_op jit(solution)/shard_map/ppermute | solution.py:518
  24.0 17.1 %all-to-all-start = ((f32[32,2,128]{2,1,0:T(2,128)}), f32[32,2,128]{2,1,0:T(2,128)S(1)}, u32[]{:S(2)}, u32[]{:S(2)}) async-start(f32[32,2,128]{2,1,0:T(2,128)} %shard_map.65), calls=%async_computation | async-start | bytes 65536 | tf_op jit(solution)/shard_map/all_to_all | solution.py:522
  33.9 7.3 %copy-start.7 = (f32[4,8,8,128]{3,2,1,0:T(8,128)S(1)}, f32[4,8,8,128]{3,2,1,0:T(8,128)}, u32[]{:S(2)}) copy-start(f32[4,8,8,128]{3,2,1,0:T(8,128)} %diagonal.5) | copy-start | bytes 393220
  33.9 7.3 %copy-start.9 = (f32[4,2,8,8,128]{4,3,2,1,0:T(8,128)S(1)}, f32[4,2,8,8,128]{4,3,2,1,0:T(8,128)}, u32[]{:S(2)}) copy-start(f32[4,2,8,8,128]{4,3,2,1,0:T(8,128)} %right.3) | copy-start | bytes 786436
  46.8 6.4 %collective-permute-start.4 = (f32[16,8,128]{2,0,1:T(8,128)}, f32[16,8,128]{2,0,1:T(8,128)S(1)}, u32[]{:S(2)}, u32[]{:S(2)}) collective-permute-start(f32[16,8,128]{2,0,1:T(8,128)} %copy.14), channel_id=1, source_target_pairs={{0,8},{8,16},{16,24},{1,9},{9,17},{17,25},{2,10},{10,18},{18,26},{... | collective-permute-start | bytes 196616 | tf_op jit(solution)/shard_map/ppermute | solution.py:518
  49.3 16.0 %all-to-all-start.1 = ((f32[32,8,128]{2,1,0:T(8,128)}), f32[32,8,128]{2,1,0:T(8,128)S(1)}, u32[]{:S(2)}, u32[]{:S(2)}) async-start(f32[32,8,128]{2,1,0:T(8,128)} %get-tuple-element.33), calls=%async_computation.1 | async-start | bytes 262144 | tf_op jit(solution)/shard_map/all_to_all | solution.py:522
  51.9 7.0 %collective-permute-start.5 = (f32[16,8,128]{2,1,0:T(8,128)S(1)}, f32[16,8,128]{2,1,0:T(8,128)S(1)}, u32[]{:S(2)}, u32[]{:S(2)}) collective-permute-start(f32[16,8,128]{2,1,0:T(8,128)S(1)} %get-tuple-element.28), channel_id=1, source_target_pairs={{8,0},{16,8},{24,16},{9,1},{17,9},{25,17},{10,2},{18,10},{26,18},{... | collective-permute-start | bytes 196616 | tf_op jit(solution)/shard_map/ppermute | solution.py:518
  53.2 5.8 %copy-start.12 = (f32[16,8,128]{2,0,1:T(8,128)}, f32[16,8,128]{2,0,1:T(8,128)S(1)}, u32[]{:S(2)}) copy-start(f32[16,8,128]{2,0,1:T(8,128)S(1)} %collective-permute-done.4) | copy-start | bytes 196612
  58.9 3.0 %collective-permute-start.6 = (f32[18,8,128]{2,1,0:T(8,128)S(1)}, f32[18,8,128]{2,1,0:T(8,128)S(1)}, u32[]{:S(2)}, u32[]{:S(2)}) collective-permute-start(f32[18,8,128]{2,1,0:T(8,128)S(1)} %pad_maximum_fusion.2), channel_id=1, source_target_pairs={{0,1},{1,2},{2,3},{3,4},{4,5},{5,6},{6,7},{8,9},{9,10},{10,11},{11... | collective-permute-start | bytes 221192 | tf_op jit(solution)/shard_map/ppermute | solution.py:518
  60.6 1.3 %copy-start.13 = (f32[16,8,128]{2,0,1:T(8,128)S(1)}, f32[16,8,128]{2,0,1:T(8,128)}, u32[]{:S(2)}) copy-start(f32[16,8,128]{2,0,1:T(8,128)} %copy-done.12) | copy-start | bytes 196612
  60.6 4.6 %collective-permute-start.7 = (f32[18,8,128]{2,1,0:T(8,128)S(1)}, f32[18,8,128]{2,1,0:T(8,128)S(1)}, u32[]{:S(2)}, u32[]{:S(2)}) collective-permute-start(f32[18,8,128]{2,1,0:T(8,128)S(1)} %pad_maximum_fusion.3), channel_id=1, source_target_pairs={{1,0},{2,1},{3,2},{4,3},{5,4},{6,5},{7,6},{9,8},{10,9},{11,10},{12... | collective-permute-start | bytes 221192 | tf_op jit(solution)/shard_map/ppermute | solution.py:518

commit v3 on v2

--- a/solution.py
+++ b/solution.py
@@ -1,5 +1,3 @@
-import functools
-
 import jax
 import jax.numpy as jnp
 from jax import lax
@@ -11,9 +9,10 @@
 RHS = 4
 LANES = 128
 LAT_UP, LAT_DOWN, RISE, FALL, DIAGONAL = 4, 8, 12, 16, 20
-WELL_EQ, WELL_ID, GUESS, RIGHT = 24, 26, 27, 35
-BACK_IN, BACK_EQ, BACK_ID, BACK_GUESS = 43, 47, 49, 50
-FACE_PLANES = 58
+WELL_EQ, WELL_ID, GUESS, REST = 24, 26, 27, 35
+BACK_IN, BACK_EQ, BACK_ID = 43, 47, 49
+FACE_PLANES = 50
+CORNER_PLANES = 5
 CORNER_ROWS = 19
 SIDE_IN, SIDE_EQ, SIDE_ID, SIDE_GUESS = 4, 8, 10, 11
 
@@ -66,7 +65,7 @@
     return result, outgoing
 
 
-def face_stencil(face, first, second, low_end, high_end, behind, entering):
+def face_stencil(face, first, second, behind):
     def planes(start):
         return lambda e: face[start + e]
 
@@ -77,11 +76,20 @@
     fall = product(planes(FALL), first, second)
     row = iota(first.shape, 0)
     for b in range(2):
-        total = result[b] + behind[b] + entering[b]
-        total = total + jnp.where(row == 0, low_end[b], roll_up(up[b], 0))
-        total = total + jnp.where(row == row.shape[0] - 1, high_end[b], roll_down(down[b], 0))
-        result[b] = total + layer_moves(rise[b], fall[b])
+        total = result[b] + behind[b] + layer_moves(rise[b], fall[b])
+        total = total + jnp.where(row == 0, 0.0, roll_up(up[b], 0))
+        result[b] = total + jnp.where(row == row.shape[0] - 1, 0.0, roll_down(down[b], 0))
     return result
+
+
+def face_entries(low_end, high_end, entering):
+    row = iota(entering[0].shape, 0)
+    return [
+        entering[b]
+        + jnp.where(row == 0, low_end[b], 0.0)
+        + jnp.where(row == row.shape[0] - 1, high_end[b], 0.0)
+        for b in range(2)
+    ]
 
 
 def spread(totals, ids):
@@ -137,27 +145,34 @@
 
 
 def segment_rows(ids, values, scratch):
-    masks_at = [ids[x] for x in range(ids.shape[0])]
-    fields = [[value[x] for x in range(ids.shape[0])] for value in values]
-    scratch[:, WELLS:, :] = jnp.zeros_like(scratch[:, WELLS:, :])
-    for w in range(WELLS):
-        masks = [at == w for at in masks_at]
-        for number, field in enumerate(fields):
-            total = jnp.where(masks[0], field[0], 0.0)
-            for x in range(1, len(masks)):
-                total = total + jnp.where(masks[x], field[x], 0.0)
-            scratch[number, w : w + 1, :] = jnp.sum(total, axis=0, keepdims=True)
-    ones = jnp.ones((8, LANES), jnp.float32)
+    scratch[...] = jnp.zeros_like(scratch)
+    count, depth = values.shape[0], ids.shape[0]
+
+    def smallest(planes):
+        least = planes[0]
+        for plane in planes[1:]:
+            least = jnp.minimum(least, plane)
+        return jnp.min(least)
+
+    def one_well(well):
+        planes = [ids[x].astype(jnp.float32) for x in range(depth)]
+        masks = [plane == well for plane in planes]
+        at = well.astype(jnp.int32)
+        for number in range(count):
+            total = jnp.where(masks[0], values[number, 0], 0.0)
+            for x in range(1, depth):
+                total = total + jnp.where(masks[x], values[number, x], 0.0)
+            scratch[number, pl.ds(at, 1), :] = jnp.sum(total, axis=0, keepdims=True)
+        return smallest([jnp.where(plane > well, plane, float(WELLS)) for plane in planes])
+
+    first = smallest([ids[x].astype(jnp.float32) for x in range(depth)])
+    lax.while_loop(lambda well: well < WELLS, one_well, first)
     rows = []
-    for number in range(len(fields)):
-        summed = lax.dot_general(
-            ones,
-            scratch[number],
-            (((1,), (1,)), ((), ())),
-            precision=lax.Precision.HIGHEST,
-            preferred_element_type=jnp.float32,
-        )
-        rows.append(summed[0:1, :])
+    for number in range(count):
+        summed = jnp.sum(scratch[number], axis=1, keepdims=True)
+        shape = scratch.shape[1:]
+        on_lanes = jnp.where(iota(shape, 0) == iota(shape, 1), summed, 0.0)
+        rows.append(jnp.sum(on_lanes, axis=0, keepdims=True))
     return rows
 
 
@@ -186,8 +201,27 @@
 
 
 def pack_kernel(
-    couplings, diagonal, wells, ids, right, guess, x_low, x_high, y_low, y_high
+    couplings_in, diagonal_in, wells_in, ids_in, right_in, guess_in,
+    x_low, x_high, y_low, y_high,
+    couplings, diagonal, wells, ids, right, guess, arrived,
 ):
+    copies = [
+        pltpu.make_async_copy(source, held, arrived.at[n])
+        for n, (source, held) in enumerate(
+            (
+                (couplings_in, couplings),
+                (diagonal_in, diagonal),
+                (wells_in, wells),
+                (ids_in, ids),
+                (right_in, right),
+                (guess_in, guess),
+            )
+        )
+    ]
+    for copy in copies:
+        copy.start()
+    for copy in copies:
+        copy.wait()
     last = guess.shape[2] - 1
     for axis, packs in ((0, (x_low, x_high)), (1, (y_low, y_high))):
         for end, pack in enumerate(packs):
@@ -215,22 +249,46 @@
             pack[WELL_ID] = cut(ids).astype(jnp.float32)
             pack[BACK_ID] = cut(ids, at=behind).astype(jnp.float32)
             for k in range(RHS):
-                for a in range(2):
-                    pack[GUESS + 2 * k + a] = cut(guess, k, a)
-                    pack[RIGHT + 2 * k + a] = cut(right, k, a)
+                here = [cut(guess, k, a) for a in range(2)]
                 entering = product(
-                    lambda e: cut(couplings, inward, e, at=behind),
+                    lambda e: pack[BACK_IN + e],
                     cut(guess, k, 0, at=behind),
                     cut(guess, k, 1, at=behind),
                 )
-                pack[BACK_GUESS + 2 * k] = entering[0]
-                pack[BACK_GUESS + 2 * k + 1] = entering[1]
-
-
-def guess_kernel(wells, ids, guess, part, scratch):
-    values = [wells[0] * guess[k, 0] + wells[1] * guess[k, 1] for k in range(RHS)]
-    values.append(wells[0] * wells[2] + wells[1] * wells[3])
-    values.append(wells[2] * wells[2] + wells[3] * wells[3])
+                local = face_stencil(pack, here[0], here[1], entering)
+                for a in range(2):
+                    pack[GUESS + 2 * k + a] = here[a]
+                    pack[REST + 2 * k + a] = cut(right, k, a) - local[a]
+
+
+def corner_kernel(y_low, y_high, fxl, fxh, low_out, high_out):
+    last = fxl.shape[1] - 1
+    for own, out, at, side in ((y_low, low_out, 0, LAT_DOWN), (y_high, high_out, last, LAT_UP)):
+        for n in range(FACE_PLANES):
+            out[n] = own[n]
+        row = FACE_PLANES * 8
+        out[FACE_PLANES + CORNER_PLANES - 1] = jnp.zeros(out.shape[1:], jnp.float32)
+        for face in (fxl, fxh):
+            for n in (*range(4), *range(side, side + 4), *range(WELL_EQ, REST)):
+                out[row // 8, row % 8 : row % 8 + 1, :] = face[n, at : at + 1, :]
+                row += 1
+
+
+def image_corner_kernel(y_low, y_high, gxl, gxh, low_out, high_out):
+    last = gxl.shape[1] - 1
+    for own, out, at in ((y_low, low_out, 0), (y_high, high_out, last)):
+        for n in range(16):
+            out[n] = own[n]
+        for x_end, face in enumerate((gxl, gxh)):
+            for n in range(8):
+                out[16 + x_end, n : n + 1, :] = face[n, at : at + 1, :]
+
+
+def guess_kernel(wells, ids, guess, part, values, scratch):
+    for k in range(RHS):
+        values[k] = wells[0] * guess[k, 0] + wells[1] * guess[k, 1]
+    values[4] = wells[0] * wells[2] + wells[1] * wells[3]
+    values[5] = wells[2] * wells[2] + wells[3] * wells[3]
     rows = segment_rows(ids, values, scratch)
     table = pack_rows(rows, jnp.zeros((8, LANES), jnp.float32))
     part[...] = jnp.broadcast_to(table[None, :2], part.shape)
@@ -238,8 +296,7 @@
 
 def residual_kernel(
     couplings, diagonal, wells, ids, right, guess, fxl, fxh, fyl, fyh, parts,
-    residual, image, residual_faces, x_low, x_high, y_low, y_high, part, small,
-    scratch,
+    residual, image, residual_faces, x_low, x_high, y_low, y_high, small,
 ):
     faces = (fxl, fxh, fyl, fyh)
     totals = jnp.sum(parts[...], axis=0)
@@ -247,7 +304,6 @@
     all_ids = ids[...]
     face_ids = [as_ids(face[WELL_ID]) for face in faces]
     last = guess.shape[2] - 1
-    table = jnp.zeros((8, LANES), jnp.float32)
     for k in range(RHS):
         s_row = unpack_row(totals, k)
         first, second = guess[k, 0], guess[k, 1]
@@ -273,18 +329,10 @@
         incoming = []
         for f in range(4):
             face = faces[f]
-            there = face_stencil(
-                face,
-                face[GUESS + 2 * k],
-                face[GUESS + 2 * k + 1],
-                ends[(f, 0)],
-                ends[(f, 1)],
-                [face[BACK_GUESS + 2 * k + b] for b in range(2)],
-                outgoing[f],
-            )
+            there = face_entries(ends[(f, 0)], ends[(f, 1)], outgoing[f])
             face_wells = spread(s_row, face_ids[f])
             outer = [
-                face[RIGHT + 2 * k + a] - there[a] - face[WELL_EQ + a] * face_wells
+                face[REST + 2 * k + a] - there[a] - face[WELL_EQ + a] * face_wells
                 for a in range(2)
             ]
             for a in range(2):
@@ -301,20 +349,25 @@
             y_low[8 + 2 * k + a] = result[a][:, 1, :]
             y_high[2 * k + a] = result[a][:, last, :]
             y_high[8 + 2 * k + a] = result[a][:, last - 1, :]
+    small[...] = jnp.concatenate(
+        [unpack_row(totals, 4), unpack_row(totals, 5), jnp.zeros((6, LANES), jnp.float32)], axis=0
+    )
+
+
+def moments_kernel(wells, ids, residual, image, part, values, scratch):
+    table = jnp.zeros((8, LANES), jnp.float32)
+    for k in range(RHS):
+        now = [residual[k, a] for a in range(2)]
+        result = [image[k, a] for a in range(2)]
+        for n, field in enumerate((now, result)):
+            values[4 * n + k] = wells[0] * field[0] + wells[1] * field[1]
+            values[8 + 4 * n + k] = wells[2] * field[0] + wells[3] * field[1]
         table = put(6, k, full_sum(now[0] * now[0] + now[1] * now[1]), table)
         table = put(6, 4 + k, full_sum(now[0] * result[0] + now[1] * result[1]), table)
         table = put(6, 8 + k, full_sum(result[0] * result[0] + result[1] * result[1]), table)
-    values = []
-    for side in (0, 2):
-        for field in (residual, image):
-            for k in range(RHS):
-                values.append(wells[side] * field[k, 0] + wells[side + 1] * field[k, 1])
-    rows = segment_rows(all_ids, values, scratch)
+    rows = segment_rows(ids, values, scratch)
     table = pack_rows(rows, table)
     part[...] = jnp.broadcast_to(table[None], part.shape)
-    small[...] = jnp.concatenate(
-        [unpack_row(totals, 4), unpack_row(totals, 5), jnp.zeros((6, LANES), jnp.float32)], axis=0
-    )
 
 
 def first_step(totals, small, k):
@@ -393,14 +446,12 @@
         incoming = []
         for f in range(4):
             face = faces[f]
-            there = face_stencil(
-                face, face_now[f][0], face_now[f][1], ends[(f, 0)], ends[(f, 1)], back_in[f],
-                outgoing[f],
-            )
+            there = face_stencil(face, face_now[f][0], face_now[f][1], back_in[f])
+            over = face_entries(ends[(f, 0)], ends[(f, 1)], outgoing[f])
             here = spread(s_image, face_ids[f])
             outer = []
             for a in range(2):
-                twice = there[a] + face[WELL_EQ + a] * here
+                twice = there[a] + over[a] + face[WELL_EQ + a] * here
                 base = (face_now[f][a] - height * residual_faces[f, 2 * k + a]) * scale
                 outer.append((twice - height * face_now[f][a]) * scale - shift * base)
             incoming.append(product(lambda e, f=f: faces[f][e], *outer))
@@ -417,7 +468,7 @@
                 dot = full_sum(fields[i][0] * fields[j][0] + fields[i][1] * fields[j][1])
                 table = put(4, 4 * number + k, dot, table)
                 number += 1
-    rows = segment_rows(all_ids, [values_scratch[n] for n in range(12)], scratch)
+    rows = segment_rows(ids, values_scratch, scratch)
     table = pack_rows(rows, table)
     part[...] = jnp.broadcast_to(table[None], part.shape)
 
@@ -500,16 +551,24 @@
             )
 
 
-def call(kernel, shapes, arguments, scratch=()):
+def call(kernel, shapes, arguments, scratch=(), own_copies=False, cost=0):
     whole = pl.BlockSpec(memory_space=pltpu.VMEM)
+    far = pl.BlockSpec(memory_space=pl.ANY)
     return pl.pallas_call(
         kernel,
         out_shape=[jax.ShapeDtypeStruct(shape, jnp.float32) for shape in shapes],
-        in_specs=[whole] * len(arguments),
+        in_specs=[far if own_copies else whole] * len(arguments),
         out_specs=[whole] * len(shapes),
-        scratch_shapes=[pltpu.VMEM(shape, jnp.float32) for shape in scratch],
+        scratch_shapes=list(scratch),
         compiler_params=pltpu.CompilerParams(vmem_limit_bytes=24 << 20),
+        cost_estimate=pl.CostEstimate(flops=cost, bytes_accessed=cost, transcendentals=0)
+        if cost
+        else None,
     )(*arguments)
+
+
+def held(*shape):
+    return pltpu.VMEM(shape, jnp.float32)
 
 
 def from_behind(value, axis, steps):
@@ -522,62 +581,67 @@
     return lax.all_to_all(part, ("gx", "gy"), 0, 0, tiled=True)
 
 
-def corner_planes(rows):
-    stacked = jnp.concatenate(rows, axis=0)
-    spare = -stacked.shape[0] % 8
-    if spare:
-        stacked = jnp.pad(stacked, ((0, spare), (0, 0)))
-    return stacked.reshape(-1, 8, LANES)
-
-
 def body(couplings, diagonal, wells, ids, right, guess):
     devices = lax.axis_size("gx") * lax.axis_size("gy")
     plane = (8, LANES)
     field = guess.shape
-    last = guess.shape[2] - 1
-
-    packs = call(
+    block = guess.shape[2:]
+    arguments = (couplings, diagonal, wells, ids, right, guess)
+
+    x_low, x_high, y_low, y_high = call(
         pack_kernel,
         [(FACE_PLANES,) + plane] * 4,
-        (couplings, diagonal, wells, ids, right, guess),
-    )
-    fxl = from_behind(packs[1], "gx", 1)
-    fxh = from_behind(packs[0], "gx", -1)
-    (part,) = call(guess_kernel, [(devices, 2, LANES)], (wells, ids, guess), [(6, LANES, LANES)])
+        arguments,
+        [pltpu.VMEM(argument.shape, argument.dtype) for argument in arguments]
+        + [pltpu.SemaphoreType.DMA((len(arguments),))],
+        own_copies=True,
+    )
+    fxl = from_behind(x_high, "gx", 1)
+    fxh = from_behind(x_low, "gx", -1)
+    (part,) = call(
+        guess_kernel,
+        [(devices, 2, LANES)],
+        (wells, ids, guess),
+        [held(6, *block), held(6, WELLS, LANES)],
+        cost=4 << 20,
+    )
     parts = exchanged(part)
-    packed = []
-    for pack, at, side in ((packs[2], 0, LAT_DOWN), (packs[3], last, LAT_UP)):
-        rows = []
-        for face in (fxl, fxh):
-            rows += [face[0:4, at], face[side : side + 4, at], face[WELL_EQ : GUESS + 8, at]]
-        packed.append(jnp.concatenate([pack, corner_planes(rows)], axis=0))
-    fyl = from_behind(packed[1], "gy", 1)
-    fyh = from_behind(packed[0], "gy", -1)
-
-    residual, image, residual_faces, x_low, x_high, y_low, y_high, part, small = call(
+    y_low, y_high = call(
+        corner_kernel,
+        [(FACE_PLANES + CORNER_PLANES,) + plane] * 2,
+        (y_low, y_high, fxl, fxh),
+    )
+    fyl = from_behind(y_high, "gy", 1)
+    fyh = from_behind(y_low, "gy", -1)
+
+    faces = (fxl, fxh, fyl, fyh)
+    residual, image, residual_faces, x_low, x_high, y_low, y_high, small = call(
         residual_kernel,
-        [field, field, (4, 8) + plane]
-        + [(16,) + plane] * 4
-        + [(devices, 8, LANES), (8, LANES)],
-        (couplings, diagonal, wells, ids, right, guess, fxl, fxh, fyl, fyh, parts),
-        [(16, LANES, LANES)],
+        [field, field, (4, 8) + plane] + [(16,) + plane] * 4 + [(8, LANES)],
+        arguments + faces + (parts,),
     )
     gxl = from_behind(x_high, "gx", 1)
     gxh = from_behind(x_low, "gx", -1)
+    (part,) = call(
+        moments_kernel,
+        [(devices, 8, LANES)],
+        (wells, ids, residual, image),
+        [held(16, *block), held(16, WELLS, LANES)],
+        cost=4 << 20,
+    )
     parts = exchanged(part)
-    packed = []
-    for pack, at in ((y_low, 0), (y_high, last)):
-        rows = [face[0:8, at] for face in (gxl, gxh)]
-        packed.append(jnp.concatenate([pack, corner_planes(rows)], axis=0))
-    gyl = from_behind(packed[1], "gy", 1)
-    gyh = from_behind(packed[0], "gy", -1)
+    y_low, y_high = call(
+        image_corner_kernel, [(18,) + plane] * 2, (y_low, y_high, gxl, gxh)
+    )
+    gyl = from_behind(y_high, "gy", 1)
+    gyh = from_behind(y_low, "gy", -1)
 
     second, third, part, totals = call(
         krylov_kernel,
         [field, field, (devices, 8, LANES), (8, LANES)],
-        (couplings, diagonal, wells, ids, fxl, fxh, fyl, fyh, gxl, gxh, gyl, gyh)
+        (couplings, diagonal, wells, ids) + faces + (gxl, gxh, gyl, gyh)
         + (residual, image, residual_faces, parts, small),
-        [(12, LANES, LANES), (12,) + guess.shape[2:]],
+        [held(12, WELLS, LANES), held(12, *block)],
     )
     parts = exchanged(part)
     (result,) = call(

time: 87 us -> 82.1 us (0.944)
  blocking collectives: 14.5 us -> 29.2 us
  starting transfers between devices: 28.8 us -> 19.1 us
  waiting for transfers between devices: 21.5 us -> 15.6 us
  Pallas kernels: 14.1 us -> 11.7 us
  local copies, waits for them, and re-layouts: 7 us -> 5.63 us
    all_to_all x1 -> x2, blocking collectives: 14.5 us -> 29.2 us  [exchanged(): return lax.all_to_all(part, ('gx', 'gy'), 0, 0, tiled=True)]
    all_to_all x2 -> x1, starting transfers between devices: 12.5 us -> 2.58 us  [exchanged(): return lax.all_to_all(part, ('gx', 'gy'), 0, 0, tiled=True)]
    all_to_all x2 -> x1, waiting for transfers between devices: 7.08 us -> 0.01 us  [exchanged(): return lax.all_to_all(part, ('gx', 'gy'), 0, 0, tiled=True)]
    pallas_call x5 -> x8, Pallas kernels: 14.1 us -> 11.7 us  [call(): pl.pallas_call(kernel, out_shape=[jax.ShapeDtypeStruct(shape, jnp.float32...]
    ppermute x8, waiting for transfers between devices: 14.4 us -> 15.6 us  [from_behind(): lax.ppermute(value, axis, [(source, source + steps) for source in range(l...]
    unnamed x28 -> x24, local copies, waits for them, and re-layouts: 5.64 us -> 5.63 us
  transfers between devices with their start and end apart: 10 -> 9, of which waited for: 5 -> 5; matrix products, arithmetic and copies ran while one was open for 0% -> 0% of each run, Pallas kernels for 3% -> 2%
where the time goes in v3:
time: 82.1 us; the launch traced here: 81.5 us
  blocking collectives  29.2 us (36%)
  starting transfers between devices  19.1 us (23%)
  waiting for transfers between devices  15.6 us (19%)
  Pallas kernels  11.7 us (14%)
  local copies, waits for them, and re-layouts  5.63 us (7%)
    all_to_all x2, blocking collectives, exchanged(): return lax.all_to_all(part, ('gx', 'gy'), 0, 0, tiled=True)  29.2 us
    ppermute x8, starting transfers between devices, from_behind(): lax.ppermute(value, axis, [(source, source + steps) for source in range(l...  16.6 us
    ppermute x8, waiting for transfers between devices, from_behind(): lax.ppermute(value, axis, [(source, source + steps) for source in range(l...  15.6 us
    pallas_call x8, Pallas kernels, call(): pl.pallas_call(kernel, out_shape=[jax.ShapeDtypeStruct(shape, jnp.float32...  11.7 us
    unnamed x24, local copies, waits for them, and re-layouts  5.63 us
    all_to_all x1, starting transfers between devices, exchanged(): return lax.all_to_all(part, ('gx', 'gy'), 0, 0, tiled=True)  2.58 us
  transfers between devices with their start and end apart: 9, of which 5 were waited for; matrix products, arithmetic and copies ran while one was open for 0% of the time, Pallas kernels for 2%

profile of v3, /device:TPU:0, one launch (start us, length us, event | category | flops | bytes accessed | tf_op | source)
XLA Modules:
  0.0 81.5 jit_solution(12556100831420779379)
XLA Ops:
  0.0 1.1 %copy-done = f32[6,4,8,8,128]{4,3,2,1,0:T(8,128)S(1)} copy-done((f32[6,4,8,8,128]{4,3,2,1,0:T(8,128)S(1)}, f32[6,4,8,8,128]{4,3,2,1,0:T(8,128)}, u32[]{:S(2)}) %copy-start) | copy-done | bytes 786456
  1.1 0.0 copy-start.2
  1.1 0.9 %copy-done.2 = f32[4,2,8,8,128]{4,3,2,1,0:T(8,128)S(1)} copy-done((f32[4,2,8,8,128]{4,3,2,1,0:T(8,128)S(1)}, f32[4,2,8,8,128]{4,3,2,1,0:T(8,128)}, u32[]{:S(2)}) %copy-start.2) | copy-done | bytes 262168
  2.1 0.0 copy-start.4
  2.1 0.9 %copy-done.4 = f32[4,8,8,128]{3,2,1,0:T(8,128)S(1)} copy-done((f32[4,8,8,128]{3,2,1,0:T(8,128)S(1)}, f32[4,8,8,128]{3,2,1,0:T(8,128)}, u32[]{:S(2)}) %copy-start.4) | copy-done | bytes 131096
  3.0 0.0 copy-start.6
  3.0 0.9 %copy-done.6 = f32[4,8,8,128]{3,2,1,0:T(8,128)S(1)} copy-done((f32[4,8,8,128]{3,2,1,0:T(8,128)S(1)}, f32[4,8,8,128]{3,2,1,0:T(8,128)}, u32[]{:S(2)}) %copy-start.6) | copy-done | bytes 131096
  3.9 0.0 copy-start.8
  3.9 0.9 %copy-done.8 = f32[4,2,8,8,128]{4,3,2,1,0:T(8,128)S(1)} copy-done((f32[4,2,8,8,128]{4,3,2,1,0:T(8,128)S(1)}, f32[4,2,8,8,128]{4,3,2,1,0:T(8,128)}, u32[]{:S(2)}) %copy-start.8) | copy-done | bytes 262168
  4.8 0.0 copy-start.10
  4.8 0.8 copy-done.10
  5.6 0.9 %shard_map.64 = (f32[50,8,128]{2,1,0:T(8,128)S(1)}, f32[50,8,128]{2,1,0:T(8,128)S(1)}, f32[50,8,128]{2,1,0:T(8,128)S(1)}, f32[50,8,128]{2,1,0:T(8,128)S(1)}) custom-call(f32[6,4,8,8,128]{4,3,2,1,0:T(8,128)S(1)} %copy-done, f32[4,8,8,128]{3,2,1,0:T(8,128)S(1)} %copy-done.6, f32[4,8,8,128]{3,2,1,0:T(8,128)S(1)} %copy-done.4, s32[8,8,128]{2,1,0:T(8,128)S(1)} %copy-done.10, ...), custom_call_target="tpu_custom_call" | custom-call | tf_op jit(solution)/shard_map/pallas_call | solution.py:557
  6.5 0.0 copy-start.1
  6.5 5.1 %collective-permute-start = (f32[50,8,128]{2,1,0:T(8,128)S(1)}, f32[50,8,128]{2,1,0:T(8,128)S(1)}, u32[]{:S(2)}, u32[]{:S(2)}) collective-permute-start(f32[50,8,128]{2,1,0:T(8,128)S(1)} %get-tuple-element.25), channel_id=1, source_target_pairs={{0,8},{8,16},{16,24},{1,9},{9,17},{17,25},{2,10},{10,18},{18,26},{... | collective-permute-start | bytes 614408 | tf_op jit(solution)/shard_map/ppermute | solution.py:577
  11.6 1.3 %collective-permute-start.1 = (f32[50,8,128]{2,1,0:T(8,128)S(1)}, f32[50,8,128]{2,1,0:T(8,128)S(1)}, u32[]{:S(2)}, u32[]{:S(2)}) collective-permute-start(f32[50,8,128]{2,1,0:T(8,128)S(1)} %get-tuple-element.26), channel_id=1, source_target_pairs={{8,0},{16,8},{24,16},{9,1},{17,9},{25,17},{10,2},{18,10},{26,18},{... | collective-permute-start | bytes 614408 | tf_op jit(solution)/shard_map/ppermute | solution.py:577
  12.9 3.0 %collective-permute-done.fxl = f32[50,8,128]{2,1,0:T(8,128)S(1)} collective-permute-done((f32[50,8,128]{2,1,0:T(8,128)S(1)}, f32[50,8,128]{2,1,0:T(8,128)S(1)}, u32[]{:S(2)}, u32[]{:S(2)}) %collective-permute-start) | collective-permute-done | bytes 204832 | tf_op jit(solution)/shard_map/ppermute | solution.py:577
  15.9 4.1 %collective-permute-done.1.fxh = f32[50,8,128]{2,1,0:T(8,128)S(1)} collective-permute-done((f32[50,8,128]{2,1,0:T(8,128)S(1)}, f32[50,8,128]{2,1,0:T(8,128)S(1)}, u32[]{:S(2)}, u32[]{:S(2)}) %collective-permute-start.1) | collective-permute-done | bytes 204832 | tf_op jit(solution)/shard_map/ppermute | solution.py:577
  20.0 0.1 shard_map.65
  20.1 1.3 %collective-permute-start.2 = (f32[55,8,128]{2,1,0:T(8,128)S(1)}, f32[55,8,128]{2,1,0:T(8,128)S(1)}, u32[]{:S(2)}, u32[]{:S(2)}) collective-permute-start(f32[55,8,128]{2,1,0:T(8,128)S(1)} %get-tuple-element.29), channel_id=1, source_target_pairs={{0,1},{1,2},{2,3},{3,4},{4,5},{5,6},{6,7},{8,9},{9,10},{10,11},{11... | collective-permute-start | bytes 675848 | tf_op jit(solution)/shard_map/ppermute | solution.py:577
  21.4 0.0 copy-start.9
  21.4 1.4 %collective-permute-start.3 = (f32[55,8,128]{2,1,0:T(8,128)S(1)}, f32[55,8,128]{2,1,0:T(8,128)S(1)}, u32[]{:S(2)}, u32[]{:S(2)}) collective-permute-start(f32[55,8,128]{2,1,0:T(8,128)S(1)} %get-tuple-element.30), channel_id=1, source_target_pairs={{1,0},{2,1},{3,2},{4,3},{5,4},{6,5},{7,6},{9,8},{10,9},{11,10},{12... | collective-permute-start | bytes 675848 | tf_op jit(solution)/shard_map/ppermute | solution.py:577
  22.8 0.0 copy-done.5
  22.9 0.0 copy-done.11
  22.9 0.0 copy-start.7
  22.9 1.5 %shard_map.66 = f32[32,2,128]{2,1,0:T(2,128)S(1)} custom-call(f32[4,8,8,128]{3,2,1,0:T(8,128)S(1)} %copy-done.5, s32[8,8,128]{2,1,0:T(8,128)S(1)} %copy-done.11, f32[4,2,8,8,128]{4,3,2,1,0:T(8,128)S(1)} %copy-done.2), custom_call_target="tpu_custom_call" | custom-call | flops 4194304 | bytes 4194304 | tf_op jit(solution)/shard_map/pallas_call | solution.py:557
  24.4 14.6 %all_to_all.15.parts = f32[32,2,128]{2,1,0:T(2,128)S(1)} all-to-all(f32[32,2,128]{2,1,0:T(2,128)S(1)} %shard_map.66), channel_id=1, replica_groups=mesh['member'=1,'gx'=4,'gy'=8] {'gx','gy'}, dimensions={0} | all-to-all | bytes 65536 | tf_op jit(solution)/shard_map/all_to_all | solution.py:581
  38.9 0.0 collective-permute-done.2.fyl
  38.9 0.0 collective-permute-done.3.fyh
  38.9 0.0 copy-done.1
  39.0 0.0 copy-done.9
  39.0 0.0 copy-done.7
  39.0 0.9 %shard_map.67 = (f32[4,2,8,8,128]{4,3,2,1,0:T(8,128)S(1)}, f32[4,2,8,8,128]{4,3,2,1,0:T(8,128)S(1)}, f32[4,8,8,128]{3,2,1,0:T(8,128)S(1)}, f32[16,8,128]{2,1,0:T...) custom-call(f32[6,4,8,8,128]{4,3,2,1,0:T(8,128)S(1)} %copy-done.1, ...), custom_call_target="tpu_custom_call" | custom-call | tf_op jit(solution)/shard_map/pallas_call | solution.py:557
  39.9 2.5 %shard_map.69 = f32[32,8,128]{2,1,0:T(8,128)} custom-call(f32[4,8,8,128]{3,2,1,0:T(8,128)S(1)} %copy-done.5, s32[8,8,128]{2,1,0:T(8,128)S(1)} %copy-done.11, f32[4,2,8,8,128]{4,3,2,1,0:T(8,128)S(1)} %get-tuple-element.31.residual, f32[4,2,8,8,128]{4,3,2,1,0:T(8,128)S(1)} %get-tuple-element.38.image), custom_call_target="tpu_custom_call" | custom-call | flops 4194304 | bytes 4194304 | tf_op jit(solution)/shard_map/pallas_call | solution.py:557
  42.4 2.6 %all-to-all-start.1 = ((f32[32,8,128]{2,1,0:T(8,128)}), f32[32,8,128]{2,1,0:T(8,128)S(1)}, u32[]{:S(2)}, u32[]{:S(2)}) async-start(f32[32,8,128]{2,1,0:T(8,128)} %shard_map.69), calls=%async_computation.1 | async-start | bytes 262144 | tf_op jit(solution)/shard_map/all_to_all | solution.py:581
  45.0 3.6 %collective-permute-start.4 = (f32[16,8,128]{2,1,0:T(8,128)S(1)}, f32[16,8,128]{2,1,0:T(8,128)S(1)}, u32[]{:S(2)}, u32[]{:S(2)}) collective-permute-start(f32[16,8,128]{2,1,0:T(8,128)S(1)} %get-tuple-element.32), channel_id=1, source_target_pairs={{0,8},{8,16},{16,24},{1,9},{9,17},{17,25},{2,10},{10,18},{18,26},{... | collective-permute-start | bytes 196616 | tf_op jit(solution)/shard_map/ppermute | solution.py:577
  48.6 1.3 %collective-permute-start.5 = (f32[16,8,128]{2,1,0:T(8,128)S(1)}, f32[16,8,128]{2,1,0:T(8,128)S(1)}, u32[]{:S(2)}, u32[]{:S(2)}) collective-permute-start(f32[16,8,128]{2,1,0:T(8,128)S(1)} %get-tuple-element.33), channel_id=1, source_target_pairs={{8,0},{16,8},{24,16},{9,1},{17,9},{25,17},{10,2},{18,10},{26,18},{... | collective-permute-start | bytes 196616 | tf_op jit(solution)/shard_map/ppermute | solution.py:577
  49.9 0.6 collective-permute-done.4.gxl
  50.4 4.3 %collective-permute-done.5.gxh = f32[16,8,128]{2,1,0:T(8,128)S(1)} collective-permute-done((f32[16,8,128]{2,1,0:T(8,128)S(1)}, f32[16,8,128]{2,1,0:T(8,128)S(1)}, u32[]{:S(2)}, u32[]{:S(2)}) %collective-permute-start.5) | collective-permute-done | bytes 65568 | tf_op jit(solution)/shard_map/ppermute | solution.py:577
  54.7 1.3 %collective-permute-start.6 = (f32[18,8,128]{2,1,0:T(8,128)S(1)}, f32[18,8,128]{2,1,0:T(8,128)S(1)}, u32[]{:S(2)}, u32[]{:S(2)}) collective-permute-start(f32[18,8,128]{2,1,0:T(8,128)S(1)} %get-tuple-element.36), channel_id=1, source_target_pairs={{0,1},{1,2},{2,3},{3,4},{4,5},{5,6},{6,7},{8,9},{9,10},{10,11},{11... | collective-permute-start | bytes 221192 | tf_op jit(solution)/shard_map/ppermute | solution.py:577
  56.0 1.3 %collective-permute-start.7 = (f32[18,8,128]{2,1,0:T(8,128)S(1)}, f32[18,8,128]{2,1,0:T(8,128)S(1)}, u32[]{:S(2)}, u32[]{:S(2)}) collective-permute-start(f32[18,8,128]{2,1,0:T(8,128)S(1)} %get-tuple-element.37), channel_id=1, source_target_pairs={{1,0},{2,1},{3,2},{4,3},{5,4},{6,5},{7,6},{9,8},{10,9},{11,10},{12... | collective-permute-start | bytes 221192 | tf_op jit(solution)/shard_map/ppermute | solution.py:577
  57.3 0.0 collective-permute-done.6.gyl
  57.3 3.6 %collective-permute-done.7.gyh = f32[18,8,128]{2,1,0:T(8,128)S(1)} collective-permute-done((f32[18,8,128]{2,1,0:T(8,128)S(1)}, f32[18,8,128]{2,1,0:T(8,128)S(1)}, u32[]{:S(2)}, u32[]{:S(2)}) %collective-permute-start.7) | collective-permute-done | bytes 73760 | tf_op jit(solution)/shard_map/ppermute | solution.py:577
  60.9 0.0 all-to-all-done.1.parts
  60.9 3.9 %shard_map.70 = (f32[4,2,8,8,128]{4,3,2,1,0:T(8,128)S(1)}, f32[4,2,8,8,128]{4,3,2,1,0:T(8,128)S(1)}, f32[32,8,128]{2,1,0:T(8,128)S(1)}, f32[8,128]{1,0:T(8,128)S(1)}) custom-call(f32[6,4,8,8,128]{4,3,2,1,0:T(8,128)S(1)} %copy-done.1, f32[4,8,8,128]{3,2,1,0:T(8,128)S(1)} %copy-done.7, f32[4,8,8,128]{3,2,1,0:T(8,128)S(1)} %copy-done.5, ...), custom_call_target="tpu_custom_call" | custom-call | tf_op jit(solution)/shard_map/pallas_call | solution.py:557
  64.8 0.0 copy-start.3
  64.9 14.7 %all_to_all.16.parts = f32[32,8,128]{2,1,0:T(8,128)S(1)} all-to-all(f32[32,8,128]{2,1,0:T(8,128)S(1)} %get-tuple-element.43), channel_id=1, replica_groups=mesh['member'=1,'gx'=4,'gy'=8] {'gx','gy'}, dimensions={0} | all-to-all | bytes 262144 | tf_op jit(solution)/shard_map/all_to_all | solution.py:581
  79.5 0.0 copy-done.3
  79.5 1.9 %shard_map.71 = f32[4,2,8,8,128]{4,3,2,1,0:T(8,128)} custom-call(f32[4,2,8,8,128]{4,3,2,1,0:T(8,128)S(1)} %copy-done.3, f32[4,2,8,8,128]{4,3,2,1,0:T(8,128)S(1)} %get-tuple-element.31.residual, f32[4,2,8,8,128]{4,3,2,1,0:T(8,128)S(1)} %get-tuple-element.41.second, f32[4,2,8,8,128]{4,3,2,1,0:T(8,128)S(1)} %get-tuple-element.42.third, ...), custom_call_target="tpu_custom_call" | custom-call | tf_op jit(solution)/shard_map/pallas_call | solution.py:557
  (4 shorter events, 0.0 us)
Async XLA Ops:
  0.0 1.1 %copy-start = (f32[6,4,8,8,128]{4,3,2,1,0:T(8,128)S(1)}, f32[6,4,8,8,128]{4,3,2,1,0:T(8,128)}, u32[]{:S(2)}) copy-start(f32[6,4,8,8,128]{4,3,2,1,0:T(8,128)} %couplings.3) | copy-start | bytes 2359300
  1.1 0.9 %copy-start.2 = (f32[4,2,8,8,128]{4,3,2,1,0:T(8,128)S(1)}, f32[4,2,8,8,128]{4,3,2,1,0:T(8,128)}, u32[]{:S(2)}) copy-start(f32[4,2,8,8,128]{4,3,2,1,0:T(8,128)} %guess.5) | copy-start | bytes 786436
  2.1 0.9 %copy-start.4 = (f32[4,8,8,128]{3,2,1,0:T(8,128)S(1)}, f32[4,8,8,128]{3,2,1,0:T(8,128)}, u32[]{:S(2)}) copy-start(f32[4,8,8,128]{3,2,1,0:T(8,128)} %wells.7) | copy-start | bytes 393220
  3.0 0.9 %copy-start.6 = (f32[4,8,8,128]{3,2,1,0:T(8,128)S(1)}, f32[4,8,8,128]{3,2,1,0:T(8,128)}, u32[]{:S(2)}) copy-start(f32[4,8,8,128]{3,2,1,0:T(8,128)} %diagonal.3) | copy-start | bytes 393220
  3.9 0.9 %copy-start.8 = (f32[4,2,8,8,128]{4,3,2,1,0:T(8,128)S(1)}, f32[4,2,8,8,128]{4,3,2,1,0:T(8,128)}, u32[]{:S(2)}) copy-start(f32[4,2,8,8,128]{4,3,2,1,0:T(8,128)} %right.1) | copy-start | bytes 786436
  4.8 0.8 copy-start.10
  5.6 17.2 %copy-start.5 = (f32[4,8,8,128]{3,2,1,0:T(8,128)S(1)}, f32[4,8,8,128]{3,2,1,0:T(8,128)}, u32[]{:S(2)}) copy-start(f32[4,8,8,128]{3,2,1,0:T(8,128)} %wells.7) | copy-start | bytes 393220
  6.5 32.4 %copy-start.1 = (f32[6,4,8,8,128]{4,3,2,1,0:T(8,128)S(1)}, f32[6,4,8,8,128]{4,3,2,1,0:T(8,128)}, u32[]{:S(2)}) copy-start(f32[6,4,8,8,128]{4,3,2,1,0:T(8,128)} %couplings.3) | copy-start | bytes 2359300
  6.5 9.4 %collective-permute-start = (f32[50,8,128]{2,1,0:T(8,128)S(1)}, f32[50,8,128]{2,1,0:T(8,128)S(1)}, u32[]{:S(2)}, u32[]{:S(2)}) collective-permute-start(f32[50,8,128]{2,1,0:T(8,128)S(1)} %get-tuple-element.25), channel_id=1, source_target_pairs={{0,8},{8,16},{16,24},{1,9},{9,17},{17,25},{2,10},{10,18},{18,26},{... | collective-permute-start | bytes 614408 | tf_op jit(solution)/shard_map/ppermute | solution.py:577
  11.6 8.4 %collective-permute-start.1 = (f32[50,8,128]{2,1,0:T(8,128)S(1)}, f32[50,8,128]{2,1,0:T(8,128)S(1)}, u32[]{:S(2)}, u32[]{:S(2)}) collective-permute-start(f32[50,8,128]{2,1,0:T(8,128)S(1)} %get-tuple-element.26), channel_id=1, source_target_pairs={{8,0},{16,8},{24,16},{9,1},{17,9},{25,17},{10,2},{18,10},{26,18},{... | collective-permute-start | bytes 614408 | tf_op jit(solution)/shard_map/ppermute | solution.py:577
  20.0 2.8 %copy-start.11 = (s32[8,8,128]{2,1,0:T(8,128)S(1)}, s32[8,8,128]{2,1,0:T(8,128)}, u32[]{:S(2)}) copy-start(s32[8,8,128]{2,1,0:T(8,128)} %ids.7) | copy-start | bytes 98308
  20.1 18.9 %collective-permute-start.2 = (f32[55,8,128]{2,1,0:T(8,128)S(1)}, f32[55,8,128]{2,1,0:T(8,128)S(1)}, u32[]{:S(2)}, u32[]{:S(2)}) collective-permute-start(f32[55,8,128]{2,1,0:T(8,128)S(1)} %get-tuple-element.29), channel_id=1, source_target_pairs={{0,1},{1,2},{2,3},{3,4},{4,5},{5,6},{6,7},{8,9},{9,10},{10,11},{11... | collective-permute-start | bytes 675848 | tf_op jit(solution)/shard_map/ppermute | solution.py:577
  21.4 17.6 %copy-start.9 = (f32[4,2,8,8,128]{4,3,2,1,0:T(8,128)S(1)}, f32[4,2,8,8,128]{4,3,2,1,0:T(8,128)}, u32[]{:S(2)}) copy-start(f32[4,2,8,8,128]{4,3,2,1,0:T(8,128)} %right.1) | copy-start | bytes 786436
  21.4 17.5 %collective-permute-start.3 = (f32[55,8,128]{2,1,0:T(8,128)S(1)}, f32[55,8,128]{2,1,0:T(8,128)S(1)}, u32[]{:S(2)}, u32[]{:S(2)}) collective-permute-start(f32[55,8,128]{2,1,0:T(8,128)S(1)} %get-tuple-element.30), channel_id=1, source_target_pairs={{1,0},{2,1},{3,2},{4,3},{5,4},{6,5},{7,6},{9,8},{10,9},{11,10},{12... | collective-permute-start | bytes 675848 | tf_op jit(solution)/shard_map/ppermute | solution.py:577
  22.9 16.1 %copy-start.7 = (f32[4,8,8,128]{3,2,1,0:T(8,128)S(1)}, f32[4,8,8,128]{3,2,1,0:T(8,128)}, u32[]{:S(2)}) copy-start(f32[4,8,8,128]{3,2,1,0:T(8,128)} %diagonal.3) | copy-start | bytes 393220
  42.4 18.5 %all-to-all-start.1 = ((f32[32,8,128]{2,1,0:T(8,128)}), f32[32,8,128]{2,1,0:T(8,128)S(1)}, u32[]{:S(2)}, u32[]{:S(2)}) async-start(f32[32,8,128]{2,1,0:T(8,128)} %shard_map.69), calls=%async_computation.1 | async-start | bytes 262144 | tf_op jit(solution)/shard_map/all_to_all | solution.py:581
  45.0 5.5 %collective-permute-start.4 = (f32[16,8,128]{2,1,0:T(8,128)S(1)}, f32[16,8,128]{2,1,0:T(8,128)S(1)}, u32[]{:S(2)}, u32[]{:S(2)}) collective-permute-start(f32[16,8,128]{2,1,0:T(8,128)S(1)} %get-tuple-element.32), channel_id=1, source_target_pairs={{0,8},{8,16},{16,24},{1,9},{9,17},{17,25},{2,10},{10,18},{18,26},{... | collective-permute-start | bytes 196616 | tf_op jit(solution)/shard_map/ppermute | solution.py:577
  48.6 6.2 %collective-permute-start.5 = (f32[16,8,128]{2,1,0:T(8,128)S(1)}, f32[16,8,128]{2,1,0:T(8,128)S(1)}, u32[]{:S(2)}, u32[]{:S(2)}) collective-permute-start(f32[16,8,128]{2,1,0:T(8,128)S(1)} %get-tuple-element.33), channel_id=1, source_target_pairs={{8,0},{16,8},{24,16},{9,1},{17,9},{25,17},{10,2},{18,10},{26,18},{... | collective-permute-start | bytes 196616 | tf_op jit(solution)/shard_map/ppermute | solution.py:577
  54.7 2.6 %collective-permute-start.6 = (f32[18,8,128]{2,1,0:T(8,128)S(1)}, f32[18,8,128]{2,1,0:T(8,128)S(1)}, u32[]{:S(2)}, u32[]{:S(2)}) collective-permute-start(f32[18,8,128]{2,1,0:T(8,128)S(1)} %get-tuple-element.36), channel_id=1, source_target_pairs={{0,1},{1,2},{2,3},{3,4},{4,5},{5,6},{6,7},{8,9},{9,10},{10,11},{11... | collective-permute-start | bytes 221192 | tf_op jit(solution)/shard_map/ppermute | solution.py:577
  56.0 4.9 %collective-permute-start.7 = (f32[18,8,128]{2,1,0:T(8,128)S(1)}, f32[18,8,128]{2,1,0:T(8,128)S(1)}, u32[]{:S(2)}, u32[]{:S(2)}) collective-permute-start(f32[18,8,128]{2,1,0:T(8,128)S(1)} %get-tuple-element.37), channel_id=1, source_target_pairs={{1,0},{2,1},{3,2},{4,3},{5,4},{6,5},{7,6},{9,8},{10,9},{11,10},{12... | collective-permute-start | bytes 221192 | tf_op jit(solution)/shard_map/ppermute | solution.py:577
  64.8 14.7 %copy-start.3 = (f32[4,2,8,8,128]{4,3,2,1,0:T(8,128)S(1)}, f32[4,2,8,8,128]{4,3,2,1,0:T(8,128)}, u32[]{:S(2)}) copy-start(f32[4,2,8,8,128]{4,3,2,1,0:T(8,128)} %guess.5) | copy-start | bytes 786436

commit v4 on v3

--- a/solution.py
+++ b/solution.py
@@ -144,9 +144,8 @@
     return jnp.sum(jnp.sum(value, axis=0, keepdims=True), axis=1, keepdims=True)
 
 
-def segment_rows(ids, values, scratch):
-    scratch[...] = jnp.zeros_like(scratch)
-    count, depth = values.shape[0], ids.shape[0]
+def list_wells(ids, present):
+    depth = ids.shape[0]
 
     def smallest(planes):
         least = planes[0]
@@ -154,19 +153,35 @@
             least = jnp.minimum(least, plane)
         return jnp.min(least)
 
-    def one_well(well):
-        planes = [ids[x].astype(jnp.float32) for x in range(depth)]
-        masks = [plane == well for plane in planes]
-        at = well.astype(jnp.int32)
+    planes = [ids[x].astype(jnp.float32) for x in range(depth)]
+
+    def one_well(state):
+        number, well = state
+        present[number] = well.astype(jnp.int32)
+        after = [jnp.where(plane > well, plane, float(WELLS)) for plane in planes]
+        return number + 1, smallest(after)
+
+    number, _ = lax.while_loop(
+        lambda state: state[1] < WELLS, one_well, (jnp.int32(1), smallest(planes))
+    )
+    present[0] = number - 1
+
+
+def segment_rows(ids, values, scratch, present):
+    scratch[...] = jnp.zeros_like(scratch)
+    count, depth = values.shape[0], ids.shape[0]
+
+    def one_well(step, _):
+        well = present[step + 1]
+        masks = [ids[x] == well for x in range(depth)]
         for number in range(count):
             total = jnp.where(masks[0], values[number, 0], 0.0)
             for x in range(1, depth):
                 total = total + jnp.where(masks[x], values[number, x], 0.0)
-            scratch[number, pl.ds(at, 1), :] = jnp.sum(total, axis=0, keepdims=True)
-        return smallest([jnp.where(plane > well, plane, float(WELLS)) for plane in planes])
-
-    first = smallest([ids[x].astype(jnp.float32) for x in range(depth)])
-    lax.while_loop(lambda well: well < WELLS, one_well, first)
+            scratch[number, pl.ds(well, 1), :] = jnp.sum(total, axis=0, keepdims=True)
+        return 0
+
+    lax.fori_loop(0, present[0], one_well, 0)
     rows = []
     for number in range(count):
         summed = jnp.sum(scratch[number], axis=1, keepdims=True)
@@ -200,68 +215,75 @@
     return jnp.sum(row, axis=1, keepdims=True)
 
 
-def pack_kernel(
-    couplings_in, diagonal_in, wells_in, ids_in, right_in, guess_in,
-    x_low, x_high, y_low, y_high,
-    couplings, diagonal, wells, ids, right, guess, arrived,
-):
-    copies = [
-        pltpu.make_async_copy(source, held, arrived.at[n])
-        for n, (source, held) in enumerate(
-            (
-                (couplings_in, couplings),
-                (diagonal_in, diagonal),
-                (wells_in, wells),
-                (ids_in, ids),
-                (right_in, right),
-                (guess_in, guess),
+def fill_pack(pack, inward, lateral, cut):
+    couplings, diagonal, wells, ids, right, guess = range(6)
+    for e in range(4):
+        pack[e] = cut(couplings, (inward, e), 0)
+        pack[LAT_UP + e] = cut(couplings, (lateral, e), 0)
+        pack[LAT_DOWN + e] = cut(couplings, (lateral + 1, e), 0)
+        pack[RISE + e] = cut(couplings, (4, e), 0)
+        pack[FALL + e] = cut(couplings, (5, e), 0)
+        pack[DIAGONAL + e] = cut(diagonal, (e,), 0)
+        pack[BACK_IN + e] = cut(couplings, (inward, e), 1)
+    for a in range(2):
+        pack[WELL_EQ + a] = cut(wells, (2 + a,), 0)
+        pack[BACK_EQ + a] = cut(wells, (2 + a,), 1)
+    pack[WELL_ID] = cut(ids, (), 0).astype(jnp.float32)
+    pack[BACK_ID] = cut(ids, (), 1).astype(jnp.float32)
+    for k in range(RHS):
+        here = [cut(guess, (k, a), 0) for a in range(2)]
+        back = [cut(guess, (k, a), 1) for a in range(2)]
+        entering = product(lambda e: pack[BACK_IN + e], *back)
+        local = face_stencil(pack, here[0], here[1], entering)
+        for a in range(2):
+            pack[GUESS + 2 * k + a] = here[a]
+            pack[REST + 2 * k + a] = cut(right, (k, a), 0) - local[a]
+
+
+def x_pack_kernel(*refs):
+    sources, packs, held_ends, arrived = refs[:6], refs[6:8], refs[8:20], refs[20]
+    copies = []
+    for n, source in enumerate(sources):
+        lead = (slice(None),) * (len(source.shape) - 3)
+        depth = source.shape[-3]
+        for end, start in enumerate((0, depth - 2)):
+            copies.append(
+                pltpu.make_async_copy(
+                    source.at[lead + (pl.ds(start, 2),)],
+                    held_ends[2 * n + end],
+                    arrived.at[2 * n + end],
+                )
             )
-        )
-    ]
     for copy in copies:
         copy.start()
     for copy in copies:
         copy.wait()
-    last = guess.shape[2] - 1
-    for axis, packs in ((0, (x_low, x_high)), (1, (y_low, y_high))):
-        for end, pack in enumerate(packs):
-            outer = 0 if end == 0 else last
-            behind = 1 if end == 0 else last - 1
-            inward = 2 * axis + (1 if end == 0 else 0)
-            lateral = 2 * (1 - axis)
-
-            def cut(ref, *index, at=outer):
-                if axis == 0:
-                    return ref[index + (at,)]
-                return ref[index + (slice(None), at, slice(None))]
-
-            for e in range(4):
-                pack[e] = cut(couplings, inward, e)
-                pack[LAT_UP + e] = cut(couplings, lateral, e)
-                pack[LAT_DOWN + e] = cut(couplings, lateral + 1, e)
-                pack[RISE + e] = cut(couplings, 4, e)
-                pack[FALL + e] = cut(couplings, 5, e)
-                pack[DIAGONAL + e] = cut(diagonal, e)
-                pack[BACK_IN + e] = cut(couplings, inward, e, at=behind)
-            for a in range(2):
-                pack[WELL_EQ + a] = cut(wells, 2 + a)
-                pack[BACK_EQ + a] = cut(wells, 2 + a, at=behind)
-            pack[WELL_ID] = cut(ids).astype(jnp.float32)
-            pack[BACK_ID] = cut(ids, at=behind).astype(jnp.float32)
-            for k in range(RHS):
-                here = [cut(guess, k, a) for a in range(2)]
-                entering = product(
-                    lambda e: pack[BACK_IN + e],
-                    cut(guess, k, 0, at=behind),
-                    cut(guess, k, 1, at=behind),
-                )
-                local = face_stencil(pack, here[0], here[1], entering)
-                for a in range(2):
-                    pack[GUESS + 2 * k + a] = here[a]
-                    pack[REST + 2 * k + a] = cut(right, k, a) - local[a]
-
-
-def corner_kernel(y_low, y_high, fxl, fxh, low_out, high_out):
+    for end, pack in enumerate(packs):
+        fill_pack(
+            pack,
+            1 - end,
+            2,
+            lambda n, index, layer: held_ends[2 * n + end][
+                index + (1 - layer if end else layer,)
+            ],
+        )
+
+
+def y_pack(arguments, packs):
+    last = arguments[-1].shape[-2] - 1
+    for end, pack in enumerate(packs):
+        fill_pack(
+            pack,
+            3 - end,
+            0,
+            lambda n, index, layer: arguments[n][
+                index + (slice(None), last - layer if end else layer, slice(None))
+            ],
+        )
+
+
+def corner_kernel(y_low, y_high, fxl, fxh, table, low_out, high_out, part):
+    part[...] = jnp.broadcast_to(table[...][None, :2], part.shape)
     last = fxl.shape[1] - 1
     for own, out, at, side in ((y_low, low_out, 0, LAT_DOWN), (y_high, high_out, last, LAT_UP)):
         for n in range(FACE_PLANES):
@@ -274,7 +296,8 @@
                 row += 1
 
 
-def image_corner_kernel(y_low, y_high, gxl, gxh, low_out, high_out):
+def image_corner_kernel(y_low, y_high, gxl, gxh, table, low_out, high_out, part):
+    part[...] = jnp.broadcast_to(table[...][None], part.shape)
     last = gxl.shape[1] - 1
     for own, out, at in ((y_low, low_out, 0), (y_high, high_out, last)):
         for n in range(16):
@@ -284,14 +307,18 @@
                 out[16 + x_end, n : n + 1, :] = face[n, at : at + 1, :]
 
 
-def guess_kernel(wells, ids, guess, part, values, scratch):
+def guess_kernel(
+    couplings, diagonal, wells, ids, right, guess,
+    table_out, present, y_low, y_high, values, scratch,
+):
+    y_pack((couplings, diagonal, wells, ids, right, guess), (y_low, y_high))
+    list_wells(ids, present)
     for k in range(RHS):
         values[k] = wells[0] * guess[k, 0] + wells[1] * guess[k, 1]
     values[4] = wells[0] * wells[2] + wells[1] * wells[3]
     values[5] = wells[2] * wells[2] + wells[3] * wells[3]
-    rows = segment_rows(ids, values, scratch)
-    table = pack_rows(rows, jnp.zeros((8, LANES), jnp.float32))
-    part[...] = jnp.broadcast_to(table[None, :2], part.shape)
+    rows = segment_rows(ids, values, scratch, present)
+    table_out[...] = pack_rows(rows, jnp.zeros((8, LANES), jnp.float32))
 
 
 def residual_kernel(
@@ -354,7 +381,7 @@
     )
 
 
-def moments_kernel(wells, ids, residual, image, part, values, scratch):
+def moments_kernel(wells, ids, residual, image, present, table_out, values, scratch):
     table = jnp.zeros((8, LANES), jnp.float32)
     for k in range(RHS):
         now = [residual[k, a] for a in range(2)]
@@ -365,9 +392,8 @@
         table = put(6, k, full_sum(now[0] * now[0] + now[1] * now[1]), table)
         table = put(6, 4 + k, full_sum(now[0] * result[0] + now[1] * result[1]), table)
         table = put(6, 8 + k, full_sum(result[0] * result[0] + result[1] * result[1]), table)
-    rows = segment_rows(ids, values, scratch)
-    table = pack_rows(rows, table)
-    part[...] = jnp.broadcast_to(table[None], part.shape)
+    rows = segment_rows(ids, values, scratch, present)
+    table_out[...] = pack_rows(rows, table)
 
 
 def first_step(totals, small, k):
@@ -391,7 +417,7 @@
 
 def krylov_kernel(
     couplings, diagonal, wells, ids, fxl, fxh, fyl, fyh, gxl, gxh, gyl, gyh,
-    residual, image, residual_faces, parts, small_in,
+    residual, image, residual_faces, parts, small_in, present,
     second_out, third_out, part, totals_out, scratch, values_scratch,
 ):
     faces, sent = (fxl, fxh, fyl, fyh), (gxl, gxh, gyl, gyh)
@@ -468,7 +494,7 @@
                 dot = full_sum(fields[i][0] * fields[j][0] + fields[i][1] * fields[j][1])
                 table = put(4, 4 * number + k, dot, table)
                 number += 1
-    rows = segment_rows(ids, values_scratch, scratch)
+    rows = segment_rows(ids, values_scratch, scratch, present)
     table = pack_rows(rows, table)
     part[...] = jnp.broadcast_to(table[None], part.shape)
 
@@ -551,16 +577,27 @@
             )
 
 
-def call(kernel, shapes, arguments, scratch=(), own_copies=False, cost=0):
+def call(kernel, shapes, arguments, scratch=(), own_copies=False, cost=0, grant=24 << 20):
     whole = pl.BlockSpec(memory_space=pltpu.VMEM)
-    far = pl.BlockSpec(memory_space=pl.ANY)
+    far = pl.BlockSpec(memory_space=pltpu.HBM)
+    scalars = pl.BlockSpec(memory_space=pltpu.SMEM)
+
+    def place(array):
+        if len(array.shape) == 1:
+            return scalars
+        return far if own_copies else whole
+
+    outs = [
+        jax.ShapeDtypeStruct(shape, jnp.float32 if len(shape) > 1 else jnp.int32)
+        for shape in shapes
+    ]
     return pl.pallas_call(
         kernel,
-        out_shape=[jax.ShapeDtypeStruct(shape, jnp.float32) for shape in shapes],
-        in_specs=[far if own_copies else whole] * len(arguments),
-        out_specs=[whole] * len(shapes),
+        out_shape=outs,
+        in_specs=[place(argument) for argument in arguments],
+        out_specs=[scalars if len(shape) == 1 else whole for shape in shapes],
         scratch_shapes=list(scratch),
-        compiler_params=pltpu.CompilerParams(vmem_limit_bytes=24 << 20),
+        compiler_params=pltpu.CompilerParams(vmem_limit_bytes=grant),
         cost_estimate=pl.CostEstimate(flops=cost, bytes_accessed=cost, transcendentals=0)
         if cost
         else None,
@@ -588,29 +625,33 @@
     block = guess.shape[2:]
     arguments = (couplings, diagonal, wells, ids, right, guess)
 
-    x_low, x_high, y_low, y_high = call(
-        pack_kernel,
-        [(FACE_PLANES,) + plane] * 4,
+    ends = []
+    for argument in arguments:
+        shape = argument.shape[:-3] + (2,) + argument.shape[-2:]
+        ends += [pltpu.VMEM(shape, argument.dtype)] * 2
+    x_low, x_high = call(
+        x_pack_kernel,
+        [(FACE_PLANES,) + plane] * 2,
         arguments,
-        [pltpu.VMEM(argument.shape, argument.dtype) for argument in arguments]
-        + [pltpu.SemaphoreType.DMA((len(arguments),))],
+        ends + [pltpu.SemaphoreType.DMA((len(ends),))],
         own_copies=True,
+        grant=60 << 20,
     )
     fxl = from_behind(x_high, "gx", 1)
     fxh = from_behind(x_low, "gx", -1)
-    (part,) = call(
+    table, present, y_low, y_high = call(
         guess_kernel,
-        [(devices, 2, LANES)],
-        (wells, ids, guess),
+        [plane, (WELLS + 1,)] + [(FACE_PLANES,) + plane] * 2,
+        arguments,
         [held(6, *block), held(6, WELLS, LANES)],
         cost=4 << 20,
     )
+    y_low, y_high, part = call(
+        corner_kernel,
+        [(FACE_PLANES + CORNER_PLANES,) + plane] * 2 + [(devices, 2, LANES)],
+        (y_low, y_high, fxl, fxh, table),
+    )
     parts = exchanged(part)
-    y_low, y_high = call(
-        corner_kernel,
-        [(FACE_PLANES + CORNER_PLANES,) + plane] * 2,
-        (y_low, y_high, fxl, fxh),
-    )
     fyl = from_behind(y_high, "gy", 1)
     fyh = from_behind(y_low, "gy", -1)
 
@@ -622,17 +663,19 @@
     )
     gxl = from_behind(x_high, "gx", 1)
     gxh = from_behind(x_low, "gx", -1)
-    (part,) = call(
+    (table,) = call(
         moments_kernel,
-        [(devices, 8, LANES)],
-        (wells, ids, residual, image),
+        [plane],
+        (wells, ids, residual, image, present),
         [held(16, *block), held(16, WELLS, LANES)],
         cost=4 << 20,
     )
+    y_low, y_high, part = call(
+        image_corner_kernel,
+        [(18,) + plane] * 2 + [(devices, 8, LANES)],
+        (y_low, y_high, gxl, gxh, table),
+    )
     parts = exchanged(part)
-    y_low, y_high = call(
-        image_corner_kernel, [(18,) + plane] * 2, (y_low, y_high, gxl, gxh)
-    )
     gyl = from_behind(y_high, "gy", 1)
     gyh = from_behind(y_low, "gy", -1)
 
@@ -640,7 +683,7 @@
         krylov_kernel,
         [field, field, (devices, 8, LANES), (8, LANES)],
         (couplings, diagonal, wells, ids) + faces + (gxl, gxh, gyl, gyh)
-        + (residual, image, residual_faces, parts, small),
+        + (residual, image, residual_faces, parts, small, present),
         [held(12, WELLS, LANES), held(12, *block)],
     )
     parts = exchanged(part)

time: 82.1 us -> 74.4 us (0.906)
  local copies, waits for them, and re-layouts: 5.63 us -> 0.02 us
  waiting for transfers between devices: 15.6 us -> 13.4 us
  Pallas kernels: 11.7 us -> 13 us
    unnamed x24 -> x12, local copies, waits for them, and re-layouts: 5.63 us -> 0.02 us
    ppermute x8, waiting for transfers between devices: 15.6 us -> 11.5 us  [from_behind(): lax.ppermute(value, axis, [(source, source + steps) for source in range(l...]
    all_to_all x1, waiting for transfers between devices: 0.01 us -> 1.9 us  [exchanged(): return lax.all_to_all(part, ('gx', 'gy'), 0, 0, tiled=True)]
    pallas_call x8, Pallas kernels: 11.7 us -> 13 us  [call(): pl.pallas_call(kernel, out_shape=outs, in_specs=[place(argument) for argu...]
  transfers between devices with their start and end apart: 9 -> 9, of which waited for: 5 -> 5; matrix products, arithmetic and copies ran while one was open for 0% -> 0% of each run, Pallas kernels for 2% -> 5%
where the time goes in v4:
time: 74.4 us; the launch traced here: 74 us
  blocking collectives  28.9 us (39%)
  starting transfers between devices  18.5 us (25%)
  waiting for transfers between devices  13.4 us (18%)
  Pallas kernels  13 us (17%)
    all_to_all x2, blocking collectives, exchanged(): return lax.all_to_all(part, ('gx', 'gy'), 0, 0, tiled=True)  28.9 us
    ppermute x8, starting transfers between devices, from_behind(): lax.ppermute(value, axis, [(source, source + steps) for source in range(l...  15.9 us
    pallas_call x8, Pallas kernels, call(): pl.pallas_call(kernel, out_shape=outs, in_specs=[place(argument) for argu...  13 us
    ppermute x8, waiting for transfers between devices, from_behind(): lax.ppermute(value, axis, [(source, source + steps) for source in range(l...  11.5 us
    all_to_all x1, starting transfers between devices, exchanged(): return lax.all_to_all(part, ('gx', 'gy'), 0, 0, tiled=True)  2.58 us
    all_to_all x1, waiting for transfers between devices, exchanged(): return lax.all_to_all(part, ('gx', 'gy'), 0, 0, tiled=True)  1.9 us
  transfers between devices with their start and end apart: 9, of which 5 were waited for; matrix products, arithmetic and copies ran while one was open for 0% of the time, Pallas kernels for 5%

profile of v4, /device:TPU:0, one launch (start us, length us, event | category | flops | bytes accessed | tf_op | source)
XLA Modules:
  0.0 74.0 jit_solution(3047568447068767581)
XLA Ops:
  0.0 0.0 copy-start.5
  0.0 0.0 copy-start.2
  0.0 0.0 copy-start.1
  0.0 0.0 copy-start.4
  0.0 0.0 copy-start
  0.0 0.0 copy-start.3
  0.0 2.2 %shard_map.64 = (f32[50,8,128]{2,1,0:T(8,128)}, f32[50,8,128]{2,1,0:T(8,128)}) custom-call(f32[6,4,8,8,128]{4,3,2,1,0:T(8,128)} %couplings.5, f32[4,8,8,128]{3,2,1,0:T(8,128)} %diagonal.5, f32[4,8,8,128]{3,2,1,0:T(8,128)} %wells.7, s32[8,8,128]{2,1,0:T(8,128)} %ids.7, f32[4,2,8,8,128]{4,3,2,1,0:T(8,128)} %right.3, f32[4,2,8,8,128]{4,3,2,1,0:T(8,128)} %guess.5), custom_call_target="tpu_custom_call" | custom-call | tf_op jit(solution)/shard_map/pallas_call | solution.py:594
  2.3 5.0 %collective-permute-start = (f32[50,8,128]{2,1,0:T(8,128)}, f32[50,8,128]{2,1,0:T(8,128)S(1)}, u32[]{:S(2)}, u32[]{:S(2)}) collective-permute-start(f32[50,8,128]{2,1,0:T(8,128)} %get-tuple-element.29), channel_id=1, source_target_pairs={{0,8},{8,16},{16,24},{1,9},{9,17},{17,25},{2,10},{10,18},{18,26},{... | collective-permute-start | bytes 614408 | tf_op jit(solution)/shard_map/ppermute | solution.py:614
  7.2 1.3 %collective-permute-start.1 = (f32[50,8,128]{2,1,0:T(8,128)}, f32[50,8,128]{2,1,0:T(8,128)S(1)}, u32[]{:S(2)}, u32[]{:S(2)}) collective-permute-start(f32[50,8,128]{2,1,0:T(8,128)} %get-tuple-element.30), channel_id=1, source_target_pairs={{8,0},{16,8},{24,16},{9,1},{17,9},{25,17},{10,2},{18,10},{26,18},{... | collective-permute-start | bytes 614408 | tf_op jit(solution)/shard_map/ppermute | solution.py:614
  8.5 0.0 copy-done.5
  8.5 0.0 copy-done.2
  8.5 0.0 copy-done.1
  8.5 0.0 copy-done.4
  8.6 0.0 copy-done
  8.6 0.0 copy-done.3
  8.6 2.2 %shard_map.65 = (f32[8,128]{1,0:T(8,128)S(1)}, s32[41]{0:T(128)S(1)}, f32[50,8,128]{2,1,0:T(8,128)S(1)}, f32[50,8,128]{2,1,0:T(8,128)S(1)}) custom-call(f32[6,4,8,8,128]{4,3,2,1,0:T(8,128)S(1)} %copy-done, f32[4,8,8,128]{3,2,1,0:T(8,128)S(1)} %copy-done.4, f32[4,8,8,128]{3,2,1,0:T(8,128)S(1)} %copy-done.2, s32[8,8,128]{2,1,0:T(8,128)S(1)} %copy-done.5, ...), custom_call_target="tpu_custom_call" | custom-call | flops 4194304 | bytes 4194304 | tf_op jit(solution)/shard_map/pallas_call | solution.py:594
  10.8 1.1 %collective-permute-done.fxl = f32[50,8,128]{2,1,0:T(8,128)S(1)} collective-permute-done((f32[50,8,128]{2,1,0:T(8,128)}, f32[50,8,128]{2,1,0:T(8,128)S(1)}, u32[]{:S(2)}, u32[]{:S(2)}) %collective-permute-start) | collective-permute-done | bytes 204832 | tf_op jit(solution)/shard_map/ppermute | solution.py:614
  11.8 4.0 %collective-permute-done.1.fxh = f32[50,8,128]{2,1,0:T(8,128)S(1)} collective-permute-done((f32[50,8,128]{2,1,0:T(8,128)}, f32[50,8,128]{2,1,0:T(8,128)S(1)}, u32[]{:S(2)}, u32[]{:S(2)}) %collective-permute-start.1) | collective-permute-done | bytes 204832 | tf_op jit(solution)/shard_map/ppermute | solution.py:614
  15.9 0.1 shard_map.66
  15.9 1.3 %collective-permute-start.2 = (f32[55,8,128]{2,1,0:T(8,128)S(1)}, f32[55,8,128]{2,1,0:T(8,128)S(1)}, u32[]{:S(2)}, u32[]{:S(2)}) collective-permute-start(f32[55,8,128]{2,1,0:T(8,128)S(1)} %get-tuple-element.34), channel_id=1, source_target_pairs={{0,1},{1,2},{2,3},{3,4},{4,5},{5,6},{6,7},{8,9},{9,10},{10,11},{11... | collective-permute-start | bytes 675848 | tf_op jit(solution)/shard_map/ppermute | solution.py:614
  17.2 1.3 %collective-permute-start.3 = (f32[55,8,128]{2,1,0:T(8,128)S(1)}, f32[55,8,128]{2,1,0:T(8,128)S(1)}, u32[]{:S(2)}, u32[]{:S(2)}) collective-permute-start(f32[55,8,128]{2,1,0:T(8,128)S(1)} %get-tuple-element.35), channel_id=1, source_target_pairs={{1,0},{2,1},{3,2},{4,3},{5,4},{6,5},{7,6},{9,8},{10,9},{11,10},{12... | collective-permute-start | bytes 675848 | tf_op jit(solution)/shard_map/ppermute | solution.py:614
  18.5 14.9 %all_to_all.15.parts = f32[32,2,128]{2,1,0:T(2,128)S(1)} all-to-all(f32[32,2,128]{2,1,0:T(2,128)S(1)} %get-tuple-element.36), channel_id=1, replica_groups=mesh['member'=1,'gx'=4,'gy'=8] {'gx','gy'}, dimensions={0} | all-to-all | bytes 65536 | tf_op jit(solution)/shard_map/all_to_all | solution.py:618
  33.4 0.0 collective-permute-done.2.fyl
  33.4 0.0 collective-permute-done.3.fyh
  33.4 0.9 %shard_map.67 = (f32[4,2,8,8,128]{4,3,2,1,0:T(8,128)S(1)}, f32[4,2,8,8,128]{4,3,2,1,0:T(8,128)S(1)}, f32[4,8,8,128]{3,2,1,0:T(8,128)S(1)}, f32[16,8,128]{2,1,0:T...) custom-call(f32[6,4,8,8,128]{4,3,2,1,0:T(8,128)S(1)} %copy-done, ...), custom_call_target="tpu_custom_call" | custom-call | tf_op jit(solution)/shard_map/pallas_call | solution.py:594
  34.3 2.5 %collective-permute-start.4 = (f32[16,8,128]{2,1,0:T(8,128)S(1)}, f32[16,8,128]{2,1,0:T(8,128)S(1)}, u32[]{:S(2)}, u32[]{:S(2)}) collective-permute-start(f32[16,8,128]{2,1,0:T(8,128)S(1)} %get-tuple-element.38), channel_id=1, source_target_pairs={{0,8},{8,16},{16,24},{1,9},{9,17},{17,25},{2,10},{10,18},{18,26},{... | collective-permute-start | bytes 196616 | tf_op jit(solution)/shard_map/ppermute | solution.py:614
  36.8 1.3 %collective-permute-start.5 = (f32[16,8,128]{2,1,0:T(8,128)S(1)}, f32[16,8,128]{2,1,0:T(8,128)S(1)}, u32[]{:S(2)}, u32[]{:S(2)}) collective-permute-start(f32[16,8,128]{2,1,0:T(8,128)S(1)} %get-tuple-element.39), channel_id=1, source_target_pairs={{8,0},{16,8},{24,16},{9,1},{17,9},{25,17},{10,2},{18,10},{26,18},{... | collective-permute-start | bytes 196616 | tf_op jit(solution)/shard_map/ppermute | solution.py:614
  38.1 1.4 %shard_map.68.table = f32[8,128]{1,0:T(8,128)S(1)} custom-call(f32[4,8,8,128]{3,2,1,0:T(8,128)S(1)} %copy-done.2, s32[8,8,128]{2,1,0:T(8,128)S(1)} %copy-done.5, f32[4,2,8,8,128]{4,3,2,1,0:T(8,128)S(1)} %get-tuple-element.37.residual, f32[4,2,8,8,128]{4,3,2,1,0:T(8,128)S(1)} %get-tuple-element.42.image, s32[41]{0:T(128)S(1)} %get-tuple-element.43.present), custom_call_target="tpu_custom_call" | custom-call | flops 4194304 | bytes 4194304 | tf_op jit(solution)/shard_map/pallas_call | solution.py:594
  39.5 0.0 collective-permute-done.4.gxl
  39.5 3.4 %collective-permute-done.5.gxh = f32[16,8,128]{2,1,0:T(8,128)S(1)} collective-permute-done((f32[16,8,128]{2,1,0:T(8,128)S(1)}, f32[16,8,128]{2,1,0:T(8,128)S(1)}, u32[]{:S(2)}, u32[]{:S(2)}) %collective-permute-start.5) | collective-permute-done | bytes 65568 | tf_op jit(solution)/shard_map/ppermute | solution.py:614
  43.0 0.7 shard_map.69
  43.7 2.6 %all-to-all-start.1 = ((f32[32,8,128]{2,1,0:T(8,128)}), f32[32,8,128]{2,1,0:T(8,128)S(1)}, u32[]{:S(2)}, u32[]{:S(2)}) async-start(f32[32,8,128]{2,1,0:T(8,128)} %get-tuple-element.47), calls=%async_computation.1 | async-start | bytes 262144 | tf_op jit(solution)/shard_map/all_to_all | solution.py:618
  46.2 2.0 %collective-permute-start.6 = (f32[18,8,128]{2,1,0:T(8,128)S(1)}, f32[18,8,128]{2,1,0:T(8,128)S(1)}, u32[]{:S(2)}, u32[]{:S(2)}) collective-permute-start(f32[18,8,128]{2,1,0:T(8,128)S(1)} %get-tuple-element.44), channel_id=1, source_target_pairs={{0,1},{1,2},{2,3},{3,4},{4,5},{5,6},{6,7},{8,9},{9,10},{10,11},{11... | collective-permute-start | bytes 221192 | tf_op jit(solution)/shard_map/ppermute | solution.py:614
  48.3 1.3 %collective-permute-start.7 = (f32[18,8,128]{2,1,0:T(8,128)S(1)}, f32[18,8,128]{2,1,0:T(8,128)S(1)}, u32[]{:S(2)}, u32[]{:S(2)}) collective-permute-start(f32[18,8,128]{2,1,0:T(8,128)S(1)} %get-tuple-element.45), channel_id=1, source_target_pairs={{1,0},{2,1},{3,2},{4,3},{5,4},{6,5},{7,6},{9,8},{10,9},{11,10},{12... | collective-permute-start | bytes 221192 | tf_op jit(solution)/shard_map/ppermute | solution.py:614
  49.6 0.0 collective-permute-done.6.gyl
  49.6 3.0 %collective-permute-done.7.gyh = f32[18,8,128]{2,1,0:T(8,128)S(1)} collective-permute-done((f32[18,8,128]{2,1,0:T(8,128)S(1)}, f32[18,8,128]{2,1,0:T(8,128)S(1)}, u32[]{:S(2)}, u32[]{:S(2)}) %collective-permute-start.7) | collective-permute-done | bytes 73760 | tf_op jit(solution)/shard_map/ppermute | solution.py:614
  52.6 1.9 %all-to-all-done.1.parts = f32[32,8,128]{2,1,0:T(8,128)S(1)} async-done(((f32[32,8,128]{2,1,0:T(8,128)}), f32[32,8,128]{2,1,0:T(8,128)S(1)}, u32[]{:S(2)}, u32[]{:S(2)}) %all-to-all-start.1) | async-done | bytes 131104 | tf_op jit(solution)/shard_map/all_to_all | solution.py:618
  54.5 3.5 %shard_map.70 = (f32[4,2,8,8,128]{4,3,2,1,0:T(8,128)S(1)}, f32[4,2,8,8,128]{4,3,2,1,0:T(8,128)S(1)}, f32[32,8,128]{2,1,0:T(8,128)S(1)}, f32[8,128]{1,0:T(8,128)S(1)}) custom-call(f32[6,4,8,8,128]{4,3,2,1,0:T(8,128)S(1)} %copy-done, f32[4,8,8,128]{3,2,1,0:T(8,128)S(1)} %copy-done.4, f32[4,8,8,128]{3,2,1,0:T(8,128)S(1)} %copy-done.2, ...), custom_call_target="tpu_custom_call" | custom-call | tf_op jit(solution)/shard_map/pallas_call | solution.py:594
  58.0 14.0 %all_to_all.16.parts = f32[32,8,128]{2,1,0:T(8,128)S(1)} all-to-all(f32[32,8,128]{2,1,0:T(8,128)S(1)} %get-tuple-element.51), channel_id=1, replica_groups=mesh['member'=1,'gx'=4,'gy'=8] {'gx','gy'}, dimensions={0} | all-to-all | bytes 262144 | tf_op jit(solution)/shard_map/all_to_all | solution.py:618
  72.0 1.9 %shard_map.71 = f32[4,2,8,8,128]{4,3,2,1,0:T(8,128)} custom-call(f32[4,2,8,8,128]{4,3,2,1,0:T(8,128)S(1)} %copy-done.1, f32[4,2,8,8,128]{4,3,2,1,0:T(8,128)S(1)} %get-tuple-element.37.residual, f32[4,2,8,8,128]{4,3,2,1,0:T(8,128)S(1)} %get-tuple-element.49.second, f32[4,2,8,8,128]{4,3,2,1,0:T(8,128)S(1)} %get-tuple-element.50.third, ...), custom_call_target="tpu_custom_call" | custom-call | tf_op jit(solution)/shard_map/pallas_call | solution.py:594
Async XLA Ops:
  0.0 8.5 %copy-start.5 = (s32[8,8,128]{2,1,0:T(8,128)S(1)}, s32[8,8,128]{2,1,0:T(8,128)}, u32[]{:S(2)}) copy-start(s32[8,8,128]{2,1,0:T(8,128)} %ids.7) | copy-start | bytes 98308
  0.0 8.5 %copy-start.2 = (f32[4,8,8,128]{3,2,1,0:T(8,128)S(1)}, f32[4,8,8,128]{3,2,1,0:T(8,128)}, u32[]{:S(2)}) copy-start(f32[4,8,8,128]{3,2,1,0:T(8,128)} %wells.7) | copy-start | bytes 393220
  0.0 8.5 %copy-start.1 = (f32[4,2,8,8,128]{4,3,2,1,0:T(8,128)S(1)}, f32[4,2,8,8,128]{4,3,2,1,0:T(8,128)}, u32[]{:S(2)}) copy-start(f32[4,2,8,8,128]{4,3,2,1,0:T(8,128)} %guess.5) | copy-start | bytes 786436
  0.0 8.5 %copy-start.4 = (f32[4,8,8,128]{3,2,1,0:T(8,128)S(1)}, f32[4,8,8,128]{3,2,1,0:T(8,128)}, u32[]{:S(2)}) copy-start(f32[4,8,8,128]{3,2,1,0:T(8,128)} %diagonal.5) | copy-start | bytes 393220
  0.0 8.5 %copy-start = (f32[6,4,8,8,128]{4,3,2,1,0:T(8,128)S(1)}, f32[6,4,8,8,128]{4,3,2,1,0:T(8,128)}, u32[]{:S(2)}) copy-start(f32[6,4,8,8,128]{4,3,2,1,0:T(8,128)} %couplings.5) | copy-start | bytes 2359300
  0.0 8.6 %copy-start.3 = (f32[4,2,8,8,128]{4,3,2,1,0:T(8,128)S(1)}, f32[4,2,8,8,128]{4,3,2,1,0:T(8,128)}, u32[]{:S(2)}) copy-start(f32[4,2,8,8,128]{4,3,2,1,0:T(8,128)} %right.3) | copy-start | bytes 786436
  2.3 9.6 %collective-permute-start = (f32[50,8,128]{2,1,0:T(8,128)}, f32[50,8,128]{2,1,0:T(8,128)S(1)}, u32[]{:S(2)}, u32[]{:S(2)}) collective-permute-start(f32[50,8,128]{2,1,0:T(8,128)} %get-tuple-element.29), channel_id=1, source_target_pairs={{0,8},{8,16},{16,24},{1,9},{9,17},{17,25},{2,10},{10,18},{18,26},{... | collective-permute-start | bytes 614408 | tf_op jit(solution)/shard_map/ppermute | solution.py:614
  7.2 8.6 %collective-permute-start.1 = (f32[50,8,128]{2,1,0:T(8,128)}, f32[50,8,128]{2,1,0:T(8,128)S(1)}, u32[]{:S(2)}, u32[]{:S(2)}) collective-permute-start(f32[50,8,128]{2,1,0:T(8,128)} %get-tuple-element.30), channel_id=1, source_target_pairs={{8,0},{16,8},{24,16},{9,1},{17,9},{25,17},{10,2},{18,10},{26,18},{... | collective-permute-start | bytes 614408 | tf_op jit(solution)/shard_map/ppermute | solution.py:614
  15.9 17.5 %collective-permute-start.2 = (f32[55,8,128]{2,1,0:T(8,128)S(1)}, f32[55,8,128]{2,1,0:T(8,128)S(1)}, u32[]{:S(2)}, u32[]{:S(2)}) collective-permute-start(f32[55,8,128]{2,1,0:T(8,128)S(1)} %get-tuple-element.34), channel_id=1, source_target_pairs={{0,1},{1,2},{2,3},{3,4},{4,5},{5,6},{6,7},{8,9},{9,10},{10,11},{11... | collective-permute-start | bytes 675848 | tf_op jit(solution)/shard_map/ppermute | solution.py:614
  17.2 16.2 %collective-permute-start.3 = (f32[55,8,128]{2,1,0:T(8,128)S(1)}, f32[55,8,128]{2,1,0:T(8,128)S(1)}, u32[]{:S(2)}, u32[]{:S(2)}) collective-permute-start(f32[55,8,128]{2,1,0:T(8,128)S(1)} %get-tuple-element.35), channel_id=1, source_target_pairs={{1,0},{2,1},{3,2},{4,3},{5,4},{6,5},{7,6},{9,8},{10,9},{11,10},{12... | collective-permute-start | bytes 675848 | tf_op jit(solution)/shard_map/ppermute | solution.py:614
  34.3 5.2 %collective-permute-start.4 = (f32[16,8,128]{2,1,0:T(8,128)S(1)}, f32[16,8,128]{2,1,0:T(8,128)S(1)}, u32[]{:S(2)}, u32[]{:S(2)}) collective-permute-start(f32[16,8,128]{2,1,0:T(8,128)S(1)} %get-tuple-element.38), channel_id=1, source_target_pairs={{0,8},{8,16},{16,24},{1,9},{9,17},{17,25},{2,10},{10,18},{18,26},{... | collective-permute-start | bytes 196616 | tf_op jit(solution)/shard_map/ppermute | solution.py:614
  36.8 6.2 %collective-permute-start.5 = (f32[16,8,128]{2,1,0:T(8,128)S(1)}, f32[16,8,128]{2,1,0:T(8,128)S(1)}, u32[]{:S(2)}, u32[]{:S(2)}) collective-permute-start(f32[16,8,128]{2,1,0:T(8,128)S(1)} %get-tuple-element.39), channel_id=1, source_target_pairs={{8,0},{16,8},{24,16},{9,1},{17,9},{25,17},{10,2},{18,10},{26,18},{... | collective-permute-start | bytes 196616 | tf_op jit(solution)/shard_map/ppermute | solution.py:614
  43.7 10.8 %all-to-all-start.1 = ((f32[32,8,128]{2,1,0:T(8,128)}), f32[32,8,128]{2,1,0:T(8,128)S(1)}, u32[]{:S(2)}, u32[]{:S(2)}) async-start(f32[32,8,128]{2,1,0:T(8,128)} %get-tuple-element.47), calls=%async_computation.1 | async-start | bytes 262144 | tf_op jit(solution)/shard_map/all_to_all | solution.py:618
  46.2 3.3 %collective-permute-start.6 = (f32[18,8,128]{2,1,0:T(8,128)S(1)}, f32[18,8,128]{2,1,0:T(8,128)S(1)}, u32[]{:S(2)}, u32[]{:S(2)}) collective-permute-start(f32[18,8,128]{2,1,0:T(8,128)S(1)} %get-tuple-element.44), channel_id=1, source_target_pairs={{0,1},{1,2},{2,3},{3,4},{4,5},{5,6},{6,7},{8,9},{9,10},{10,11},{11... | collective-permute-start | bytes 221192 | tf_op jit(solution)/shard_map/ppermute | solution.py:614
  48.3 4.3 %collective-permute-start.7 = (f32[18,8,128]{2,1,0:T(8,128)S(1)}, f32[18,8,128]{2,1,0:T(8,128)S(1)}, u32[]{:S(2)}, u32[]{:S(2)}) collective-permute-start(f32[18,8,128]{2,1,0:T(8,128)S(1)} %get-tuple-element.45), channel_id=1, source_target_pairs={{1,0},{2,1},{3,2},{4,3},{5,4},{6,5},{7,6},{9,8},{10,9},{11,10},{12... | collective-permute-start | bytes 221192 | tf_op jit(solution)/shard_map/ppermute | solution.py:614

commit v5 on v4

--- a/solution.py
+++ b/solution.py
@@ -282,8 +282,7 @@
         )
 
 
-def corner_kernel(y_low, y_high, fxl, fxh, table, low_out, high_out, part):
-    part[...] = jnp.broadcast_to(table[...][None, :2], part.shape)
+def corner_kernel(y_low, y_high, fxl, fxh, low_out, high_out):
     last = fxl.shape[1] - 1
     for own, out, at, side in ((y_low, low_out, 0, LAT_DOWN), (y_high, high_out, last, LAT_UP)):
         for n in range(FACE_PLANES):
@@ -296,8 +295,7 @@
                 row += 1
 
 
-def image_corner_kernel(y_low, y_high, gxl, gxh, table, low_out, high_out, part):
-    part[...] = jnp.broadcast_to(table[...][None], part.shape)
+def image_corner_kernel(y_low, y_high, gxl, gxh, low_out, high_out):
     last = gxl.shape[1] - 1
     for own, out, at in ((y_low, low_out, 0), (y_high, high_out, last)):
         for n in range(16):
@@ -646,12 +644,12 @@
         [held(6, *block), held(6, WELLS, LANES)],
         cost=4 << 20,
     )
-    y_low, y_high, part = call(
+    y_low, y_high = call(
         corner_kernel,
-        [(FACE_PLANES + CORNER_PLANES,) + plane] * 2 + [(devices, 2, LANES)],
-        (y_low, y_high, fxl, fxh, table),
-    )
-    parts = exchanged(part)
+        [(FACE_PLANES + CORNER_PLANES,) + plane] * 2,
+        (y_low, y_high, fxl, fxh),
+    )
+    parts = lax.all_gather(table, ("gx", "gy"))
     fyl = from_behind(y_high, "gy", 1)
     fyh = from_behind(y_low, "gy", -1)
 
@@ -670,12 +668,10 @@
         [held(16, *block), held(16, WELLS, LANES)],
         cost=4 << 20,
     )
-    y_low, y_high, part = call(
-        image_corner_kernel,
-        [(18,) + plane] * 2 + [(devices, 8, LANES)],
-        (y_low, y_high, gxl, gxh, table),
-    )
-    parts = exchanged(part)
+    y_low, y_high = call(
+        image_corner_kernel, [(18,) + plane] * 2, (y_low, y_high, gxl, gxh)
+    )
+    parts = lax.all_gather(table, ("gx", "gy"))
     gyl = from_behind(y_high, "gy", 1)
     gyh = from_behind(y_low, "gy", -1)
 

time: 74.4 us -> 129 us (1.73)
  blocking collectives: 28.9 us -> 92.2 us
  starting transfers between devices: 18.5 us -> 14.2 us
  waiting for transfers between devices: 13.4 us -> 10.8 us
  Pallas kernels: 13 us -> 11 us
    all_gather x0 -> x2, blocking collectives: none -> 82.3 us  [body(): parts = lax.all_gather(table, ('gx', 'gy'))]
    all_to_all x2 -> x1, blocking collectives: 28.9 us -> 9.93 us  [exchanged(): return lax.all_to_all(part, ('gx', 'gy'), 0, 0, tiled=True)]
    all_to_all x1 -> x0, starting transfers between devices: 2.58 us -> none  [exchanged(): return lax.all_to_all(part, ('gx', 'gy'), 0, 0, tiled=True)]
    pallas_call x8, Pallas kernels: 13 us -> 11 us  [call(): pl.pallas_call(kernel, out_shape=outs, in_specs=[place(argument) for argu...]
    all_to_all x1 -> x0, waiting for transfers between devices: 1.9 us -> none  [exchanged(): return lax.all_to_all(part, ('gx', 'gy'), 0, 0, tiled=True)]
    ppermute x8, starting transfers between devices: 15.9 us -> 14.2 us  [from_behind(): lax.ppermute(value, axis, [(source, source + steps) for source in range(l...]
  transfers between devices with their start and end apart: 9 -> 8, of which waited for: 5 -> 4; matrix products, arithmetic and copies ran while one was open for 0% -> 0% of each run, Pallas kernels for 5% -> 2%
where the time goes in v5:
time: 129 us; the launch traced here: 128 us
  blocking collectives  92.2 us (71%)
  starting transfers between devices  14.2 us (11%)
  Pallas kernels  11 us (9%)
  waiting for transfers between devices  10.8 us (8%)
    all_gather x2, blocking collectives, body(): parts = lax.all_gather(table, ('gx', 'gy'))  82.3 us
    ppermute x8, starting transfers between devices, from_behind(): lax.ppermute(value, axis, [(source, source + steps) for source in range(l...  14.2 us
    pallas_call x8, Pallas kernels, call(): pl.pallas_call(kernel, out_shape=outs, in_specs=[place(argument) for argu...  11 us
    ppermute x8, waiting for transfers between devices, from_behind(): lax.ppermute(value, axis, [(source, source + steps) for source in range(l...  10.8 us
    all_to_all x1, blocking collectives, exchanged(): return lax.all_to_all(part, ('gx', 'gy'), 0, 0, tiled=True)  9.93 us
  transfers between devices with their start and end apart: 8, of which 4 were waited for; matrix products, arithmetic and copies ran while one was open for 0% of the time, Pallas kernels for 2%

profile of v5, /device:TPU:0, one launch (start us, length us, event | category | flops | bytes accessed | tf_op | source)
XLA Modules:
  0.0 128.4 jit_solution(14125109976932543421)
XLA Ops:
  0.0 0.0 copy-start.5
  0.0 0.0 copy-start.2
  0.0 0.0 copy-start.1
  0.0 0.0 copy-start.4
  0.0 0.0 copy-start
  0.0 0.0 copy-start.3
  0.0 2.2 %shard_map.64 = (f32[50,8,128]{2,1,0:T(8,128)}, f32[50,8,128]{2,1,0:T(8,128)}) custom-call(f32[6,4,8,8,128]{4,3,2,1,0:T(8,128)} %couplings.5, f32[4,8,8,128]{3,2,1,0:T(8,128)} %diagonal.5, f32[4,8,8,128]{3,2,1,0:T(8,128)} %wells.7, s32[8,8,128]{2,1,0:T(8,128)} %ids.7, f32[4,2,8,8,128]{4,3,2,1,0:T(8,128)} %right.3, f32[4,2,8,8,128]{4,3,2,1,0:T(8,128)} %guess.5), custom_call_target="tpu_custom_call" | custom-call | tf_op jit(solution)/shard_map/pallas_call | solution.py:592
  2.3 5.0 %collective-permute-start = (f32[50,8,128]{2,1,0:T(8,128)}, f32[50,8,128]{2,1,0:T(8,128)S(1)}, u32[]{:S(2)}, u32[]{:S(2)}) collective-permute-start(f32[50,8,128]{2,1,0:T(8,128)} %get-tuple-element.27), channel_id=1, source_target_pairs={{0,8},{8,16},{16,24},{1,9},{9,17},{17,25},{2,10},{10,18},{18,26},{... | collective-permute-start | bytes 614408 | tf_op jit(solution)/shard_map/ppermute | solution.py:612
  7.2 1.3 %collective-permute-start.1 = (f32[50,8,128]{2,1,0:T(8,128)}, f32[50,8,128]{2,1,0:T(8,128)S(1)}, u32[]{:S(2)}, u32[]{:S(2)}) collective-permute-start(f32[50,8,128]{2,1,0:T(8,128)} %get-tuple-element.28), channel_id=1, source_target_pairs={{8,0},{16,8},{24,16},{9,1},{17,9},{25,17},{10,2},{18,10},{26,18},{... | collective-permute-start | bytes 614408 | tf_op jit(solution)/shard_map/ppermute | solution.py:612
  8.5 0.0 copy-done.5
  8.5 0.0 copy-done.2
  8.5 0.0 copy-done.1
  8.5 0.0 copy-done.4
  8.6 0.0 copy-done
  8.6 0.0 copy-done.3
  8.6 1.4 %shard_map.65 = (f32[8,128]{1,0:T(8,128)S(1)}, s32[41]{0:T(128)S(1)}, f32[50,8,128]{2,1,0:T(8,128)S(1)}, f32[50,8,128]{2,1,0:T(8,128)S(1)}) custom-call(f32[6,4,8,8,128]{4,3,2,1,0:T(8,128)S(1)} %copy-done, f32[4,8,8,128]{3,2,1,0:T(8,128)S(1)} %copy-done.4, f32[4,8,8,128]{3,2,1,0:T(8,128)S(1)} %copy-done.2, s32[8,8,128]{2,1,0:T(8,128)S(1)} %copy-done.5, ...), custom_call_target="tpu_custom_call" | custom-call | flops 4194304 | bytes 4194304 | tf_op jit(solution)/shard_map/pallas_call | solution.py:592
  10.0 1.8 %collective-permute-done.fxl = f32[50,8,128]{2,1,0:T(8,128)S(1)} collective-permute-done((f32[50,8,128]{2,1,0:T(8,128)}, f32[50,8,128]{2,1,0:T(8,128)S(1)}, u32[]{:S(2)}, u32[]{:S(2)}) %collective-permute-start) | collective-permute-done | bytes 204832 | tf_op jit(solution)/shard_map/ppermute | solution.py:612
  11.8 4.0 %collective-permute-done.1.fxh = f32[50,8,128]{2,1,0:T(8,128)S(1)} collective-permute-done((f32[50,8,128]{2,1,0:T(8,128)}, f32[50,8,128]{2,1,0:T(8,128)S(1)}, u32[]{:S(2)}, u32[]{:S(2)}) %collective-permute-start.1) | collective-permute-done | bytes 204832 | tf_op jit(solution)/shard_map/ppermute | solution.py:612
  15.9 0.1 shard_map.66
  15.9 1.3 %collective-permute-start.2 = (f32[55,8,128]{2,1,0:T(8,128)S(1)}, f32[55,8,128]{2,1,0:T(8,128)S(1)}, u32[]{:S(2)}, u32[]{:S(2)}) collective-permute-start(f32[55,8,128]{2,1,0:T(8,128)S(1)} %get-tuple-element.31), channel_id=1, source_target_pairs={{0,1},{1,2},{2,3},{3,4},{4,5},{5,6},{6,7},{8,9},{9,10},{10,11},{11... | collective-permute-start | bytes 675848 | tf_op jit(solution)/shard_map/ppermute | solution.py:612
  17.2 1.3 %collective-permute-start.3 = (f32[55,8,128]{2,1,0:T(8,128)S(1)}, f32[55,8,128]{2,1,0:T(8,128)S(1)}, u32[]{:S(2)}, u32[]{:S(2)}) collective-permute-start(f32[55,8,128]{2,1,0:T(8,128)S(1)} %get-tuple-element.32), channel_id=1, source_target_pairs={{1,0},{2,1},{3,2},{4,3},{5,4},{6,5},{7,6},{9,8},{10,9},{11,10},{12... | collective-permute-start | bytes 675848 | tf_op jit(solution)/shard_map/ppermute | solution.py:612
  18.5 43.2 %all-gather = f32[256,128]{1,0:T(8,128)S(1)} all-gather(f32[8,128]{1,0:T(8,128)S(1)} %get-tuple-element.33), channel_id=2, replica_groups=mesh['member'=1,'gx'=4,'gy'=8] {'gx','gy'}, dimensions={0}, use_global_device_ids=true | all-gather | bytes 135168 | tf_op jit(solution)/shard_map/all_gather | solution.py:652
  61.7 0.0 collective-permute-done.2.fyl
  61.7 0.0 collective-permute-done.3.fyh
  61.7 1.0 shard_map.67
  62.7 1.3 %collective-permute-start.4 = (f32[16,8,128]{2,1,0:T(8,128)S(1)}, f32[16,8,128]{2,1,0:T(8,128)S(1)}, u32[]{:S(2)}, u32[]{:S(2)}) collective-permute-start(f32[16,8,128]{2,1,0:T(8,128)S(1)} %get-tuple-element.35), channel_id=1, source_target_pairs={{0,8},{8,16},{16,24},{1,9},{9,17},{17,25},{2,10},{10,18},{18,26},{... | collective-permute-start | bytes 196616 | tf_op jit(solution)/shard_map/ppermute | solution.py:612
  64.0 1.3 %collective-permute-start.5 = (f32[16,8,128]{2,1,0:T(8,128)S(1)}, f32[16,8,128]{2,1,0:T(8,128)S(1)}, u32[]{:S(2)}, u32[]{:S(2)}) collective-permute-start(f32[16,8,128]{2,1,0:T(8,128)S(1)} %get-tuple-element.36), channel_id=1, source_target_pairs={{8,0},{16,8},{24,16},{9,1},{17,9},{25,17},{10,2},{18,10},{26,18},{... | collective-permute-start | bytes 196616 | tf_op jit(solution)/shard_map/ppermute | solution.py:612
  65.3 0.8 collective-permute-done.4.gxl
  66.1 4.1 %collective-permute-done.5.gxh = f32[16,8,128]{2,1,0:T(8,128)S(1)} collective-permute-done((f32[16,8,128]{2,1,0:T(8,128)S(1)}, f32[16,8,128]{2,1,0:T(8,128)S(1)}, u32[]{:S(2)}, u32[]{:S(2)}) %collective-permute-start.5) | collective-permute-done | bytes 65568 | tf_op jit(solution)/shard_map/ppermute | solution.py:612
  70.2 1.4 %collective-permute-start.6 = (f32[18,8,128]{2,1,0:T(8,128)S(1)}, f32[18,8,128]{2,1,0:T(8,128)S(1)}, u32[]{:S(2)}, u32[]{:S(2)}) collective-permute-start(f32[18,8,128]{2,1,0:T(8,128)S(1)} %get-tuple-element.39), channel_id=1, source_target_pairs={{0,1},{1,2},{2,3},{3,4},{4,5},{5,6},{6,7},{8,9},{9,10},{10,11},{11... | collective-permute-start | bytes 221192 | tf_op jit(solution)/shard_map/ppermute | solution.py:612
  71.7 1.3 %collective-permute-start.7 = (f32[18,8,128]{2,1,0:T(8,128)S(1)}, f32[18,8,128]{2,1,0:T(8,128)S(1)}, u32[]{:S(2)}, u32[]{:S(2)}) collective-permute-start(f32[18,8,128]{2,1,0:T(8,128)S(1)} %get-tuple-element.40), channel_id=1, source_target_pairs={{1,0},{2,1},{3,2},{4,3},{5,4},{6,5},{7,6},{9,8},{10,9},{11,10},{12... | collective-permute-start | bytes 221192 | tf_op jit(solution)/shard_map/ppermute | solution.py:612
  73.0 1.1 shard_map.69
  74.1 39.1 %all-gather.1 = f32[256,128]{1,0:T(8,128)S(1)} all-gather(f32[8,128]{1,0:T(8,128)S(1)} %shard_map.69), channel_id=3, replica_groups=mesh['member'=1,'gx'=4,'gy'=8] {'gx','gy'}, dimensions={0}, use_global_device_ids=true | all-gather | bytes 135168 | tf_op jit(solution)/shard_map/all_gather | solution.py:674
  113.2 0.0 collective-permute-done.6.gyl
  113.2 0.0 collective-permute-done.7.gyh
  113.3 3.3 %shard_map.70 = (f32[4,2,8,8,128]{4,3,2,1,0:T(8,128)S(1)}, f32[4,2,8,8,128]{4,3,2,1,0:T(8,128)S(1)}, f32[32,8,128]{2,1,0:T(8,128)S(1)}, f32[8,128]{1,0:T(8,128)S(1)}) custom-call(f32[6,4,8,8,128]{4,3,2,1,0:T(8,128)S(1)} %copy-done, f32[4,8,8,128]{3,2,1,0:T(8,128)S(1)} %copy-done.4, f32[4,8,8,128]{3,2,1,0:T(8,128)S(1)} %copy-done.2, ...), custom_call_target="tpu_custom_call" | custom-call | tf_op jit(solution)/shard_map/pallas_call | solution.py:592
  116.6 9.9 %all_to_all.5.parts = f32[32,8,128]{2,1,0:T(8,128)S(1)} all-to-all(f32[32,8,128]{2,1,0:T(8,128)S(1)} %get-tuple-element.47), channel_id=1, replica_groups=mesh['member'=1,'gx'=4,'gy'=8] {'gx','gy'}, dimensions={0} | all-to-all | bytes 262144 | tf_op jit(solution)/shard_map/all_to_all | solution.py:616
  126.5 1.9 %shard_map.71 = f32[4,2,8,8,128]{4,3,2,1,0:T(8,128)} custom-call(f32[4,2,8,8,128]{4,3,2,1,0:T(8,128)S(1)} %copy-done.1, f32[4,2,8,8,128]{4,3,2,1,0:T(8,128)S(1)} %get-tuple-element.34.residual, f32[4,2,8,8,128]{4,3,2,1,0:T(8,128)S(1)} %get-tuple-element.45.second, f32[4,2,8,8,128]{4,3,2,1,0:T(8,128)S(1)} %get-tuple-element.46.third, ...), custom_call_target="tpu_custom_call" | custom-call | tf_op jit(solution)/shard_map/pallas_call | solution.py:592
  (1 shorter events, 0.0 us)
Async XLA Ops:
  0.0 8.5 %copy-start.5 = (s32[8,8,128]{2,1,0:T(8,128)S(1)}, s32[8,8,128]{2,1,0:T(8,128)}, u32[]{:S(2)}) copy-start(s32[8,8,128]{2,1,0:T(8,128)} %ids.7) | copy-start | bytes 98308
  0.0 8.5 %copy-start.2 = (f32[4,8,8,128]{3,2,1,0:T(8,128)S(1)}, f32[4,8,8,128]{3,2,1,0:T(8,128)}, u32[]{:S(2)}) copy-start(f32[4,8,8,128]{3,2,1,0:T(8,128)} %wells.7) | copy-start | bytes 393220
  0.0 8.5 %copy-start.1 = (f32[4,2,8,8,128]{4,3,2,1,0:T(8,128)S(1)}, f32[4,2,8,8,128]{4,3,2,1,0:T(8,128)}, u32[]{:S(2)}) copy-start(f32[4,2,8,8,128]{4,3,2,1,0:T(8,128)} %guess.5) | copy-start | bytes 786436
  0.0 8.5 %copy-start.4 = (f32[4,8,8,128]{3,2,1,0:T(8,128)S(1)}, f32[4,8,8,128]{3,2,1,0:T(8,128)}, u32[]{:S(2)}) copy-start(f32[4,8,8,128]{3,2,1,0:T(8,128)} %diagonal.5) | copy-start | bytes 393220
  0.0 8.5 %copy-start = (f32[6,4,8,8,128]{4,3,2,1,0:T(8,128)S(1)}, f32[6,4,8,8,128]{4,3,2,1,0:T(8,128)}, u32[]{:S(2)}) copy-start(f32[6,4,8,8,128]{4,3,2,1,0:T(8,128)} %couplings.5) | copy-start | bytes 2359300
  0.0 8.5 %copy-start.3 = (f32[4,2,8,8,128]{4,3,2,1,0:T(8,128)S(1)}, f32[4,2,8,8,128]{4,3,2,1,0:T(8,128)}, u32[]{:S(2)}) copy-start(f32[4,2,8,8,128]{4,3,2,1,0:T(8,128)} %right.3) | copy-start | bytes 786436
  2.3 9.6 %collective-permute-start = (f32[50,8,128]{2,1,0:T(8,128)}, f32[50,8,128]{2,1,0:T(8,128)S(1)}, u32[]{:S(2)}, u32[]{:S(2)}) collective-permute-start(f32[50,8,128]{2,1,0:T(8,128)} %get-tuple-element.27), channel_id=1, source_target_pairs={{0,8},{8,16},{16,24},{1,9},{9,17},{17,25},{2,10},{10,18},{18,26},{... | collective-permute-start | bytes 614408 | tf_op jit(solution)/shard_map/ppermute | solution.py:612
  7.2 8.6 %collective-permute-start.1 = (f32[50,8,128]{2,1,0:T(8,128)}, f32[50,8,128]{2,1,0:T(8,128)S(1)}, u32[]{:S(2)}, u32[]{:S(2)}) collective-permute-start(f32[50,8,128]{2,1,0:T(8,128)} %get-tuple-element.28), channel_id=1, source_target_pairs={{8,0},{16,8},{24,16},{9,1},{17,9},{25,17},{10,2},{18,10},{26,18},{... | collective-permute-start | bytes 614408 | tf_op jit(solution)/shard_map/ppermute | solution.py:612
  15.9 45.8 %collective-permute-start.2 = (f32[55,8,128]{2,1,0:T(8,128)S(1)}, f32[55,8,128]{2,1,0:T(8,128)S(1)}, u32[]{:S(2)}, u32[]{:S(2)}) collective-permute-start(f32[55,8,128]{2,1,0:T(8,128)S(1)} %get-tuple-element.31), channel_id=1, source_target_pairs={{0,1},{1,2},{2,3},{3,4},{4,5},{5,6},{6,7},{8,9},{9,10},{10,11},{11... | collective-permute-start | bytes 675848 | tf_op jit(solution)/shard_map/ppermute | solution.py:612
  17.2 44.5 %collective-permute-start.3 = (f32[55,8,128]{2,1,0:T(8,128)S(1)}, f32[55,8,128]{2,1,0:T(8,128)S(1)}, u32[]{:S(2)}, u32[]{:S(2)}) collective-permute-start(f32[55,8,128]{2,1,0:T(8,128)S(1)} %get-tuple-element.32), channel_id=1, source_target_pairs={{1,0},{2,1},{3,2},{4,3},{5,4},{6,5},{7,6},{9,8},{10,9},{11,10},{12... | collective-permute-start | bytes 675848 | tf_op jit(solution)/shard_map/ppermute | solution.py:612
  62.7 3.4 %collective-permute-start.4 = (f32[16,8,128]{2,1,0:T(8,128)S(1)}, f32[16,8,128]{2,1,0:T(8,128)S(1)}, u32[]{:S(2)}, u32[]{:S(2)}) collective-permute-start(f32[16,8,128]{2,1,0:T(8,128)S(1)} %get-tuple-element.35), channel_id=1, source_target_pairs={{0,8},{8,16},{16,24},{1,9},{9,17},{17,25},{2,10},{10,18},{18,26},{... | collective-permute-start | bytes 196616 | tf_op jit(solution)/shard_map/ppermute | solution.py:612
  64.0 6.2 %collective-permute-start.5 = (f32[16,8,128]{2,1,0:T(8,128)S(1)}, f32[16,8,128]{2,1,0:T(8,128)S(1)}, u32[]{:S(2)}, u32[]{:S(2)}) collective-permute-start(f32[16,8,128]{2,1,0:T(8,128)S(1)} %get-tuple-element.36), channel_id=1, source_target_pairs={{8,0},{16,8},{24,16},{9,1},{17,9},{25,17},{10,2},{18,10},{26,18},{... | collective-permute-start | bytes 196616 | tf_op jit(solution)/shard_map/ppermute | solution.py:612
  70.2 43.0 %collective-permute-start.6 = (f32[18,8,128]{2,1,0:T(8,128)S(1)}, f32[18,8,128]{2,1,0:T(8,128)S(1)}, u32[]{:S(2)}, u32[]{:S(2)}) collective-permute-start(f32[18,8,128]{2,1,0:T(8,128)S(1)} %get-tuple-element.39), channel_id=1, source_target_pairs={{0,1},{1,2},{2,3},{3,4},{4,5},{5,6},{6,7},{8,9},{9,10},{10,11},{11... | collective-permute-start | bytes 221192 | tf_op jit(solution)/shard_map/ppermute | solution.py:612
  71.7 41.6 %collective-permute-start.7 = (f32[18,8,128]{2,1,0:T(8,128)S(1)}, f32[18,8,128]{2,1,0:T(8,128)S(1)}, u32[]{:S(2)}, u32[]{:S(2)}) collective-permute-start(f32[18,8,128]{2,1,0:T(8,128)S(1)} %get-tuple-element.40), channel_id=1, source_target_pairs={{1,0},{2,1},{3,2},{4,3},{5,4},{6,5},{7,6},{9,8},{10,9},{11,10},{12... | collective-permute-start | bytes 221192 | tf_op jit(solution)/shard_map/ppermute | solution.py:612

commit v6 on v5

--- a/solution.py
+++ b/solution.py
@@ -133,15 +133,9 @@
     return ends
 
 
-def put(row_number, lane_number, value, table):
-    at = (iota(table.shape, 0) == row_number) & (iota(table.shape, 1) == lane_number)
-    return jnp.where(at, value, table)
-
-
-def full_sum(value):
-    while value.ndim > 2:
-        value = jnp.sum(value, axis=0)
-    return jnp.sum(jnp.sum(value, axis=0, keepdims=True), axis=1, keepdims=True)
+def tile_sum(first, second):
+    value = first[0] * second[0] + first[1] * second[1]
+    return jnp.sum(jnp.sum(value, axis=0), axis=0, keepdims=True)
 
 
 def list_wells(ids, present):
@@ -207,8 +201,34 @@
     return jnp.where(iota(row.shape, 1) < WELLS, row, 0.0)
 
 
-def lane(table, row_number, lane_number):
-    return table[row_number : row_number + 1, lane_number : lane_number + 1]
+def place_rows(rows, table):
+    for number, row in enumerate(rows):
+        group, k = divmod(number, RHS)
+        at = k + RHS * (group // 3)
+        placed = pltpu.roll(row, WELLS * group, 1) if group in (1, 2) else row
+        table = table + jnp.where(
+            iota(table.shape, 0) == at, jnp.broadcast_to(placed, table.shape), 0.0
+        )
+    return table
+
+
+def place_columns(dots, first_lane, table):
+    for number in range(dots.shape[0]):
+        column = jnp.sum(dots[number], axis=1, keepdims=True)
+        table = table + jnp.where(iota(table.shape, 1) == first_lane + number, column, 0.0)
+    return table
+
+
+def take_group(table, group):
+    if group in (1, 2):
+        table = pltpu.roll(table, LANES - WELLS * group, 1)
+    start = RHS * (group // 3)
+    rows = table[start : start + RHS, :]
+    return jnp.where(iota(rows.shape, 1) < WELLS, rows, 0.0)
+
+
+def take_column(table, lane):
+    return table[RHS : 2 * RHS, lane : lane + 1]
 
 
 def lane_sum(row):
@@ -307,7 +327,7 @@
 
 def guess_kernel(
     couplings, diagonal, wells, ids, right, guess,
-    table_out, present, y_low, y_high, values, scratch,
+    part, present, y_low, y_high, values, scratch,
 ):
     y_pack((couplings, diagonal, wells, ids, right, guess), (y_low, y_high))
     list_wells(ids, present)
@@ -316,7 +336,8 @@
     values[4] = wells[0] * wells[2] + wells[1] * wells[3]
     values[5] = wells[2] * wells[2] + wells[3] * wells[3]
     rows = segment_rows(ids, values, scratch, present)
-    table_out[...] = pack_rows(rows, jnp.zeros((8, LANES), jnp.float32))
+    table = pack_rows(rows, jnp.zeros((8, LANES), jnp.float32))
+    part[...] = jnp.broadcast_to(table[None, :2], part.shape)
 
 
 def residual_kernel(
@@ -379,26 +400,30 @@
     )
 
 
-def moments_kernel(wells, ids, residual, image, present, table_out, values, scratch):
-    table = jnp.zeros((8, LANES), jnp.float32)
+def moments_kernel(
+    wells, ids, residual, image, present, part, values, scratch, dots
+):
+    dots[...] = jnp.zeros_like(dots)
     for k in range(RHS):
         now = [residual[k, a] for a in range(2)]
         result = [image[k, a] for a in range(2)]
         for n, field in enumerate((now, result)):
             values[4 * n + k] = wells[0] * field[0] + wells[1] * field[1]
             values[8 + 4 * n + k] = wells[2] * field[0] + wells[3] * field[1]
-        table = put(6, k, full_sum(now[0] * now[0] + now[1] * now[1]), table)
-        table = put(6, 4 + k, full_sum(now[0] * result[0] + now[1] * result[1]), table)
-        table = put(6, 8 + k, full_sum(result[0] * result[0] + result[1] * result[1]), table)
+        row = slice(RHS + k, RHS + k + 1)
+        dots[0, row, :] = tile_sum(now, now)
+        dots[1, row, :] = tile_sum(now, result)
+        dots[2, row, :] = tile_sum(result, result)
     rows = segment_rows(ids, values, scratch, present)
-    table_out[...] = pack_rows(rows, table)
-
-
-def first_step(totals, small, k):
-    s_row, us_row = unpack_row(totals, k), unpack_row(totals, 4 + k)
-    p_row, ps_row = unpack_row(totals, 8 + k), unpack_row(totals, 12 + k)
+    table = place_rows(rows, jnp.zeros((8, LANES), jnp.float32))
+    table = place_columns(dots, WELLS, table)
+    part[...] = jnp.broadcast_to(table[None], part.shape)
+
+
+def first_step(totals, small):
+    s_row, us_row, p_row, ps_row = (take_group(totals, group) for group in range(4))
     within, equation = small[0:1, :], small[1:2, :]
-    rr, rs, ss = (lane(totals, 6, 4 * i + k) for i in range(3))
+    rr, rs, ss = (take_column(totals, WELLS + i) for i in range(3))
     height = (rs + lane_sum(p_row * s_row)) / rr
     square = ss + lane_sum(2.0 * ps_row * s_row + equation * s_row * s_row)
     left = jnp.maximum(square - height * height * rr, 1e-7 * square)
@@ -407,21 +432,28 @@
     s_second = (s_image - height * s_row) * scale
     p_second = (ps_row + equation * s_row - height * p_row) * scale
     shift = rs / rr + lane_sum(p_second * s_second)
-    return dict(
-        rr=rr, height=height, scale=scale, shift=shift, s_row=s_row, s_image=s_image,
-        p_row=p_row, p_second=p_second,
-    )
+    unit = lax.rsqrt(rr)
+    following = left * scale * unit
+    return s_row, s_image, p_row, p_second, (unit, rr * unit, height, shift, following, scale)
 
 
 def krylov_kernel(
     couplings, diagonal, wells, ids, fxl, fxh, fyl, fyh, gxl, gxh, gyl, gyh,
     residual, image, residual_faces, parts, small_in, present,
-    second_out, third_out, part, totals_out, scratch, values_scratch,
+    second_out, third_out, part, known, scratch, values_scratch, dots,
 ):
     faces, sent = (fxl, fxh, fyl, fyh), (gxl, gxh, gyl, gyh)
     totals = jnp.sum(parts[...], axis=0)
-    totals_out[...] = totals
     small = small_in[...]
+    s_rows, s_images, p_rows, p_seconds, scalars = first_step(totals, small)
+    known[0:RHS, :] = p_rows
+    known[RHS : 2 * RHS, :] = p_seconds
+    columns = jnp.zeros((RHS, LANES), jnp.float32)
+    for n, column in enumerate(scalars):
+        columns = columns + jnp.where(iota(columns.shape, 1) == n, column, 0.0)
+    known[2 * RHS : 3 * RHS, :] = columns
+    known[3 * RHS :, :] = jnp.broadcast_to(small[1:2, :], (RHS, LANES))
+    dots[...] = jnp.zeros_like(dots)
     corners = corners_of(faces, FACE_PLANES, CORNER_ROWS)
     sent_corners = corners_of(sent, 16, 8)
     all_ids = ids[...]
@@ -430,12 +462,9 @@
     corner_ids = [
         as_ids(jnp.broadcast_to(corner.row(SIDE_ID), (8, LANES))) for corner in corners
     ]
-    table = jnp.zeros((8, LANES), jnp.float32)
-    values = []
     for k in range(RHS):
-        step = first_step(totals, small, k)
-        height, scale, shift = step["height"], step["scale"], step["shift"]
-        s_row, s_image = step["s_row"], step["s_image"]
+        unit, _, height, shift, _, scale = (column[k : k + 1, :] for column in scalars)
+        s_row, s_image = s_rows[k : k + 1, :], s_images[k : k + 1, :]
         at_wells = spread(s_row, all_ids)
         now = [image[k, a] + wells[2 + a] * at_wells for a in range(2)]
         face_now, back_in = [], []
@@ -484,94 +513,93 @@
         values_scratch[k] = wells[0] * third[0] + wells[1] * third[1]
         values_scratch[4 + k] = wells[2] * third[0] + wells[3] * third[1]
         values_scratch[8 + k] = wells[2] * fourth[0] + wells[3] * fourth[1]
-        unit = lax.rsqrt(step["rr"])
         fields = [[residual[k, a] * unit for a in range(2)], second, third, fourth]
         number = 0
         for i in range(4):
             for j in range(i, 4):
-                dot = full_sum(fields[i][0] * fields[j][0] + fields[i][1] * fields[j][1])
-                table = put(4, 4 * number + k, dot, table)
+                dots[number, RHS + k : RHS + k + 1, :] = tile_sum(fields[i], fields[j])
                 number += 1
     rows = segment_rows(ids, values_scratch, scratch, present)
-    table = pack_rows(rows, table)
+    table = place_rows(rows, jnp.zeros((8, LANES), jnp.float32))
+    table = place_columns(dots, 0, table)
     part[...] = jnp.broadcast_to(table[None], part.shape)
 
 
-def solve_kernel(
-    guess, residual, second, third, parts, first_totals, small_in, solution
-):
+def solve_kernel(guess, residual, second, third, parts, known, solution):
     totals = jnp.sum(parts[...], axis=0)
-    before, small = first_totals[...], small_in[...]
-    equation = small[1:2, :]
+    s_third, p_third, p_fourth = (take_group(totals, group) for group in range(3))
+    p_first, p_second = known[0:RHS, :], known[RHS : 2 * RHS, :]
+    unit, beta, height, shift, following = (
+        known[2 * RHS : 3 * RHS, n : n + 1] for n in range(5)
+    )
+    equation = known[3 * RHS :, :]
+    gram = {}
+    number = 0
+    for i in range(4):
+        for j in range(i, 4):
+            gram[(i, j)] = take_column(totals, number)
+            number += 1
+    gram[(0, 3)] += lane_sum(p_first * s_third) * unit
+    gram[(1, 3)] += lane_sum(p_second * s_third)
+    gram[(2, 3)] += lane_sum(p_third * s_third)
+    gram[(3, 3)] += lane_sum(2.0 * p_fourth * s_third + equation * s_third * s_third)
+    tiny = 1e-30
+    inverse = [lax.rsqrt(jnp.maximum(gram[(i, i)], tiny)) for i in range(4)]
+    length = [jnp.maximum(gram[(i, i)], tiny) * inverse[i] for i in range(4)]
+    upper = {}
+    for i in range(4):
+        for j in range(i, 4):
+            entry = gram[(i, j)] * inverse[i] * inverse[j]
+            for m in range(i):
+                entry = entry - upper[(m, i)] * upper[(m, j)]
+            if i == j:
+                pivot = lax.rsqrt(jnp.maximum(entry, 1e-6))
+                upper[(i, i)] = jnp.maximum(entry, 1e-6) * pivot
+                over = pivot
+            else:
+                upper[(i, j)] = entry * over
+    columns = [
+        [(0, height * length[0]), (1, following * length[1])],
+        [(1, shift * length[1]), (2, length[2])],
+        [(2, shift * length[2]), (3, length[3])],
+    ]
+    zero = jnp.zeros_like(shift)
+    hessenberg = [[zero] * 3 for _ in range(4)]
+    for j in range(3):
+        for i in range(j + 2):
+            for m, factor in columns[j]:
+                if m >= i:
+                    hessenberg[i][j] = hessenberg[i][j] + upper[(i, m)] * factor
+    target = [beta * length[0] * upper[(0, 0)], zero, zero, zero]
+    turns = []
+    for j in range(3):
+        top, bottom = hessenberg[j][j], hessenberg[j + 1][j]
+        turn = lax.rsqrt(top * top + bottom * bottom)
+        turns.append(turn)
+        cosine, sine = top * turn, bottom * turn
+        for m in range(j, 3):
+            high, low = hessenberg[j][m], hessenberg[j + 1][m]
+            hessenberg[j][m] = cosine * high + sine * low
+            hessenberg[j + 1][m] = cosine * low - sine * high
+        high, low = target[j], target[j + 1]
+        target[j] = cosine * high + sine * low
+        target[j + 1] = cosine * low - sine * high
+    weights = [zero] * 3
+    for i in (2, 1, 0):
+        value = target[i]
+        for j in range(i + 1, 3):
+            value = value - hessenberg[i][j] * weights[j]
+        weights[i] = value * turns[i]
     for k in range(RHS):
-        step = first_step(before, small, k)
-        unit = lax.rsqrt(step["rr"])
-        beta = step["rr"] * unit
-        s_third, p_third = unpack_row(totals, k), unpack_row(totals, 4 + k)
-        p_fourth = unpack_row(totals, 8 + k)
-        gram = {}
-        number = 0
-        for i in range(4):
-            for j in range(i, 4):
-                gram[(i, j)] = lane(totals, 4, 4 * number + k)
-                number += 1
-        gram[(0, 3)] += lane_sum(step["p_row"] * s_third) * unit
-        gram[(1, 3)] += lane_sum(step["p_second"] * s_third)
-        gram[(2, 3)] += lane_sum(p_third * s_third)
-        gram[(3, 3)] += lane_sum(2.0 * p_fourth * s_third + equation * s_third * s_third)
-        tiny = 1e-30
-        inverse = [lax.rsqrt(jnp.maximum(gram[(i, i)], tiny)) for i in range(4)]
-        length = [jnp.maximum(gram[(i, i)], tiny) * inverse[i] for i in range(4)]
-        upper = {}
-        for i in range(4):
-            for j in range(i, 4):
-                entry = gram[(i, j)] * inverse[i] * inverse[j]
-                for m in range(i):
-                    entry = entry - upper[(m, i)] * upper[(m, j)]
-                if i == j:
-                    pivot = lax.rsqrt(jnp.maximum(entry, 1e-6))
-                    upper[(i, i)] = jnp.maximum(entry, 1e-6) * pivot
-                    over = pivot
-                else:
-                    upper[(i, j)] = entry * over
-        shift = step["shift"]
-        following = lax.rsqrt(step["rr"]) / step["scale"]
-        columns = [
-            [(0, step["height"] * length[0]), (1, following * length[1])],
-            [(1, shift * length[1]), (2, length[2])],
-            [(2, shift * length[2]), (3, length[3])],
-        ]
-        zero = jnp.zeros_like(shift)
-        hessenberg = [[zero] * 3 for _ in range(4)]
-        for j in range(3):
-            for i in range(j + 2):
-                for m, factor in columns[j]:
-                    if m >= i:
-                        hessenberg[i][j] = hessenberg[i][j] + upper[(i, m)] * factor
-        target = [beta * length[0] * upper[(0, 0)], zero, zero, zero]
-        for j in range(3):
-            top, bottom = hessenberg[j][j], hessenberg[j + 1][j]
-            turn = lax.rsqrt(top * top + bottom * bottom)
-            cosine, sine = top * turn, bottom * turn
-            for m in range(j, 3):
-                high, low = hessenberg[j][m], hessenberg[j + 1][m]
-                hessenberg[j][m] = cosine * high + sine * low
-                hessenberg[j + 1][m] = cosine * low - sine * high
-            high, low = target[j], target[j + 1]
-            target[j] = cosine * high + sine * low
-            target[j + 1] = cosine * low - sine * high
-        weights = [zero] * 3
-        for i in (2, 1, 0):
-            value = target[i]
-            for j in range(i + 1, 3):
-                value = value - hessenberg[i][j] * weights[j]
-            weights[i] = value / hessenberg[i][i]
+        on_first, on_second, on_third = (
+            column[k : k + 1, :] for column in (weights[0] * unit, weights[1], weights[2])
+        )
         for a in range(2):
             solution[k, a] = (
                 guess[k, a]
-                + (weights[0] * unit) * residual[k, a]
-                + weights[1] * second[k, a]
-                + weights[2] * third[k, a]
+                + on_first * residual[k, a]
+                + on_second * second[k, a]
+                + on_third * third[k, a]
             )
 
 
@@ -637,19 +665,20 @@
     )
     fxl = from_behind(x_high, "gx", 1)
     fxh = from_behind(x_low, "gx", -1)
-    table, present, y_low, y_high = call(
+    part, present, y_low, y_high = call(
         guess_kernel,
-        [plane, (WELLS + 1,)] + [(FACE_PLANES,) + plane] * 2,
+        [(devices, 2, LANES), (WELLS + 1,)] + [(FACE_PLANES,) + plane] * 2,
         arguments,
         [held(6, *block), held(6, WELLS, LANES)],
         cost=4 << 20,
     )
+    parts = exchanged(part)
     y_low, y_high = call(
         corner_kernel,
         [(FACE_PLANES + CORNER_PLANES,) + plane] * 2,
         (y_low, y_high, fxl, fxh),
-    )
-    parts = lax.all_gather(table, ("gx", "gy"))
+        cost=256 << 20,
+    )
     fyl = from_behind(y_high, "gy", 1)
     fyh = from_behind(y_low, "gy", -1)
 
@@ -661,32 +690,35 @@
     )
     gxl = from_behind(x_high, "gx", 1)
     gxh = from_behind(x_low, "gx", -1)
-    (table,) = call(
+    (part,) = call(
         moments_kernel,
-        [plane],
+        [(devices, 8, LANES)],
         (wells, ids, residual, image, present),
-        [held(16, *block), held(16, WELLS, LANES)],
+        [held(16, *block), held(16, WELLS, LANES), held(3, *plane)],
         cost=4 << 20,
     )
+    parts = exchanged(part)
     y_low, y_high = call(
-        image_corner_kernel, [(18,) + plane] * 2, (y_low, y_high, gxl, gxh)
-    )
-    parts = lax.all_gather(table, ("gx", "gy"))
+        image_corner_kernel,
+        [(18,) + plane] * 2,
+        (y_low, y_high, gxl, gxh),
+        cost=256 << 20,
+    )
     gyl = from_behind(y_high, "gy", 1)
     gyh = from_behind(y_low, "gy", -1)
 
-    second, third, part, totals = call(
+    second, third, part, known = call(
         krylov_kernel,
-        [field, field, (devices, 8, LANES), (8, LANES)],
+        [field, field, (devices, 8, LANES), (4 * RHS, LANES)],
         (couplings, diagonal, wells, ids) + faces + (gxl, gxh, gyl, gyh)
         + (residual, image, residual_faces, parts, small, present),
-        [held(12, WELLS, LANES), held(12, *block)],
+        [held(12, WELLS, LANES), held(12, *block), held(10, *plane)],
     )
     parts = exchanged(part)
     (result,) = call(
         solve_kernel,
         [field],
-        (guess, residual, second, third, parts, totals, small),
+        (guess, residual, second, third, parts, known),
     )
     return result
 

time: 129 us -> 75 us (0.58)
  blocking collectives: 92.2 us -> 30.4 us
  starting transfers between devices: 14.2 us -> 18.9 us
  waiting for transfers between devices: 10.8 us -> 14.1 us
    all_gather x2 -> x0, blocking collectives: 82.3 us -> none  [body(): parts = lax.all_gather(table, ('gx', 'gy'))]
    all_to_all x1 -> x2, blocking collectives: 9.93 us -> 30.4 us  [exchanged(): return lax.all_to_all(part, ('gx', 'gy'), 0, 0, tiled=True)]
    ppermute x8, waiting for transfers between devices: 10.8 us -> 14.1 us  [from_behind(): lax.ppermute(value, axis, [(source, source + steps) for source in range(l...]
    all_to_all x0 -> x1, starting transfers between devices: none -> 2.58 us  [exchanged(): return lax.all_to_all(part, ('gx', 'gy'), 0, 0, tiled=True)]
    ppermute x8, starting transfers between devices: 14.2 us -> 16.3 us  [from_behind(): lax.ppermute(value, axis, [(source, source + steps) for source in range(l...]
  transfers between devices with their start and end apart: 8 -> 9, of which waited for: 4 -> 5; matrix products, arithmetic and copies ran while one was open for 0% -> 0% of each run, Pallas kernels for 2% -> 2%
where the time goes in v6:
time: 75 us; the launch traced here: 74.6 us
  blocking collectives  30.4 us (41%)
  starting transfers between devices  18.9 us (25%)
  waiting for transfers between devices  14.1 us (19%)
  Pallas kernels  11 us (15%)
    all_to_all x2, blocking collectives, exchanged(): return lax.all_to_all(part, ('gx', 'gy'), 0, 0, tiled=True)  30.4 us
    ppermute x8, starting transfers between devices, from_behind(): lax.ppermute(value, axis, [(source, source + steps) for source in range(l...  16.3 us
    ppermute x8, waiting for transfers between devices, from_behind(): lax.ppermute(value, axis, [(source, source + steps) for source in range(l...  14.1 us
    pallas_call x8, Pallas kernels, call(): pl.pallas_call(kernel, out_shape=outs, in_specs=[place(argument) for argu...  11 us
    all_to_all x1, starting transfers between devices, exchanged(): return lax.all_to_all(part, ('gx', 'gy'), 0, 0, tiled=True)  2.58 us
  transfers between devices with their start and end apart: 9, of which 5 were waited for; matrix products, arithmetic and copies ran while one was open for 0% of the time, Pallas kernels for 2%

profile of v6, /device:TPU:0, one launch (start us, length us, event | category | flops | bytes accessed | tf_op | source)
XLA Modules:
  0.0 74.6 jit_solution(881882993276668547)
XLA Ops:
  0.0 0.0 copy-start.5
  0.0 0.0 copy-start.2
  0.0 0.0 copy-start.1
  0.0 0.0 copy-start.4
  0.0 0.0 copy-start
  0.0 0.0 copy-start.3
  0.0 2.2 %shard_map.64 = (f32[50,8,128]{2,1,0:T(8,128)}, f32[50,8,128]{2,1,0:T(8,128)}) custom-call(f32[6,4,8,8,128]{4,3,2,1,0:T(8,128)} %couplings.5, f32[4,8,8,128]{3,2,1,0:T(8,128)} %diagonal.5, f32[4,8,8,128]{3,2,1,0:T(8,128)} %wells.7, s32[8,8,128]{2,1,0:T(8,128)} %ids.7, f32[4,2,8,8,128]{4,3,2,1,0:T(8,128)} %right.3, f32[4,2,8,8,128]{4,3,2,1,0:T(8,128)} %guess.5), custom_call_target="tpu_custom_call" | custom-call | tf_op jit(solution)/shard_map/pallas_call | solution.py:620
  2.3 5.0 %collective-permute-start = (f32[50,8,128]{2,1,0:T(8,128)}, f32[50,8,128]{2,1,0:T(8,128)S(1)}, u32[]{:S(2)}, u32[]{:S(2)}) collective-permute-start(f32[50,8,128]{2,1,0:T(8,128)} %get-tuple-element.27), channel_id=1, source_target_pairs={{0,8},{8,16},{16,24},{1,9},{9,17},{17,25},{2,10},{10,18},{18,26},{... | collective-permute-start | bytes 614408 | tf_op jit(solution)/shard_map/ppermute | solution.py:640
  7.2 1.3 %collective-permute-start.1 = (f32[50,8,128]{2,1,0:T(8,128)}, f32[50,8,128]{2,1,0:T(8,128)S(1)}, u32[]{:S(2)}, u32[]{:S(2)}) collective-permute-start(f32[50,8,128]{2,1,0:T(8,128)} %get-tuple-element.28), channel_id=1, source_target_pairs={{8,0},{16,8},{24,16},{9,1},{17,9},{25,17},{10,2},{18,10},{26,18},{... | collective-permute-start | bytes 614408 | tf_op jit(solution)/shard_map/ppermute | solution.py:640
  8.5 0.0 copy-done.5
  8.5 0.0 copy-done.2
  8.5 0.0 copy-done.1
  8.5 0.0 copy-done.4
  8.6 0.0 copy-done
  8.6 0.0 copy-done.3
  8.6 1.6 %shard_map.65 = (f32[32,2,128]{2,1,0:T(2,128)S(1)}, s32[41]{0:T(128)S(1)}, f32[50,8,128]{2,1,0:T(8,128)S(1)}, f32[50,8,128]{2,1,0:T(8,128)S(1)}) custom-call(f32[6,4,8,8,128]{4,3,2,1,0:T(8,128)S(1)} %copy-done, f32[4,8,8,128]{3,2,1,0:T(8,128)S(1)} %copy-done.4, f32[4,8,8,128]{3,2,1,0:T(8,128)S(1)} %copy-done.2, s32[8,8,128]{2,1,0:T(8,128)S(1)} %copy-done.5, ...), custom_call_target="tpu_custom_call" | custom-call | flops 4194304 | bytes 4194304 | tf_op jit(solution)/shard_map/pallas_call | solution.py:620
  10.1 1.7 %collective-permute-done.fxl = f32[50,8,128]{2,1,0:T(8,128)S(1)} collective-permute-done((f32[50,8,128]{2,1,0:T(8,128)}, f32[50,8,128]{2,1,0:T(8,128)S(1)}, u32[]{:S(2)}, u32[]{:S(2)}) %collective-permute-start) | collective-permute-done | bytes 204832 | tf_op jit(solution)/shard_map/ppermute | solution.py:640
  11.8 4.0 %collective-permute-done.1.fxh = f32[50,8,128]{2,1,0:T(8,128)S(1)} collective-permute-done((f32[50,8,128]{2,1,0:T(8,128)}, f32[50,8,128]{2,1,0:T(8,128)S(1)}, u32[]{:S(2)}, u32[]{:S(2)}) %collective-permute-start.1) | collective-permute-done | bytes 204832 | tf_op jit(solution)/shard_map/ppermute | solution.py:640
  15.9 0.1 shard_map.66
  15.9 1.3 %collective-permute-start.2 = (f32[55,8,128]{2,1,0:T(8,128)S(1)}, f32[55,8,128]{2,1,0:T(8,128)S(1)}, u32[]{:S(2)}, u32[]{:S(2)}) collective-permute-start(f32[55,8,128]{2,1,0:T(8,128)S(1)} %get-tuple-element.31), channel_id=1, source_target_pairs={{0,1},{1,2},{2,3},{3,4},{4,5},{5,6},{6,7},{8,9},{9,10},{10,11},{11... | collective-permute-start | bytes 675848 | tf_op jit(solution)/shard_map/ppermute | solution.py:640
  17.2 1.3 %collective-permute-start.3 = (f32[55,8,128]{2,1,0:T(8,128)S(1)}, f32[55,8,128]{2,1,0:T(8,128)S(1)}, u32[]{:S(2)}, u32[]{:S(2)}) collective-permute-start(f32[55,8,128]{2,1,0:T(8,128)S(1)} %get-tuple-element.32), channel_id=1, source_target_pairs={{1,0},{2,1},{3,2},{4,3},{5,4},{6,5},{7,6},{9,8},{10,9},{11,10},{12... | collective-permute-start | bytes 675848 | tf_op jit(solution)/shard_map/ppermute | solution.py:640
  18.5 14.9 %all_to_all.15.parts = f32[32,2,128]{2,1,0:T(2,128)S(1)} all-to-all(f32[32,2,128]{2,1,0:T(2,128)S(1)} %get-tuple-element.33), channel_id=1, replica_groups=mesh['member'=1,'gx'=4,'gy'=8] {'gx','gy'}, dimensions={0} | all-to-all | bytes 65536 | tf_op jit(solution)/shard_map/all_to_all | solution.py:644
  33.4 0.0 collective-permute-done.2.fyl
  33.4 0.0 collective-permute-done.3.fyh
  33.4 0.9 %shard_map.67 = (f32[4,2,8,8,128]{4,3,2,1,0:T(8,128)S(1)}, f32[4,2,8,8,128]{4,3,2,1,0:T(8,128)S(1)}, f32[4,8,8,128]{3,2,1,0:T(8,128)S(1)}, f32[16,8,128]{2,1,0:T...) custom-call(f32[6,4,8,8,128]{4,3,2,1,0:T(8,128)S(1)} %copy-done, ...), custom_call_target="tpu_custom_call" | custom-call | tf_op jit(solution)/shard_map/pallas_call | solution.py:620
  34.3 1.8 %shard_map.69 = f32[32,8,128]{2,1,0:T(8,128)} custom-call(f32[4,8,8,128]{3,2,1,0:T(8,128)S(1)} %copy-done.2, s32[8,8,128]{2,1,0:T(8,128)S(1)} %copy-done.5, f32[4,2,8,8,128]{4,3,2,1,0:T(8,128)S(1)} %get-tuple-element.34.residual, f32[4,2,8,8,128]{4,3,2,1,0:T(8,128)S(1)} %get-tuple-element.41.image, s32[41]{0:T(128)S(1)} %get-tuple-element.43.present), custom_call_target="tpu_custom_call" | custom-call | flops 4194304 | bytes 4194304 | tf_op jit(solution)/shard_map/pallas_call | solution.py:620
  36.1 2.6 %all-to-all-start.1 = ((f32[32,8,128]{2,1,0:T(8,128)}), f32[32,8,128]{2,1,0:T(8,128)S(1)}, u32[]{:S(2)}, u32[]{:S(2)}) async-start(f32[32,8,128]{2,1,0:T(8,128)} %shard_map.69), calls=%async_computation.1 | async-start | bytes 262144 | tf_op jit(solution)/shard_map/all_to_all | solution.py:644
  38.7 3.6 %collective-permute-start.4 = (f32[16,8,128]{2,1,0:T(8,128)S(1)}, f32[16,8,128]{2,1,0:T(8,128)S(1)}, u32[]{:S(2)}, u32[]{:S(2)}) collective-permute-start(f32[16,8,128]{2,1,0:T(8,128)S(1)} %get-tuple-element.35), channel_id=1, source_target_pairs={{0,8},{8,16},{16,24},{1,9},{9,17},{17,25},{2,10},{10,18},{18,26},{... | collective-permute-start | bytes 196616 | tf_op jit(solution)/shard_map/ppermute | solution.py:640
  42.3 1.3 %collective-permute-start.5 = (f32[16,8,128]{2,1,0:T(8,128)S(1)}, f32[16,8,128]{2,1,0:T(8,128)S(1)}, u32[]{:S(2)}, u32[]{:S(2)}) collective-permute-start(f32[16,8,128]{2,1,0:T(8,128)S(1)} %get-tuple-element.36), channel_id=1, source_target_pairs={{8,0},{16,8},{24,16},{9,1},{17,9},{25,17},{10,2},{18,10},{26,18},{... | collective-permute-start | bytes 196616 | tf_op jit(solution)/shard_map/ppermute | solution.py:640
  43.6 0.6 collective-permute-done.4.gxl
  44.2 4.3 %collective-permute-done.5.gxh = f32[16,8,128]{2,1,0:T(8,128)S(1)} collective-permute-done((f32[16,8,128]{2,1,0:T(8,128)S(1)}, f32[16,8,128]{2,1,0:T(8,128)S(1)}, u32[]{:S(2)}, u32[]{:S(2)}) %collective-permute-start.5) | collective-permute-done | bytes 65568 | tf_op jit(solution)/shard_map/ppermute | solution.py:640
  48.5 1.3 %collective-permute-start.6 = (f32[18,8,128]{2,1,0:T(8,128)S(1)}, f32[18,8,128]{2,1,0:T(8,128)S(1)}, u32[]{:S(2)}, u32[]{:S(2)}) collective-permute-start(f32[18,8,128]{2,1,0:T(8,128)S(1)} %get-tuple-element.39), channel_id=1, source_target_pairs={{0,1},{1,2},{2,3},{3,4},{4,5},{5,6},{6,7},{8,9},{9,10},{10,11},{11... | collective-permute-start | bytes 221192 | tf_op jit(solution)/shard_map/ppermute | solution.py:640
  49.8 1.3 %collective-permute-start.7 = (f32[18,8,128]{2,1,0:T(8,128)S(1)}, f32[18,8,128]{2,1,0:T(8,128)S(1)}, u32[]{:S(2)}, u32[]{:S(2)}) collective-permute-start(f32[18,8,128]{2,1,0:T(8,128)S(1)} %get-tuple-element.40), channel_id=1, source_target_pairs={{1,0},{2,1},{3,2},{4,3},{5,4},{6,5},{7,6},{9,8},{10,9},{11,10},{12... | collective-permute-start | bytes 221192 | tf_op jit(solution)/shard_map/ppermute | solution.py:640
  51.1 0.0 collective-permute-done.6.gyl
  51.1 3.6 %collective-permute-done.7.gyh = f32[18,8,128]{2,1,0:T(8,128)S(1)} collective-permute-done((f32[18,8,128]{2,1,0:T(8,128)S(1)}, f32[18,8,128]{2,1,0:T(8,128)S(1)}, u32[]{:S(2)}, u32[]{:S(2)}) %collective-permute-start.7) | collective-permute-done | bytes 73760 | tf_op jit(solution)/shard_map/ppermute | solution.py:640
  54.7 0.0 all-to-all-done.1.parts
  54.7 2.7 %shard_map.70 = (f32[4,2,8,8,128]{4,3,2,1,0:T(8,128)S(1)}, f32[4,2,8,8,128]{4,3,2,1,0:T(8,128)S(1)}, f32[32,8,128]{2,1,0:T(8,128)S(1)}, f32[16,128]{1,0:T(8,128)S(1)}) custom-call(f32[6,4,8,8,128]{4,3,2,1,0:T(8,128)S(1)} %copy-done, f32[4,8,8,128]{3,2,1,0:T(8,128)S(1)} %copy-done.4, f32[4,8,8,128]{3,2,1,0:T(8,128)S(1)} %copy-done.2, ...), custom_call_target="tpu_custom_call" | custom-call | tf_op jit(solution)/shard_map/pallas_call | solution.py:620
  57.4 15.6 %all_to_all.16.parts = f32[32,8,128]{2,1,0:T(8,128)S(1)} all-to-all(f32[32,8,128]{2,1,0:T(8,128)S(1)} %get-tuple-element.47), channel_id=1, replica_groups=mesh['member'=1,'gx'=4,'gy'=8] {'gx','gy'}, dimensions={0} | all-to-all | bytes 262144 | tf_op jit(solution)/shard_map/all_to_all | solution.py:644
  73.0 1.6 %shard_map.71 = f32[4,2,8,8,128]{4,3,2,1,0:T(8,128)} custom-call(f32[4,2,8,8,128]{4,3,2,1,0:T(8,128)S(1)} %copy-done.1, f32[4,2,8,8,128]{4,3,2,1,0:T(8,128)S(1)} %get-tuple-element.34.residual, f32[4,2,8,8,128]{4,3,2,1,0:T(8,128)S(1)} %get-tuple-element.45.second, f32[4,2,8,8,128]{4,3,2,1,0:T(8,128)S(1)} %get-tuple-element.46.third, ...), custom_call_target="tpu_custom_call" | custom-call | tf_op jit(solution)/shard_map/pallas_call | solution.py:620
  (1 shorter events, 0.0 us)
Async XLA Ops:
  0.0 8.5 %copy-start.5 = (s32[8,8,128]{2,1,0:T(8,128)S(1)}, s32[8,8,128]{2,1,0:T(8,128)}, u32[]{:S(2)}) copy-start(s32[8,8,128]{2,1,0:T(8,128)} %ids.7) | copy-start | bytes 98308
  0.0 8.5 %copy-start.2 = (f32[4,8,8,128]{3,2,1,0:T(8,128)S(1)}, f32[4,8,8,128]{3,2,1,0:T(8,128)}, u32[]{:S(2)}) copy-start(f32[4,8,8,128]{3,2,1,0:T(8,128)} %wells.7) | copy-start | bytes 393220
  0.0 8.5 %copy-start.1 = (f32[4,2,8,8,128]{4,3,2,1,0:T(8,128)S(1)}, f32[4,2,8,8,128]{4,3,2,1,0:T(8,128)}, u32[]{:S(2)}) copy-start(f32[4,2,8,8,128]{4,3,2,1,0:T(8,128)} %guess.5) | copy-start | bytes 786436
  0.0 8.5 %copy-start.4 = (f32[4,8,8,128]{3,2,1,0:T(8,128)S(1)}, f32[4,8,8,128]{3,2,1,0:T(8,128)}, u32[]{:S(2)}) copy-start(f32[4,8,8,128]{3,2,1,0:T(8,128)} %diagonal.5) | copy-start | bytes 393220
  0.0 8.5 %copy-start = (f32[6,4,8,8,128]{4,3,2,1,0:T(8,128)S(1)}, f32[6,4,8,8,128]{4,3,2,1,0:T(8,128)}, u32[]{:S(2)}) copy-start(f32[6,4,8,8,128]{4,3,2,1,0:T(8,128)} %couplings.5) | copy-start | bytes 2359300
  0.0 8.6 %copy-start.3 = (f32[4,2,8,8,128]{4,3,2,1,0:T(8,128)S(1)}, f32[4,2,8,8,128]{4,3,2,1,0:T(8,128)}, u32[]{:S(2)}) copy-start(f32[4,2,8,8,128]{4,3,2,1,0:T(8,128)} %right.3) | copy-start | bytes 786436
  2.3 9.6 %collective-permute-start = (f32[50,8,128]{2,1,0:T(8,128)}, f32[50,8,128]{2,1,0:T(8,128)S(1)}, u32[]{:S(2)}, u32[]{:S(2)}) collective-permute-start(f32[50,8,128]{2,1,0:T(8,128)} %get-tuple-element.27), channel_id=1, source_target_pairs={{0,8},{8,16},{16,24},{1,9},{9,17},{17,25},{2,10},{10,18},{18,26},{... | collective-permute-start | bytes 614408 | tf_op jit(solution)/shard_map/ppermute | solution.py:640
  7.2 8.6 %collective-permute-start.1 = (f32[50,8,128]{2,1,0:T(8,128)}, f32[50,8,128]{2,1,0:T(8,128)S(1)}, u32[]{:S(2)}, u32[]{:S(2)}) collective-permute-start(f32[50,8,128]{2,1,0:T(8,128)} %get-tuple-element.28), channel_id=1, source_target_pairs={{8,0},{16,8},{24,16},{9,1},{17,9},{25,17},{10,2},{18,10},{26,18},{... | collective-permute-start | bytes 614408 | tf_op jit(solution)/shard_map/ppermute | solution.py:640
  15.9 17.5 %collective-permute-start.2 = (f32[55,8,128]{2,1,0:T(8,128)S(1)}, f32[55,8,128]{2,1,0:T(8,128)S(1)}, u32[]{:S(2)}, u32[]{:S(2)}) collective-permute-start(f32[55,8,128]{2,1,0:T(8,128)S(1)} %get-tuple-element.31), channel_id=1, source_target_pairs={{0,1},{1,2},{2,3},{3,4},{4,5},{5,6},{6,7},{8,9},{9,10},{10,11},{11... | collective-permute-start | bytes 675848 | tf_op jit(solution)/shard_map/ppermute | solution.py:640
  17.2 16.2 %collective-permute-start.3 = (f32[55,8,128]{2,1,0:T(8,128)S(1)}, f32[55,8,128]{2,1,0:T(8,128)S(1)}, u32[]{:S(2)}, u32[]{:S(2)}) collective-permute-start(f32[55,8,128]{2,1,0:T(8,128)S(1)} %get-tuple-element.32), channel_id=1, source_target_pairs={{1,0},{2,1},{3,2},{4,3},{5,4},{6,5},{7,6},{9,8},{10,9},{11,10},{12... | collective-permute-start | bytes 675848 | tf_op jit(solution)/shard_map/ppermute | solution.py:640
  36.1 18.5 %all-to-all-start.1 = ((f32[32,8,128]{2,1,0:T(8,128)}), f32[32,8,128]{2,1,0:T(8,128)S(1)}, u32[]{:S(2)}, u32[]{:S(2)}) async-start(f32[32,8,128]{2,1,0:T(8,128)} %shard_map.69), calls=%async_computation.1 | async-start | bytes 262144 | tf_op jit(solution)/shard_map/all_to_all | solution.py:644
  38.7 5.5 %collective-permute-start.4 = (f32[16,8,128]{2,1,0:T(8,128)S(1)}, f32[16,8,128]{2,1,0:T(8,128)S(1)}, u32[]{:S(2)}, u32[]{:S(2)}) collective-permute-start(f32[16,8,128]{2,1,0:T(8,128)S(1)} %get-tuple-element.35), channel_id=1, source_target_pairs={{0,8},{8,16},{16,24},{1,9},{9,17},{17,25},{2,10},{10,18},{18,26},{... | collective-permute-start | bytes 196616 | tf_op jit(solution)/shard_map/ppermute | solution.py:640
  42.3 6.2 %collective-permute-start.5 = (f32[16,8,128]{2,1,0:T(8,128)S(1)}, f32[16,8,128]{2,1,0:T(8,128)S(1)}, u32[]{:S(2)}, u32[]{:S(2)}) collective-permute-start(f32[16,8,128]{2,1,0:T(8,128)S(1)} %get-tuple-element.36), channel_id=1, source_target_pairs={{8,0},{16,8},{24,16},{9,1},{17,9},{25,17},{10,2},{18,10},{26,18},{... | collective-permute-start | bytes 196616 | tf_op jit(solution)/shard_map/ppermute | solution.py:640
  48.5 2.6 %collective-permute-start.6 = (f32[18,8,128]{2,1,0:T(8,128)S(1)}, f32[18,8,128]{2,1,0:T(8,128)S(1)}, u32[]{:S(2)}, u32[]{:S(2)}) collective-permute-start(f32[18,8,128]{2,1,0:T(8,128)S(1)} %get-tuple-element.39), channel_id=1, source_target_pairs={{0,1},{1,2},{2,3},{3,4},{4,5},{5,6},{6,7},{8,9},{9,10},{10,11},{11... | collective-permute-start | bytes 221192 | tf_op jit(solution)/shard_map/ppermute | solution.py:640
  49.8 4.9 %collective-permute-start.7 = (f32[18,8,128]{2,1,0:T(8,128)S(1)}, f32[18,8,128]{2,1,0:T(8,128)S(1)}, u32[]{:S(2)}, u32[]{:S(2)}) collective-permute-start(f32[18,8,128]{2,1,0:T(8,128)S(1)} %get-tuple-element.40), channel_id=1, source_target_pairs={{1,0},{2,1},{3,2},{4,3},{5,4},{6,5},{7,6},{9,8},{10,9},{11,10},{12... | collective-permute-start | bytes 221192 | tf_op jit(solution)/shard_map/ppermute | solution.py:640

commit v7 on v6

--- a/solution.py
+++ b/solution.py
@@ -337,7 +337,7 @@
     values[5] = wells[2] * wells[2] + wells[3] * wells[3]
     rows = segment_rows(ids, values, scratch, present)
     table = pack_rows(rows, jnp.zeros((8, LANES), jnp.float32))
-    part[...] = jnp.broadcast_to(table[None, :2], part.shape)
+    part[...] = jnp.broadcast_to(table[None], part.shape)
 
 
 def residual_kernel(
@@ -634,6 +634,21 @@
     return pltpu.VMEM(shape, jnp.float32)
 
 
+def nothing(value, other, same):
+    pass
+
+
+def after(value, other):
+    anywhere = pl.BlockSpec(memory_space=pl.ANY)
+    return pl.pallas_call(
+        nothing,
+        out_shape=jax.ShapeDtypeStruct(value.shape, value.dtype),
+        in_specs=[anywhere] * 2,
+        out_specs=anywhere,
+        input_output_aliases={0: 0},
+    )(value, other)
+
+
 def from_behind(value, axis, steps):
     count = lax.axis_size(axis)
     leading, last = (max(0, -steps), min(count, count - steps))
@@ -667,17 +682,16 @@
     fxh = from_behind(x_low, "gx", -1)
     part, present, y_low, y_high = call(
         guess_kernel,
-        [(devices, 2, LANES), (WELLS + 1,)] + [(FACE_PLANES,) + plane] * 2,
+        [(devices, 8, LANES), (WELLS + 1,)] + [(FACE_PLANES,) + plane] * 2,
         arguments,
         [held(6, *block), held(6, WELLS, LANES)],
         cost=4 << 20,
     )
-    parts = exchanged(part)
+    parts = exchanged(after(part, fxl))
     y_low, y_high = call(
         corner_kernel,
         [(FACE_PLANES + CORNER_PLANES,) + plane] * 2,
         (y_low, y_high, fxl, fxh),
-        cost=256 << 20,
     )
     fyl = from_behind(y_high, "gy", 1)
     fyh = from_behind(y_low, "gy", -1)
@@ -697,12 +711,11 @@
         [held(16, *block), held(16, WELLS, LANES), held(3, *plane)],
         cost=4 << 20,
     )
-    parts = exchanged(part)
+    parts = exchanged(after(part, gxl))
     y_low, y_high = call(
         image_corner_kernel,
         [(18,) + plane] * 2,
         (y_low, y_high, gxl, gxh),
-        cost=256 << 20,
     )
     gyl = from_behind(y_high, "gy", 1)
     gyh = from_behind(y_low, "gy", -1)

time: 75 us -> 75.3 us (level)
  blocking collectives: 30.4 us -> 14.5 us
  starting transfers between devices: 18.9 us -> 32.1 us
  local copies, waits for them, and re-layouts: 0.02 us -> 2.6 us
    all_to_all x2 -> x1, blocking collectives: 30.4 us -> 14.5 us  [exchanged(): return lax.all_to_all(part, ('gx', 'gy'), 0, 0, tiled=True)]
    all_to_all x1 -> x2, starting transfers between devices: 2.58 us -> 15.6 us  [exchanged(): return lax.all_to_all(part, ('gx', 'gy'), 0, 0, tiled=True)]
    unnamed x12 -> x24, local copies, waits for them, and re-layouts: 0.02 us -> 2.6 us
    all_to_all x1 -> x2, waiting for transfers between devices: 0.01 us -> 1.47 us  [exchanged(): return lax.all_to_all(part, ('gx', 'gy'), 0, 0, tiled=True)]
    ppermute x8, waiting for transfers between devices: 14.1 us -> 13 us  [from_behind(): lax.ppermute(value, axis, [(source, source + steps) for source in range(l...]
  transfers between devices with their start and end apart: 9 -> 10, of which waited for: 5 -> 5; matrix products, arithmetic and copies ran while one was open for 0% -> 0% of each run, Pallas kernels for 2% -> 4%
where the time goes in v7:
time: 75.3 us; the launch traced here: 74.8 us
  starting transfers between devices  32.1 us (43%)
  blocking collectives  14.5 us (19%)
  waiting for transfers between devices  14.4 us (19%)
  Pallas kernels  10.9 us (14%)
  local copies, waits for them, and re-layouts  2.6 us (3%)
    ppermute x8, starting transfers between devices, from_behind(): lax.ppermute(value, axis, [(source, source + steps) for source in range(l...  16.5 us
    all_to_all x2, starting transfers between devices, exchanged(): return lax.all_to_all(part, ('gx', 'gy'), 0, 0, tiled=True)  15.6 us
    all_to_all x1, blocking collectives, exchanged(): return lax.all_to_all(part, ('gx', 'gy'), 0, 0, tiled=True)  14.5 us
    ppermute x8, waiting for transfers between devices, from_behind(): lax.ppermute(value, axis, [(source, source + steps) for source in range(l...  13 us
    pallas_call x8, Pallas kernels, call(): pl.pallas_call(kernel, out_shape=outs, in_specs=[place(argument) for argu...  10.9 us
    unnamed x24, local copies, waits for them, and re-layouts  2.6 us
  transfers between devices with their start and end apart: 10, of which 5 were waited for; matrix products, arithmetic and copies ran while one was open for 0% of the time, Pallas kernels for 4%

profile of v7, /device:TPU:0, one launch (start us, length us, event | category | flops | bytes accessed | tf_op | source)
XLA Modules:
  0.0 74.8 jit_solution(3118348250712613138)
XLA Ops:
  0.0 0.0 copy-start.4
  0.0 0.0 copy-start.1
  0.0 0.0 copy-start.6
  0.0 0.0 copy-start
  0.0 0.0 copy-start.5
  0.0 2.2 %shard_map.64 = (f32[50,8,128]{2,1,0:T(8,128)}, f32[50,8,128]{2,1,0:T(8,128)}) custom-call(f32[6,4,8,8,128]{4,3,2,1,0:T(8,128)} %couplings.5, f32[4,8,8,128]{3,2,1,0:T(8,128)} %diagonal.5, f32[4,8,8,128]{3,2,1,0:T(8,128)} %wells.7, s32[8,8,128]{2,1,0:T(8,128)} %ids.7, f32[4,2,8,8,128]{4,3,2,1,0:T(8,128)} %right.3, f32[4,2,8,8,128]{4,3,2,1,0:T(8,128)} %guess.5), custom_call_target="tpu_custom_call" | custom-call | tf_op jit(solution)/shard_map/pallas_call | solution.py:620
  2.2 5.0 %collective-permute-start = (f32[50,8,128]{2,1,0:T(8,128)}, f32[50,8,128]{2,1,0:T(8,128)S(1)}, u32[]{:S(2)}, u32[]{:S(2)}) collective-permute-start(f32[50,8,128]{2,1,0:T(8,128)} %get-tuple-element.27), channel_id=1, source_target_pairs={{0,8},{8,16},{16,24},{1,9},{9,17},{17,25},{2,10},{10,18},{18,26},{... | collective-permute-start | bytes 614408 | tf_op jit(solution)/shard_map/ppermute | solution.py:655
  7.2 1.3 %collective-permute-start.1 = (f32[50,8,128]{2,1,0:T(8,128)}, f32[50,8,128]{2,1,0:T(8,128)S(1)}, u32[]{:S(2)}, u32[]{:S(2)}) collective-permute-start(f32[50,8,128]{2,1,0:T(8,128)} %get-tuple-element.28), channel_id=1, source_target_pairs={{8,0},{16,8},{24,16},{9,1},{17,9},{25,17},{10,2},{18,10},{26,18},{... | collective-permute-start | bytes 614408 | tf_op jit(solution)/shard_map/ppermute | solution.py:655
  8.5 0.0 copy-done.8
  8.5 0.0 copy-done.4
  8.5 0.0 copy-done.1
  8.5 0.0 copy-done.6
  8.5 0.0 copy-done
  8.6 0.0 copy-done.5
  8.6 1.9 %shard_map.65 = (f32[32,8,128]{2,1,0:T(8,128)S(1)}, s32[41]{0:T(128)S(1)}, f32[50,8,128]{2,1,0:T(8,128)S(1)}, f32[50,8,128]{2,1,0:T(8,128)S(1)}) custom-call(f32[6,4,8,8,128]{4,3,2,1,0:T(8,128)S(1)} %copy-done, f32[4,8,8,128]{3,2,1,0:T(8,128)S(1)} %copy-done.6, f32[4,8,8,128]{3,2,1,0:T(8,128)S(1)} %copy-done.4, s32[8,8,128]{2,1,0:T(8,128)S(1)} %copy-done.8, ...), custom_call_target="tpu_custom_call" | custom-call | flops 4194304 | bytes 4194304 | tf_op jit(solution)/shard_map/pallas_call | solution.py:620
  10.5 0.0 copy-start.11
  10.5 0.6 copy-done.11
  11.1 0.7 collective-permute-done.fxl.other
  11.8 0.0 copy-start.2
  11.8 0.7 copy-done.2
  12.5 6.6 %all-to-all-start = ((f32[32,8,128]{2,1,0:T(8,128)}), f32[32,8,128]{2,1,0:T(8,128)S(1)}, u32[]{:S(2)}, u32[]{:S(2)}) async-start(f32[32,8,128]{2,1,0:T(8,128)} %shard_map.67), calls=%async_computation | async-start | bytes 262144 | tf_op jit(solution)/shard_map/all_to_all | solution.py:659
  19.2 0.0 collective-permute-done.1.fxh
  19.2 0.0 copy-done.3
  19.2 0.1 shard_map.66
  19.2 2.2 %collective-permute-start.2 = (f32[55,8,128]{2,1,0:T(8,128)S(1)}, f32[55,8,128]{2,1,0:T(8,128)S(1)}, u32[]{:S(2)}, u32[]{:S(2)}) collective-permute-start(f32[55,8,128]{2,1,0:T(8,128)S(1)} %get-tuple-element.31), channel_id=1, source_target_pairs={{0,1},{1,2},{2,3},{3,4},{4,5},{5,6},{6,7},{8,9},{9,10},{10,11},{11... | collective-permute-start | bytes 675848 | tf_op jit(solution)/shard_map/ppermute | solution.py:655
  21.4 1.3 %collective-permute-start.3 = (f32[55,8,128]{2,1,0:T(8,128)S(1)}, f32[55,8,128]{2,1,0:T(8,128)S(1)}, u32[]{:S(2)}, u32[]{:S(2)}) collective-permute-start(f32[55,8,128]{2,1,0:T(8,128)S(1)} %get-tuple-element.32), channel_id=1, source_target_pairs={{1,0},{2,1},{3,2},{4,3},{5,4},{6,5},{7,6},{9,8},{10,9},{11,10},{12... | collective-permute-start | bytes 675848 | tf_op jit(solution)/shard_map/ppermute | solution.py:655
  22.7 0.0 collective-permute-done.2.fyl
  22.7 3.2 %collective-permute-done.3.fyh = f32[55,8,128]{2,1,0:T(8,128)S(1)} collective-permute-done((f32[55,8,128]{2,1,0:T(8,128)S(1)}, f32[55,8,128]{2,1,0:T(8,128)S(1)}, u32[]{:S(2)}, u32[]{:S(2)}) %collective-permute-start.3) | collective-permute-done | bytes 225312 | tf_op jit(solution)/shard_map/ppermute | solution.py:655
  25.9 1.5 %all-to-all-done.parts = f32[32,8,128]{2,1,0:T(8,128)S(1)} async-done(((f32[32,8,128]{2,1,0:T(8,128)}), f32[32,8,128]{2,1,0:T(8,128)S(1)}, u32[]{:S(2)}, u32[]{:S(2)}) %all-to-all-start) | async-done | bytes 131104 | tf_op jit(solution)/shard_map/all_to_all | solution.py:659
  27.4 0.9 %shard_map.68 = (f32[4,2,8,8,128]{4,3,2,1,0:T(8,128)S(1)}, f32[4,2,8,8,128]{4,3,2,1,0:T(8,128)S(1)}, f32[4,8,8,128]{3,2,1,0:T(8,128)S(1)}, f32[16,8,128]{2,1,0:T...) custom-call(f32[6,4,8,8,128]{4,3,2,1,0:T(8,128)S(1)} %copy-done, ...), custom_call_target="tpu_custom_call" | custom-call | tf_op jit(solution)/shard_map/pallas_call | solution.py:620
  28.3 2.6 %collective-permute-start.4 = (f32[16,8,128]{2,1,0:T(8,128)S(1)}, f32[16,8,128]{2,1,0:T(8,128)S(1)}, u32[]{:S(2)}, u32[]{:S(2)}) collective-permute-start(f32[16,8,128]{2,1,0:T(8,128)S(1)} %get-tuple-element.35), channel_id=1, source_target_pairs={{0,8},{8,16},{16,24},{1,9},{9,17},{17,25},{2,10},{10,18},{18,26},{... | collective-permute-start | bytes 196616 | tf_op jit(solution)/shard_map/ppermute | solution.py:655
  30.9 1.3 %shard_map.70.value = f32[32,8,128]{2,1,0:T(8,128)S(1)} custom-call(f32[4,8,8,128]{3,2,1,0:T(8,128)S(1)} %copy-done.4, s32[8,8,128]{2,1,0:T(8,128)S(1)} %copy-done.8, f32[4,2,8,8,128]{4,3,2,1,0:T(8,128)S(1)} %get-tuple-element.34.residual, f32[4,2,8,8,128]{4,3,2,1,0:T(8,128)S(1)} %get-tuple-element.41.image, s32[41]{0:T(128)S(1)} %get-tuple-element.43.present), custom_call_target="tpu_custom_call" | custom-call | flops 4194304 | bytes 4194304 | tf_op jit(solution)/shard_map/pallas_call | solution.py:620
  32.2 0.0 copy-start.7
  32.2 0.6 copy-done.7
  32.8 0.0 collective-permute-done.4.gxl.other
  32.8 0.6 copy-done.9
  33.4 9.0 %all-to-all-start.1 = ((f32[32,8,128]{2,1,0:T(8,128)}), f32[32,8,128]{2,1,0:T(8,128)S(1)}, u32[]{:S(2)}, u32[]{:S(2)}) async-start(f32[32,8,128]{2,1,0:T(8,128)} %shard_map.71), calls=%async_computation.1 | async-start | bytes 262144 | tf_op jit(solution)/shard_map/all_to_all | solution.py:659
  42.4 1.3 %collective-permute-start.5 = (f32[16,8,128]{2,1,0:T(8,128)S(1)}, f32[16,8,128]{2,1,0:T(8,128)S(1)}, u32[]{:S(2)}, u32[]{:S(2)}) collective-permute-start(f32[16,8,128]{2,1,0:T(8,128)S(1)} %get-tuple-element.36), channel_id=1, source_target_pairs={{8,0},{16,8},{24,16},{9,1},{17,9},{25,17},{10,2},{18,10},{26,18},{... | collective-permute-start | bytes 196616 | tf_op jit(solution)/shard_map/ppermute | solution.py:655
  43.7 5.8 %collective-permute-done.5.gxh = f32[16,8,128]{2,1,0:T(8,128)S(1)} collective-permute-done((f32[16,8,128]{2,1,0:T(8,128)S(1)}, f32[16,8,128]{2,1,0:T(8,128)S(1)}, u32[]{:S(2)}, u32[]{:S(2)}) %collective-permute-start.5) | collective-permute-done | bytes 65568 | tf_op jit(solution)/shard_map/ppermute | solution.py:655
  49.5 0.0 copy-done.10
  49.5 1.6 %collective-permute-start.6 = (f32[18,8,128]{2,1,0:T(8,128)S(1)}, f32[18,8,128]{2,1,0:T(8,128)S(1)}, u32[]{:S(2)}, u32[]{:S(2)}) collective-permute-start(f32[18,8,128]{2,1,0:T(8,128)S(1)} %get-tuple-element.39), channel_id=1, source_target_pairs={{0,1},{1,2},{2,3},{3,4},{4,5},{5,6},{6,7},{8,9},{9,10},{10,11},{11... | collective-permute-start | bytes 221192 | tf_op jit(solution)/shard_map/ppermute | solution.py:655
  51.2 1.3 %collective-permute-start.7 = (f32[18,8,128]{2,1,0:T(8,128)S(1)}, f32[18,8,128]{2,1,0:T(8,128)S(1)}, u32[]{:S(2)}, u32[]{:S(2)}) collective-permute-start(f32[18,8,128]{2,1,0:T(8,128)S(1)} %get-tuple-element.40), channel_id=1, source_target_pairs={{1,0},{2,1},{3,2},{4,3},{5,4},{6,5},{7,6},{9,8},{10,9},{11,10},{12... | collective-permute-start | bytes 221192 | tf_op jit(solution)/shard_map/ppermute | solution.py:655
  52.5 0.0 collective-permute-done.6.gyl
  52.5 3.3 %collective-permute-done.7.gyh = f32[18,8,128]{2,1,0:T(8,128)S(1)} collective-permute-done((f32[18,8,128]{2,1,0:T(8,128)S(1)}, f32[18,8,128]{2,1,0:T(8,128)S(1)}, u32[]{:S(2)}, u32[]{:S(2)}) %collective-permute-start.7) | collective-permute-done | bytes 73760 | tf_op jit(solution)/shard_map/ppermute | solution.py:655
  55.8 0.0 all-to-all-done.1.parts
  55.8 2.9 %shard_map.72 = (f32[4,2,8,8,128]{4,3,2,1,0:T(8,128)S(1)}, f32[4,2,8,8,128]{4,3,2,1,0:T(8,128)S(1)}, f32[32,8,128]{2,1,0:T(8,128)S(1)}, f32[16,128]{1,0:T(8,128)S(1)}) custom-call(f32[6,4,8,8,128]{4,3,2,1,0:T(8,128)S(1)} %copy-done, f32[4,8,8,128]{3,2,1,0:T(8,128)S(1)} %copy-done.6, f32[4,8,8,128]{3,2,1,0:T(8,128)S(1)} %copy-done.4, ...), custom_call_target="tpu_custom_call" | custom-call | tf_op jit(solution)/shard_map/pallas_call | solution.py:620
  58.7 14.5 %all_to_all.15.parts = f32[32,8,128]{2,1,0:T(8,128)S(1)} all-to-all(f32[32,8,128]{2,1,0:T(8,128)S(1)} %get-tuple-element.47), channel_id=1, replica_groups=mesh['member'=1,'gx'=4,'gy'=8] {'gx','gy'}, dimensions={0} | all-to-all | bytes 262144 | tf_op jit(solution)/shard_map/all_to_all | solution.py:659
  73.2 1.6 %shard_map.73 = f32[4,2,8,8,128]{4,3,2,1,0:T(8,128)} custom-call(f32[4,2,8,8,128]{4,3,2,1,0:T(8,128)S(1)} %copy-done.1, f32[4,2,8,8,128]{4,3,2,1,0:T(8,128)S(1)} %get-tuple-element.34.residual, f32[4,2,8,8,128]{4,3,2,1,0:T(8,128)S(1)} %get-tuple-element.45.second, f32[4,2,8,8,128]{4,3,2,1,0:T(8,128)S(1)} %get-tuple-element.46.third, ...), custom_call_target="tpu_custom_call" | custom-call | tf_op jit(solution)/shard_map/pallas_call | solution.py:620
  (7 shorter events, 0.0 us)
Async XLA Ops:
  0.0 8.5 %copy-start.8 = (s32[8,8,128]{2,1,0:T(8,128)S(1)}, s32[8,8,128]{2,1,0:T(8,128)}, u32[]{:S(2)}) copy-start(s32[8,8,128]{2,1,0:T(8,128)} %ids.7) | copy-start | bytes 98308
  0.0 8.5 %copy-start.4 = (f32[4,8,8,128]{3,2,1,0:T(8,128)S(1)}, f32[4,8,8,128]{3,2,1,0:T(8,128)}, u32[]{:S(2)}) copy-start(f32[4,8,8,128]{3,2,1,0:T(8,128)} %wells.7) | copy-start | bytes 393220
  0.0 8.5 %copy-start.1 = (f32[4,2,8,8,128]{4,3,2,1,0:T(8,128)S(1)}, f32[4,2,8,8,128]{4,3,2,1,0:T(8,128)}, u32[]{:S(2)}) copy-start(f32[4,2,8,8,128]{4,3,2,1,0:T(8,128)} %guess.5) | copy-start | bytes 786436
  0.0 8.5 %copy-start.6 = (f32[4,8,8,128]{3,2,1,0:T(8,128)S(1)}, f32[4,8,8,128]{3,2,1,0:T(8,128)}, u32[]{:S(2)}) copy-start(f32[4,8,8,128]{3,2,1,0:T(8,128)} %diagonal.5) | copy-start | bytes 393220
  0.0 8.5 %copy-start = (f32[6,4,8,8,128]{4,3,2,1,0:T(8,128)S(1)}, f32[6,4,8,8,128]{4,3,2,1,0:T(8,128)}, u32[]{:S(2)}) copy-start(f32[6,4,8,8,128]{4,3,2,1,0:T(8,128)} %couplings.5) | copy-start | bytes 2359300
  0.0 8.5 %copy-start.5 = (f32[4,2,8,8,128]{4,3,2,1,0:T(8,128)S(1)}, f32[4,2,8,8,128]{4,3,2,1,0:T(8,128)}, u32[]{:S(2)}) copy-start(f32[4,2,8,8,128]{4,3,2,1,0:T(8,128)} %right.3) | copy-start | bytes 786436
  2.2 9.6 %collective-permute-start = (f32[50,8,128]{2,1,0:T(8,128)}, f32[50,8,128]{2,1,0:T(8,128)S(1)}, u32[]{:S(2)}, u32[]{:S(2)}) collective-permute-start(f32[50,8,128]{2,1,0:T(8,128)} %get-tuple-element.27), channel_id=1, source_target_pairs={{0,8},{8,16},{16,24},{1,9},{9,17},{17,25},{2,10},{10,18},{18,26},{... | collective-permute-start | bytes 614408 | tf_op jit(solution)/shard_map/ppermute | solution.py:655
  7.2 12.0 %collective-permute-start.1 = (f32[50,8,128]{2,1,0:T(8,128)}, f32[50,8,128]{2,1,0:T(8,128)S(1)}, u32[]{:S(2)}, u32[]{:S(2)}) collective-permute-start(f32[50,8,128]{2,1,0:T(8,128)} %get-tuple-element.28), channel_id=1, source_target_pairs={{8,0},{16,8},{24,16},{9,1},{17,9},{25,17},{10,2},{18,10},{26,18},{... | collective-permute-start | bytes 614408 | tf_op jit(solution)/shard_map/ppermute | solution.py:655
  10.5 0.7 copy-start.11
  11.8 0.7 copy-start.2
  12.5 6.7 %copy-start.3 = (f32[50,8,128]{2,1,0:T(8,128)S(1)}, f32[50,8,128]{2,1,0:T(8,128)}, u32[]{:S(2)}) copy-start(f32[50,8,128]{2,1,0:T(8,128)} %copy-done.2) | copy-start | bytes 614404
  12.5 14.9 %all-to-all-start = ((f32[32,8,128]{2,1,0:T(8,128)}), f32[32,8,128]{2,1,0:T(8,128)S(1)}, u32[]{:S(2)}, u32[]{:S(2)}) async-start(f32[32,8,128]{2,1,0:T(8,128)} %shard_map.67), calls=%async_computation | async-start | bytes 262144 | tf_op jit(solution)/shard_map/all_to_all | solution.py:659
  19.2 3.5 %collective-permute-start.2 = (f32[55,8,128]{2,1,0:T(8,128)S(1)}, f32[55,8,128]{2,1,0:T(8,128)S(1)}, u32[]{:S(2)}, u32[]{:S(2)}) collective-permute-start(f32[55,8,128]{2,1,0:T(8,128)S(1)} %get-tuple-element.31), channel_id=1, source_target_pairs={{0,1},{1,2},{2,3},{3,4},{4,5},{5,6},{6,7},{8,9},{9,10},{10,11},{11... | collective-permute-start | bytes 675848 | tf_op jit(solution)/shard_map/ppermute | solution.py:655
  21.4 4.5 %collective-permute-start.3 = (f32[55,8,128]{2,1,0:T(8,128)S(1)}, f32[55,8,128]{2,1,0:T(8,128)S(1)}, u32[]{:S(2)}, u32[]{:S(2)}) collective-permute-start(f32[55,8,128]{2,1,0:T(8,128)S(1)} %get-tuple-element.32), channel_id=1, source_target_pairs={{1,0},{2,1},{3,2},{4,3},{5,4},{6,5},{7,6},{9,8},{10,9},{11,10},{12... | collective-permute-start | bytes 675848 | tf_op jit(solution)/shard_map/ppermute | solution.py:655
  28.3 4.5 %collective-permute-start.4 = (f32[16,8,128]{2,1,0:T(8,128)S(1)}, f32[16,8,128]{2,1,0:T(8,128)S(1)}, u32[]{:S(2)}, u32[]{:S(2)}) collective-permute-start(f32[16,8,128]{2,1,0:T(8,128)S(1)} %get-tuple-element.35), channel_id=1, source_target_pairs={{0,8},{8,16},{16,24},{1,9},{9,17},{17,25},{2,10},{10,18},{18,26},{... | collective-permute-start | bytes 196616 | tf_op jit(solution)/shard_map/ppermute | solution.py:655
  32.2 0.7 copy-start.7
  32.8 0.6 copy-start.9
  33.4 16.1 %copy-start.10 = (f32[16,8,128]{2,1,0:T(8,128)S(1)}, f32[16,8,128]{2,1,0:T(8,128)}, u32[]{:S(2)}) copy-start(f32[16,8,128]{2,1,0:T(8,128)} %copy-done.9) | copy-start | bytes 196612
  33.4 22.3 %all-to-all-start.1 = ((f32[32,8,128]{2,1,0:T(8,128)}), f32[32,8,128]{2,1,0:T(8,128)S(1)}, u32[]{:S(2)}, u32[]{:S(2)}) async-start(f32[32,8,128]{2,1,0:T(8,128)} %shard_map.71), calls=%async_computation.1 | async-start | bytes 262144 | tf_op jit(solution)/shard_map/all_to_all | solution.py:659
  42.4 7.1 %collective-permute-start.5 = (f32[16,8,128]{2,1,0:T(8,128)S(1)}, f32[16,8,128]{2,1,0:T(8,128)S(1)}, u32[]{:S(2)}, u32[]{:S(2)}) collective-permute-start(f32[16,8,128]{2,1,0:T(8,128)S(1)} %get-tuple-element.36), channel_id=1, source_target_pairs={{8,0},{16,8},{24,16},{9,1},{17,9},{25,17},{10,2},{18,10},{26,18},{... | collective-permute-start | bytes 196616 | tf_op jit(solution)/shard_map/ppermute | solution.py:655
  49.5 3.0 %collective-permute-start.6 = (f32[18,8,128]{2,1,0:T(8,128)S(1)}, f32[18,8,128]{2,1,0:T(8,128)S(1)}, u32[]{:S(2)}, u32[]{:S(2)}) collective-permute-start(f32[18,8,128]{2,1,0:T(8,128)S(1)} %get-tuple-element.39), channel_id=1, source_target_pairs={{0,1},{1,2},{2,3},{3,4},{4,5},{5,6},{6,7},{8,9},{9,10},{10,11},{11... | collective-permute-start | bytes 221192 | tf_op jit(solution)/shard_map/ppermute | solution.py:655
  51.2 4.6 %collective-permute-start.7 = (f32[18,8,128]{2,1,0:T(8,128)S(1)}, f32[18,8,128]{2,1,0:T(8,128)S(1)}, u32[]{:S(2)}, u32[]{:S(2)}) collective-permute-start(f32[18,8,128]{2,1,0:T(8,128)S(1)} %get-tuple-element.40), channel_id=1, source_target_pairs={{1,0},{2,1},{3,2},{4,3},{5,4},{6,5},{7,6},{9,8},{10,9},{11,10},{12... | collective-permute-start | bytes 221192 | tf_op jit(solution)/shard_map/ppermute | solution.py:655

commit v8 on v6

--- a/solution.py
+++ b/solution.py
@@ -302,7 +302,12 @@
         )
 
 
-def corner_kernel(y_low, y_high, fxl, fxh, low_out, high_out):
+def fold(parts, part):
+    part[...] = jnp.broadcast_to(jnp.sum(parts[...], axis=0)[None], part.shape)
+
+
+def corner_kernel(y_low, y_high, fxl, fxh, parts, low_out, high_out, part):
+    fold(parts, part)
     last = fxl.shape[1] - 1
     for own, out, at, side in ((y_low, low_out, 0, LAT_DOWN), (y_high, high_out, last, LAT_UP)):
         for n in range(FACE_PLANES):
@@ -315,7 +320,8 @@
                 row += 1
 
 
-def image_corner_kernel(y_low, y_high, gxl, gxh, low_out, high_out):
+def image_corner_kernel(y_low, y_high, gxl, gxh, parts, low_out, high_out, part):
+    fold(parts, part)
     last = gxl.shape[1] - 1
     for own, out, at in ((y_low, low_out, 0), (y_high, high_out, last)):
         for n in range(16):
@@ -640,12 +646,12 @@
     return lax.ppermute(value, axis, [(source, source + steps) for source in range(leading, last)])
 
 
-def exchanged(part):
-    return lax.all_to_all(part, ("gx", "gy"), 0, 0, tiled=True)
+def exchanged(part, axis):
+    return lax.all_to_all(part, axis, 0, 0, tiled=True)
 
 
 def body(couplings, diagonal, wells, ids, right, guess):
-    devices = lax.axis_size("gx") * lax.axis_size("gy")
+    across, along = lax.axis_size("gx"), lax.axis_size("gy")
     plane = (8, LANES)
     field = guess.shape
     block = guess.shape[2:]
@@ -667,18 +673,18 @@
     fxh = from_behind(x_low, "gx", -1)
     part, present, y_low, y_high = call(
         guess_kernel,
-        [(devices, 2, LANES), (WELLS + 1,)] + [(FACE_PLANES,) + plane] * 2,
+        [(across, 2, LANES), (WELLS + 1,)] + [(FACE_PLANES,) + plane] * 2,
         arguments,
         [held(6, *block), held(6, WELLS, LANES)],
         cost=4 << 20,
     )
-    parts = exchanged(part)
-    y_low, y_high = call(
+    parts = exchanged(part, "gx")
+    y_low, y_high, part = call(
         corner_kernel,
-        [(FACE_PLANES + CORNER_PLANES,) + plane] * 2,
-        (y_low, y_high, fxl, fxh),
-        cost=256 << 20,
-    )
+        [(FACE_PLANES + CORNER_PLANES,) + plane] * 2 + [(along, 2, LANES)],
+        (y_low, y_high, fxl, fxh, parts),
+    )
+    parts = exchanged(part, "gy")
     fyl = from_behind(y_high, "gy", 1)
     fyh = from_behind(y_low, "gy", -1)
 
@@ -692,29 +698,31 @@
     gxh = from_behind(x_low, "gx", -1)
     (part,) = call(
         moments_kernel,
-        [(devices, 8, LANES)],
+        [(across, 8, LANES)],
         (wells, ids, residual, image, present),
         [held(16, *block), held(16, WELLS, LANES), held(3, *plane)],
         cost=4 << 20,
     )
-    parts = exchanged(part)
-    y_low, y_high = call(
+    parts = exchanged(part, "gx")
+    y_low, y_high, part = call(
         image_corner_kernel,
-        [(18,) + plane] * 2,
-        (y_low, y_high, gxl, gxh),
-        cost=256 << 20,
-    )
+        [(18,) + plane] * 2 + [(along, 8, LANES)],
+        (y_low, y_high, gxl, gxh, parts),
+    )
+    parts = exchanged(part, "gy")
     gyl = from_behind(y_high, "gy", 1)
     gyh = from_behind(y_low, "gy", -1)
 
     second, third, part, known = call(
         krylov_kernel,
-        [field, field, (devices, 8, LANES), (4 * RHS, LANES)],
+        [field, field, (across, 8, LANES), (4 * RHS, LANES)],
         (couplings, diagonal, wells, ids) + faces + (gxl, gxh, gyl, gyh)
         + (residual, image, residual_faces, parts, small, present),
         [held(12, WELLS, LANES), held(12, *block), held(10, *plane)],
     )
-    parts = exchanged(part)
+    parts = exchanged(part, "gx")
+    (part,) = call(fold, [(along, 8, LANES)], (parts,))
+    parts = exchanged(part, "gy")
     (result,) = call(
         solve_kernel,
         [field],

time: 75 us -> 83.3 us (1.11)
  blocking collectives: 30.4 us -> 56.4 us
  waiting for transfers between devices: 14.1 us -> 0.02 us
  starting transfers between devices: 18.9 us -> 15.2 us
    all_to_all x2 -> x6, blocking collectives: 30.4 us -> 56.4 us  [exchanged(): return lax.all_to_all(part, axis, 0, 0, tiled=True)]
    ppermute x8, waiting for transfers between devices: 14.1 us -> 0.02 us  [from_behind(): lax.ppermute(value, axis, [(source, source + steps) for source in range(l...]
    all_to_all x1 -> x0, starting transfers between devices: 2.58 us -> none  [exchanged(): return lax.all_to_all(part, ('gx', 'gy'), 0, 0, tiled=True)]
    ppermute x8, starting transfers between devices: 16.3 us -> 15.2 us  [from_behind(): lax.ppermute(value, axis, [(source, source + steps) for source in range(l...]
    pallas_call x8 -> x9, Pallas kernels: 11 us -> 11.1 us  [call(): pl.pallas_call(kernel, out_shape=outs, in_specs=[place(argument) for argu...]
  transfers between devices with their start and end apart: 9 -> 8, of which waited for: 5 -> 0; matrix products, arithmetic and copies ran while one was open for 0% -> 0% of each run, Pallas kernels for 2% -> 4%
where the time goes in v8:
time: 83.3 us; the launch traced here: 82.9 us
  blocking collectives  56.4 us (68%)
  starting transfers between devices  15.2 us (18%)
  Pallas kernels  11.1 us (13%)
    all_to_all x6, blocking collectives, exchanged(): return lax.all_to_all(part, axis, 0, 0, tiled=True)  56.4 us
    ppermute x8, starting transfers between devices, from_behind(): lax.ppermute(value, axis, [(source, source + steps) for source in range(l...  15.2 us
    pallas_call x9, Pallas kernels, call(): pl.pallas_call(kernel, out_shape=outs, in_specs=[place(argument) for argu...  11.1 us
  transfers between devices with their start and end apart: 8, of which 0 were waited for; matrix products, arithmetic and copies ran while one was open for 0% of the time, Pallas kernels for 4%

profile of v8, /device:TPU:0, one launch (start us, length us, event | category | flops | bytes accessed | tf_op | source)
XLA Modules:
  0.0 82.9 jit_solution(603753138960726426)
XLA Ops:
  0.0 0.0 copy-start.5
  0.0 0.0 copy-start.2
  0.0 0.0 copy-start.1
  0.0 0.0 copy-start.4
  0.0 0.0 copy-start
  0.0 0.0 copy-start.3
  0.0 2.2 %shard_map.64 = (f32[50,8,128]{2,1,0:T(8,128)}, f32[50,8,128]{2,1,0:T(8,128)}) custom-call(f32[6,4,8,8,128]{4,3,2,1,0:T(8,128)} %couplings.5, f32[4,8,8,128]{3,2,1,0:T(8,128)} %diagonal.5, f32[4,8,8,128]{3,2,1,0:T(8,128)} %wells.7, s32[8,8,128]{2,1,0:T(8,128)} %ids.7, f32[4,2,8,8,128]{4,3,2,1,0:T(8,128)} %right.3, f32[4,2,8,8,128]{4,3,2,1,0:T(8,128)} %guess.5), custom_call_target="tpu_custom_call" | custom-call | tf_op jit(solution)/shard_map/pallas_call | solution.py:626
  2.3 5.0 %collective-permute-start = (f32[50,8,128]{2,1,0:T(8,128)}, f32[50,8,128]{2,1,0:T(8,128)S(1)}, u32[]{:S(2)}, u32[]{:S(2)}) collective-permute-start(f32[50,8,128]{2,1,0:T(8,128)} %get-tuple-element.29), channel_id=1, source_target_pairs={{0,8},{8,16},{16,24},{1,9},{9,17},{17,25},{2,10},{10,18},{18,26},{... | collective-permute-start | bytes 614408 | tf_op jit(solution)/shard_map/ppermute | solution.py:646
  7.2 1.3 %collective-permute-start.1 = (f32[50,8,128]{2,1,0:T(8,128)}, f32[50,8,128]{2,1,0:T(8,128)S(1)}, u32[]{:S(2)}, u32[]{:S(2)}) collective-permute-start(f32[50,8,128]{2,1,0:T(8,128)} %get-tuple-element.30), channel_id=1, source_target_pairs={{8,0},{16,8},{24,16},{9,1},{17,9},{25,17},{10,2},{18,10},{26,18},{... | collective-permute-start | bytes 614408 | tf_op jit(solution)/shard_map/ppermute | solution.py:646
  8.5 0.0 copy-done.5
  8.5 0.0 copy-done.2
  8.5 0.0 copy-done.1
  8.5 0.0 copy-done.4
  8.6 0.0 copy-done
  8.6 0.0 copy-done.3
  8.6 2.0 %shard_map.65 = (f32[4,2,128]{2,1,0:T(2,128)S(1)}, s32[41]{0:T(128)S(1)}, f32[50,8,128]{2,1,0:T(8,128)S(1)}, f32[50,8,128]{2,1,0:T(8,128)S(1)}) custom-call(f32[6,4,8,8,128]{4,3,2,1,0:T(8,128)S(1)} %copy-done, f32[4,8,8,128]{3,2,1,0:T(8,128)S(1)} %copy-done.4, f32[4,8,8,128]{3,2,1,0:T(8,128)S(1)} %copy-done.2, s32[8,8,128]{2,1,0:T(8,128)S(1)} %copy-done.5, ...), custom_call_target="tpu_custom_call" | custom-call | flops 4194304 | bytes 4194304 | tf_op jit(solution)/shard_map/pallas_call | solution.py:626
  10.6 10.5 %all_to_all.30.parts = f32[4,2,128]{2,1,0:T(2,128)S(1)} all-to-all(f32[4,2,128]{2,1,0:T(2,128)S(1)} %get-tuple-element.33), channel_id=1, replica_groups=mesh['member'=1,'gx'=4,'gy'=8] {'gx'}, dimensions={0} | all-to-all | bytes 8192 | tf_op jit(solution)/shard_map/all_to_all | solution.py:650
  21.1 0.0 collective-permute-done.fxl
  21.1 0.0 collective-permute-done.1.fxh
  21.1 0.1 shard_map.66
  21.2 1.3 %collective-permute-start.2 = (f32[55,8,128]{2,1,0:T(8,128)S(1)}, f32[55,8,128]{2,1,0:T(8,128)S(1)}, u32[]{:S(2)}, u32[]{:S(2)}) collective-permute-start(f32[55,8,128]{2,1,0:T(8,128)S(1)} %get-tuple-element.34), channel_id=1, source_target_pairs={{0,1},{1,2},{2,3},{3,4},{4,5},{5,6},{6,7},{8,9},{9,10},{10,11},{11... | collective-permute-start | bytes 675848 | tf_op jit(solution)/shard_map/ppermute | solution.py:646
  22.5 1.3 %collective-permute-start.3 = (f32[55,8,128]{2,1,0:T(8,128)S(1)}, f32[55,8,128]{2,1,0:T(8,128)S(1)}, u32[]{:S(2)}, u32[]{:S(2)}) collective-permute-start(f32[55,8,128]{2,1,0:T(8,128)S(1)} %get-tuple-element.35), channel_id=1, source_target_pairs={{1,0},{2,1},{3,2},{4,3},{5,4},{6,5},{7,6},{9,8},{10,9},{11,10},{12... | collective-permute-start | bytes 675848 | tf_op jit(solution)/shard_map/ppermute | solution.py:646
  23.8 11.0 %all_to_all.31.parts = f32[8,2,128]{2,1,0:T(2,128)S(1)} all-to-all(f32[8,2,128]{2,1,0:T(2,128)S(1)} %get-tuple-element.36), channel_id=1, replica_groups=mesh['member'=1,'gx'=4,'gy'=8] {'gy'}, dimensions={0} | all-to-all | bytes 16384 | tf_op jit(solution)/shard_map/all_to_all | solution.py:650
  34.8 0.0 collective-permute-done.2.fyl
  34.8 0.0 collective-permute-done.3.fyh
  34.8 0.9 %shard_map.67 = (f32[4,2,8,8,128]{4,3,2,1,0:T(8,128)S(1)}, f32[4,2,8,8,128]{4,3,2,1,0:T(8,128)S(1)}, f32[4,8,8,128]{3,2,1,0:T(8,128)S(1)}, f32[16,8,128]{2,1,0:T...) custom-call(f32[6,4,8,8,128]{4,3,2,1,0:T(8,128)S(1)} %copy-done, ...), custom_call_target="tpu_custom_call" | custom-call | tf_op jit(solution)/shard_map/pallas_call | solution.py:626
  35.8 2.5 %collective-permute-start.4 = (f32[16,8,128]{2,1,0:T(8,128)S(1)}, f32[16,8,128]{2,1,0:T(8,128)S(1)}, u32[]{:S(2)}, u32[]{:S(2)}) collective-permute-start(f32[16,8,128]{2,1,0:T(8,128)S(1)} %get-tuple-element.38), channel_id=1, source_target_pairs={{0,8},{8,16},{16,24},{1,9},{9,17},{17,25},{2,10},{10,18},{18,26},{... | collective-permute-start | bytes 196616 | tf_op jit(solution)/shard_map/ppermute | solution.py:646
  38.3 1.3 %collective-permute-start.5 = (f32[16,8,128]{2,1,0:T(8,128)S(1)}, f32[16,8,128]{2,1,0:T(8,128)S(1)}, u32[]{:S(2)}, u32[]{:S(2)}) collective-permute-start(f32[16,8,128]{2,1,0:T(8,128)S(1)} %get-tuple-element.39), channel_id=1, source_target_pairs={{8,0},{16,8},{24,16},{9,1},{17,9},{25,17},{10,2},{18,10},{26,18},{... | collective-permute-start | bytes 196616 | tf_op jit(solution)/shard_map/ppermute | solution.py:646
  39.6 1.3 %shard_map.68 = f32[4,8,128]{2,1,0:T(8,128)S(1)} custom-call(f32[4,8,8,128]{3,2,1,0:T(8,128)S(1)} %copy-done.2, s32[8,8,128]{2,1,0:T(8,128)S(1)} %copy-done.5, f32[4,2,8,8,128]{4,3,2,1,0:T(8,128)S(1)} %get-tuple-element.37.residual, f32[4,2,8,8,128]{4,3,2,1,0:T(8,128)S(1)} %get-tuple-element.42.image, s32[41]{0:T(128)S(1)} %get-tuple-element.43.present), custom_call_target="tpu_custom_call" | custom-call | flops 4194304 | bytes 4194304 | tf_op jit(solution)/shard_map/pallas_call | solution.py:626
  40.9 9.4 %all_to_all.32.parts = f32[4,8,128]{2,1,0:T(8,128)S(1)} all-to-all(f32[4,8,128]{2,1,0:T(8,128)S(1)} %shard_map.68), channel_id=1, replica_groups=mesh['member'=1,'gx'=4,'gy'=8] {'gx'}, dimensions={0} | all-to-all | bytes 32768 | tf_op jit(solution)/shard_map/all_to_all | solution.py:650
  50.2 0.0 collective-permute-done.4.gxl
  50.2 0.0 collective-permute-done.5.gxh
  50.3 1.3 %collective-permute-start.6 = (f32[18,8,128]{2,1,0:T(8,128)S(1)}, f32[18,8,128]{2,1,0:T(8,128)S(1)}, u32[]{:S(2)}, u32[]{:S(2)}) collective-permute-start(f32[18,8,128]{2,1,0:T(8,128)S(1)} %get-tuple-element.44), channel_id=1, source_target_pairs={{0,1},{1,2},{2,3},{3,4},{4,5},{5,6},{6,7},{8,9},{9,10},{10,11},{11... | collective-permute-start | bytes 221192 | tf_op jit(solution)/shard_map/ppermute | solution.py:646
  51.6 1.3 %collective-permute-start.7 = (f32[18,8,128]{2,1,0:T(8,128)S(1)}, f32[18,8,128]{2,1,0:T(8,128)S(1)}, u32[]{:S(2)}, u32[]{:S(2)}) collective-permute-start(f32[18,8,128]{2,1,0:T(8,128)S(1)} %get-tuple-element.45), channel_id=1, source_target_pairs={{1,0},{2,1},{3,2},{4,3},{5,4},{6,5},{7,6},{9,8},{10,9},{11,10},{12... | collective-permute-start | bytes 221192 | tf_op jit(solution)/shard_map/ppermute | solution.py:646
  52.9 10.3 %all_to_all.33.parts = f32[8,8,128]{2,1,0:T(8,128)S(1)} all-to-all(f32[8,8,128]{2,1,0:T(8,128)S(1)} %get-tuple-element.47), channel_id=1, replica_groups=mesh['member'=1,'gx'=4,'gy'=8] {'gy'}, dimensions={0} | all-to-all | bytes 65536 | tf_op jit(solution)/shard_map/all_to_all | solution.py:650
  63.2 0.0 collective-permute-done.6.gyl
  63.2 0.0 collective-permute-done.7.gyh
  63.2 2.9 %shard_map.70 = (f32[4,2,8,8,128]{4,3,2,1,0:T(8,128)S(1)}, f32[4,2,8,8,128]{4,3,2,1,0:T(8,128)S(1)}, f32[4,8,128]{2,1,0:T(8,128)S(1)}, f32[16,128]{1,0:T(8,128)S(1)}) custom-call(f32[6,4,8,8,128]{4,3,2,1,0:T(8,128)S(1)} %copy-done, f32[4,8,8,128]{3,2,1,0:T(8,128)S(1)} %copy-done.4, f32[4,8,8,128]{3,2,1,0:T(8,128)S(1)} %copy-done.2, ...), custom_call_target="tpu_custom_call" | custom-call | tf_op jit(solution)/shard_map/pallas_call | solution.py:626
  66.1 8.0 %all_to_all.34.parts = f32[4,8,128]{2,1,0:T(8,128)S(1)} all-to-all(f32[4,8,128]{2,1,0:T(8,128)S(1)} %get-tuple-element.51), channel_id=1, replica_groups=mesh['member'=1,'gx'=4,'gy'=8] {'gx'}, dimensions={0} | all-to-all | bytes 32768 | tf_op jit(solution)/shard_map/all_to_all | solution.py:650
  74.1 7.2 %all_to_all.35.parts = f32[8,8,128]{2,1,0:T(8,128)S(1)} all-to-all(f32[8,8,128]{2,1,0:T(8,128)S(1)} %shard_map.71), channel_id=1, replica_groups=mesh['member'=1,'gx'=4,'gy'=8] {'gy'}, dimensions={0} | all-to-all | bytes 65536 | tf_op jit(solution)/shard_map/all_to_all | solution.py:650
  81.3 1.6 %shard_map.72 = f32[4,2,8,8,128]{4,3,2,1,0:T(8,128)} custom-call(f32[4,2,8,8,128]{4,3,2,1,0:T(8,128)S(1)} %copy-done.1, f32[4,2,8,8,128]{4,3,2,1,0:T(8,128)S(1)} %get-tuple-element.37.residual, f32[4,2,8,8,128]{4,3,2,1,0:T(8,128)S(1)} %get-tuple-element.49.second, f32[4,2,8,8,128]{4,3,2,1,0:T(8,128)S(1)} %get-tuple-element.50.third, ...), custom_call_target="tpu_custom_call" | custom-call | tf_op jit(solution)/shard_map/pallas_call | solution.py:626
  (2 shorter events, 0.0 us)
Async XLA Ops:
  0.0 8.5 %copy-start.5 = (s32[8,8,128]{2,1,0:T(8,128)S(1)}, s32[8,8,128]{2,1,0:T(8,128)}, u32[]{:S(2)}) copy-start(s32[8,8,128]{2,1,0:T(8,128)} %ids.7) | copy-start | bytes 98308
  0.0 8.5 %copy-start.2 = (f32[4,8,8,128]{3,2,1,0:T(8,128)S(1)}, f32[4,8,8,128]{3,2,1,0:T(8,128)}, u32[]{:S(2)}) copy-start(f32[4,8,8,128]{3,2,1,0:T(8,128)} %wells.7) | copy-start | bytes 393220
  0.0 8.5 %copy-start.1 = (f32[4,2,8,8,128]{4,3,2,1,0:T(8,128)S(1)}, f32[4,2,8,8,128]{4,3,2,1,0:T(8,128)}, u32[]{:S(2)}) copy-start(f32[4,2,8,8,128]{4,3,2,1,0:T(8,128)} %guess.5) | copy-start | bytes 786436
  0.0 8.5 %copy-start.4 = (f32[4,8,8,128]{3,2,1,0:T(8,128)S(1)}, f32[4,8,8,128]{3,2,1,0:T(8,128)}, u32[]{:S(2)}) copy-start(f32[4,8,8,128]{3,2,1,0:T(8,128)} %diagonal.5) | copy-start | bytes 393220
  0.0 8.5 %copy-start = (f32[6,4,8,8,128]{4,3,2,1,0:T(8,128)S(1)}, f32[6,4,8,8,128]{4,3,2,1,0:T(8,128)}, u32[]{:S(2)}) copy-start(f32[6,4,8,8,128]{4,3,2,1,0:T(8,128)} %couplings.5) | copy-start | bytes 2359300
  0.0 8.5 %copy-start.3 = (f32[4,2,8,8,128]{4,3,2,1,0:T(8,128)S(1)}, f32[4,2,8,8,128]{4,3,2,1,0:T(8,128)}, u32[]{:S(2)}) copy-start(f32[4,2,8,8,128]{4,3,2,1,0:T(8,128)} %right.3) | copy-start | bytes 786436
  2.3 18.9 %collective-permute-start = (f32[50,8,128]{2,1,0:T(8,128)}, f32[50,8,128]{2,1,0:T(8,128)S(1)}, u32[]{:S(2)}, u32[]{:S(2)}) collective-permute-start(f32[50,8,128]{2,1,0:T(8,128)} %get-tuple-element.29), channel_id=1, source_target_pairs={{0,8},{8,16},{16,24},{1,9},{9,17},{17,25},{2,10},{10,18},{18,26},{... | collective-permute-start | bytes 614408 | tf_op jit(solution)/shard_map/ppermute | solution.py:646
  7.2 13.9 %collective-permute-start.1 = (f32[50,8,128]{2,1,0:T(8,128)}, f32[50,8,128]{2,1,0:T(8,128)S(1)}, u32[]{:S(2)}, u32[]{:S(2)}) collective-permute-start(f32[50,8,128]{2,1,0:T(8,128)} %get-tuple-element.30), channel_id=1, source_target_pairs={{8,0},{16,8},{24,16},{9,1},{17,9},{25,17},{10,2},{18,10},{26,18},{... | collective-permute-start | bytes 614408 | tf_op jit(solution)/shard_map/ppermute | solution.py:646
  21.2 13.6 %collective-permute-start.2 = (f32[55,8,128]{2,1,0:T(8,128)S(1)}, f32[55,8,128]{2,1,0:T(8,128)S(1)}, u32[]{:S(2)}, u32[]{:S(2)}) collective-permute-start(f32[55,8,128]{2,1,0:T(8,128)S(1)} %get-tuple-element.34), channel_id=1, source_target_pairs={{0,1},{1,2},{2,3},{3,4},{4,5},{5,6},{6,7},{8,9},{9,10},{10,11},{11... | collective-permute-start | bytes 675848 | tf_op jit(solution)/shard_map/ppermute | solution.py:646
  22.5 12.3 %collective-permute-start.3 = (f32[55,8,128]{2,1,0:T(8,128)S(1)}, f32[55,8,128]{2,1,0:T(8,128)S(1)}, u32[]{:S(2)}, u32[]{:S(2)}) collective-permute-start(f32[55,8,128]{2,1,0:T(8,128)S(1)} %get-tuple-element.35), channel_id=1, source_target_pairs={{1,0},{2,1},{3,2},{4,3},{5,4},{6,5},{7,6},{9,8},{10,9},{11,10},{12... | collective-permute-start | bytes 675848 | tf_op jit(solution)/shard_map/ppermute | solution.py:646
  35.8 14.5 %collective-permute-start.4 = (f32[16,8,128]{2,1,0:T(8,128)S(1)}, f32[16,8,128]{2,1,0:T(8,128)S(1)}, u32[]{:S(2)}, u32[]{:S(2)}) collective-permute-start(f32[16,8,128]{2,1,0:T(8,128)S(1)} %get-tuple-element.38), channel_id=1, source_target_pairs={{0,8},{8,16},{16,24},{1,9},{9,17},{17,25},{2,10},{10,18},{18,26},{... | collective-permute-start | bytes 196616 | tf_op jit(solution)/shard_map/ppermute | solution.py:646
  38.3 12.0 %collective-permute-start.5 = (f32[16,8,128]{2,1,0:T(8,128)S(1)}, f32[16,8,128]{2,1,0:T(8,128)S(1)}, u32[]{:S(2)}, u32[]{:S(2)}) collective-permute-start(f32[16,8,128]{2,1,0:T(8,128)S(1)} %get-tuple-element.39), channel_id=1, source_target_pairs={{8,0},{16,8},{24,16},{9,1},{17,9},{25,17},{10,2},{18,10},{26,18},{... | collective-permute-start | bytes 196616 | tf_op jit(solution)/shard_map/ppermute | solution.py:646
  50.3 12.9 %collective-permute-start.6 = (f32[18,8,128]{2,1,0:T(8,128)S(1)}, f32[18,8,128]{2,1,0:T(8,128)S(1)}, u32[]{:S(2)}, u32[]{:S(2)}) collective-permute-start(f32[18,8,128]{2,1,0:T(8,128)S(1)} %get-tuple-element.44), channel_id=1, source_target_pairs={{0,1},{1,2},{2,3},{3,4},{4,5},{5,6},{6,7},{8,9},{9,10},{10,11},{11... | collective-permute-start | bytes 221192 | tf_op jit(solution)/shard_map/ppermute | solution.py:646
  51.6 11.6 %collective-permute-start.7 = (f32[18,8,128]{2,1,0:T(8,128)S(1)}, f32[18,8,128]{2,1,0:T(8,128)S(1)}, u32[]{:S(2)}, u32[]{:S(2)}) collective-permute-start(f32[18,8,128]{2,1,0:T(8,128)S(1)} %get-tuple-element.45), channel_id=1, source_target_pairs={{1,0},{2,1},{3,2},{4,3},{5,4},{6,5},{7,6},{9,8},{10,9},{11,10},{12... | collective-permute-start | bytes 221192 | tf_op jit(solution)/shard_map/ppermute | solution.py:646

commit v9 on v6

--- a/solution.py
+++ b/solution.py
@@ -8,11 +8,14 @@
 WELLS = 40
 RHS = 4
 LANES = 128
-LAT_UP, LAT_DOWN, RISE, FALL, DIAGONAL = 4, 8, 12, 16, 20
-WELL_EQ, WELL_ID, GUESS, REST = 24, 26, 27, 35
-BACK_IN, BACK_EQ, BACK_ID = 43, 47, 49
-FACE_PLANES = 50
+WELL_EQ, WELL_ID, GUESS, REST, ENDS = 4, 6, 7, 15, 23
+FACE_PLANES = 23
 CORNER_PLANES = 5
+LAT_UP, LAT_DOWN, RISE, FALL, DIAGONAL = 0, 4, 8, 12, 16
+BACK_IN, BACK_EQ, BACK_ID = 20, 24, 26
+LATE_PLANES = 27
+IMAGE_PLANES = 16
+SENT_PLANES = IMAGE_PLANES + LATE_PLANES
 CORNER_ROWS = 19
 SIDE_IN, SIDE_EQ, SIDE_ID, SIDE_GUESS = 4, 8, 10, 11
 
@@ -65,9 +68,9 @@
     return result, outgoing
 
 
-def face_stencil(face, first, second, behind):
+def face_stencil(late, first, second, behind):
     def planes(start):
-        return lambda e: face[start + e]
+        return lambda e: late(start + e)
 
     result = product(planes(DIAGONAL), first, second)
     up = product(planes(LAT_UP), first, second)
@@ -235,29 +238,44 @@
     return jnp.sum(row, axis=1, keepdims=True)
 
 
+COUPLINGS, DIAGONALS, WELL_FIELDS, IDS, RIGHT_SIDE, START = range(6)
+
+
+def late_plane(cut, inward, lateral):
+    def plane(n):
+        if n < DIAGONAL:
+            return cut(COUPLINGS, ((lateral, lateral + 1, 4, 5)[n // 4], n % 4), 0)
+        if n < BACK_IN:
+            return cut(DIAGONALS, (n - DIAGONAL,), 0)
+        if n < BACK_EQ:
+            return cut(COUPLINGS, (inward, n - BACK_IN), 1)
+        if n < BACK_ID:
+            return cut(WELL_FIELDS, (2 + n - BACK_EQ,), 1)
+        return cut(IDS, (), 1).astype(jnp.float32)
+
+    return plane
+
+
 def fill_pack(pack, inward, lateral, cut):
-    couplings, diagonal, wells, ids, right, guess = range(6)
+    late = late_plane(cut, inward, lateral)
     for e in range(4):
-        pack[e] = cut(couplings, (inward, e), 0)
-        pack[LAT_UP + e] = cut(couplings, (lateral, e), 0)
-        pack[LAT_DOWN + e] = cut(couplings, (lateral + 1, e), 0)
-        pack[RISE + e] = cut(couplings, (4, e), 0)
-        pack[FALL + e] = cut(couplings, (5, e), 0)
-        pack[DIAGONAL + e] = cut(diagonal, (e,), 0)
-        pack[BACK_IN + e] = cut(couplings, (inward, e), 1)
+        pack[e] = cut(COUPLINGS, (inward, e), 0)
     for a in range(2):
-        pack[WELL_EQ + a] = cut(wells, (2 + a,), 0)
-        pack[BACK_EQ + a] = cut(wells, (2 + a,), 1)
-    pack[WELL_ID] = cut(ids, (), 0).astype(jnp.float32)
-    pack[BACK_ID] = cut(ids, (), 1).astype(jnp.float32)
+        pack[WELL_EQ + a] = cut(WELL_FIELDS, (2 + a,), 0)
+    pack[WELL_ID] = cut(IDS, (), 0).astype(jnp.float32)
     for k in range(RHS):
-        here = [cut(guess, (k, a), 0) for a in range(2)]
-        back = [cut(guess, (k, a), 1) for a in range(2)]
-        entering = product(lambda e: pack[BACK_IN + e], *back)
-        local = face_stencil(pack, here[0], here[1], entering)
+        here = [cut(START, (k, a), 0) for a in range(2)]
+        back = [cut(START, (k, a), 1) for a in range(2)]
+        entering = product(lambda e: late(BACK_IN + e), *back)
+        local = face_stencil(late, here[0], here[1], entering)
         for a in range(2):
             pack[GUESS + 2 * k + a] = here[a]
-            pack[REST + 2 * k + a] = cut(right, (k, a), 0) - local[a]
+            pack[REST + 2 * k + a] = cut(RIGHT_SIDE, (k, a), 0) - local[a]
+    if pack.shape[0] > ENDS:
+        end = pack.shape[1] - 1
+        for e in range(4):
+            pack[ENDS, e : e + 1, :] = late(LAT_UP + e)[end : end + 1, :]
+            pack[ENDS, 4 + e : 5 + e, :] = late(LAT_DOWN + e)[0:1, :]
 
 
 def x_pack_kernel(*refs):
@@ -289,59 +307,84 @@
         )
 
 
-def y_pack(arguments, packs):
+def block_packs(arguments, y_packs, x_late, y_late):
     last = arguments[-1].shape[-2] - 1
-    for end, pack in enumerate(packs):
-        fill_pack(
-            pack,
-            3 - end,
-            0,
-            lambda n, index, layer: arguments[n][
-                index + (slice(None), last - layer if end else layer, slice(None))
-            ],
-        )
+    for end in range(2):
+
+        def cut_x(n, index, layer):
+            return arguments[n][index + (last - layer if end else layer,)]
+
+        def cut_y(n, index, layer):
+            return arguments[n][index + (slice(None), last - layer if end else layer, slice(None))]
+
+        fill_pack(y_packs[end], 3 - end, 0, cut_y)
+        x_plane, y_plane = late_plane(cut_x, 1 - end, 2), late_plane(cut_y, 3 - end, 0)
+        for n in range(LATE_PLANES):
+            x_late[end][n] = x_plane(n)
+            y_late[end][n] = y_plane(n)
+
+
+def spread_kernel(table, *rest):
+    part = rest[-1]
+    part[...] = jnp.broadcast_to(table[...][None], part.shape)
 
 
 def corner_kernel(y_low, y_high, fxl, fxh, low_out, high_out):
     last = fxl.shape[1] - 1
-    for own, out, at, side in ((y_low, low_out, 0, LAT_DOWN), (y_high, high_out, last, LAT_UP)):
+    for own, out, at, side in ((y_low, low_out, 0, 4), (y_high, high_out, last, 0)):
         for n in range(FACE_PLANES):
             out[n] = own[n]
         row = FACE_PLANES * 8
         out[FACE_PLANES + CORNER_PLANES - 1] = jnp.zeros(out.shape[1:], jnp.float32)
         for face in (fxl, fxh):
-            for n in (*range(4), *range(side, side + 4), *range(WELL_EQ, REST)):
-                out[row // 8, row % 8 : row % 8 + 1, :] = face[n, at : at + 1, :]
+            rows = [(n, at) for n in range(4)]
+            rows += [(ENDS, side + e) for e in range(4)]
+            rows += [(n, at) for n in range(WELL_EQ, REST)]
+            for n, y in rows:
+                out[row // 8, row % 8 : row % 8 + 1, :] = face[n, y : y + 1, :]
                 row += 1
 
 
-def image_corner_kernel(y_low, y_high, gxl, gxh, low_out, high_out):
+def image_corner_kernel(
+    y_low, y_high, late_low, late_high, gxl, gxh, low_out, high_out
+):
     last = gxl.shape[1] - 1
-    for own, out, at in ((y_low, low_out, 0), (y_high, high_out, last)):
-        for n in range(16):
+    for own, late, out, at in (
+        (y_low, late_low, low_out, 0),
+        (y_high, late_high, high_out, last),
+    ):
+        for n in range(IMAGE_PLANES):
             out[n] = own[n]
+        for n in range(LATE_PLANES):
+            out[IMAGE_PLANES + n] = late[n]
         for x_end, face in enumerate((gxl, gxh)):
             for n in range(8):
-                out[16 + x_end, n : n + 1, :] = face[n, at : at + 1, :]
+                out[SENT_PLANES + x_end, n : n + 1, :] = face[n, at : at + 1, :]
 
 
 def guess_kernel(
     couplings, diagonal, wells, ids, right, guess,
-    part, present, y_low, y_high, values, scratch,
+    table_out, present, y_low, y_high, x_late_low, x_late_high, y_late_low, y_late_high,
+    values, scratch,
 ):
-    y_pack((couplings, diagonal, wells, ids, right, guess), (y_low, y_high))
+    block_packs(
+        (couplings, diagonal, wells, ids, right, guess),
+        (y_low, y_high),
+        (x_late_low, x_late_high),
+        (y_late_low, y_late_high),
+    )
     list_wells(ids, present)
     for k in range(RHS):
         values[k] = wells[0] * guess[k, 0] + wells[1] * guess[k, 1]
     values[4] = wells[0] * wells[2] + wells[1] * wells[3]
     values[5] = wells[2] * wells[2] + wells[3] * wells[3]
     rows = segment_rows(ids, values, scratch, present)
-    table = pack_rows(rows, jnp.zeros((8, LANES), jnp.float32))
-    part[...] = jnp.broadcast_to(table[None, :2], part.shape)
+    table_out[...] = pack_rows(rows, jnp.zeros((8, LANES), jnp.float32))
 
 
 def residual_kernel(
     couplings, diagonal, wells, ids, right, guess, fxl, fxh, fyl, fyh, parts,
+    x_late_low, x_late_high,
     residual, image, residual_faces, x_low, x_high, y_low, y_high, small,
 ):
     faces = (fxl, fxh, fyl, fyh)
@@ -395,13 +438,16 @@
             y_low[8 + 2 * k + a] = result[a][:, 1, :]
             y_high[2 * k + a] = result[a][:, last, :]
             y_high[8 + 2 * k + a] = result[a][:, last - 1, :]
+    for late, pack in ((x_late_low, x_low), (x_late_high, x_high)):
+        for n in range(LATE_PLANES):
+            pack[IMAGE_PLANES + n] = late[n]
     small[...] = jnp.concatenate(
         [unpack_row(totals, 4), unpack_row(totals, 5), jnp.zeros((6, LANES), jnp.float32)], axis=0
     )
 
 
 def moments_kernel(
-    wells, ids, residual, image, present, part, values, scratch, dots
+    wells, ids, residual, image, present, table_out, values, scratch, dots
 ):
     dots[...] = jnp.zeros_like(dots)
     for k in range(RHS):
@@ -416,8 +462,7 @@
         dots[2, row, :] = tile_sum(result, result)
     rows = segment_rows(ids, values, scratch, present)
     table = place_rows(rows, jnp.zeros((8, LANES), jnp.float32))
-    table = place_columns(dots, WELLS, table)
-    part[...] = jnp.broadcast_to(table[None], part.shape)
+    table_out[...] = place_columns(dots, WELLS, table)
 
 
 def first_step(totals, small):
@@ -455,10 +500,10 @@
     known[3 * RHS :, :] = jnp.broadcast_to(small[1:2, :], (RHS, LANES))
     dots[...] = jnp.zeros_like(dots)
     corners = corners_of(faces, FACE_PLANES, CORNER_ROWS)
-    sent_corners = corners_of(sent, 16, 8)
+    sent_corners = corners_of(sent, SENT_PLANES, 8)
     all_ids = ids[...]
     face_ids = [as_ids(face[WELL_ID]) for face in faces]
-    back_ids = [as_ids(face[BACK_ID]) for face in faces]
+    back_ids = [as_ids(got[IMAGE_PLANES + BACK_ID]) for got in sent]
     corner_ids = [
         as_ids(jnp.broadcast_to(corner.row(SIDE_ID), (8, LANES))) for corner in corners
     ]
@@ -473,8 +518,10 @@
             here = spread(s_row, face_ids[f])
             face_now.append([got[2 * k + a] + face[WELL_EQ + a] * here for a in range(2)])
             there = spread(s_row, back_ids[f])
-            back = [got[8 + 2 * k + a] + face[BACK_EQ + a] * there for a in range(2)]
-            back_in.append(product(lambda e, f=f: faces[f][BACK_IN + e], *back))
+            back = [
+                got[8 + 2 * k + a] + got[IMAGE_PLANES + BACK_EQ + a] * there for a in range(2)
+            ]
+            back_in.append(product(lambda e, f=f: sent[f][IMAGE_PLANES + BACK_IN + e], *back))
         corner_now = []
         for c in range(4):
             here = spread(s_row, corner_ids[c])[0:1, :]
@@ -499,7 +546,9 @@
         incoming = []
         for f in range(4):
             face = faces[f]
-            there = face_stencil(face, face_now[f][0], face_now[f][1], back_in[f])
+            there = face_stencil(
+                lambda n, f=f: sent[f][IMAGE_PLANES + n], *face_now[f], back_in[f]
+            )
             over = face_entries(ends[(f, 0)], ends[(f, 1)], outgoing[f])
             here = spread(s_image, face_ids[f])
             outer = []
@@ -657,7 +706,7 @@
         ends += [pltpu.VMEM(shape, argument.dtype)] * 2
     x_low, x_high = call(
         x_pack_kernel,
-        [(FACE_PLANES,) + plane] * 2,
+        [(FACE_PLANES + 1,) + plane] * 2,
         arguments,
         ends + [pltpu.SemaphoreType.DMA((len(ends),))],
         own_copies=True,
@@ -665,19 +714,19 @@
     )
     fxl = from_behind(x_high, "gx", 1)
     fxh = from_behind(x_low, "gx", -1)
-    part, present, y_low, y_high = call(
+    table, present, y_low, y_high, *late = call(
         guess_kernel,
-        [(devices, 2, LANES), (WELLS + 1,)] + [(FACE_PLANES,) + plane] * 2,
+        [plane, (WELLS + 1,)] + [(FACE_PLANES,) + plane] * 2 + [(LATE_PLANES,) + plane] * 4,
         arguments,
         [held(6, *block), held(6, WELLS, LANES)],
         cost=4 << 20,
     )
+    (part,) = call(spread_kernel, [(devices, 8, LANES)], (table, fxl))
     parts = exchanged(part)
     y_low, y_high = call(
         corner_kernel,
         [(FACE_PLANES + CORNER_PLANES,) + plane] * 2,
         (y_low, y_high, fxl, fxh),
-        cost=256 << 20,
     )
     fyl = from_behind(y_high, "gy", 1)
     fyh = from_behind(y_low, "gy", -1)
@@ -685,24 +734,27 @@
     faces = (fxl, fxh, fyl, fyh)
     residual, image, residual_faces, x_low, x_high, y_low, y_high, small = call(
         residual_kernel,
-        [field, field, (4, 8) + plane] + [(16,) + plane] * 4 + [(8, LANES)],
-        arguments + faces + (parts,),
+        [field, field, (4, 8) + plane]
+        + [(SENT_PLANES,) + plane] * 2
+        + [(IMAGE_PLANES,) + plane] * 2
+        + [(8, LANES)],
+        arguments + faces + (parts, late[0], late[1]),
     )
     gxl = from_behind(x_high, "gx", 1)
     gxh = from_behind(x_low, "gx", -1)
-    (part,) = call(
+    (table,) = call(
         moments_kernel,
-        [(devices, 8, LANES)],
+        [plane],
         (wells, ids, residual, image, present),
         [held(16, *block), held(16, WELLS, LANES), held(3, *plane)],
         cost=4 << 20,
     )
+    (part,) = call(spread_kernel, [(devices, 8, LANES)], (table, gxl, gxh))
     parts = exchanged(part)
     y_low, y_high = call(
         image_corner_kernel,
-        [(18,) + plane] * 2,
-        (y_low, y_high, gxl, gxh),
-        cost=256 << 20,
+        [(SENT_PLANES + 2,) + plane] * 2,
+        (y_low, y_high, late[2], late[3], gxl, gxh),
     )
     gyl = from_behind(y_high, "gy", 1)
     gyh = from_behind(y_low, "gy", -1)

time: 75 us -> 78.1 us (1.041)
  blocking collectives: 30.4 us -> 15.4 us
  starting transfers between devices: 18.9 us -> 29.9 us
  waiting for transfers between devices: 14.1 us -> 19.2 us
  Pallas kernels: 11 us -> 12.9 us
    all_to_all x2 -> x1, blocking collectives: 30.4 us -> 15.4 us  [exchanged(): return lax.all_to_all(part, ('gx', 'gy'), 0, 0, tiled=True)]
    all_to_all x1 -> x2, starting transfers between devices: 2.58 us -> 12.6 us  [exchanged(): return lax.all_to_all(part, ('gx', 'gy'), 0, 0, tiled=True)]
    ppermute x8, waiting for transfers between devices: 14.1 us -> 17.6 us  [from_behind(): lax.ppermute(value, axis, [(source, source + steps) for source in range(l...]
    pallas_call x8 -> x10, Pallas kernels: 11 us -> 12.9 us  [call(): pl.pallas_call(kernel, out_shape=outs, in_specs=[place(argument) for argu...]
    all_to_all x1 -> x2, waiting for transfers between devices: 0.01 us -> 1.57 us  [exchanged(): return lax.all_to_all(part, ('gx', 'gy'), 0, 0, tiled=True)]
    ppermute x8, starting transfers between devices: 16.3 us -> 17.3 us  [from_behind(): lax.ppermute(value, axis, [(source, source + steps) for source in range(l...]
  transfers between devices with their start and end apart: 9 -> 10, of which waited for: 5 -> 6; matrix products, arithmetic and copies ran while one was open for 0% -> 0% of each run, Pallas kernels for 2% -> 5%
where the time goes in v9:
time: 78.1 us; the launch traced here: 77.6 us
  starting transfers between devices  29.9 us (38%)
  waiting for transfers between devices  19.2 us (25%)
  blocking collectives  15.4 us (20%)
  Pallas kernels  12.9 us (17%)
    ppermute x8, waiting for transfers between devices, from_behind(): lax.ppermute(value, axis, [(source, source + steps) for source in range(l...  17.6 us
    ppermute x8, starting transfers between devices, from_behind(): lax.ppermute(value, axis, [(source, source + steps) for source in range(l...  17.3 us
    all_to_all x1, blocking collectives, exchanged(): return lax.all_to_all(part, ('gx', 'gy'), 0, 0, tiled=True)  15.4 us
    pallas_call x10, Pallas kernels, call(): pl.pallas_call(kernel, out_shape=outs, in_specs=[place(argument) for argu...  12.9 us
    all_to_all x2, starting transfers between devices, exchanged(): return lax.all_to_all(part, ('gx', 'gy'), 0, 0, tiled=True)  12.6 us
    all_to_all x2, waiting for transfers between devices, exchanged(): return lax.all_to_all(part, ('gx', 'gy'), 0, 0, tiled=True)  1.57 us
  transfers between devices with their start and end apart: 10, of which 6 were waited for; matrix products, arithmetic and copies ran while one was open for 0% of the time, Pallas kernels for 5%

profile of v9, /device:TPU:0, one launch (start us, length us, event | category | flops | bytes accessed | tf_op | source)
XLA Modules:
  0.0 77.6 jit_solution(9747990086348562939)
XLA Ops:
  0.0 0.0 copy-start.5
  0.0 0.0 copy-start.2
  0.0 0.0 copy-start.1
  0.0 0.0 copy-start.4
  0.0 0.0 copy-start
  0.0 0.0 copy-start.3
  0.0 2.2 %shard_map.64 = (f32[24,8,128]{2,1,0:T(8,128)}, f32[24,8,128]{2,1,0:T(8,128)}) custom-call(f32[6,4,8,8,128]{4,3,2,1,0:T(8,128)} %couplings.5, f32[4,8,8,128]{3,2,1,0:T(8,128)} %diagonal.5, f32[4,8,8,128]{3,2,1,0:T(8,128)} %wells.7, s32[8,8,128]{2,1,0:T(8,128)} %ids.7, f32[4,2,8,8,128]{4,3,2,1,0:T(8,128)} %right.3, f32[4,2,8,8,128]{4,3,2,1,0:T(8,128)} %guess.5), custom_call_target="tpu_custom_call" | custom-call | tf_op jit(solution)/shard_map/pallas_call | solution.py:669
  2.2 4.9 %collective-permute-start = (f32[24,8,128]{2,1,0:T(8,128)}, f32[24,8,128]{2,1,0:T(8,128)S(1)}, u32[]{:S(2)}, u32[]{:S(2)}) collective-permute-start(f32[24,8,128]{2,1,0:T(8,128)} %get-tuple-element.31), channel_id=1, source_target_pairs={{0,8},{8,16},{16,24},{1,9},{9,17},{17,25},{2,10},{10,18},{18,26},{... | collective-permute-start | bytes 294920 | tf_op jit(solution)/shard_map/ppermute | solution.py:689
  7.1 0.0 copy-done.5
  7.1 0.0 copy-done.2
  7.2 0.0 copy-done.1
  7.2 0.0 copy-done.4
  7.2 0.0 copy-done
  7.2 0.0 copy-done.3
  7.2 2.5 %shard_map.65 = (f32[8,128]{1,0:T(8,128)S(1)}, s32[41]{0:T(128)S(1)}, f32[23,8,128]{2,1,0:T(8,128)S(1)}, f32[23,8,128]{2,1,0:T(8,128)S(1)}, f32[27,8,128]{2,1,0:...) custom-call(f32[6,4,8,8,128]{4,3,2,1,0:T(8,128)S(1)} %copy-done, ...), custom_call_target="tpu_custom_call" | custom-call | flops 4194304 | bytes 4194304 | tf_op jit(solution)/shard_map/pallas_call | solution.py:669
  9.7 0.0 collective-permute-done.fxl.rest_0_
  9.8 0.7 shard_map.67
  10.4 0.0 copy-start.6
  10.4 6.5 %all-to-all-start = ((f32[32,8,128]{2,1,0:T(8,128)}), f32[32,8,128]{2,1,0:T(8,128)S(1)}, u32[]{:S(2)}, u32[]{:S(2)}) async-start(f32[32,8,128]{2,1,0:T(8,128)} %shard_map.67), calls=%async_computation | async-start | bytes 262144 | tf_op jit(solution)/shard_map/all_to_all | solution.py:693
  16.9 0.0 copy-done.6
  16.9 1.3 %collective-permute-start.1 = (f32[24,8,128]{2,1,0:T(8,128)S(1)}, f32[24,8,128]{2,1,0:T(8,128)S(1)}, u32[]{:S(2)}, u32[]{:S(2)}) collective-permute-start(f32[24,8,128]{2,1,0:T(8,128)S(1)} %copy-done.6), channel_id=1, source_target_pairs={{8,0},{16,8},{24,16},{9,1},{17,9},{25,17},{10,2},{18,10},{26,18},{... | collective-permute-start | bytes 294920 | tf_op jit(solution)/shard_map/ppermute | solution.py:689
  18.2 6.5 %collective-permute-done.1.fxh = f32[24,8,128]{2,1,0:T(8,128)S(1)} collective-permute-done((f32[24,8,128]{2,1,0:T(8,128)S(1)}, f32[24,8,128]{2,1,0:T(8,128)S(1)}, u32[]{:S(2)}, u32[]{:S(2)}) %collective-permute-start.1) | collective-permute-done | bytes 98336 | tf_op jit(solution)/shard_map/ppermute | solution.py:689
  24.7 1.7 %collective-permute-start.2 = (f32[28,8,128]{2,1,0:T(8,128)S(1)}, f32[28,8,128]{2,1,0:T(8,128)S(1)}, u32[]{:S(2)}, u32[]{:S(2)}) collective-permute-start(f32[28,8,128]{2,1,0:T(8,128)S(1)} %get-tuple-element.35), channel_id=1, source_target_pairs={{0,1},{1,2},{2,3},{3,4},{4,5},{5,6},{6,7},{8,9},{9,10},{10,11},{11... | collective-permute-start | bytes 344072 | tf_op jit(solution)/shard_map/ppermute | solution.py:689
  26.4 1.3 %collective-permute-start.3 = (f32[28,8,128]{2,1,0:T(8,128)S(1)}, f32[28,8,128]{2,1,0:T(8,128)S(1)}, u32[]{:S(2)}, u32[]{:S(2)}) collective-permute-start(f32[28,8,128]{2,1,0:T(8,128)S(1)} %get-tuple-element.36), channel_id=1, source_target_pairs={{1,0},{2,1},{3,2},{4,3},{5,4},{6,5},{7,6},{9,8},{10,9},{11,10},{12... | collective-permute-start | bytes 344072 | tf_op jit(solution)/shard_map/ppermute | solution.py:689
  27.7 0.0 collective-permute-done.2.fyl
  27.7 3.3 %collective-permute-done.3.fyh = f32[28,8,128]{2,1,0:T(8,128)S(1)} collective-permute-done((f32[28,8,128]{2,1,0:T(8,128)S(1)}, f32[28,8,128]{2,1,0:T(8,128)S(1)}, u32[]{:S(2)}, u32[]{:S(2)}) %collective-permute-start.3) | collective-permute-done | bytes 114720 | tf_op jit(solution)/shard_map/ppermute | solution.py:689
  31.0 0.0 all-to-all-done.parts
  31.0 0.9 %shard_map.68 = (f32[4,2,8,8,128]{4,3,2,1,0:T(8,128)S(1)}, f32[4,2,8,8,128]{4,3,2,1,0:T(8,128)S(1)}, f32[4,8,8,128]{3,2,1,0:T(8,128)S(1)}, f32[43,8,128]{2,1,0:T...) custom-call(f32[6,4,8,8,128]{4,3,2,1,0:T(8,128)S(1)} %copy-done, ...), custom_call_target="tpu_custom_call" | custom-call | tf_op jit(solution)/shard_map/pallas_call | solution.py:669
  32.0 3.3 %collective-permute-start.4 = (f32[43,8,128]{2,1,0:T(8,128)S(1)}, f32[43,8,128]{2,1,0:T(8,128)S(1)}, u32[]{:S(2)}, u32[]{:S(2)}) collective-permute-start(f32[43,8,128]{2,1,0:T(8,128)S(1)} %get-tuple-element.41), channel_id=1, source_target_pairs={{0,8},{8,16},{16,24},{1,9},{9,17},{17,25},{2,10},{10,18},{18,26},{... | collective-permute-start | bytes 528392 | tf_op jit(solution)/shard_map/ppermute | solution.py:689
  35.3 1.3 %collective-permute-start.5 = (f32[43,8,128]{2,1,0:T(8,128)S(1)}, f32[43,8,128]{2,1,0:T(8,128)S(1)}, u32[]{:S(2)}, u32[]{:S(2)}) collective-permute-start(f32[43,8,128]{2,1,0:T(8,128)S(1)} %get-tuple-element.42), channel_id=1, source_target_pairs={{8,0},{16,8},{24,16},{9,1},{17,9},{25,17},{10,2},{18,10},{26,18},{... | collective-permute-start | bytes 528392 | tf_op jit(solution)/shard_map/ppermute | solution.py:689
  36.6 1.3 %shard_map.70.table = f32[8,128]{1,0:T(8,128)S(1)} custom-call(f32[4,8,8,128]{3,2,1,0:T(8,128)S(1)} %copy-done.2, s32[8,8,128]{2,1,0:T(8,128)S(1)} %copy-done.5, f32[4,2,8,8,128]{4,3,2,1,0:T(8,128)S(1)} %get-tuple-element.40.residual, f32[4,2,8,8,128]{4,3,2,1,0:T(8,128)S(1)} %get-tuple-element.49.image, s32[41]{0:T(128)S(1)} %get-tuple-element.51.present), custom_call_target="tpu_custom_call" | custom-call | flops 4194304 | bytes 4194304 | tf_op jit(solution)/shard_map/pallas_call | solution.py:669
  37.9 0.3 collective-permute-done.4.gxl.rest_0_
  38.2 4.4 %collective-permute-done.5.gxh.rest_1_ = f32[43,8,128]{2,1,0:T(8,128)S(1)} collective-permute-done((f32[43,8,128]{2,1,0:T(8,128)S(1)}, f32[43,8,128]{2,1,0:T(8,128)S(1)}, u32[]{:S(2)}, u32[]{:S(2)}) %collective-permute-start.5) | collective-permute-done | bytes 176160 | tf_op jit(solution)/shard_map/ppermute | solution.py:689
  42.6 0.7 shard_map.71
  43.3 6.1 %all-to-all-start.1 = ((f32[32,8,128]{2,1,0:T(8,128)}), f32[32,8,128]{2,1,0:T(8,128)S(1)}, u32[]{:S(2)}, u32[]{:S(2)}) async-start(f32[32,8,128]{2,1,0:T(8,128)} %shard_map.71), calls=%async_computation.1 | async-start | bytes 262144 | tf_op jit(solution)/shard_map/all_to_all | solution.py:693
  49.5 2.2 %collective-permute-start.6 = (f32[45,8,128]{2,1,0:T(8,128)S(1)}, f32[45,8,128]{2,1,0:T(8,128)S(1)}, u32[]{:S(2)}, u32[]{:S(2)}) collective-permute-start(f32[45,8,128]{2,1,0:T(8,128)S(1)} %get-tuple-element.47), channel_id=1, source_target_pairs={{0,1},{1,2},{2,3},{3,4},{4,5},{5,6},{6,7},{8,9},{9,10},{10,11},{11... | collective-permute-start | bytes 552968 | tf_op jit(solution)/shard_map/ppermute | solution.py:689
  51.6 1.3 %collective-permute-start.7 = (f32[45,8,128]{2,1,0:T(8,128)S(1)}, f32[45,8,128]{2,1,0:T(8,128)S(1)}, u32[]{:S(2)}, u32[]{:S(2)}) collective-permute-start(f32[45,8,128]{2,1,0:T(8,128)S(1)} %get-tuple-element.48), channel_id=1, source_target_pairs={{1,0},{2,1},{3,2},{4,3},{5,4},{6,5},{7,6},{9,8},{10,9},{11,10},{12... | collective-permute-start | bytes 552968 | tf_op jit(solution)/shard_map/ppermute | solution.py:689
  52.9 0.0 collective-permute-done.6.gyl
  52.9 3.1 %collective-permute-done.7.gyh = f32[45,8,128]{2,1,0:T(8,128)S(1)} collective-permute-done((f32[45,8,128]{2,1,0:T(8,128)S(1)}, f32[45,8,128]{2,1,0:T(8,128)S(1)}, u32[]{:S(2)}, u32[]{:S(2)}) %collective-permute-start.7) | collective-permute-done | bytes 184352 | tf_op jit(solution)/shard_map/ppermute | solution.py:689
  56.1 1.6 %all-to-all-done.1.parts = f32[32,8,128]{2,1,0:T(8,128)S(1)} async-done(((f32[32,8,128]{2,1,0:T(8,128)}), f32[32,8,128]{2,1,0:T(8,128)S(1)}, u32[]{:S(2)}, u32[]{:S(2)}) %all-to-all-start.1) | async-done | bytes 131104 | tf_op jit(solution)/shard_map/all_to_all | solution.py:693
  57.6 2.9 %shard_map.72 = (f32[4,2,8,8,128]{4,3,2,1,0:T(8,128)S(1)}, f32[4,2,8,8,128]{4,3,2,1,0:T(8,128)S(1)}, f32[32,8,128]{2,1,0:T(8,128)S(1)}, f32[16,128]{1,0:T(8,128)S(1)}) custom-call(f32[6,4,8,8,128]{4,3,2,1,0:T(8,128)S(1)} %copy-done, f32[4,8,8,128]{3,2,1,0:T(8,128)S(1)} %copy-done.4, f32[4,8,8,128]{3,2,1,0:T(8,128)S(1)} %copy-done.2, ...), custom_call_target="tpu_custom_call" | custom-call | tf_op jit(solution)/shard_map/pallas_call | solution.py:669
  60.6 15.4 %all_to_all.15.parts = f32[32,8,128]{2,1,0:T(8,128)S(1)} all-to-all(f32[32,8,128]{2,1,0:T(8,128)S(1)} %get-tuple-element.55), channel_id=1, replica_groups=mesh['member'=1,'gx'=4,'gy'=8] {'gx','gy'}, dimensions={0} | all-to-all | bytes 262144 | tf_op jit(solution)/shard_map/all_to_all | solution.py:693
  76.0 1.6 %shard_map.73 = f32[4,2,8,8,128]{4,3,2,1,0:T(8,128)} custom-call(f32[4,2,8,8,128]{4,3,2,1,0:T(8,128)S(1)} %copy-done.1, f32[4,2,8,8,128]{4,3,2,1,0:T(8,128)S(1)} %get-tuple-element.40.residual, f32[4,2,8,8,128]{4,3,2,1,0:T(8,128)S(1)} %get-tuple-element.53.second, f32[4,2,8,8,128]{4,3,2,1,0:T(8,128)S(1)} %get-tuple-element.54.third, ...), custom_call_target="tpu_custom_call" | custom-call | tf_op jit(solution)/shard_map/pallas_call | solution.py:669
  (2 shorter events, 0.1 us)
Async XLA Ops:
  0.0 7.1 %copy-start.5 = (s32[8,8,128]{2,1,0:T(8,128)S(1)}, s32[8,8,128]{2,1,0:T(8,128)}, u32[]{:S(2)}) copy-start(s32[8,8,128]{2,1,0:T(8,128)} %ids.7) | copy-start | bytes 98308
  0.0 7.1 %copy-start.2 = (f32[4,8,8,128]{3,2,1,0:T(8,128)S(1)}, f32[4,8,8,128]{3,2,1,0:T(8,128)}, u32[]{:S(2)}) copy-start(f32[4,8,8,128]{3,2,1,0:T(8,128)} %wells.7) | copy-start | bytes 393220
  0.0 7.2 %copy-start.1 = (f32[4,2,8,8,128]{4,3,2,1,0:T(8,128)S(1)}, f32[4,2,8,8,128]{4,3,2,1,0:T(8,128)}, u32[]{:S(2)}) copy-start(f32[4,2,8,8,128]{4,3,2,1,0:T(8,128)} %guess.5) | copy-start | bytes 786436
  0.0 7.2 %copy-start.4 = (f32[4,8,8,128]{3,2,1,0:T(8,128)S(1)}, f32[4,8,8,128]{3,2,1,0:T(8,128)}, u32[]{:S(2)}) copy-start(f32[4,8,8,128]{3,2,1,0:T(8,128)} %diagonal.5) | copy-start | bytes 393220
  0.0 7.2 %copy-start = (f32[6,4,8,8,128]{4,3,2,1,0:T(8,128)S(1)}, f32[6,4,8,8,128]{4,3,2,1,0:T(8,128)}, u32[]{:S(2)}) copy-start(f32[6,4,8,8,128]{4,3,2,1,0:T(8,128)} %couplings.5) | copy-start | bytes 2359300
  0.0 7.2 %copy-start.3 = (f32[4,2,8,8,128]{4,3,2,1,0:T(8,128)S(1)}, f32[4,2,8,8,128]{4,3,2,1,0:T(8,128)}, u32[]{:S(2)}) copy-start(f32[4,2,8,8,128]{4,3,2,1,0:T(8,128)} %right.3) | copy-start | bytes 786436
  2.2 7.6 %collective-permute-start = (f32[24,8,128]{2,1,0:T(8,128)}, f32[24,8,128]{2,1,0:T(8,128)S(1)}, u32[]{:S(2)}, u32[]{:S(2)}) collective-permute-start(f32[24,8,128]{2,1,0:T(8,128)} %get-tuple-element.31), channel_id=1, source_target_pairs={{0,8},{8,16},{16,24},{1,9},{9,17},{17,25},{2,10},{10,18},{18,26},{... | collective-permute-start | bytes 294920 | tf_op jit(solution)/shard_map/ppermute | solution.py:689
  10.4 6.5 %copy-start.6 = (f32[24,8,128]{2,1,0:T(8,128)S(1)}, f32[24,8,128]{2,1,0:T(8,128)}, u32[]{:S(2)}) copy-start(f32[24,8,128]{2,1,0:T(8,128)} %get-tuple-element.32) | copy-start | bytes 294916
  10.4 20.6 %all-to-all-start = ((f32[32,8,128]{2,1,0:T(8,128)}), f32[32,8,128]{2,1,0:T(8,128)S(1)}, u32[]{:S(2)}, u32[]{:S(2)}) async-start(f32[32,8,128]{2,1,0:T(8,128)} %shard_map.67), calls=%async_computation | async-start | bytes 262144 | tf_op jit(solution)/shard_map/all_to_all | solution.py:693
  16.9 7.8 %collective-permute-start.1 = (f32[24,8,128]{2,1,0:T(8,128)S(1)}, f32[24,8,128]{2,1,0:T(8,128)S(1)}, u32[]{:S(2)}, u32[]{:S(2)}) collective-permute-start(f32[24,8,128]{2,1,0:T(8,128)S(1)} %copy-done.6), channel_id=1, source_target_pairs={{8,0},{16,8},{24,16},{9,1},{17,9},{25,17},{10,2},{18,10},{26,18},{... | collective-permute-start | bytes 294920 | tf_op jit(solution)/shard_map/ppermute | solution.py:689
  24.7 3.0 %collective-permute-start.2 = (f32[28,8,128]{2,1,0:T(8,128)S(1)}, f32[28,8,128]{2,1,0:T(8,128)S(1)}, u32[]{:S(2)}, u32[]{:S(2)}) collective-permute-start(f32[28,8,128]{2,1,0:T(8,128)S(1)} %get-tuple-element.35), channel_id=1, source_target_pairs={{0,1},{1,2},{2,3},{3,4},{4,5},{5,6},{6,7},{8,9},{9,10},{10,11},{11... | collective-permute-start | bytes 344072 | tf_op jit(solution)/shard_map/ppermute | solution.py:689
  26.4 4.6 %collective-permute-start.3 = (f32[28,8,128]{2,1,0:T(8,128)S(1)}, f32[28,8,128]{2,1,0:T(8,128)S(1)}, u32[]{:S(2)}, u32[]{:S(2)}) collective-permute-start(f32[28,8,128]{2,1,0:T(8,128)S(1)} %get-tuple-element.36), channel_id=1, source_target_pairs={{1,0},{2,1},{3,2},{4,3},{5,4},{6,5},{7,6},{9,8},{10,9},{11,10},{12... | collective-permute-start | bytes 344072 | tf_op jit(solution)/shard_map/ppermute | solution.py:689
  32.0 6.2 %collective-permute-start.4 = (f32[43,8,128]{2,1,0:T(8,128)S(1)}, f32[43,8,128]{2,1,0:T(8,128)S(1)}, u32[]{:S(2)}, u32[]{:S(2)}) collective-permute-start(f32[43,8,128]{2,1,0:T(8,128)S(1)} %get-tuple-element.41), channel_id=1, source_target_pairs={{0,8},{8,16},{16,24},{1,9},{9,17},{17,25},{2,10},{10,18},{18,26},{... | collective-permute-start | bytes 528392 | tf_op jit(solution)/shard_map/ppermute | solution.py:689
  35.3 7.3 %collective-permute-start.5 = (f32[43,8,128]{2,1,0:T(8,128)S(1)}, f32[43,8,128]{2,1,0:T(8,128)S(1)}, u32[]{:S(2)}, u32[]{:S(2)}) collective-permute-start(f32[43,8,128]{2,1,0:T(8,128)S(1)} %get-tuple-element.42), channel_id=1, source_target_pairs={{8,0},{16,8},{24,16},{9,1},{17,9},{25,17},{10,2},{18,10},{26,18},{... | collective-permute-start | bytes 528392 | tf_op jit(solution)/shard_map/ppermute | solution.py:689
  43.3 14.4 %all-to-all-start.1 = ((f32[32,8,128]{2,1,0:T(8,128)}), f32[32,8,128]{2,1,0:T(8,128)S(1)}, u32[]{:S(2)}, u32[]{:S(2)}) async-start(f32[32,8,128]{2,1,0:T(8,128)} %shard_map.71), calls=%async_computation.1 | async-start | bytes 262144 | tf_op jit(solution)/shard_map/all_to_all | solution.py:693
  49.5 3.5 %collective-permute-start.6 = (f32[45,8,128]{2,1,0:T(8,128)S(1)}, f32[45,8,128]{2,1,0:T(8,128)S(1)}, u32[]{:S(2)}, u32[]{:S(2)}) collective-permute-start(f32[45,8,128]{2,1,0:T(8,128)S(1)} %get-tuple-element.47), channel_id=1, source_target_pairs={{0,1},{1,2},{2,3},{3,4},{4,5},{5,6},{6,7},{8,9},{9,10},{10,11},{11... | collective-permute-start | bytes 552968 | tf_op jit(solution)/shard_map/ppermute | solution.py:689
  51.6 4.4 %collective-permute-start.7 = (f32[45,8,128]{2,1,0:T(8,128)S(1)}, f32[45,8,128]{2,1,0:T(8,128)S(1)}, u32[]{:S(2)}, u32[]{:S(2)}) collective-permute-start(f32[45,8,128]{2,1,0:T(8,128)S(1)} %get-tuple-element.48), channel_id=1, source_target_pairs={{1,0},{2,1},{3,2},{4,3},{5,4},{6,5},{7,6},{9,8},{10,9},{11,10},{12... | collective-permute-start | bytes 552968 | tf_op jit(solution)/shard_map/ppermute | solution.py:689

commit v10 on v6

--- a/solution.py
+++ b/solution.py
@@ -302,7 +302,8 @@
         )
 
 
-def corner_kernel(y_low, y_high, fxl, fxh, low_out, high_out):
+def corner_kernel(y_low, y_high, fxl, fxh, table, low_out, high_out, part):
+    part[...] = jnp.broadcast_to(table[...][None, :2], part.shape)
     last = fxl.shape[1] - 1
     for own, out, at, side in ((y_low, low_out, 0, LAT_DOWN), (y_high, high_out, last, LAT_UP)):
         for n in range(FACE_PLANES):
@@ -315,7 +316,8 @@
                 row += 1
 
 
-def image_corner_kernel(y_low, y_high, gxl, gxh, low_out, high_out):
+def image_corner_kernel(y_low, y_high, gxl, gxh, table, low_out, high_out, part):
+    part[...] = jnp.broadcast_to(table[...][None], part.shape)
     last = gxl.shape[1] - 1
     for own, out, at in ((y_low, low_out, 0), (y_high, high_out, last)):
         for n in range(16):
@@ -327,7 +329,7 @@
 
 def guess_kernel(
     couplings, diagonal, wells, ids, right, guess,
-    part, present, y_low, y_high, values, scratch,
+    table_out, present, y_low, y_high, values, scratch,
 ):
     y_pack((couplings, diagonal, wells, ids, right, guess), (y_low, y_high))
     list_wells(ids, present)
@@ -336,8 +338,7 @@
     values[4] = wells[0] * wells[2] + wells[1] * wells[3]
     values[5] = wells[2] * wells[2] + wells[3] * wells[3]
     rows = segment_rows(ids, values, scratch, present)
-    table = pack_rows(rows, jnp.zeros((8, LANES), jnp.float32))
-    part[...] = jnp.broadcast_to(table[None, :2], part.shape)
+    table_out[...] = pack_rows(rows, jnp.zeros((8, LANES), jnp.float32))
 
 
 def residual_kernel(
@@ -401,7 +402,7 @@
 
 
 def moments_kernel(
-    wells, ids, residual, image, present, part, values, scratch, dots
+    wells, ids, residual, image, present, table_out, values, scratch, dots
 ):
     dots[...] = jnp.zeros_like(dots)
     for k in range(RHS):
@@ -416,8 +417,7 @@
         dots[2, row, :] = tile_sum(result, result)
     rows = segment_rows(ids, values, scratch, present)
     table = place_rows(rows, jnp.zeros((8, LANES), jnp.float32))
-    table = place_columns(dots, WELLS, table)
-    part[...] = jnp.broadcast_to(table[None], part.shape)
+    table_out[...] = place_columns(dots, WELLS, table)
 
 
 def first_step(totals, small):
@@ -658,27 +658,25 @@
     x_low, x_high = call(
         x_pack_kernel,
         [(FACE_PLANES,) + plane] * 2,
-        arguments,
+        [pltpu.with_memory_space_constraint(argument, pltpu.HBM) for argument in arguments],
         ends + [pltpu.SemaphoreType.DMA((len(ends),))],
         own_copies=True,
-        grant=60 << 20,
     )
     fxl = from_behind(x_high, "gx", 1)
     fxh = from_behind(x_low, "gx", -1)
-    part, present, y_low, y_high = call(
+    table, present, y_low, y_high = call(
         guess_kernel,
-        [(devices, 2, LANES), (WELLS + 1,)] + [(FACE_PLANES,) + plane] * 2,
+        [plane, (WELLS + 1,)] + [(FACE_PLANES,) + plane] * 2,
         arguments,
         [held(6, *block), held(6, WELLS, LANES)],
         cost=4 << 20,
     )
+    y_low, y_high, part = call(
+        corner_kernel,
+        [(FACE_PLANES + CORNER_PLANES,) + plane] * 2 + [(devices, 2, LANES)],
+        (y_low, y_high, fxl, fxh, table),
+    )
     parts = exchanged(part)
-    y_low, y_high = call(
-        corner_kernel,
-        [(FACE_PLANES + CORNER_PLANES,) + plane] * 2,
-        (y_low, y_high, fxl, fxh),
-        cost=256 << 20,
-    )
     fyl = from_behind(y_high, "gy", 1)
     fyh = from_behind(y_low, "gy", -1)
 
@@ -690,20 +688,19 @@
     )
     gxl = from_behind(x_high, "gx", 1)
     gxh = from_behind(x_low, "gx", -1)
-    (part,) = call(
+    (table,) = call(
         moments_kernel,
-        [(devices, 8, LANES)],
+        [plane],
         (wells, ids, residual, image, present),
         [held(16, *block), held(16, WELLS, LANES), held(3, *plane)],
         cost=4 << 20,
     )
+    y_low, y_high, part = call(
+        image_corner_kernel,
+        [(18,) + plane] * 2 + [(devices, 8, LANES)],
+        (y_low, y_high, gxl, gxh, table),
+    )
     parts = exchanged(part)
-    y_low, y_high = call(
-        image_corner_kernel,
-        [(18,) + plane] * 2,
-        (y_low, y_high, gxl, gxh),
-        cost=256 << 20,
-    )
     gyl = from_behind(y_high, "gy", 1)
     gyh = from_behind(y_low, "gy", -1)
 

time: 75 us -> 72.6 us (0.968)
  blocking collectives: 30.4 us -> 29.1 us
    ppermute x8, waiting for transfers between devices: 14.1 us -> 11.8 us  [from_behind(): lax.ppermute(value, axis, [(source, source + steps) for source in range(l...]
    all_to_all x1, waiting for transfers between devices: 0.01 us -> 1.9 us  [exchanged(): return lax.all_to_all(part, ('gx', 'gy'), 0, 0, tiled=True)]
    all_to_all x2, blocking collectives: 30.4 us -> 29.1 us  [exchanged(): return lax.all_to_all(part, ('gx', 'gy'), 0, 0, tiled=True)]
  transfers between devices with their start and end apart: 9 -> 9, of which waited for: 5 -> 5; matrix products, arithmetic and copies ran while one was open for 0% -> 0% of each run, Pallas kernels for 2% -> 4%
where the time goes in v10:
time: 72.6 us; the launch traced here: 72.2 us
  blocking collectives  29.1 us (40%)
  starting transfers between devices  18.5 us (25%)
  waiting for transfers between devices  13.7 us (19%)
  Pallas kernels  10.8 us (15%)
    all_to_all x2, blocking collectives, exchanged(): return lax.all_to_all(part, ('gx', 'gy'), 0, 0, tiled=True)  29.1 us
    ppermute x8, starting transfers between devices, from_behind(): lax.ppermute(value, axis, [(source, source + steps) for source in range(l...  15.9 us
    ppermute x8, waiting for transfers between devices, from_behind(): lax.ppermute(value, axis, [(source, source + steps) for source in range(l...  11.8 us
    pallas_call x8, Pallas kernels, call(): pl.pallas_call(kernel, out_shape=outs, in_specs=[place(argument) for argu...  10.8 us
    all_to_all x1, starting transfers between devices, exchanged(): return lax.all_to_all(part, ('gx', 'gy'), 0, 0, tiled=True)  2.58 us
    all_to_all x1, waiting for transfers between devices, exchanged(): return lax.all_to_all(part, ('gx', 'gy'), 0, 0, tiled=True)  1.9 us
  transfers between devices with their start and end apart: 9, of which 5 were waited for; matrix products, arithmetic and copies ran while one was open for 0% of the time, Pallas kernels for 4%

profile of v10, /device:TPU:0, one launch (start us, length us, event | category | flops | bytes accessed | tf_op | source)
XLA Modules:
  0.0 72.2 jit_solution(4468854548941243025)
XLA Ops:
  0.0 0.0 copy-start.5
  0.0 0.0 copy-start.2
  0.0 0.0 copy-start.1
  0.0 0.0 copy-start.4
  0.0 0.0 copy-start
  0.0 0.0 copy-start.3
  0.0 1.5 %shard_map.64 = (f32[50,8,128]{2,1,0:T(8,128)S(1)}, f32[50,8,128]{2,1,0:T(8,128)S(1)}) custom-call(f32[6,4,8,8,128]{4,3,2,1,0:T(8,128)} %couplings.5, f32[4,8,8,128]{3,2,1,0:T(8,128)} %diagonal.5, f32[4,8,8,128]{3,2,1,0:T(8,128)} %wells.7, s32[8,8,128]{2,1,0:T(8,128)} %ids.7, f32[4,2,8,8,128]{4,3,2,1,0:T(8,128)} %right.3, f32[4,2,8,8,128]{4,3,2,1,0:T(8,128)} %guess.5), custom_call_target="tpu_custom_call" | custom-call | tf_op jit(solution)/shard_map/pallas_call | solution.py:620
  1.5 5.0 %collective-permute-start = (f32[50,8,128]{2,1,0:T(8,128)S(1)}, f32[50,8,128]{2,1,0:T(8,128)S(1)}, u32[]{:S(2)}, u32[]{:S(2)}) collective-permute-start(f32[50,8,128]{2,1,0:T(8,128)S(1)} %get-tuple-element.29), channel_id=1, source_target_pairs={{0,8},{8,16},{16,24},{1,9},{9,17},{17,25},{2,10},{10,18},{18,26},{... | collective-permute-start | bytes 614408 | tf_op jit(solution)/shard_map/ppermute | solution.py:640
  6.5 1.3 %collective-permute-start.1 = (f32[50,8,128]{2,1,0:T(8,128)S(1)}, f32[50,8,128]{2,1,0:T(8,128)S(1)}, u32[]{:S(2)}, u32[]{:S(2)}) collective-permute-start(f32[50,8,128]{2,1,0:T(8,128)S(1)} %get-tuple-element.30), channel_id=1, source_target_pairs={{8,0},{16,8},{24,16},{9,1},{17,9},{25,17},{10,2},{18,10},{26,18},{... | collective-permute-start | bytes 614408 | tf_op jit(solution)/shard_map/ppermute | solution.py:640
  7.8 0.0 copy-done.5
  7.8 0.0 copy-done.2
  7.8 0.0 copy-done.1
  7.8 0.0 copy-done.4
  7.8 0.0 copy-done
  7.8 0.0 copy-done.3
  7.9 1.9 %shard_map.65 = (f32[8,128]{1,0:T(8,128)S(1)}, s32[41]{0:T(128)S(1)}, f32[50,8,128]{2,1,0:T(8,128)S(1)}, f32[50,8,128]{2,1,0:T(8,128)S(1)}) custom-call(f32[6,4,8,8,128]{4,3,2,1,0:T(8,128)S(1)} %copy-done, f32[4,8,8,128]{3,2,1,0:T(8,128)S(1)} %copy-done.4, f32[4,8,8,128]{3,2,1,0:T(8,128)S(1)} %copy-done.2, s32[8,8,128]{2,1,0:T(8,128)S(1)} %copy-done.5, ...), custom_call_target="tpu_custom_call" | custom-call | flops 4194304 | bytes 4194304 | tf_op jit(solution)/shard_map/pallas_call | solution.py:620
  9.7 1.1 %collective-permute-done.fxl = f32[50,8,128]{2,1,0:T(8,128)S(1)} collective-permute-done((f32[50,8,128]{2,1,0:T(8,128)S(1)}, f32[50,8,128]{2,1,0:T(8,128)S(1)}, u32[]{:S(2)}, u32[]{:S(2)}) %collective-permute-start) | collective-permute-done | bytes 204832 | tf_op jit(solution)/shard_map/ppermute | solution.py:640
  10.8 4.1 %collective-permute-done.1.fxh = f32[50,8,128]{2,1,0:T(8,128)S(1)} collective-permute-done((f32[50,8,128]{2,1,0:T(8,128)S(1)}, f32[50,8,128]{2,1,0:T(8,128)S(1)}, u32[]{:S(2)}, u32[]{:S(2)}) %collective-permute-start.1) | collective-permute-done | bytes 204832 | tf_op jit(solution)/shard_map/ppermute | solution.py:640
  14.9 0.1 shard_map.66
  15.0 1.3 %collective-permute-start.2 = (f32[55,8,128]{2,1,0:T(8,128)S(1)}, f32[55,8,128]{2,1,0:T(8,128)S(1)}, u32[]{:S(2)}, u32[]{:S(2)}) collective-permute-start(f32[55,8,128]{2,1,0:T(8,128)S(1)} %get-tuple-element.34), channel_id=1, source_target_pairs={{0,1},{1,2},{2,3},{3,4},{4,5},{5,6},{6,7},{8,9},{9,10},{10,11},{11... | collective-permute-start | bytes 675848 | tf_op jit(solution)/shard_map/ppermute | solution.py:640
  16.3 1.3 %collective-permute-start.3 = (f32[55,8,128]{2,1,0:T(8,128)S(1)}, f32[55,8,128]{2,1,0:T(8,128)S(1)}, u32[]{:S(2)}, u32[]{:S(2)}) collective-permute-start(f32[55,8,128]{2,1,0:T(8,128)S(1)} %get-tuple-element.35), channel_id=1, source_target_pairs={{1,0},{2,1},{3,2},{4,3},{5,4},{6,5},{7,6},{9,8},{10,9},{11,10},{12... | collective-permute-start | bytes 675848 | tf_op jit(solution)/shard_map/ppermute | solution.py:640
  17.6 14.9 %all_to_all.15.parts = f32[32,2,128]{2,1,0:T(2,128)S(1)} all-to-all(f32[32,2,128]{2,1,0:T(2,128)S(1)} %get-tuple-element.36), channel_id=1, replica_groups=mesh['member'=1,'gx'=4,'gy'=8] {'gx','gy'}, dimensions={0} | all-to-all | bytes 65536 | tf_op jit(solution)/shard_map/all_to_all | solution.py:644
  32.5 0.0 collective-permute-done.2.fyl
  32.5 0.0 collective-permute-done.3.fyh
  32.5 0.9 %shard_map.67 = (f32[4,2,8,8,128]{4,3,2,1,0:T(8,128)S(1)}, f32[4,2,8,8,128]{4,3,2,1,0:T(8,128)S(1)}, f32[4,8,8,128]{3,2,1,0:T(8,128)S(1)}, f32[16,8,128]{2,1,0:T...) custom-call(f32[6,4,8,8,128]{4,3,2,1,0:T(8,128)S(1)} %copy-done, ...), custom_call_target="tpu_custom_call" | custom-call | tf_op jit(solution)/shard_map/pallas_call | solution.py:620
  33.4 2.5 %collective-permute-start.4 = (f32[16,8,128]{2,1,0:T(8,128)S(1)}, f32[16,8,128]{2,1,0:T(8,128)S(1)}, u32[]{:S(2)}, u32[]{:S(2)}) collective-permute-start(f32[16,8,128]{2,1,0:T(8,128)S(1)} %get-tuple-element.38), channel_id=1, source_target_pairs={{0,8},{8,16},{16,24},{1,9},{9,17},{17,25},{2,10},{10,18},{18,26},{... | collective-permute-start | bytes 196616 | tf_op jit(solution)/shard_map/ppermute | solution.py:640
  35.9 1.3 %collective-permute-start.5 = (f32[16,8,128]{2,1,0:T(8,128)S(1)}, f32[16,8,128]{2,1,0:T(8,128)S(1)}, u32[]{:S(2)}, u32[]{:S(2)}) collective-permute-start(f32[16,8,128]{2,1,0:T(8,128)S(1)} %get-tuple-element.39), channel_id=1, source_target_pairs={{8,0},{16,8},{24,16},{9,1},{17,9},{25,17},{10,2},{18,10},{26,18},{... | collective-permute-start | bytes 196616 | tf_op jit(solution)/shard_map/ppermute | solution.py:640
  37.2 1.3 %shard_map.68.table = f32[8,128]{1,0:T(8,128)S(1)} custom-call(f32[4,8,8,128]{3,2,1,0:T(8,128)S(1)} %copy-done.2, s32[8,8,128]{2,1,0:T(8,128)S(1)} %copy-done.5, f32[4,2,8,8,128]{4,3,2,1,0:T(8,128)S(1)} %get-tuple-element.37.residual, f32[4,2,8,8,128]{4,3,2,1,0:T(8,128)S(1)} %get-tuple-element.42.image, s32[41]{0:T(128)S(1)} %get-tuple-element.43.present), custom_call_target="tpu_custom_call" | custom-call | flops 4194304 | bytes 4194304 | tf_op jit(solution)/shard_map/pallas_call | solution.py:620
  38.4 0.0 collective-permute-done.4.gxl
  38.4 3.6 %collective-permute-done.5.gxh = f32[16,8,128]{2,1,0:T(8,128)S(1)} collective-permute-done((f32[16,8,128]{2,1,0:T(8,128)S(1)}, f32[16,8,128]{2,1,0:T(8,128)S(1)}, u32[]{:S(2)}, u32[]{:S(2)}) %collective-permute-start.5) | collective-permute-done | bytes 65568 | tf_op jit(solution)/shard_map/ppermute | solution.py:640
  42.0 0.7 shard_map.69
  42.7 2.6 %all-to-all-start.1 = ((f32[32,8,128]{2,1,0:T(8,128)}), f32[32,8,128]{2,1,0:T(8,128)S(1)}, u32[]{:S(2)}, u32[]{:S(2)}) async-start(f32[32,8,128]{2,1,0:T(8,128)} %get-tuple-element.47), calls=%async_computation.1 | async-start | bytes 262144 | tf_op jit(solution)/shard_map/all_to_all | solution.py:644
  45.3 2.0 %collective-permute-start.6 = (f32[18,8,128]{2,1,0:T(8,128)S(1)}, f32[18,8,128]{2,1,0:T(8,128)S(1)}, u32[]{:S(2)}, u32[]{:S(2)}) collective-permute-start(f32[18,8,128]{2,1,0:T(8,128)S(1)} %get-tuple-element.44), channel_id=1, source_target_pairs={{0,1},{1,2},{2,3},{3,4},{4,5},{5,6},{6,7},{8,9},{9,10},{10,11},{11... | collective-permute-start | bytes 221192 | tf_op jit(solution)/shard_map/ppermute | solution.py:640
  47.3 1.3 %collective-permute-start.7 = (f32[18,8,128]{2,1,0:T(8,128)S(1)}, f32[18,8,128]{2,1,0:T(8,128)S(1)}, u32[]{:S(2)}, u32[]{:S(2)}) collective-permute-start(f32[18,8,128]{2,1,0:T(8,128)S(1)} %get-tuple-element.45), channel_id=1, source_target_pairs={{1,0},{2,1},{3,2},{4,3},{5,4},{6,5},{7,6},{9,8},{10,9},{11,10},{12... | collective-permute-start | bytes 221192 | tf_op jit(solution)/shard_map/ppermute | solution.py:640
  48.6 0.0 collective-permute-done.6.gyl
  48.6 3.0 %collective-permute-done.7.gyh = f32[18,8,128]{2,1,0:T(8,128)S(1)} collective-permute-done((f32[18,8,128]{2,1,0:T(8,128)S(1)}, f32[18,8,128]{2,1,0:T(8,128)S(1)}, u32[]{:S(2)}, u32[]{:S(2)}) %collective-permute-start.7) | collective-permute-done | bytes 73760 | tf_op jit(solution)/shard_map/ppermute | solution.py:640
  51.6 1.9 %all-to-all-done.1.parts = f32[32,8,128]{2,1,0:T(8,128)S(1)} async-done(((f32[32,8,128]{2,1,0:T(8,128)}), f32[32,8,128]{2,1,0:T(8,128)S(1)}, u32[]{:S(2)}, u32[]{:S(2)}) %all-to-all-start.1) | async-done | bytes 131104 | tf_op jit(solution)/shard_map/all_to_all | solution.py:644
  53.5 2.8 %shard_map.70 = (f32[4,2,8,8,128]{4,3,2,1,0:T(8,128)S(1)}, f32[4,2,8,8,128]{4,3,2,1,0:T(8,128)S(1)}, f32[32,8,128]{2,1,0:T(8,128)S(1)}, f32[16,128]{1,0:T(8,128)S(1)}) custom-call(f32[6,4,8,8,128]{4,3,2,1,0:T(8,128)S(1)} %copy-done, f32[4,8,8,128]{3,2,1,0:T(8,128)S(1)} %copy-done.4, f32[4,8,8,128]{3,2,1,0:T(8,128)S(1)} %copy-done.2, ...), custom_call_target="tpu_custom_call" | custom-call | tf_op jit(solution)/shard_map/pallas_call | solution.py:620
  56.4 14.2 %all_to_all.16.parts = f32[32,8,128]{2,1,0:T(8,128)S(1)} all-to-all(f32[32,8,128]{2,1,0:T(8,128)S(1)} %get-tuple-element.51), channel_id=1, replica_groups=mesh['member'=1,'gx'=4,'gy'=8] {'gx','gy'}, dimensions={0} | all-to-all | bytes 262144 | tf_op jit(solution)/shard_map/all_to_all | solution.py:644
  70.6 1.6 %shard_map.71 = f32[4,2,8,8,128]{4,3,2,1,0:T(8,128)} custom-call(f32[4,2,8,8,128]{4,3,2,1,0:T(8,128)S(1)} %copy-done.1, f32[4,2,8,8,128]{4,3,2,1,0:T(8,128)S(1)} %get-tuple-element.37.residual, f32[4,2,8,8,128]{4,3,2,1,0:T(8,128)S(1)} %get-tuple-element.49.second, f32[4,2,8,8,128]{4,3,2,1,0:T(8,128)S(1)} %get-tuple-element.50.third, ...), custom_call_target="tpu_custom_call" | custom-call | tf_op jit(solution)/shard_map/pallas_call | solution.py:620
Async XLA Ops:
  0.0 7.8 %copy-start.5 = (s32[8,8,128]{2,1,0:T(8,128)S(1)}, s32[8,8,128]{2,1,0:T(8,128)}, u32[]{:S(2)}) copy-start(s32[8,8,128]{2,1,0:T(8,128)} %ids.7) | copy-start | bytes 98308
  0.0 7.8 %copy-start.2 = (f32[4,8,8,128]{3,2,1,0:T(8,128)S(1)}, f32[4,8,8,128]{3,2,1,0:T(8,128)}, u32[]{:S(2)}) copy-start(f32[4,8,8,128]{3,2,1,0:T(8,128)} %wells.7) | copy-start | bytes 393220
  0.0 7.8 %copy-start.1 = (f32[4,2,8,8,128]{4,3,2,1,0:T(8,128)S(1)}, f32[4,2,8,8,128]{4,3,2,1,0:T(8,128)}, u32[]{:S(2)}) copy-start(f32[4,2,8,8,128]{4,3,2,1,0:T(8,128)} %guess.5) | copy-start | bytes 786436
  0.0 7.8 %copy-start.4 = (f32[4,8,8,128]{3,2,1,0:T(8,128)S(1)}, f32[4,8,8,128]{3,2,1,0:T(8,128)}, u32[]{:S(2)}) copy-start(f32[4,8,8,128]{3,2,1,0:T(8,128)} %diagonal.5) | copy-start | bytes 393220
  0.0 7.8 %copy-start = (f32[6,4,8,8,128]{4,3,2,1,0:T(8,128)S(1)}, f32[6,4,8,8,128]{4,3,2,1,0:T(8,128)}, u32[]{:S(2)}) copy-start(f32[6,4,8,8,128]{4,3,2,1,0:T(8,128)} %couplings.5) | copy-start | bytes 2359300
  0.0 7.8 %copy-start.3 = (f32[4,2,8,8,128]{4,3,2,1,0:T(8,128)S(1)}, f32[4,2,8,8,128]{4,3,2,1,0:T(8,128)}, u32[]{:S(2)}) copy-start(f32[4,2,8,8,128]{4,3,2,1,0:T(8,128)} %right.3) | copy-start | bytes 786436
  1.5 9.3 %collective-permute-start = (f32[50,8,128]{2,1,0:T(8,128)S(1)}, f32[50,8,128]{2,1,0:T(8,128)S(1)}, u32[]{:S(2)}, u32[]{:S(2)}) collective-permute-start(f32[50,8,128]{2,1,0:T(8,128)S(1)} %get-tuple-element.29), channel_id=1, source_target_pairs={{0,8},{8,16},{16,24},{1,9},{9,17},{17,25},{2,10},{10,18},{18,26},{... | collective-permute-start | bytes 614408 | tf_op jit(solution)/shard_map/ppermute | solution.py:640
  6.5 8.4 %collective-permute-start.1 = (f32[50,8,128]{2,1,0:T(8,128)S(1)}, f32[50,8,128]{2,1,0:T(8,128)S(1)}, u32[]{:S(2)}, u32[]{:S(2)}) collective-permute-start(f32[50,8,128]{2,1,0:T(8,128)S(1)} %get-tuple-element.30), channel_id=1, source_target_pairs={{8,0},{16,8},{24,16},{9,1},{17,9},{25,17},{10,2},{18,10},{26,18},{... | collective-permute-start | bytes 614408 | tf_op jit(solution)/shard_map/ppermute | solution.py:640
  15.0 17.5 %collective-permute-start.2 = (f32[55,8,128]{2,1,0:T(8,128)S(1)}, f32[55,8,128]{2,1,0:T(8,128)S(1)}, u32[]{:S(2)}, u32[]{:S(2)}) collective-permute-start(f32[55,8,128]{2,1,0:T(8,128)S(1)} %get-tuple-element.34), channel_id=1, source_target_pairs={{0,1},{1,2},{2,3},{3,4},{4,5},{5,6},{6,7},{8,9},{9,10},{10,11},{11... | collective-permute-start | bytes 675848 | tf_op jit(solution)/shard_map/ppermute | solution.py:640
  16.3 16.2 %collective-permute-start.3 = (f32[55,8,128]{2,1,0:T(8,128)S(1)}, f32[55,8,128]{2,1,0:T(8,128)S(1)}, u32[]{:S(2)}, u32[]{:S(2)}) collective-permute-start(f32[55,8,128]{2,1,0:T(8,128)S(1)} %get-tuple-element.35), channel_id=1, source_target_pairs={{1,0},{2,1},{3,2},{4,3},{5,4},{6,5},{7,6},{9,8},{10,9},{11,10},{12... | collective-permute-start | bytes 675848 | tf_op jit(solution)/shard_map/ppermute | solution.py:640
  33.4 5.1 %collective-permute-start.4 = (f32[16,8,128]{2,1,0:T(8,128)S(1)}, f32[16,8,128]{2,1,0:T(8,128)S(1)}, u32[]{:S(2)}, u32[]{:S(2)}) collective-permute-start(f32[16,8,128]{2,1,0:T(8,128)S(1)} %get-tuple-element.38), channel_id=1, source_target_pairs={{0,8},{8,16},{16,24},{1,9},{9,17},{17,25},{2,10},{10,18},{18,26},{... | collective-permute-start | bytes 196616 | tf_op jit(solution)/shard_map/ppermute | solution.py:640
  35.9 6.2 %collective-permute-start.5 = (f32[16,8,128]{2,1,0:T(8,128)S(1)}, f32[16,8,128]{2,1,0:T(8,128)S(1)}, u32[]{:S(2)}, u32[]{:S(2)}) collective-permute-start(f32[16,8,128]{2,1,0:T(8,128)S(1)} %get-tuple-element.39), channel_id=1, source_target_pairs={{8,0},{16,8},{24,16},{9,1},{17,9},{25,17},{10,2},{18,10},{26,18},{... | collective-permute-start | bytes 196616 | tf_op jit(solution)/shard_map/ppermute | solution.py:640
  42.7 10.8 %all-to-all-start.1 = ((f32[32,8,128]{2,1,0:T(8,128)}), f32[32,8,128]{2,1,0:T(8,128)S(1)}, u32[]{:S(2)}, u32[]{:S(2)}) async-start(f32[32,8,128]{2,1,0:T(8,128)} %get-tuple-element.47), calls=%async_computation.1 | async-start | bytes 262144 | tf_op jit(solution)/shard_map/all_to_all | solution.py:644
  45.3 3.3 %collective-permute-start.6 = (f32[18,8,128]{2,1,0:T(8,128)S(1)}, f32[18,8,128]{2,1,0:T(8,128)S(1)}, u32[]{:S(2)}, u32[]{:S(2)}) collective-permute-start(f32[18,8,128]{2,1,0:T(8,128)S(1)} %get-tuple-element.44), channel_id=1, source_target_pairs={{0,1},{1,2},{2,3},{3,4},{4,5},{5,6},{6,7},{8,9},{9,10},{10,11},{11... | collective-permute-start | bytes 221192 | tf_op jit(solution)/shard_map/ppermute | solution.py:640
  47.3 4.3 %collective-permute-start.7 = (f32[18,8,128]{2,1,0:T(8,128)S(1)}, f32[18,8,128]{2,1,0:T(8,128)S(1)}, u32[]{:S(2)}, u32[]{:S(2)}) collective-permute-start(f32[18,8,128]{2,1,0:T(8,128)S(1)} %get-tuple-element.45), channel_id=1, source_target_pairs={{1,0},{2,1},{3,2},{4,3},{5,4},{6,5},{7,6},{9,8},{10,9},{11,10},{12... | collective-permute-start | bytes 221192 | tf_op jit(solution)/shard_map/ppermute | solution.py:640

commit v11 on v9

--- a/solution.py
+++ b/solution.py
@@ -8,14 +8,16 @@
 WELLS = 40
 RHS = 4
 LANES = 128
-WELL_EQ, WELL_ID, GUESS, REST, ENDS = 4, 6, 7, 15, 23
-FACE_PLANES = 23
+WELL_EQ, WELL_ID, GUESS, REST = 4, 6, 7, 15
+UP_WELL, DOWN_WELL, RISE_WELL, FALL_WELL, DIAGONAL_WELL = 23, 25, 27, 29, 31
+BACK_WELL, BACK_ID = 33, 35
+FACE_PLANES = 36
+ENDS = 36
 CORNER_PLANES = 5
-LAT_UP, LAT_DOWN, RISE, FALL, DIAGONAL = 0, 4, 8, 12, 16
-BACK_IN, BACK_EQ, BACK_ID = 20, 24, 26
-LATE_PLANES = 27
+LAT_UP, LAT_DOWN, RISE, FALL, DIAGONAL, BACK_IN = 0, 4, 8, 12, 16, 20
+LAYER_BLOCKS = 24
 IMAGE_PLANES = 16
-SENT_PLANES = IMAGE_PLANES + LATE_PLANES
+TABLE_ROWS = 6
 CORNER_ROWS = 19
 SIDE_IN, SIDE_EQ, SIDE_ID, SIDE_GUESS = 4, 8, 10, 11
 
@@ -68,16 +70,17 @@
     return result, outgoing
 
 
-def face_stencil(late, first, second, behind):
-    def planes(start):
-        return lambda e: late(start + e)
-
-    result = product(planes(DIAGONAL), first, second)
-    up = product(planes(LAT_UP), first, second)
-    down = product(planes(LAT_DOWN), first, second)
-    rise = product(planes(RISE), first, second)
-    fall = product(planes(FALL), first, second)
-    row = iota(first.shape, 0)
+def face_stencil(blocks, first, second, behind):
+    def times(start):
+        return product(lambda e: blocks(start + e), first, second)
+
+    moves = [times(start) for start in (DIAGONAL, LAT_UP, LAT_DOWN, RISE, FALL)]
+    return face_moves(*moves, behind)
+
+
+def face_moves(kept, up, down, rise, fall, behind):
+    result = list(kept)
+    row = iota(kept[0].shape, 0)
     for b in range(2):
         total = result[b] + behind[b] + layer_moves(rise[b], fall[b])
         total = total + jnp.where(row == 0, 0.0, roll_up(up[b], 0))
@@ -241,41 +244,51 @@
 COUPLINGS, DIAGONALS, WELL_FIELDS, IDS, RIGHT_SIDE, START = range(6)
 
 
-def late_plane(cut, inward, lateral):
+def layer_blocks(cut, inward, lateral):
     def plane(n):
         if n < DIAGONAL:
             return cut(COUPLINGS, ((lateral, lateral + 1, 4, 5)[n // 4], n % 4), 0)
         if n < BACK_IN:
             return cut(DIAGONALS, (n - DIAGONAL,), 0)
-        if n < BACK_EQ:
-            return cut(COUPLINGS, (inward, n - BACK_IN), 1)
-        if n < BACK_ID:
-            return cut(WELL_FIELDS, (2 + n - BACK_EQ,), 1)
-        return cut(IDS, (), 1).astype(jnp.float32)
+        return cut(COUPLINGS, (inward, n - BACK_IN), 1)
 
     return plane
 
 
 def fill_pack(pack, inward, lateral, cut):
-    late = late_plane(cut, inward, lateral)
+    blocks = layer_blocks(cut, inward, lateral)
     for e in range(4):
         pack[e] = cut(COUPLINGS, (inward, e), 0)
+    wells = [cut(WELL_FIELDS, (2 + a,), 0) for a in range(2)]
     for a in range(2):
-        pack[WELL_EQ + a] = cut(WELL_FIELDS, (2 + a,), 0)
+        pack[WELL_EQ + a] = wells[a]
     pack[WELL_ID] = cut(IDS, (), 0).astype(jnp.float32)
+    pack[BACK_ID] = cut(IDS, (), 1).astype(jnp.float32)
+    for start, at in (
+        (LAT_UP, UP_WELL),
+        (LAT_DOWN, DOWN_WELL),
+        (RISE, RISE_WELL),
+        (FALL, FALL_WELL),
+        (DIAGONAL, DIAGONAL_WELL),
+        (BACK_IN, BACK_WELL),
+    ):
+        if start == BACK_IN:
+            wells = [cut(WELL_FIELDS, (2 + a,), 1) for a in range(2)]
+        for b, value in enumerate(product(lambda e: blocks(start + e), *wells)):
+            pack[at + b] = value
     for k in range(RHS):
         here = [cut(START, (k, a), 0) for a in range(2)]
         back = [cut(START, (k, a), 1) for a in range(2)]
-        entering = product(lambda e: late(BACK_IN + e), *back)
-        local = face_stencil(late, here[0], here[1], entering)
+        entering = product(lambda e: blocks(BACK_IN + e), *back)
+        local = face_stencil(blocks, here[0], here[1], entering)
         for a in range(2):
             pack[GUESS + 2 * k + a] = here[a]
             pack[REST + 2 * k + a] = cut(RIGHT_SIDE, (k, a), 0) - local[a]
     if pack.shape[0] > ENDS:
         end = pack.shape[1] - 1
         for e in range(4):
-            pack[ENDS, e : e + 1, :] = late(LAT_UP + e)[end : end + 1, :]
-            pack[ENDS, 4 + e : 5 + e, :] = late(LAT_DOWN + e)[0:1, :]
+            pack[ENDS, e : e + 1, :] = blocks(LAT_UP + e)[end : end + 1, :]
+            pack[ENDS, 4 + e : 5 + e, :] = blocks(LAT_DOWN + e)[0:1, :]
 
 
 def x_pack_kernel(*refs):
@@ -307,26 +320,21 @@
         )
 
 
-def block_packs(arguments, y_packs, x_late, y_late):
+def y_packs(arguments, packs, all_blocks):
     last = arguments[-1].shape[-2] - 1
     for end in range(2):
 
-        def cut_x(n, index, layer):
-            return arguments[n][index + (last - layer if end else layer,)]
-
-        def cut_y(n, index, layer):
+        def cut(n, index, layer):
             return arguments[n][index + (slice(None), last - layer if end else layer, slice(None))]
 
-        fill_pack(y_packs[end], 3 - end, 0, cut_y)
-        x_plane, y_plane = late_plane(cut_x, 1 - end, 2), late_plane(cut_y, 3 - end, 0)
-        for n in range(LATE_PLANES):
-            x_late[end][n] = x_plane(n)
-            y_late[end][n] = y_plane(n)
-
-
-def spread_kernel(table, *rest):
-    part = rest[-1]
-    part[...] = jnp.broadcast_to(table[...][None], part.shape)
+        fill_pack(packs[end], 3 - end, 0, cut)
+        blocks = layer_blocks(cut, 3 - end, 0)
+        for n in range(LAYER_BLOCKS):
+            all_blocks[end][n] = blocks(n)
+
+
+def spread_kernel(table, face, part):
+    part[...] = jnp.broadcast_to(table[...][None, : part.shape[1]], part.shape)
 
 
 def corner_kernel(y_low, y_high, fxl, fxh, low_out, high_out):
@@ -345,33 +353,23 @@
                 row += 1
 
 
-def image_corner_kernel(
-    y_low, y_high, late_low, late_high, gxl, gxh, low_out, high_out
-):
+def image_corner_kernel(y_low, y_high, gxl, gxh, table, low_out, high_out, part):
+    part[...] = jnp.broadcast_to(table[...][None], part.shape)
     last = gxl.shape[1] - 1
-    for own, late, out, at in (
-        (y_low, late_low, low_out, 0),
-        (y_high, late_high, high_out, last),
-    ):
+    for own, out, at in ((y_low, low_out, 0), (y_high, high_out, last)):
         for n in range(IMAGE_PLANES):
             out[n] = own[n]
-        for n in range(LATE_PLANES):
-            out[IMAGE_PLANES + n] = late[n]
         for x_end, face in enumerate((gxl, gxh)):
             for n in range(8):
-                out[SENT_PLANES + x_end, n : n + 1, :] = face[n, at : at + 1, :]
+                out[IMAGE_PLANES + x_end, n : n + 1, :] = face[n, at : at + 1, :]
 
 
 def guess_kernel(
     couplings, diagonal, wells, ids, right, guess,
-    table_out, present, y_low, y_high, x_late_low, x_late_high, y_late_low, y_late_high,
-    values, scratch,
+    table_out, present, y_low, y_high, low_blocks, high_blocks, values, scratch,
 ):
-    block_packs(
-        (couplings, diagonal, wells, ids, right, guess),
-        (y_low, y_high),
-        (x_late_low, x_late_high),
-        (y_late_low, y_late_high),
+    y_packs(
+        (couplings, diagonal, wells, ids, right, guess), (y_low, y_high), (low_blocks, high_blocks)
     )
     list_wells(ids, present)
     for k in range(RHS):
@@ -384,7 +382,7 @@
 
 def residual_kernel(
     couplings, diagonal, wells, ids, right, guess, fxl, fxh, fyl, fyh, parts,
-    x_late_low, x_late_high,
+    low_blocks, high_blocks,
     residual, image, residual_faces, x_low, x_high, y_low, y_high, small,
 ):
     faces = (fxl, fxh, fyl, fyh)
@@ -430,17 +428,39 @@
         result, _ = block_stencil(couplings, diagonal, now[0], now[1], incoming)
         for a in range(2):
             image[k, a] = result[a]
-            x_low[2 * k + a] = result[a][0]
-            x_low[8 + 2 * k + a] = result[a][1]
-            x_high[2 * k + a] = result[a][last]
-            x_high[8 + 2 * k + a] = result[a][last - 1]
-            y_low[2 * k + a] = result[a][:, 0, :]
-            y_low[8 + 2 * k + a] = result[a][:, 1, :]
-            y_high[2 * k + a] = result[a][:, last, :]
-            y_high[8 + 2 * k + a] = result[a][:, last - 1, :]
-    for late, pack in ((x_late_low, x_low), (x_late_high, x_high)):
-        for n in range(LATE_PLANES):
-            pack[IMAGE_PLANES + n] = late[n]
+        for pack, here, back, blocks in (
+            (
+                x_low,
+                [value[0] for value in result],
+                [value[1] for value in result],
+                layer_blocks(lambda n, i, layer: (couplings, diagonal)[n][i + (layer,)], 1, 2),
+            ),
+            (
+                x_high,
+                [value[last] for value in result],
+                [value[last - 1] for value in result],
+                layer_blocks(
+                    lambda n, i, layer: (couplings, diagonal)[n][i + (last - layer,)], 0, 2
+                ),
+            ),
+            (
+                y_low,
+                [value[:, 0, :] for value in result],
+                [value[:, 1, :] for value in result],
+                lambda n: low_blocks[n],
+            ),
+            (
+                y_high,
+                [value[:, last, :] for value in result],
+                [value[:, last - 1, :] for value in result],
+                lambda n: high_blocks[n],
+            ),
+        ):
+            entering = product(lambda e: blocks(BACK_IN + e), *back)
+            local = face_stencil(blocks, here[0], here[1], entering)
+            for a in range(2):
+                pack[2 * k + a] = here[a]
+                pack[8 + 2 * k + a] = local[a]
     small[...] = jnp.concatenate(
         [unpack_row(totals, 4), unpack_row(totals, 5), jnp.zeros((6, LANES), jnp.float32)], axis=0
     )
@@ -500,10 +520,10 @@
     known[3 * RHS :, :] = jnp.broadcast_to(small[1:2, :], (RHS, LANES))
     dots[...] = jnp.zeros_like(dots)
     corners = corners_of(faces, FACE_PLANES, CORNER_ROWS)
-    sent_corners = corners_of(sent, SENT_PLANES, 8)
+    sent_corners = corners_of(sent, IMAGE_PLANES, 8)
     all_ids = ids[...]
     face_ids = [as_ids(face[WELL_ID]) for face in faces]
-    back_ids = [as_ids(got[IMAGE_PLANES + BACK_ID]) for got in sent]
+    back_ids = [as_ids(face[BACK_ID]) for face in faces]
     corner_ids = [
         as_ids(jnp.broadcast_to(corner.row(SIDE_ID), (8, LANES))) for corner in corners
     ]
@@ -512,16 +532,19 @@
         s_row, s_image = s_rows[k : k + 1, :], s_images[k : k + 1, :]
         at_wells = spread(s_row, all_ids)
         now = [image[k, a] + wells[2 + a] * at_wells for a in range(2)]
-        face_now, back_in = [], []
+        face_now, local = [], []
         for f in range(4):
             face, got = faces[f], sent[f]
             here = spread(s_row, face_ids[f])
+            behind = spread(s_row, back_ids[f])
             face_now.append([got[2 * k + a] + face[WELL_EQ + a] * here for a in range(2)])
-            there = spread(s_row, back_ids[f])
-            back = [
-                got[8 + 2 * k + a] + got[IMAGE_PLANES + BACK_EQ + a] * there for a in range(2)
+            moves = [
+                [face[at + b] * here for b in range(2)]
+                for at in (DIAGONAL_WELL, UP_WELL, DOWN_WELL, RISE_WELL, FALL_WELL)
             ]
-            back_in.append(product(lambda e, f=f: sent[f][IMAGE_PLANES + BACK_IN + e], *back))
+            entering = [face[BACK_WELL + b] * behind for b in range(2)]
+            there = face_moves(*moves, entering)
+            local.append([got[8 + 2 * k + b] + there[b] for b in range(2)])
         corner_now = []
         for c in range(4):
             here = spread(s_row, corner_ids[c])[0:1, :]
@@ -546,14 +569,11 @@
         incoming = []
         for f in range(4):
             face = faces[f]
-            there = face_stencil(
-                lambda n, f=f: sent[f][IMAGE_PLANES + n], *face_now[f], back_in[f]
-            )
             over = face_entries(ends[(f, 0)], ends[(f, 1)], outgoing[f])
             here = spread(s_image, face_ids[f])
             outer = []
             for a in range(2):
-                twice = there[a] + over[a] + face[WELL_EQ + a] * here
+                twice = local[f][a] + over[a] + face[WELL_EQ + a] * here
                 base = (face_now[f][a] - height * residual_faces[f, 2 * k + a]) * scale
                 outer.append((twice - height * face_now[f][a]) * scale - shift * base)
             incoming.append(product(lambda e, f=f: faces[f][e], *outer))
@@ -707,21 +727,20 @@
     x_low, x_high = call(
         x_pack_kernel,
         [(FACE_PLANES + 1,) + plane] * 2,
-        arguments,
+        [pltpu.with_memory_space_constraint(argument, pltpu.HBM) for argument in arguments],
         ends + [pltpu.SemaphoreType.DMA((len(ends),))],
         own_copies=True,
-        grant=60 << 20,
     )
     fxl = from_behind(x_high, "gx", 1)
     fxh = from_behind(x_low, "gx", -1)
-    table, present, y_low, y_high, *late = call(
+    table, present, y_low, y_high, *y_blocks = call(
         guess_kernel,
-        [plane, (WELLS + 1,)] + [(FACE_PLANES,) + plane] * 2 + [(LATE_PLANES,) + plane] * 4,
+        [plane, (WELLS + 1,)] + [(FACE_PLANES,) + plane] * 2 + [(LAYER_BLOCKS,) + plane] * 2,
         arguments,
         [held(6, *block), held(6, WELLS, LANES)],
         cost=4 << 20,
     )
-    (part,) = call(spread_kernel, [(devices, 8, LANES)], (table, fxl))
+    (part,) = call(spread_kernel, [(devices, TABLE_ROWS, LANES)], (table, fxl))
     parts = exchanged(part)
     y_low, y_high = call(
         corner_kernel,
@@ -734,11 +753,8 @@
     faces = (fxl, fxh, fyl, fyh)
     residual, image, residual_faces, x_low, x_high, y_low, y_high, small = call(
         residual_kernel,
-        [field, field, (4, 8) + plane]
-        + [(SENT_PLANES,) + plane] * 2
-        + [(IMAGE_PLANES,) + plane] * 2
-        + [(8, LANES)],
-        arguments + faces + (parts, late[0], late[1]),
+        [field, field, (4, 8) + plane] + [(IMAGE_PLANES,) + plane] * 4 + [(8, LANES)],
+        arguments + faces + (parts, *y_blocks),
     )
     gxl = from_behind(x_high, "gx", 1)
     gxh = from_behind(x_low, "gx", -1)
@@ -749,13 +765,12 @@
         [held(16, *block), held(16, WELLS, LANES), held(3, *plane)],
         cost=4 << 20,
     )
-    (part,) = call(spread_kernel, [(devices, 8, LANES)], (table, gxl, gxh))
+    y_low, y_high, part = call(
+        image_corner_kernel,
+        [(IMAGE_PLANES + 2,) + plane] * 2 + [(devices, 8, LANES)],
+        (y_low, y_high, gxl, gxh, table),
+    )
     parts = exchanged(part)
-    y_low, y_high = call(
-        image_corner_kernel,
-        [(SENT_PLANES + 2,) + plane] * 2,
-        (y_low, y_high, late[2], late[3], gxl, gxh),
-    )
     gyl = from_behind(y_high, "gy", 1)
     gyh = from_behind(y_low, "gy", -1)
 

time: 78.1 us -> 70.4 us (0.901)
  waiting for transfers between devices: 19.2 us -> 12.7 us
  Pallas kernels: 12.9 us -> 14.6 us
  blocking collectives: 15.4 us -> 13.9 us
  starting transfers between devices: 29.9 us -> 28.5 us
    ppermute x8, waiting for transfers between devices: 17.6 us -> 9.36 us  [from_behind(): lax.ppermute(value, axis, [(source, source + steps) for source in range(l...]
    all_to_all x2, waiting for transfers between devices: 1.57 us -> 3.34 us  [exchanged(): return lax.all_to_all(part, ('gx', 'gy'), 0, 0, tiled=True)]
    pallas_call x10 -> x9, Pallas kernels: 12.9 us -> 14.6 us  [call(): pl.pallas_call(kernel, out_shape=outs, in_specs=[place(argument) for argu...]
    all_to_all x1, blocking collectives: 15.4 us -> 13.9 us  [exchanged(): return lax.all_to_all(part, ('gx', 'gy'), 0, 0, tiled=True)]
    all_to_all x2, starting transfers between devices: 12.6 us -> 11.5 us  [exchanged(): return lax.all_to_all(part, ('gx', 'gy'), 0, 0, tiled=True)]
  transfers between devices with their start and end apart: 10 -> 10, of which waited for: 6 -> 5; matrix products, arithmetic and copies ran while one was open for 0% -> 0% of each run, Pallas kernels for 5% -> 8%
where the time goes in v11:
time: 70.4 us; the launch traced here: 69.9 us
  starting transfers between devices  28.5 us (40%)
  Pallas kernels  14.6 us (21%)
  blocking collectives  13.9 us (20%)
  waiting for transfers between devices  12.7 us (18%)
    ppermute x8, starting transfers between devices, from_behind(): lax.ppermute(value, axis, [(source, source + steps) for source in range(l...  17 us
    pallas_call x9, Pallas kernels, call(): pl.pallas_call(kernel, out_shape=outs, in_specs=[place(argument) for argu...  14.6 us
    all_to_all x1, blocking collectives, exchanged(): return lax.all_to_all(part, ('gx', 'gy'), 0, 0, tiled=True)  13.9 us
    all_to_all x2, starting transfers between devices, exchanged(): return lax.all_to_all(part, ('gx', 'gy'), 0, 0, tiled=True)  11.5 us
    ppermute x8, waiting for transfers between devices, from_behind(): lax.ppermute(value, axis, [(source, source + steps) for source in range(l...  9.36 us
    all_to_all x2, waiting for transfers between devices, exchanged(): return lax.all_to_all(part, ('gx', 'gy'), 0, 0, tiled=True)  3.34 us
  transfers between devices with their start and end apart: 10, of which 5 were waited for; matrix products, arithmetic and copies ran while one was open for 0% of the time, Pallas kernels for 8%

profile of v11, /device:TPU:0, one launch (start us, length us, event | category | flops | bytes accessed | tf_op | source)
XLA Modules:
  0.0 69.9 jit_solution(7118572588622741840)
XLA Ops:
  0.0 0.0 copy-start.5
  0.0 0.0 copy-start.2
  0.0 0.0 copy-start.1
  0.0 0.0 copy-start.4
  0.0 0.0 copy-start
  0.0 0.0 copy-start.3
  0.0 1.5 %shard_map.64 = (f32[37,8,128]{2,1,0:T(8,128)S(1)}, f32[37,8,128]{2,1,0:T(8,128)S(1)}) custom-call(f32[6,4,8,8,128]{4,3,2,1,0:T(8,128)} %couplings.5, f32[4,8,8,128]{3,2,1,0:T(8,128)} %diagonal.5, f32[4,8,8,128]{3,2,1,0:T(8,128)} %wells.7, s32[8,8,128]{2,1,0:T(8,128)} %ids.7, f32[4,2,8,8,128]{4,3,2,1,0:T(8,128)} %right.3, f32[4,2,8,8,128]{4,3,2,1,0:T(8,128)} %guess.5), custom_call_target="tpu_custom_call" | custom-call | tf_op jit(solution)/shard_map/pallas_call | solution.py:689
  1.5 5.0 %collective-permute-start = (f32[37,8,128]{2,1,0:T(8,128)S(1)}, f32[37,8,128]{2,1,0:T(8,128)S(1)}, u32[]{:S(2)}, u32[]{:S(2)}) collective-permute-start(f32[37,8,128]{2,1,0:T(8,128)S(1)} %get-tuple-element.30), channel_id=1, source_target_pairs={{0,8},{8,16},{16,24},{1,9},{9,17},{17,25},{2,10},{10,18},{18,26},{... | collective-permute-start | bytes 454664 | tf_op jit(solution)/shard_map/ppermute | solution.py:709
  6.5 1.3 %collective-permute-start.1 = (f32[37,8,128]{2,1,0:T(8,128)S(1)}, f32[37,8,128]{2,1,0:T(8,128)S(1)}, u32[]{:S(2)}, u32[]{:S(2)}) collective-permute-start(f32[37,8,128]{2,1,0:T(8,128)S(1)} %get-tuple-element.31), channel_id=1, source_target_pairs={{8,0},{16,8},{24,16},{9,1},{17,9},{25,17},{10,2},{18,10},{26,18},{... | collective-permute-start | bytes 454664 | tf_op jit(solution)/shard_map/ppermute | solution.py:709
  7.8 0.0 copy-done.5
  7.8 0.0 copy-done.2
  7.8 0.0 copy-done.1
  7.8 0.0 copy-done.4
  7.8 0.0 copy-done
  7.9 0.0 copy-done.3
  7.9 3.5 %shard_map.65 = (f32[8,128]{1,0:T(8,128)S(1)}, s32[41]{0:T(128)S(1)}, f32[36,8,128]{2,1,0:T(8,128)S(1)}, f32[36,8,128]{2,1,0:T(8,128)S(1)}, f32[24,8,128]{2,1,0:T(8,128)S(1)}, /*index=5*/f32[24,8,128]{2,1,0:T(8,128)S(1)}) custom-call(f32[6,4,8,8,128]{4,3,2,1,0:T(8,128)S(1)} %copy-done, f32[4,8,8,128]{3,2,1,0:T(8,128)S(1)} %copy-done.4, ...), custom_call_target="tpu_custom_call" | custom-call | flops 4194304 | bytes 4194304 | tf_op jit(solution)/shard_map/pallas_call | solution.py:689
  11.3 0.0 collective-permute-done.fxl.face
  11.3 0.7 shard_map.67
  12.0 5.2 %all-to-all-start = ((f32[32,6,128]{2,1,0:T(8,128)}), f32[32,6,128]{2,1,0:T(8,128)S(1)}, u32[]{:S(2)}, u32[]{:S(2)}) async-start(f32[32,6,128]{2,1,0:T(8,128)} %shard_map.67), calls=%async_computation | async-start | bytes 262144 | tf_op jit(solution)/shard_map/all_to_all | solution.py:713
  17.2 0.0 collective-permute-done.1.fxh
  17.2 2.2 %collective-permute-start.2 = (f32[41,8,128]{2,1,0:T(8,128)S(1)}, f32[41,8,128]{2,1,0:T(8,128)S(1)}, u32[]{:S(2)}, u32[]{:S(2)}) collective-permute-start(f32[41,8,128]{2,1,0:T(8,128)S(1)} %get-tuple-element.34), channel_id=1, source_target_pairs={{0,1},{1,2},{2,3},{3,4},{4,5},{5,6},{6,7},{8,9},{9,10},{10,11},{11... | collective-permute-start | bytes 503816 | tf_op jit(solution)/shard_map/ppermute | solution.py:709
  19.4 1.3 %collective-permute-start.3 = (f32[41,8,128]{2,1,0:T(8,128)S(1)}, f32[41,8,128]{2,1,0:T(8,128)S(1)}, u32[]{:S(2)}, u32[]{:S(2)}) collective-permute-start(f32[41,8,128]{2,1,0:T(8,128)S(1)} %get-tuple-element.35), channel_id=1, source_target_pairs={{1,0},{2,1},{3,2},{4,3},{5,4},{6,5},{7,6},{9,8},{10,9},{11,10},{12... | collective-permute-start | bytes 503816 | tf_op jit(solution)/shard_map/ppermute | solution.py:709
  20.7 0.0 collective-permute-done.2.fyl
  20.7 3.1 %collective-permute-done.3.fyh = f32[41,8,128]{2,1,0:T(8,128)S(1)} collective-permute-done((f32[41,8,128]{2,1,0:T(8,128)S(1)}, f32[41,8,128]{2,1,0:T(8,128)S(1)}, u32[]{:S(2)}, u32[]{:S(2)}) %collective-permute-start.3) | collective-permute-done | bytes 167968 | tf_op jit(solution)/shard_map/ppermute | solution.py:709
  23.8 1.6 %all-to-all-done.parts = f32[32,6,128]{2,1,0:T(8,128)S(1)} async-done(((f32[32,6,128]{2,1,0:T(8,128)}), f32[32,6,128]{2,1,0:T(8,128)S(1)}, u32[]{:S(2)}, u32[]{:S(2)}) %all-to-all-start) | async-done | bytes 98336 | tf_op jit(solution)/shard_map/all_to_all | solution.py:713
  25.4 1.2 %shard_map.68 = (f32[4,2,8,8,128]{4,3,2,1,0:T(8,128)S(1)}, f32[4,2,8,8,128]{4,3,2,1,0:T(8,128)S(1)}, f32[4,8,8,128]{3,2,1,0:T(8,128)S(1)}, f32[16,8,128]{2,1,0:T...) custom-call(f32[6,4,8,8,128]{4,3,2,1,0:T(8,128)S(1)} %copy-done, ...), custom_call_target="tpu_custom_call" | custom-call | tf_op jit(solution)/shard_map/pallas_call | solution.py:689
  26.6 2.6 %collective-permute-start.4 = (f32[16,8,128]{2,1,0:T(8,128)S(1)}, f32[16,8,128]{2,1,0:T(8,128)S(1)}, u32[]{:S(2)}, u32[]{:S(2)}) collective-permute-start(f32[16,8,128]{2,1,0:T(8,128)S(1)} %get-tuple-element.40), channel_id=1, source_target_pairs={{0,8},{8,16},{16,24},{1,9},{9,17},{17,25},{2,10},{10,18},{18,26},{... | collective-permute-start | bytes 196616 | tf_op jit(solution)/shard_map/ppermute | solution.py:709
  29.2 1.3 %collective-permute-start.5 = (f32[16,8,128]{2,1,0:T(8,128)S(1)}, f32[16,8,128]{2,1,0:T(8,128)S(1)}, u32[]{:S(2)}, u32[]{:S(2)}) collective-permute-start(f32[16,8,128]{2,1,0:T(8,128)S(1)} %get-tuple-element.41), channel_id=1, source_target_pairs={{8,0},{16,8},{24,16},{9,1},{17,9},{25,17},{10,2},{18,10},{26,18},{... | collective-permute-start | bytes 196616 | tf_op jit(solution)/shard_map/ppermute | solution.py:709
  30.5 1.6 %shard_map.69.table = f32[8,128]{1,0:T(8,128)S(1)} custom-call(f32[4,8,8,128]{3,2,1,0:T(8,128)S(1)} %copy-done.2, s32[8,8,128]{2,1,0:T(8,128)S(1)} %copy-done.5, f32[4,2,8,8,128]{4,3,2,1,0:T(8,128)S(1)} %get-tuple-element.39.residual, f32[4,2,8,8,128]{4,3,2,1,0:T(8,128)S(1)} %get-tuple-element.44.image, s32[41]{0:T(128)S(1)} %get-tuple-element.45.present), custom_call_target="tpu_custom_call" | custom-call | flops 4194304 | bytes 4194304 | tf_op jit(solution)/shard_map/pallas_call | solution.py:689
  32.1 0.0 collective-permute-done.4.gxl
  32.1 3.3 %collective-permute-done.5.gxh = f32[16,8,128]{2,1,0:T(8,128)S(1)} collective-permute-done((f32[16,8,128]{2,1,0:T(8,128)S(1)}, f32[16,8,128]{2,1,0:T(8,128)S(1)}, u32[]{:S(2)}, u32[]{:S(2)}) %collective-permute-start.5) | collective-permute-done | bytes 65568 | tf_op jit(solution)/shard_map/ppermute | solution.py:709
  35.3 0.7 shard_map.70
  36.0 6.3 %all-to-all-start.1 = ((f32[32,8,128]{2,1,0:T(8,128)}), f32[32,8,128]{2,1,0:T(8,128)S(1)}, u32[]{:S(2)}, u32[]{:S(2)}) async-start(f32[32,8,128]{2,1,0:T(8,128)} %get-tuple-element.49), calls=%async_computation.1 | async-start | bytes 262144 | tf_op jit(solution)/shard_map/all_to_all | solution.py:713
  42.3 2.2 %collective-permute-start.6 = (f32[18,8,128]{2,1,0:T(8,128)S(1)}, f32[18,8,128]{2,1,0:T(8,128)S(1)}, u32[]{:S(2)}, u32[]{:S(2)}) collective-permute-start(f32[18,8,128]{2,1,0:T(8,128)S(1)} %get-tuple-element.46), channel_id=1, source_target_pairs={{0,1},{1,2},{2,3},{3,4},{4,5},{5,6},{6,7},{8,9},{9,10},{10,11},{11... | collective-permute-start | bytes 221192 | tf_op jit(solution)/shard_map/ppermute | solution.py:709
  44.5 1.3 %collective-permute-start.7 = (f32[18,8,128]{2,1,0:T(8,128)S(1)}, f32[18,8,128]{2,1,0:T(8,128)S(1)}, u32[]{:S(2)}, u32[]{:S(2)}) collective-permute-start(f32[18,8,128]{2,1,0:T(8,128)S(1)} %get-tuple-element.47), channel_id=1, source_target_pairs={{1,0},{2,1},{3,2},{4,3},{5,4},{6,5},{7,6},{9,8},{10,9},{11,10},{12... | collective-permute-start | bytes 221192 | tf_op jit(solution)/shard_map/ppermute | solution.py:709
  45.8 0.0 collective-permute-done.6.gyl
  45.8 3.0 %collective-permute-done.7.gyh = f32[18,8,128]{2,1,0:T(8,128)S(1)} collective-permute-done((f32[18,8,128]{2,1,0:T(8,128)S(1)}, f32[18,8,128]{2,1,0:T(8,128)S(1)}, u32[]{:S(2)}, u32[]{:S(2)}) %collective-permute-start.7) | collective-permute-done | bytes 73760 | tf_op jit(solution)/shard_map/ppermute | solution.py:709
  48.8 1.8 %all-to-all-done.1.parts = f32[32,8,128]{2,1,0:T(8,128)S(1)} async-done(((f32[32,8,128]{2,1,0:T(8,128)}), f32[32,8,128]{2,1,0:T(8,128)S(1)}, u32[]{:S(2)}, u32[]{:S(2)}) %all-to-all-start.1) | async-done | bytes 131104 | tf_op jit(solution)/shard_map/all_to_all | solution.py:713
  50.5 3.9 %shard_map.71 = (f32[4,2,8,8,128]{4,3,2,1,0:T(8,128)S(1)}, f32[4,2,8,8,128]{4,3,2,1,0:T(8,128)S(1)}, f32[32,8,128]{2,1,0:T(8,128)S(1)}, f32[16,128]{1,0:T(8,128)S(1)}) custom-call(f32[6,4,8,8,128]{4,3,2,1,0:T(8,128)S(1)} %copy-done, f32[4,8,8,128]{3,2,1,0:T(8,128)S(1)} %copy-done.4, f32[4,8,8,128]{3,2,1,0:T(8,128)S(1)} %copy-done.2, ...), custom_call_target="tpu_custom_call" | custom-call | tf_op jit(solution)/shard_map/pallas_call | solution.py:689
  54.4 13.9 %all_to_all.15.parts = f32[32,8,128]{2,1,0:T(8,128)S(1)} all-to-all(f32[32,8,128]{2,1,0:T(8,128)S(1)} %get-tuple-element.53), channel_id=1, replica_groups=mesh['member'=1,'gx'=4,'gy'=8] {'gx','gy'}, dimensions={0} | all-to-all | bytes 262144 | tf_op jit(solution)/shard_map/all_to_all | solution.py:713
  68.3 1.6 %shard_map.72 = f32[4,2,8,8,128]{4,3,2,1,0:T(8,128)} custom-call(f32[4,2,8,8,128]{4,3,2,1,0:T(8,128)S(1)} %copy-done.1, f32[4,2,8,8,128]{4,3,2,1,0:T(8,128)S(1)} %get-tuple-element.39.residual, f32[4,2,8,8,128]{4,3,2,1,0:T(8,128)S(1)} %get-tuple-element.51.second, f32[4,2,8,8,128]{4,3,2,1,0:T(8,128)S(1)} %get-tuple-element.52.third, ...), custom_call_target="tpu_custom_call" | custom-call | tf_op jit(solution)/shard_map/pallas_call | solution.py:689
  (1 shorter events, 0.0 us)
Async XLA Ops:
  0.0 7.8 %copy-start.5 = (s32[8,8,128]{2,1,0:T(8,128)S(1)}, s32[8,8,128]{2,1,0:T(8,128)}, u32[]{:S(2)}) copy-start(s32[8,8,128]{2,1,0:T(8,128)} %ids.7) | copy-start | bytes 98308
  0.0 7.8 %copy-start.2 = (f32[4,8,8,128]{3,2,1,0:T(8,128)S(1)}, f32[4,8,8,128]{3,2,1,0:T(8,128)}, u32[]{:S(2)}) copy-start(f32[4,8,8,128]{3,2,1,0:T(8,128)} %wells.7) | copy-start | bytes 393220
  0.0 7.8 %copy-start.1 = (f32[4,2,8,8,128]{4,3,2,1,0:T(8,128)S(1)}, f32[4,2,8,8,128]{4,3,2,1,0:T(8,128)}, u32[]{:S(2)}) copy-start(f32[4,2,8,8,128]{4,3,2,1,0:T(8,128)} %guess.5) | copy-start | bytes 786436
  0.0 7.8 %copy-start.4 = (f32[4,8,8,128]{3,2,1,0:T(8,128)S(1)}, f32[4,8,8,128]{3,2,1,0:T(8,128)}, u32[]{:S(2)}) copy-start(f32[4,8,8,128]{3,2,1,0:T(8,128)} %diagonal.5) | copy-start | bytes 393220
  0.0 7.8 %copy-start = (f32[6,4,8,8,128]{4,3,2,1,0:T(8,128)S(1)}, f32[6,4,8,8,128]{4,3,2,1,0:T(8,128)}, u32[]{:S(2)}) copy-start(f32[6,4,8,8,128]{4,3,2,1,0:T(8,128)} %couplings.5) | copy-start | bytes 2359300
  0.0 7.8 %copy-start.3 = (f32[4,2,8,8,128]{4,3,2,1,0:T(8,128)S(1)}, f32[4,2,8,8,128]{4,3,2,1,0:T(8,128)}, u32[]{:S(2)}) copy-start(f32[4,2,8,8,128]{4,3,2,1,0:T(8,128)} %right.3) | copy-start | bytes 786436
  1.5 9.8 %collective-permute-start = (f32[37,8,128]{2,1,0:T(8,128)S(1)}, f32[37,8,128]{2,1,0:T(8,128)S(1)}, u32[]{:S(2)}, u32[]{:S(2)}) collective-permute-start(f32[37,8,128]{2,1,0:T(8,128)S(1)} %get-tuple-element.30), channel_id=1, source_target_pairs={{0,8},{8,16},{16,24},{1,9},{9,17},{17,25},{2,10},{10,18},{18,26},{... | collective-permute-start | bytes 454664 | tf_op jit(solution)/shard_map/ppermute | solution.py:709
  6.5 10.7 %collective-permute-start.1 = (f32[37,8,128]{2,1,0:T(8,128)S(1)}, f32[37,8,128]{2,1,0:T(8,128)S(1)}, u32[]{:S(2)}, u32[]{:S(2)}) collective-permute-start(f32[37,8,128]{2,1,0:T(8,128)S(1)} %get-tuple-element.31), channel_id=1, source_target_pairs={{8,0},{16,8},{24,16},{9,1},{17,9},{25,17},{10,2},{18,10},{26,18},{... | collective-permute-start | bytes 454664 | tf_op jit(solution)/shard_map/ppermute | solution.py:709
  12.0 13.4 %all-to-all-start = ((f32[32,6,128]{2,1,0:T(8,128)}), f32[32,6,128]{2,1,0:T(8,128)S(1)}, u32[]{:S(2)}, u32[]{:S(2)}) async-start(f32[32,6,128]{2,1,0:T(8,128)} %shard_map.67), calls=%async_computation | async-start | bytes 262144 | tf_op jit(solution)/shard_map/all_to_all | solution.py:713
  17.2 3.5 %collective-permute-start.2 = (f32[41,8,128]{2,1,0:T(8,128)S(1)}, f32[41,8,128]{2,1,0:T(8,128)S(1)}, u32[]{:S(2)}, u32[]{:S(2)}) collective-permute-start(f32[41,8,128]{2,1,0:T(8,128)S(1)} %get-tuple-element.34), channel_id=1, source_target_pairs={{0,1},{1,2},{2,3},{3,4},{4,5},{5,6},{6,7},{8,9},{9,10},{10,11},{11... | collective-permute-start | bytes 503816 | tf_op jit(solution)/shard_map/ppermute | solution.py:709
  19.4 4.4 %collective-permute-start.3 = (f32[41,8,128]{2,1,0:T(8,128)S(1)}, f32[41,8,128]{2,1,0:T(8,128)S(1)}, u32[]{:S(2)}, u32[]{:S(2)}) collective-permute-start(f32[41,8,128]{2,1,0:T(8,128)S(1)} %get-tuple-element.35), channel_id=1, source_target_pairs={{1,0},{2,1},{3,2},{4,3},{5,4},{6,5},{7,6},{9,8},{10,9},{11,10},{12... | collective-permute-start | bytes 503816 | tf_op jit(solution)/shard_map/ppermute | solution.py:709
  26.6 5.5 %collective-permute-start.4 = (f32[16,8,128]{2,1,0:T(8,128)S(1)}, f32[16,8,128]{2,1,0:T(8,128)S(1)}, u32[]{:S(2)}, u32[]{:S(2)}) collective-permute-start(f32[16,8,128]{2,1,0:T(8,128)S(1)} %get-tuple-element.40), channel_id=1, source_target_pairs={{0,8},{8,16},{16,24},{1,9},{9,17},{17,25},{2,10},{10,18},{18,26},{... | collective-permute-start | bytes 196616 | tf_op jit(solution)/shard_map/ppermute | solution.py:709
  29.2 6.2 %collective-permute-start.5 = (f32[16,8,128]{2,1,0:T(8,128)S(1)}, f32[16,8,128]{2,1,0:T(8,128)S(1)}, u32[]{:S(2)}, u32[]{:S(2)}) collective-permute-start(f32[16,8,128]{2,1,0:T(8,128)S(1)} %get-tuple-element.41), channel_id=1, source_target_pairs={{8,0},{16,8},{24,16},{9,1},{17,9},{25,17},{10,2},{18,10},{26,18},{... | collective-permute-start | bytes 196616 | tf_op jit(solution)/shard_map/ppermute | solution.py:709
  36.0 14.5 %all-to-all-start.1 = ((f32[32,8,128]{2,1,0:T(8,128)}), f32[32,8,128]{2,1,0:T(8,128)S(1)}, u32[]{:S(2)}, u32[]{:S(2)}) async-start(f32[32,8,128]{2,1,0:T(8,128)} %get-tuple-element.49), calls=%async_computation.1 | async-start | bytes 262144 | tf_op jit(solution)/shard_map/all_to_all | solution.py:713
  42.3 3.5 %collective-permute-start.6 = (f32[18,8,128]{2,1,0:T(8,128)S(1)}, f32[18,8,128]{2,1,0:T(8,128)S(1)}, u32[]{:S(2)}, u32[]{:S(2)}) collective-permute-start(f32[18,8,128]{2,1,0:T(8,128)S(1)} %get-tuple-element.46), channel_id=1, source_target_pairs={{0,1},{1,2},{2,3},{3,4},{4,5},{5,6},{6,7},{8,9},{9,10},{10,11},{11... | collective-permute-start | bytes 221192 | tf_op jit(solution)/shard_map/ppermute | solution.py:709
  44.5 4.3 %collective-permute-start.7 = (f32[18,8,128]{2,1,0:T(8,128)S(1)}, f32[18,8,128]{2,1,0:T(8,128)S(1)}, u32[]{:S(2)}, u32[]{:S(2)}) collective-permute-start(f32[18,8,128]{2,1,0:T(8,128)S(1)} %get-tuple-element.47), channel_id=1, source_target_pairs={{1,0},{2,1},{3,2},{4,3},{5,4},{6,5},{7,6},{9,8},{10,9},{11,10},{12... | collective-permute-start | bytes 221192 | tf_op jit(solution)/shard_map/ppermute | solution.py:709

commit v12 on v11

--- a/solution.py
+++ b/solution.py
@@ -18,6 +18,7 @@
 LAYER_BLOCKS = 24
 IMAGE_PLANES = 16
 TABLE_ROWS = 6
+GRAM_ENTRIES = 10
 CORNER_ROWS = 19
 SIDE_IN, SIDE_EQ, SIDE_ID, SIDE_GUESS = 4, 8, 10, 11
 
@@ -333,8 +334,11 @@
             all_blocks[end][n] = blocks(n)
 
 
-def spread_kernel(table, face, part):
-    part[...] = jnp.broadcast_to(table[...][None, : part.shape[1]], part.shape)
+def send_out(table, chunks, part, sent):
+    chunks[...] = jnp.broadcast_to(table[None, : chunks.shape[1]], chunks.shape)
+    copy = pltpu.make_async_copy(chunks, part, sent.at[0])
+    copy.start()
+    return copy
 
 
 def corner_kernel(y_low, y_high, fxl, fxh, low_out, high_out):
@@ -353,8 +357,7 @@
                 row += 1
 
 
-def image_corner_kernel(y_low, y_high, gxl, gxh, table, low_out, high_out, part):
-    part[...] = jnp.broadcast_to(table[...][None], part.shape)
+def image_corner_kernel(y_low, y_high, gxl, gxh, low_out, high_out):
     last = gxl.shape[1] - 1
     for own, out, at in ((y_low, low_out, 0), (y_high, high_out, last)):
         for n in range(IMAGE_PLANES):
@@ -366,18 +369,21 @@
 
 def guess_kernel(
     couplings, diagonal, wells, ids, right, guess,
-    table_out, present, y_low, y_high, low_blocks, high_blocks, values, scratch,
+    part, present, y_low, y_high, low_blocks, high_blocks,
+    values, scratch, chunks, sent,
 ):
-    y_packs(
-        (couplings, diagonal, wells, ids, right, guess), (y_low, y_high), (low_blocks, high_blocks)
-    )
     list_wells(ids, present)
     for k in range(RHS):
         values[k] = wells[0] * guess[k, 0] + wells[1] * guess[k, 1]
     values[4] = wells[0] * wells[2] + wells[1] * wells[3]
     values[5] = wells[2] * wells[2] + wells[3] * wells[3]
     rows = segment_rows(ids, values, scratch, present)
-    table_out[...] = pack_rows(rows, jnp.zeros((8, LANES), jnp.float32))
+    table = pack_rows(rows, jnp.zeros((8, LANES), jnp.float32))
+    copy = send_out(table, chunks, part, sent)
+    y_packs(
+        (couplings, diagonal, wells, ids, right, guess), (y_low, y_high), (low_blocks, high_blocks)
+    )
+    copy.wait()
 
 
 def residual_kernel(
@@ -467,7 +473,7 @@
 
 
 def moments_kernel(
-    wells, ids, residual, image, present, table_out, values, scratch, dots
+    wells, ids, residual, image, present, part, values, scratch, dots, chunks, sent
 ):
     dots[...] = jnp.zeros_like(dots)
     for k in range(RHS):
@@ -482,7 +488,7 @@
         dots[2, row, :] = tile_sum(result, result)
     rows = segment_rows(ids, values, scratch, present)
     table = place_rows(rows, jnp.zeros((8, LANES), jnp.float32))
-    table_out[...] = place_columns(dots, WELLS, table)
+    send_out(place_columns(dots, WELLS, table), chunks, part, sent).wait()
 
 
 def first_step(totals, small):
@@ -532,19 +538,13 @@
         s_row, s_image = s_rows[k : k + 1, :], s_images[k : k + 1, :]
         at_wells = spread(s_row, all_ids)
         now = [image[k, a] + wells[2 + a] * at_wells for a in range(2)]
-        face_now, local = [], []
+        face_now, spread_now = [], []
         for f in range(4):
-            face, got = faces[f], sent[f]
             here = spread(s_row, face_ids[f])
-            behind = spread(s_row, back_ids[f])
-            face_now.append([got[2 * k + a] + face[WELL_EQ + a] * here for a in range(2)])
-            moves = [
-                [face[at + b] * here for b in range(2)]
-                for at in (DIAGONAL_WELL, UP_WELL, DOWN_WELL, RISE_WELL, FALL_WELL)
-            ]
-            entering = [face[BACK_WELL + b] * behind for b in range(2)]
-            there = face_moves(*moves, entering)
-            local.append([got[8 + 2 * k + b] + there[b] for b in range(2)])
+            spread_now.append((here, spread(s_row, back_ids[f])))
+            face_now.append(
+                [sent[f][2 * k + a] + faces[f][WELL_EQ + a] * here for a in range(2)]
+            )
         corner_now = []
         for c in range(4):
             here = spread(s_row, corner_ids[c])[0:1, :]
@@ -569,11 +569,18 @@
         incoming = []
         for f in range(4):
             face = faces[f]
+            here, behind = spread_now[f]
+            moves = [
+                [face[at + b] * here for b in range(2)]
+                for at in (DIAGONAL_WELL, UP_WELL, DOWN_WELL, RISE_WELL, FALL_WELL)
+            ]
+            there = face_moves(*moves, [face[BACK_WELL + b] * behind for b in range(2)])
+            local = [sent[f][8 + 2 * k + b] + there[b] for b in range(2)]
             over = face_entries(ends[(f, 0)], ends[(f, 1)], outgoing[f])
             here = spread(s_image, face_ids[f])
             outer = []
             for a in range(2):
-                twice = local[f][a] + over[a] + face[WELL_EQ + a] * here
+                twice = local[a] + over[a] + face[WELL_EQ + a] * here
                 base = (face_now[f][a] - height * residual_faces[f, 2 * k + a]) * scale
                 outer.append((twice - height * face_now[f][a]) * scale - shift * base)
             incoming.append(product(lambda e, f=f: faces[f][e], *outer))
@@ -591,11 +598,19 @@
     rows = segment_rows(ids, values_scratch, scratch, present)
     table = place_rows(rows, jnp.zeros((8, LANES), jnp.float32))
     table = place_columns(dots, 0, table)
-    part[...] = jnp.broadcast_to(table[None], part.shape)
+    gram = table[RHS : RHS + 1, :]
+    for k in range(1, RHS):
+        gram = gram + pltpu.roll(table[RHS + k : RHS + k + 1, :], GRAM_ENTRIES * k, 1)
+    flat = jnp.concatenate([table[k : k + 1, :] for k in range(RHS)] + [gram], axis=1)
+    part[...] = jnp.broadcast_to(flat[None], part.shape)
 
 
 def solve_kernel(guess, residual, second, third, parts, known, solution):
-    totals = jnp.sum(parts[...], axis=0)
+    flat = jnp.sum(parts[...], axis=0)
+    rows = [flat[:, LANES * n : LANES * (n + 1)] for n in range(RHS + 1)]
+    for k in range(1, RHS):
+        rows.append(pltpu.roll(rows[RHS], LANES - GRAM_ENTRIES * k, 1))
+    totals = jnp.concatenate(rows, axis=0)
     s_third, p_third, p_fourth = (take_group(totals, group) for group in range(3))
     p_first, p_second = known[0:RHS, :], known[RHS : 2 * RHS, :]
     unit, beta, height, shift, following = (
@@ -672,7 +687,7 @@
             )
 
 
-def call(kernel, shapes, arguments, scratch=(), own_copies=False, cost=0, grant=24 << 20):
+def call(kernel, shapes, arguments, scratch=(), own_copies=False, cost=0, grant=24 << 20, out=0):
     whole = pl.BlockSpec(memory_space=pltpu.VMEM)
     far = pl.BlockSpec(memory_space=pltpu.HBM)
     scalars = pl.BlockSpec(memory_space=pltpu.SMEM)
@@ -686,17 +701,34 @@
         jax.ShapeDtypeStruct(shape, jnp.float32 if len(shape) > 1 else jnp.int32)
         for shape in shapes
     ]
+    outs[:out] = [pltpu.HBM(shape, jnp.float32) for shape in shapes[:out]]
     return pl.pallas_call(
         kernel,
         out_shape=outs,
         in_specs=[place(argument) for argument in arguments],
-        out_specs=[scalars if len(shape) == 1 else whole for shape in shapes],
+        out_specs=[far] * out + [scalars if len(shape) == 1 else whole for shape in shapes[out:]],
         scratch_shapes=list(scratch),
         compiler_params=pltpu.CompilerParams(vmem_limit_bytes=grant),
         cost_estimate=pl.CostEstimate(flops=cost, bytes_accessed=cost, transcendentals=0)
         if cost
         else None,
     )(*arguments)
+
+
+def nothing(value, *rest):
+    pass
+
+
+def after(value, *others):
+    far = pl.BlockSpec(memory_space=pltpu.HBM)
+    anywhere = pl.BlockSpec(memory_space=pl.ANY)
+    return pl.pallas_call(
+        nothing,
+        out_shape=pltpu.HBM(value.shape, value.dtype),
+        in_specs=[far] + [anywhere] * len(others),
+        out_specs=far,
+        input_output_aliases={0: 0},
+    )(pltpu.with_memory_space_constraint(value, pltpu.HBM), *others)
 
 
 def held(*shape):
@@ -733,15 +765,19 @@
     )
     fxl = from_behind(x_high, "gx", 1)
     fxh = from_behind(x_low, "gx", -1)
-    table, present, y_low, y_high, *y_blocks = call(
+    first_chunks, chunks = (devices, TABLE_ROWS, LANES), (devices, 8, LANES)
+    sent = pltpu.SemaphoreType.DMA((1,))
+    part, present, y_low, y_high, *y_blocks = call(
         guess_kernel,
-        [plane, (WELLS + 1,)] + [(FACE_PLANES,) + plane] * 2 + [(LAYER_BLOCKS,) + plane] * 2,
+        [first_chunks, (WELLS + 1,)]
+        + [(FACE_PLANES,) + plane] * 2
+        + [(LAYER_BLOCKS,) + plane] * 2,
         arguments,
-        [held(6, *block), held(6, WELLS, LANES)],
+        [held(6, *block), held(6, WELLS, LANES), held(*first_chunks), sent],
         cost=4 << 20,
-    )
-    (part,) = call(spread_kernel, [(devices, TABLE_ROWS, LANES)], (table, fxl))
-    parts = exchanged(part)
+        out=1,
+    )
+    parts = exchanged(after(part, fxl))
     y_low, y_high = call(
         corner_kernel,
         [(FACE_PLANES + CORNER_PLANES,) + plane] * 2,
@@ -758,25 +794,26 @@
     )
     gxl = from_behind(x_high, "gx", 1)
     gxh = from_behind(x_low, "gx", -1)
-    (table,) = call(
+    (part,) = call(
         moments_kernel,
-        [plane],
+        [chunks],
         (wells, ids, residual, image, present),
-        [held(16, *block), held(16, WELLS, LANES), held(3, *plane)],
+        [held(16, *block), held(16, WELLS, LANES), held(3, *plane), held(*chunks), sent],
         cost=4 << 20,
-    )
-    y_low, y_high, part = call(
+        out=1,
+    )
+    parts = exchanged(after(part, gxl, gxh))
+    y_low, y_high = call(
         image_corner_kernel,
-        [(IMAGE_PLANES + 2,) + plane] * 2 + [(devices, 8, LANES)],
-        (y_low, y_high, gxl, gxh, table),
-    )
-    parts = exchanged(part)
+        [(IMAGE_PLANES + 2,) + plane] * 2,
+        (y_low, y_high, gxl, gxh),
+    )
     gyl = from_behind(y_high, "gy", 1)
     gyh = from_behind(y_low, "gy", -1)
 
     second, third, part, known = call(
         krylov_kernel,
-        [field, field, (devices, 8, LANES), (4 * RHS, LANES)],
+        [field, field, (devices, 1, (RHS + 1) * LANES), (4 * RHS, LANES)],
         (couplings, diagonal, wells, ids) + faces + (gxl, gxh, gyl, gyh)
         + (residual, image, residual_faces, parts, small, present),
         [held(12, WELLS, LANES), held(12, *block), held(10, *plane)],

time: 70.4 us -> 69.3 us (0.984)
  Pallas kernels: 14.6 us -> 12.7 us
  local copies, waits for them, and re-layouts: 0.02 us -> 1.31 us
    pallas_call x9 -> x8, Pallas kernels: 14.6 us -> 12.7 us  [call(): pl.pallas_call(kernel, out_shape=outs, in_specs=[place(argument) for argu...]
    unnamed x12 -> x24, local copies, waits for them, and re-layouts: 0.02 us -> 1.31 us
where the time goes in v12:
time: 69.3 us; the launch traced here: 68.9 us
  starting transfers between devices  29.1 us (42%)
  blocking collectives  13.4 us (19%)
  Pallas kernels  12.7 us (18%)
  waiting for transfers between devices  12.1 us (17%)
  local copies, waits for them, and re-layouts  1.31 us (2%)
    ppermute x8, starting transfers between devices, from_behind(): lax.ppermute(value, axis, [(source, source + steps) for source in range(l...  17 us
    all_to_all x1, blocking collectives, exchanged(): return lax.all_to_all(part, ('gx', 'gy'), 0, 0, tiled=True)  13.4 us
    pallas_call x8, Pallas kernels, call(): pl.pallas_call(kernel, out_shape=outs, in_specs=[place(argument) for argu...  12.7 us
    all_to_all x2, starting transfers between devices, exchanged(): return lax.all_to_all(part, ('gx', 'gy'), 0, 0, tiled=True)  12.1 us
    ppermute x8, waiting for transfers between devices, from_behind(): lax.ppermute(value, axis, [(source, source + steps) for source in range(l...  8.84 us
    all_to_all x2, waiting for transfers between devices, exchanged(): return lax.all_to_all(part, ('gx', 'gy'), 0, 0, tiled=True)  3.28 us
  transfers between devices with their start and end apart: 10, of which 5 were waited for; matrix products, arithmetic and copies ran while one was open for 0% of the time, Pallas kernels for 8%

profile of v12, /device:TPU:0, one launch (start us, length us, event | category | flops | bytes accessed | tf_op | source)
XLA Modules:
  0.0 68.9 jit_solution(2915121525537651191)
XLA Ops:
  0.0 0.0 copy-start.2
  0.0 0.0 copy-start.1
  0.0 0.0 copy-start.6
  0.0 0.0 copy-start
  0.0 0.0 copy-start.5
  0.0 1.5 %shard_map.64 = (f32[37,8,128]{2,1,0:T(8,128)S(1)}, f32[37,8,128]{2,1,0:T(8,128)S(1)}) custom-call(f32[6,4,8,8,128]{4,3,2,1,0:T(8,128)} %couplings.5, f32[4,8,8,128]{3,2,1,0:T(8,128)} %diagonal.5, f32[4,8,8,128]{3,2,1,0:T(8,128)} %wells.7, s32[8,8,128]{2,1,0:T(8,128)} %ids.7, f32[4,2,8,8,128]{4,3,2,1,0:T(8,128)} %right.3, f32[4,2,8,8,128]{4,3,2,1,0:T(8,128)} %guess.5), custom_call_target="tpu_custom_call" | custom-call | tf_op jit(solution)/shard_map/pallas_call | solution.py:705
  1.5 5.0 %collective-permute-start = (f32[37,8,128]{2,1,0:T(8,128)S(1)}, f32[37,8,128]{2,1,0:T(8,128)S(1)}, u32[]{:S(2)}, u32[]{:S(2)}) collective-permute-start(f32[37,8,128]{2,1,0:T(8,128)S(1)} %get-tuple-element.29), channel_id=1, source_target_pairs={{0,8},{8,16},{16,24},{1,9},{9,17},{17,25},{2,10},{10,18},{18,26},{... | collective-permute-start | bytes 454664 | tf_op jit(solution)/shard_map/ppermute | solution.py:741
  6.5 1.3 %collective-permute-start.1 = (f32[37,8,128]{2,1,0:T(8,128)S(1)}, f32[37,8,128]{2,1,0:T(8,128)S(1)}, u32[]{:S(2)}, u32[]{:S(2)}) collective-permute-start(f32[37,8,128]{2,1,0:T(8,128)S(1)} %get-tuple-element.30), channel_id=1, source_target_pairs={{8,0},{16,8},{24,16},{9,1},{17,9},{25,17},{10,2},{18,10},{26,18},{... | collective-permute-start | bytes 454664 | tf_op jit(solution)/shard_map/ppermute | solution.py:741
  7.8 0.0 copy-done.7
  7.8 0.0 copy-done.2
  7.8 0.0 copy-done.1
  7.8 0.0 copy-done.6
  7.8 0.0 copy-done
  7.9 0.0 copy-done.5
  7.9 3.1 %shard_map.65 = (f32[32,6,128]{2,1,0:T(8,128)}, s32[41]{0:T(128)S(1)}, f32[36,8,128]{2,1,0:T(8,128)S(1)}, f32[36,8,128]{2,1,0:T(8,128)S(1)}, f32[24,8,128]{2,1,0:T(8,128)S(1)}, /*index=5*/f32[24,8,128]{2,1,0:T(8,128)S(1)}) custom-call(f32[6,4,8,8,128]{4,3,2,1,0:T(8,128)S(1)} %copy-done, f32[4,8,8,128]{3,2,1,0:T(8,128)S(1)} %copy-done.6, ...), custom_call_target="tpu_custom_call" | custom-call | flops 4194304 | bytes 4194304 | tf_op jit(solution)/shard_map/pallas_call | solution.py:705
  11.0 0.0 collective-permute-done.fxl.rest_0_
  11.0 0.0 copy-start.3
  11.0 0.7 copy-done.3
  11.6 0.0 copy-start.4
  11.6 5.8 %all-to-all-start = ((f32[32,6,128]{2,1,0:T(8,128)}), f32[32,6,128]{2,1,0:T(8,128)S(1)}, u32[]{:S(2)}, u32[]{:S(2)}) async-start(f32[32,6,128]{2,1,0:T(8,128)} %shard_map.67), calls=%async_computation | async-start | bytes 262144 | tf_op jit(solution)/shard_map/all_to_all | solution.py:745
  17.5 0.0 collective-permute-done.1.fxh
  17.5 0.0 copy-done.4
  17.5 2.2 %collective-permute-start.2 = (f32[41,8,128]{2,1,0:T(8,128)S(1)}, f32[41,8,128]{2,1,0:T(8,128)S(1)}, u32[]{:S(2)}, u32[]{:S(2)}) collective-permute-start(f32[41,8,128]{2,1,0:T(8,128)S(1)} %get-tuple-element.33), channel_id=1, source_target_pairs={{0,1},{1,2},{2,3},{3,4},{4,5},{5,6},{6,7},{8,9},{9,10},{10,11},{11... | collective-permute-start | bytes 503816 | tf_op jit(solution)/shard_map/ppermute | solution.py:741
  19.7 1.3 %collective-permute-start.3 = (f32[41,8,128]{2,1,0:T(8,128)S(1)}, f32[41,8,128]{2,1,0:T(8,128)S(1)}, u32[]{:S(2)}, u32[]{:S(2)}) collective-permute-start(f32[41,8,128]{2,1,0:T(8,128)S(1)} %get-tuple-element.34), channel_id=1, source_target_pairs={{1,0},{2,1},{3,2},{4,3},{5,4},{6,5},{7,6},{9,8},{10,9},{11,10},{12... | collective-permute-start | bytes 503816 | tf_op jit(solution)/shard_map/ppermute | solution.py:741
  21.0 0.0 collective-permute-done.2.fyl
  21.0 3.1 %collective-permute-done.3.fyh = f32[41,8,128]{2,1,0:T(8,128)S(1)} collective-permute-done((f32[41,8,128]{2,1,0:T(8,128)S(1)}, f32[41,8,128]{2,1,0:T(8,128)S(1)}, u32[]{:S(2)}, u32[]{:S(2)}) %collective-permute-start.3) | collective-permute-done | bytes 167968 | tf_op jit(solution)/shard_map/ppermute | solution.py:741
  24.1 1.6 %all-to-all-done.parts = f32[32,6,128]{2,1,0:T(8,128)S(1)} async-done(((f32[32,6,128]{2,1,0:T(8,128)}), f32[32,6,128]{2,1,0:T(8,128)S(1)}, u32[]{:S(2)}, u32[]{:S(2)}) %all-to-all-start) | async-done | bytes 98336 | tf_op jit(solution)/shard_map/all_to_all | solution.py:745
  25.7 1.1 %shard_map.68 = (f32[4,2,8,8,128]{4,3,2,1,0:T(8,128)S(1)}, f32[4,2,8,8,128]{4,3,2,1,0:T(8,128)S(1)}, f32[4,8,8,128]{3,2,1,0:T(8,128)S(1)}, f32[16,8,128]{2,1,0:T...) custom-call(f32[6,4,8,8,128]{4,3,2,1,0:T(8,128)S(1)} %copy-done, ...), custom_call_target="tpu_custom_call" | custom-call | tf_op jit(solution)/shard_map/pallas_call | solution.py:705
  26.8 2.6 %collective-permute-start.4 = (f32[16,8,128]{2,1,0:T(8,128)S(1)}, f32[16,8,128]{2,1,0:T(8,128)S(1)}, u32[]{:S(2)}, u32[]{:S(2)}) collective-permute-start(f32[16,8,128]{2,1,0:T(8,128)S(1)} %get-tuple-element.39), channel_id=1, source_target_pairs={{0,8},{8,16},{16,24},{1,9},{9,17},{17,25},{2,10},{10,18},{18,26},{... | collective-permute-start | bytes 196616 | tf_op jit(solution)/shard_map/ppermute | solution.py:741
  29.4 1.3 %collective-permute-start.5 = (f32[16,8,128]{2,1,0:T(8,128)S(1)}, f32[16,8,128]{2,1,0:T(8,128)S(1)}, u32[]{:S(2)}, u32[]{:S(2)}) collective-permute-start(f32[16,8,128]{2,1,0:T(8,128)S(1)} %get-tuple-element.40), channel_id=1, source_target_pairs={{8,0},{16,8},{24,16},{9,1},{17,9},{25,17},{10,2},{18,10},{26,18},{... | collective-permute-start | bytes 196616 | tf_op jit(solution)/shard_map/ppermute | solution.py:741
  30.7 2.1 %shard_map.70.value = f32[32,8,128]{2,1,0:T(8,128)} custom-call(f32[4,8,8,128]{3,2,1,0:T(8,128)S(1)} %copy-done.2, s32[8,8,128]{2,1,0:T(8,128)S(1)} %copy-done.7, f32[4,2,8,8,128]{4,3,2,1,0:T(8,128)S(1)} %get-tuple-element.38.residual, f32[4,2,8,8,128]{4,3,2,1,0:T(8,128)S(1)} %get-tuple-element.45.image, s32[41]{0:T(128)S(1)} %get-tuple-element.47.present), custom_call_target="tpu_custom_call" | custom-call | flops 4194304 | bytes 4194304 | tf_op jit(solution)/shard_map/pallas_call | solution.py:705
  32.8 0.0 collective-permute-done.4.gxl.rest_0_
  32.8 0.0 copy-start.8
  32.8 2.7 %collective-permute-done.5.gxh.rest_1_ = f32[16,8,128]{2,1,0:T(8,128)S(1)} collective-permute-done((f32[16,8,128]{2,1,0:T(8,128)S(1)}, f32[16,8,128]{2,1,0:T(8,128)S(1)}, u32[]{:S(2)}, u32[]{:S(2)}) %collective-permute-start.5) | collective-permute-done | bytes 65568 | tf_op jit(solution)/shard_map/ppermute | solution.py:741
  35.6 0.0 copy-done.8
  35.6 0.0 copy-start.10
  35.6 0.6 copy-done.10
  36.2 6.3 %all-to-all-start.1 = ((f32[32,8,128]{2,1,0:T(8,128)}), f32[32,8,128]{2,1,0:T(8,128)S(1)}, u32[]{:S(2)}, u32[]{:S(2)}) async-start(f32[32,8,128]{2,1,0:T(8,128)} %shard_map.71), calls=%async_computation.1 | async-start | bytes 262144 | tf_op jit(solution)/shard_map/all_to_all | solution.py:745
  42.5 0.0 copy-done.9
  42.5 0.0 copy-done.11
  42.6 2.2 %collective-permute-start.6 = (f32[18,8,128]{2,1,0:T(8,128)S(1)}, f32[18,8,128]{2,1,0:T(8,128)S(1)}, u32[]{:S(2)}, u32[]{:S(2)}) collective-permute-start(f32[18,8,128]{2,1,0:T(8,128)S(1)} %get-tuple-element.43), channel_id=1, source_target_pairs={{0,1},{1,2},{2,3},{3,4},{4,5},{5,6},{6,7},{8,9},{9,10},{10,11},{11... | collective-permute-start | bytes 221192 | tf_op jit(solution)/shard_map/ppermute | solution.py:741
  44.7 1.3 %collective-permute-start.7 = (f32[18,8,128]{2,1,0:T(8,128)S(1)}, f32[18,8,128]{2,1,0:T(8,128)S(1)}, u32[]{:S(2)}, u32[]{:S(2)}) collective-permute-start(f32[18,8,128]{2,1,0:T(8,128)S(1)} %get-tuple-element.44), channel_id=1, source_target_pairs={{1,0},{2,1},{3,2},{4,3},{5,4},{6,5},{7,6},{9,8},{10,9},{11,10},{12... | collective-permute-start | bytes 221192 | tf_op jit(solution)/shard_map/ppermute | solution.py:741
  46.0 0.0 collective-permute-done.6.gyl
  46.0 3.0 %collective-permute-done.7.gyh = f32[18,8,128]{2,1,0:T(8,128)S(1)} collective-permute-done((f32[18,8,128]{2,1,0:T(8,128)S(1)}, f32[18,8,128]{2,1,0:T(8,128)S(1)}, u32[]{:S(2)}, u32[]{:S(2)}) %collective-permute-start.7) | collective-permute-done | bytes 73760 | tf_op jit(solution)/shard_map/ppermute | solution.py:741
  49.0 1.7 %all-to-all-done.1.parts = f32[32,8,128]{2,1,0:T(8,128)S(1)} async-done(((f32[32,8,128]{2,1,0:T(8,128)}), f32[32,8,128]{2,1,0:T(8,128)S(1)}, u32[]{:S(2)}, u32[]{:S(2)}) %all-to-all-start.1) | async-done | bytes 131104 | tf_op jit(solution)/shard_map/all_to_all | solution.py:745
  50.7 3.0 %shard_map.72 = (f32[4,2,8,8,128]{4,3,2,1,0:T(8,128)S(1)}, f32[4,2,8,8,128]{4,3,2,1,0:T(8,128)S(1)}, f32[32,1,640]{2,1,0:T(1,128)S(1)}, f32[16,128]{1,0:T(8,128)S(1)}) custom-call(f32[6,4,8,8,128]{4,3,2,1,0:T(8,128)S(1)} %copy-done, f32[4,8,8,128]{3,2,1,0:T(8,128)S(1)} %copy-done.6, f32[4,8,8,128]{3,2,1,0:T(8,128)S(1)} %copy-done.2, ...), custom_call_target="tpu_custom_call" | custom-call | tf_op jit(solution)/shard_map/pallas_call | solution.py:705
  53.8 13.4 %all_to_all.15.parts = f32[32,1,640]{2,1,0:T(1,128)S(1)} all-to-all(f32[32,1,640]{2,1,0:T(1,128)S(1)} %get-tuple-element.51), channel_id=1, replica_groups=mesh['member'=1,'gx'=4,'gy'=8] {'gx','gy'}, dimensions={0} | all-to-all | bytes 163840 | tf_op jit(solution)/shard_map/all_to_all | solution.py:745
  67.2 1.7 %shard_map.73 = f32[4,2,8,8,128]{4,3,2,1,0:T(8,128)} custom-call(f32[4,2,8,8,128]{4,3,2,1,0:T(8,128)S(1)} %copy-done.1, f32[4,2,8,8,128]{4,3,2,1,0:T(8,128)S(1)} %get-tuple-element.38.residual, f32[4,2,8,8,128]{4,3,2,1,0:T(8,128)S(1)} %get-tuple-element.49.second, f32[4,2,8,8,128]{4,3,2,1,0:T(8,128)S(1)} %get-tuple-element.50.third, ...), custom_call_target="tpu_custom_call" | custom-call | tf_op jit(solution)/shard_map/pallas_call | solution.py:705
  (7 shorter events, 0.1 us)
Async XLA Ops:
  0.0 7.8 %copy-start.7 = (s32[8,8,128]{2,1,0:T(8,128)S(1)}, s32[8,8,128]{2,1,0:T(8,128)}, u32[]{:S(2)}) copy-start(s32[8,8,128]{2,1,0:T(8,128)} %ids.7) | copy-start | bytes 98308
  0.0 7.8 %copy-start.2 = (f32[4,8,8,128]{3,2,1,0:T(8,128)S(1)}, f32[4,8,8,128]{3,2,1,0:T(8,128)}, u32[]{:S(2)}) copy-start(f32[4,8,8,128]{3,2,1,0:T(8,128)} %wells.7) | copy-start | bytes 393220
  0.0 7.8 %copy-start.1 = (f32[4,2,8,8,128]{4,3,2,1,0:T(8,128)S(1)}, f32[4,2,8,8,128]{4,3,2,1,0:T(8,128)}, u32[]{:S(2)}) copy-start(f32[4,2,8,8,128]{4,3,2,1,0:T(8,128)} %guess.5) | copy-start | bytes 786436
  0.0 7.8 %copy-start.6 = (f32[4,8,8,128]{3,2,1,0:T(8,128)S(1)}, f32[4,8,8,128]{3,2,1,0:T(8,128)}, u32[]{:S(2)}) copy-start(f32[4,8,8,128]{3,2,1,0:T(8,128)} %diagonal.5) | copy-start | bytes 393220
  0.0 7.8 %copy-start = (f32[6,4,8,8,128]{4,3,2,1,0:T(8,128)S(1)}, f32[6,4,8,8,128]{4,3,2,1,0:T(8,128)}, u32[]{:S(2)}) copy-start(f32[6,4,8,8,128]{4,3,2,1,0:T(8,128)} %couplings.5) | copy-start | bytes 2359300
  0.0 7.8 %copy-start.5 = (f32[4,2,8,8,128]{4,3,2,1,0:T(8,128)S(1)}, f32[4,2,8,8,128]{4,3,2,1,0:T(8,128)}, u32[]{:S(2)}) copy-start(f32[4,2,8,8,128]{4,3,2,1,0:T(8,128)} %right.3) | copy-start | bytes 786436
  1.5 9.4 %collective-permute-start = (f32[37,8,128]{2,1,0:T(8,128)S(1)}, f32[37,8,128]{2,1,0:T(8,128)S(1)}, u32[]{:S(2)}, u32[]{:S(2)}) collective-permute-start(f32[37,8,128]{2,1,0:T(8,128)S(1)} %get-tuple-element.29), channel_id=1, source_target_pairs={{0,8},{8,16},{16,24},{1,9},{9,17},{17,25},{2,10},{10,18},{18,26},{... | collective-permute-start | bytes 454664 | tf_op jit(solution)/shard_map/ppermute | solution.py:741
  6.5 11.0 %collective-permute-start.1 = (f32[37,8,128]{2,1,0:T(8,128)S(1)}, f32[37,8,128]{2,1,0:T(8,128)S(1)}, u32[]{:S(2)}, u32[]{:S(2)}) collective-permute-start(f32[37,8,128]{2,1,0:T(8,128)S(1)} %get-tuple-element.30), channel_id=1, source_target_pairs={{8,0},{16,8},{24,16},{9,1},{17,9},{25,17},{10,2},{18,10},{26,18},{... | collective-permute-start | bytes 454664 | tf_op jit(solution)/shard_map/ppermute | solution.py:741
  11.0 0.7 copy-start.3
  11.6 5.8 %copy-start.4 = (f32[37,8,128]{2,1,0:T(8,128)S(1)}, f32[37,8,128]{2,1,0:T(8,128)}, u32[]{:S(2)}) copy-start(f32[37,8,128]{2,1,0:T(8,128)} %copy-done.3) | copy-start | bytes 454660
  11.6 14.0 %all-to-all-start = ((f32[32,6,128]{2,1,0:T(8,128)}), f32[32,6,128]{2,1,0:T(8,128)S(1)}, u32[]{:S(2)}, u32[]{:S(2)}) async-start(f32[32,6,128]{2,1,0:T(8,128)} %shard_map.67), calls=%async_computation | async-start | bytes 262144 | tf_op jit(solution)/shard_map/all_to_all | solution.py:745
  17.5 3.5 %collective-permute-start.2 = (f32[41,8,128]{2,1,0:T(8,128)S(1)}, f32[41,8,128]{2,1,0:T(8,128)S(1)}, u32[]{:S(2)}, u32[]{:S(2)}) collective-permute-start(f32[41,8,128]{2,1,0:T(8,128)S(1)} %get-tuple-element.33), channel_id=1, source_target_pairs={{0,1},{1,2},{2,3},{3,4},{4,5},{5,6},{6,7},{8,9},{9,10},{10,11},{11... | collective-permute-start | bytes 503816 | tf_op jit(solution)/shard_map/ppermute | solution.py:741
  19.7 4.4 %collective-permute-start.3 = (f32[41,8,128]{2,1,0:T(8,128)S(1)}, f32[41,8,128]{2,1,0:T(8,128)S(1)}, u32[]{:S(2)}, u32[]{:S(2)}) collective-permute-start(f32[41,8,128]{2,1,0:T(8,128)S(1)} %get-tuple-element.34), channel_id=1, source_target_pairs={{1,0},{2,1},{3,2},{4,3},{5,4},{6,5},{7,6},{9,8},{10,9},{11,10},{12... | collective-permute-start | bytes 503816 | tf_op jit(solution)/shard_map/ppermute | solution.py:741
  26.8 6.0 %collective-permute-start.4 = (f32[16,8,128]{2,1,0:T(8,128)S(1)}, f32[16,8,128]{2,1,0:T(8,128)S(1)}, u32[]{:S(2)}, u32[]{:S(2)}) collective-permute-start(f32[16,8,128]{2,1,0:T(8,128)S(1)} %get-tuple-element.39), channel_id=1, source_target_pairs={{0,8},{8,16},{16,24},{1,9},{9,17},{17,25},{2,10},{10,18},{18,26},{... | collective-permute-start | bytes 196616 | tf_op jit(solution)/shard_map/ppermute | solution.py:741
  29.4 6.2 %collective-permute-start.5 = (f32[16,8,128]{2,1,0:T(8,128)S(1)}, f32[16,8,128]{2,1,0:T(8,128)S(1)}, u32[]{:S(2)}, u32[]{:S(2)}) collective-permute-start(f32[16,8,128]{2,1,0:T(8,128)S(1)} %get-tuple-element.40), channel_id=1, source_target_pairs={{8,0},{16,8},{24,16},{9,1},{17,9},{25,17},{10,2},{18,10},{26,18},{... | collective-permute-start | bytes 196616 | tf_op jit(solution)/shard_map/ppermute | solution.py:741
  32.8 2.7 %copy-start.8 = (f32[16,8,128]{2,1,0:T(8,128)}, f32[16,8,128]{2,1,0:T(8,128)S(1)}, u32[]{:S(2)}) copy-start(f32[16,8,128]{2,1,0:T(8,128)S(1)} %collective-permute-done.4.gxl.rest_0_) | copy-start | bytes 196612
  35.6 0.6 copy-start.10
  36.2 6.3 %copy-start.9 = (f32[16,8,128]{2,1,0:T(8,128)S(1)}, f32[16,8,128]{2,1,0:T(8,128)}, u32[]{:S(2)}) copy-start(f32[16,8,128]{2,1,0:T(8,128)} %copy-done.8) | copy-start | bytes 196612
  36.2 6.3 %copy-start.11 = (f32[16,8,128]{2,1,0:T(8,128)S(1)}, f32[16,8,128]{2,1,0:T(8,128)}, u32[]{:S(2)}) copy-start(f32[16,8,128]{2,1,0:T(8,128)} %copy-done.10) | copy-start | bytes 196612
  36.2 14.6 %all-to-all-start.1 = ((f32[32,8,128]{2,1,0:T(8,128)}), f32[32,8,128]{2,1,0:T(8,128)S(1)}, u32[]{:S(2)}, u32[]{:S(2)}) async-start(f32[32,8,128]{2,1,0:T(8,128)} %shard_map.71), calls=%async_computation.1 | async-start | bytes 262144 | tf_op jit(solution)/shard_map/all_to_all | solution.py:745
  42.6 3.5 %collective-permute-start.6 = (f32[18,8,128]{2,1,0:T(8,128)S(1)}, f32[18,8,128]{2,1,0:T(8,128)S(1)}, u32[]{:S(2)}, u32[]{:S(2)}) collective-permute-start(f32[18,8,128]{2,1,0:T(8,128)S(1)} %get-tuple-element.43), channel_id=1, source_target_pairs={{0,1},{1,2},{2,3},{3,4},{4,5},{5,6},{6,7},{8,9},{9,10},{10,11},{11... | collective-permute-start | bytes 221192 | tf_op jit(solution)/shard_map/ppermute | solution.py:741
  44.7 4.3 %collective-permute-start.7 = (f32[18,8,128]{2,1,0:T(8,128)S(1)}, f32[18,8,128]{2,1,0:T(8,128)S(1)}, u32[]{:S(2)}, u32[]{:S(2)}) collective-permute-start(f32[18,8,128]{2,1,0:T(8,128)S(1)} %get-tuple-element.44), channel_id=1, source_target_pairs={{1,0},{2,1},{3,2},{4,3},{5,4},{6,5},{7,6},{9,8},{10,9},{11,10},{12... | collective-permute-start | bytes 221192 | tf_op jit(solution)/shard_map/ppermute | solution.py:741

commit v13 on v12

--- a/solution.py
+++ b/solution.py
@@ -335,7 +335,8 @@
 
 
 def send_out(table, chunks, part, sent):
-    chunks[...] = jnp.broadcast_to(table[None, : chunks.shape[1]], chunks.shape)
+    rows = min(chunks.shape[1], table.shape[0])
+    chunks[:, :rows, :] = jnp.broadcast_to(table[None, :rows], (chunks.shape[0], rows, LANES))
     copy = pltpu.make_async_copy(chunks, part, sent.at[0])
     copy.start()
     return copy
@@ -357,14 +358,12 @@
                 row += 1
 
 
-def image_corner_kernel(y_low, y_high, gxl, gxh, low_out, high_out):
-    last = gxl.shape[1] - 1
-    for own, out, at in ((y_low, low_out, 0), (y_high, high_out, last)):
-        for n in range(IMAGE_PLANES):
-            out[n] = own[n]
-        for x_end, face in enumerate((gxl, gxh)):
-            for n in range(8):
-                out[IMAGE_PLANES + x_end, n : n + 1, :] = face[n, at : at + 1, :]
+def diagonal_device(x_end, y_end):
+    across, along = lax.axis_index("gx"), lax.axis_index("gy")
+    there_x, there_y = across + 2 * x_end - 1, along + 2 * y_end - 1
+    count_x, count_y = lax.axis_size("gx"), lax.axis_size("gy")
+    exists = (there_x >= 0) & (there_x < count_x) & (there_y >= 0) & (there_y < count_y)
+    return exists, jnp.where(exists, there_x * count_y + there_y, 0)
 
 
 def guess_kernel(
@@ -488,6 +487,21 @@
         dots[2, row, :] = tile_sum(result, result)
     rows = segment_rows(ids, values, scratch, present)
     table = place_rows(rows, jnp.zeros((8, LANES), jnp.float32))
+    chunks[:, 8:, :] = jnp.zeros_like(chunks[:, 8:, :])
+    last = image.shape[2] - 1
+    for x_end in range(2):
+        for y_end in range(2):
+            exists, place = diagonal_device(x_end, y_end)
+
+            @pl.when(exists)
+            def _():
+                for k in range(RHS):
+                    for a in range(2):
+                        row, y = 8 + 2 * k + a, last * y_end
+                        chunks[pl.ds(place, 1), row : row + 1, :] = image[
+                            k, a, last * x_end, y : y + 1, :
+                        ][None]
+
     send_out(place_columns(dots, WELLS, table), chunks, part, sent).wait()
 
 
@@ -514,7 +528,7 @@
     second_out, third_out, part, known, scratch, values_scratch, dots,
 ):
     faces, sent = (fxl, fxh, fyl, fyh), (gxl, gxh, gyl, gyh)
-    totals = jnp.sum(parts[...], axis=0)
+    totals = jnp.sum(parts[:, 0:8, :], axis=0)
     small = small_in[...]
     s_rows, s_images, p_rows, p_seconds, scalars = first_step(totals, small)
     known[0:RHS, :] = p_rows
@@ -526,7 +540,7 @@
     known[3 * RHS :, :] = jnp.broadcast_to(small[1:2, :], (RHS, LANES))
     dots[...] = jnp.zeros_like(dots)
     corners = corners_of(faces, FACE_PLANES, CORNER_ROWS)
-    sent_corners = corners_of(sent, IMAGE_PLANES, 8)
+    places = [diagonal_device(c % 2, c // 2)[1] for c in range(4)]
     all_ids = ids[...]
     face_ids = [as_ids(face[WELL_ID]) for face in faces]
     back_ids = [as_ids(face[BACK_ID]) for face in faces]
@@ -550,7 +564,7 @@
             here = spread(s_row, corner_ids[c])[0:1, :]
             corner_now.append(
                 [
-                    sent_corners[c].row(2 * k + a) + corners[c].row(SIDE_EQ + a) * here
+                    parts[pl.ds(places[c], 1), 8 + 2 * k + a, :] + corners[c].row(SIDE_EQ + a) * here
                     for a in range(2)
                 ]
             )
@@ -721,11 +735,11 @@
 
 def after(value, *others):
     far = pl.BlockSpec(memory_space=pltpu.HBM)
-    anywhere = pl.BlockSpec(memory_space=pl.ANY)
+    near = pl.BlockSpec(memory_space=pltpu.VMEM)
     return pl.pallas_call(
         nothing,
         out_shape=pltpu.HBM(value.shape, value.dtype),
-        in_specs=[far] + [anywhere] * len(others),
+        in_specs=[far] + [near] * len(others),
         out_specs=far,
         input_output_aliases={0: 0},
     )(pltpu.with_memory_space_constraint(value, pltpu.HBM), *others)
@@ -765,7 +779,7 @@
     )
     fxl = from_behind(x_high, "gx", 1)
     fxh = from_behind(x_low, "gx", -1)
-    first_chunks, chunks = (devices, TABLE_ROWS, LANES), (devices, 8, LANES)
+    first_chunks, chunks = (devices, TABLE_ROWS, LANES), (devices, 16, LANES)
     sent = pltpu.SemaphoreType.DMA((1,))
     part, present, y_low, y_high, *y_blocks = call(
         guess_kernel,
@@ -802,12 +816,7 @@
         cost=4 << 20,
         out=1,
     )
-    parts = exchanged(after(part, gxl, gxh))
-    y_low, y_high = call(
-        image_corner_kernel,
-        [(IMAGE_PLANES + 2,) + plane] * 2,
-        (y_low, y_high, gxl, gxh),
-    )
+    parts = exchanged(part)
     gyl = from_behind(y_high, "gy", 1)
     gyh = from_behind(y_low, "gy", -1)
 

time: 69.3 us -> 70.1 us (1.012)
  waiting for transfers between devices: 12.1 us -> 7.73 us
  blocking collectives: 13.4 us -> 16.5 us
  starting transfers between devices: 29.1 us -> 31.5 us
    all_to_all x1, blocking collectives: 13.4 us -> 16.5 us  [exchanged(): return lax.all_to_all(part, ('gx', 'gy'), 0, 0, tiled=True)]
    ppermute x8, waiting for transfers between devices: 8.84 us -> 6.17 us  [from_behind(): lax.ppermute(value, axis, [(source, source + steps) for source in range(l...]
    all_to_all x2, waiting for transfers between devices: 3.28 us -> 1.56 us  [exchanged(): return lax.all_to_all(part, ('gx', 'gy'), 0, 0, tiled=True)]
    all_to_all x2, starting transfers between devices: 12.1 us -> 13.7 us  [exchanged(): return lax.all_to_all(part, ('gx', 'gy'), 0, 0, tiled=True)]
    pallas_call x2 -> x1, Pallas kernels: 0.01 us -> 0.91 us  [after(): pl.pallas_call(nothing, out_shape=pltpu.HBM(value.shape, value.dtype), in...]
    ppermute x8, starting transfers between devices: 17 us -> 17.7 us  [from_behind(): lax.ppermute(value, axis, [(source, source + steps) for source in range(l...]
    pallas_call x8 -> x7, Pallas kernels: 12.7 us -> 12 us  [call(): pl.pallas_call(kernel, out_shape=outs, in_specs=[place(argument) for argu...]
  transfers between devices with their start and end apart: 10 -> 10, of which waited for: 5 -> 4; matrix products, arithmetic and copies ran while one was open for 0% -> 0% of each run, Pallas kernels for 8% -> 5%
where the time goes in v13:
time: 70.1 us; the launch traced here: 69.6 us
  starting transfers between devices  31.5 us (45%)
  blocking collectives  16.5 us (24%)
  Pallas kernels  13 us (19%)
  waiting for transfers between devices  7.73 us (11%)
    ppermute x8, starting transfers between devices, from_behind(): lax.ppermute(value, axis, [(source, source + steps) for source in range(l...  17.7 us
    all_to_all x1, blocking collectives, exchanged(): return lax.all_to_all(part, ('gx', 'gy'), 0, 0, tiled=True)  16.5 us
    all_to_all x2, starting transfers between devices, exchanged(): return lax.all_to_all(part, ('gx', 'gy'), 0, 0, tiled=True)  13.7 us
    pallas_call x7, Pallas kernels, call(): pl.pallas_call(kernel, out_shape=outs, in_specs=[place(argument) for argu...  12 us
    ppermute x8, waiting for transfers between devices, from_behind(): lax.ppermute(value, axis, [(source, source + steps) for source in range(l...  6.17 us
    all_to_all x2, waiting for transfers between devices, exchanged(): return lax.all_to_all(part, ('gx', 'gy'), 0, 0, tiled=True)  1.56 us
  transfers between devices with their start and end apart: 10, of which 4 were waited for; matrix products, arithmetic and copies ran while one was open for 0% of the time, Pallas kernels for 5%

profile of v13, /device:TPU:0, one launch (start us, length us, event | category | flops | bytes accessed | tf_op | source)
XLA Modules:
  0.0 69.6 jit_solution(17415105564389701871)
XLA Ops:
  0.0 0.0 copy-start.7
  0.0 0.0 copy-start.2
  0.0 0.0 copy-start.1
  0.0 0.0 copy-start.6
  0.0 0.0 copy-start
  0.0 0.0 copy-start.5
  0.0 1.5 %shard_map.64 = (f32[37,8,128]{2,1,0:T(8,128)S(1)}, f32[37,8,128]{2,1,0:T(8,128)S(1)}) custom-call(f32[6,4,8,8,128]{4,3,2,1,0:T(8,128)} %couplings.5, f32[4,8,8,128]{3,2,1,0:T(8,128)} %diagonal.5, f32[4,8,8,128]{3,2,1,0:T(8,128)} %wells.7, s32[8,8,128]{2,1,0:T(8,128)} %ids.7, f32[4,2,8,8,128]{4,3,2,1,0:T(8,128)} %right.3, f32[4,2,8,8,128]{4,3,2,1,0:T(8,128)} %guess.5), custom_call_target="tpu_custom_call" | custom-call | tf_op jit(solution)/shard_map/pallas_call | solution.py:719
  1.5 5.0 %collective-permute-start = (f32[37,8,128]{2,1,0:T(8,128)S(1)}, f32[37,8,128]{2,1,0:T(8,128)S(1)}, u32[]{:S(2)}, u32[]{:S(2)}) collective-permute-start(f32[37,8,128]{2,1,0:T(8,128)S(1)} %get-tuple-element.27), channel_id=1, source_target_pairs={{0,8},{8,16},{16,24},{1,9},{9,17},{17,25},{2,10},{10,18},{18,26},{... | collective-permute-start | bytes 454664 | tf_op jit(solution)/shard_map/ppermute | solution.py:755
  6.5 1.3 %collective-permute-start.1 = (f32[37,8,128]{2,1,0:T(8,128)S(1)}, f32[37,8,128]{2,1,0:T(8,128)S(1)}, u32[]{:S(2)}, u32[]{:S(2)}) collective-permute-start(f32[37,8,128]{2,1,0:T(8,128)S(1)} %get-tuple-element.28), channel_id=1, source_target_pairs={{8,0},{16,8},{24,16},{9,1},{17,9},{25,17},{10,2},{18,10},{26,18},{... | collective-permute-start | bytes 454664 | tf_op jit(solution)/shard_map/ppermute | solution.py:755
  7.8 0.0 copy-done.7
  7.8 0.0 copy-done.2
  7.8 0.0 copy-done.1
  7.8 0.0 copy-done.6
  7.8 0.0 copy-done
  7.9 0.0 copy-done.5
  7.9 2.3 %shard_map.65 = (f32[32,6,128]{2,1,0:T(8,128)}, s32[41]{0:T(128)S(1)}, f32[36,8,128]{2,1,0:T(8,128)S(1)}, f32[36,8,128]{2,1,0:T(8,128)S(1)}, f32[24,8,128]{2,1,0:T(8,128)S(1)}, /*index=5*/f32[24,8,128]{2,1,0:T(8,128)S(1)}) custom-call(f32[6,4,8,8,128]{4,3,2,1,0:T(8,128)S(1)} %copy-done, f32[4,8,8,128]{3,2,1,0:T(8,128)S(1)} %copy-done.6, ...), custom_call_target="tpu_custom_call" | custom-call | flops 4194304 | bytes 4194304 | tf_op jit(solution)/shard_map/pallas_call | solution.py:719
  10.2 0.0 collective-permute-done.fxl.rest_0_
  10.2 0.0 copy-start.3
  10.2 0.7 copy-done.3
  10.9 0.9 %shard_map.67 = f32[32,6,128]{2,1,0:T(8,128)} custom-call(f32[32,6,128]{2,1,0:T(8,128)} %get-tuple-element.33.value, f32[37,8,128]{2,1,0:T(8,128)} %copy-done.3), custom_call_target="tpu_custom_call", output_to_operand_aliasing={{}: (0, {})} | custom-call | tf_op jit(solution)/shard_map/pallas_call | solution.py:739
  11.8 0.0 copy-start.4
  11.8 6.4 %all-to-all-start = ((f32[32,6,128]{2,1,0:T(8,128)}), f32[32,6,128]{2,1,0:T(8,128)S(1)}, u32[]{:S(2)}, u32[]{:S(2)}) async-start(f32[32,6,128]{2,1,0:T(8,128)} %shard_map.67), calls=%async_computation | async-start | bytes 262144 | tf_op jit(solution)/shard_map/all_to_all | solution.py:759
  18.2 0.0 collective-permute-done.1.fxh
  18.2 0.0 copy-done.4
  18.3 2.2 %collective-permute-start.2 = (f32[41,8,128]{2,1,0:T(8,128)S(1)}, f32[41,8,128]{2,1,0:T(8,128)S(1)}, u32[]{:S(2)}, u32[]{:S(2)}) collective-permute-start(f32[41,8,128]{2,1,0:T(8,128)S(1)} %get-tuple-element.31), channel_id=1, source_target_pairs={{0,1},{1,2},{2,3},{3,4},{4,5},{5,6},{6,7},{8,9},{9,10},{10,11},{11... | collective-permute-start | bytes 503816 | tf_op jit(solution)/shard_map/ppermute | solution.py:755
  20.5 1.3 %collective-permute-start.3 = (f32[41,8,128]{2,1,0:T(8,128)S(1)}, f32[41,8,128]{2,1,0:T(8,128)S(1)}, u32[]{:S(2)}, u32[]{:S(2)}) collective-permute-start(f32[41,8,128]{2,1,0:T(8,128)S(1)} %get-tuple-element.32), channel_id=1, source_target_pairs={{1,0},{2,1},{3,2},{4,3},{5,4},{6,5},{7,6},{9,8},{10,9},{11,10},{12... | collective-permute-start | bytes 503816 | tf_op jit(solution)/shard_map/ppermute | solution.py:755
  21.8 0.0 collective-permute-done.2.fyl
  21.8 3.1 %collective-permute-done.3.fyh = f32[41,8,128]{2,1,0:T(8,128)S(1)} collective-permute-done((f32[41,8,128]{2,1,0:T(8,128)S(1)}, f32[41,8,128]{2,1,0:T(8,128)S(1)}, u32[]{:S(2)}, u32[]{:S(2)}) %collective-permute-start.3) | collective-permute-done | bytes 167968 | tf_op jit(solution)/shard_map/ppermute | solution.py:755
  24.9 1.6 %all-to-all-done.parts = f32[32,6,128]{2,1,0:T(8,128)S(1)} async-done(((f32[32,6,128]{2,1,0:T(8,128)}), f32[32,6,128]{2,1,0:T(8,128)S(1)}, u32[]{:S(2)}, u32[]{:S(2)}) %all-to-all-start) | async-done | bytes 98336 | tf_op jit(solution)/shard_map/all_to_all | solution.py:759
  26.5 1.7 %shard_map.68 = (f32[4,2,8,8,128]{4,3,2,1,0:T(8,128)S(1)}, f32[4,2,8,8,128]{4,3,2,1,0:T(8,128)S(1)}, f32[4,8,8,128]{3,2,1,0:T(8,128)S(1)}, f32[16,8,128]{2,1,0:T...) custom-call(f32[6,4,8,8,128]{4,3,2,1,0:T(8,128)S(1)} %copy-done, ...), custom_call_target="tpu_custom_call" | custom-call | tf_op jit(solution)/shard_map/pallas_call | solution.py:719
  28.2 1.9 %shard_map.69 = f32[32,16,128]{2,1,0:T(8,128)} custom-call(f32[4,8,8,128]{3,2,1,0:T(8,128)S(1)} %copy-done.2, s32[8,8,128]{2,1,0:T(8,128)S(1)} %copy-done.7, f32[4,2,8,8,128]{4,3,2,1,0:T(8,128)S(1)} %get-tuple-element.36.residual, f32[4,2,8,8,128]{4,3,2,1,0:T(8,128)S(1)} %get-tuple-element.41.image, s32[41]{0:T(128)S(1)} %get-tuple-element.43.present), custom_call_target="tpu_custom_call" | custom-call | flops 4194304 | bytes 4194304 | tf_op jit(solution)/shard_map/pallas_call | solution.py:719
  30.1 7.3 %all-to-all-start.1 = ((f32[32,16,128]{2,1,0:T(8,128)}), f32[32,16,128]{2,1,0:T(8,128)S(1)}, u32[]{:S(2)}, u32[]{:S(2)}) async-start(f32[32,16,128]{2,1,0:T(8,128)} %shard_map.69), calls=%async_computation.1 | async-start | bytes 524288 | tf_op jit(solution)/shard_map/all_to_all | solution.py:759
  37.4 3.7 %collective-permute-start.4 = (f32[16,8,128]{2,1,0:T(8,128)}, f32[16,8,128]{2,1,0:T(8,128)S(1)}, u32[]{:S(2)}, u32[]{:S(2)}) collective-permute-start(f32[16,8,128]{2,1,0:T(8,128)} %get-tuple-element.37), channel_id=1, source_target_pairs={{0,8},{8,16},{16,24},{1,9},{9,17},{17,25},{2,10},{10,18},{18,26},{... | collective-permute-start | bytes 196616 | tf_op jit(solution)/shard_map/ppermute | solution.py:755
  41.1 1.3 %collective-permute-start.5 = (f32[16,8,128]{2,1,0:T(8,128)S(1)}, f32[16,8,128]{2,1,0:T(8,128)S(1)}, u32[]{:S(2)}, u32[]{:S(2)}) collective-permute-start(f32[16,8,128]{2,1,0:T(8,128)S(1)} %get-tuple-element.38), channel_id=1, source_target_pairs={{8,0},{16,8},{24,16},{9,1},{17,9},{25,17},{10,2},{18,10},{26,18},{... | collective-permute-start | bytes 196616 | tf_op jit(solution)/shard_map/ppermute | solution.py:755
  42.4 1.8 %collective-permute-start.6 = (f32[16,8,128]{2,1,0:T(8,128)S(1)}, f32[16,8,128]{2,1,0:T(8,128)S(1)}, u32[]{:S(2)}, u32[]{:S(2)}) collective-permute-start(f32[16,8,128]{2,1,0:T(8,128)S(1)} %get-tuple-element.39), channel_id=1, source_target_pairs={{0,1},{1,2},{2,3},{3,4},{4,5},{5,6},{6,7},{8,9},{9,10},{10,11},{11... | collective-permute-start | bytes 196616 | tf_op jit(solution)/shard_map/ppermute | solution.py:755
  44.2 1.3 %collective-permute-start.7 = (f32[16,8,128]{2,1,0:T(8,128)S(1)}, f32[16,8,128]{2,1,0:T(8,128)S(1)}, u32[]{:S(2)}, u32[]{:S(2)}) collective-permute-start(f32[16,8,128]{2,1,0:T(8,128)S(1)} %get-tuple-element.40), channel_id=1, source_target_pairs={{1,0},{2,1},{3,2},{4,3},{5,4},{6,5},{7,6},{9,8},{10,9},{11,10},{12... | collective-permute-start | bytes 196616 | tf_op jit(solution)/shard_map/ppermute | solution.py:755
  45.5 0.0 collective-permute-done.4.gxl
  45.5 2.0 %collective-permute-done.5.gxh = f32[16,8,128]{2,1,0:T(8,128)S(1)} collective-permute-done((f32[16,8,128]{2,1,0:T(8,128)S(1)}, f32[16,8,128]{2,1,0:T(8,128)S(1)}, u32[]{:S(2)}, u32[]{:S(2)}) %collective-permute-start.5) | collective-permute-done | bytes 65568 | tf_op jit(solution)/shard_map/ppermute | solution.py:755
  47.5 0.0 collective-permute-done.6.gyl
  47.5 1.0 %collective-permute-done.7.gyh = f32[16,8,128]{2,1,0:T(8,128)S(1)} collective-permute-done((f32[16,8,128]{2,1,0:T(8,128)S(1)}, f32[16,8,128]{2,1,0:T(8,128)S(1)}, u32[]{:S(2)}, u32[]{:S(2)}) %collective-permute-start.7) | collective-permute-done | bytes 65568 | tf_op jit(solution)/shard_map/ppermute | solution.py:755
  48.5 0.0 all-to-all-done.1.parts
  48.5 2.8 %shard_map.70 = (f32[4,2,8,8,128]{4,3,2,1,0:T(8,128)S(1)}, f32[4,2,8,8,128]{4,3,2,1,0:T(8,128)S(1)}, f32[32,1,640]{2,1,0:T(1,128)S(1)}, f32[16,128]{1,0:T(8,128)S(1)}) custom-call(f32[6,4,8,8,128]{4,3,2,1,0:T(8,128)S(1)} %copy-done, f32[4,8,8,128]{3,2,1,0:T(8,128)S(1)} %copy-done.6, f32[4,8,8,128]{3,2,1,0:T(8,128)S(1)} %copy-done.2, ...), custom_call_target="tpu_custom_call" | custom-call | tf_op jit(solution)/shard_map/pallas_call | solution.py:719
  51.4 16.5 %all_to_all.15.parts = f32[32,1,640]{2,1,0:T(1,128)S(1)} all-to-all(f32[32,1,640]{2,1,0:T(1,128)S(1)} %get-tuple-element.47), channel_id=1, replica_groups=mesh['member'=1,'gx'=4,'gy'=8] {'gx','gy'}, dimensions={0} | all-to-all | bytes 163840 | tf_op jit(solution)/shard_map/all_to_all | solution.py:759
  67.9 1.7 %shard_map.71 = f32[4,2,8,8,128]{4,3,2,1,0:T(8,128)} custom-call(f32[4,2,8,8,128]{4,3,2,1,0:T(8,128)S(1)} %copy-done.1, f32[4,2,8,8,128]{4,3,2,1,0:T(8,128)S(1)} %get-tuple-element.36.residual, f32[4,2,8,8,128]{4,3,2,1,0:T(8,128)S(1)} %get-tuple-element.45.second, f32[4,2,8,8,128]{4,3,2,1,0:T(8,128)S(1)} %get-tuple-element.46.third, ...), custom_call_target="tpu_custom_call" | custom-call | tf_op jit(solution)/shard_map/pallas_call | solution.py:719
  (1 shorter events, 0.0 us)
Async XLA Ops:
  0.0 7.8 %copy-start.7 = (s32[8,8,128]{2,1,0:T(8,128)S(1)}, s32[8,8,128]{2,1,0:T(8,128)}, u32[]{:S(2)}) copy-start(s32[8,8,128]{2,1,0:T(8,128)} %ids.7) | copy-start | bytes 98308
  0.0 7.8 %copy-start.2 = (f32[4,8,8,128]{3,2,1,0:T(8,128)S(1)}, f32[4,8,8,128]{3,2,1,0:T(8,128)}, u32[]{:S(2)}) copy-start(f32[4,8,8,128]{3,2,1,0:T(8,128)} %wells.7) | copy-start | bytes 393220
  0.0 7.8 %copy-start.1 = (f32[4,2,8,8,128]{4,3,2,1,0:T(8,128)S(1)}, f32[4,2,8,8,128]{4,3,2,1,0:T(8,128)}, u32[]{:S(2)}) copy-start(f32[4,2,8,8,128]{4,3,2,1,0:T(8,128)} %guess.5) | copy-start | bytes 786436
  0.0 7.8 %copy-start.6 = (f32[4,8,8,128]{3,2,1,0:T(8,128)S(1)}, f32[4,8,8,128]{3,2,1,0:T(8,128)}, u32[]{:S(2)}) copy-start(f32[4,8,8,128]{3,2,1,0:T(8,128)} %diagonal.5) | copy-start | bytes 393220
  0.0 7.8 %copy-start = (f32[6,4,8,8,128]{4,3,2,1,0:T(8,128)S(1)}, f32[6,4,8,8,128]{4,3,2,1,0:T(8,128)}, u32[]{:S(2)}) copy-start(f32[6,4,8,8,128]{4,3,2,1,0:T(8,128)} %couplings.5) | copy-start | bytes 2359300
  0.0 7.8 %copy-start.5 = (f32[4,2,8,8,128]{4,3,2,1,0:T(8,128)S(1)}, f32[4,2,8,8,128]{4,3,2,1,0:T(8,128)}, u32[]{:S(2)}) copy-start(f32[4,2,8,8,128]{4,3,2,1,0:T(8,128)} %right.3) | copy-start | bytes 786436
  1.5 8.6 %collective-permute-start = (f32[37,8,128]{2,1,0:T(8,128)S(1)}, f32[37,8,128]{2,1,0:T(8,128)S(1)}, u32[]{:S(2)}, u32[]{:S(2)}) collective-permute-start(f32[37,8,128]{2,1,0:T(8,128)S(1)} %get-tuple-element.27), channel_id=1, source_target_pairs={{0,8},{8,16},{16,24},{1,9},{9,17},{17,25},{2,10},{10,18},{18,26},{... | collective-permute-start | bytes 454664 | tf_op jit(solution)/shard_map/ppermute | solution.py:755
  6.5 11.7 %collective-permute-start.1 = (f32[37,8,128]{2,1,0:T(8,128)S(1)}, f32[37,8,128]{2,1,0:T(8,128)S(1)}, u32[]{:S(2)}, u32[]{:S(2)}) collective-permute-start(f32[37,8,128]{2,1,0:T(8,128)S(1)} %get-tuple-element.28), channel_id=1, source_target_pairs={{8,0},{16,8},{24,16},{9,1},{17,9},{25,17},{10,2},{18,10},{26,18},{... | collective-permute-start | bytes 454664 | tf_op jit(solution)/shard_map/ppermute | solution.py:755
  10.2 0.7 copy-start.3
  11.8 6.5 %copy-start.4 = (f32[37,8,128]{2,1,0:T(8,128)S(1)}, f32[37,8,128]{2,1,0:T(8,128)}, u32[]{:S(2)}) copy-start(f32[37,8,128]{2,1,0:T(8,128)} %copy-done.3) | copy-start | bytes 454660
  11.8 14.7 %all-to-all-start = ((f32[32,6,128]{2,1,0:T(8,128)}), f32[32,6,128]{2,1,0:T(8,128)S(1)}, u32[]{:S(2)}, u32[]{:S(2)}) async-start(f32[32,6,128]{2,1,0:T(8,128)} %shard_map.67), calls=%async_computation | async-start | bytes 262144 | tf_op jit(solution)/shard_map/all_to_all | solution.py:759
  18.3 3.5 %collective-permute-start.2 = (f32[41,8,128]{2,1,0:T(8,128)S(1)}, f32[41,8,128]{2,1,0:T(8,128)S(1)}, u32[]{:S(2)}, u32[]{:S(2)}) collective-permute-start(f32[41,8,128]{2,1,0:T(8,128)S(1)} %get-tuple-element.31), channel_id=1, source_target_pairs={{0,1},{1,2},{2,3},{3,4},{4,5},{5,6},{6,7},{8,9},{9,10},{10,11},{11... | collective-permute-start | bytes 503816 | tf_op jit(solution)/shard_map/ppermute | solution.py:755
  20.5 4.4 %collective-permute-start.3 = (f32[41,8,128]{2,1,0:T(8,128)S(1)}, f32[41,8,128]{2,1,0:T(8,128)S(1)}, u32[]{:S(2)}, u32[]{:S(2)}) collective-permute-start(f32[41,8,128]{2,1,0:T(8,128)S(1)} %get-tuple-element.32), channel_id=1, source_target_pairs={{1,0},{2,1},{3,2},{4,3},{5,4},{6,5},{7,6},{9,8},{10,9},{11,10},{12... | collective-permute-start | bytes 503816 | tf_op jit(solution)/shard_map/ppermute | solution.py:755
  30.1 18.4 %all-to-all-start.1 = ((f32[32,16,128]{2,1,0:T(8,128)}), f32[32,16,128]{2,1,0:T(8,128)S(1)}, u32[]{:S(2)}, u32[]{:S(2)}) async-start(f32[32,16,128]{2,1,0:T(8,128)} %shard_map.69), calls=%async_computation.1 | async-start | bytes 524288 | tf_op jit(solution)/shard_map/all_to_all | solution.py:759
  37.4 8.1 %collective-permute-start.4 = (f32[16,8,128]{2,1,0:T(8,128)}, f32[16,8,128]{2,1,0:T(8,128)S(1)}, u32[]{:S(2)}, u32[]{:S(2)}) collective-permute-start(f32[16,8,128]{2,1,0:T(8,128)} %get-tuple-element.37), channel_id=1, source_target_pairs={{0,8},{8,16},{16,24},{1,9},{9,17},{17,25},{2,10},{10,18},{18,26},{... | collective-permute-start | bytes 196616 | tf_op jit(solution)/shard_map/ppermute | solution.py:755
  41.1 6.4 %collective-permute-start.5 = (f32[16,8,128]{2,1,0:T(8,128)S(1)}, f32[16,8,128]{2,1,0:T(8,128)S(1)}, u32[]{:S(2)}, u32[]{:S(2)}) collective-permute-start(f32[16,8,128]{2,1,0:T(8,128)S(1)} %get-tuple-element.38), channel_id=1, source_target_pairs={{8,0},{16,8},{24,16},{9,1},{17,9},{25,17},{10,2},{18,10},{26,18},{... | collective-permute-start | bytes 196616 | tf_op jit(solution)/shard_map/ppermute | solution.py:755
  42.4 5.1 %collective-permute-start.6 = (f32[16,8,128]{2,1,0:T(8,128)S(1)}, f32[16,8,128]{2,1,0:T(8,128)S(1)}, u32[]{:S(2)}, u32[]{:S(2)}) collective-permute-start(f32[16,8,128]{2,1,0:T(8,128)S(1)} %get-tuple-element.39), channel_id=1, source_target_pairs={{0,1},{1,2},{2,3},{3,4},{4,5},{5,6},{6,7},{8,9},{9,10},{10,11},{11... | collective-permute-start | bytes 196616 | tf_op jit(solution)/shard_map/ppermute | solution.py:755
  44.2 4.4 %collective-permute-start.7 = (f32[16,8,128]{2,1,0:T(8,128)S(1)}, f32[16,8,128]{2,1,0:T(8,128)S(1)}, u32[]{:S(2)}, u32[]{:S(2)}) collective-permute-start(f32[16,8,128]{2,1,0:T(8,128)S(1)} %get-tuple-element.40), channel_id=1, source_target_pairs={{1,0},{2,1},{3,2},{4,3},{5,4},{6,5},{7,6},{9,8},{10,9},{11,10},{12... | collective-permute-start | bytes 196616 | tf_op jit(solution)/shard_map/ppermute | solution.py:755

commit v14 on v12

--- a/solution.py
+++ b/solution.py
@@ -321,17 +321,13 @@
         )
 
 
-def y_packs(arguments, packs, all_blocks):
-    last = arguments[-1].shape[-2] - 1
-    for end in range(2):
-
-        def cut(n, index, layer):
-            return arguments[n][index + (slice(None), last - layer if end else layer, slice(None))]
-
-        fill_pack(packs[end], 3 - end, 0, cut)
-        blocks = layer_blocks(cut, 3 - end, 0)
-        for n in range(LAYER_BLOCKS):
-            all_blocks[end][n] = blocks(n)
+def y_cut(arguments, end):
+    last = arguments[0].shape[-2] - 1
+
+    def cut(n, index, layer):
+        return arguments[n][index + (slice(None), last - layer if end else layer, slice(None))]
+
+    return cut
 
 
 def send_out(table, chunks, part, sent):
@@ -369,8 +365,7 @@
 
 def guess_kernel(
     couplings, diagonal, wells, ids, right, guess,
-    part, present, y_low, y_high, low_blocks, high_blocks,
-    values, scratch, chunks, sent,
+    part, present, y_low, y_high, values, scratch, chunks, sent,
 ):
     list_wells(ids, present)
     for k in range(RHS):
@@ -380,15 +375,33 @@
     rows = segment_rows(ids, values, scratch, present)
     table = pack_rows(rows, jnp.zeros((8, LANES), jnp.float32))
     copy = send_out(table, chunks, part, sent)
-    y_packs(
-        (couplings, diagonal, wells, ids, right, guess), (y_low, y_high), (low_blocks, high_blocks)
-    )
+    arguments = (couplings, diagonal, wells, ids, right, guess)
+    for end, pack in enumerate((y_low, y_high)):
+        fill_pack(pack, 3 - end, 0, y_cut(arguments, end))
     copy.wait()
 
 
+def block_kernel(
+    couplings, diagonal, right, guess, sent_face, rest, leaving, low_blocks, high_blocks
+):
+    nothing_enters = [[jnp.zeros(guess.shape[3:], jnp.float32)] * 2] * 4
+    for k in range(RHS):
+        inside, outgoing = block_stencil(
+            couplings, diagonal, guess[k, 0], guess[k, 1], nothing_enters
+        )
+        for a in range(2):
+            rest[k, a] = right[k, a] - inside[a]
+            for f in range(4):
+                leaving[f, 2 * k + a] = outgoing[f][a]
+    for end, kept in enumerate((low_blocks, high_blocks)):
+        blocks = layer_blocks(y_cut((couplings, diagonal), end), 3 - end, 0)
+        for n in range(LAYER_BLOCKS):
+            kept[n] = blocks(n)
+
+
 def residual_kernel(
-    couplings, diagonal, wells, ids, right, guess, fxl, fxh, fyl, fyh, parts,
-    low_blocks, high_blocks,
+    couplings, diagonal, wells, ids, fxl, fxh, fyl, fyh, parts,
+    rest, leaving, low_blocks, high_blocks,
     residual, image, residual_faces, x_low, x_high, y_low, y_high, small,
 ):
     faces = (fxl, fxh, fyl, fyh)
@@ -396,11 +409,11 @@
     corners = corners_of(faces, FACE_PLANES, CORNER_ROWS)
     all_ids = ids[...]
     face_ids = [as_ids(face[WELL_ID]) for face in faces]
-    last = guess.shape[2] - 1
+    last = rest.shape[2] - 1
+    row = iota(rest.shape[2:], 1)
     for k in range(RHS):
         s_row = unpack_row(totals, k)
-        first, second = guess[k, 0], guess[k, 1]
-        incoming = [
+        entering = [
             product(
                 lambda e, f=f: faces[f][e],
                 faces[f][GUESS + 2 * k],
@@ -408,11 +421,19 @@
             )
             for f in range(4)
         ]
-        applied, outgoing = block_stencil(couplings, diagonal, first, second, incoming)
+        outgoing = [[leaving[f, 2 * k + b] for b in range(2)] for f in range(4)]
         at_wells = spread(s_row, all_ids)
-        now = [
-            right[k, a] - applied[a] - wells[2 + a] * at_wells for a in range(2)
-        ]
+        now = []
+        for a in range(2):
+            value = rest[k, a] - wells[2 + a] * at_wells
+            over_x = [
+                (value[0] - entering[0][a])[None],
+                value[1:last],
+                (value[last] - entering[1][a])[None],
+            ]
+            value = jnp.concatenate(over_x, axis=0)
+            value = value - jnp.where(row == 0, entering[2][a][:, None, :], 0.0)
+            now.append(value - jnp.where(row == last, entering[3][a][:, None, :], 0.0))
         for a in range(2):
             residual[k, a] = now[a]
         ends = corner_inputs(
@@ -721,13 +742,14 @@
 
 def after(value, *others):
     far = pl.BlockSpec(memory_space=pltpu.HBM)
-    anywhere = pl.BlockSpec(memory_space=pl.ANY)
+    near = pl.BlockSpec(memory_space=pltpu.VMEM)
     return pl.pallas_call(
         nothing,
         out_shape=pltpu.HBM(value.shape, value.dtype),
-        in_specs=[far] + [anywhere] * len(others),
+        in_specs=[far] + [near] * len(others),
         out_specs=far,
         input_output_aliases={0: 0},
+        compiler_params=pltpu.CompilerParams(vmem_limit_bytes=1 << 20),
     )(pltpu.with_memory_space_constraint(value, pltpu.HBM), *others)
 
 
@@ -767,11 +789,9 @@
     fxh = from_behind(x_low, "gx", -1)
     first_chunks, chunks = (devices, TABLE_ROWS, LANES), (devices, 8, LANES)
     sent = pltpu.SemaphoreType.DMA((1,))
-    part, present, y_low, y_high, *y_blocks = call(
+    part, present, y_low, y_high = call(
         guess_kernel,
-        [first_chunks, (WELLS + 1,)]
-        + [(FACE_PLANES,) + plane] * 2
-        + [(LAYER_BLOCKS,) + plane] * 2,
+        [first_chunks, (WELLS + 1,)] + [(FACE_PLANES,) + plane] * 2,
         arguments,
         [held(6, *block), held(6, WELLS, LANES), held(*first_chunks), sent],
         cost=4 << 20,
@@ -786,11 +806,18 @@
     fyl = from_behind(y_high, "gy", 1)
     fyh = from_behind(y_low, "gy", -1)
 
+    ahead = call(
+        block_kernel,
+        [field, (4, 8) + plane] + [(LAYER_BLOCKS,) + plane] * 2,
+        (couplings, diagonal, right, guess, y_low),
+        cost=4 << 20,
+    )
+
     faces = (fxl, fxh, fyl, fyh)
     residual, image, residual_faces, x_low, x_high, y_low, y_high, small = call(
         residual_kernel,
         [field, field, (4, 8) + plane] + [(IMAGE_PLANES,) + plane] * 4 + [(8, LANES)],
-        arguments + faces + (parts, *y_blocks),
+        (couplings, diagonal, wells, ids) + faces + (parts, *ahead),
     )
     gxl = from_behind(x_high, "gx", 1)
     gxh = from_behind(x_low, "gx", -1)

time: 69.3 us -> 68.1 us (0.983)
  local copies, waits for them, and re-layouts: 1.31 us -> 0.02 us
  Pallas kernels: 12.7 us -> 13.5 us
    unnamed x24 -> x12, local copies, waits for them, and re-layouts: 1.31 us -> 0.02 us
    pallas_call x8 -> x9, Pallas kernels: 12.7 us -> 13.5 us  [call(): pl.pallas_call(kernel, out_shape=outs, in_specs=[place(argument) for argu...]
  transfers between devices with their start and end apart: 10 -> 10, of which waited for: 5 -> 5; matrix products, arithmetic and copies ran while one was open for 0% -> 0% of each run, Pallas kernels for 8% -> 9%
where the time goes in v14:
time: 68.1 us; the launch traced here: 67.7 us
  starting transfers between devices  28.8 us (42%)
  Pallas kernels  13.5 us (20%)
  blocking collectives  13.4 us (20%)
  waiting for transfers between devices  11.7 us (17%)
    ppermute x8, starting transfers between devices, from_behind(): lax.ppermute(value, axis, [(source, source + steps) for source in range(l...  17 us
    pallas_call x9, Pallas kernels, call(): pl.pallas_call(kernel, out_shape=outs, in_specs=[place(argument) for argu...  13.5 us
    all_to_all x1, blocking collectives, exchanged(): return lax.all_to_all(part, ('gx', 'gy'), 0, 0, tiled=True)  13.4 us
    all_to_all x2, starting transfers between devices, exchanged(): return lax.all_to_all(part, ('gx', 'gy'), 0, 0, tiled=True)  11.8 us
    ppermute x8, waiting for transfers between devices, from_behind(): lax.ppermute(value, axis, [(source, source + steps) for source in range(l...  8.34 us
    all_to_all x2, waiting for transfers between devices, exchanged(): return lax.all_to_all(part, ('gx', 'gy'), 0, 0, tiled=True)  3.31 us
  transfers between devices with their start and end apart: 10, of which 5 were waited for; matrix products, arithmetic and copies ran while one was open for 0% of the time, Pallas kernels for 9%

profile of v14, /device:TPU:0, one launch (start us, length us, event | category | flops | bytes accessed | tf_op | source)
XLA Modules:
  0.0 67.7 jit_solution(7233713360159444818)
XLA Ops:
  0.0 0.0 copy-start.5
  0.0 0.0 copy-start.3
  0.0 0.0 copy-start.2
  0.0 0.0 copy-start
  0.0 0.0 copy-start.1
  0.0 0.0 copy-start.4
  0.0 1.5 %shard_map.64 = (f32[37,8,128]{2,1,0:T(8,128)S(1)}, f32[37,8,128]{2,1,0:T(8,128)S(1)}) custom-call(f32[6,4,8,8,128]{4,3,2,1,0:T(8,128)} %couplings.7, f32[4,8,8,128]{3,2,1,0:T(8,128)} %diagonal.7, f32[4,8,8,128]{3,2,1,0:T(8,128)} %wells.7, s32[8,8,128]{2,1,0:T(8,128)} %ids.7, f32[4,2,8,8,128]{4,3,2,1,0:T(8,128)} %right.3, f32[4,2,8,8,128]{4,3,2,1,0:T(8,128)} %guess.5), custom_call_target="tpu_custom_call" | custom-call | tf_op jit(solution)/shard_map/pallas_call | solution.py:726
  1.5 5.0 %collective-permute-start = (f32[37,8,128]{2,1,0:T(8,128)S(1)}, f32[37,8,128]{2,1,0:T(8,128)S(1)}, u32[]{:S(2)}, u32[]{:S(2)}) collective-permute-start(f32[37,8,128]{2,1,0:T(8,128)S(1)} %get-tuple-element.31), channel_id=1, source_target_pairs={{0,8},{8,16},{16,24},{1,9},{9,17},{17,25},{2,10},{10,18},{18,26},{... | collective-permute-start | bytes 454664 | tf_op jit(solution)/shard_map/ppermute | solution.py:763
  6.5 1.3 %collective-permute-start.1 = (f32[37,8,128]{2,1,0:T(8,128)S(1)}, f32[37,8,128]{2,1,0:T(8,128)S(1)}, u32[]{:S(2)}, u32[]{:S(2)}) collective-permute-start(f32[37,8,128]{2,1,0:T(8,128)S(1)} %get-tuple-element.32), channel_id=1, source_target_pairs={{8,0},{16,8},{24,16},{9,1},{17,9},{25,17},{10,2},{18,10},{26,18},{... | collective-permute-start | bytes 454664 | tf_op jit(solution)/shard_map/ppermute | solution.py:763
  7.8 0.0 copy-done.5
  7.8 0.0 copy-done.3
  7.8 0.0 copy-done.2
  7.8 0.0 copy-done
  7.8 0.0 copy-done.1
  7.9 0.0 copy-done.4
  7.9 3.6 %shard_map.65 = (f32[32,6,128]{2,1,0:T(8,128)}, s32[41]{0:T(128)S(1)}, f32[36,8,128]{2,1,0:T(8,128)S(1)}, f32[36,8,128]{2,1,0:T(8,128)S(1)}) custom-call(f32[6,4,8,8,128]{4,3,2,1,0:T(8,128)S(1)} %copy-done, f32[4,8,8,128]{3,2,1,0:T(8,128)S(1)} %copy-done.2, f32[4,8,8,128]{3,2,1,0:T(8,128)S(1)} %copy-done.3, s32[8,8,128]{2,1,0:T(8,128)S(1)} %copy-done.5, ...), custom_call_target="tpu_custom_call" | custom-call | flops 4194304 | bytes 4194304 | tf_op jit(solution)/shard_map/pallas_call | solution.py:726
  11.5 0.0 collective-permute-done.fxl.rest_0_
  11.5 5.5 %all-to-all-start = ((f32[32,6,128]{2,1,0:T(8,128)}), f32[32,6,128]{2,1,0:T(8,128)S(1)}, u32[]{:S(2)}, u32[]{:S(2)}) async-start(f32[32,6,128]{2,1,0:T(8,128)} %shard_map.67), calls=%async_computation | async-start | bytes 262144 | tf_op jit(solution)/shard_map/all_to_all | solution.py:767
  17.0 0.0 collective-permute-done.1.fxh
  17.1 2.2 %collective-permute-start.2 = (f32[41,8,128]{2,1,0:T(8,128)S(1)}, f32[41,8,128]{2,1,0:T(8,128)S(1)}, u32[]{:S(2)}, u32[]{:S(2)}) collective-permute-start(f32[41,8,128]{2,1,0:T(8,128)S(1)} %get-tuple-element.35), channel_id=1, source_target_pairs={{0,1},{1,2},{2,3},{3,4},{4,5},{5,6},{6,7},{8,9},{9,10},{10,11},{11... | collective-permute-start | bytes 503816 | tf_op jit(solution)/shard_map/ppermute | solution.py:763
  19.3 1.3 %collective-permute-start.3 = (f32[41,8,128]{2,1,0:T(8,128)S(1)}, f32[41,8,128]{2,1,0:T(8,128)S(1)}, u32[]{:S(2)}, u32[]{:S(2)}) collective-permute-start(f32[41,8,128]{2,1,0:T(8,128)S(1)} %get-tuple-element.36.sent_face), channel_id=1, source_target_pairs={{1,0},{2,1},{3,2},{4,3},{5,4},{6,5},{7,6},{9,8},{10,9},{11,10},{12... | collective-permute-start | bytes 503816 | tf_op jit(solution)/shard_map/ppermute | solution.py:763
  20.6 0.4 shard_map.68
  21.0 0.0 collective-permute-done.2.fyl
  21.0 2.7 %collective-permute-done.3.fyh = f32[41,8,128]{2,1,0:T(8,128)S(1)} collective-permute-done((f32[41,8,128]{2,1,0:T(8,128)S(1)}, f32[41,8,128]{2,1,0:T(8,128)S(1)}, u32[]{:S(2)}, u32[]{:S(2)}) %collective-permute-start.3) | collective-permute-done | bytes 167968 | tf_op jit(solution)/shard_map/ppermute | solution.py:763
  23.7 1.6 %all-to-all-done.parts = f32[32,6,128]{2,1,0:T(8,128)S(1)} async-done(((f32[32,6,128]{2,1,0:T(8,128)}), f32[32,6,128]{2,1,0:T(8,128)S(1)}, u32[]{:S(2)}, u32[]{:S(2)}) %all-to-all-start) | async-done | bytes 98336 | tf_op jit(solution)/shard_map/all_to_all | solution.py:767
  25.3 0.8 %shard_map.69 = (f32[4,2,8,8,128]{4,3,2,1,0:T(8,128)S(1)}, f32[4,2,8,8,128]{4,3,2,1,0:T(8,128)S(1)}, f32[4,8,8,128]{3,2,1,0:T(8,128)S(1)}, f32[16,8,128]{2,1,0:T...) custom-call(f32[6,4,8,8,128]{4,3,2,1,0:T(8,128)S(1)} %copy-done, ...), custom_call_target="tpu_custom_call" | custom-call | tf_op jit(solution)/shard_map/pallas_call | solution.py:726
  26.1 2.6 %collective-permute-start.4 = (f32[16,8,128]{2,1,0:T(8,128)S(1)}, f32[16,8,128]{2,1,0:T(8,128)S(1)}, u32[]{:S(2)}, u32[]{:S(2)}) collective-permute-start(f32[16,8,128]{2,1,0:T(8,128)S(1)} %get-tuple-element.43), channel_id=1, source_target_pairs={{0,8},{8,16},{16,24},{1,9},{9,17},{17,25},{2,10},{10,18},{18,26},{... | collective-permute-start | bytes 196616 | tf_op jit(solution)/shard_map/ppermute | solution.py:763
  28.7 1.3 %collective-permute-start.5 = (f32[16,8,128]{2,1,0:T(8,128)S(1)}, f32[16,8,128]{2,1,0:T(8,128)S(1)}, u32[]{:S(2)}, u32[]{:S(2)}) collective-permute-start(f32[16,8,128]{2,1,0:T(8,128)S(1)} %get-tuple-element.44), channel_id=1, source_target_pairs={{8,0},{16,8},{24,16},{9,1},{17,9},{25,17},{10,2},{18,10},{26,18},{... | collective-permute-start | bytes 196616 | tf_op jit(solution)/shard_map/ppermute | solution.py:763
  30.0 2.2 %shard_map.71.value = f32[32,8,128]{2,1,0:T(8,128)} custom-call(f32[4,8,8,128]{3,2,1,0:T(8,128)S(1)} %copy-done.3, s32[8,8,128]{2,1,0:T(8,128)S(1)} %copy-done.5, f32[4,2,8,8,128]{4,3,2,1,0:T(8,128)S(1)} %get-tuple-element.42.residual, f32[4,2,8,8,128]{4,3,2,1,0:T(8,128)S(1)} %get-tuple-element.49.image, s32[41]{0:T(128)S(1)} %get-tuple-element.51.present), custom_call_target="tpu_custom_call" | custom-call | flops 4194304 | bytes 4194304 | tf_op jit(solution)/shard_map/pallas_call | solution.py:726
  32.1 0.0 collective-permute-done.4.gxl.rest_0_
  32.2 2.7 %collective-permute-done.5.gxh.rest_1_ = f32[16,8,128]{2,1,0:T(8,128)S(1)} collective-permute-done((f32[16,8,128]{2,1,0:T(8,128)S(1)}, f32[16,8,128]{2,1,0:T(8,128)S(1)}, u32[]{:S(2)}, u32[]{:S(2)}) %collective-permute-start.5) | collective-permute-done | bytes 65568 | tf_op jit(solution)/shard_map/ppermute | solution.py:763
  34.8 6.3 %all-to-all-start.1 = ((f32[32,8,128]{2,1,0:T(8,128)}), f32[32,8,128]{2,1,0:T(8,128)S(1)}, u32[]{:S(2)}, u32[]{:S(2)}) async-start(f32[32,8,128]{2,1,0:T(8,128)} %shard_map.72), calls=%async_computation.1 | async-start | bytes 262144 | tf_op jit(solution)/shard_map/all_to_all | solution.py:767
  41.2 2.2 %collective-permute-start.6 = (f32[18,8,128]{2,1,0:T(8,128)S(1)}, f32[18,8,128]{2,1,0:T(8,128)S(1)}, u32[]{:S(2)}, u32[]{:S(2)}) collective-permute-start(f32[18,8,128]{2,1,0:T(8,128)S(1)} %get-tuple-element.47), channel_id=1, source_target_pairs={{0,1},{1,2},{2,3},{3,4},{4,5},{5,6},{6,7},{8,9},{9,10},{10,11},{11... | collective-permute-start | bytes 221192 | tf_op jit(solution)/shard_map/ppermute | solution.py:763
  43.4 1.3 %collective-permute-start.7 = (f32[18,8,128]{2,1,0:T(8,128)S(1)}, f32[18,8,128]{2,1,0:T(8,128)S(1)}, u32[]{:S(2)}, u32[]{:S(2)}) collective-permute-start(f32[18,8,128]{2,1,0:T(8,128)S(1)} %get-tuple-element.48), channel_id=1, source_target_pairs={{1,0},{2,1},{3,2},{4,3},{5,4},{6,5},{7,6},{9,8},{10,9},{11,10},{12... | collective-permute-start | bytes 221192 | tf_op jit(solution)/shard_map/ppermute | solution.py:763
  44.7 0.0 collective-permute-done.6.gyl
  44.7 3.0 %collective-permute-done.7.gyh = f32[18,8,128]{2,1,0:T(8,128)S(1)} collective-permute-done((f32[18,8,128]{2,1,0:T(8,128)S(1)}, f32[18,8,128]{2,1,0:T(8,128)S(1)}, u32[]{:S(2)}, u32[]{:S(2)}) %collective-permute-start.7) | collective-permute-done | bytes 73760 | tf_op jit(solution)/shard_map/ppermute | solution.py:763
  47.7 1.7 %all-to-all-done.1.parts = f32[32,8,128]{2,1,0:T(8,128)S(1)} async-done(((f32[32,8,128]{2,1,0:T(8,128)}), f32[32,8,128]{2,1,0:T(8,128)S(1)}, u32[]{:S(2)}, u32[]{:S(2)}) %all-to-all-start.1) | async-done | bytes 131104 | tf_op jit(solution)/shard_map/all_to_all | solution.py:767
  49.4 3.1 %shard_map.73 = (f32[4,2,8,8,128]{4,3,2,1,0:T(8,128)S(1)}, f32[4,2,8,8,128]{4,3,2,1,0:T(8,128)S(1)}, f32[32,1,640]{2,1,0:T(1,128)S(1)}, f32[16,128]{1,0:T(8,128)S(1)}) custom-call(f32[6,4,8,8,128]{4,3,2,1,0:T(8,128)S(1)} %copy-done, f32[4,8,8,128]{3,2,1,0:T(8,128)S(1)} %copy-done.2, f32[4,8,8,128]{3,2,1,0:T(8,128)S(1)} %copy-done.3, ...), custom_call_target="tpu_custom_call" | custom-call | tf_op jit(solution)/shard_map/pallas_call | solution.py:726
  52.5 13.4 %all_to_all.15.parts = f32[32,1,640]{2,1,0:T(1,128)S(1)} all-to-all(f32[32,1,640]{2,1,0:T(1,128)S(1)} %get-tuple-element.55), channel_id=1, replica_groups=mesh['member'=1,'gx'=4,'gy'=8] {'gx','gy'}, dimensions={0} | all-to-all | bytes 163840 | tf_op jit(solution)/shard_map/all_to_all | solution.py:767
  66.0 1.7 %shard_map.74 = f32[4,2,8,8,128]{4,3,2,1,0:T(8,128)} custom-call(f32[4,2,8,8,128]{4,3,2,1,0:T(8,128)S(1)} %copy-done.1, f32[4,2,8,8,128]{4,3,2,1,0:T(8,128)S(1)} %get-tuple-element.42.residual, f32[4,2,8,8,128]{4,3,2,1,0:T(8,128)S(1)} %get-tuple-element.53.second, f32[4,2,8,8,128]{4,3,2,1,0:T(8,128)S(1)} %get-tuple-element.54.third, ...), custom_call_target="tpu_custom_call" | custom-call | tf_op jit(solution)/shard_map/pallas_call | solution.py:726
  (4 shorter events, 0.1 us)
Async XLA Ops:
  0.0 7.8 %copy-start.5 = (s32[8,8,128]{2,1,0:T(8,128)S(1)}, s32[8,8,128]{2,1,0:T(8,128)}, u32[]{:S(2)}) copy-start(s32[8,8,128]{2,1,0:T(8,128)} %ids.7) | copy-start | bytes 98308
  0.0 7.8 %copy-start.3 = (f32[4,8,8,128]{3,2,1,0:T(8,128)S(1)}, f32[4,8,8,128]{3,2,1,0:T(8,128)}, u32[]{:S(2)}) copy-start(f32[4,8,8,128]{3,2,1,0:T(8,128)} %wells.7) | copy-start | bytes 393220
  0.0 7.8 %copy-start.2 = (f32[4,8,8,128]{3,2,1,0:T(8,128)S(1)}, f32[4,8,8,128]{3,2,1,0:T(8,128)}, u32[]{:S(2)}) copy-start(f32[4,8,8,128]{3,2,1,0:T(8,128)} %diagonal.7) | copy-start | bytes 393220
  0.0 7.8 %copy-start = (f32[6,4,8,8,128]{4,3,2,1,0:T(8,128)S(1)}, f32[6,4,8,8,128]{4,3,2,1,0:T(8,128)}, u32[]{:S(2)}) copy-start(f32[6,4,8,8,128]{4,3,2,1,0:T(8,128)} %couplings.7) | copy-start | bytes 2359300
  0.0 7.8 %copy-start.1 = (f32[4,2,8,8,128]{4,3,2,1,0:T(8,128)S(1)}, f32[4,2,8,8,128]{4,3,2,1,0:T(8,128)}, u32[]{:S(2)}) copy-start(f32[4,2,8,8,128]{4,3,2,1,0:T(8,128)} %guess.5) | copy-start | bytes 786436
  0.0 7.8 %copy-start.4 = (f32[4,2,8,8,128]{4,3,2,1,0:T(8,128)S(1)}, f32[4,2,8,8,128]{4,3,2,1,0:T(8,128)}, u32[]{:S(2)}) copy-start(f32[4,2,8,8,128]{4,3,2,1,0:T(8,128)} %right.3) | copy-start | bytes 786436
  1.5 10.0 %collective-permute-start = (f32[37,8,128]{2,1,0:T(8,128)S(1)}, f32[37,8,128]{2,1,0:T(8,128)S(1)}, u32[]{:S(2)}, u32[]{:S(2)}) collective-permute-start(f32[37,8,128]{2,1,0:T(8,128)S(1)} %get-tuple-element.31), channel_id=1, source_target_pairs={{0,8},{8,16},{16,24},{1,9},{9,17},{17,25},{2,10},{10,18},{18,26},{... | collective-permute-start | bytes 454664 | tf_op jit(solution)/shard_map/ppermute | solution.py:763
  6.5 10.5 %collective-permute-start.1 = (f32[37,8,128]{2,1,0:T(8,128)S(1)}, f32[37,8,128]{2,1,0:T(8,128)S(1)}, u32[]{:S(2)}, u32[]{:S(2)}) collective-permute-start(f32[37,8,128]{2,1,0:T(8,128)S(1)} %get-tuple-element.32), channel_id=1, source_target_pairs={{8,0},{16,8},{24,16},{9,1},{17,9},{25,17},{10,2},{18,10},{26,18},{... | collective-permute-start | bytes 454664 | tf_op jit(solution)/shard_map/ppermute | solution.py:763
  11.5 13.7 %all-to-all-start = ((f32[32,6,128]{2,1,0:T(8,128)}), f32[32,6,128]{2,1,0:T(8,128)S(1)}, u32[]{:S(2)}, u32[]{:S(2)}) async-start(f32[32,6,128]{2,1,0:T(8,128)} %shard_map.67), calls=%async_computation | async-start | bytes 262144 | tf_op jit(solution)/shard_map/all_to_all | solution.py:767
  17.1 3.9 %collective-permute-start.2 = (f32[41,8,128]{2,1,0:T(8,128)S(1)}, f32[41,8,128]{2,1,0:T(8,128)S(1)}, u32[]{:S(2)}, u32[]{:S(2)}) collective-permute-start(f32[41,8,128]{2,1,0:T(8,128)S(1)} %get-tuple-element.35), channel_id=1, source_target_pairs={{0,1},{1,2},{2,3},{3,4},{4,5},{5,6},{6,7},{8,9},{9,10},{10,11},{11... | collective-permute-start | bytes 503816 | tf_op jit(solution)/shard_map/ppermute | solution.py:763
  19.3 4.4 %collective-permute-start.3 = (f32[41,8,128]{2,1,0:T(8,128)S(1)}, f32[41,8,128]{2,1,0:T(8,128)S(1)}, u32[]{:S(2)}, u32[]{:S(2)}) collective-permute-start(f32[41,8,128]{2,1,0:T(8,128)S(1)} %get-tuple-element.36.sent_face), channel_id=1, source_target_pairs={{1,0},{2,1},{3,2},{4,3},{5,4},{6,5},{7,6},{9,8},{10,9},{11,10},{12... | collective-permute-start | bytes 503816 | tf_op jit(solution)/shard_map/ppermute | solution.py:763
  26.1 6.0 %collective-permute-start.4 = (f32[16,8,128]{2,1,0:T(8,128)S(1)}, f32[16,8,128]{2,1,0:T(8,128)S(1)}, u32[]{:S(2)}, u32[]{:S(2)}) collective-permute-start(f32[16,8,128]{2,1,0:T(8,128)S(1)} %get-tuple-element.43), channel_id=1, source_target_pairs={{0,8},{8,16},{16,24},{1,9},{9,17},{17,25},{2,10},{10,18},{18,26},{... | collective-permute-start | bytes 196616 | tf_op jit(solution)/shard_map/ppermute | solution.py:763
  28.7 6.2 %collective-permute-start.5 = (f32[16,8,128]{2,1,0:T(8,128)S(1)}, f32[16,8,128]{2,1,0:T(8,128)S(1)}, u32[]{:S(2)}, u32[]{:S(2)}) collective-permute-start(f32[16,8,128]{2,1,0:T(8,128)S(1)} %get-tuple-element.44), channel_id=1, source_target_pairs={{8,0},{16,8},{24,16},{9,1},{17,9},{25,17},{10,2},{18,10},{26,18},{... | collective-permute-start | bytes 196616 | tf_op jit(solution)/shard_map/ppermute | solution.py:763
  34.8 14.5 %all-to-all-start.1 = ((f32[32,8,128]{2,1,0:T(8,128)}), f32[32,8,128]{2,1,0:T(8,128)S(1)}, u32[]{:S(2)}, u32[]{:S(2)}) async-start(f32[32,8,128]{2,1,0:T(8,128)} %shard_map.72), calls=%async_computation.1 | async-start | bytes 262144 | tf_op jit(solution)/shard_map/all_to_all | solution.py:767
  41.2 3.5 %collective-permute-start.6 = (f32[18,8,128]{2,1,0:T(8,128)S(1)}, f32[18,8,128]{2,1,0:T(8,128)S(1)}, u32[]{:S(2)}, u32[]{:S(2)}) collective-permute-start(f32[18,8,128]{2,1,0:T(8,128)S(1)} %get-tuple-element.47), channel_id=1, source_target_pairs={{0,1},{1,2},{2,3},{3,4},{4,5},{5,6},{6,7},{8,9},{9,10},{10,11},{11... | collective-permute-start | bytes 221192 | tf_op jit(solution)/shard_map/ppermute | solution.py:763
  43.4 4.3 %collective-permute-start.7 = (f32[18,8,128]{2,1,0:T(8,128)S(1)}, f32[18,8,128]{2,1,0:T(8,128)S(1)}, u32[]{:S(2)}, u32[]{:S(2)}) collective-permute-start(f32[18,8,128]{2,1,0:T(8,128)S(1)} %get-tuple-element.48), channel_id=1, source_target_pairs={{1,0},{2,1},{3,2},{4,3},{5,4},{6,5},{7,6},{9,8},{10,9},{11,10},{12... | collective-permute-start | bytes 221192 | tf_op jit(solution)/shard_map/ppermute | solution.py:763

commit v15 on v14

--- a/solution.py
+++ b/solution.py
@@ -146,26 +146,44 @@
 
 
 def list_wells(ids, present):
-    depth = ids.shape[0]
-
-    def smallest(planes):
-        least = planes[0]
-        for plane in planes[1:]:
-            least = jnp.minimum(least, plane)
-        return jnp.min(least)
-
-    planes = [ids[x].astype(jnp.float32) for x in range(depth)]
-
-    def one_well(state):
-        number, well = state
-        present[number] = well.astype(jnp.int32)
-        after = [jnp.where(plane > well, plane, float(WELLS)) for plane in planes]
-        return number + 1, smallest(after)
-
-    number, _ = lax.while_loop(
-        lambda state: state[1] < WELLS, one_well, (jnp.int32(1), smallest(planes))
-    )
-    present[0] = number - 1
+    planes = [ids[x].astype(jnp.float32) for x in range(ids.shape[0])]
+    middle = WELLS // 2
+    halves = ((0.0, float(middle)), (float(middle), float(WELLS)))
+
+    def least(above, top):
+        found = [jnp.where((p > above) & (p < top), p, top) for p in planes]
+        value = found[0]
+        for other in found[1:]:
+            value = jnp.minimum(value, other)
+        return jnp.min(value)
+
+    def greatest(base, below):
+        found = [jnp.where((p >= base) & (p < below), p, base - 1.0) for p in planes]
+        value = found[0]
+        for other in found[1:]:
+            value = jnp.maximum(value, other)
+        return jnp.max(value)
+
+    def some_left(state):
+        return (state[1] <= state[2]) | (state[3] <= state[4])
+
+    def step(state):
+        number, ends = state[0], state[1:]
+        after = []
+        for half, (base, top) in enumerate(halves):
+            low, high = ends[2 * half], ends[2 * half + 1]
+            present[number] = low.astype(jnp.int32)
+            number = number + jnp.where(low <= high, 1, 0)
+            present[number] = high.astype(jnp.int32)
+            number = number + jnp.where(low < high, 1, 0)
+            after += [least(low, top), greatest(base, high)]
+        return (number, *after)
+
+    ends = []
+    for base, top in halves:
+        ends += [least(base - 1.0, top), greatest(base, top)]
+    state = lax.while_loop(some_left, step, (jnp.int32(1), *ends))
+    present[0] = state[0] - 1
 
 
 def segment_rows(ids, values, scratch, present):
@@ -240,6 +258,26 @@
 
 def lane_sum(row):
     return jnp.sum(row, axis=1, keepdims=True)
+
+
+def on_even(axis):
+    return lax.rem(lax.axis_index(axis), 2) == 0
+
+
+def by_pair(axis, low, high, first, second):
+    @pl.when(on_even(axis))
+    def _():
+        first[...] = high[...]
+        second[...] = low[...]
+
+    @pl.when(jnp.logical_not(on_even(axis)))
+    def _():
+        first[...] = low[...]
+        second[...] = high[...]
+
+
+def by_side(axis, first, second, low, high):
+    by_pair(axis, second, first, high, low)
 
 
 COUPLINGS, DIAGONALS, WELL_FIELDS, IDS, RIGHT_SIDE, START = range(6)
@@ -293,7 +331,8 @@
 
 
 def x_pack_kernel(*refs):
-    sources, packs, held_ends, arrived = refs[:6], refs[6:8], refs[8:20], refs[20]
+    sources, first, second, held_ends, arrived = refs[:6], refs[6], refs[7], refs[8:20], refs[20]
+    packs = refs[21:23]
     copies = []
     for n, source in enumerate(sources):
         lead = (slice(None),) * (len(source.shape) - 3)
@@ -319,6 +358,7 @@
                 index + (1 - layer if end else layer,)
             ],
         )
+    by_pair("gx", *packs, first, second)
 
 
 def y_cut(arguments, end):
@@ -337,9 +377,10 @@
     return copy
 
 
-def corner_kernel(y_low, y_high, fxl, fxh, low_out, high_out):
+def corner_kernel(y_low, y_high, came_first, came_second, first, second, fxl, fxh, *outs):
+    by_side("gx", came_first, came_second, fxl, fxh)
     last = fxl.shape[1] - 1
-    for own, out, at, side in ((y_low, low_out, 0, 4), (y_high, high_out, last, 0)):
+    for own, out, at, side in ((y_low, outs[0], 0, 4), (y_high, outs[1], last, 0)):
         for n in range(FACE_PLANES):
             out[n] = own[n]
         row = FACE_PLANES * 8
@@ -351,16 +392,19 @@
             for n, y in rows:
                 out[row // 8, row % 8 : row % 8 + 1, :] = face[n, y : y + 1, :]
                 row += 1
-
-
-def image_corner_kernel(y_low, y_high, gxl, gxh, low_out, high_out):
+    by_pair("gy", *outs, first, second)
+
+
+def image_corner_kernel(y_low, y_high, came_first, came_second, first, second, gxl, gxh, *outs):
+    by_side("gx", came_first, came_second, gxl, gxh)
     last = gxl.shape[1] - 1
-    for own, out, at in ((y_low, low_out, 0), (y_high, high_out, last)):
+    for own, out, at in ((y_low, outs[0], 0), (y_high, outs[1], last)):
         for n in range(IMAGE_PLANES):
             out[n] = own[n]
         for x_end, face in enumerate((gxl, gxh)):
             for n in range(8):
                 out[IMAGE_PLANES + x_end, n : n + 1, :] = face[n, at : at + 1, :]
+    by_pair("gy", *outs, first, second)
 
 
 def guess_kernel(
@@ -400,10 +444,12 @@
 
 
 def residual_kernel(
-    couplings, diagonal, wells, ids, fxl, fxh, fyl, fyh, parts,
+    couplings, diagonal, wells, ids, fxl, fxh, came_first, came_second, parts,
     rest, leaving, low_blocks, high_blocks,
-    residual, image, residual_faces, x_low, x_high, y_low, y_high, small,
+    residual, image, residual_faces, x_first, x_second, y_low, y_high, small, fyl, fyh,
+    x_low, x_high,
 ):
+    by_side("gy", came_first, came_second, fyl, fyh)
     faces = (fxl, fxh, fyl, fyh)
     totals = jnp.sum(parts[...], axis=0)
     corners = corners_of(faces, FACE_PLANES, CORNER_ROWS)
@@ -488,6 +534,7 @@
             for a in range(2):
                 pack[2 * k + a] = here[a]
                 pack[8 + 2 * k + a] = local[a]
+    by_pair("gx", x_low, x_high, x_first, x_second)
     small[...] = jnp.concatenate(
         [unpack_row(totals, 4), unpack_row(totals, 5), jnp.zeros((6, LANES), jnp.float32)], axis=0
     )
@@ -530,10 +577,11 @@
 
 
 def krylov_kernel(
-    couplings, diagonal, wells, ids, fxl, fxh, fyl, fyh, gxl, gxh, gyl, gyh,
+    couplings, diagonal, wells, ids, fxl, fxh, fyl, fyh, gxl, gxh, came_first, came_second,
     residual, image, residual_faces, parts, small_in, present,
-    second_out, third_out, part, known, scratch, values_scratch, dots,
+    second_out, third_out, part, known, scratch, values_scratch, dots, gyl, gyh,
 ):
+    by_side("gy", came_first, came_second, gyl, gyh)
     faces, sent = (fxl, fxh, fyl, fyh), (gxl, gxh, gyl, gyh)
     totals = jnp.sum(parts[...], axis=0)
     small = small_in[...]
@@ -757,10 +805,14 @@
     return pltpu.VMEM(shape, jnp.float32)
 
 
-def from_behind(value, axis, steps):
-    count = lax.axis_size(axis)
-    leading, last = (max(0, -steps), min(count, count - steps))
-    return lax.ppermute(value, axis, [(source, source + steps) for source in range(leading, last)])
+def swapped(first, second, axis):
+    results = []
+    for start, value in enumerate((first, second)):
+        pairs = []
+        for low in range(start, lax.axis_size(axis) - 1, 2):
+            pairs += [(low, low + 1), (low + 1, low)]
+        results.append(lax.ppermute(value, axis, pairs) if pairs else jnp.zeros_like(value))
+    return results
 
 
 def exchanged(part):
@@ -778,49 +830,53 @@
     for argument in arguments:
         shape = argument.shape[:-3] + (2,) + argument.shape[-2:]
         ends += [pltpu.VMEM(shape, argument.dtype)] * 2
-    x_low, x_high = call(
+    x_first, x_second = call(
         x_pack_kernel,
         [(FACE_PLANES + 1,) + plane] * 2,
         [pltpu.with_memory_space_constraint(argument, pltpu.HBM) for argument in arguments],
-        ends + [pltpu.SemaphoreType.DMA((len(ends),))],
+        ends
+        + [pltpu.SemaphoreType.DMA((len(ends),))]
+        + [held(FACE_PLANES + 1, *plane)] * 2,
         own_copies=True,
     )
-    fxl = from_behind(x_high, "gx", 1)
-    fxh = from_behind(x_low, "gx", -1)
+    came_x = swapped(x_first, x_second, "gx")
     first_chunks, chunks = (devices, TABLE_ROWS, LANES), (devices, 8, LANES)
     sent = pltpu.SemaphoreType.DMA((1,))
     part, present, y_low, y_high = call(
         guess_kernel,
-        [first_chunks, (WELLS + 1,)] + [(FACE_PLANES,) + plane] * 2,
+        [first_chunks, (WELLS + 8,)] + [(FACE_PLANES,) + plane] * 2,
         arguments,
         [held(6, *block), held(6, WELLS, LANES), held(*first_chunks), sent],
         cost=4 << 20,
         out=1,
     )
-    parts = exchanged(after(part, fxl))
-    y_low, y_high = call(
+    parts = exchanged(after(part, came_x[0]))
+    y_shape = (FACE_PLANES + CORNER_PLANES,) + plane
+    y_first, y_second, fxl, fxh = call(
         corner_kernel,
-        [(FACE_PLANES + CORNER_PLANES,) + plane] * 2,
-        (y_low, y_high, fxl, fxh),
-    )
-    fyl = from_behind(y_high, "gy", 1)
-    fyh = from_behind(y_low, "gy", -1)
-
+        [y_shape] * 2 + [(FACE_PLANES + 1,) + plane] * 2,
+        (y_low, y_high, *came_x),
+        [held(*y_shape)] * 2,
+    )
+    came_y = swapped(y_first, y_second, "gy")
     ahead = call(
         block_kernel,
         [field, (4, 8) + plane] + [(LAYER_BLOCKS,) + plane] * 2,
-        (couplings, diagonal, right, guess, y_low),
+        (couplings, diagonal, right, guess, y_first),
         cost=4 << 20,
     )
 
+    residual, image, residual_faces, x_first, x_second, y_low, y_high, small, fyl, fyh = call(
+        residual_kernel,
+        [field, field, (4, 8) + plane]
+        + [(IMAGE_PLANES,) + plane] * 4
+        + [(8, LANES)]
+        + [y_shape] * 2,
+        (couplings, diagonal, wells, ids, fxl, fxh, *came_y, parts, *ahead),
+        [held(IMAGE_PLANES, *plane)] * 2,
+    )
     faces = (fxl, fxh, fyl, fyh)
-    residual, image, residual_faces, x_low, x_high, y_low, y_high, small = call(
-        residual_kernel,
-        [field, field, (4, 8) + plane] + [(IMAGE_PLANES,) + plane] * 4 + [(8, LANES)],
-        (couplings, diagonal, wells, ids) + faces + (parts, *ahead),
-    )
-    gxl = from_behind(x_high, "gx", 1)
-    gxh = from_behind(x_low, "gx", -1)
+    came_x = swapped(x_first, x_second, "gx")
     (part,) = call(
         moments_kernel,
         [chunks],
@@ -829,21 +885,23 @@
         cost=4 << 20,
         out=1,
     )
-    parts = exchanged(after(part, gxl, gxh))
-    y_low, y_high = call(
+    parts = exchanged(after(part, *came_x))
+    y_shape = (IMAGE_PLANES + 2,) + plane
+    y_first, y_second, gxl, gxh = call(
         image_corner_kernel,
-        [(IMAGE_PLANES + 2,) + plane] * 2,
-        (y_low, y_high, gxl, gxh),
-    )
-    gyl = from_behind(y_high, "gy", 1)
-    gyh = from_behind(y_low, "gy", -1)
+        [y_shape] * 2 + [(IMAGE_PLANES,) + plane] * 2,
+        (y_low, y_high, *came_x),
+        [held(*y_shape)] * 2,
+    )
+    came_y = swapped(y_first, y_second, "gy")
 
     second, third, part, known = call(
         krylov_kernel,
         [field, field, (devices, 1, (RHS + 1) * LANES), (4 * RHS, LANES)],
-        (couplings, diagonal, wells, ids) + faces + (gxl, gxh, gyl, gyh)
+        (couplings, diagonal, wells, ids) + faces + (gxl, gxh, *came_y)
         + (residual, image, residual_faces, parts, small, present),
-        [held(12, WELLS, LANES), held(12, *block), held(10, *plane)],
+        [held(12, WELLS, LANES), held(12, *block), held(10, *plane)]
+        + [held(*y_shape)] * 2,
     )
     parts = exchanged(part)
     (result,) = call(

time: 68.1 us -> 62.8 us (0.922)
  starting transfers between devices: 28.8 us -> 24 us
  local copies, waits for them, and re-layouts: 0.02 us -> 3.08 us
  blocking collectives: 13.4 us -> 10.7 us
  waiting for transfers between devices: 11.7 us -> 10.3 us
    ppermute x8, waiting for transfers between devices: 8.34 us -> 0.96 us  [swapped(): lax.ppermute(value, axis, pairs)]
    ppermute x8, starting transfers between devices: 17 us -> 9.95 us  [swapped(): lax.ppermute(value, axis, pairs)]
    all_to_all x2, waiting for transfers between devices: 3.31 us -> 9.32 us  [exchanged(): return lax.all_to_all(part, ('gx', 'gy'), 0, 0, tiled=True)]
    unnamed x12 -> x28, local copies, waits for them, and re-layouts: 0.02 us -> 3.08 us
    all_to_all x1, blocking collectives: 13.4 us -> 10.7 us  [exchanged(): return lax.all_to_all(part, ('gx', 'gy'), 0, 0, tiled=True)]
    all_to_all x2, starting transfers between devices: 11.8 us -> 14 us  [exchanged(): return lax.all_to_all(part, ('gx', 'gy'), 0, 0, tiled=True)]
  transfers between devices with their start and end apart: 10 -> 10, of which waited for: 5 -> 4; matrix products, arithmetic and copies ran while one was open for 0% -> 0% of each run, Pallas kernels for 9% -> 10%
where the time goes in v15:
time: 62.8 us; the launch traced here: 62.4 us
  starting transfers between devices  24 us (38%)
  Pallas kernels  14.1 us (22%)
  blocking collectives  10.7 us (17%)
  waiting for transfers between devices  10.3 us (16%)
  local copies, waits for them, and re-layouts  3.08 us (5%)
    pallas_call x9, Pallas kernels, call(): pl.pallas_call(kernel, out_shape=outs, in_specs=[place(argument) for argu...  14.1 us
    all_to_all x2, starting transfers between devices, exchanged(): return lax.all_to_all(part, ('gx', 'gy'), 0, 0, tiled=True)  14 us
    all_to_all x1, blocking collectives, exchanged(): return lax.all_to_all(part, ('gx', 'gy'), 0, 0, tiled=True)  10.7 us
    ppermute x8, starting transfers between devices, swapped(): lax.ppermute(value, axis, pairs)  9.95 us
    all_to_all x2, waiting for transfers between devices, exchanged(): return lax.all_to_all(part, ('gx', 'gy'), 0, 0, tiled=True)  9.32 us
    unnamed x28, local copies, waits for them, and re-layouts  3.08 us
  transfers between devices with their start and end apart: 10, of which 4 were waited for; matrix products, arithmetic and copies ran while one was open for 0% of the time, Pallas kernels for 10%

profile of v15, /device:TPU:0, one launch (start us, length us, event | category | flops | bytes accessed | tf_op | source)
XLA Modules:
  0.0 62.4 jit_solution(13289272043875724952)
XLA Ops:
  0.0 0.0 copy-start.3
  0.0 0.0 copy-start.2
  0.0 0.0 copy-start.4
  0.0 1.5 %shard_map.65 = (f32[37,8,128]{2,1,0:T(8,128)S(1)}, f32[37,8,128]{2,1,0:T(8,128)S(1)}) custom-call(f32[6,4,8,8,128]{4,3,2,1,0:T(8,128)} %couplings.7, f32[4,8,8,128]{3,2,1,0:T(8,128)} %diagonal.7, f32[4,8,8,128]{3,2,1,0:T(8,128)} %wells.7, s32[8,8,128]{2,1,0:T(8,128)} %ids.7, f32[4,2,8,8,128]{4,3,2,1,0:T(8,128)} %right.3, f32[4,2,8,8,128]{4,3,2,1,0:T(8,128)} %guess.5), custom_call_target="tpu_custom_call" | custom-call | tf_op jit(solution)/shard_map/pallas_call | solution.py:774
  1.6 3.1 %collective-permute-start = (f32[37,8,128]{2,1,0:T(8,128)S(1)}, f32[37,8,128]{2,1,0:T(8,128)S(1)}, u32[]{:S(2)}, u32[]{:S(2)}) collective-permute-start(f32[37,8,128]{2,1,0:T(8,128)S(1)} %get-tuple-element.39), channel_id=1, source_target_pairs={{0,8},{8,0},{16,24},{24,16},{1,9},{9,1},{17,25},{25,17},{2,10},{10... | collective-permute-start | bytes 454664 | tf_op jit(solution)/shard_map/ppermute | solution.py:814
  4.7 0.7 %collective-permute-start.1 = (f32[37,8,128]{2,1,0:T(8,128)S(1)}, f32[37,8,128]{2,1,0:T(8,128)S(1)}, u32[]{:S(2)}, u32[]{:S(2)}) collective-permute-start(f32[37,8,128]{2,1,0:T(8,128)S(1)} %get-tuple-element.40), channel_id=1, source_target_pairs={{8,16},{16,8},{9,17},{17,9},{10,18},{18,10},{11,19},{19,11},{12,20... | collective-permute-start | bytes 454664 | tf_op jit(solution)/shard_map/ppermute | solution.py:814
  5.3 0.0 copy-done.5
  5.3 0.0 copy-done.3
  5.4 0.0 copy-done.2
  5.4 0.0 copy-done
  5.4 0.0 copy-done.1
  5.4 0.0 copy-done.4
  5.4 3.3 %shard_map.64 = (f32[32,6,128]{2,1,0:T(8,128)}, s32[48]{0:T(128)S(1)}, f32[36,8,128]{2,1,0:T(8,128)S(1)}, f32[36,8,128]{2,1,0:T(8,128)S(1)}) custom-call(f32[6,4,8,8,128]{4,3,2,1,0:T(8,128)S(1)} %copy-done, f32[4,8,8,128]{3,2,1,0:T(8,128)S(1)} %copy-done.2, f32[4,8,8,128]{3,2,1,0:T(8,128)S(1)} %copy-done.3, s32[8,8,128]{2,1,0:T(8,128)S(1)} %copy-done.5, ...), custom_call_target="tpu_custom_call" | custom-call | flops 4194304 | bytes 4194304 | tf_op jit(solution)/shard_map/pallas_call | solution.py:774
  8.7 0.0 collective-permute-done.came_first.rest_0_
  8.7 5.9 %all-to-all-start = ((f32[32,6,128]{2,1,0:T(8,128)}), f32[32,6,128]{2,1,0:T(8,128)S(1)}, u32[]{:S(2)}, u32[]{:S(2)}) async-start(f32[32,6,128]{2,1,0:T(8,128)} %shard_map.67), calls=%async_computation | async-start | bytes 262144 | tf_op jit(solution)/shard_map/all_to_all | solution.py:819
  14.6 0.0 collective-permute-done.1.came_second
  14.6 0.1 shard_map.66
  14.8 0.7 %collective-permute-start.3 = (f32[41,8,128]{2,1,0:T(8,128)S(1)}, f32[41,8,128]{2,1,0:T(8,128)S(1)}, u32[]{:S(2)}, u32[]{:S(2)}) collective-permute-start(f32[41,8,128]{2,1,0:T(8,128)S(1)} %get-tuple-element.44), channel_id=1, source_target_pairs={{1,2},{2,1},{3,4},{4,3},{5,6},{6,5},{9,10},{10,9},{11,12},{12,11},... | collective-permute-start | bytes 503816 | tf_op jit(solution)/shard_map/ppermute | solution.py:814
  15.4 3.2 %collective-permute-start.2 = (f32[41,8,128]{2,1,0:T(8,128)S(1)}, f32[41,8,128]{2,1,0:T(8,128)S(1)}, u32[]{:S(2)}, u32[]{:S(2)}) collective-permute-start(f32[41,8,128]{2,1,0:T(8,128)S(1)} %get-tuple-element.43.sent_face), channel_id=1, source_target_pairs={{0,1},{1,0},{2,3},{3,2},{4,5},{5,4},{6,7},{7,6},{8,9},{9,8},{10,11... | collective-permute-start | bytes 503816 | tf_op jit(solution)/shard_map/ppermute | solution.py:814
  18.6 0.4 shard_map.68
  19.1 0.0 copy-start.6
  19.1 0.6 %copy-done.6 = f32[24,8,128]{2,1,0:T(8,128)} copy-done((f32[24,8,128]{2,1,0:T(8,128)}, f32[24,8,128]{2,1,0:T(8,128)S(1)}, u32[]{:S(2)}) %copy-start.6) | copy-done | bytes 98328
  19.7 0.6 %copy-done.8 = f32[24,8,128]{2,1,0:T(8,128)} copy-done((f32[24,8,128]{2,1,0:T(8,128)}, f32[24,8,128]{2,1,0:T(8,128)S(1)}, u32[]{:S(2)}) %copy-start.8) | copy-done | bytes 98328
  20.3 0.0 collective-permute-done.3.came_second
  20.3 0.0 collective-permute-done.2.came_first
  20.3 2.5 %all-to-all-done.parts = f32[32,6,128]{2,1,0:T(8,128)S(1)} async-done(((f32[32,6,128]{2,1,0:T(8,128)}), f32[32,6,128]{2,1,0:T(8,128)S(1)}, u32[]{:S(2)}, u32[]{:S(2)}) %all-to-all-start) | async-done | bytes 98336 | tf_op jit(solution)/shard_map/all_to_all | solution.py:819
  22.9 0.9 %copy-done.7 = f32[24,8,128]{2,1,0:T(8,128)S(1)} copy-done((f32[24,8,128]{2,1,0:T(8,128)S(1)}, f32[24,8,128]{2,1,0:T(8,128)}, u32[]{:S(2)}) %copy-start.7) | copy-done | bytes 98328
  23.8 0.9 %copy-done.9 = f32[24,8,128]{2,1,0:T(8,128)S(1)} copy-done((f32[24,8,128]{2,1,0:T(8,128)S(1)}, f32[24,8,128]{2,1,0:T(8,128)}, u32[]{:S(2)}) %copy-start.9) | copy-done | bytes 98328
  24.6 0.9 %shard_map.69 = (f32[4,2,8,8,128]{4,3,2,1,0:T(8,128)S(1)}, f32[4,2,8,8,128]{4,3,2,1,0:T(8,128)S(1)}, f32[4,8,8,128]{3,2,1,0:T(8,128)S(1)}, f32[16,8,128]{2,1,0:T...) custom-call(f32[6,4,8,8,128]{4,3,2,1,0:T(8,128)S(1)} %copy-done, ...), custom_call_target="tpu_custom_call" | custom-call | tf_op jit(solution)/shard_map/pallas_call | solution.py:774
  25.6 0.7 %collective-permute-start.4 = (f32[16,8,128]{2,1,0:T(8,128)S(1)}, f32[16,8,128]{2,1,0:T(8,128)S(1)}, u32[]{:S(2)}, u32[]{:S(2)}) collective-permute-start(f32[16,8,128]{2,1,0:T(8,128)S(1)} %get-tuple-element.55), channel_id=1, source_target_pairs={{0,8},{8,0},{16,24},{24,16},{1,9},{9,1},{17,25},{25,17},{2,10},{10... | collective-permute-start | bytes 196616 | tf_op jit(solution)/shard_map/ppermute | solution.py:814
  26.3 0.7 %collective-permute-start.5 = (f32[16,8,128]{2,1,0:T(8,128)S(1)}, f32[16,8,128]{2,1,0:T(8,128)S(1)}, u32[]{:S(2)}, u32[]{:S(2)}) collective-permute-start(f32[16,8,128]{2,1,0:T(8,128)S(1)} %get-tuple-element.56), channel_id=1, source_target_pairs={{8,16},{16,8},{9,17},{17,9},{10,18},{18,10},{11,19},{19,11},{12,20... | collective-permute-start | bytes 196616 | tf_op jit(solution)/shard_map/ppermute | solution.py:814
  27.0 2.6 %shard_map.71.value = f32[32,8,128]{2,1,0:T(8,128)} custom-call(f32[4,8,8,128]{3,2,1,0:T(8,128)S(1)} %copy-done.3, s32[8,8,128]{2,1,0:T(8,128)S(1)} %copy-done.5, f32[4,2,8,8,128]{4,3,2,1,0:T(8,128)S(1)} %get-tuple-element.50.residual, f32[4,2,8,8,128]{4,3,2,1,0:T(8,128)S(1)} %get-tuple-element.61.image, s32[48]{0:T(128)S(1)} %get-tuple-element.63.present), custom_call_target="tpu_custom_call" | custom-call | flops 4194304 | bytes 4194304 | tf_op jit(solution)/shard_map/pallas_call | solution.py:774
  29.5 0.0 copy-done.10
  29.5 0.0 copy-done.12
  29.6 0.6 collective-permute-done.4.came_first.rest_0_
  30.1 0.0 collective-permute-done.5.came_second.rest_1_
  30.2 8.1 %all-to-all-start.1 = ((f32[32,8,128]{2,1,0:T(8,128)}), f32[32,8,128]{2,1,0:T(8,128)S(1)}, u32[]{:S(2)}, u32[]{:S(2)}) async-start(f32[32,8,128]{2,1,0:T(8,128)} %shard_map.72), calls=%async_computation.1 | async-start | bytes 262144 | tf_op jit(solution)/shard_map/all_to_all | solution.py:819
  38.3 0.0 copy-done.11
  38.3 0.0 copy-done.13
  38.3 0.1 shard_map.70
  38.4 0.3 collective-permute-start.6
  38.7 0.7 %collective-permute-start.7 = (f32[18,8,128]{2,1,0:T(8,128)S(1)}, f32[18,8,128]{2,1,0:T(8,128)S(1)}, u32[]{:S(2)}, u32[]{:S(2)}) collective-permute-start(f32[18,8,128]{2,1,0:T(8,128)S(1)} %get-tuple-element.60), channel_id=1, source_target_pairs={{1,2},{2,1},{3,4},{4,3},{5,6},{6,5},{9,10},{10,9},{11,12},{12,11},... | collective-permute-start | bytes 221192 | tf_op jit(solution)/shard_map/ppermute | solution.py:814
  39.4 0.4 collective-permute-done.6.came_first
  39.7 0.0 collective-permute-done.7.came_second
  39.7 6.8 %all-to-all-done.1.parts = f32[32,8,128]{2,1,0:T(8,128)S(1)} async-done(((f32[32,8,128]{2,1,0:T(8,128)}), f32[32,8,128]{2,1,0:T(8,128)S(1)}, u32[]{:S(2)}, u32[]{:S(2)}) %all-to-all-start.1) | async-done | bytes 131104 | tf_op jit(solution)/shard_map/all_to_all | solution.py:819
  46.5 3.5 %shard_map.73 = (f32[4,2,8,8,128]{4,3,2,1,0:T(8,128)S(1)}, f32[4,2,8,8,128]{4,3,2,1,0:T(8,128)S(1)}, f32[32,1,640]{2,1,0:T(1,128)S(1)}, f32[16,128]{1,0:T(8,128)S(1)}) custom-call(f32[6,4,8,8,128]{4,3,2,1,0:T(8,128)S(1)} %copy-done, f32[4,8,8,128]{3,2,1,0:T(8,128)S(1)} %copy-done.2, f32[4,8,8,128]{3,2,1,0:T(8,128)S(1)} %copy-done.3, ...), custom_call_target="tpu_custom_call" | custom-call | tf_op jit(solution)/shard_map/pallas_call | solution.py:774
  50.0 10.7 %all_to_all.15.parts = f32[32,1,640]{2,1,0:T(1,128)S(1)} all-to-all(f32[32,1,640]{2,1,0:T(1,128)S(1)} %get-tuple-element.67), channel_id=1, replica_groups=mesh['member'=1,'gx'=4,'gy'=8] {'gx','gy'}, dimensions={0} | all-to-all | bytes 163840 | tf_op jit(solution)/shard_map/all_to_all | solution.py:819
  60.7 1.7 %shard_map.74 = f32[4,2,8,8,128]{4,3,2,1,0:T(8,128)} custom-call(f32[4,2,8,8,128]{4,3,2,1,0:T(8,128)S(1)} %copy-done.1, f32[4,2,8,8,128]{4,3,2,1,0:T(8,128)S(1)} %get-tuple-element.50.residual, f32[4,2,8,8,128]{4,3,2,1,0:T(8,128)S(1)} %get-tuple-element.65.second, f32[4,2,8,8,128]{4,3,2,1,0:T(8,128)S(1)} %get-tuple-element.66.third, ...), custom_call_target="tpu_custom_call" | custom-call | tf_op jit(solution)/shard_map/pallas_call | solution.py:774
  (12 shorter events, 0.0 us)
Async XLA Ops:
  0.0 5.3 %copy-start.5 = (s32[8,8,128]{2,1,0:T(8,128)S(1)}, s32[8,8,128]{2,1,0:T(8,128)}, u32[]{:S(2)}) copy-start(s32[8,8,128]{2,1,0:T(8,128)} %ids.7) | copy-start | bytes 98308
  0.0 5.3 %copy-start.3 = (f32[4,8,8,128]{3,2,1,0:T(8,128)S(1)}, f32[4,8,8,128]{3,2,1,0:T(8,128)}, u32[]{:S(2)}) copy-start(f32[4,8,8,128]{3,2,1,0:T(8,128)} %wells.7) | copy-start | bytes 393220
  0.0 5.4 %copy-start.2 = (f32[4,8,8,128]{3,2,1,0:T(8,128)S(1)}, f32[4,8,8,128]{3,2,1,0:T(8,128)}, u32[]{:S(2)}) copy-start(f32[4,8,8,128]{3,2,1,0:T(8,128)} %diagonal.7) | copy-start | bytes 393220
  0.0 5.4 %copy-start = (f32[6,4,8,8,128]{4,3,2,1,0:T(8,128)S(1)}, f32[6,4,8,8,128]{4,3,2,1,0:T(8,128)}, u32[]{:S(2)}) copy-start(f32[6,4,8,8,128]{4,3,2,1,0:T(8,128)} %couplings.7) | copy-start | bytes 2359300
  0.0 5.4 %copy-start.1 = (f32[4,2,8,8,128]{4,3,2,1,0:T(8,128)S(1)}, f32[4,2,8,8,128]{4,3,2,1,0:T(8,128)}, u32[]{:S(2)}) copy-start(f32[4,2,8,8,128]{4,3,2,1,0:T(8,128)} %guess.5) | copy-start | bytes 786436
  0.0 5.4 %copy-start.4 = (f32[4,2,8,8,128]{4,3,2,1,0:T(8,128)S(1)}, f32[4,2,8,8,128]{4,3,2,1,0:T(8,128)}, u32[]{:S(2)}) copy-start(f32[4,2,8,8,128]{4,3,2,1,0:T(8,128)} %right.3) | copy-start | bytes 786436
  1.6 7.1 %collective-permute-start = (f32[37,8,128]{2,1,0:T(8,128)S(1)}, f32[37,8,128]{2,1,0:T(8,128)S(1)}, u32[]{:S(2)}, u32[]{:S(2)}) collective-permute-start(f32[37,8,128]{2,1,0:T(8,128)S(1)} %get-tuple-element.39), channel_id=1, source_target_pairs={{0,8},{8,0},{16,24},{24,16},{1,9},{9,1},{17,25},{25,17},{2,10},{10... | collective-permute-start | bytes 454664 | tf_op jit(solution)/shard_map/ppermute | solution.py:814
  4.7 10.0 %collective-permute-start.1 = (f32[37,8,128]{2,1,0:T(8,128)S(1)}, f32[37,8,128]{2,1,0:T(8,128)S(1)}, u32[]{:S(2)}, u32[]{:S(2)}) collective-permute-start(f32[37,8,128]{2,1,0:T(8,128)S(1)} %get-tuple-element.40), channel_id=1, source_target_pairs={{8,16},{16,8},{9,17},{17,9},{10,18},{18,10},{11,19},{19,11},{12,20... | collective-permute-start | bytes 454664 | tf_op jit(solution)/shard_map/ppermute | solution.py:814
  8.7 14.2 %all-to-all-start = ((f32[32,6,128]{2,1,0:T(8,128)}), f32[32,6,128]{2,1,0:T(8,128)S(1)}, u32[]{:S(2)}, u32[]{:S(2)}) async-start(f32[32,6,128]{2,1,0:T(8,128)} %shard_map.67), calls=%async_computation | async-start | bytes 262144 | tf_op jit(solution)/shard_map/all_to_all | solution.py:819
  14.8 5.6 %collective-permute-start.3 = (f32[41,8,128]{2,1,0:T(8,128)S(1)}, f32[41,8,128]{2,1,0:T(8,128)S(1)}, u32[]{:S(2)}, u32[]{:S(2)}) collective-permute-start(f32[41,8,128]{2,1,0:T(8,128)S(1)} %get-tuple-element.44), channel_id=1, source_target_pairs={{1,2},{2,1},{3,4},{4,3},{5,6},{6,5},{9,10},{10,9},{11,12},{12,11},... | collective-permute-start | bytes 503816 | tf_op jit(solution)/shard_map/ppermute | solution.py:814
  15.4 4.9 %collective-permute-start.2 = (f32[41,8,128]{2,1,0:T(8,128)S(1)}, f32[41,8,128]{2,1,0:T(8,128)S(1)}, u32[]{:S(2)}, u32[]{:S(2)}) collective-permute-start(f32[41,8,128]{2,1,0:T(8,128)S(1)} %get-tuple-element.43.sent_face), channel_id=1, source_target_pairs={{0,1},{1,0},{2,3},{3,2},{4,5},{5,4},{6,7},{7,6},{8,9},{9,8},{10,11... | collective-permute-start | bytes 503816 | tf_op jit(solution)/shard_map/ppermute | solution.py:814
  19.1 0.6 %copy-start.6 = (f32[24,8,128]{2,1,0:T(8,128)}, f32[24,8,128]{2,1,0:T(8,128)S(1)}, u32[]{:S(2)}) copy-start(f32[24,8,128]{2,1,0:T(8,128)S(1)} %get-tuple-element.48.low_blocks) | copy-start | bytes 294916
  19.7 0.6 %copy-start.8 = (f32[24,8,128]{2,1,0:T(8,128)}, f32[24,8,128]{2,1,0:T(8,128)S(1)}, u32[]{:S(2)}) copy-start(f32[24,8,128]{2,1,0:T(8,128)S(1)} %get-tuple-element.49.high_blocks) | copy-start | bytes 294916
  22.9 0.9 %copy-start.7 = (f32[24,8,128]{2,1,0:T(8,128)S(1)}, f32[24,8,128]{2,1,0:T(8,128)}, u32[]{:S(2)}) copy-start(f32[24,8,128]{2,1,0:T(8,128)} %copy-done.6) | copy-start | bytes 294916
  23.8 0.9 %copy-start.9 = (f32[24,8,128]{2,1,0:T(8,128)S(1)}, f32[24,8,128]{2,1,0:T(8,128)}, u32[]{:S(2)}) copy-start(f32[24,8,128]{2,1,0:T(8,128)} %copy-done.8) | copy-start | bytes 294916
  25.6 3.9 %copy-start.10 = (f32[16,8,128]{2,1,0:T(8,128)}, f32[16,8,128]{2,1,0:T(8,128)S(1)}, u32[]{:S(2)}) copy-start(f32[16,8,128]{2,1,0:T(8,128)S(1)} %get-tuple-element.53.y_low) | copy-start | bytes 196612
  25.6 4.0 %copy-start.12 = (f32[16,8,128]{2,1,0:T(8,128)}, f32[16,8,128]{2,1,0:T(8,128)S(1)}, u32[]{:S(2)}) copy-start(f32[16,8,128]{2,1,0:T(8,128)S(1)} %get-tuple-element.54.y_high) | copy-start | bytes 196612
  25.6 4.6 %collective-permute-start.4 = (f32[16,8,128]{2,1,0:T(8,128)S(1)}, f32[16,8,128]{2,1,0:T(8,128)S(1)}, u32[]{:S(2)}, u32[]{:S(2)}) collective-permute-start(f32[16,8,128]{2,1,0:T(8,128)S(1)} %get-tuple-element.55), channel_id=1, source_target_pairs={{0,8},{8,0},{16,24},{24,16},{1,9},{9,1},{17,25},{25,17},{2,10},{10... | collective-permute-start | bytes 196616 | tf_op jit(solution)/shard_map/ppermute | solution.py:814
  26.3 3.8 %collective-permute-start.5 = (f32[16,8,128]{2,1,0:T(8,128)S(1)}, f32[16,8,128]{2,1,0:T(8,128)S(1)}, u32[]{:S(2)}, u32[]{:S(2)}) collective-permute-start(f32[16,8,128]{2,1,0:T(8,128)S(1)} %get-tuple-element.56), channel_id=1, source_target_pairs={{8,16},{16,8},{9,17},{17,9},{10,18},{18,10},{11,19},{19,11},{12,20... | collective-permute-start | bytes 196616 | tf_op jit(solution)/shard_map/ppermute | solution.py:814
  30.2 8.1 %copy-start.11 = (f32[16,8,128]{2,1,0:T(8,128)S(1)}, f32[16,8,128]{2,1,0:T(8,128)}, u32[]{:S(2)}) copy-start(f32[16,8,128]{2,1,0:T(8,128)} %copy-done.10) | copy-start | bytes 196612
  30.2 8.1 %copy-start.13 = (f32[16,8,128]{2,1,0:T(8,128)S(1)}, f32[16,8,128]{2,1,0:T(8,128)}, u32[]{:S(2)}) copy-start(f32[16,8,128]{2,1,0:T(8,128)} %copy-done.12) | copy-start | bytes 196612
  30.2 16.4 %all-to-all-start.1 = ((f32[32,8,128]{2,1,0:T(8,128)}), f32[32,8,128]{2,1,0:T(8,128)S(1)}, u32[]{:S(2)}, u32[]{:S(2)}) async-start(f32[32,8,128]{2,1,0:T(8,128)} %shard_map.72), calls=%async_computation.1 | async-start | bytes 262144 | tf_op jit(solution)/shard_map/all_to_all | solution.py:819
  38.4 1.3 %collective-permute-start.6 = (f32[18,8,128]{2,1,0:T(8,128)S(1)}, f32[18,8,128]{2,1,0:T(8,128)S(1)}, u32[]{:S(2)}, u32[]{:S(2)}) collective-permute-start(f32[18,8,128]{2,1,0:T(8,128)S(1)} %get-tuple-element.59), channel_id=1, source_target_pairs={{0,1},{1,0},{2,3},{3,2},{4,5},{5,4},{6,7},{7,6},{8,9},{9,8},{10,11... | collective-permute-start | bytes 221192 | tf_op jit(solution)/shard_map/ppermute | solution.py:814
  38.7 1.0 %collective-permute-start.7 = (f32[18,8,128]{2,1,0:T(8,128)S(1)}, f32[18,8,128]{2,1,0:T(8,128)S(1)}, u32[]{:S(2)}, u32[]{:S(2)}) collective-permute-start(f32[18,8,128]{2,1,0:T(8,128)S(1)} %get-tuple-element.60), channel_id=1, source_target_pairs={{1,2},{2,1},{3,4},{4,3},{5,6},{6,5},{9,10},{10,9},{11,12},{12,11},... | collective-permute-start | bytes 221192 | tf_op jit(solution)/shard_map/ppermute | solution.py:814

commit v16 on v15

--- a/solution.py
+++ b/solution.py
@@ -371,7 +371,8 @@
 
 
 def send_out(table, chunks, part, sent):
-    chunks[...] = jnp.broadcast_to(table[None, : chunks.shape[1]], chunks.shape)
+    rows = min(chunks.shape[1], table.shape[0])
+    chunks[:, :rows, :] = jnp.broadcast_to(table[None, :rows], (chunks.shape[0], rows, LANES))
     copy = pltpu.make_async_copy(chunks, part, sent.at[0])
     copy.start()
     return copy
@@ -395,16 +396,12 @@
     by_pair("gy", *outs, first, second)
 
 
-def image_corner_kernel(y_low, y_high, came_first, came_second, first, second, gxl, gxh, *outs):
-    by_side("gx", came_first, came_second, gxl, gxh)
-    last = gxl.shape[1] - 1
-    for own, out, at in ((y_low, outs[0], 0), (y_high, outs[1], last)):
-        for n in range(IMAGE_PLANES):
-            out[n] = own[n]
-        for x_end, face in enumerate((gxl, gxh)):
-            for n in range(8):
-                out[IMAGE_PLANES + x_end, n : n + 1, :] = face[n, at : at + 1, :]
-    by_pair("gy", *outs, first, second)
+def diagonal_device(x_end, y_end):
+    across, along = lax.axis_index("gx"), lax.axis_index("gy")
+    there_x, there_y = across + 2 * x_end - 1, along + 2 * y_end - 1
+    count_x, count_y = lax.axis_size("gx"), lax.axis_size("gy")
+    exists = (there_x >= 0) & (there_x < count_x) & (there_y >= 0) & (there_y < count_y)
+    return exists, jnp.where(exists, there_x * count_y + there_y, 0)
 
 
 def guess_kernel(
@@ -426,7 +423,7 @@
 
 
 def block_kernel(
-    couplings, diagonal, right, guess, sent_face, rest, leaving, low_blocks, high_blocks
+    couplings, diagonal, right, guess, sent_face, rest, leaving
 ):
     nothing_enters = [[jnp.zeros(guess.shape[3:], jnp.float32)] * 2] * 4
     for k in range(RHS):
@@ -437,17 +434,13 @@
             rest[k, a] = right[k, a] - inside[a]
             for f in range(4):
                 leaving[f, 2 * k + a] = outgoing[f][a]
-    for end, kept in enumerate((low_blocks, high_blocks)):
-        blocks = layer_blocks(y_cut((couplings, diagonal), end), 3 - end, 0)
-        for n in range(LAYER_BLOCKS):
-            kept[n] = blocks(n)
 
 
 def residual_kernel(
     couplings, diagonal, wells, ids, fxl, fxh, came_first, came_second, parts,
-    rest, leaving, low_blocks, high_blocks,
-    residual, image, residual_faces, x_first, x_second, y_low, y_high, small, fyl, fyh,
-    x_low, x_high,
+    rest, leaving,
+    residual, image, residual_faces, x_first, x_second, y_first, y_second, small, fyl, fyh,
+    x_low, x_high, y_low, y_high,
 ):
     by_side("gy", came_first, came_second, fyl, fyh)
     faces = (fxl, fxh, fyl, fyh)
@@ -501,40 +494,30 @@
         result, _ = block_stencil(couplings, diagonal, now[0], now[1], incoming)
         for a in range(2):
             image[k, a] = result[a]
-        for pack, here, back, blocks in (
-            (
-                x_low,
-                [value[0] for value in result],
-                [value[1] for value in result],
-                layer_blocks(lambda n, i, layer: (couplings, diagonal)[n][i + (layer,)], 1, 2),
-            ),
-            (
-                x_high,
-                [value[last] for value in result],
-                [value[last - 1] for value in result],
-                layer_blocks(
-                    lambda n, i, layer: (couplings, diagonal)[n][i + (last - layer,)], 0, 2
-                ),
-            ),
-            (
-                y_low,
-                [value[:, 0, :] for value in result],
-                [value[:, 1, :] for value in result],
-                lambda n: low_blocks[n],
-            ),
-            (
-                y_high,
-                [value[:, last, :] for value in result],
-                [value[:, last - 1, :] for value in result],
-                lambda n: high_blocks[n],
-            ),
-        ):
-            entering = product(lambda e: blocks(BACK_IN + e), *back)
-            local = face_stencil(blocks, here[0], here[1], entering)
-            for a in range(2):
-                pack[2 * k + a] = here[a]
-                pack[8 + 2 * k + a] = local[a]
+    own = (couplings, diagonal)
+    for axis, packs in enumerate(((x_low, x_high), (y_low, y_high))):
+        for end, pack in enumerate(packs):
+
+            def cut(ref, index, layer):
+                at = last - layer if end else layer
+                return ref[index + ((at,) if axis == 0 else (slice(None), at, slice(None)))]
+
+            plane = layer_blocks(
+                lambda n, index, layer: cut(own[n], index, layer),
+                2 * axis + 1 - end,
+                2 * (1 - axis),
+            )
+            blocks = [plane(n) for n in range(LAYER_BLOCKS)]
+            for k in range(RHS):
+                here = [cut(image, (k, a), 0) for a in range(2)]
+                back = [cut(image, (k, a), 1) for a in range(2)]
+                entering = product(lambda e: blocks[BACK_IN + e], *back)
+                local = face_stencil(lambda n: blocks[n], here[0], here[1], entering)
+                for a in range(2):
+                    pack[2 * k + a] = here[a]
+                    pack[8 + 2 * k + a] = local[a]
     by_pair("gx", x_low, x_high, x_first, x_second)
+    by_pair("gy", y_low, y_high, y_first, y_second)
     small[...] = jnp.concatenate(
         [unpack_row(totals, 4), unpack_row(totals, 5), jnp.zeros((6, LANES), jnp.float32)], axis=0
     )
@@ -556,6 +539,21 @@
         dots[2, row, :] = tile_sum(result, result)
     rows = segment_rows(ids, values, scratch, present)
     table = place_rows(rows, jnp.zeros((8, LANES), jnp.float32))
+    chunks[:, 8:, :] = jnp.zeros_like(chunks[:, 8:, :])
+    last = image.shape[2] - 1
+    for x_end in range(2):
+        for y_end in range(2):
+            exists, place = diagonal_device(x_end, y_end)
+
+            @pl.when(exists)
+            def _():
+                for k in range(RHS):
+                    for a in range(2):
+                        row, y = 8 + 2 * k + a, last * y_end
+                        chunks[pl.ds(place, 1), row : row + 1, :] = image[
+                            k, a, last * x_end, y : y + 1, :
+                        ][None]
+
     send_out(place_columns(dots, WELLS, table), chunks, part, sent).wait()
 
 
@@ -577,13 +575,14 @@
 
 
 def krylov_kernel(
-    couplings, diagonal, wells, ids, fxl, fxh, fyl, fyh, gxl, gxh, came_first, came_second,
+    couplings, diagonal, wells, ids, fxl, fxh, fyl, fyh, x_first, x_second, y_first, y_second,
     residual, image, residual_faces, parts, small_in, present,
-    second_out, third_out, part, known, scratch, values_scratch, dots, gyl, gyh,
+    second_out, third_out, part, known, scratch, values_scratch, dots, gxl, gxh, gyl, gyh,
 ):
-    by_side("gy", came_first, came_second, gyl, gyh)
+    by_side("gx", x_first, x_second, gxl, gxh)
+    by_side("gy", y_first, y_second, gyl, gyh)
     faces, sent = (fxl, fxh, fyl, fyh), (gxl, gxh, gyl, gyh)
-    totals = jnp.sum(parts[...], axis=0)
+    totals = jnp.sum(parts[:, 0:8, :], axis=0)
     small = small_in[...]
     s_rows, s_images, p_rows, p_seconds, scalars = first_step(totals, small)
     known[0:RHS, :] = p_rows
@@ -595,7 +594,7 @@
     known[3 * RHS :, :] = jnp.broadcast_to(small[1:2, :], (RHS, LANES))
     dots[...] = jnp.zeros_like(dots)
     corners = corners_of(faces, FACE_PLANES, CORNER_ROWS)
-    sent_corners = corners_of(sent, IMAGE_PLANES, 8)
+    places = [diagonal_device(c % 2, c // 2)[1] for c in range(4)]
     all_ids = ids[...]
     face_ids = [as_ids(face[WELL_ID]) for face in faces]
     back_ids = [as_ids(face[BACK_ID]) for face in faces]
@@ -619,7 +618,7 @@
             here = spread(s_row, corner_ids[c])[0:1, :]
             corner_now.append(
                 [
-                    sent_corners[c].row(2 * k + a) + corners[c].row(SIDE_EQ + a) * here
+                    parts[pl.ds(places[c], 1), 8 + 2 * k + a, :] + corners[c].row(SIDE_EQ + a) * here
                     for a in range(2)
                 ]
             )
@@ -674,7 +673,11 @@
     part[...] = jnp.broadcast_to(flat[None], part.shape)
 
 
-def solve_kernel(guess, residual, second, third, parts, known, solution):
+def solve_kernel(
+    guess_in, residual, second, third, parts, known, solution, guess, arrived
+):
+    copy = pltpu.make_async_copy(guess_in, guess, arrived.at[0])
+    copy.start()
     flat = jnp.sum(parts[...], axis=0)
     rows = [flat[:, LANES * n : LANES * (n + 1)] for n in range(RHS + 1)]
     for k in range(1, RHS):
@@ -743,6 +746,7 @@
         for j in range(i + 1, 3):
             value = value - hessenberg[i][j] * weights[j]
         weights[i] = value * turns[i]
+    copy.wait()
     for k in range(RHS):
         on_first, on_second, on_third = (
             column[k : k + 1, :] for column in (weights[0] * unit, weights[1], weights[2])
@@ -756,15 +760,15 @@
             )
 
 
-def call(kernel, shapes, arguments, scratch=(), own_copies=False, cost=0, grant=24 << 20, out=0):
+def call(kernel, shapes, arguments, scratch=(), far_inputs=0, cost=0, grant=24 << 20, out=0):
     whole = pl.BlockSpec(memory_space=pltpu.VMEM)
     far = pl.BlockSpec(memory_space=pltpu.HBM)
     scalars = pl.BlockSpec(memory_space=pltpu.SMEM)
 
-    def place(array):
+    def place(number, array):
         if len(array.shape) == 1:
             return scalars
-        return far if own_copies else whole
+        return far if number < far_inputs else whole
 
     outs = [
         jax.ShapeDtypeStruct(shape, jnp.float32 if len(shape) > 1 else jnp.int32)
@@ -774,7 +778,7 @@
     return pl.pallas_call(
         kernel,
         out_shape=outs,
-        in_specs=[place(argument) for argument in arguments],
+        in_specs=[place(*numbered) for numbered in enumerate(arguments)],
         out_specs=[far] * out + [scalars if len(shape) == 1 else whole for shape in shapes[out:]],
         scratch_shapes=list(scratch),
         compiler_params=pltpu.CompilerParams(vmem_limit_bytes=grant),
@@ -837,10 +841,10 @@
         ends
         + [pltpu.SemaphoreType.DMA((len(ends),))]
         + [held(FACE_PLANES + 1, *plane)] * 2,
-        own_copies=True,
+        far_inputs=len(arguments),
     )
     came_x = swapped(x_first, x_second, "gx")
-    first_chunks, chunks = (devices, TABLE_ROWS, LANES), (devices, 8, LANES)
+    first_chunks, chunks = (devices, TABLE_ROWS, LANES), (devices, 16, LANES)
     sent = pltpu.SemaphoreType.DMA((1,))
     part, present, y_low, y_high = call(
         guess_kernel,
@@ -861,22 +865,22 @@
     came_y = swapped(y_first, y_second, "gy")
     ahead = call(
         block_kernel,
-        [field, (4, 8) + plane] + [(LAYER_BLOCKS,) + plane] * 2,
+        [field, (4, 8) + plane],
         (couplings, diagonal, right, guess, y_first),
         cost=4 << 20,
     )
 
-    residual, image, residual_faces, x_first, x_second, y_low, y_high, small, fyl, fyh = call(
+    residual, image, residual_faces, *packs, small, fyl, fyh = call(
         residual_kernel,
         [field, field, (4, 8) + plane]
         + [(IMAGE_PLANES,) + plane] * 4
         + [(8, LANES)]
         + [y_shape] * 2,
         (couplings, diagonal, wells, ids, fxl, fxh, *came_y, parts, *ahead),
-        [held(IMAGE_PLANES, *plane)] * 2,
+        [held(IMAGE_PLANES, *plane)] * 4,
     )
     faces = (fxl, fxh, fyl, fyh)
-    came_x = swapped(x_first, x_second, "gx")
+    came_x, came_y = swapped(*packs[:2], "gx"), swapped(*packs[2:], "gy")
     (part,) = call(
         moments_kernel,
         [chunks],
@@ -885,29 +889,25 @@
         cost=4 << 20,
         out=1,
     )
-    parts = exchanged(after(part, *came_x))
-    y_shape = (IMAGE_PLANES + 2,) + plane
-    y_first, y_second, gxl, gxh = call(
-        image_corner_kernel,
-        [y_shape] * 2 + [(IMAGE_PLANES,) + plane] * 2,
-        (y_low, y_high, *came_x),
-        [held(*y_shape)] * 2,
-    )
-    came_y = swapped(y_first, y_second, "gy")
-
+    parts = exchanged(part)
     second, third, part, known = call(
         krylov_kernel,
         [field, field, (devices, 1, (RHS + 1) * LANES), (4 * RHS, LANES)],
-        (couplings, diagonal, wells, ids) + faces + (gxl, gxh, *came_y)
+        (couplings, diagonal, wells, ids) + faces + (*came_x, *came_y)
         + (residual, image, residual_faces, parts, small, present),
         [held(12, WELLS, LANES), held(12, *block), held(10, *plane)]
-        + [held(*y_shape)] * 2,
+        + [held(IMAGE_PLANES, *plane)] * 4,
     )
     parts = exchanged(part)
     (result,) = call(
         solve_kernel,
         [field],
-        (guess, residual, second, third, parts, known),
+        (
+            pltpu.with_memory_space_constraint(guess, pltpu.HBM),
+            residual, second, third, parts, known,
+        ),
+        [held(*field), pltpu.SemaphoreType.DMA((1,))],
+        far_inputs=1,
     )
     return result
 

time: 62.8 us -> 59.9 us (0.954)
  local copies, waits for them, and re-layouts: 3.08 us -> 0.02 us
  waiting for transfers between devices: 10.3 us -> 11.8 us
  blocking collectives: 10.7 us -> 12 us
  Pallas kernels: 14.1 us -> 12.8 us
  starting transfers between devices: 24 us -> 22.9 us
    ppermute x8, waiting for transfers between devices: 0.96 us -> 5.53 us  [swapped(): lax.ppermute(value, axis, pairs)]
    unnamed x28 -> x12, local copies, waits for them, and re-layouts: 3.08 us -> 0.02 us
    all_to_all x2, waiting for transfers between devices: 9.32 us -> 6.31 us  [exchanged(): return lax.all_to_all(part, ('gx', 'gy'), 0, 0, tiled=True)]
    all_to_all x2, starting transfers between devices: 14 us -> 12 us  [exchanged(): return lax.all_to_all(part, ('gx', 'gy'), 0, 0, tiled=True)]
    pallas_call x9 -> x8, Pallas kernels: 14.1 us -> 12.8 us  [call(): pl.pallas_call(kernel, out_shape=outs, in_specs=[place(*numbered) for num...]
    all_to_all x1, blocking collectives: 10.7 us -> 12 us  [exchanged(): return lax.all_to_all(part, ('gx', 'gy'), 0, 0, tiled=True)]
    ppermute x8, starting transfers between devices: 9.95 us -> 10.8 us  [swapped(): lax.ppermute(value, axis, pairs)]
  transfers between devices with their start and end apart: 10 -> 10, of which waited for: 4 -> 5; matrix products, arithmetic and copies ran while one was open for 0% -> 0% of each run, Pallas kernels for 10% -> 5%
where the time goes in v16:
time: 59.9 us; the launch traced here: 59.7 us
  starting transfers between devices  22.9 us (38%)
  Pallas kernels  12.8 us (21%)
  blocking collectives  12 us (20%)
  waiting for transfers between devices  11.8 us (20%)
    pallas_call x8, Pallas kernels, call(): pl.pallas_call(kernel, out_shape=outs, in_specs=[place(*numbered) for num...  12.8 us
    all_to_all x2, starting transfers between devices, exchanged(): return lax.all_to_all(part, ('gx', 'gy'), 0, 0, tiled=True)  12 us
    all_to_all x1, blocking collectives, exchanged(): return lax.all_to_all(part, ('gx', 'gy'), 0, 0, tiled=True)  12 us
    ppermute x8, starting transfers between devices, swapped(): lax.ppermute(value, axis, pairs)  10.8 us
    all_to_all x2, waiting for transfers between devices, exchanged(): return lax.all_to_all(part, ('gx', 'gy'), 0, 0, tiled=True)  6.31 us
    ppermute x8, waiting for transfers between devices, swapped(): lax.ppermute(value, axis, pairs)  5.53 us
  transfers between devices with their start and end apart: 10, of which 5 were waited for; matrix products, arithmetic and copies ran while one was open for 0% of the time, Pallas kernels for 5%

profile of v16, /device:TPU:0, one launch (start us, length us, event | category | flops | bytes accessed | tf_op | source)
XLA Modules:
  0.0 59.7 jit_solution(12506181528205172578)
XLA Ops:
  0.0 0.0 copy-start.5
  0.0 0.0 copy-start.3
  0.0 0.0 copy-start.2
  0.0 0.0 copy-start
  0.0 0.0 copy-start.1
  0.0 0.0 copy-start.4
  0.0 1.5 %shard_map.65 = (f32[37,8,128]{2,1,0:T(8,128)S(1)}, f32[37,8,128]{2,1,0:T(8,128)S(1)}) custom-call(f32[6,4,8,8,128]{4,3,2,1,0:T(8,128)} %couplings.7, f32[4,8,8,128]{3,2,1,0:T(8,128)} %diagonal.7, f32[4,8,8,128]{3,2,1,0:T(8,128)} %wells.7, s32[8,8,128]{2,1,0:T(8,128)} %ids.7, f32[4,2,8,8,128]{4,3,2,1,0:T(8,128)} %right.3, f32[4,2,8,8,128]{4,3,2,1,0:T(8,128)} %guess_in.1), custom_call_target="tpu_custom_call" | custom-call | tf_op jit(solution)/shard_map/pallas_call | solution.py:778
  1.6 3.1 %collective-permute-start = (f32[37,8,128]{2,1,0:T(8,128)S(1)}, f32[37,8,128]{2,1,0:T(8,128)S(1)}, u32[]{:S(2)}, u32[]{:S(2)}) collective-permute-start(f32[37,8,128]{2,1,0:T(8,128)S(1)} %get-tuple-element.33), channel_id=1, source_target_pairs={{0,8},{8,0},{16,24},{24,16},{1,9},{9,1},{17,25},{25,17},{2,10},{10... | collective-permute-start | bytes 454664 | tf_op jit(solution)/shard_map/ppermute | solution.py:818
  4.7 0.7 %collective-permute-start.1 = (f32[37,8,128]{2,1,0:T(8,128)S(1)}, f32[37,8,128]{2,1,0:T(8,128)S(1)}, u32[]{:S(2)}, u32[]{:S(2)}) collective-permute-start(f32[37,8,128]{2,1,0:T(8,128)S(1)} %get-tuple-element.34), channel_id=1, source_target_pairs={{8,16},{16,8},{9,17},{17,9},{10,18},{18,10},{11,19},{19,11},{12,20... | collective-permute-start | bytes 454664 | tf_op jit(solution)/shard_map/ppermute | solution.py:818
  5.3 0.0 copy-done.5
  5.3 0.0 copy-done.3
  5.4 0.0 copy-done.2
  5.4 0.0 copy-done
  5.4 0.0 copy-done.1
  5.4 0.0 copy-done.4
  5.4 2.5 %shard_map.64 = (f32[32,6,128]{2,1,0:T(8,128)}, s32[48]{0:T(128)S(1)}, f32[36,8,128]{2,1,0:T(8,128)S(1)}, f32[36,8,128]{2,1,0:T(8,128)S(1)}) custom-call(f32[6,4,8,8,128]{4,3,2,1,0:T(8,128)S(1)} %copy-done, f32[4,8,8,128]{3,2,1,0:T(8,128)S(1)} %copy-done.2, f32[4,8,8,128]{3,2,1,0:T(8,128)S(1)} %copy-done.3, s32[8,8,128]{2,1,0:T(8,128)S(1)} %copy-done.5, ...), custom_call_target="tpu_custom_call" | custom-call | flops 4194304 | bytes 4194304 | tf_op jit(solution)/shard_map/pallas_call | solution.py:778
  7.9 0.7 %collective-permute-done.came_first.rest_0_ = f32[37,8,128]{2,1,0:T(8,128)S(1)} collective-permute-done((f32[37,8,128]{2,1,0:T(8,128)S(1)}, f32[37,8,128]{2,1,0:T(8,128)S(1)}, u32[]{:S(2)}, u32[]{:S(2)}) %collective-permute-start) | collective-permute-done | bytes 151584 | tf_op jit(solution)/shard_map/ppermute | solution.py:818
  8.6 6.2 %all-to-all-start = ((f32[32,6,128]{2,1,0:T(8,128)}), f32[32,6,128]{2,1,0:T(8,128)S(1)}, u32[]{:S(2)}, u32[]{:S(2)}) async-start(f32[32,6,128]{2,1,0:T(8,128)} %shard_map.67), calls=%async_computation | async-start | bytes 262144 | tf_op jit(solution)/shard_map/all_to_all | solution.py:823
  14.8 0.0 collective-permute-done.1.came_second
  14.8 0.1 shard_map.66
  14.9 0.7 %collective-permute-start.3 = (f32[41,8,128]{2,1,0:T(8,128)S(1)}, f32[41,8,128]{2,1,0:T(8,128)S(1)}, u32[]{:S(2)}, u32[]{:S(2)}) collective-permute-start(f32[41,8,128]{2,1,0:T(8,128)S(1)} %get-tuple-element.38), channel_id=1, source_target_pairs={{1,2},{2,1},{3,4},{4,3},{5,6},{6,5},{9,10},{10,9},{11,12},{12,11},... | collective-permute-start | bytes 503816 | tf_op jit(solution)/shard_map/ppermute | solution.py:818
  15.6 3.2 %collective-permute-start.2 = (f32[41,8,128]{2,1,0:T(8,128)S(1)}, f32[41,8,128]{2,1,0:T(8,128)S(1)}, u32[]{:S(2)}, u32[]{:S(2)}) collective-permute-start(f32[41,8,128]{2,1,0:T(8,128)S(1)} %get-tuple-element.37.sent_face), channel_id=1, source_target_pairs={{0,1},{1,0},{2,3},{3,2},{4,5},{5,4},{6,7},{7,6},{8,9},{9,8},{10,11... | collective-permute-start | bytes 503816 | tf_op jit(solution)/shard_map/ppermute | solution.py:818
  18.8 0.3 shard_map.68
  19.1 0.0 collective-permute-done.3.came_second
  19.1 0.7 %collective-permute-done.2.came_first = f32[41,8,128]{2,1,0:T(8,128)S(1)} collective-permute-done((f32[41,8,128]{2,1,0:T(8,128)S(1)}, f32[41,8,128]{2,1,0:T(8,128)S(1)}, u32[]{:S(2)}, u32[]{:S(2)}) %collective-permute-start.2) | collective-permute-done | bytes 167968 | tf_op jit(solution)/shard_map/ppermute | solution.py:818
  19.8 3.2 %all-to-all-done.parts = f32[32,6,128]{2,1,0:T(8,128)S(1)} async-done(((f32[32,6,128]{2,1,0:T(8,128)}), f32[32,6,128]{2,1,0:T(8,128)S(1)}, u32[]{:S(2)}, u32[]{:S(2)}) %all-to-all-start) | async-done | bytes 98336 | tf_op jit(solution)/shard_map/all_to_all | solution.py:823
  23.0 1.4 %shard_map.69 = (f32[4,2,8,8,128]{4,3,2,1,0:T(8,128)S(1)}, f32[4,2,8,8,128]{4,3,2,1,0:T(8,128)S(1)}, f32[4,8,8,128]{3,2,1,0:T(8,128)S(1)}, f32[16,8,128]{2,1,0:T...) custom-call(f32[6,4,8,8,128]{4,3,2,1,0:T(8,128)S(1)} %copy-done, ...), custom_call_target="tpu_custom_call" | custom-call | tf_op jit(solution)/shard_map/pallas_call | solution.py:778
  24.5 2.0 %shard_map.70 = f32[32,16,128]{2,1,0:T(8,128)} custom-call(f32[4,8,8,128]{3,2,1,0:T(8,128)S(1)} %copy-done.3, s32[8,8,128]{2,1,0:T(8,128)S(1)} %copy-done.5, f32[4,2,8,8,128]{4,3,2,1,0:T(8,128)S(1)} %get-tuple-element.42.residual, f32[4,2,8,8,128]{4,3,2,1,0:T(8,128)S(1)} %get-tuple-element.49.image, s32[48]{0:T(128)S(1)} %get-tuple-element.51.present), custom_call_target="tpu_custom_call" | custom-call | flops 4194304 | bytes 4194304 | tf_op jit(solution)/shard_map/pallas_call | solution.py:778
  26.5 5.8 %all-to-all-start.1 = ((f32[32,16,128]{2,1,0:T(8,128)}), f32[32,16,128]{2,1,0:T(8,128)S(1)}, u32[]{:S(2)}, u32[]{:S(2)}) async-start(f32[32,16,128]{2,1,0:T(8,128)} %shard_map.70), calls=%async_computation.1 | async-start | bytes 524288 | tf_op jit(solution)/shard_map/all_to_all | solution.py:823
  32.3 1.8 %collective-permute-start.4 = (f32[16,8,128]{2,1,0:T(8,128)S(1)}, f32[16,8,128]{2,1,0:T(8,128)S(1)}, u32[]{:S(2)}, u32[]{:S(2)}) collective-permute-start(f32[16,8,128]{2,1,0:T(8,128)S(1)} %get-tuple-element.45), channel_id=1, source_target_pairs={{0,8},{8,0},{16,24},{24,16},{1,9},{9,1},{17,25},{25,17},{2,10},{10... | collective-permute-start | bytes 196616 | tf_op jit(solution)/shard_map/ppermute | solution.py:818
  34.2 0.7 %collective-permute-start.5 = (f32[16,8,128]{2,1,0:T(8,128)S(1)}, f32[16,8,128]{2,1,0:T(8,128)S(1)}, u32[]{:S(2)}, u32[]{:S(2)}) collective-permute-start(f32[16,8,128]{2,1,0:T(8,128)S(1)} %get-tuple-element.46), channel_id=1, source_target_pairs={{8,16},{16,8},{9,17},{17,9},{10,18},{18,10},{11,19},{19,11},{12,20... | collective-permute-start | bytes 196616 | tf_op jit(solution)/shard_map/ppermute | solution.py:818
  34.8 0.1 collective-permute-start.6
  34.9 0.7 %collective-permute-start.7 = (f32[16,8,128]{2,1,0:T(8,128)S(1)}, f32[16,8,128]{2,1,0:T(8,128)S(1)}, u32[]{:S(2)}, u32[]{:S(2)}) collective-permute-start(f32[16,8,128]{2,1,0:T(8,128)S(1)} %get-tuple-element.48), channel_id=1, source_target_pairs={{1,2},{2,1},{3,4},{4,3},{5,6},{6,5},{9,10},{10,9},{11,12},{12,11},... | collective-permute-start | bytes 196616 | tf_op jit(solution)/shard_map/ppermute | solution.py:818
  35.6 4.2 %collective-permute-done.4.x_first = f32[16,8,128]{2,1,0:T(8,128)S(1)} collective-permute-done((f32[16,8,128]{2,1,0:T(8,128)S(1)}, f32[16,8,128]{2,1,0:T(8,128)S(1)}, u32[]{:S(2)}, u32[]{:S(2)}) %collective-permute-start.4) | collective-permute-done | bytes 65568 | tf_op jit(solution)/shard_map/ppermute | solution.py:818
  39.8 0.0 collective-permute-done.5.x_second
  39.8 0.0 collective-permute-done.6.y_first
  39.8 0.0 collective-permute-done.7.y_second
  39.8 3.1 %all-to-all-done.1.parts = f32[32,16,128]{2,1,0:T(8,128)S(1)} async-done(((f32[32,16,128]{2,1,0:T(8,128)}), f32[32,16,128]{2,1,0:T(8,128)S(1)}, u32[]{:S(2)}, u32[]{:S(2)}) %all-to-all-start.1) | async-done | bytes 262176 | tf_op jit(solution)/shard_map/all_to_all | solution.py:823
  42.9 3.0 %shard_map.71 = (f32[4,2,8,8,128]{4,3,2,1,0:T(8,128)S(1)}, f32[4,2,8,8,128]{4,3,2,1,0:T(8,128)S(1)}, f32[32,1,640]{2,1,0:T(1,128)S(1)}, f32[16,128]{1,0:T(8,128)S(1)}) custom-call(f32[6,4,8,8,128]{4,3,2,1,0:T(8,128)S(1)} %copy-done, f32[4,8,8,128]{3,2,1,0:T(8,128)S(1)} %copy-done.2, f32[4,8,8,128]{3,2,1,0:T(8,128)S(1)} %copy-done.3, ...), custom_call_target="tpu_custom_call" | custom-call | tf_op jit(solution)/shard_map/pallas_call | solution.py:778
  45.8 12.0 %all_to_all.15.parts = f32[32,1,640]{2,1,0:T(1,128)S(1)} all-to-all(f32[32,1,640]{2,1,0:T(1,128)S(1)} %get-tuple-element.55), channel_id=1, replica_groups=mesh['member'=1,'gx'=4,'gy'=8] {'gx','gy'}, dimensions={0} | all-to-all | bytes 163840 | tf_op jit(solution)/shard_map/all_to_all | solution.py:823
  57.8 1.9 %shard_map.72 = f32[4,2,8,8,128]{4,3,2,1,0:T(8,128)} custom-call(f32[4,2,8,8,128]{4,3,2,1,0:T(8,128)} %guess_in.1, f32[4,2,8,8,128]{4,3,2,1,0:T(8,128)S(1)} %get-tuple-element.42.residual, f32[4,2,8,8,128]{4,3,2,1,0:T(8,128)S(1)} %get-tuple-element.53.second, f32[4,2,8,8,128]{4,3,2,1,0:T(8,128)S(1)} %get-tuple-element.54.third, ...), custom_call_target="tpu_custom_call" | custom-call | tf_op jit(solution)/shard_map/pallas_call | solution.py:778
  (1 shorter events, 0.0 us)
Async XLA Ops:
  0.0 5.3 %copy-start.5 = (s32[8,8,128]{2,1,0:T(8,128)S(1)}, s32[8,8,128]{2,1,0:T(8,128)}, u32[]{:S(2)}) copy-start(s32[8,8,128]{2,1,0:T(8,128)} %ids.7) | copy-start | bytes 98308
  0.0 5.3 %copy-start.3 = (f32[4,8,8,128]{3,2,1,0:T(8,128)S(1)}, f32[4,8,8,128]{3,2,1,0:T(8,128)}, u32[]{:S(2)}) copy-start(f32[4,8,8,128]{3,2,1,0:T(8,128)} %wells.7) | copy-start | bytes 393220
  0.0 5.4 %copy-start.2 = (f32[4,8,8,128]{3,2,1,0:T(8,128)S(1)}, f32[4,8,8,128]{3,2,1,0:T(8,128)}, u32[]{:S(2)}) copy-start(f32[4,8,8,128]{3,2,1,0:T(8,128)} %diagonal.7) | copy-start | bytes 393220
  0.0 5.4 %copy-start = (f32[6,4,8,8,128]{4,3,2,1,0:T(8,128)S(1)}, f32[6,4,8,8,128]{4,3,2,1,0:T(8,128)}, u32[]{:S(2)}) copy-start(f32[6,4,8,8,128]{4,3,2,1,0:T(8,128)} %couplings.7) | copy-start | bytes 2359300
  0.0 5.4 %copy-start.1 = (f32[4,2,8,8,128]{4,3,2,1,0:T(8,128)S(1)}, f32[4,2,8,8,128]{4,3,2,1,0:T(8,128)}, u32[]{:S(2)}) copy-start(f32[4,2,8,8,128]{4,3,2,1,0:T(8,128)} %guess_in.1) | copy-start | bytes 786436
  0.0 5.4 %copy-start.4 = (f32[4,2,8,8,128]{4,3,2,1,0:T(8,128)S(1)}, f32[4,2,8,8,128]{4,3,2,1,0:T(8,128)}, u32[]{:S(2)}) copy-start(f32[4,2,8,8,128]{4,3,2,1,0:T(8,128)} %right.3) | copy-start | bytes 786436
  1.6 7.0 %collective-permute-start = (f32[37,8,128]{2,1,0:T(8,128)S(1)}, f32[37,8,128]{2,1,0:T(8,128)S(1)}, u32[]{:S(2)}, u32[]{:S(2)}) collective-permute-start(f32[37,8,128]{2,1,0:T(8,128)S(1)} %get-tuple-element.33), channel_id=1, source_target_pairs={{0,8},{8,0},{16,24},{24,16},{1,9},{9,1},{17,25},{25,17},{2,10},{10... | collective-permute-start | bytes 454664 | tf_op jit(solution)/shard_map/ppermute | solution.py:818
  4.7 10.1 %collective-permute-start.1 = (f32[37,8,128]{2,1,0:T(8,128)S(1)}, f32[37,8,128]{2,1,0:T(8,128)S(1)}, u32[]{:S(2)}, u32[]{:S(2)}) collective-permute-start(f32[37,8,128]{2,1,0:T(8,128)S(1)} %get-tuple-element.34), channel_id=1, source_target_pairs={{8,16},{16,8},{9,17},{17,9},{10,18},{18,10},{11,19},{19,11},{12,20... | collective-permute-start | bytes 454664 | tf_op jit(solution)/shard_map/ppermute | solution.py:818
  8.6 14.4 %all-to-all-start = ((f32[32,6,128]{2,1,0:T(8,128)}), f32[32,6,128]{2,1,0:T(8,128)S(1)}, u32[]{:S(2)}, u32[]{:S(2)}) async-start(f32[32,6,128]{2,1,0:T(8,128)} %shard_map.67), calls=%async_computation | async-start | bytes 262144 | tf_op jit(solution)/shard_map/all_to_all | solution.py:823
  14.9 4.2 %collective-permute-start.3 = (f32[41,8,128]{2,1,0:T(8,128)S(1)}, f32[41,8,128]{2,1,0:T(8,128)S(1)}, u32[]{:S(2)}, u32[]{:S(2)}) collective-permute-start(f32[41,8,128]{2,1,0:T(8,128)S(1)} %get-tuple-element.38), channel_id=1, source_target_pairs={{1,2},{2,1},{3,4},{4,3},{5,6},{6,5},{9,10},{10,9},{11,12},{12,11},... | collective-permute-start | bytes 503816 | tf_op jit(solution)/shard_map/ppermute | solution.py:818
  15.6 4.2 %collective-permute-start.2 = (f32[41,8,128]{2,1,0:T(8,128)S(1)}, f32[41,8,128]{2,1,0:T(8,128)S(1)}, u32[]{:S(2)}, u32[]{:S(2)}) collective-permute-start(f32[41,8,128]{2,1,0:T(8,128)S(1)} %get-tuple-element.37.sent_face), channel_id=1, source_target_pairs={{0,1},{1,0},{2,3},{3,2},{4,5},{5,4},{6,7},{7,6},{8,9},{9,8},{10,11... | collective-permute-start | bytes 503816 | tf_op jit(solution)/shard_map/ppermute | solution.py:818
  26.5 16.4 %all-to-all-start.1 = ((f32[32,16,128]{2,1,0:T(8,128)}), f32[32,16,128]{2,1,0:T(8,128)S(1)}, u32[]{:S(2)}, u32[]{:S(2)}) async-start(f32[32,16,128]{2,1,0:T(8,128)} %shard_map.70), calls=%async_computation.1 | async-start | bytes 524288 | tf_op jit(solution)/shard_map/all_to_all | solution.py:823
  32.3 7.4 %collective-permute-start.4 = (f32[16,8,128]{2,1,0:T(8,128)S(1)}, f32[16,8,128]{2,1,0:T(8,128)S(1)}, u32[]{:S(2)}, u32[]{:S(2)}) collective-permute-start(f32[16,8,128]{2,1,0:T(8,128)S(1)} %get-tuple-element.45), channel_id=1, source_target_pairs={{0,8},{8,0},{16,24},{24,16},{1,9},{9,1},{17,25},{25,17},{2,10},{10... | collective-permute-start | bytes 196616 | tf_op jit(solution)/shard_map/ppermute | solution.py:818
  34.2 5.6 %collective-permute-start.5 = (f32[16,8,128]{2,1,0:T(8,128)S(1)}, f32[16,8,128]{2,1,0:T(8,128)S(1)}, u32[]{:S(2)}, u32[]{:S(2)}) collective-permute-start(f32[16,8,128]{2,1,0:T(8,128)S(1)} %get-tuple-element.46), channel_id=1, source_target_pairs={{8,16},{16,8},{9,17},{17,9},{10,18},{18,10},{11,19},{19,11},{12,20... | collective-permute-start | bytes 196616 | tf_op jit(solution)/shard_map/ppermute | solution.py:818
  34.8 4.9 %collective-permute-start.6 = (f32[16,8,128]{2,1,0:T(8,128)S(1)}, f32[16,8,128]{2,1,0:T(8,128)S(1)}, u32[]{:S(2)}, u32[]{:S(2)}) collective-permute-start(f32[16,8,128]{2,1,0:T(8,128)S(1)} %get-tuple-element.47), channel_id=1, source_target_pairs={{0,1},{1,0},{2,3},{3,2},{4,5},{5,4},{6,7},{7,6},{8,9},{9,8},{10,11... | collective-permute-start | bytes 196616 | tf_op jit(solution)/shard_map/ppermute | solution.py:818
  34.9 4.8 %collective-permute-start.7 = (f32[16,8,128]{2,1,0:T(8,128)S(1)}, f32[16,8,128]{2,1,0:T(8,128)S(1)}, u32[]{:S(2)}, u32[]{:S(2)}) collective-permute-start(f32[16,8,128]{2,1,0:T(8,128)S(1)} %get-tuple-element.48), channel_id=1, source_target_pairs={{1,2},{2,1},{3,4},{4,3},{5,6},{6,5},{9,10},{10,9},{11,12},{12,11},... | collective-permute-start | bytes 196616 | tf_op jit(solution)/shard_map/ppermute | solution.py:818

commit v17 on v16

--- a/solution.py
+++ b/solution.py
@@ -809,14 +809,15 @@
     return pltpu.VMEM(shape, jnp.float32)
 
 
+def swap(value, axis, start):
+    pairs = []
+    for low in range(start, lax.axis_size(axis) - 1, 2):
+        pairs += [(low, low + 1), (low + 1, low)]
+    return lax.ppermute(value, axis, pairs) if pairs else jnp.zeros_like(value)
+
+
 def swapped(first, second, axis):
-    results = []
-    for start, value in enumerate((first, second)):
-        pairs = []
-        for low in range(start, lax.axis_size(axis) - 1, 2):
-            pairs += [(low, low + 1), (low + 1, low)]
-        results.append(lax.ppermute(value, axis, pairs) if pairs else jnp.zeros_like(value))
-    return results
+    return swap(first, axis, 0), swap(second, axis, 1)
 
 
 def exchanged(part):
@@ -880,7 +881,10 @@
         [held(IMAGE_PLANES, *plane)] * 4,
     )
     faces = (fxl, fxh, fyl, fyh)
-    came_x, came_y = swapped(*packs[:2], "gx"), swapped(*packs[2:], "gy")
+    came_y1 = swap(packs[3], "gy", 1)
+    came_x1 = swap(packs[1], "gx", 1)
+    came_x0 = swap(packs[0], "gx", 0)
+    came_y0 = swap(packs[2], "gy", 0)
     (part,) = call(
         moments_kernel,
         [chunks],
@@ -893,7 +897,7 @@
     second, third, part, known = call(
         krylov_kernel,
         [field, field, (devices, 1, (RHS + 1) * LANES), (4 * RHS, LANES)],
-        (couplings, diagonal, wells, ids) + faces + (*came_x, *came_y)
+        (couplings, diagonal, wells, ids) + faces + (came_x0, came_x1, came_y0, came_y1)
         + (residual, image, residual_faces, parts, small, present),
         [held(12, WELLS, LANES), held(12, *block), held(10, *plane)]
         + [held(IMAGE_PLANES, *plane)] * 4,

time: 59.9 us -> 59.7 us (level)
  starting transfers between devices: 22.9 us -> 22.3 us
where the time goes in v17:
time: 59.7 us; the launch traced here: 59.3 us
  starting transfers between devices  22.3 us (37%)
  Pallas kernels  13.3 us (22%)
  blocking collectives  11.8 us (20%)
  waiting for transfers between devices  11.6 us (19%)
    pallas_call x8, Pallas kernels, call(): pl.pallas_call(kernel, out_shape=outs, in_specs=[place(*numbered) for num...  13.3 us
    all_to_all x1, blocking collectives, exchanged(): return lax.all_to_all(part, ('gx', 'gy'), 0, 0, tiled=True)  11.8 us
    all_to_all x2, starting transfers between devices, exchanged(): return lax.all_to_all(part, ('gx', 'gy'), 0, 0, tiled=True)  11.4 us
    ppermute x8, starting transfers between devices, swap(): return lax.ppermute(value, axis, pairs) if pairs else jnp.zeros_like(value)  10.8 us
    all_to_all x2, waiting for transfers between devices, exchanged(): return lax.all_to_all(part, ('gx', 'gy'), 0, 0, tiled=True)  6.31 us
    ppermute x8, waiting for transfers between devices, swap(): return lax.ppermute(value, axis, pairs) if pairs else jnp.zeros_like(value)  5.3 us
  transfers between devices with their start and end apart: 10, of which 5 were waited for; matrix products, arithmetic and copies ran while one was open for 0% of the time, Pallas kernels for 5%

profile of v17, /device:TPU:0, one launch (start us, length us, event | category | flops | bytes accessed | tf_op | source)
XLA Modules:
  0.0 59.3 jit_solution(12506181528205172578)
XLA Ops:
  0.0 0.0 copy-start.5
  0.0 0.0 copy-start.3
  0.0 0.0 copy-start.2
  0.0 0.0 copy-start
  0.0 0.0 copy-start.1
  0.0 0.0 copy-start.4
  0.0 1.5 %shard_map.65 = (f32[37,8,128]{2,1,0:T(8,128)S(1)}, f32[37,8,128]{2,1,0:T(8,128)S(1)}) custom-call(f32[6,4,8,8,128]{4,3,2,1,0:T(8,128)} %couplings.7, f32[4,8,8,128]{3,2,1,0:T(8,128)} %diagonal.7, f32[4,8,8,128]{3,2,1,0:T(8,128)} %wells.7, s32[8,8,128]{2,1,0:T(8,128)} %ids.7, f32[4,2,8,8,128]{4,3,2,1,0:T(8,128)} %right.3, f32[4,2,8,8,128]{4,3,2,1,0:T(8,128)} %guess_in.1), custom_call_target="tpu_custom_call" | custom-call | tf_op jit(solution)/shard_map/pallas_call | solution.py:778
  1.6 3.1 %collective-permute-start = (f32[37,8,128]{2,1,0:T(8,128)S(1)}, f32[37,8,128]{2,1,0:T(8,128)S(1)}, u32[]{:S(2)}, u32[]{:S(2)}) collective-permute-start(f32[37,8,128]{2,1,0:T(8,128)S(1)} %get-tuple-element.33), channel_id=1, source_target_pairs={{0,8},{8,0},{16,24},{24,16},{1,9},{9,1},{17,25},{25,17},{2,10},{10... | collective-permute-start | bytes 454664 | tf_op jit(solution)/shard_map/ppermute | solution.py:816
  4.7 0.7 %collective-permute-start.1 = (f32[37,8,128]{2,1,0:T(8,128)S(1)}, f32[37,8,128]{2,1,0:T(8,128)S(1)}, u32[]{:S(2)}, u32[]{:S(2)}) collective-permute-start(f32[37,8,128]{2,1,0:T(8,128)S(1)} %get-tuple-element.34), channel_id=1, source_target_pairs={{8,16},{16,8},{9,17},{17,9},{10,18},{18,10},{11,19},{19,11},{12,20... | collective-permute-start | bytes 454664 | tf_op jit(solution)/shard_map/ppermute | solution.py:816
  5.3 0.0 copy-done.5
  5.3 0.0 copy-done.3
  5.4 0.0 copy-done.2
  5.4 0.0 copy-done
  5.4 0.0 copy-done.1
  5.4 0.0 copy-done.4
  5.4 2.8 %shard_map.64 = (f32[32,6,128]{2,1,0:T(8,128)}, s32[48]{0:T(128)S(1)}, f32[36,8,128]{2,1,0:T(8,128)S(1)}, f32[36,8,128]{2,1,0:T(8,128)S(1)}) custom-call(f32[6,4,8,8,128]{4,3,2,1,0:T(8,128)S(1)} %copy-done, f32[4,8,8,128]{3,2,1,0:T(8,128)S(1)} %copy-done.2, f32[4,8,8,128]{3,2,1,0:T(8,128)S(1)} %copy-done.3, s32[8,8,128]{2,1,0:T(8,128)S(1)} %copy-done.5, ...), custom_call_target="tpu_custom_call" | custom-call | flops 4194304 | bytes 4194304 | tf_op jit(solution)/shard_map/pallas_call | solution.py:778
  8.2 0.4 collective-permute-done.came_first.rest_0_
  8.6 6.0 %all-to-all-start = ((f32[32,6,128]{2,1,0:T(8,128)}), f32[32,6,128]{2,1,0:T(8,128)S(1)}, u32[]{:S(2)}, u32[]{:S(2)}) async-start(f32[32,6,128]{2,1,0:T(8,128)} %shard_map.67), calls=%async_computation | async-start | bytes 262144 | tf_op jit(solution)/shard_map/all_to_all | solution.py:824
  14.6 0.0 collective-permute-done.1.came_second
  14.6 0.1 shard_map.66
  14.8 0.7 %collective-permute-start.3 = (f32[41,8,128]{2,1,0:T(8,128)S(1)}, f32[41,8,128]{2,1,0:T(8,128)S(1)}, u32[]{:S(2)}, u32[]{:S(2)}) collective-permute-start(f32[41,8,128]{2,1,0:T(8,128)S(1)} %get-tuple-element.38), channel_id=1, source_target_pairs={{1,2},{2,1},{3,4},{4,3},{5,6},{6,5},{9,10},{10,9},{11,12},{12,11},... | collective-permute-start | bytes 503816 | tf_op jit(solution)/shard_map/ppermute | solution.py:816
  15.4 3.2 %collective-permute-start.2 = (f32[41,8,128]{2,1,0:T(8,128)S(1)}, f32[41,8,128]{2,1,0:T(8,128)S(1)}, u32[]{:S(2)}, u32[]{:S(2)}) collective-permute-start(f32[41,8,128]{2,1,0:T(8,128)S(1)} %get-tuple-element.37.sent_face), channel_id=1, source_target_pairs={{0,1},{1,0},{2,3},{3,2},{4,5},{5,4},{6,7},{7,6},{8,9},{9,8},{10,11... | collective-permute-start | bytes 503816 | tf_op jit(solution)/shard_map/ppermute | solution.py:816
  18.6 0.3 shard_map.68
  18.9 0.0 collective-permute-done.3.came_second
  19.0 0.7 %collective-permute-done.2.came_first = f32[41,8,128]{2,1,0:T(8,128)S(1)} collective-permute-done((f32[41,8,128]{2,1,0:T(8,128)S(1)}, f32[41,8,128]{2,1,0:T(8,128)S(1)}, u32[]{:S(2)}, u32[]{:S(2)}) %collective-permute-start.2) | collective-permute-done | bytes 167968 | tf_op jit(solution)/shard_map/ppermute | solution.py:816
  19.7 3.2 %all-to-all-done.parts = f32[32,6,128]{2,1,0:T(8,128)S(1)} async-done(((f32[32,6,128]{2,1,0:T(8,128)}), f32[32,6,128]{2,1,0:T(8,128)S(1)}, u32[]{:S(2)}, u32[]{:S(2)}) %all-to-all-start) | async-done | bytes 98336 | tf_op jit(solution)/shard_map/all_to_all | solution.py:824
  22.9 1.4 %shard_map.69 = (f32[4,2,8,8,128]{4,3,2,1,0:T(8,128)S(1)}, f32[4,2,8,8,128]{4,3,2,1,0:T(8,128)S(1)}, f32[4,8,8,128]{3,2,1,0:T(8,128)S(1)}, f32[16,8,128]{2,1,0:T...) custom-call(f32[6,4,8,8,128]{4,3,2,1,0:T(8,128)S(1)} %copy-done, ...), custom_call_target="tpu_custom_call" | custom-call | tf_op jit(solution)/shard_map/pallas_call | solution.py:778
  24.3 2.2 %shard_map.70 = f32[32,16,128]{2,1,0:T(8,128)} custom-call(f32[4,8,8,128]{3,2,1,0:T(8,128)S(1)} %copy-done.3, s32[8,8,128]{2,1,0:T(8,128)S(1)} %copy-done.5, f32[4,2,8,8,128]{4,3,2,1,0:T(8,128)S(1)} %get-tuple-element.42.residual, f32[4,2,8,8,128]{4,3,2,1,0:T(8,128)S(1)} %get-tuple-element.49.image, s32[48]{0:T(128)S(1)} %get-tuple-element.51.present), custom_call_target="tpu_custom_call" | custom-call | flops 4194304 | bytes 4194304 | tf_op jit(solution)/shard_map/pallas_call | solution.py:778
  26.5 5.4 %all-to-all-start.1 = ((f32[32,16,128]{2,1,0:T(8,128)}), f32[32,16,128]{2,1,0:T(8,128)S(1)}, u32[]{:S(2)}, u32[]{:S(2)}) async-start(f32[32,16,128]{2,1,0:T(8,128)} %shard_map.70), calls=%async_computation.1 | async-start | bytes 524288 | tf_op jit(solution)/shard_map/all_to_all | solution.py:824
  31.9 1.8 %collective-permute-start.4 = (f32[16,8,128]{2,1,0:T(8,128)S(1)}, f32[16,8,128]{2,1,0:T(8,128)S(1)}, u32[]{:S(2)}, u32[]{:S(2)}) collective-permute-start(f32[16,8,128]{2,1,0:T(8,128)S(1)} %get-tuple-element.45), channel_id=1, source_target_pairs={{0,8},{8,0},{16,24},{24,16},{1,9},{9,1},{17,25},{25,17},{2,10},{10... | collective-permute-start | bytes 196616 | tf_op jit(solution)/shard_map/ppermute | solution.py:816
  33.8 0.7 %collective-permute-start.5 = (f32[16,8,128]{2,1,0:T(8,128)S(1)}, f32[16,8,128]{2,1,0:T(8,128)S(1)}, u32[]{:S(2)}, u32[]{:S(2)}) collective-permute-start(f32[16,8,128]{2,1,0:T(8,128)S(1)} %get-tuple-element.46), channel_id=1, source_target_pairs={{8,16},{16,8},{9,17},{17,9},{10,18},{18,10},{11,19},{19,11},{12,20... | collective-permute-start | bytes 196616 | tf_op jit(solution)/shard_map/ppermute | solution.py:816
  34.4 0.1 collective-permute-start.6
  34.5 0.7 %collective-permute-start.7 = (f32[16,8,128]{2,1,0:T(8,128)S(1)}, f32[16,8,128]{2,1,0:T(8,128)S(1)}, u32[]{:S(2)}, u32[]{:S(2)}) collective-permute-start(f32[16,8,128]{2,1,0:T(8,128)S(1)} %get-tuple-element.48), channel_id=1, source_target_pairs={{1,2},{2,1},{3,4},{4,3},{5,6},{6,5},{9,10},{10,9},{11,12},{12,11},... | collective-permute-start | bytes 196616 | tf_op jit(solution)/shard_map/ppermute | solution.py:816
  35.2 4.2 %collective-permute-done.4.x_first = f32[16,8,128]{2,1,0:T(8,128)S(1)} collective-permute-done((f32[16,8,128]{2,1,0:T(8,128)S(1)}, f32[16,8,128]{2,1,0:T(8,128)S(1)}, u32[]{:S(2)}, u32[]{:S(2)}) %collective-permute-start.4) | collective-permute-done | bytes 65568 | tf_op jit(solution)/shard_map/ppermute | solution.py:816
  39.3 0.0 collective-permute-done.5.x_second
  39.3 0.0 collective-permute-done.6.y_first
  39.3 0.0 collective-permute-done.7.y_second
  39.4 3.1 %all-to-all-done.1.parts = f32[32,16,128]{2,1,0:T(8,128)S(1)} async-done(((f32[32,16,128]{2,1,0:T(8,128)}), f32[32,16,128]{2,1,0:T(8,128)S(1)}, u32[]{:S(2)}, u32[]{:S(2)}) %all-to-all-start.1) | async-done | bytes 262176 | tf_op jit(solution)/shard_map/all_to_all | solution.py:824
  42.5 3.1 %shard_map.71 = (f32[4,2,8,8,128]{4,3,2,1,0:T(8,128)S(1)}, f32[4,2,8,8,128]{4,3,2,1,0:T(8,128)S(1)}, f32[32,1,640]{2,1,0:T(1,128)S(1)}, f32[16,128]{1,0:T(8,128)S(1)}) custom-call(f32[6,4,8,8,128]{4,3,2,1,0:T(8,128)S(1)} %copy-done, f32[4,8,8,128]{3,2,1,0:T(8,128)S(1)} %copy-done.2, f32[4,8,8,128]{3,2,1,0:T(8,128)S(1)} %copy-done.3, ...), custom_call_target="tpu_custom_call" | custom-call | tf_op jit(solution)/shard_map/pallas_call | solution.py:778
  45.6 11.8 %all_to_all.15.parts = f32[32,1,640]{2,1,0:T(1,128)S(1)} all-to-all(f32[32,1,640]{2,1,0:T(1,128)S(1)} %get-tuple-element.55), channel_id=1, replica_groups=mesh['member'=1,'gx'=4,'gy'=8] {'gx','gy'}, dimensions={0} | all-to-all | bytes 163840 | tf_op jit(solution)/shard_map/all_to_all | solution.py:824
  57.4 1.9 %shard_map.72 = f32[4,2,8,8,128]{4,3,2,1,0:T(8,128)} custom-call(f32[4,2,8,8,128]{4,3,2,1,0:T(8,128)} %guess_in.1, f32[4,2,8,8,128]{4,3,2,1,0:T(8,128)S(1)} %get-tuple-element.42.residual, f32[4,2,8,8,128]{4,3,2,1,0:T(8,128)S(1)} %get-tuple-element.53.second, f32[4,2,8,8,128]{4,3,2,1,0:T(8,128)S(1)} %get-tuple-element.54.third, ...), custom_call_target="tpu_custom_call" | custom-call | tf_op jit(solution)/shard_map/pallas_call | solution.py:778
  (1 shorter events, 0.0 us)
Async XLA Ops:
  0.0 5.3 %copy-start.5 = (s32[8,8,128]{2,1,0:T(8,128)S(1)}, s32[8,8,128]{2,1,0:T(8,128)}, u32[]{:S(2)}) copy-start(s32[8,8,128]{2,1,0:T(8,128)} %ids.7) | copy-start | bytes 98308
  0.0 5.3 %copy-start.3 = (f32[4,8,8,128]{3,2,1,0:T(8,128)S(1)}, f32[4,8,8,128]{3,2,1,0:T(8,128)}, u32[]{:S(2)}) copy-start(f32[4,8,8,128]{3,2,1,0:T(8,128)} %wells.7) | copy-start | bytes 393220
  0.0 5.4 %copy-start.2 = (f32[4,8,8,128]{3,2,1,0:T(8,128)S(1)}, f32[4,8,8,128]{3,2,1,0:T(8,128)}, u32[]{:S(2)}) copy-start(f32[4,8,8,128]{3,2,1,0:T(8,128)} %diagonal.7) | copy-start | bytes 393220
  0.0 5.4 %copy-start = (f32[6,4,8,8,128]{4,3,2,1,0:T(8,128)S(1)}, f32[6,4,8,8,128]{4,3,2,1,0:T(8,128)}, u32[]{:S(2)}) copy-start(f32[6,4,8,8,128]{4,3,2,1,0:T(8,128)} %couplings.7) | copy-start | bytes 2359300
  0.0 5.4 %copy-start.1 = (f32[4,2,8,8,128]{4,3,2,1,0:T(8,128)S(1)}, f32[4,2,8,8,128]{4,3,2,1,0:T(8,128)}, u32[]{:S(2)}) copy-start(f32[4,2,8,8,128]{4,3,2,1,0:T(8,128)} %guess_in.1) | copy-start | bytes 786436
  0.0 5.4 %copy-start.4 = (f32[4,2,8,8,128]{4,3,2,1,0:T(8,128)S(1)}, f32[4,2,8,8,128]{4,3,2,1,0:T(8,128)}, u32[]{:S(2)}) copy-start(f32[4,2,8,8,128]{4,3,2,1,0:T(8,128)} %right.3) | copy-start | bytes 786436
  1.6 7.0 %collective-permute-start = (f32[37,8,128]{2,1,0:T(8,128)S(1)}, f32[37,8,128]{2,1,0:T(8,128)S(1)}, u32[]{:S(2)}, u32[]{:S(2)}) collective-permute-start(f32[37,8,128]{2,1,0:T(8,128)S(1)} %get-tuple-element.33), channel_id=1, source_target_pairs={{0,8},{8,0},{16,24},{24,16},{1,9},{9,1},{17,25},{25,17},{2,10},{10... | collective-permute-start | bytes 454664 | tf_op jit(solution)/shard_map/ppermute | solution.py:816
  4.7 10.0 %collective-permute-start.1 = (f32[37,8,128]{2,1,0:T(8,128)S(1)}, f32[37,8,128]{2,1,0:T(8,128)S(1)}, u32[]{:S(2)}, u32[]{:S(2)}) collective-permute-start(f32[37,8,128]{2,1,0:T(8,128)S(1)} %get-tuple-element.34), channel_id=1, source_target_pairs={{8,16},{16,8},{9,17},{17,9},{10,18},{18,10},{11,19},{19,11},{12,20... | collective-permute-start | bytes 454664 | tf_op jit(solution)/shard_map/ppermute | solution.py:816
  8.6 14.3 %all-to-all-start = ((f32[32,6,128]{2,1,0:T(8,128)}), f32[32,6,128]{2,1,0:T(8,128)S(1)}, u32[]{:S(2)}, u32[]{:S(2)}) async-start(f32[32,6,128]{2,1,0:T(8,128)} %shard_map.67), calls=%async_computation | async-start | bytes 262144 | tf_op jit(solution)/shard_map/all_to_all | solution.py:824
  14.8 4.2 %collective-permute-start.3 = (f32[41,8,128]{2,1,0:T(8,128)S(1)}, f32[41,8,128]{2,1,0:T(8,128)S(1)}, u32[]{:S(2)}, u32[]{:S(2)}) collective-permute-start(f32[41,8,128]{2,1,0:T(8,128)S(1)} %get-tuple-element.38), channel_id=1, source_target_pairs={{1,2},{2,1},{3,4},{4,3},{5,6},{6,5},{9,10},{10,9},{11,12},{12,11},... | collective-permute-start | bytes 503816 | tf_op jit(solution)/shard_map/ppermute | solution.py:816
  15.4 4.2 %collective-permute-start.2 = (f32[41,8,128]{2,1,0:T(8,128)S(1)}, f32[41,8,128]{2,1,0:T(8,128)S(1)}, u32[]{:S(2)}, u32[]{:S(2)}) collective-permute-start(f32[41,8,128]{2,1,0:T(8,128)S(1)} %get-tuple-element.37.sent_face), channel_id=1, source_target_pairs={{0,1},{1,0},{2,3},{3,2},{4,5},{5,4},{6,7},{7,6},{8,9},{9,8},{10,11... | collective-permute-start | bytes 503816 | tf_op jit(solution)/shard_map/ppermute | solution.py:816
  26.5 16.0 %all-to-all-start.1 = ((f32[32,16,128]{2,1,0:T(8,128)}), f32[32,16,128]{2,1,0:T(8,128)S(1)}, u32[]{:S(2)}, u32[]{:S(2)}) async-start(f32[32,16,128]{2,1,0:T(8,128)} %shard_map.70), calls=%async_computation.1 | async-start | bytes 524288 | tf_op jit(solution)/shard_map/all_to_all | solution.py:824
  31.9 7.4 %collective-permute-start.4 = (f32[16,8,128]{2,1,0:T(8,128)S(1)}, f32[16,8,128]{2,1,0:T(8,128)S(1)}, u32[]{:S(2)}, u32[]{:S(2)}) collective-permute-start(f32[16,8,128]{2,1,0:T(8,128)S(1)} %get-tuple-element.45), channel_id=1, source_target_pairs={{0,8},{8,0},{16,24},{24,16},{1,9},{9,1},{17,25},{25,17},{2,10},{10... | collective-permute-start | bytes 196616 | tf_op jit(solution)/shard_map/ppermute | solution.py:816
  33.8 5.6 %collective-permute-start.5 = (f32[16,8,128]{2,1,0:T(8,128)S(1)}, f32[16,8,128]{2,1,0:T(8,128)S(1)}, u32[]{:S(2)}, u32[]{:S(2)}) collective-permute-start(f32[16,8,128]{2,1,0:T(8,128)S(1)} %get-tuple-element.46), channel_id=1, source_target_pairs={{8,16},{16,8},{9,17},{17,9},{10,18},{18,10},{11,19},{19,11},{12,20... | collective-permute-start | bytes 196616 | tf_op jit(solution)/shard_map/ppermute | solution.py:816
  34.4 4.9 %collective-permute-start.6 = (f32[16,8,128]{2,1,0:T(8,128)S(1)}, f32[16,8,128]{2,1,0:T(8,128)S(1)}, u32[]{:S(2)}, u32[]{:S(2)}) collective-permute-start(f32[16,8,128]{2,1,0:T(8,128)S(1)} %get-tuple-element.47), channel_id=1, source_target_pairs={{0,1},{1,0},{2,3},{3,2},{4,5},{5,4},{6,7},{7,6},{8,9},{9,8},{10,11... | collective-permute-start | bytes 196616 | tf_op jit(solution)/shard_map/ppermute | solution.py:816
  34.5 4.8 %collective-permute-start.7 = (f32[16,8,128]{2,1,0:T(8,128)S(1)}, f32[16,8,128]{2,1,0:T(8,128)S(1)}, u32[]{:S(2)}, u32[]{:S(2)}) collective-permute-start(f32[16,8,128]{2,1,0:T(8,128)S(1)} %get-tuple-element.48), channel_id=1, source_target_pairs={{1,2},{2,1},{3,4},{4,3},{5,6},{6,5},{9,10},{10,9},{11,12},{12,11},... | collective-permute-start | bytes 196616 | tf_op jit(solution)/shard_map/ppermute | solution.py:816

commit v18 on v17

--- a/solution.py
+++ b/solution.py
@@ -264,16 +264,23 @@
     return lax.rem(lax.axis_index(axis), 2) == 0
 
 
+def copied(source, target):
+    count = min(source.shape[0], target.shape[0])
+    target[0:count] = source[0:count]
+    if target.shape[0] > count:
+        target[count:] = jnp.zeros_like(target[count:])
+
+
 def by_pair(axis, low, high, first, second):
     @pl.when(on_even(axis))
     def _():
-        first[...] = high[...]
-        second[...] = low[...]
+        copied(high, first)
+        copied(low, second)
 
     @pl.when(jnp.logical_not(on_even(axis)))
     def _():
-        first[...] = low[...]
-        second[...] = high[...]
+        copied(low, first)
+        copied(high, second)
 
 
 def by_side(axis, first, second, low, high):
@@ -874,7 +881,7 @@
     residual, image, residual_faces, *packs, small, fyl, fyh = call(
         residual_kernel,
         [field, field, (4, 8) + plane]
-        + [(IMAGE_PLANES,) + plane] * 4
+        + [(IMAGE_PLANES + spare,) + plane for spare in (1, 2, 0, 3)]
         + [(8, LANES)]
         + [y_shape] * 2,
         (couplings, diagonal, wells, ids, fxl, fxh, *came_y, parts, *ahead),

time: 59.7 us -> 58.7 us (0.983)
  waiting for transfers between devices: 11.6 us -> 6.46 us
  starting transfers between devices: 22.3 us -> 27 us
  blocking collectives: 11.8 us -> 10.5 us
  Pallas kernels: 13.3 us -> 14 us
    ppermute x8, starting transfers between devices: 10.8 us -> 15.8 us  [swap(): return lax.ppermute(value, axis, pairs) if pairs else jnp.zeros_like(value)]
    ppermute x8, waiting for transfers between devices: 5.3 us -> 1.8 us  [swap(): return lax.ppermute(value, axis, pairs) if pairs else jnp.zeros_like(value)]
    all_to_all x2, waiting for transfers between devices: 6.31 us -> 4.65 us  [exchanged(): return lax.all_to_all(part, ('gx', 'gy'), 0, 0, tiled=True)]
    all_to_all x1, blocking collectives: 11.8 us -> 10.5 us  [exchanged(): return lax.all_to_all(part, ('gx', 'gy'), 0, 0, tiled=True)]
    pallas_call x8, Pallas kernels: 13.3 us -> 14 us  [call(): pl.pallas_call(kernel, out_shape=outs, in_specs=[place(*numbered) for num...]
  transfers between devices with their start and end apart: 10 -> 10, of which waited for: 5 -> 5; matrix products, arithmetic and copies ran while one was open for 0% -> 0% of each run, Pallas kernels for 5% -> 6%
where the time goes in v18:
time: 58.7 us; the launch traced here: 58.2 us
  starting transfers between devices  27 us (46%)
  Pallas kernels  14 us (24%)
  blocking collectives  10.5 us (18%)
  waiting for transfers between devices  6.46 us (11%)
    ppermute x8, starting transfers between devices, swap(): return lax.ppermute(value, axis, pairs) if pairs else jnp.zeros_like(value)  15.8 us
    pallas_call x8, Pallas kernels, call(): pl.pallas_call(kernel, out_shape=outs, in_specs=[place(*numbered) for num...  14 us
    all_to_all x2, starting transfers between devices, exchanged(): return lax.all_to_all(part, ('gx', 'gy'), 0, 0, tiled=True)  11.2 us
    all_to_all x1, blocking collectives, exchanged(): return lax.all_to_all(part, ('gx', 'gy'), 0, 0, tiled=True)  10.5 us
    all_to_all x2, waiting for transfers between devices, exchanged(): return lax.all_to_all(part, ('gx', 'gy'), 0, 0, tiled=True)  4.65 us
    ppermute x8, waiting for transfers between devices, swap(): return lax.ppermute(value, axis, pairs) if pairs else jnp.zeros_like(value)  1.8 us
  transfers between devices with their start and end apart: 10, of which 5 were waited for; matrix products, arithmetic and copies ran while one was open for 0% of the time, Pallas kernels for 6%

profile of v18, /device:TPU:0, one launch (start us, length us, event | category | flops | bytes accessed | tf_op | source)
XLA Modules:
  0.0 58.2 jit_solution(914705034593881543)
XLA Ops:
  0.0 0.0 copy-start.5
  0.0 0.0 copy-start.3
  0.0 0.0 copy-start.2
  0.0 0.0 copy-start
  0.0 0.0 copy-start.1
  0.0 0.0 copy-start.4
  0.0 1.5 %shard_map.65 = (f32[37,8,128]{2,1,0:T(8,128)S(1)}, f32[37,8,128]{2,1,0:T(8,128)S(1)}) custom-call(f32[6,4,8,8,128]{4,3,2,1,0:T(8,128)} %couplings.7, f32[4,8,8,128]{3,2,1,0:T(8,128)} %diagonal.7, f32[4,8,8,128]{3,2,1,0:T(8,128)} %wells.7, s32[8,8,128]{2,1,0:T(8,128)} %ids.7, f32[4,2,8,8,128]{4,3,2,1,0:T(8,128)} %right.3, f32[4,2,8,8,128]{4,3,2,1,0:T(8,128)} %guess_in.1), custom_call_target="tpu_custom_call" | custom-call | tf_op jit(solution)/shard_map/pallas_call | solution.py:785
  1.6 3.1 %collective-permute-start = (f32[37,8,128]{2,1,0:T(8,128)S(1)}, f32[37,8,128]{2,1,0:T(8,128)S(1)}, u32[]{:S(2)}, u32[]{:S(2)}) collective-permute-start(f32[37,8,128]{2,1,0:T(8,128)S(1)} %get-tuple-element.33), channel_id=1, source_target_pairs={{0,8},{8,0},{16,24},{24,16},{1,9},{9,1},{17,25},{25,17},{2,10},{10... | collective-permute-start | bytes 454664 | tf_op jit(solution)/shard_map/ppermute | solution.py:823
  4.7 0.7 %collective-permute-start.1 = (f32[37,8,128]{2,1,0:T(8,128)S(1)}, f32[37,8,128]{2,1,0:T(8,128)S(1)}, u32[]{:S(2)}, u32[]{:S(2)}) collective-permute-start(f32[37,8,128]{2,1,0:T(8,128)S(1)} %get-tuple-element.34), channel_id=1, source_target_pairs={{8,16},{16,8},{9,17},{17,9},{10,18},{18,10},{11,19},{19,11},{12,20... | collective-permute-start | bytes 454664 | tf_op jit(solution)/shard_map/ppermute | solution.py:823
  5.3 0.0 copy-done.5
  5.3 0.0 copy-done.3
  5.4 0.0 copy-done.2
  5.4 0.0 copy-done
  5.4 0.0 copy-done.1
  5.4 0.0 copy-done.4
  5.4 3.0 %shard_map.64 = (f32[32,6,128]{2,1,0:T(8,128)}, s32[48]{0:T(128)S(1)}, f32[36,8,128]{2,1,0:T(8,128)S(1)}, f32[36,8,128]{2,1,0:T(8,128)S(1)}) custom-call(f32[6,4,8,8,128]{4,3,2,1,0:T(8,128)S(1)} %copy-done, f32[4,8,8,128]{3,2,1,0:T(8,128)S(1)} %copy-done.2, f32[4,8,8,128]{3,2,1,0:T(8,128)S(1)} %copy-done.3, s32[8,8,128]{2,1,0:T(8,128)S(1)} %copy-done.5, ...), custom_call_target="tpu_custom_call" | custom-call | flops 4194304 | bytes 4194304 | tf_op jit(solution)/shard_map/pallas_call | solution.py:785
  8.4 0.2 collective-permute-done.came_first.rest_0_
  8.6 6.0 %all-to-all-start = ((f32[32,6,128]{2,1,0:T(8,128)}), f32[32,6,128]{2,1,0:T(8,128)S(1)}, u32[]{:S(2)}, u32[]{:S(2)}) async-start(f32[32,6,128]{2,1,0:T(8,128)} %shard_map.67), calls=%async_computation | async-start | bytes 262144 | tf_op jit(solution)/shard_map/all_to_all | solution.py:831
  14.6 0.0 collective-permute-done.1.came_second
  14.6 0.1 shard_map.66
  14.8 0.7 %collective-permute-start.3 = (f32[41,8,128]{2,1,0:T(8,128)S(1)}, f32[41,8,128]{2,1,0:T(8,128)S(1)}, u32[]{:S(2)}, u32[]{:S(2)}) collective-permute-start(f32[41,8,128]{2,1,0:T(8,128)S(1)} %get-tuple-element.38), channel_id=1, source_target_pairs={{1,2},{2,1},{3,4},{4,3},{5,6},{6,5},{9,10},{10,9},{11,12},{12,11},... | collective-permute-start | bytes 503816 | tf_op jit(solution)/shard_map/ppermute | solution.py:823
  15.4 3.2 %collective-permute-start.2 = (f32[41,8,128]{2,1,0:T(8,128)S(1)}, f32[41,8,128]{2,1,0:T(8,128)S(1)}, u32[]{:S(2)}, u32[]{:S(2)}) collective-permute-start(f32[41,8,128]{2,1,0:T(8,128)S(1)} %get-tuple-element.37.sent_face), channel_id=1, source_target_pairs={{0,1},{1,0},{2,3},{3,2},{4,5},{5,4},{6,7},{7,6},{8,9},{9,8},{10,11... | collective-permute-start | bytes 503816 | tf_op jit(solution)/shard_map/ppermute | solution.py:823
  18.6 0.3 shard_map.68
  18.9 0.0 collective-permute-done.3.came_second
  19.0 0.7 %collective-permute-done.2.came_first = f32[41,8,128]{2,1,0:T(8,128)S(1)} collective-permute-done((f32[41,8,128]{2,1,0:T(8,128)S(1)}, f32[41,8,128]{2,1,0:T(8,128)S(1)}, u32[]{:S(2)}, u32[]{:S(2)}) %collective-permute-start.2) | collective-permute-done | bytes 167968 | tf_op jit(solution)/shard_map/ppermute | solution.py:823
  19.7 3.2 %all-to-all-done.parts = f32[32,6,128]{2,1,0:T(8,128)S(1)} async-done(((f32[32,6,128]{2,1,0:T(8,128)}), f32[32,6,128]{2,1,0:T(8,128)S(1)}, u32[]{:S(2)}, u32[]{:S(2)}) %all-to-all-start) | async-done | bytes 98336 | tf_op jit(solution)/shard_map/all_to_all | solution.py:831
  22.9 1.4 %shard_map.69 = (f32[4,2,8,8,128]{4,3,2,1,0:T(8,128)S(1)}, f32[4,2,8,8,128]{4,3,2,1,0:T(8,128)S(1)}, f32[4,8,8,128]{3,2,1,0:T(8,128)S(1)}, f32[17,8,128]{2,1,0:T...) custom-call(f32[6,4,8,8,128]{4,3,2,1,0:T(8,128)S(1)} %copy-done, ...), custom_call_target="tpu_custom_call" | custom-call | tf_op jit(solution)/shard_map/pallas_call | solution.py:785
  24.3 2.4 %shard_map.70 = f32[32,16,128]{2,1,0:T(8,128)} custom-call(f32[4,8,8,128]{3,2,1,0:T(8,128)S(1)} %copy-done.3, s32[8,8,128]{2,1,0:T(8,128)S(1)} %copy-done.5, f32[4,2,8,8,128]{4,3,2,1,0:T(8,128)S(1)} %get-tuple-element.42.residual, f32[4,2,8,8,128]{4,3,2,1,0:T(8,128)S(1)} %get-tuple-element.49.image, s32[48]{0:T(128)S(1)} %get-tuple-element.51.present), custom_call_target="tpu_custom_call" | custom-call | flops 4194304 | bytes 4194304 | tf_op jit(solution)/shard_map/pallas_call | solution.py:785
  26.7 5.2 %all-to-all-start.1 = ((f32[32,16,128]{2,1,0:T(8,128)}), f32[32,16,128]{2,1,0:T(8,128)S(1)}, u32[]{:S(2)}, u32[]{:S(2)}) async-start(f32[32,16,128]{2,1,0:T(8,128)} %shard_map.70), calls=%async_computation.1 | async-start | bytes 524288 | tf_op jit(solution)/shard_map/all_to_all | solution.py:831
  31.9 0.7 %collective-permute-start.7 = (f32[19,8,128]{2,1,0:T(8,128)S(1)}, f32[19,8,128]{2,1,0:T(8,128)S(1)}, u32[]{:S(2)}, u32[]{:S(2)}) collective-permute-start(f32[19,8,128]{2,1,0:T(8,128)S(1)} %get-tuple-element.48), channel_id=1, source_target_pairs={{1,2},{2,1},{3,4},{4,3},{5,6},{6,5},{9,10},{10,9},{11,12},{12,11},... | collective-permute-start | bytes 233480 | tf_op jit(solution)/shard_map/ppermute | solution.py:823
  32.6 0.7 %collective-permute-start.5 = (f32[18,8,128]{2,1,0:T(8,128)S(1)}, f32[18,8,128]{2,1,0:T(8,128)S(1)}, u32[]{:S(2)}, u32[]{:S(2)}) collective-permute-start(f32[18,8,128]{2,1,0:T(8,128)S(1)} %get-tuple-element.46), channel_id=1, source_target_pairs={{8,16},{16,8},{9,17},{17,9},{10,18},{18,10},{11,19},{19,11},{12,20... | collective-permute-start | bytes 221192 | tf_op jit(solution)/shard_map/ppermute | solution.py:823
  33.3 4.5 %collective-permute-start.4 = (f32[17,8,128]{2,1,0:T(8,128)S(1)}, f32[17,8,128]{2,1,0:T(8,128)S(1)}, u32[]{:S(2)}, u32[]{:S(2)}) collective-permute-start(f32[17,8,128]{2,1,0:T(8,128)S(1)} %get-tuple-element.45), channel_id=1, source_target_pairs={{0,8},{8,0},{16,24},{24,16},{1,9},{9,1},{17,25},{25,17},{2,10},{10... | collective-permute-start | bytes 208904 | tf_op jit(solution)/shard_map/ppermute | solution.py:823
  37.8 2.3 %collective-permute-start.6 = (f32[16,8,128]{2,1,0:T(8,128)S(1)}, f32[16,8,128]{2,1,0:T(8,128)S(1)}, u32[]{:S(2)}, u32[]{:S(2)}) collective-permute-start(f32[16,8,128]{2,1,0:T(8,128)S(1)} %get-tuple-element.47), channel_id=1, source_target_pairs={{0,1},{1,0},{2,3},{3,2},{4,5},{5,4},{6,7},{7,6},{8,9},{9,8},{10,11... | collective-permute-start | bytes 196616 | tf_op jit(solution)/shard_map/ppermute | solution.py:823
  40.1 0.9 %collective-permute-done.6.y_first = f32[16,8,128]{2,1,0:T(8,128)S(1)} collective-permute-done((f32[16,8,128]{2,1,0:T(8,128)S(1)}, f32[16,8,128]{2,1,0:T(8,128)S(1)}, u32[]{:S(2)}, u32[]{:S(2)}) %collective-permute-start.6) | collective-permute-done | bytes 65568 | tf_op jit(solution)/shard_map/ppermute | solution.py:823
  41.0 0.0 collective-permute-done.4.x_first
  41.0 0.0 collective-permute-done.5.x_second
  41.0 0.0 collective-permute-done.7.y_second
  41.0 1.4 %all-to-all-done.1.parts = f32[32,16,128]{2,1,0:T(8,128)S(1)} async-done(((f32[32,16,128]{2,1,0:T(8,128)}), f32[32,16,128]{2,1,0:T(8,128)S(1)}, u32[]{:S(2)}, u32[]{:S(2)}) %all-to-all-start.1) | async-done | bytes 262176 | tf_op jit(solution)/shard_map/all_to_all | solution.py:831
  42.5 3.3 %shard_map.71 = (f32[4,2,8,8,128]{4,3,2,1,0:T(8,128)S(1)}, f32[4,2,8,8,128]{4,3,2,1,0:T(8,128)S(1)}, f32[32,1,640]{2,1,0:T(1,128)S(1)}, f32[16,128]{1,0:T(8,128)S(1)}) custom-call(f32[6,4,8,8,128]{4,3,2,1,0:T(8,128)S(1)} %copy-done, f32[4,8,8,128]{3,2,1,0:T(8,128)S(1)} %copy-done.2, f32[4,8,8,128]{3,2,1,0:T(8,128)S(1)} %copy-done.3, ...), custom_call_target="tpu_custom_call" | custom-call | tf_op jit(solution)/shard_map/pallas_call | solution.py:785
  45.8 10.5 %all_to_all.15.parts = f32[32,1,640]{2,1,0:T(1,128)S(1)} all-to-all(f32[32,1,640]{2,1,0:T(1,128)S(1)} %get-tuple-element.55), channel_id=1, replica_groups=mesh['member'=1,'gx'=4,'gy'=8] {'gx','gy'}, dimensions={0} | all-to-all | bytes 163840 | tf_op jit(solution)/shard_map/all_to_all | solution.py:831
  56.3 1.9 %shard_map.72 = f32[4,2,8,8,128]{4,3,2,1,0:T(8,128)} custom-call(f32[4,2,8,8,128]{4,3,2,1,0:T(8,128)} %guess_in.1, f32[4,2,8,8,128]{4,3,2,1,0:T(8,128)S(1)} %get-tuple-element.42.residual, f32[4,2,8,8,128]{4,3,2,1,0:T(8,128)S(1)} %get-tuple-element.53.second, f32[4,2,8,8,128]{4,3,2,1,0:T(8,128)S(1)} %get-tuple-element.54.third, ...), custom_call_target="tpu_custom_call" | custom-call | tf_op jit(solution)/shard_map/pallas_call | solution.py:785
  (1 shorter events, 0.0 us)
Async XLA Ops:
  0.0 5.3 %copy-start.5 = (s32[8,8,128]{2,1,0:T(8,128)S(1)}, s32[8,8,128]{2,1,0:T(8,128)}, u32[]{:S(2)}) copy-start(s32[8,8,128]{2,1,0:T(8,128)} %ids.7) | copy-start | bytes 98308
  0.0 5.3 %copy-start.3 = (f32[4,8,8,128]{3,2,1,0:T(8,128)S(1)}, f32[4,8,8,128]{3,2,1,0:T(8,128)}, u32[]{:S(2)}) copy-start(f32[4,8,8,128]{3,2,1,0:T(8,128)} %wells.7) | copy-start | bytes 393220
  0.0 5.4 %copy-start.2 = (f32[4,8,8,128]{3,2,1,0:T(8,128)S(1)}, f32[4,8,8,128]{3,2,1,0:T(8,128)}, u32[]{:S(2)}) copy-start(f32[4,8,8,128]{3,2,1,0:T(8,128)} %diagonal.7) | copy-start | bytes 393220
  0.0 5.4 %copy-start = (f32[6,4,8,8,128]{4,3,2,1,0:T(8,128)S(1)}, f32[6,4,8,8,128]{4,3,2,1,0:T(8,128)}, u32[]{:S(2)}) copy-start(f32[6,4,8,8,128]{4,3,2,1,0:T(8,128)} %couplings.7) | copy-start | bytes 2359300
  0.0 5.4 %copy-start.1 = (f32[4,2,8,8,128]{4,3,2,1,0:T(8,128)S(1)}, f32[4,2,8,8,128]{4,3,2,1,0:T(8,128)}, u32[]{:S(2)}) copy-start(f32[4,2,8,8,128]{4,3,2,1,0:T(8,128)} %guess_in.1) | copy-start | bytes 786436
  0.0 5.4 %copy-start.4 = (f32[4,2,8,8,128]{4,3,2,1,0:T(8,128)S(1)}, f32[4,2,8,8,128]{4,3,2,1,0:T(8,128)}, u32[]{:S(2)}) copy-start(f32[4,2,8,8,128]{4,3,2,1,0:T(8,128)} %right.3) | copy-start | bytes 786436
  1.6 7.0 %collective-permute-start = (f32[37,8,128]{2,1,0:T(8,128)S(1)}, f32[37,8,128]{2,1,0:T(8,128)S(1)}, u32[]{:S(2)}, u32[]{:S(2)}) collective-permute-start(f32[37,8,128]{2,1,0:T(8,128)S(1)} %get-tuple-element.33), channel_id=1, source_target_pairs={{0,8},{8,0},{16,24},{24,16},{1,9},{9,1},{17,25},{25,17},{2,10},{10... | collective-permute-start | bytes 454664 | tf_op jit(solution)/shard_map/ppermute | solution.py:823
  4.7 10.0 %collective-permute-start.1 = (f32[37,8,128]{2,1,0:T(8,128)S(1)}, f32[37,8,128]{2,1,0:T(8,128)S(1)}, u32[]{:S(2)}, u32[]{:S(2)}) collective-permute-start(f32[37,8,128]{2,1,0:T(8,128)S(1)} %get-tuple-element.34), channel_id=1, source_target_pairs={{8,16},{16,8},{9,17},{17,9},{10,18},{18,10},{11,19},{19,11},{12,20... | collective-permute-start | bytes 454664 | tf_op jit(solution)/shard_map/ppermute | solution.py:823
  8.6 14.3 %all-to-all-start = ((f32[32,6,128]{2,1,0:T(8,128)}), f32[32,6,128]{2,1,0:T(8,128)S(1)}, u32[]{:S(2)}, u32[]{:S(2)}) async-start(f32[32,6,128]{2,1,0:T(8,128)} %shard_map.67), calls=%async_computation | async-start | bytes 262144 | tf_op jit(solution)/shard_map/all_to_all | solution.py:831
  14.8 4.2 %collective-permute-start.3 = (f32[41,8,128]{2,1,0:T(8,128)S(1)}, f32[41,8,128]{2,1,0:T(8,128)S(1)}, u32[]{:S(2)}, u32[]{:S(2)}) collective-permute-start(f32[41,8,128]{2,1,0:T(8,128)S(1)} %get-tuple-element.38), channel_id=1, source_target_pairs={{1,2},{2,1},{3,4},{4,3},{5,6},{6,5},{9,10},{10,9},{11,12},{12,11},... | collective-permute-start | bytes 503816 | tf_op jit(solution)/shard_map/ppermute | solution.py:823
  15.4 4.2 %collective-permute-start.2 = (f32[41,8,128]{2,1,0:T(8,128)S(1)}, f32[41,8,128]{2,1,0:T(8,128)S(1)}, u32[]{:S(2)}, u32[]{:S(2)}) collective-permute-start(f32[41,8,128]{2,1,0:T(8,128)S(1)} %get-tuple-element.37.sent_face), channel_id=1, source_target_pairs={{0,1},{1,0},{2,3},{3,2},{4,5},{5,4},{6,7},{7,6},{8,9},{9,8},{10,11... | collective-permute-start | bytes 503816 | tf_op jit(solution)/shard_map/ppermute | solution.py:823
  26.7 15.7 %all-to-all-start.1 = ((f32[32,16,128]{2,1,0:T(8,128)}), f32[32,16,128]{2,1,0:T(8,128)S(1)}, u32[]{:S(2)}, u32[]{:S(2)}) async-start(f32[32,16,128]{2,1,0:T(8,128)} %shard_map.70), calls=%async_computation.1 | async-start | bytes 524288 | tf_op jit(solution)/shard_map/all_to_all | solution.py:831
  31.9 9.1 %collective-permute-start.7 = (f32[19,8,128]{2,1,0:T(8,128)S(1)}, f32[19,8,128]{2,1,0:T(8,128)S(1)}, u32[]{:S(2)}, u32[]{:S(2)}) collective-permute-start(f32[19,8,128]{2,1,0:T(8,128)S(1)} %get-tuple-element.48), channel_id=1, source_target_pairs={{1,2},{2,1},{3,4},{4,3},{5,6},{6,5},{9,10},{10,9},{11,12},{12,11},... | collective-permute-start | bytes 233480 | tf_op jit(solution)/shard_map/ppermute | solution.py:823
  32.6 8.4 %collective-permute-start.5 = (f32[18,8,128]{2,1,0:T(8,128)S(1)}, f32[18,8,128]{2,1,0:T(8,128)S(1)}, u32[]{:S(2)}, u32[]{:S(2)}) collective-permute-start(f32[18,8,128]{2,1,0:T(8,128)S(1)} %get-tuple-element.46), channel_id=1, source_target_pairs={{8,16},{16,8},{9,17},{17,9},{10,18},{18,10},{11,19},{19,11},{12,20... | collective-permute-start | bytes 221192 | tf_op jit(solution)/shard_map/ppermute | solution.py:823
  33.3 7.7 %collective-permute-start.4 = (f32[17,8,128]{2,1,0:T(8,128)S(1)}, f32[17,8,128]{2,1,0:T(8,128)S(1)}, u32[]{:S(2)}, u32[]{:S(2)}) collective-permute-start(f32[17,8,128]{2,1,0:T(8,128)S(1)} %get-tuple-element.45), channel_id=1, source_target_pairs={{0,8},{8,0},{16,24},{24,16},{1,9},{9,1},{17,25},{25,17},{2,10},{10... | collective-permute-start | bytes 208904 | tf_op jit(solution)/shard_map/ppermute | solution.py:823
  37.8 3.2 %collective-permute-start.6 = (f32[16,8,128]{2,1,0:T(8,128)S(1)}, f32[16,8,128]{2,1,0:T(8,128)S(1)}, u32[]{:S(2)}, u32[]{:S(2)}) collective-permute-start(f32[16,8,128]{2,1,0:T(8,128)S(1)} %get-tuple-element.47), channel_id=1, source_target_pairs={{0,1},{1,0},{2,3},{3,2},{4,5},{5,4},{6,7},{7,6},{8,9},{9,8},{10,11... | collective-permute-start | bytes 196616 | tf_op jit(solution)/shard_map/ppermute | solution.py:823

commit v19 on v18

--- a/solution.py
+++ b/solution.py
@@ -844,7 +844,7 @@
         ends += [pltpu.VMEM(shape, argument.dtype)] * 2
     x_first, x_second = call(
         x_pack_kernel,
-        [(FACE_PLANES + 1,) + plane] * 2,
+        [(FACE_PLANES + 1,) + plane, (FACE_PLANES + 2,) + plane],
         [pltpu.with_memory_space_constraint(argument, pltpu.HBM) for argument in arguments],
         ends
         + [pltpu.SemaphoreType.DMA((len(ends),))]

time: 58.7 us -> 58.8 us (level)
  Pallas kernels: 14 us -> 12.9 us
  starting transfers between devices: 27 us -> 27.6 us
    pallas_call x8, Pallas kernels: 14 us -> 12.9 us  [call(): pl.pallas_call(kernel, out_shape=outs, in_specs=[place(*numbered) for num...]
    all_to_all x2, starting transfers between devices: 11.2 us -> 11.8 us  [exchanged(): return lax.all_to_all(part, ('gx', 'gy'), 0, 0, tiled=True)]
  transfers between devices with their start and end apart: 10 -> 10, of which waited for: 5 -> 5; matrix products, arithmetic and copies ran while one was open for 0% -> 0% of each run, Pallas kernels for 6% -> 5%
where the time goes in v19:
time: 58.8 us; the launch traced here: 58.5 us
  starting transfers between devices  27.6 us (47%)
  Pallas kernels  12.9 us (22%)
  blocking collectives  11 us (19%)
  waiting for transfers between devices  6.91 us (12%)
    ppermute x8, starting transfers between devices, swap(): return lax.ppermute(value, axis, pairs) if pairs else jnp.zeros_like(value)  15.8 us
    pallas_call x8, Pallas kernels, call(): pl.pallas_call(kernel, out_shape=outs, in_specs=[place(*numbered) for num...  12.9 us
    all_to_all x2, starting transfers between devices, exchanged(): return lax.all_to_all(part, ('gx', 'gy'), 0, 0, tiled=True)  11.8 us
    all_to_all x1, blocking collectives, exchanged(): return lax.all_to_all(part, ('gx', 'gy'), 0, 0, tiled=True)  11 us
    all_to_all x2, waiting for transfers between devices, exchanged(): return lax.all_to_all(part, ('gx', 'gy'), 0, 0, tiled=True)  4.65 us
    ppermute x8, waiting for transfers between devices, swap(): return lax.ppermute(value, axis, pairs) if pairs else jnp.zeros_like(value)  2.26 us
  transfers between devices with their start and end apart: 10, of which 5 were waited for; matrix products, arithmetic and copies ran while one was open for 0% of the time, Pallas kernels for 5%

profile of v19, /device:TPU:0, one launch (start us, length us, event | category | flops | bytes accessed | tf_op | source)
XLA Modules:
  0.0 58.5 jit_solution(17754071804555504150)
XLA Ops:
  0.0 0.0 copy-start.5
  0.0 0.0 copy-start.3
  0.0 0.0 copy-start.2
  0.0 0.0 copy-start
  0.0 0.0 copy-start.1
  0.0 0.0 copy-start.4
  0.0 1.5 %shard_map.65 = (f32[37,8,128]{2,1,0:T(8,128)S(1)}, f32[38,8,128]{2,1,0:T(8,128)S(1)}) custom-call(f32[6,4,8,8,128]{4,3,2,1,0:T(8,128)} %couplings.7, f32[4,8,8,128]{3,2,1,0:T(8,128)} %diagonal.7, f32[4,8,8,128]{3,2,1,0:T(8,128)} %wells.7, s32[8,8,128]{2,1,0:T(8,128)} %ids.7, f32[4,2,8,8,128]{4,3,2,1,0:T(8,128)} %right.3, f32[4,2,8,8,128]{4,3,2,1,0:T(8,128)} %guess_in.1), custom_call_target="tpu_custom_call" | custom-call | tf_op jit(solution)/shard_map/pallas_call | solution.py:785
  1.6 3.1 %collective-permute-start = (f32[37,8,128]{2,1,0:T(8,128)S(1)}, f32[37,8,128]{2,1,0:T(8,128)S(1)}, u32[]{:S(2)}, u32[]{:S(2)}) collective-permute-start(f32[37,8,128]{2,1,0:T(8,128)S(1)} %get-tuple-element.33), channel_id=1, source_target_pairs={{0,8},{8,0},{16,24},{24,16},{1,9},{9,1},{17,25},{25,17},{2,10},{10... | collective-permute-start | bytes 454664 | tf_op jit(solution)/shard_map/ppermute | solution.py:823
  4.7 0.7 %collective-permute-start.1 = (f32[38,8,128]{2,1,0:T(8,128)S(1)}, f32[38,8,128]{2,1,0:T(8,128)S(1)}, u32[]{:S(2)}, u32[]{:S(2)}) collective-permute-start(f32[38,8,128]{2,1,0:T(8,128)S(1)} %get-tuple-element.34), channel_id=1, source_target_pairs={{8,16},{16,8},{9,17},{17,9},{10,18},{18,10},{11,19},{19,11},{12,20... | collective-permute-start | bytes 466952 | tf_op jit(solution)/shard_map/ppermute | solution.py:823
  5.3 0.0 copy-done.5
  5.3 0.0 copy-done.3
  5.4 0.0 copy-done.2
  5.4 0.0 copy-done
  5.4 0.0 copy-done.1
  5.4 0.0 copy-done.4
  5.4 2.6 %shard_map.64 = (f32[32,6,128]{2,1,0:T(8,128)}, s32[48]{0:T(128)S(1)}, f32[36,8,128]{2,1,0:T(8,128)S(1)}, f32[36,8,128]{2,1,0:T(8,128)S(1)}) custom-call(f32[6,4,8,8,128]{4,3,2,1,0:T(8,128)S(1)} %copy-done, f32[4,8,8,128]{3,2,1,0:T(8,128)S(1)} %copy-done.2, f32[4,8,8,128]{3,2,1,0:T(8,128)S(1)} %copy-done.3, s32[8,8,128]{2,1,0:T(8,128)S(1)} %copy-done.5, ...), custom_call_target="tpu_custom_call" | custom-call | flops 4194304 | bytes 4194304 | tf_op jit(solution)/shard_map/pallas_call | solution.py:785
  8.0 0.6 %collective-permute-done.came_first.rest_0_ = f32[37,8,128]{2,1,0:T(8,128)S(1)} collective-permute-done((f32[37,8,128]{2,1,0:T(8,128)S(1)}, f32[37,8,128]{2,1,0:T(8,128)S(1)}, u32[]{:S(2)}, u32[]{:S(2)}) %collective-permute-start) | collective-permute-done | bytes 151584 | tf_op jit(solution)/shard_map/ppermute | solution.py:823
  8.6 6.0 %all-to-all-start = ((f32[32,6,128]{2,1,0:T(8,128)}), f32[32,6,128]{2,1,0:T(8,128)S(1)}, u32[]{:S(2)}, u32[]{:S(2)}) async-start(f32[32,6,128]{2,1,0:T(8,128)} %shard_map.67), calls=%async_computation | async-start | bytes 262144 | tf_op jit(solution)/shard_map/all_to_all | solution.py:831
  14.6 0.0 collective-permute-done.1.came_second
  14.7 0.1 shard_map.66
  14.8 0.7 %collective-permute-start.3 = (f32[41,8,128]{2,1,0:T(8,128)S(1)}, f32[41,8,128]{2,1,0:T(8,128)S(1)}, u32[]{:S(2)}, u32[]{:S(2)}) collective-permute-start(f32[41,8,128]{2,1,0:T(8,128)S(1)} %get-tuple-element.38), channel_id=1, source_target_pairs={{1,2},{2,1},{3,4},{4,3},{5,6},{6,5},{9,10},{10,9},{11,12},{12,11},... | collective-permute-start | bytes 503816 | tf_op jit(solution)/shard_map/ppermute | solution.py:823
  15.5 3.2 %collective-permute-start.2 = (f32[41,8,128]{2,1,0:T(8,128)S(1)}, f32[41,8,128]{2,1,0:T(8,128)S(1)}, u32[]{:S(2)}, u32[]{:S(2)}) collective-permute-start(f32[41,8,128]{2,1,0:T(8,128)S(1)} %get-tuple-element.37.sent_face), channel_id=1, source_target_pairs={{0,1},{1,0},{2,3},{3,2},{4,5},{5,4},{6,7},{7,6},{8,9},{9,8},{10,11... | collective-permute-start | bytes 503816 | tf_op jit(solution)/shard_map/ppermute | solution.py:823
  18.6 0.3 shard_map.68
  19.0 0.0 collective-permute-done.3.came_second
  19.0 0.7 %collective-permute-done.2.came_first = f32[41,8,128]{2,1,0:T(8,128)S(1)} collective-permute-done((f32[41,8,128]{2,1,0:T(8,128)S(1)}, f32[41,8,128]{2,1,0:T(8,128)S(1)}, u32[]{:S(2)}, u32[]{:S(2)}) %collective-permute-start.2) | collective-permute-done | bytes 167968 | tf_op jit(solution)/shard_map/ppermute | solution.py:823
  19.7 3.2 %all-to-all-done.parts = f32[32,6,128]{2,1,0:T(8,128)S(1)} async-done(((f32[32,6,128]{2,1,0:T(8,128)}), f32[32,6,128]{2,1,0:T(8,128)S(1)}, u32[]{:S(2)}, u32[]{:S(2)}) %all-to-all-start) | async-done | bytes 98336 | tf_op jit(solution)/shard_map/all_to_all | solution.py:831
  22.9 1.4 %shard_map.69 = (f32[4,2,8,8,128]{4,3,2,1,0:T(8,128)S(1)}, f32[4,2,8,8,128]{4,3,2,1,0:T(8,128)S(1)}, f32[4,8,8,128]{3,2,1,0:T(8,128)S(1)}, f32[17,8,128]{2,1,0:T...) custom-call(f32[6,4,8,8,128]{4,3,2,1,0:T(8,128)S(1)} %copy-done, ...), custom_call_target="tpu_custom_call" | custom-call | tf_op jit(solution)/shard_map/pallas_call | solution.py:785
  24.3 2.1 %shard_map.70 = f32[32,16,128]{2,1,0:T(8,128)} custom-call(f32[4,8,8,128]{3,2,1,0:T(8,128)S(1)} %copy-done.3, s32[8,8,128]{2,1,0:T(8,128)S(1)} %copy-done.5, f32[4,2,8,8,128]{4,3,2,1,0:T(8,128)S(1)} %get-tuple-element.42.residual, f32[4,2,8,8,128]{4,3,2,1,0:T(8,128)S(1)} %get-tuple-element.49.image, s32[48]{0:T(128)S(1)} %get-tuple-element.51.present), custom_call_target="tpu_custom_call" | custom-call | flops 4194304 | bytes 4194304 | tf_op jit(solution)/shard_map/pallas_call | solution.py:785
  26.4 5.8 %all-to-all-start.1 = ((f32[32,16,128]{2,1,0:T(8,128)}), f32[32,16,128]{2,1,0:T(8,128)S(1)}, u32[]{:S(2)}, u32[]{:S(2)}) async-start(f32[32,16,128]{2,1,0:T(8,128)} %shard_map.70), calls=%async_computation.1 | async-start | bytes 524288 | tf_op jit(solution)/shard_map/all_to_all | solution.py:831
  32.2 0.7 %collective-permute-start.7 = (f32[19,8,128]{2,1,0:T(8,128)S(1)}, f32[19,8,128]{2,1,0:T(8,128)S(1)}, u32[]{:S(2)}, u32[]{:S(2)}) collective-permute-start(f32[19,8,128]{2,1,0:T(8,128)S(1)} %get-tuple-element.48), channel_id=1, source_target_pairs={{1,2},{2,1},{3,4},{4,3},{5,6},{6,5},{9,10},{10,9},{11,12},{12,11},... | collective-permute-start | bytes 233480 | tf_op jit(solution)/shard_map/ppermute | solution.py:823
  32.9 0.7 %collective-permute-start.5 = (f32[18,8,128]{2,1,0:T(8,128)S(1)}, f32[18,8,128]{2,1,0:T(8,128)S(1)}, u32[]{:S(2)}, u32[]{:S(2)}) collective-permute-start(f32[18,8,128]{2,1,0:T(8,128)S(1)} %get-tuple-element.46), channel_id=1, source_target_pairs={{8,16},{16,8},{9,17},{17,9},{10,18},{18,10},{11,19},{19,11},{12,20... | collective-permute-start | bytes 221192 | tf_op jit(solution)/shard_map/ppermute | solution.py:823
  33.5 4.5 %collective-permute-start.4 = (f32[17,8,128]{2,1,0:T(8,128)S(1)}, f32[17,8,128]{2,1,0:T(8,128)S(1)}, u32[]{:S(2)}, u32[]{:S(2)}) collective-permute-start(f32[17,8,128]{2,1,0:T(8,128)S(1)} %get-tuple-element.45), channel_id=1, source_target_pairs={{0,8},{8,0},{16,24},{24,16},{1,9},{9,1},{17,25},{25,17},{2,10},{10... | collective-permute-start | bytes 208904 | tf_op jit(solution)/shard_map/ppermute | solution.py:823
  38.1 2.3 %collective-permute-start.6 = (f32[16,8,128]{2,1,0:T(8,128)S(1)}, f32[16,8,128]{2,1,0:T(8,128)S(1)}, u32[]{:S(2)}, u32[]{:S(2)}) collective-permute-start(f32[16,8,128]{2,1,0:T(8,128)S(1)} %get-tuple-element.47), channel_id=1, source_target_pairs={{0,1},{1,0},{2,3},{3,2},{4,5},{5,4},{6,7},{7,6},{8,9},{9,8},{10,11... | collective-permute-start | bytes 196616 | tf_op jit(solution)/shard_map/ppermute | solution.py:823
  40.3 0.9 %collective-permute-done.6.y_first = f32[16,8,128]{2,1,0:T(8,128)S(1)} collective-permute-done((f32[16,8,128]{2,1,0:T(8,128)S(1)}, f32[16,8,128]{2,1,0:T(8,128)S(1)}, u32[]{:S(2)}, u32[]{:S(2)}) %collective-permute-start.6) | collective-permute-done | bytes 65568 | tf_op jit(solution)/shard_map/ppermute | solution.py:823
  41.2 0.0 collective-permute-done.4.x_first
  41.3 0.0 collective-permute-done.5.x_second
  41.3 0.0 collective-permute-done.7.y_second
  41.3 1.4 %all-to-all-done.1.parts = f32[32,16,128]{2,1,0:T(8,128)S(1)} async-done(((f32[32,16,128]{2,1,0:T(8,128)}), f32[32,16,128]{2,1,0:T(8,128)S(1)}, u32[]{:S(2)}, u32[]{:S(2)}) %all-to-all-start.1) | async-done | bytes 262176 | tf_op jit(solution)/shard_map/all_to_all | solution.py:831
  42.7 3.0 %shard_map.71 = (f32[4,2,8,8,128]{4,3,2,1,0:T(8,128)S(1)}, f32[4,2,8,8,128]{4,3,2,1,0:T(8,128)S(1)}, f32[32,1,640]{2,1,0:T(1,128)S(1)}, f32[16,128]{1,0:T(8,128)S(1)}) custom-call(f32[6,4,8,8,128]{4,3,2,1,0:T(8,128)S(1)} %copy-done, f32[4,8,8,128]{3,2,1,0:T(8,128)S(1)} %copy-done.2, f32[4,8,8,128]{3,2,1,0:T(8,128)S(1)} %copy-done.3, ...), custom_call_target="tpu_custom_call" | custom-call | tf_op jit(solution)/shard_map/pallas_call | solution.py:785
  45.7 11.0 %all_to_all.15.parts = f32[32,1,640]{2,1,0:T(1,128)S(1)} all-to-all(f32[32,1,640]{2,1,0:T(1,128)S(1)} %get-tuple-element.55), channel_id=1, replica_groups=mesh['member'=1,'gx'=4,'gy'=8] {'gx','gy'}, dimensions={0} | all-to-all | bytes 163840 | tf_op jit(solution)/shard_map/all_to_all | solution.py:831
  56.7 1.9 %shard_map.72 = f32[4,2,8,8,128]{4,3,2,1,0:T(8,128)} custom-call(f32[4,2,8,8,128]{4,3,2,1,0:T(8,128)} %guess_in.1, f32[4,2,8,8,128]{4,3,2,1,0:T(8,128)S(1)} %get-tuple-element.42.residual, f32[4,2,8,8,128]{4,3,2,1,0:T(8,128)S(1)} %get-tuple-element.53.second, f32[4,2,8,8,128]{4,3,2,1,0:T(8,128)S(1)} %get-tuple-element.54.third, ...), custom_call_target="tpu_custom_call" | custom-call | tf_op jit(solution)/shard_map/pallas_call | solution.py:785
  (1 shorter events, 0.0 us)
Async XLA Ops:
  0.0 5.3 %copy-start.5 = (s32[8,8,128]{2,1,0:T(8,128)S(1)}, s32[8,8,128]{2,1,0:T(8,128)}, u32[]{:S(2)}) copy-start(s32[8,8,128]{2,1,0:T(8,128)} %ids.7) | copy-start | bytes 98308
  0.0 5.3 %copy-start.3 = (f32[4,8,8,128]{3,2,1,0:T(8,128)S(1)}, f32[4,8,8,128]{3,2,1,0:T(8,128)}, u32[]{:S(2)}) copy-start(f32[4,8,8,128]{3,2,1,0:T(8,128)} %wells.7) | copy-start | bytes 393220
  0.0 5.4 %copy-start.2 = (f32[4,8,8,128]{3,2,1,0:T(8,128)S(1)}, f32[4,8,8,128]{3,2,1,0:T(8,128)}, u32[]{:S(2)}) copy-start(f32[4,8,8,128]{3,2,1,0:T(8,128)} %diagonal.7) | copy-start | bytes 393220
  0.0 5.4 %copy-start = (f32[6,4,8,8,128]{4,3,2,1,0:T(8,128)S(1)}, f32[6,4,8,8,128]{4,3,2,1,0:T(8,128)}, u32[]{:S(2)}) copy-start(f32[6,4,8,8,128]{4,3,2,1,0:T(8,128)} %couplings.7) | copy-start | bytes 2359300
  0.0 5.4 %copy-start.1 = (f32[4,2,8,8,128]{4,3,2,1,0:T(8,128)S(1)}, f32[4,2,8,8,128]{4,3,2,1,0:T(8,128)}, u32[]{:S(2)}) copy-start(f32[4,2,8,8,128]{4,3,2,1,0:T(8,128)} %guess_in.1) | copy-start | bytes 786436
  0.0 5.4 %copy-start.4 = (f32[4,2,8,8,128]{4,3,2,1,0:T(8,128)S(1)}, f32[4,2,8,8,128]{4,3,2,1,0:T(8,128)}, u32[]{:S(2)}) copy-start(f32[4,2,8,8,128]{4,3,2,1,0:T(8,128)} %right.3) | copy-start | bytes 786436
  1.6 7.0 %collective-permute-start = (f32[37,8,128]{2,1,0:T(8,128)S(1)}, f32[37,8,128]{2,1,0:T(8,128)S(1)}, u32[]{:S(2)}, u32[]{:S(2)}) collective-permute-start(f32[37,8,128]{2,1,0:T(8,128)S(1)} %get-tuple-element.33), channel_id=1, source_target_pairs={{0,8},{8,0},{16,24},{24,16},{1,9},{9,1},{17,25},{25,17},{2,10},{10... | collective-permute-start | bytes 454664 | tf_op jit(solution)/shard_map/ppermute | solution.py:823
  4.7 10.0 %collective-permute-start.1 = (f32[38,8,128]{2,1,0:T(8,128)S(1)}, f32[38,8,128]{2,1,0:T(8,128)S(1)}, u32[]{:S(2)}, u32[]{:S(2)}) collective-permute-start(f32[38,8,128]{2,1,0:T(8,128)S(1)} %get-tuple-element.34), channel_id=1, source_target_pairs={{8,16},{16,8},{9,17},{17,9},{10,18},{18,10},{11,19},{19,11},{12,20... | collective-permute-start | bytes 466952 | tf_op jit(solution)/shard_map/ppermute | solution.py:823
  8.6 14.3 %all-to-all-start = ((f32[32,6,128]{2,1,0:T(8,128)}), f32[32,6,128]{2,1,0:T(8,128)S(1)}, u32[]{:S(2)}, u32[]{:S(2)}) async-start(f32[32,6,128]{2,1,0:T(8,128)} %shard_map.67), calls=%async_computation | async-start | bytes 262144 | tf_op jit(solution)/shard_map/all_to_all | solution.py:831
  14.8 4.2 %collective-permute-start.3 = (f32[41,8,128]{2,1,0:T(8,128)S(1)}, f32[41,8,128]{2,1,0:T(8,128)S(1)}, u32[]{:S(2)}, u32[]{:S(2)}) collective-permute-start(f32[41,8,128]{2,1,0:T(8,128)S(1)} %get-tuple-element.38), channel_id=1, source_target_pairs={{1,2},{2,1},{3,4},{4,3},{5,6},{6,5},{9,10},{10,9},{11,12},{12,11},... | collective-permute-start | bytes 503816 | tf_op jit(solution)/shard_map/ppermute | solution.py:823
  15.5 4.2 %collective-permute-start.2 = (f32[41,8,128]{2,1,0:T(8,128)S(1)}, f32[41,8,128]{2,1,0:T(8,128)S(1)}, u32[]{:S(2)}, u32[]{:S(2)}) collective-permute-start(f32[41,8,128]{2,1,0:T(8,128)S(1)} %get-tuple-element.37.sent_face), channel_id=1, source_target_pairs={{0,1},{1,0},{2,3},{3,2},{4,5},{5,4},{6,7},{7,6},{8,9},{9,8},{10,11... | collective-permute-start | bytes 503816 | tf_op jit(solution)/shard_map/ppermute | solution.py:823
  26.4 16.3 %all-to-all-start.1 = ((f32[32,16,128]{2,1,0:T(8,128)}), f32[32,16,128]{2,1,0:T(8,128)S(1)}, u32[]{:S(2)}, u32[]{:S(2)}) async-start(f32[32,16,128]{2,1,0:T(8,128)} %shard_map.70), calls=%async_computation.1 | async-start | bytes 524288 | tf_op jit(solution)/shard_map/all_to_all | solution.py:831
  32.2 9.1 %collective-permute-start.7 = (f32[19,8,128]{2,1,0:T(8,128)S(1)}, f32[19,8,128]{2,1,0:T(8,128)S(1)}, u32[]{:S(2)}, u32[]{:S(2)}) collective-permute-start(f32[19,8,128]{2,1,0:T(8,128)S(1)} %get-tuple-element.48), channel_id=1, source_target_pairs={{1,2},{2,1},{3,4},{4,3},{5,6},{6,5},{9,10},{10,9},{11,12},{12,11},... | collective-permute-start | bytes 233480 | tf_op jit(solution)/shard_map/ppermute | solution.py:823
  32.9 8.4 %collective-permute-start.5 = (f32[18,8,128]{2,1,0:T(8,128)S(1)}, f32[18,8,128]{2,1,0:T(8,128)S(1)}, u32[]{:S(2)}, u32[]{:S(2)}) collective-permute-start(f32[18,8,128]{2,1,0:T(8,128)S(1)} %get-tuple-element.46), channel_id=1, source_target_pairs={{8,16},{16,8},{9,17},{17,9},{10,18},{18,10},{11,19},{19,11},{12,20... | collective-permute-start | bytes 221192 | tf_op jit(solution)/shard_map/ppermute | solution.py:823
  33.5 7.7 %collective-permute-start.4 = (f32[17,8,128]{2,1,0:T(8,128)S(1)}, f32[17,8,128]{2,1,0:T(8,128)S(1)}, u32[]{:S(2)}, u32[]{:S(2)}) collective-permute-start(f32[17,8,128]{2,1,0:T(8,128)S(1)} %get-tuple-element.45), channel_id=1, source_target_pairs={{0,8},{8,0},{16,24},{24,16},{1,9},{9,1},{17,25},{25,17},{2,10},{10... | collective-permute-start | bytes 208904 | tf_op jit(solution)/shard_map/ppermute | solution.py:823
  38.1 3.2 %collective-permute-start.6 = (f32[16,8,128]{2,1,0:T(8,128)S(1)}, f32[16,8,128]{2,1,0:T(8,128)S(1)}, u32[]{:S(2)}, u32[]{:S(2)}) collective-permute-start(f32[16,8,128]{2,1,0:T(8,128)S(1)} %get-tuple-element.47), channel_id=1, source_target_pairs={{0,1},{1,0},{2,3},{3,2},{4,5},{5,4},{6,7},{7,6},{8,9},{9,8},{10,11... | collective-permute-start | bytes 196616 | tf_op jit(solution)/shard_map/ppermute | solution.py:823

commit v20 on v18

--- a/solution.py
+++ b/solution.py
@@ -862,7 +862,7 @@
         cost=4 << 20,
         out=1,
     )
-    parts = exchanged(after(part, came_x[0]))
+    parts = exchanged(after(part, came_x[1]))
     y_shape = (FACE_PLANES + CORNER_PLANES,) + plane
     y_first, y_second, fxl, fxh = call(
         corner_kernel,

time: 58.7 us -> 59.6 us (1.015)
  starting transfers between devices: 27 us -> 29 us
  Pallas kernels: 14 us -> 12.7 us
    ppermute x8, starting transfers between devices: 15.8 us -> 18.6 us  [swap(): return lax.ppermute(value, axis, pairs) if pairs else jnp.zeros_like(value)]
    pallas_call x8, Pallas kernels: 14 us -> 12.7 us  [call(): pl.pallas_call(kernel, out_shape=outs, in_specs=[place(*numbered) for num...]
    all_to_all x2, starting transfers between devices: 11.2 us -> 10.4 us  [exchanged(): return lax.all_to_all(part, ('gx', 'gy'), 0, 0, tiled=True)]
  transfers between devices with their start and end apart: 10 -> 10, of which waited for: 5 -> 4; matrix products, arithmetic and copies ran while one was open for 0% -> 0% of each run, Pallas kernels for 6% -> 5%
where the time goes in v20:
time: 59.6 us; the launch traced here: 59 us
  starting transfers between devices  29 us (49%)
  Pallas kernels  12.7 us (21%)
  blocking collectives  10.9 us (18%)
  waiting for transfers between devices  6.28 us (11%)
    ppermute x8, starting transfers between devices, swap(): return lax.ppermute(value, axis, pairs) if pairs else jnp.zeros_like(value)  18.6 us
    pallas_call x8, Pallas kernels, call(): pl.pallas_call(kernel, out_shape=outs, in_specs=[place(*numbered) for num...  12.7 us
    all_to_all x1, blocking collectives, exchanged(): return lax.all_to_all(part, ('gx', 'gy'), 0, 0, tiled=True)  10.9 us
    all_to_all x2, starting transfers between devices, exchanged(): return lax.all_to_all(part, ('gx', 'gy'), 0, 0, tiled=True)  10.4 us
    all_to_all x2, waiting for transfers between devices, exchanged(): return lax.all_to_all(part, ('gx', 'gy'), 0, 0, tiled=True)  4.65 us
    ppermute x8, waiting for transfers between devices, swap(): return lax.ppermute(value, axis, pairs) if pairs else jnp.zeros_like(value)  1.63 us
  transfers between devices with their start and end apart: 10, of which 4 were waited for; matrix products, arithmetic and copies ran while one was open for 0% of the time, Pallas kernels for 5%

profile of v20, /device:TPU:0, one launch (start us, length us, event | category | flops | bytes accessed | tf_op | source)
XLA Modules:
  0.0 59.0 jit_solution(10812265328800714535)
XLA Ops:
  0.0 0.0 copy-start.5
  0.0 0.0 copy-start.3
  0.0 0.0 copy-start.2
  0.0 0.0 copy-start
  0.0 0.0 copy-start.1
  0.0 0.0 copy-start.4
  0.0 1.5 %shard_map.65 = (f32[37,8,128]{2,1,0:T(8,128)S(1)}, f32[37,8,128]{2,1,0:T(8,128)S(1)}) custom-call(f32[6,4,8,8,128]{4,3,2,1,0:T(8,128)} %couplings.7, f32[4,8,8,128]{3,2,1,0:T(8,128)} %diagonal.7, f32[4,8,8,128]{3,2,1,0:T(8,128)} %wells.7, s32[8,8,128]{2,1,0:T(8,128)} %ids.7, f32[4,2,8,8,128]{4,3,2,1,0:T(8,128)} %right.3, f32[4,2,8,8,128]{4,3,2,1,0:T(8,128)} %guess_in.1), custom_call_target="tpu_custom_call" | custom-call | tf_op jit(solution)/shard_map/pallas_call | solution.py:785
  1.6 0.7 %collective-permute-start.1 = (f32[37,8,128]{2,1,0:T(8,128)S(1)}, f32[37,8,128]{2,1,0:T(8,128)S(1)}, u32[]{:S(2)}, u32[]{:S(2)}) collective-permute-start(f32[37,8,128]{2,1,0:T(8,128)S(1)} %get-tuple-element.34), channel_id=1, source_target_pairs={{8,16},{16,8},{9,17},{17,9},{10,18},{18,10},{11,19},{19,11},{12,20... | collective-permute-start | bytes 454664 | tf_op jit(solution)/shard_map/ppermute | solution.py:823
  2.2 5.9 %collective-permute-start = (f32[37,8,128]{2,1,0:T(8,128)S(1)}, f32[37,8,128]{2,1,0:T(8,128)S(1)}, u32[]{:S(2)}, u32[]{:S(2)}) collective-permute-start(f32[37,8,128]{2,1,0:T(8,128)S(1)} %get-tuple-element.33), channel_id=1, source_target_pairs={{0,8},{8,0},{16,24},{24,16},{1,9},{9,1},{17,25},{25,17},{2,10},{10... | collective-permute-start | bytes 454664 | tf_op jit(solution)/shard_map/ppermute | solution.py:823
  8.2 0.0 copy-done.5
  8.2 0.0 copy-done.3
  8.2 0.0 copy-done.2
  8.2 0.0 copy-done
  8.2 0.0 copy-done.1
  8.2 0.0 copy-done.4
  8.2 2.5 %shard_map.64 = (f32[32,6,128]{2,1,0:T(8,128)}, s32[48]{0:T(128)S(1)}, f32[36,8,128]{2,1,0:T(8,128)S(1)}, f32[36,8,128]{2,1,0:T(8,128)S(1)}) custom-call(f32[6,4,8,8,128]{4,3,2,1,0:T(8,128)S(1)} %copy-done, f32[4,8,8,128]{3,2,1,0:T(8,128)S(1)} %copy-done.2, f32[4,8,8,128]{3,2,1,0:T(8,128)S(1)} %copy-done.3, s32[8,8,128]{2,1,0:T(8,128)S(1)} %copy-done.5, ...), custom_call_target="tpu_custom_call" | custom-call | flops 4194304 | bytes 4194304 | tf_op jit(solution)/shard_map/pallas_call | solution.py:785
  10.7 0.0 collective-permute-done.1.came_second.rest_0_
  10.7 4.7 %all-to-all-start = ((f32[32,6,128]{2,1,0:T(8,128)}), f32[32,6,128]{2,1,0:T(8,128)S(1)}, u32[]{:S(2)}, u32[]{:S(2)}) async-start(f32[32,6,128]{2,1,0:T(8,128)} %shard_map.67), calls=%async_computation | async-start | bytes 262144 | tf_op jit(solution)/shard_map/all_to_all | solution.py:831
  15.4 0.0 collective-permute-done.came_first
  15.4 0.1 shard_map.66
  15.6 0.7 %collective-permute-start.3 = (f32[41,8,128]{2,1,0:T(8,128)S(1)}, f32[41,8,128]{2,1,0:T(8,128)S(1)}, u32[]{:S(2)}, u32[]{:S(2)}) collective-permute-start(f32[41,8,128]{2,1,0:T(8,128)S(1)} %get-tuple-element.38), channel_id=1, source_target_pairs={{1,2},{2,1},{3,4},{4,3},{5,6},{6,5},{9,10},{10,9},{11,12},{12,11},... | collective-permute-start | bytes 503816 | tf_op jit(solution)/shard_map/ppermute | solution.py:823
  16.2 3.2 %collective-permute-start.2 = (f32[41,8,128]{2,1,0:T(8,128)S(1)}, f32[41,8,128]{2,1,0:T(8,128)S(1)}, u32[]{:S(2)}, u32[]{:S(2)}) collective-permute-start(f32[41,8,128]{2,1,0:T(8,128)S(1)} %get-tuple-element.37.sent_face), channel_id=1, source_target_pairs={{0,1},{1,0},{2,3},{3,2},{4,5},{5,4},{6,7},{7,6},{8,9},{9,8},{10,11... | collective-permute-start | bytes 503816 | tf_op jit(solution)/shard_map/ppermute | solution.py:823
  19.4 0.3 shard_map.68
  19.8 0.0 collective-permute-done.3.came_second
  19.8 0.7 %collective-permute-done.2.came_first = f32[41,8,128]{2,1,0:T(8,128)S(1)} collective-permute-done((f32[41,8,128]{2,1,0:T(8,128)S(1)}, f32[41,8,128]{2,1,0:T(8,128)S(1)}, u32[]{:S(2)}, u32[]{:S(2)}) %collective-permute-start.2) | collective-permute-done | bytes 167968 | tf_op jit(solution)/shard_map/ppermute | solution.py:823
  20.5 3.2 %all-to-all-done.parts = f32[32,6,128]{2,1,0:T(8,128)S(1)} async-done(((f32[32,6,128]{2,1,0:T(8,128)}), f32[32,6,128]{2,1,0:T(8,128)S(1)}, u32[]{:S(2)}, u32[]{:S(2)}) %all-to-all-start) | async-done | bytes 98336 | tf_op jit(solution)/shard_map/all_to_all | solution.py:831
  23.7 1.4 %shard_map.69 = (f32[4,2,8,8,128]{4,3,2,1,0:T(8,128)S(1)}, f32[4,2,8,8,128]{4,3,2,1,0:T(8,128)S(1)}, f32[4,8,8,128]{3,2,1,0:T(8,128)S(1)}, f32[17,8,128]{2,1,0:T...) custom-call(f32[6,4,8,8,128]{4,3,2,1,0:T(8,128)S(1)} %copy-done, ...), custom_call_target="tpu_custom_call" | custom-call | tf_op jit(solution)/shard_map/pallas_call | solution.py:785
  25.1 2.0 %shard_map.70 = f32[32,16,128]{2,1,0:T(8,128)} custom-call(f32[4,8,8,128]{3,2,1,0:T(8,128)S(1)} %copy-done.3, s32[8,8,128]{2,1,0:T(8,128)S(1)} %copy-done.5, f32[4,2,8,8,128]{4,3,2,1,0:T(8,128)S(1)} %get-tuple-element.42.residual, f32[4,2,8,8,128]{4,3,2,1,0:T(8,128)S(1)} %get-tuple-element.49.image, s32[48]{0:T(128)S(1)} %get-tuple-element.51.present), custom_call_target="tpu_custom_call" | custom-call | flops 4194304 | bytes 4194304 | tf_op jit(solution)/shard_map/pallas_call | solution.py:785
  27.1 5.7 %all-to-all-start.1 = ((f32[32,16,128]{2,1,0:T(8,128)}), f32[32,16,128]{2,1,0:T(8,128)S(1)}, u32[]{:S(2)}, u32[]{:S(2)}) async-start(f32[32,16,128]{2,1,0:T(8,128)} %shard_map.70), calls=%async_computation.1 | async-start | bytes 524288 | tf_op jit(solution)/shard_map/all_to_all | solution.py:831
  32.8 0.7 %collective-permute-start.7 = (f32[19,8,128]{2,1,0:T(8,128)S(1)}, f32[19,8,128]{2,1,0:T(8,128)S(1)}, u32[]{:S(2)}, u32[]{:S(2)}) collective-permute-start(f32[19,8,128]{2,1,0:T(8,128)S(1)} %get-tuple-element.48), channel_id=1, source_target_pairs={{1,2},{2,1},{3,4},{4,3},{5,6},{6,5},{9,10},{10,9},{11,12},{12,11},... | collective-permute-start | bytes 233480 | tf_op jit(solution)/shard_map/ppermute | solution.py:823
  33.5 0.7 %collective-permute-start.5 = (f32[18,8,128]{2,1,0:T(8,128)S(1)}, f32[18,8,128]{2,1,0:T(8,128)S(1)}, u32[]{:S(2)}, u32[]{:S(2)}) collective-permute-start(f32[18,8,128]{2,1,0:T(8,128)S(1)} %get-tuple-element.46), channel_id=1, source_target_pairs={{8,16},{16,8},{9,17},{17,9},{10,18},{18,10},{11,19},{19,11},{12,20... | collective-permute-start | bytes 221192 | tf_op jit(solution)/shard_map/ppermute | solution.py:823
  34.1 4.5 %collective-permute-start.4 = (f32[17,8,128]{2,1,0:T(8,128)S(1)}, f32[17,8,128]{2,1,0:T(8,128)S(1)}, u32[]{:S(2)}, u32[]{:S(2)}) collective-permute-start(f32[17,8,128]{2,1,0:T(8,128)S(1)} %get-tuple-element.45), channel_id=1, source_target_pairs={{0,8},{8,0},{16,24},{24,16},{1,9},{9,1},{17,25},{25,17},{2,10},{10... | collective-permute-start | bytes 208904 | tf_op jit(solution)/shard_map/ppermute | solution.py:823
  38.7 2.3 %collective-permute-start.6 = (f32[16,8,128]{2,1,0:T(8,128)S(1)}, f32[16,8,128]{2,1,0:T(8,128)S(1)}, u32[]{:S(2)}, u32[]{:S(2)}) collective-permute-start(f32[16,8,128]{2,1,0:T(8,128)S(1)} %get-tuple-element.47), channel_id=1, source_target_pairs={{0,1},{1,0},{2,3},{3,2},{4,5},{5,4},{6,7},{7,6},{8,9},{9,8},{10,11... | collective-permute-start | bytes 196616 | tf_op jit(solution)/shard_map/ppermute | solution.py:823
  41.0 0.9 %collective-permute-done.6.y_first = f32[16,8,128]{2,1,0:T(8,128)S(1)} collective-permute-done((f32[16,8,128]{2,1,0:T(8,128)S(1)}, f32[16,8,128]{2,1,0:T(8,128)S(1)}, u32[]{:S(2)}, u32[]{:S(2)}) %collective-permute-start.6) | collective-permute-done | bytes 65568 | tf_op jit(solution)/shard_map/ppermute | solution.py:823
  41.9 0.0 collective-permute-done.4.x_first
  41.9 0.0 collective-permute-done.5.x_second
  41.9 0.0 collective-permute-done.7.y_second
  41.9 1.4 %all-to-all-done.1.parts = f32[32,16,128]{2,1,0:T(8,128)S(1)} async-done(((f32[32,16,128]{2,1,0:T(8,128)}), f32[32,16,128]{2,1,0:T(8,128)S(1)}, u32[]{:S(2)}, u32[]{:S(2)}) %all-to-all-start.1) | async-done | bytes 262176 | tf_op jit(solution)/shard_map/all_to_all | solution.py:831
  43.3 2.9 %shard_map.71 = (f32[4,2,8,8,128]{4,3,2,1,0:T(8,128)S(1)}, f32[4,2,8,8,128]{4,3,2,1,0:T(8,128)S(1)}, f32[32,1,640]{2,1,0:T(1,128)S(1)}, f32[16,128]{1,0:T(8,128)S(1)}) custom-call(f32[6,4,8,8,128]{4,3,2,1,0:T(8,128)S(1)} %copy-done, f32[4,8,8,128]{3,2,1,0:T(8,128)S(1)} %copy-done.2, f32[4,8,8,128]{3,2,1,0:T(8,128)S(1)} %copy-done.3, ...), custom_call_target="tpu_custom_call" | custom-call | tf_op jit(solution)/shard_map/pallas_call | solution.py:785
  46.3 10.9 %all_to_all.15.parts = f32[32,1,640]{2,1,0:T(1,128)S(1)} all-to-all(f32[32,1,640]{2,1,0:T(1,128)S(1)} %get-tuple-element.55), channel_id=1, replica_groups=mesh['member'=1,'gx'=4,'gy'=8] {'gx','gy'}, dimensions={0} | all-to-all | bytes 163840 | tf_op jit(solution)/shard_map/all_to_all | solution.py:831
  57.2 1.9 %shard_map.72 = f32[4,2,8,8,128]{4,3,2,1,0:T(8,128)} custom-call(f32[4,2,8,8,128]{4,3,2,1,0:T(8,128)} %guess_in.1, f32[4,2,8,8,128]{4,3,2,1,0:T(8,128)S(1)} %get-tuple-element.42.residual, f32[4,2,8,8,128]{4,3,2,1,0:T(8,128)S(1)} %get-tuple-element.53.second, f32[4,2,8,8,128]{4,3,2,1,0:T(8,128)S(1)} %get-tuple-element.54.third, ...), custom_call_target="tpu_custom_call" | custom-call | tf_op jit(solution)/shard_map/pallas_call | solution.py:785
  (1 shorter events, 0.0 us)
Async XLA Ops:
  0.0 8.2 %copy-start.5 = (s32[8,8,128]{2,1,0:T(8,128)S(1)}, s32[8,8,128]{2,1,0:T(8,128)}, u32[]{:S(2)}) copy-start(s32[8,8,128]{2,1,0:T(8,128)} %ids.7) | copy-start | bytes 98308
  0.0 8.2 %copy-start.3 = (f32[4,8,8,128]{3,2,1,0:T(8,128)S(1)}, f32[4,8,8,128]{3,2,1,0:T(8,128)}, u32[]{:S(2)}) copy-start(f32[4,8,8,128]{3,2,1,0:T(8,128)} %wells.7) | copy-start | bytes 393220
  0.0 8.2 %copy-start.2 = (f32[4,8,8,128]{3,2,1,0:T(8,128)S(1)}, f32[4,8,8,128]{3,2,1,0:T(8,128)}, u32[]{:S(2)}) copy-start(f32[4,8,8,128]{3,2,1,0:T(8,128)} %diagonal.7) | copy-start | bytes 393220
  0.0 8.2 %copy-start = (f32[6,4,8,8,128]{4,3,2,1,0:T(8,128)S(1)}, f32[6,4,8,8,128]{4,3,2,1,0:T(8,128)}, u32[]{:S(2)}) copy-start(f32[6,4,8,8,128]{4,3,2,1,0:T(8,128)} %couplings.7) | copy-start | bytes 2359300
  0.0 8.2 %copy-start.1 = (f32[4,2,8,8,128]{4,3,2,1,0:T(8,128)S(1)}, f32[4,2,8,8,128]{4,3,2,1,0:T(8,128)}, u32[]{:S(2)}) copy-start(f32[4,2,8,8,128]{4,3,2,1,0:T(8,128)} %guess_in.1) | copy-start | bytes 786436
  0.0 8.2 %copy-start.4 = (f32[4,2,8,8,128]{4,3,2,1,0:T(8,128)S(1)}, f32[4,2,8,8,128]{4,3,2,1,0:T(8,128)}, u32[]{:S(2)}) copy-start(f32[4,2,8,8,128]{4,3,2,1,0:T(8,128)} %right.3) | copy-start | bytes 786436
  1.6 9.1 %collective-permute-start.1 = (f32[37,8,128]{2,1,0:T(8,128)S(1)}, f32[37,8,128]{2,1,0:T(8,128)S(1)}, u32[]{:S(2)}, u32[]{:S(2)}) collective-permute-start(f32[37,8,128]{2,1,0:T(8,128)S(1)} %get-tuple-element.34), channel_id=1, source_target_pairs={{8,16},{16,8},{9,17},{17,9},{10,18},{18,10},{11,19},{19,11},{12,20... | collective-permute-start | bytes 454664 | tf_op jit(solution)/shard_map/ppermute | solution.py:823
  2.2 13.2 %collective-permute-start = (f32[37,8,128]{2,1,0:T(8,128)S(1)}, f32[37,8,128]{2,1,0:T(8,128)S(1)}, u32[]{:S(2)}, u32[]{:S(2)}) collective-permute-start(f32[37,8,128]{2,1,0:T(8,128)S(1)} %get-tuple-element.33), channel_id=1, source_target_pairs={{0,8},{8,0},{16,24},{24,16},{1,9},{9,1},{17,25},{25,17},{2,10},{10... | collective-permute-start | bytes 454664 | tf_op jit(solution)/shard_map/ppermute | solution.py:823
  10.7 12.9 %all-to-all-start = ((f32[32,6,128]{2,1,0:T(8,128)}), f32[32,6,128]{2,1,0:T(8,128)S(1)}, u32[]{:S(2)}, u32[]{:S(2)}) async-start(f32[32,6,128]{2,1,0:T(8,128)} %shard_map.67), calls=%async_computation | async-start | bytes 262144 | tf_op jit(solution)/shard_map/all_to_all | solution.py:831
  15.6 4.2 %collective-permute-start.3 = (f32[41,8,128]{2,1,0:T(8,128)S(1)}, f32[41,8,128]{2,1,0:T(8,128)S(1)}, u32[]{:S(2)}, u32[]{:S(2)}) collective-permute-start(f32[41,8,128]{2,1,0:T(8,128)S(1)} %get-tuple-element.38), channel_id=1, source_target_pairs={{1,2},{2,1},{3,4},{4,3},{5,6},{6,5},{9,10},{10,9},{11,12},{12,11},... | collective-permute-start | bytes 503816 | tf_op jit(solution)/shard_map/ppermute | solution.py:823
  16.2 4.2 %collective-permute-start.2 = (f32[41,8,128]{2,1,0:T(8,128)S(1)}, f32[41,8,128]{2,1,0:T(8,128)S(1)}, u32[]{:S(2)}, u32[]{:S(2)}) collective-permute-start(f32[41,8,128]{2,1,0:T(8,128)S(1)} %get-tuple-element.37.sent_face), channel_id=1, source_target_pairs={{0,1},{1,0},{2,3},{3,2},{4,5},{5,4},{6,7},{7,6},{8,9},{9,8},{10,11... | collective-permute-start | bytes 503816 | tf_op jit(solution)/shard_map/ppermute | solution.py:823
  27.1 16.2 %all-to-all-start.1 = ((f32[32,16,128]{2,1,0:T(8,128)}), f32[32,16,128]{2,1,0:T(8,128)S(1)}, u32[]{:S(2)}, u32[]{:S(2)}) async-start(f32[32,16,128]{2,1,0:T(8,128)} %shard_map.70), calls=%async_computation.1 | async-start | bytes 524288 | tf_op jit(solution)/shard_map/all_to_all | solution.py:831
  32.8 9.1 %collective-permute-start.7 = (f32[19,8,128]{2,1,0:T(8,128)S(1)}, f32[19,8,128]{2,1,0:T(8,128)S(1)}, u32[]{:S(2)}, u32[]{:S(2)}) collective-permute-start(f32[19,8,128]{2,1,0:T(8,128)S(1)} %get-tuple-element.48), channel_id=1, source_target_pairs={{1,2},{2,1},{3,4},{4,3},{5,6},{6,5},{9,10},{10,9},{11,12},{12,11},... | collective-permute-start | bytes 233480 | tf_op jit(solution)/shard_map/ppermute | solution.py:823
  33.5 8.4 %collective-permute-start.5 = (f32[18,8,128]{2,1,0:T(8,128)S(1)}, f32[18,8,128]{2,1,0:T(8,128)S(1)}, u32[]{:S(2)}, u32[]{:S(2)}) collective-permute-start(f32[18,8,128]{2,1,0:T(8,128)S(1)} %get-tuple-element.46), channel_id=1, source_target_pairs={{8,16},{16,8},{9,17},{17,9},{10,18},{18,10},{11,19},{19,11},{12,20... | collective-permute-start | bytes 221192 | tf_op jit(solution)/shard_map/ppermute | solution.py:823
  34.1 7.7 %collective-permute-start.4 = (f32[17,8,128]{2,1,0:T(8,128)S(1)}, f32[17,8,128]{2,1,0:T(8,128)S(1)}, u32[]{:S(2)}, u32[]{:S(2)}) collective-permute-start(f32[17,8,128]{2,1,0:T(8,128)S(1)} %get-tuple-element.45), channel_id=1, source_target_pairs={{0,8},{8,0},{16,24},{24,16},{1,9},{9,1},{17,25},{25,17},{2,10},{10... | collective-permute-start | bytes 208904 | tf_op jit(solution)/shard_map/ppermute | solution.py:823
  38.7 3.2 %collective-permute-start.6 = (f32[16,8,128]{2,1,0:T(8,128)S(1)}, f32[16,8,128]{2,1,0:T(8,128)S(1)}, u32[]{:S(2)}, u32[]{:S(2)}) collective-permute-start(f32[16,8,128]{2,1,0:T(8,128)S(1)} %get-tuple-element.47), channel_id=1, source_target_pairs={{0,1},{1,0},{2,3},{3,2},{4,5},{5,4},{6,7},{7,6},{8,9},{9,8},{10,11... | collective-permute-start | bytes 196616 | tf_op jit(solution)/shard_map/ppermute | solution.py:823

commit v21 on v18

--- a/solution.py
+++ b/solution.py
@@ -881,7 +881,7 @@
     residual, image, residual_faces, *packs, small, fyl, fyh = call(
         residual_kernel,
         [field, field, (4, 8) + plane]
-        + [(IMAGE_PLANES + spare,) + plane for spare in (1, 2, 0, 3)]
+        + [(IMAGE_PLANES + spare,) + plane for spare in (2, 1, 0, 3)]
         + [(8, LANES)]
         + [y_shape] * 2,
         (couplings, diagonal, wells, ids, fxl, fxh, *came_y, parts, *ahead),

time: 58.7 us -> 59.5 us (1.014)
  waiting for transfers between devices: 6.46 us -> 9.09 us
  starting transfers between devices: 27 us -> 24.9 us
  blocking collectives: 10.5 us -> 11.5 us
  Pallas kernels: 14 us -> 13.3 us
    all_to_all x2, waiting for transfers between devices: 4.65 us -> 7.04 us  [exchanged(): return lax.all_to_all(part, ('gx', 'gy'), 0, 0, tiled=True)]
    ppermute x8, starting transfers between devices: 15.8 us -> 13.4 us  [swap(): return lax.ppermute(value, axis, pairs) if pairs else jnp.zeros_like(value)]
    all_to_all x1, blocking collectives: 10.5 us -> 11.5 us  [exchanged(): return lax.all_to_all(part, ('gx', 'gy'), 0, 0, tiled=True)]
    pallas_call x8, Pallas kernels: 14 us -> 13.3 us  [call(): pl.pallas_call(kernel, out_shape=outs, in_specs=[place(*numbered) for num...]
  transfers between devices with their start and end apart: 10 -> 10, of which waited for: 5 -> 5; matrix products, arithmetic and copies ran while one was open for 0% -> 0% of each run, Pallas kernels for 6% -> 5%
where the time goes in v21:
time: 59.5 us; the launch traced here: 59.1 us
  starting transfers between devices  24.9 us (42%)
  Pallas kernels  13.3 us (22%)
  blocking collectives  11.5 us (19%)
  waiting for transfers between devices  9.09 us (15%)
    ppermute x8, starting transfers between devices, swap(): return lax.ppermute(value, axis, pairs) if pairs else jnp.zeros_like(value)  13.4 us
    pallas_call x8, Pallas kernels, call(): pl.pallas_call(kernel, out_shape=outs, in_specs=[place(*numbered) for num...  13.3 us
    all_to_all x2, starting transfers between devices, exchanged(): return lax.all_to_all(part, ('gx', 'gy'), 0, 0, tiled=True)  11.5 us
    all_to_all x1, blocking collectives, exchanged(): return lax.all_to_all(part, ('gx', 'gy'), 0, 0, tiled=True)  11.5 us
    all_to_all x2, waiting for transfers between devices, exchanged(): return lax.all_to_all(part, ('gx', 'gy'), 0, 0, tiled=True)  7.04 us
    ppermute x8, waiting for transfers between devices, swap(): return lax.ppermute(value, axis, pairs) if pairs else jnp.zeros_like(value)  2.04 us
  transfers between devices with their start and end apart: 10, of which 5 were waited for; matrix products, arithmetic and copies ran while one was open for 0% of the time, Pallas kernels for 5%

profile of v21, /device:TPU:0, one launch (start us, length us, event | category | flops | bytes accessed | tf_op | source)
XLA Modules:
  0.0 59.1 jit_solution(9913491413690057447)
XLA Ops:
  0.0 0.0 copy-start.5
  0.0 0.0 copy-start.3
  0.0 0.0 copy-start.2
  0.0 0.0 copy-start
  0.0 0.0 copy-start.1
  0.0 0.0 copy-start.4
  0.0 1.5 %shard_map.65 = (f32[37,8,128]{2,1,0:T(8,128)S(1)}, f32[37,8,128]{2,1,0:T(8,128)S(1)}) custom-call(f32[6,4,8,8,128]{4,3,2,1,0:T(8,128)} %couplings.7, f32[4,8,8,128]{3,2,1,0:T(8,128)} %diagonal.7, f32[4,8,8,128]{3,2,1,0:T(8,128)} %wells.7, s32[8,8,128]{2,1,0:T(8,128)} %ids.7, f32[4,2,8,8,128]{4,3,2,1,0:T(8,128)} %right.3, f32[4,2,8,8,128]{4,3,2,1,0:T(8,128)} %guess_in.1), custom_call_target="tpu_custom_call" | custom-call | tf_op jit(solution)/shard_map/pallas_call | solution.py:785
  1.6 3.1 %collective-permute-start = (f32[37,8,128]{2,1,0:T(8,128)S(1)}, f32[37,8,128]{2,1,0:T(8,128)S(1)}, u32[]{:S(2)}, u32[]{:S(2)}) collective-permute-start(f32[37,8,128]{2,1,0:T(8,128)S(1)} %get-tuple-element.33), channel_id=1, source_target_pairs={{0,8},{8,0},{16,24},{24,16},{1,9},{9,1},{17,25},{25,17},{2,10},{10... | collective-permute-start | bytes 454664 | tf_op jit(solution)/shard_map/ppermute | solution.py:823
  4.7 0.7 %collective-permute-start.1 = (f32[37,8,128]{2,1,0:T(8,128)S(1)}, f32[37,8,128]{2,1,0:T(8,128)S(1)}, u32[]{:S(2)}, u32[]{:S(2)}) collective-permute-start(f32[37,8,128]{2,1,0:T(8,128)S(1)} %get-tuple-element.34), channel_id=1, source_target_pairs={{8,16},{16,8},{9,17},{17,9},{10,18},{18,10},{11,19},{19,11},{12,20... | collective-permute-start | bytes 454664 | tf_op jit(solution)/shard_map/ppermute | solution.py:823
  5.3 0.0 copy-done.5
  5.3 0.0 copy-done.3
  5.4 0.0 copy-done.2
  5.4 0.0 copy-done
  5.4 0.0 copy-done.1
  5.4 0.0 copy-done.4
  5.4 2.8 %shard_map.64 = (f32[32,6,128]{2,1,0:T(8,128)}, s32[48]{0:T(128)S(1)}, f32[36,8,128]{2,1,0:T(8,128)S(1)}, f32[36,8,128]{2,1,0:T(8,128)S(1)}) custom-call(f32[6,4,8,8,128]{4,3,2,1,0:T(8,128)S(1)} %copy-done, f32[4,8,8,128]{3,2,1,0:T(8,128)S(1)} %copy-done.2, f32[4,8,8,128]{3,2,1,0:T(8,128)S(1)} %copy-done.3, s32[8,8,128]{2,1,0:T(8,128)S(1)} %copy-done.5, ...), custom_call_target="tpu_custom_call" | custom-call | flops 4194304 | bytes 4194304 | tf_op jit(solution)/shard_map/pallas_call | solution.py:785
  8.2 0.4 collective-permute-done.came_first.rest_0_
  8.6 6.0 %all-to-all-start = ((f32[32,6,128]{2,1,0:T(8,128)}), f32[32,6,128]{2,1,0:T(8,128)S(1)}, u32[]{:S(2)}, u32[]{:S(2)}) async-start(f32[32,6,128]{2,1,0:T(8,128)} %shard_map.67), calls=%async_computation | async-start | bytes 262144 | tf_op jit(solution)/shard_map/all_to_all | solution.py:831
  14.6 0.0 collective-permute-done.1.came_second
  14.6 0.1 shard_map.66
  14.8 0.7 %collective-permute-start.3 = (f32[41,8,128]{2,1,0:T(8,128)S(1)}, f32[41,8,128]{2,1,0:T(8,128)S(1)}, u32[]{:S(2)}, u32[]{:S(2)}) collective-permute-start(f32[41,8,128]{2,1,0:T(8,128)S(1)} %get-tuple-element.38), channel_id=1, source_target_pairs={{1,2},{2,1},{3,4},{4,3},{5,6},{6,5},{9,10},{10,9},{11,12},{12,11},... | collective-permute-start | bytes 503816 | tf_op jit(solution)/shard_map/ppermute | solution.py:823
  15.4 3.2 %collective-permute-start.2 = (f32[41,8,128]{2,1,0:T(8,128)S(1)}, f32[41,8,128]{2,1,0:T(8,128)S(1)}, u32[]{:S(2)}, u32[]{:S(2)}) collective-permute-start(f32[41,8,128]{2,1,0:T(8,128)S(1)} %get-tuple-element.37.sent_face), channel_id=1, source_target_pairs={{0,1},{1,0},{2,3},{3,2},{4,5},{5,4},{6,7},{7,6},{8,9},{9,8},{10,11... | collective-permute-start | bytes 503816 | tf_op jit(solution)/shard_map/ppermute | solution.py:823
  18.6 0.3 shard_map.68
  18.9 0.0 collective-permute-done.3.came_second
  19.0 0.7 %collective-permute-done.2.came_first = f32[41,8,128]{2,1,0:T(8,128)S(1)} collective-permute-done((f32[41,8,128]{2,1,0:T(8,128)S(1)}, f32[41,8,128]{2,1,0:T(8,128)S(1)}, u32[]{:S(2)}, u32[]{:S(2)}) %collective-permute-start.2) | collective-permute-done | bytes 167968 | tf_op jit(solution)/shard_map/ppermute | solution.py:823
  19.7 3.2 %all-to-all-done.parts = f32[32,6,128]{2,1,0:T(8,128)S(1)} async-done(((f32[32,6,128]{2,1,0:T(8,128)}), f32[32,6,128]{2,1,0:T(8,128)S(1)}, u32[]{:S(2)}, u32[]{:S(2)}) %all-to-all-start) | async-done | bytes 98336 | tf_op jit(solution)/shard_map/all_to_all | solution.py:831
  22.9 1.4 %shard_map.69 = (f32[4,2,8,8,128]{4,3,2,1,0:T(8,128)S(1)}, f32[4,2,8,8,128]{4,3,2,1,0:T(8,128)S(1)}, f32[4,8,8,128]{3,2,1,0:T(8,128)S(1)}, f32[18,8,128]{2,1,0:T...) custom-call(f32[6,4,8,8,128]{4,3,2,1,0:T(8,128)S(1)} %copy-done, ...), custom_call_target="tpu_custom_call" | custom-call | tf_op jit(solution)/shard_map/pallas_call | solution.py:785
  24.3 2.2 %shard_map.70 = f32[32,16,128]{2,1,0:T(8,128)} custom-call(f32[4,8,8,128]{3,2,1,0:T(8,128)S(1)} %copy-done.3, s32[8,8,128]{2,1,0:T(8,128)S(1)} %copy-done.5, f32[4,2,8,8,128]{4,3,2,1,0:T(8,128)S(1)} %get-tuple-element.42.residual, f32[4,2,8,8,128]{4,3,2,1,0:T(8,128)S(1)} %get-tuple-element.49.image, s32[48]{0:T(128)S(1)} %get-tuple-element.51.present), custom_call_target="tpu_custom_call" | custom-call | flops 4194304 | bytes 4194304 | tf_op jit(solution)/shard_map/pallas_call | solution.py:785
  26.5 5.5 %all-to-all-start.1 = ((f32[32,16,128]{2,1,0:T(8,128)}), f32[32,16,128]{2,1,0:T(8,128)S(1)}, u32[]{:S(2)}, u32[]{:S(2)}) async-start(f32[32,16,128]{2,1,0:T(8,128)} %shard_map.70), calls=%async_computation.1 | async-start | bytes 524288 | tf_op jit(solution)/shard_map/all_to_all | solution.py:831
  32.0 0.7 %collective-permute-start.7 = (f32[19,8,128]{2,1,0:T(8,128)S(1)}, f32[19,8,128]{2,1,0:T(8,128)S(1)}, u32[]{:S(2)}, u32[]{:S(2)}) collective-permute-start(f32[19,8,128]{2,1,0:T(8,128)S(1)} %get-tuple-element.48), channel_id=1, source_target_pairs={{1,2},{2,1},{3,4},{4,3},{5,6},{6,5},{9,10},{10,9},{11,12},{12,11},... | collective-permute-start | bytes 233480 | tf_op jit(solution)/shard_map/ppermute | solution.py:823
  32.7 1.8 %collective-permute-start.4 = (f32[18,8,128]{2,1,0:T(8,128)S(1)}, f32[18,8,128]{2,1,0:T(8,128)S(1)}, u32[]{:S(2)}, u32[]{:S(2)}) collective-permute-start(f32[18,8,128]{2,1,0:T(8,128)S(1)} %get-tuple-element.45), channel_id=1, source_target_pairs={{0,8},{8,0},{16,24},{24,16},{1,9},{9,1},{17,25},{25,17},{2,10},{10... | collective-permute-start | bytes 221192 | tf_op jit(solution)/shard_map/ppermute | solution.py:823
  34.6 0.7 %collective-permute-start.5 = (f32[17,8,128]{2,1,0:T(8,128)S(1)}, f32[17,8,128]{2,1,0:T(8,128)S(1)}, u32[]{:S(2)}, u32[]{:S(2)}) collective-permute-start(f32[17,8,128]{2,1,0:T(8,128)S(1)} %get-tuple-element.46), channel_id=1, source_target_pairs={{8,16},{16,8},{9,17},{17,9},{10,18},{18,10},{11,19},{19,11},{12,20... | collective-permute-start | bytes 208904 | tf_op jit(solution)/shard_map/ppermute | solution.py:823
  35.2 2.6 %collective-permute-start.6 = (f32[16,8,128]{2,1,0:T(8,128)S(1)}, f32[16,8,128]{2,1,0:T(8,128)S(1)}, u32[]{:S(2)}, u32[]{:S(2)}) collective-permute-start(f32[16,8,128]{2,1,0:T(8,128)S(1)} %get-tuple-element.47), channel_id=1, source_target_pairs={{0,1},{1,0},{2,3},{3,2},{4,5},{5,4},{6,7},{7,6},{8,9},{9,8},{10,11... | collective-permute-start | bytes 196616 | tf_op jit(solution)/shard_map/ppermute | solution.py:823
  37.8 0.9 %collective-permute-done.6.y_first = f32[16,8,128]{2,1,0:T(8,128)S(1)} collective-permute-done((f32[16,8,128]{2,1,0:T(8,128)S(1)}, f32[16,8,128]{2,1,0:T(8,128)S(1)}, u32[]{:S(2)}, u32[]{:S(2)}) %collective-permute-start.6) | collective-permute-done | bytes 65568 | tf_op jit(solution)/shard_map/ppermute | solution.py:823
  38.7 0.0 collective-permute-done.5.x_second
  38.7 0.0 collective-permute-done.4.x_first
  38.7 0.0 collective-permute-done.7.y_second
  38.7 3.8 %all-to-all-done.1.parts = f32[32,16,128]{2,1,0:T(8,128)S(1)} async-done(((f32[32,16,128]{2,1,0:T(8,128)}), f32[32,16,128]{2,1,0:T(8,128)S(1)}, u32[]{:S(2)}, u32[]{:S(2)}) %all-to-all-start.1) | async-done | bytes 262176 | tf_op jit(solution)/shard_map/all_to_all | solution.py:831
  42.6 3.1 %shard_map.71 = (f32[4,2,8,8,128]{4,3,2,1,0:T(8,128)S(1)}, f32[4,2,8,8,128]{4,3,2,1,0:T(8,128)S(1)}, f32[32,1,640]{2,1,0:T(1,128)S(1)}, f32[16,128]{1,0:T(8,128)S(1)}) custom-call(f32[6,4,8,8,128]{4,3,2,1,0:T(8,128)S(1)} %copy-done, f32[4,8,8,128]{3,2,1,0:T(8,128)S(1)} %copy-done.2, f32[4,8,8,128]{3,2,1,0:T(8,128)S(1)} %copy-done.3, ...), custom_call_target="tpu_custom_call" | custom-call | tf_op jit(solution)/shard_map/pallas_call | solution.py:785
  45.7 11.5 %all_to_all.15.parts = f32[32,1,640]{2,1,0:T(1,128)S(1)} all-to-all(f32[32,1,640]{2,1,0:T(1,128)S(1)} %get-tuple-element.55), channel_id=1, replica_groups=mesh['member'=1,'gx'=4,'gy'=8] {'gx','gy'}, dimensions={0} | all-to-all | bytes 163840 | tf_op jit(solution)/shard_map/all_to_all | solution.py:831
  57.2 1.9 %shard_map.72 = f32[4,2,8,8,128]{4,3,2,1,0:T(8,128)} custom-call(f32[4,2,8,8,128]{4,3,2,1,0:T(8,128)} %guess_in.1, f32[4,2,8,8,128]{4,3,2,1,0:T(8,128)S(1)} %get-tuple-element.42.residual, f32[4,2,8,8,128]{4,3,2,1,0:T(8,128)S(1)} %get-tuple-element.53.second, f32[4,2,8,8,128]{4,3,2,1,0:T(8,128)S(1)} %get-tuple-element.54.third, ...), custom_call_target="tpu_custom_call" | custom-call | tf_op jit(solution)/shard_map/pallas_call | solution.py:785
  (1 shorter events, 0.0 us)
Async XLA Ops:
  0.0 5.3 %copy-start.5 = (s32[8,8,128]{2,1,0:T(8,128)S(1)}, s32[8,8,128]{2,1,0:T(8,128)}, u32[]{:S(2)}) copy-start(s32[8,8,128]{2,1,0:T(8,128)} %ids.7) | copy-start | bytes 98308
  0.0 5.3 %copy-start.3 = (f32[4,8,8,128]{3,2,1,0:T(8,128)S(1)}, f32[4,8,8,128]{3,2,1,0:T(8,128)}, u32[]{:S(2)}) copy-start(f32[4,8,8,128]{3,2,1,0:T(8,128)} %wells.7) | copy-start | bytes 393220
  0.0 5.4 %copy-start.2 = (f32[4,8,8,128]{3,2,1,0:T(8,128)S(1)}, f32[4,8,8,128]{3,2,1,0:T(8,128)}, u32[]{:S(2)}) copy-start(f32[4,8,8,128]{3,2,1,0:T(8,128)} %diagonal.7) | copy-start | bytes 393220
  0.0 5.4 %copy-start = (f32[6,4,8,8,128]{4,3,2,1,0:T(8,128)S(1)}, f32[6,4,8,8,128]{4,3,2,1,0:T(8,128)}, u32[]{:S(2)}) copy-start(f32[6,4,8,8,128]{4,3,2,1,0:T(8,128)} %couplings.7) | copy-start | bytes 2359300
  0.0 5.4 %copy-start.1 = (f32[4,2,8,8,128]{4,3,2,1,0:T(8,128)S(1)}, f32[4,2,8,8,128]{4,3,2,1,0:T(8,128)}, u32[]{:S(2)}) copy-start(f32[4,2,8,8,128]{4,3,2,1,0:T(8,128)} %guess_in.1) | copy-start | bytes 786436
  0.0 5.4 %copy-start.4 = (f32[4,2,8,8,128]{4,3,2,1,0:T(8,128)S(1)}, f32[4,2,8,8,128]{4,3,2,1,0:T(8,128)}, u32[]{:S(2)}) copy-start(f32[4,2,8,8,128]{4,3,2,1,0:T(8,128)} %right.3) | copy-start | bytes 786436
  1.6 7.0 %collective-permute-start = (f32[37,8,128]{2,1,0:T(8,128)S(1)}, f32[37,8,128]{2,1,0:T(8,128)S(1)}, u32[]{:S(2)}, u32[]{:S(2)}) collective-permute-start(f32[37,8,128]{2,1,0:T(8,128)S(1)} %get-tuple-element.33), channel_id=1, source_target_pairs={{0,8},{8,0},{16,24},{24,16},{1,9},{9,1},{17,25},{25,17},{2,10},{10... | collective-permute-start | bytes 454664 | tf_op jit(solution)/shard_map/ppermute | solution.py:823
  4.7 10.0 %collective-permute-start.1 = (f32[37,8,128]{2,1,0:T(8,128)S(1)}, f32[37,8,128]{2,1,0:T(8,128)S(1)}, u32[]{:S(2)}, u32[]{:S(2)}) collective-permute-start(f32[37,8,128]{2,1,0:T(8,128)S(1)} %get-tuple-element.34), channel_id=1, source_target_pairs={{8,16},{16,8},{9,17},{17,9},{10,18},{18,10},{11,19},{19,11},{12,20... | collective-permute-start | bytes 454664 | tf_op jit(solution)/shard_map/ppermute | solution.py:823
  8.6 14.3 %all-to-all-start = ((f32[32,6,128]{2,1,0:T(8,128)}), f32[32,6,128]{2,1,0:T(8,128)S(1)}, u32[]{:S(2)}, u32[]{:S(2)}) async-start(f32[32,6,128]{2,1,0:T(8,128)} %shard_map.67), calls=%async_computation | async-start | bytes 262144 | tf_op jit(solution)/shard_map/all_to_all | solution.py:831
  14.8 4.2 %collective-permute-start.3 = (f32[41,8,128]{2,1,0:T(8,128)S(1)}, f32[41,8,128]{2,1,0:T(8,128)S(1)}, u32[]{:S(2)}, u32[]{:S(2)}) collective-permute-start(f32[41,8,128]{2,1,0:T(8,128)S(1)} %get-tuple-element.38), channel_id=1, source_target_pairs={{1,2},{2,1},{3,4},{4,3},{5,6},{6,5},{9,10},{10,9},{11,12},{12,11},... | collective-permute-start | bytes 503816 | tf_op jit(solution)/shard_map/ppermute | solution.py:823
  15.4 4.2 %collective-permute-start.2 = (f32[41,8,128]{2,1,0:T(8,128)S(1)}, f32[41,8,128]{2,1,0:T(8,128)S(1)}, u32[]{:S(2)}, u32[]{:S(2)}) collective-permute-start(f32[41,8,128]{2,1,0:T(8,128)S(1)} %get-tuple-element.37.sent_face), channel_id=1, source_target_pairs={{0,1},{1,0},{2,3},{3,2},{4,5},{5,4},{6,7},{7,6},{8,9},{9,8},{10,11... | collective-permute-start | bytes 503816 | tf_op jit(solution)/shard_map/ppermute | solution.py:823
  26.5 16.1 %all-to-all-start.1 = ((f32[32,16,128]{2,1,0:T(8,128)}), f32[32,16,128]{2,1,0:T(8,128)S(1)}, u32[]{:S(2)}, u32[]{:S(2)}) async-start(f32[32,16,128]{2,1,0:T(8,128)} %shard_map.70), calls=%async_computation.1 | async-start | bytes 524288 | tf_op jit(solution)/shard_map/all_to_all | solution.py:831
  32.0 6.7 %collective-permute-start.7 = (f32[19,8,128]{2,1,0:T(8,128)S(1)}, f32[19,8,128]{2,1,0:T(8,128)S(1)}, u32[]{:S(2)}, u32[]{:S(2)}) collective-permute-start(f32[19,8,128]{2,1,0:T(8,128)S(1)} %get-tuple-element.48), channel_id=1, source_target_pairs={{1,2},{2,1},{3,4},{4,3},{5,6},{6,5},{9,10},{10,9},{11,12},{12,11},... | collective-permute-start | bytes 233480 | tf_op jit(solution)/shard_map/ppermute | solution.py:823
  32.7 6.0 %collective-permute-start.4 = (f32[18,8,128]{2,1,0:T(8,128)S(1)}, f32[18,8,128]{2,1,0:T(8,128)S(1)}, u32[]{:S(2)}, u32[]{:S(2)}) collective-permute-start(f32[18,8,128]{2,1,0:T(8,128)S(1)} %get-tuple-element.45), channel_id=1, source_target_pairs={{0,8},{8,0},{16,24},{24,16},{1,9},{9,1},{17,25},{25,17},{2,10},{10... | collective-permute-start | bytes 221192 | tf_op jit(solution)/shard_map/ppermute | solution.py:823
  34.6 4.2 %collective-permute-start.5 = (f32[17,8,128]{2,1,0:T(8,128)S(1)}, f32[17,8,128]{2,1,0:T(8,128)S(1)}, u32[]{:S(2)}, u32[]{:S(2)}) collective-permute-start(f32[17,8,128]{2,1,0:T(8,128)S(1)} %get-tuple-element.46), channel_id=1, source_target_pairs={{8,16},{16,8},{9,17},{17,9},{10,18},{18,10},{11,19},{19,11},{12,20... | collective-permute-start | bytes 208904 | tf_op jit(solution)/shard_map/ppermute | solution.py:823
  35.2 3.5 %collective-permute-start.6 = (f32[16,8,128]{2,1,0:T(8,128)S(1)}, f32[16,8,128]{2,1,0:T(8,128)S(1)}, u32[]{:S(2)}, u32[]{:S(2)}) collective-permute-start(f32[16,8,128]{2,1,0:T(8,128)S(1)} %get-tuple-element.47), channel_id=1, source_target_pairs={{0,1},{1,0},{2,3},{3,2},{4,5},{5,4},{6,7},{7,6},{8,9},{9,8},{10,11... | collective-permute-start | bytes 196616 | tf_op jit(solution)/shard_map/ppermute | solution.py:823

commit v22 on v19

--- a/solution.py
+++ b/solution.py
@@ -17,7 +17,7 @@
 LAT_UP, LAT_DOWN, RISE, FALL, DIAGONAL, BACK_IN = 0, 4, 8, 12, 16, 20
 LAYER_BLOCKS = 24
 IMAGE_PLANES = 16
-TABLE_ROWS = 6
+TABLE_ROWS = 4
 GRAM_ENTRIES = 10
 CORNER_ROWS = 19
 SIDE_IN, SIDE_EQ, SIDE_ID, SIDE_GUESS = 4, 8, 10, 11

time: 58.8 us -> 58.6 us (level)
  waiting for transfers between devices: 6.91 us -> 10.6 us
  starting transfers between devices: 27.6 us -> 24 us
    all_to_all x2, starting transfers between devices: 11.8 us -> 5.66 us  [exchanged(): return lax.all_to_all(part, ('gx', 'gy'), 0, 0, tiled=True)]
    all_to_all x2, waiting for transfers between devices: 4.65 us -> 8.54 us  [exchanged(): return lax.all_to_all(part, ('gx', 'gy'), 0, 0, tiled=True)]
    ppermute x8, starting transfers between devices: 15.8 us -> 18.3 us  [swap(): return lax.ppermute(value, axis, pairs) if pairs else jnp.zeros_like(value)]
  transfers between devices with their start and end apart: 10 -> 10, of which waited for: 5 -> 4; matrix products, arithmetic and copies ran while one was open for 0% -> 0% of each run, Pallas kernels for 5% -> 5%
where the time goes in v22:
time: 58.6 us; the launch traced here: 58.3 us
  starting transfers between devices  24 us (41%)
  Pallas kernels  12.5 us (21%)
  blocking collectives  11.1 us (19%)
  waiting for transfers between devices  10.6 us (18%)
    ppermute x8, starting transfers between devices, swap(): return lax.ppermute(value, axis, pairs) if pairs else jnp.zeros_like(value)  18.3 us
    pallas_call x8, Pallas kernels, call(): pl.pallas_call(kernel, out_shape=outs, in_specs=[place(*numbered) for num...  12.5 us
    all_to_all x1, blocking collectives, exchanged(): return lax.all_to_all(part, ('gx', 'gy'), 0, 0, tiled=True)  11.1 us
    all_to_all x2, waiting for transfers between devices, exchanged(): return lax.all_to_all(part, ('gx', 'gy'), 0, 0, tiled=True)  8.54 us
    all_to_all x2, starting transfers between devices, exchanged(): return lax.all_to_all(part, ('gx', 'gy'), 0, 0, tiled=True)  5.66 us
    ppermute x8, waiting for transfers between devices, swap(): return lax.ppermute(value, axis, pairs) if pairs else jnp.zeros_like(value)  2.07 us
  transfers between devices with their start and end apart: 10, of which 4 were waited for; matrix products, arithmetic and copies ran while one was open for 0% of the time, Pallas kernels for 5%

profile of v22, /device:TPU:0, one launch (start us, length us, event | category | flops | bytes accessed | tf_op | source)
XLA Modules:
  0.0 58.3 jit_solution(5507872608868527273)
XLA Ops:
  0.0 0.0 copy-start.5
  0.0 0.0 copy-start.3
  0.0 0.0 copy-start.2
  0.0 0.0 copy-start
  0.0 0.0 copy-start.1
  0.0 0.0 copy-start.4
  0.0 1.5 %shard_map.65 = (f32[37,8,128]{2,1,0:T(8,128)S(1)}, f32[38,8,128]{2,1,0:T(8,128)S(1)}) custom-call(f32[6,4,8,8,128]{4,3,2,1,0:T(8,128)} %couplings.7, f32[4,8,8,128]{3,2,1,0:T(8,128)} %diagonal.7, f32[4,8,8,128]{3,2,1,0:T(8,128)} %wells.7, s32[8,8,128]{2,1,0:T(8,128)} %ids.7, f32[4,2,8,8,128]{4,3,2,1,0:T(8,128)} %right.3, f32[4,2,8,8,128]{4,3,2,1,0:T(8,128)} %guess_in.1), custom_call_target="tpu_custom_call" | custom-call | tf_op jit(solution)/shard_map/pallas_call | solution.py:785
  1.6 0.7 %collective-permute-start.1 = (f32[38,8,128]{2,1,0:T(8,128)S(1)}, f32[38,8,128]{2,1,0:T(8,128)S(1)}, u32[]{:S(2)}, u32[]{:S(2)}) collective-permute-start(f32[38,8,128]{2,1,0:T(8,128)S(1)} %get-tuple-element.34), channel_id=1, source_target_pairs={{8,16},{16,8},{9,17},{17,9},{10,18},{18,10},{11,19},{19,11},{12,20... | collective-permute-start | bytes 466952 | tf_op jit(solution)/shard_map/ppermute | solution.py:823
  2.2 5.9 %collective-permute-start = (f32[37,8,128]{2,1,0:T(8,128)S(1)}, f32[37,8,128]{2,1,0:T(8,128)S(1)}, u32[]{:S(2)}, u32[]{:S(2)}) collective-permute-start(f32[37,8,128]{2,1,0:T(8,128)S(1)} %get-tuple-element.33), channel_id=1, source_target_pairs={{0,8},{8,0},{16,24},{24,16},{1,9},{9,1},{17,25},{25,17},{2,10},{10... | collective-permute-start | bytes 454664 | tf_op jit(solution)/shard_map/ppermute | solution.py:823
  8.2 0.0 copy-done.5
  8.2 0.0 copy-done.3
  8.2 0.0 copy-done.2
  8.2 0.0 copy-done
  8.2 0.0 copy-done.1
  8.2 0.0 copy-done.4
  8.2 2.5 %shard_map.64 = (f32[32,4,128]{2,1,0:T(4,128)}, s32[48]{0:T(128)S(1)}, f32[36,8,128]{2,1,0:T(8,128)S(1)}, f32[36,8,128]{2,1,0:T(8,128)S(1)}) custom-call(f32[6,4,8,8,128]{4,3,2,1,0:T(8,128)S(1)} %copy-done, f32[4,8,8,128]{3,2,1,0:T(8,128)S(1)} %copy-done.2, f32[4,8,8,128]{3,2,1,0:T(8,128)S(1)} %copy-done.3, s32[8,8,128]{2,1,0:T(8,128)S(1)} %copy-done.5, ...), custom_call_target="tpu_custom_call" | custom-call | flops 4194304 | bytes 4194304 | tf_op jit(solution)/shard_map/pallas_call | solution.py:785
  10.7 1.1 %collective-permute-done.came_first.rest_0_ = f32[37,8,128]{2,1,0:T(8,128)S(1)} collective-permute-done((f32[37,8,128]{2,1,0:T(8,128)S(1)}, f32[37,8,128]{2,1,0:T(8,128)S(1)}, u32[]{:S(2)}, u32[]{:S(2)}) %collective-permute-start) | collective-permute-done | bytes 151584 | tf_op jit(solution)/shard_map/ppermute | solution.py:823
  11.8 0.0 collective-permute-done.1.came_second
  11.8 0.1 shard_map.66
  11.9 0.7 %collective-permute-start.3 = (f32[41,8,128]{2,1,0:T(8,128)S(1)}, f32[41,8,128]{2,1,0:T(8,128)S(1)}, u32[]{:S(2)}, u32[]{:S(2)}) collective-permute-start(f32[41,8,128]{2,1,0:T(8,128)S(1)} %get-tuple-element.38), channel_id=1, source_target_pairs={{1,2},{2,1},{3,4},{4,3},{5,6},{6,5},{9,10},{10,9},{11,12},{12,11},... | collective-permute-start | bytes 503816 | tf_op jit(solution)/shard_map/ppermute | solution.py:823
  12.6 2.9 %collective-permute-start.2 = (f32[41,8,128]{2,1,0:T(8,128)S(1)}, f32[41,8,128]{2,1,0:T(8,128)S(1)}, u32[]{:S(2)}, u32[]{:S(2)}) collective-permute-start(f32[41,8,128]{2,1,0:T(8,128)S(1)} %get-tuple-element.37.sent_face), channel_id=1, source_target_pairs={{0,1},{1,0},{2,3},{3,2},{4,5},{5,4},{6,7},{7,6},{8,9},{9,8},{10,11... | collective-permute-start | bytes 503816 | tf_op jit(solution)/shard_map/ppermute | solution.py:823
  15.5 3.1 %all-to-all-start = ((f32[32,4,128]{2,1,0:T(4,128)}), f32[32,4,128]{2,1,0:T(4,128)S(1)}, u32[]{:S(2)}, u32[]{:S(2)}) async-start(f32[32,4,128]{2,1,0:T(4,128)} %shard_map.67), calls=%async_computation | async-start | bytes 131072 | tf_op jit(solution)/shard_map/all_to_all | solution.py:831
  18.6 0.3 shard_map.68
  18.9 7.1 %all-to-all-done.parts = f32[32,4,128]{2,1,0:T(4,128)S(1)} async-done(((f32[32,4,128]{2,1,0:T(4,128)}), f32[32,4,128]{2,1,0:T(4,128)S(1)}, u32[]{:S(2)}, u32[]{:S(2)}) %all-to-all-start) | async-done | bytes 65568 | tf_op jit(solution)/shard_map/all_to_all | solution.py:831
  26.0 0.0 collective-permute-done.3.came_second
  26.0 0.0 collective-permute-done.2.came_first
  26.0 1.4 %shard_map.69 = (f32[4,2,8,8,128]{4,3,2,1,0:T(8,128)S(1)}, f32[4,2,8,8,128]{4,3,2,1,0:T(8,128)S(1)}, f32[4,8,8,128]{3,2,1,0:T(8,128)S(1)}, f32[17,8,128]{2,1,0:T...) custom-call(f32[6,4,8,8,128]{4,3,2,1,0:T(8,128)S(1)} %copy-done, ...), custom_call_target="tpu_custom_call" | custom-call | tf_op jit(solution)/shard_map/pallas_call | solution.py:785
  27.4 1.9 %shard_map.70 = f32[32,16,128]{2,1,0:T(8,128)} custom-call(f32[4,8,8,128]{3,2,1,0:T(8,128)S(1)} %copy-done.3, s32[8,8,128]{2,1,0:T(8,128)S(1)} %copy-done.5, f32[4,2,8,8,128]{4,3,2,1,0:T(8,128)S(1)} %get-tuple-element.42.residual, f32[4,2,8,8,128]{4,3,2,1,0:T(8,128)S(1)} %get-tuple-element.49.image, s32[48]{0:T(128)S(1)} %get-tuple-element.51.present), custom_call_target="tpu_custom_call" | custom-call | flops 4194304 | bytes 4194304 | tf_op jit(solution)/shard_map/pallas_call | solution.py:785
  29.3 2.6 %all-to-all-start.1 = ((f32[32,16,128]{2,1,0:T(8,128)}), f32[32,16,128]{2,1,0:T(8,128)S(1)}, u32[]{:S(2)}, u32[]{:S(2)}) async-start(f32[32,16,128]{2,1,0:T(8,128)} %shard_map.70), calls=%async_computation.1 | async-start | bytes 524288 | tf_op jit(solution)/shard_map/all_to_all | solution.py:831
  32.0 0.7 %collective-permute-start.7 = (f32[19,8,128]{2,1,0:T(8,128)S(1)}, f32[19,8,128]{2,1,0:T(8,128)S(1)}, u32[]{:S(2)}, u32[]{:S(2)}) collective-permute-start(f32[19,8,128]{2,1,0:T(8,128)S(1)} %get-tuple-element.48), channel_id=1, source_target_pairs={{1,2},{2,1},{3,4},{4,3},{5,6},{6,5},{9,10},{10,9},{11,12},{12,11},... | collective-permute-start | bytes 233480 | tf_op jit(solution)/shard_map/ppermute | solution.py:823
  32.6 0.7 %collective-permute-start.5 = (f32[18,8,128]{2,1,0:T(8,128)S(1)}, f32[18,8,128]{2,1,0:T(8,128)S(1)}, u32[]{:S(2)}, u32[]{:S(2)}) collective-permute-start(f32[18,8,128]{2,1,0:T(8,128)S(1)} %get-tuple-element.46), channel_id=1, source_target_pairs={{8,16},{16,8},{9,17},{17,9},{10,18},{18,10},{11,19},{19,11},{12,20... | collective-permute-start | bytes 221192 | tf_op jit(solution)/shard_map/ppermute | solution.py:823
  33.3 4.5 %collective-permute-start.4 = (f32[17,8,128]{2,1,0:T(8,128)S(1)}, f32[17,8,128]{2,1,0:T(8,128)S(1)}, u32[]{:S(2)}, u32[]{:S(2)}) collective-permute-start(f32[17,8,128]{2,1,0:T(8,128)S(1)} %get-tuple-element.45), channel_id=1, source_target_pairs={{0,8},{8,0},{16,24},{24,16},{1,9},{9,1},{17,25},{25,17},{2,10},{10... | collective-permute-start | bytes 208904 | tf_op jit(solution)/shard_map/ppermute | solution.py:823
  37.8 2.3 %collective-permute-start.6 = (f32[16,8,128]{2,1,0:T(8,128)S(1)}, f32[16,8,128]{2,1,0:T(8,128)S(1)}, u32[]{:S(2)}, u32[]{:S(2)}) collective-permute-start(f32[16,8,128]{2,1,0:T(8,128)S(1)} %get-tuple-element.47), channel_id=1, source_target_pairs={{0,1},{1,0},{2,3},{3,2},{4,5},{5,4},{6,7},{7,6},{8,9},{9,8},{10,11... | collective-permute-start | bytes 196616 | tf_op jit(solution)/shard_map/ppermute | solution.py:823
  40.1 0.9 %collective-permute-done.6.y_first = f32[16,8,128]{2,1,0:T(8,128)S(1)} collective-permute-done((f32[16,8,128]{2,1,0:T(8,128)S(1)}, f32[16,8,128]{2,1,0:T(8,128)S(1)}, u32[]{:S(2)}, u32[]{:S(2)}) %collective-permute-start.6) | collective-permute-done | bytes 65568 | tf_op jit(solution)/shard_map/ppermute | solution.py:823
  41.0 0.0 collective-permute-done.4.x_first
  41.0 0.0 collective-permute-done.5.x_second
  41.0 0.0 collective-permute-done.7.y_second
  41.0 1.5 %all-to-all-done.1.parts = f32[32,16,128]{2,1,0:T(8,128)S(1)} async-done(((f32[32,16,128]{2,1,0:T(8,128)}), f32[32,16,128]{2,1,0:T(8,128)S(1)}, u32[]{:S(2)}, u32[]{:S(2)}) %all-to-all-start.1) | async-done | bytes 262176 | tf_op jit(solution)/shard_map/all_to_all | solution.py:831
  42.5 2.9 %shard_map.71 = (f32[4,2,8,8,128]{4,3,2,1,0:T(8,128)S(1)}, f32[4,2,8,8,128]{4,3,2,1,0:T(8,128)S(1)}, f32[32,1,640]{2,1,0:T(1,128)S(1)}, f32[16,128]{1,0:T(8,128)S(1)}) custom-call(f32[6,4,8,8,128]{4,3,2,1,0:T(8,128)S(1)} %copy-done, f32[4,8,8,128]{3,2,1,0:T(8,128)S(1)} %copy-done.2, f32[4,8,8,128]{3,2,1,0:T(8,128)S(1)} %copy-done.3, ...), custom_call_target="tpu_custom_call" | custom-call | tf_op jit(solution)/shard_map/pallas_call | solution.py:785
  45.4 11.1 %all_to_all.15.parts = f32[32,1,640]{2,1,0:T(1,128)S(1)} all-to-all(f32[32,1,640]{2,1,0:T(1,128)S(1)} %get-tuple-element.55), channel_id=1, replica_groups=mesh['member'=1,'gx'=4,'gy'=8] {'gx','gy'}, dimensions={0} | all-to-all | bytes 163840 | tf_op jit(solution)/shard_map/all_to_all | solution.py:831
  56.5 1.9 %shard_map.72 = f32[4,2,8,8,128]{4,3,2,1,0:T(8,128)} custom-call(f32[4,2,8,8,128]{4,3,2,1,0:T(8,128)} %guess_in.1, f32[4,2,8,8,128]{4,3,2,1,0:T(8,128)S(1)} %get-tuple-element.42.residual, f32[4,2,8,8,128]{4,3,2,1,0:T(8,128)S(1)} %get-tuple-element.53.second, f32[4,2,8,8,128]{4,3,2,1,0:T(8,128)S(1)} %get-tuple-element.54.third, ...), custom_call_target="tpu_custom_call" | custom-call | tf_op jit(solution)/shard_map/pallas_call | solution.py:785
  (1 shorter events, 0.0 us)
Async XLA Ops:
  0.0 8.2 %copy-start.5 = (s32[8,8,128]{2,1,0:T(8,128)S(1)}, s32[8,8,128]{2,1,0:T(8,128)}, u32[]{:S(2)}) copy-start(s32[8,8,128]{2,1,0:T(8,128)} %ids.7) | copy-start | bytes 98308
  0.0 8.2 %copy-start.3 = (f32[4,8,8,128]{3,2,1,0:T(8,128)S(1)}, f32[4,8,8,128]{3,2,1,0:T(8,128)}, u32[]{:S(2)}) copy-start(f32[4,8,8,128]{3,2,1,0:T(8,128)} %wells.7) | copy-start | bytes 393220
  0.0 8.2 %copy-start.2 = (f32[4,8,8,128]{3,2,1,0:T(8,128)S(1)}, f32[4,8,8,128]{3,2,1,0:T(8,128)}, u32[]{:S(2)}) copy-start(f32[4,8,8,128]{3,2,1,0:T(8,128)} %diagonal.7) | copy-start | bytes 393220
  0.0 8.2 %copy-start = (f32[6,4,8,8,128]{4,3,2,1,0:T(8,128)S(1)}, f32[6,4,8,8,128]{4,3,2,1,0:T(8,128)}, u32[]{:S(2)}) copy-start(f32[6,4,8,8,128]{4,3,2,1,0:T(8,128)} %couplings.7) | copy-start | bytes 2359300
  0.0 8.2 %copy-start.1 = (f32[4,2,8,8,128]{4,3,2,1,0:T(8,128)S(1)}, f32[4,2,8,8,128]{4,3,2,1,0:T(8,128)}, u32[]{:S(2)}) copy-start(f32[4,2,8,8,128]{4,3,2,1,0:T(8,128)} %guess_in.1) | copy-start | bytes 786436
  0.0 8.2 %copy-start.4 = (f32[4,2,8,8,128]{4,3,2,1,0:T(8,128)S(1)}, f32[4,2,8,8,128]{4,3,2,1,0:T(8,128)}, u32[]{:S(2)}) copy-start(f32[4,2,8,8,128]{4,3,2,1,0:T(8,128)} %right.3) | copy-start | bytes 786436
  1.6 10.3 %collective-permute-start.1 = (f32[38,8,128]{2,1,0:T(8,128)S(1)}, f32[38,8,128]{2,1,0:T(8,128)S(1)}, u32[]{:S(2)}, u32[]{:S(2)}) collective-permute-start(f32[38,8,128]{2,1,0:T(8,128)S(1)} %get-tuple-element.34), channel_id=1, source_target_pairs={{8,16},{16,8},{9,17},{17,9},{10,18},{18,10},{11,19},{19,11},{12,20... | collective-permute-start | bytes 466952 | tf_op jit(solution)/shard_map/ppermute | solution.py:823
  2.2 9.6 %collective-permute-start = (f32[37,8,128]{2,1,0:T(8,128)S(1)}, f32[37,8,128]{2,1,0:T(8,128)S(1)}, u32[]{:S(2)}, u32[]{:S(2)}) collective-permute-start(f32[37,8,128]{2,1,0:T(8,128)S(1)} %get-tuple-element.33), channel_id=1, source_target_pairs={{0,8},{8,0},{16,24},{24,16},{1,9},{9,1},{17,25},{25,17},{2,10},{10... | collective-permute-start | bytes 454664 | tf_op jit(solution)/shard_map/ppermute | solution.py:823
  11.9 14.1 %collective-permute-start.3 = (f32[41,8,128]{2,1,0:T(8,128)S(1)}, f32[41,8,128]{2,1,0:T(8,128)S(1)}, u32[]{:S(2)}, u32[]{:S(2)}) collective-permute-start(f32[41,8,128]{2,1,0:T(8,128)S(1)} %get-tuple-element.38), channel_id=1, source_target_pairs={{1,2},{2,1},{3,4},{4,3},{5,6},{6,5},{9,10},{10,9},{11,12},{12,11},... | collective-permute-start | bytes 503816 | tf_op jit(solution)/shard_map/ppermute | solution.py:823
  12.6 13.4 %collective-permute-start.2 = (f32[41,8,128]{2,1,0:T(8,128)S(1)}, f32[41,8,128]{2,1,0:T(8,128)S(1)}, u32[]{:S(2)}, u32[]{:S(2)}) collective-permute-start(f32[41,8,128]{2,1,0:T(8,128)S(1)} %get-tuple-element.37.sent_face), channel_id=1, source_target_pairs={{0,1},{1,0},{2,3},{3,2},{4,5},{5,4},{6,7},{7,6},{8,9},{9,8},{10,11... | collective-permute-start | bytes 503816 | tf_op jit(solution)/shard_map/ppermute | solution.py:823
  15.5 10.5 %all-to-all-start = ((f32[32,4,128]{2,1,0:T(4,128)}), f32[32,4,128]{2,1,0:T(4,128)S(1)}, u32[]{:S(2)}, u32[]{:S(2)}) async-start(f32[32,4,128]{2,1,0:T(4,128)} %shard_map.67), calls=%async_computation | async-start | bytes 131072 | tf_op jit(solution)/shard_map/all_to_all | solution.py:831
  29.3 13.1 %all-to-all-start.1 = ((f32[32,16,128]{2,1,0:T(8,128)}), f32[32,16,128]{2,1,0:T(8,128)S(1)}, u32[]{:S(2)}, u32[]{:S(2)}) async-start(f32[32,16,128]{2,1,0:T(8,128)} %shard_map.70), calls=%async_computation.1 | async-start | bytes 524288 | tf_op jit(solution)/shard_map/all_to_all | solution.py:831
  32.0 9.1 %collective-permute-start.7 = (f32[19,8,128]{2,1,0:T(8,128)S(1)}, f32[19,8,128]{2,1,0:T(8,128)S(1)}, u32[]{:S(2)}, u32[]{:S(2)}) collective-permute-start(f32[19,8,128]{2,1,0:T(8,128)S(1)} %get-tuple-element.48), channel_id=1, source_target_pairs={{1,2},{2,1},{3,4},{4,3},{5,6},{6,5},{9,10},{10,9},{11,12},{12,11},... | collective-permute-start | bytes 233480 | tf_op jit(solution)/shard_map/ppermute | solution.py:823
  32.6 8.4 %collective-permute-start.5 = (f32[18,8,128]{2,1,0:T(8,128)S(1)}, f32[18,8,128]{2,1,0:T(8,128)S(1)}, u32[]{:S(2)}, u32[]{:S(2)}) collective-permute-start(f32[18,8,128]{2,1,0:T(8,128)S(1)} %get-tuple-element.46), channel_id=1, source_target_pairs={{8,16},{16,8},{9,17},{17,9},{10,18},{18,10},{11,19},{19,11},{12,20... | collective-permute-start | bytes 221192 | tf_op jit(solution)/shard_map/ppermute | solution.py:823
  33.3 7.7 %collective-permute-start.4 = (f32[17,8,128]{2,1,0:T(8,128)S(1)}, f32[17,8,128]{2,1,0:T(8,128)S(1)}, u32[]{:S(2)}, u32[]{:S(2)}) collective-permute-start(f32[17,8,128]{2,1,0:T(8,128)S(1)} %get-tuple-element.45), channel_id=1, source_target_pairs={{0,8},{8,0},{16,24},{24,16},{1,9},{9,1},{17,25},{25,17},{2,10},{10... | collective-permute-start | bytes 208904 | tf_op jit(solution)/shard_map/ppermute | solution.py:823
  37.8 3.2 %collective-permute-start.6 = (f32[16,8,128]{2,1,0:T(8,128)S(1)}, f32[16,8,128]{2,1,0:T(8,128)S(1)}, u32[]{:S(2)}, u32[]{:S(2)}) collective-permute-start(f32[16,8,128]{2,1,0:T(8,128)S(1)} %get-tuple-element.47), channel_id=1, source_target_pairs={{0,1},{1,0},{2,3},{3,2},{4,5},{5,4},{6,7},{7,6},{8,9},{9,8},{10,11... | collective-permute-start | bytes 196616 | tf_op jit(solution)/shard_map/ppermute | solution.py:823

commit v23 on v22

--- a/solution.py
+++ b/solution.py
@@ -17,7 +17,7 @@
 LAT_UP, LAT_DOWN, RISE, FALL, DIAGONAL, BACK_IN = 0, 4, 8, 12, 16, 20
 LAYER_BLOCKS = 24
 IMAGE_PLANES = 16
-TABLE_ROWS = 4
+TABLE_ROWS = 2
 GRAM_ENTRIES = 10
 CORNER_ROWS = 19
 SIDE_IN, SIDE_EQ, SIDE_ID, SIDE_GUESS = 4, 8, 10, 11

time: 58.6 us -> 58.7 us (level)
  no operation moved by 1% of the time
where the time goes in v23:
time: 58.7 us; the launch traced here: 58.3 us
  starting transfers between devices  24 us (41%)
  Pallas kernels  12.7 us (22%)
  blocking collectives  11 us (19%)
  waiting for transfers between devices  10.4 us (18%)
    ppermute x8, starting transfers between devices, swap(): return lax.ppermute(value, axis, pairs) if pairs else jnp.zeros_like(value)  18.3 us
    pallas_call x8, Pallas kernels, call(): pl.pallas_call(kernel, out_shape=outs, in_specs=[place(*numbered) for num...  12.7 us
    all_to_all x1, blocking collectives, exchanged(): return lax.all_to_all(part, ('gx', 'gy'), 0, 0, tiled=True)  11 us
    all_to_all x2, waiting for transfers between devices, exchanged(): return lax.all_to_all(part, ('gx', 'gy'), 0, 0, tiled=True)  8.38 us
    all_to_all x2, starting transfers between devices, exchanged(): return lax.all_to_all(part, ('gx', 'gy'), 0, 0, tiled=True)  5.66 us
    ppermute x8, waiting for transfers between devices, swap(): return lax.ppermute(value, axis, pairs) if pairs else jnp.zeros_like(value)  2.02 us
  transfers between devices with their start and end apart: 10, of which 4 were waited for; matrix products, arithmetic and copies ran while one was open for 0% of the time, Pallas kernels for 5%

profile of v23, /device:TPU:0, one launch (start us, length us, event | category | flops | bytes accessed | tf_op | source)
XLA Modules:
  0.0 58.3 jit_solution(9278711983404866757)
XLA Ops:
  0.0 0.0 copy-start.5
  0.0 0.0 copy-start.3
  0.0 0.0 copy-start.2
  0.0 0.0 copy-start
  0.0 0.0 copy-start.1
  0.0 0.0 copy-start.4
  0.0 1.5 %shard_map.65 = (f32[37,8,128]{2,1,0:T(8,128)S(1)}, f32[38,8,128]{2,1,0:T(8,128)S(1)}) custom-call(f32[6,4,8,8,128]{4,3,2,1,0:T(8,128)} %couplings.7, f32[4,8,8,128]{3,2,1,0:T(8,128)} %diagonal.7, f32[4,8,8,128]{3,2,1,0:T(8,128)} %wells.7, s32[8,8,128]{2,1,0:T(8,128)} %ids.7, f32[4,2,8,8,128]{4,3,2,1,0:T(8,128)} %right.3, f32[4,2,8,8,128]{4,3,2,1,0:T(8,128)} %guess_in.1), custom_call_target="tpu_custom_call" | custom-call | tf_op jit(solution)/shard_map/pallas_call | solution.py:785
  1.6 0.7 %collective-permute-start.1 = (f32[38,8,128]{2,1,0:T(8,128)S(1)}, f32[38,8,128]{2,1,0:T(8,128)S(1)}, u32[]{:S(2)}, u32[]{:S(2)}) collective-permute-start(f32[38,8,128]{2,1,0:T(8,128)S(1)} %get-tuple-element.34), channel_id=1, source_target_pairs={{8,16},{16,8},{9,17},{17,9},{10,18},{18,10},{11,19},{19,11},{12,20... | collective-permute-start | bytes 466952 | tf_op jit(solution)/shard_map/ppermute | solution.py:823
  2.2 5.9 %collective-permute-start = (f32[37,8,128]{2,1,0:T(8,128)S(1)}, f32[37,8,128]{2,1,0:T(8,128)S(1)}, u32[]{:S(2)}, u32[]{:S(2)}) collective-permute-start(f32[37,8,128]{2,1,0:T(8,128)S(1)} %get-tuple-element.33), channel_id=1, source_target_pairs={{0,8},{8,0},{16,24},{24,16},{1,9},{9,1},{17,25},{25,17},{2,10},{10... | collective-permute-start | bytes 454664 | tf_op jit(solution)/shard_map/ppermute | solution.py:823
  8.2 0.0 copy-done.5
  8.2 0.0 copy-done.3
  8.2 0.0 copy-done.2
  8.2 0.0 copy-done
  8.2 0.0 copy-done.1
  8.2 0.0 copy-done.4
  8.2 2.5 %shard_map.64 = (f32[32,2,128]{2,1,0:T(2,128)}, s32[48]{0:T(128)S(1)}, f32[36,8,128]{2,1,0:T(8,128)S(1)}, f32[36,8,128]{2,1,0:T(8,128)S(1)}) custom-call(f32[6,4,8,8,128]{4,3,2,1,0:T(8,128)S(1)} %copy-done, f32[4,8,8,128]{3,2,1,0:T(8,128)S(1)} %copy-done.2, f32[4,8,8,128]{3,2,1,0:T(8,128)S(1)} %copy-done.3, s32[8,8,128]{2,1,0:T(8,128)S(1)} %copy-done.5, ...), custom_call_target="tpu_custom_call" | custom-call | flops 4194304 | bytes 4194304 | tf_op jit(solution)/shard_map/pallas_call | solution.py:785
  10.7 1.1 %collective-permute-done.came_first.rest_0_ = f32[37,8,128]{2,1,0:T(8,128)S(1)} collective-permute-done((f32[37,8,128]{2,1,0:T(8,128)S(1)}, f32[37,8,128]{2,1,0:T(8,128)S(1)}, u32[]{:S(2)}, u32[]{:S(2)}) %collective-permute-start) | collective-permute-done | bytes 151584 | tf_op jit(solution)/shard_map/ppermute | solution.py:823
  11.8 0.0 collective-permute-done.1.came_second
  11.8 0.1 shard_map.66
  11.9 0.7 %collective-permute-start.3 = (f32[41,8,128]{2,1,0:T(8,128)S(1)}, f32[41,8,128]{2,1,0:T(8,128)S(1)}, u32[]{:S(2)}, u32[]{:S(2)}) collective-permute-start(f32[41,8,128]{2,1,0:T(8,128)S(1)} %get-tuple-element.38), channel_id=1, source_target_pairs={{1,2},{2,1},{3,4},{4,3},{5,6},{6,5},{9,10},{10,9},{11,12},{12,11},... | collective-permute-start | bytes 503816 | tf_op jit(solution)/shard_map/ppermute | solution.py:823
  12.6 2.9 %collective-permute-start.2 = (f32[41,8,128]{2,1,0:T(8,128)S(1)}, f32[41,8,128]{2,1,0:T(8,128)S(1)}, u32[]{:S(2)}, u32[]{:S(2)}) collective-permute-start(f32[41,8,128]{2,1,0:T(8,128)S(1)} %get-tuple-element.37.sent_face), channel_id=1, source_target_pairs={{0,1},{1,0},{2,3},{3,2},{4,5},{5,4},{6,7},{7,6},{8,9},{9,8},{10,11... | collective-permute-start | bytes 503816 | tf_op jit(solution)/shard_map/ppermute | solution.py:823
  15.5 3.1 %all-to-all-start = ((f32[32,2,128]{2,1,0:T(2,128)}), f32[32,2,128]{2,1,0:T(2,128)S(1)}, u32[]{:S(2)}, u32[]{:S(2)}) async-start(f32[32,2,128]{2,1,0:T(2,128)} %shard_map.67), calls=%async_computation | async-start | bytes 65536 | tf_op jit(solution)/shard_map/all_to_all | solution.py:831
  18.6 0.3 shard_map.68
  18.9 6.9 %all-to-all-done.parts = f32[32,2,128]{2,1,0:T(2,128)S(1)} async-done(((f32[32,2,128]{2,1,0:T(2,128)}), f32[32,2,128]{2,1,0:T(2,128)S(1)}, u32[]{:S(2)}, u32[]{:S(2)}) %all-to-all-start) | async-done | bytes 32800 | tf_op jit(solution)/shard_map/all_to_all | solution.py:831
  25.8 0.0 collective-permute-done.3.came_second
  25.8 0.0 collective-permute-done.2.came_first
  25.8 1.4 %shard_map.69 = (f32[4,2,8,8,128]{4,3,2,1,0:T(8,128)S(1)}, f32[4,2,8,8,128]{4,3,2,1,0:T(8,128)S(1)}, f32[4,8,8,128]{3,2,1,0:T(8,128)S(1)}, f32[17,8,128]{2,1,0:T...) custom-call(f32[6,4,8,8,128]{4,3,2,1,0:T(8,128)S(1)} %copy-done, ...), custom_call_target="tpu_custom_call" | custom-call | tf_op jit(solution)/shard_map/pallas_call | solution.py:785
  27.3 2.0 %shard_map.70 = f32[32,16,128]{2,1,0:T(8,128)} custom-call(f32[4,8,8,128]{3,2,1,0:T(8,128)S(1)} %copy-done.3, s32[8,8,128]{2,1,0:T(8,128)S(1)} %copy-done.5, f32[4,2,8,8,128]{4,3,2,1,0:T(8,128)S(1)} %get-tuple-element.42.residual, f32[4,2,8,8,128]{4,3,2,1,0:T(8,128)S(1)} %get-tuple-element.49.image, s32[48]{0:T(128)S(1)} %get-tuple-element.51.present), custom_call_target="tpu_custom_call" | custom-call | flops 4194304 | bytes 4194304 | tf_op jit(solution)/shard_map/pallas_call | solution.py:785
  29.3 2.6 %all-to-all-start.1 = ((f32[32,16,128]{2,1,0:T(8,128)}), f32[32,16,128]{2,1,0:T(8,128)S(1)}, u32[]{:S(2)}, u32[]{:S(2)}) async-start(f32[32,16,128]{2,1,0:T(8,128)} %shard_map.70), calls=%async_computation.1 | async-start | bytes 524288 | tf_op jit(solution)/shard_map/all_to_all | solution.py:831
  31.9 0.7 %collective-permute-start.7 = (f32[19,8,128]{2,1,0:T(8,128)S(1)}, f32[19,8,128]{2,1,0:T(8,128)S(1)}, u32[]{:S(2)}, u32[]{:S(2)}) collective-permute-start(f32[19,8,128]{2,1,0:T(8,128)S(1)} %get-tuple-element.48), channel_id=1, source_target_pairs={{1,2},{2,1},{3,4},{4,3},{5,6},{6,5},{9,10},{10,9},{11,12},{12,11},... | collective-permute-start | bytes 233480 | tf_op jit(solution)/shard_map/ppermute | solution.py:823
  32.6 0.7 %collective-permute-start.5 = (f32[18,8,128]{2,1,0:T(8,128)S(1)}, f32[18,8,128]{2,1,0:T(8,128)S(1)}, u32[]{:S(2)}, u32[]{:S(2)}) collective-permute-start(f32[18,8,128]{2,1,0:T(8,128)S(1)} %get-tuple-element.46), channel_id=1, source_target_pairs={{8,16},{16,8},{9,17},{17,9},{10,18},{18,10},{11,19},{19,11},{12,20... | collective-permute-start | bytes 221192 | tf_op jit(solution)/shard_map/ppermute | solution.py:823
  33.3 4.5 %collective-permute-start.4 = (f32[17,8,128]{2,1,0:T(8,128)S(1)}, f32[17,8,128]{2,1,0:T(8,128)S(1)}, u32[]{:S(2)}, u32[]{:S(2)}) collective-permute-start(f32[17,8,128]{2,1,0:T(8,128)S(1)} %get-tuple-element.45), channel_id=1, source_target_pairs={{0,8},{8,0},{16,24},{24,16},{1,9},{9,1},{17,25},{25,17},{2,10},{10... | collective-permute-start | bytes 208904 | tf_op jit(solution)/shard_map/ppermute | solution.py:823
  37.8 2.3 %collective-permute-start.6 = (f32[16,8,128]{2,1,0:T(8,128)S(1)}, f32[16,8,128]{2,1,0:T(8,128)S(1)}, u32[]{:S(2)}, u32[]{:S(2)}) collective-permute-start(f32[16,8,128]{2,1,0:T(8,128)S(1)} %get-tuple-element.47), channel_id=1, source_target_pairs={{0,1},{1,0},{2,3},{3,2},{4,5},{5,4},{6,7},{7,6},{8,9},{9,8},{10,11... | collective-permute-start | bytes 196616 | tf_op jit(solution)/shard_map/ppermute | solution.py:823
  40.1 0.9 %collective-permute-done.6.y_first = f32[16,8,128]{2,1,0:T(8,128)S(1)} collective-permute-done((f32[16,8,128]{2,1,0:T(8,128)S(1)}, f32[16,8,128]{2,1,0:T(8,128)S(1)}, u32[]{:S(2)}, u32[]{:S(2)}) %collective-permute-start.6) | collective-permute-done | bytes 65568 | tf_op jit(solution)/shard_map/ppermute | solution.py:823
  41.0 0.0 collective-permute-done.4.x_first
  41.0 0.0 collective-permute-done.5.x_second
  41.0 0.0 collective-permute-done.7.y_second
  41.0 1.5 %all-to-all-done.1.parts = f32[32,16,128]{2,1,0:T(8,128)S(1)} async-done(((f32[32,16,128]{2,1,0:T(8,128)}), f32[32,16,128]{2,1,0:T(8,128)S(1)}, u32[]{:S(2)}, u32[]{:S(2)}) %all-to-all-start.1) | async-done | bytes 262176 | tf_op jit(solution)/shard_map/all_to_all | solution.py:831
  42.4 3.0 %shard_map.71 = (f32[4,2,8,8,128]{4,3,2,1,0:T(8,128)S(1)}, f32[4,2,8,8,128]{4,3,2,1,0:T(8,128)S(1)}, f32[32,1,640]{2,1,0:T(1,128)S(1)}, f32[16,128]{1,0:T(8,128)S(1)}) custom-call(f32[6,4,8,8,128]{4,3,2,1,0:T(8,128)S(1)} %copy-done, f32[4,8,8,128]{3,2,1,0:T(8,128)S(1)} %copy-done.2, f32[4,8,8,128]{3,2,1,0:T(8,128)S(1)} %copy-done.3, ...), custom_call_target="tpu_custom_call" | custom-call | tf_op jit(solution)/shard_map/pallas_call | solution.py:785
  45.4 11.0 %all_to_all.15.parts = f32[32,1,640]{2,1,0:T(1,128)S(1)} all-to-all(f32[32,1,640]{2,1,0:T(1,128)S(1)} %get-tuple-element.55), channel_id=1, replica_groups=mesh['member'=1,'gx'=4,'gy'=8] {'gx','gy'}, dimensions={0} | all-to-all | bytes 163840 | tf_op jit(solution)/shard_map/all_to_all | solution.py:831
  56.4 1.9 %shard_map.72 = f32[4,2,8,8,128]{4,3,2,1,0:T(8,128)} custom-call(f32[4,2,8,8,128]{4,3,2,1,0:T(8,128)} %guess_in.1, f32[4,2,8,8,128]{4,3,2,1,0:T(8,128)S(1)} %get-tuple-element.42.residual, f32[4,2,8,8,128]{4,3,2,1,0:T(8,128)S(1)} %get-tuple-element.53.second, f32[4,2,8,8,128]{4,3,2,1,0:T(8,128)S(1)} %get-tuple-element.54.third, ...), custom_call_target="tpu_custom_call" | custom-call | tf_op jit(solution)/shard_map/pallas_call | solution.py:785
  (1 shorter events, 0.0 us)
Async XLA Ops:
  0.0 8.2 %copy-start.5 = (s32[8,8,128]{2,1,0:T(8,128)S(1)}, s32[8,8,128]{2,1,0:T(8,128)}, u32[]{:S(2)}) copy-start(s32[8,8,128]{2,1,0:T(8,128)} %ids.7) | copy-start | bytes 98308
  0.0 8.2 %copy-start.3 = (f32[4,8,8,128]{3,2,1,0:T(8,128)S(1)}, f32[4,8,8,128]{3,2,1,0:T(8,128)}, u32[]{:S(2)}) copy-start(f32[4,8,8,128]{3,2,1,0:T(8,128)} %wells.7) | copy-start | bytes 393220
  0.0 8.2 %copy-start.2 = (f32[4,8,8,128]{3,2,1,0:T(8,128)S(1)}, f32[4,8,8,128]{3,2,1,0:T(8,128)}, u32[]{:S(2)}) copy-start(f32[4,8,8,128]{3,2,1,0:T(8,128)} %diagonal.7) | copy-start | bytes 393220
  0.0 8.2 %copy-start = (f32[6,4,8,8,128]{4,3,2,1,0:T(8,128)S(1)}, f32[6,4,8,8,128]{4,3,2,1,0:T(8,128)}, u32[]{:S(2)}) copy-start(f32[6,4,8,8,128]{4,3,2,1,0:T(8,128)} %couplings.7) | copy-start | bytes 2359300
  0.0 8.2 %copy-start.1 = (f32[4,2,8,8,128]{4,3,2,1,0:T(8,128)S(1)}, f32[4,2,8,8,128]{4,3,2,1,0:T(8,128)}, u32[]{:S(2)}) copy-start(f32[4,2,8,8,128]{4,3,2,1,0:T(8,128)} %guess_in.1) | copy-start | bytes 786436
  0.0 8.2 %copy-start.4 = (f32[4,2,8,8,128]{4,3,2,1,0:T(8,128)S(1)}, f32[4,2,8,8,128]{4,3,2,1,0:T(8,128)}, u32[]{:S(2)}) copy-start(f32[4,2,8,8,128]{4,3,2,1,0:T(8,128)} %right.3) | copy-start | bytes 786436
  1.6 10.3 %collective-permute-start.1 = (f32[38,8,128]{2,1,0:T(8,128)S(1)}, f32[38,8,128]{2,1,0:T(8,128)S(1)}, u32[]{:S(2)}, u32[]{:S(2)}) collective-permute-start(f32[38,8,128]{2,1,0:T(8,128)S(1)} %get-tuple-element.34), channel_id=1, source_target_pairs={{8,16},{16,8},{9,17},{17,9},{10,18},{18,10},{11,19},{19,11},{12,20... | collective-permute-start | bytes 466952 | tf_op jit(solution)/shard_map/ppermute | solution.py:823
  2.2 9.6 %collective-permute-start = (f32[37,8,128]{2,1,0:T(8,128)S(1)}, f32[37,8,128]{2,1,0:T(8,128)S(1)}, u32[]{:S(2)}, u32[]{:S(2)}) collective-permute-start(f32[37,8,128]{2,1,0:T(8,128)S(1)} %get-tuple-element.33), channel_id=1, source_target_pairs={{0,8},{8,0},{16,24},{24,16},{1,9},{9,1},{17,25},{25,17},{2,10},{10... | collective-permute-start | bytes 454664 | tf_op jit(solution)/shard_map/ppermute | solution.py:823
  11.9 13.9 %collective-permute-start.3 = (f32[41,8,128]{2,1,0:T(8,128)S(1)}, f32[41,8,128]{2,1,0:T(8,128)S(1)}, u32[]{:S(2)}, u32[]{:S(2)}) collective-permute-start(f32[41,8,128]{2,1,0:T(8,128)S(1)} %get-tuple-element.38), channel_id=1, source_target_pairs={{1,2},{2,1},{3,4},{4,3},{5,6},{6,5},{9,10},{10,9},{11,12},{12,11},... | collective-permute-start | bytes 503816 | tf_op jit(solution)/shard_map/ppermute | solution.py:823
  12.6 13.2 %collective-permute-start.2 = (f32[41,8,128]{2,1,0:T(8,128)S(1)}, f32[41,8,128]{2,1,0:T(8,128)S(1)}, u32[]{:S(2)}, u32[]{:S(2)}) collective-permute-start(f32[41,8,128]{2,1,0:T(8,128)S(1)} %get-tuple-element.37.sent_face), channel_id=1, source_target_pairs={{0,1},{1,0},{2,3},{3,2},{4,5},{5,4},{6,7},{7,6},{8,9},{9,8},{10,11... | collective-permute-start | bytes 503816 | tf_op jit(solution)/shard_map/ppermute | solution.py:823
  15.5 10.3 %all-to-all-start = ((f32[32,2,128]{2,1,0:T(2,128)}), f32[32,2,128]{2,1,0:T(2,128)S(1)}, u32[]{:S(2)}, u32[]{:S(2)}) async-start(f32[32,2,128]{2,1,0:T(2,128)} %shard_map.67), calls=%async_computation | async-start | bytes 65536 | tf_op jit(solution)/shard_map/all_to_all | solution.py:831
  29.3 13.1 %all-to-all-start.1 = ((f32[32,16,128]{2,1,0:T(8,128)}), f32[32,16,128]{2,1,0:T(8,128)S(1)}, u32[]{:S(2)}, u32[]{:S(2)}) async-start(f32[32,16,128]{2,1,0:T(8,128)} %shard_map.70), calls=%async_computation.1 | async-start | bytes 524288 | tf_op jit(solution)/shard_map/all_to_all | solution.py:831
  31.9 9.1 %collective-permute-start.7 = (f32[19,8,128]{2,1,0:T(8,128)S(1)}, f32[19,8,128]{2,1,0:T(8,128)S(1)}, u32[]{:S(2)}, u32[]{:S(2)}) collective-permute-start(f32[19,8,128]{2,1,0:T(8,128)S(1)} %get-tuple-element.48), channel_id=1, source_target_pairs={{1,2},{2,1},{3,4},{4,3},{5,6},{6,5},{9,10},{10,9},{11,12},{12,11},... | collective-permute-start | bytes 233480 | tf_op jit(solution)/shard_map/ppermute | solution.py:823
  32.6 8.4 %collective-permute-start.5 = (f32[18,8,128]{2,1,0:T(8,128)S(1)}, f32[18,8,128]{2,1,0:T(8,128)S(1)}, u32[]{:S(2)}, u32[]{:S(2)}) collective-permute-start(f32[18,8,128]{2,1,0:T(8,128)S(1)} %get-tuple-element.46), channel_id=1, source_target_pairs={{8,16},{16,8},{9,17},{17,9},{10,18},{18,10},{11,19},{19,11},{12,20... | collective-permute-start | bytes 221192 | tf_op jit(solution)/shard_map/ppermute | solution.py:823
  33.3 7.7 %collective-permute-start.4 = (f32[17,8,128]{2,1,0:T(8,128)S(1)}, f32[17,8,128]{2,1,0:T(8,128)S(1)}, u32[]{:S(2)}, u32[]{:S(2)}) collective-permute-start(f32[17,8,128]{2,1,0:T(8,128)S(1)} %get-tuple-element.45), channel_id=1, source_target_pairs={{0,8},{8,0},{16,24},{24,16},{1,9},{9,1},{17,25},{25,17},{2,10},{10... | collective-permute-start | bytes 208904 | tf_op jit(solution)/shard_map/ppermute | solution.py:823
  37.8 3.2 %collective-permute-start.6 = (f32[16,8,128]{2,1,0:T(8,128)S(1)}, f32[16,8,128]{2,1,0:T(8,128)S(1)}, u32[]{:S(2)}, u32[]{:S(2)}) collective-permute-start(f32[16,8,128]{2,1,0:T(8,128)S(1)} %get-tuple-element.47), channel_id=1, source_target_pairs={{0,1},{1,0},{2,3},{3,2},{4,5},{5,4},{6,7},{7,6},{8,9},{9,8},{10,11... | collective-permute-start | bytes 196616 | tf_op jit(solution)/shard_map/ppermute | solution.py:823

commit v24 on v22

--- a/solution.py
+++ b/solution.py
@@ -862,7 +862,7 @@
         cost=4 << 20,
         out=1,
     )
-    parts = exchanged(after(part, came_x[0]))
+    parts = exchanged(part)
     y_shape = (FACE_PLANES + CORNER_PLANES,) + plane
     y_first, y_second, fxl, fxh = call(
         corner_kernel,

time: 58.6 us -> 58.8 us (level)
  Pallas kernels: 12.5 us -> 13.6 us
    pallas_call x8, Pallas kernels: 12.5 us -> 13.6 us  [call(): pl.pallas_call(kernel, out_shape=outs, in_specs=[place(*numbered) for num...]
  transfers between devices with their start and end apart: 10 -> 10, of which waited for: 4 -> 4; matrix products, arithmetic and copies ran while one was open for 0% -> 0% of each run, Pallas kernels for 5% -> 6%
where the time goes in v24:
time: 58.8 us; the launch traced here: 58.5 us
  starting transfers between devices  24 us (41%)
  Pallas kernels  13.6 us (23%)
  blocking collectives  10.6 us (18%)
  waiting for transfers between devices  10.1 us (17%)
    ppermute x8, starting transfers between devices, swap(): return lax.ppermute(value, axis, pairs) if pairs else jnp.zeros_like(value)  18.3 us
    pallas_call x8, Pallas kernels, call(): pl.pallas_call(kernel, out_shape=outs, in_specs=[place(*numbered) for num...  13.6 us
    all_to_all x1, blocking collectives, exchanged(): return lax.all_to_all(part, ('gx', 'gy'), 0, 0, tiled=True)  10.6 us
    all_to_all x2, waiting for transfers between devices, exchanged(): return lax.all_to_all(part, ('gx', 'gy'), 0, 0, tiled=True)  8.54 us
    all_to_all x2, starting transfers between devices, exchanged(): return lax.all_to_all(part, ('gx', 'gy'), 0, 0, tiled=True)  5.66 us
    ppermute x8, waiting for transfers between devices, swap(): return lax.ppermute(value, axis, pairs) if pairs else jnp.zeros_like(value)  1.61 us
  transfers between devices with their start and end apart: 10, of which 4 were waited for; matrix products, arithmetic and copies ran while one was open for 0% of the time, Pallas kernels for 6%

profile of v24, /device:TPU:0, one launch (start us, length us, event | category | flops | bytes accessed | tf_op | source)
XLA Modules:
  0.0 58.5 jit_solution(17977958235168771269)
XLA Ops:
  0.0 0.0 copy-start.5
  0.0 0.0 copy-start.3
  0.0 0.0 copy-start.2
  0.0 0.0 copy-start
  0.0 0.0 copy-start.1
  0.0 0.0 copy-start.4
  0.0 1.5 %shard_map.65 = (f32[37,8,128]{2,1,0:T(8,128)S(1)}, f32[38,8,128]{2,1,0:T(8,128)S(1)}) custom-call(f32[6,4,8,8,128]{4,3,2,1,0:T(8,128)} %couplings.7, f32[4,8,8,128]{3,2,1,0:T(8,128)} %diagonal.7, f32[4,8,8,128]{3,2,1,0:T(8,128)} %wells.7, s32[8,8,128]{2,1,0:T(8,128)} %ids.7, f32[4,2,8,8,128]{4,3,2,1,0:T(8,128)} %right.3, f32[4,2,8,8,128]{4,3,2,1,0:T(8,128)} %guess_in.1), custom_call_target="tpu_custom_call" | custom-call | tf_op jit(solution)/shard_map/pallas_call | solution.py:785
  1.6 0.7 %collective-permute-start.1 = (f32[38,8,128]{2,1,0:T(8,128)S(1)}, f32[38,8,128]{2,1,0:T(8,128)S(1)}, u32[]{:S(2)}, u32[]{:S(2)}) collective-permute-start(f32[38,8,128]{2,1,0:T(8,128)S(1)} %get-tuple-element.34), channel_id=1, source_target_pairs={{8,16},{16,8},{9,17},{17,9},{10,18},{18,10},{11,19},{19,11},{12,20... | collective-permute-start | bytes 466952 | tf_op jit(solution)/shard_map/ppermute | solution.py:823
  2.2 5.9 %collective-permute-start = (f32[37,8,128]{2,1,0:T(8,128)S(1)}, f32[37,8,128]{2,1,0:T(8,128)S(1)}, u32[]{:S(2)}, u32[]{:S(2)}) collective-permute-start(f32[37,8,128]{2,1,0:T(8,128)S(1)} %get-tuple-element.33), channel_id=1, source_target_pairs={{0,8},{8,0},{16,24},{24,16},{1,9},{9,1},{17,25},{25,17},{2,10},{10... | collective-permute-start | bytes 454664 | tf_op jit(solution)/shard_map/ppermute | solution.py:823
  8.2 0.0 copy-done.5
  8.2 0.0 copy-done.3
  8.2 0.0 copy-done.2
  8.2 0.0 copy-done
  8.2 0.0 copy-done.1
  8.2 0.0 copy-done.4
  8.2 2.9 %shard_map.64 = (f32[32,4,128]{2,1,0:T(4,128)}, s32[48]{0:T(128)S(1)}, f32[36,8,128]{2,1,0:T(8,128)S(1)}, f32[36,8,128]{2,1,0:T(8,128)S(1)}) custom-call(f32[6,4,8,8,128]{4,3,2,1,0:T(8,128)S(1)} %copy-done, f32[4,8,8,128]{3,2,1,0:T(8,128)S(1)} %copy-done.2, f32[4,8,8,128]{3,2,1,0:T(8,128)S(1)} %copy-done.3, s32[8,8,128]{2,1,0:T(8,128)S(1)} %copy-done.5, ...), custom_call_target="tpu_custom_call" | custom-call | flops 4194304 | bytes 4194304 | tf_op jit(solution)/shard_map/pallas_call | solution.py:785
  11.1 0.7 %collective-permute-done.came_first = f32[37,8,128]{2,1,0:T(8,128)S(1)} collective-permute-done((f32[37,8,128]{2,1,0:T(8,128)S(1)}, f32[37,8,128]{2,1,0:T(8,128)S(1)}, u32[]{:S(2)}, u32[]{:S(2)}) %collective-permute-start) | collective-permute-done | bytes 151584 | tf_op jit(solution)/shard_map/ppermute | solution.py:823
  11.8 0.0 collective-permute-done.1.came_second
  11.8 0.1 shard_map.66
  11.9 0.7 %collective-permute-start.3 = (f32[41,8,128]{2,1,0:T(8,128)S(1)}, f32[41,8,128]{2,1,0:T(8,128)S(1)}, u32[]{:S(2)}, u32[]{:S(2)}) collective-permute-start(f32[41,8,128]{2,1,0:T(8,128)S(1)} %get-tuple-element.38), channel_id=1, source_target_pairs={{1,2},{2,1},{3,4},{4,3},{5,6},{6,5},{9,10},{10,9},{11,12},{12,11},... | collective-permute-start | bytes 503816 | tf_op jit(solution)/shard_map/ppermute | solution.py:823
  12.6 2.9 %collective-permute-start.2 = (f32[41,8,128]{2,1,0:T(8,128)S(1)}, f32[41,8,128]{2,1,0:T(8,128)S(1)}, u32[]{:S(2)}, u32[]{:S(2)}) collective-permute-start(f32[41,8,128]{2,1,0:T(8,128)S(1)} %get-tuple-element.37.sent_face), channel_id=1, source_target_pairs={{0,1},{1,0},{2,3},{3,2},{4,5},{5,4},{6,7},{7,6},{8,9},{9,8},{10,11... | collective-permute-start | bytes 503816 | tf_op jit(solution)/shard_map/ppermute | solution.py:823
  15.5 3.1 %all-to-all-start = ((f32[32,4,128]{2,1,0:T(4,128)}), f32[32,4,128]{2,1,0:T(4,128)S(1)}, u32[]{:S(2)}, u32[]{:S(2)}) async-start(f32[32,4,128]{2,1,0:T(4,128)} %get-tuple-element.39), calls=%async_computation | async-start | bytes 131072 | tf_op jit(solution)/shard_map/all_to_all | solution.py:831
  18.6 0.3 shard_map.67
  18.9 7.1 %all-to-all-done.parts = f32[32,4,128]{2,1,0:T(4,128)S(1)} async-done(((f32[32,4,128]{2,1,0:T(4,128)}), f32[32,4,128]{2,1,0:T(4,128)S(1)}, u32[]{:S(2)}, u32[]{:S(2)}) %all-to-all-start) | async-done | bytes 65568 | tf_op jit(solution)/shard_map/all_to_all | solution.py:831
  26.0 0.0 collective-permute-done.3.came_second
  26.0 0.0 collective-permute-done.2.came_first
  26.0 1.4 %shard_map.68 = (f32[4,2,8,8,128]{4,3,2,1,0:T(8,128)S(1)}, f32[4,2,8,8,128]{4,3,2,1,0:T(8,128)S(1)}, f32[4,8,8,128]{3,2,1,0:T(8,128)S(1)}, f32[17,8,128]{2,1,0:T...) custom-call(f32[6,4,8,8,128]{4,3,2,1,0:T(8,128)S(1)} %copy-done, ...), custom_call_target="tpu_custom_call" | custom-call | tf_op jit(solution)/shard_map/pallas_call | solution.py:785
  27.4 2.3 %shard_map.69 = f32[32,16,128]{2,1,0:T(8,128)} custom-call(f32[4,8,8,128]{3,2,1,0:T(8,128)S(1)} %copy-done.3, s32[8,8,128]{2,1,0:T(8,128)S(1)} %copy-done.5, f32[4,2,8,8,128]{4,3,2,1,0:T(8,128)S(1)} %get-tuple-element.42.residual, f32[4,2,8,8,128]{4,3,2,1,0:T(8,128)S(1)} %get-tuple-element.49.image, s32[48]{0:T(128)S(1)} %get-tuple-element.51.present), custom_call_target="tpu_custom_call" | custom-call | flops 4194304 | bytes 4194304 | tf_op jit(solution)/shard_map/pallas_call | solution.py:785
  29.7 2.6 %all-to-all-start.1 = ((f32[32,16,128]{2,1,0:T(8,128)}), f32[32,16,128]{2,1,0:T(8,128)S(1)}, u32[]{:S(2)}, u32[]{:S(2)}) async-start(f32[32,16,128]{2,1,0:T(8,128)} %shard_map.69), calls=%async_computation.1 | async-start | bytes 524288 | tf_op jit(solution)/shard_map/all_to_all | solution.py:831
  32.3 0.7 %collective-permute-start.7 = (f32[19,8,128]{2,1,0:T(8,128)S(1)}, f32[19,8,128]{2,1,0:T(8,128)S(1)}, u32[]{:S(2)}, u32[]{:S(2)}) collective-permute-start(f32[19,8,128]{2,1,0:T(8,128)S(1)} %get-tuple-element.48), channel_id=1, source_target_pairs={{1,2},{2,1},{3,4},{4,3},{5,6},{6,5},{9,10},{10,9},{11,12},{12,11},... | collective-permute-start | bytes 233480 | tf_op jit(solution)/shard_map/ppermute | solution.py:823
  33.0 0.7 %collective-permute-start.5 = (f32[18,8,128]{2,1,0:T(8,128)S(1)}, f32[18,8,128]{2,1,0:T(8,128)S(1)}, u32[]{:S(2)}, u32[]{:S(2)}) collective-permute-start(f32[18,8,128]{2,1,0:T(8,128)S(1)} %get-tuple-element.46), channel_id=1, source_target_pairs={{8,16},{16,8},{9,17},{17,9},{10,18},{18,10},{11,19},{19,11},{12,20... | collective-permute-start | bytes 221192 | tf_op jit(solution)/shard_map/ppermute | solution.py:823
  33.6 4.5 %collective-permute-start.4 = (f32[17,8,128]{2,1,0:T(8,128)S(1)}, f32[17,8,128]{2,1,0:T(8,128)S(1)}, u32[]{:S(2)}, u32[]{:S(2)}) collective-permute-start(f32[17,8,128]{2,1,0:T(8,128)S(1)} %get-tuple-element.45), channel_id=1, source_target_pairs={{0,8},{8,0},{16,24},{24,16},{1,9},{9,1},{17,25},{25,17},{2,10},{10... | collective-permute-start | bytes 208904 | tf_op jit(solution)/shard_map/ppermute | solution.py:823
  38.2 2.3 %collective-permute-start.6 = (f32[16,8,128]{2,1,0:T(8,128)S(1)}, f32[16,8,128]{2,1,0:T(8,128)S(1)}, u32[]{:S(2)}, u32[]{:S(2)}) collective-permute-start(f32[16,8,128]{2,1,0:T(8,128)S(1)} %get-tuple-element.47), channel_id=1, source_target_pairs={{0,1},{1,0},{2,3},{3,2},{4,5},{5,4},{6,7},{7,6},{8,9},{9,8},{10,11... | collective-permute-start | bytes 196616 | tf_op jit(solution)/shard_map/ppermute | solution.py:823
  40.4 0.9 %collective-permute-done.6.y_first = f32[16,8,128]{2,1,0:T(8,128)S(1)} collective-permute-done((f32[16,8,128]{2,1,0:T(8,128)S(1)}, f32[16,8,128]{2,1,0:T(8,128)S(1)}, u32[]{:S(2)}, u32[]{:S(2)}) %collective-permute-start.6) | collective-permute-done | bytes 65568 | tf_op jit(solution)/shard_map/ppermute | solution.py:823
  41.3 0.0 collective-permute-done.4.x_first
  41.4 0.0 collective-permute-done.5.x_second
  41.4 0.0 collective-permute-done.7.y_second
  41.4 1.5 %all-to-all-done.1.parts = f32[32,16,128]{2,1,0:T(8,128)S(1)} async-done(((f32[32,16,128]{2,1,0:T(8,128)}), f32[32,16,128]{2,1,0:T(8,128)S(1)}, u32[]{:S(2)}, u32[]{:S(2)}) %all-to-all-start.1) | async-done | bytes 262176 | tf_op jit(solution)/shard_map/all_to_all | solution.py:831
  42.8 3.2 %shard_map.70 = (f32[4,2,8,8,128]{4,3,2,1,0:T(8,128)S(1)}, f32[4,2,8,8,128]{4,3,2,1,0:T(8,128)S(1)}, f32[32,1,640]{2,1,0:T(1,128)S(1)}, f32[16,128]{1,0:T(8,128)S(1)}) custom-call(f32[6,4,8,8,128]{4,3,2,1,0:T(8,128)S(1)} %copy-done, f32[4,8,8,128]{3,2,1,0:T(8,128)S(1)} %copy-done.2, f32[4,8,8,128]{3,2,1,0:T(8,128)S(1)} %copy-done.3, ...), custom_call_target="tpu_custom_call" | custom-call | tf_op jit(solution)/shard_map/pallas_call | solution.py:785
  46.0 10.6 %all_to_all.15.parts = f32[32,1,640]{2,1,0:T(1,128)S(1)} all-to-all(f32[32,1,640]{2,1,0:T(1,128)S(1)} %get-tuple-element.55), channel_id=1, replica_groups=mesh['member'=1,'gx'=4,'gy'=8] {'gx','gy'}, dimensions={0} | all-to-all | bytes 163840 | tf_op jit(solution)/shard_map/all_to_all | solution.py:831
  56.6 1.9 %shard_map.71 = f32[4,2,8,8,128]{4,3,2,1,0:T(8,128)} custom-call(f32[4,2,8,8,128]{4,3,2,1,0:T(8,128)} %guess_in.1, f32[4,2,8,8,128]{4,3,2,1,0:T(8,128)S(1)} %get-tuple-element.42.residual, f32[4,2,8,8,128]{4,3,2,1,0:T(8,128)S(1)} %get-tuple-element.53.second, f32[4,2,8,8,128]{4,3,2,1,0:T(8,128)S(1)} %get-tuple-element.54.third, ...), custom_call_target="tpu_custom_call" | custom-call | tf_op jit(solution)/shard_map/pallas_call | solution.py:785
Async XLA Ops:
  0.0 8.2 %copy-start.5 = (s32[8,8,128]{2,1,0:T(8,128)S(1)}, s32[8,8,128]{2,1,0:T(8,128)}, u32[]{:S(2)}) copy-start(s32[8,8,128]{2,1,0:T(8,128)} %ids.7) | copy-start | bytes 98308
  0.0 8.2 %copy-start.3 = (f32[4,8,8,128]{3,2,1,0:T(8,128)S(1)}, f32[4,8,8,128]{3,2,1,0:T(8,128)}, u32[]{:S(2)}) copy-start(f32[4,8,8,128]{3,2,1,0:T(8,128)} %wells.7) | copy-start | bytes 393220
  0.0 8.2 %copy-start.2 = (f32[4,8,8,128]{3,2,1,0:T(8,128)S(1)}, f32[4,8,8,128]{3,2,1,0:T(8,128)}, u32[]{:S(2)}) copy-start(f32[4,8,8,128]{3,2,1,0:T(8,128)} %diagonal.7) | copy-start | bytes 393220
  0.0 8.2 %copy-start = (f32[6,4,8,8,128]{4,3,2,1,0:T(8,128)S(1)}, f32[6,4,8,8,128]{4,3,2,1,0:T(8,128)}, u32[]{:S(2)}) copy-start(f32[6,4,8,8,128]{4,3,2,1,0:T(8,128)} %couplings.7) | copy-start | bytes 2359300
  0.0 8.2 %copy-start.1 = (f32[4,2,8,8,128]{4,3,2,1,0:T(8,128)S(1)}, f32[4,2,8,8,128]{4,3,2,1,0:T(8,128)}, u32[]{:S(2)}) copy-start(f32[4,2,8,8,128]{4,3,2,1,0:T(8,128)} %guess_in.1) | copy-start | bytes 786436
  0.0 8.2 %copy-start.4 = (f32[4,2,8,8,128]{4,3,2,1,0:T(8,128)S(1)}, f32[4,2,8,8,128]{4,3,2,1,0:T(8,128)}, u32[]{:S(2)}) copy-start(f32[4,2,8,8,128]{4,3,2,1,0:T(8,128)} %right.3) | copy-start | bytes 786436
  1.6 10.3 %collective-permute-start.1 = (f32[38,8,128]{2,1,0:T(8,128)S(1)}, f32[38,8,128]{2,1,0:T(8,128)S(1)}, u32[]{:S(2)}, u32[]{:S(2)}) collective-permute-start(f32[38,8,128]{2,1,0:T(8,128)S(1)} %get-tuple-element.34), channel_id=1, source_target_pairs={{8,16},{16,8},{9,17},{17,9},{10,18},{18,10},{11,19},{19,11},{12,20... | collective-permute-start | bytes 466952 | tf_op jit(solution)/shard_map/ppermute | solution.py:823
  2.2 9.6 %collective-permute-start = (f32[37,8,128]{2,1,0:T(8,128)S(1)}, f32[37,8,128]{2,1,0:T(8,128)S(1)}, u32[]{:S(2)}, u32[]{:S(2)}) collective-permute-start(f32[37,8,128]{2,1,0:T(8,128)S(1)} %get-tuple-element.33), channel_id=1, source_target_pairs={{0,8},{8,0},{16,24},{24,16},{1,9},{9,1},{17,25},{25,17},{2,10},{10... | collective-permute-start | bytes 454664 | tf_op jit(solution)/shard_map/ppermute | solution.py:823
  11.9 14.1 %collective-permute-start.3 = (f32[41,8,128]{2,1,0:T(8,128)S(1)}, f32[41,8,128]{2,1,0:T(8,128)S(1)}, u32[]{:S(2)}, u32[]{:S(2)}) collective-permute-start(f32[41,8,128]{2,1,0:T(8,128)S(1)} %get-tuple-element.38), channel_id=1, source_target_pairs={{1,2},{2,1},{3,4},{4,3},{5,6},{6,5},{9,10},{10,9},{11,12},{12,11},... | collective-permute-start | bytes 503816 | tf_op jit(solution)/shard_map/ppermute | solution.py:823
  12.6 13.4 %collective-permute-start.2 = (f32[41,8,128]{2,1,0:T(8,128)S(1)}, f32[41,8,128]{2,1,0:T(8,128)S(1)}, u32[]{:S(2)}, u32[]{:S(2)}) collective-permute-start(f32[41,8,128]{2,1,0:T(8,128)S(1)} %get-tuple-element.37.sent_face), channel_id=1, source_target_pairs={{0,1},{1,0},{2,3},{3,2},{4,5},{5,4},{6,7},{7,6},{8,9},{9,8},{10,11... | collective-permute-start | bytes 503816 | tf_op jit(solution)/shard_map/ppermute | solution.py:823
  15.5 10.5 %all-to-all-start = ((f32[32,4,128]{2,1,0:T(4,128)}), f32[32,4,128]{2,1,0:T(4,128)S(1)}, u32[]{:S(2)}, u32[]{:S(2)}) async-start(f32[32,4,128]{2,1,0:T(4,128)} %get-tuple-element.39), calls=%async_computation | async-start | bytes 131072 | tf_op jit(solution)/shard_map/all_to_all | solution.py:831
  29.7 13.1 %all-to-all-start.1 = ((f32[32,16,128]{2,1,0:T(8,128)}), f32[32,16,128]{2,1,0:T(8,128)S(1)}, u32[]{:S(2)}, u32[]{:S(2)}) async-start(f32[32,16,128]{2,1,0:T(8,128)} %shard_map.69), calls=%async_computation.1 | async-start | bytes 524288 | tf_op jit(solution)/shard_map/all_to_all | solution.py:831
  32.3 9.1 %collective-permute-start.7 = (f32[19,8,128]{2,1,0:T(8,128)S(1)}, f32[19,8,128]{2,1,0:T(8,128)S(1)}, u32[]{:S(2)}, u32[]{:S(2)}) collective-permute-start(f32[19,8,128]{2,1,0:T(8,128)S(1)} %get-tuple-element.48), channel_id=1, source_target_pairs={{1,2},{2,1},{3,4},{4,3},{5,6},{6,5},{9,10},{10,9},{11,12},{12,11},... | collective-permute-start | bytes 233480 | tf_op jit(solution)/shard_map/ppermute | solution.py:823
  33.0 8.4 %collective-permute-start.5 = (f32[18,8,128]{2,1,0:T(8,128)S(1)}, f32[18,8,128]{2,1,0:T(8,128)S(1)}, u32[]{:S(2)}, u32[]{:S(2)}) collective-permute-start(f32[18,8,128]{2,1,0:T(8,128)S(1)} %get-tuple-element.46), channel_id=1, source_target_pairs={{8,16},{16,8},{9,17},{17,9},{10,18},{18,10},{11,19},{19,11},{12,20... | collective-permute-start | bytes 221192 | tf_op jit(solution)/shard_map/ppermute | solution.py:823
  33.6 7.7 %collective-permute-start.4 = (f32[17,8,128]{2,1,0:T(8,128)S(1)}, f32[17,8,128]{2,1,0:T(8,128)S(1)}, u32[]{:S(2)}, u32[]{:S(2)}) collective-permute-start(f32[17,8,128]{2,1,0:T(8,128)S(1)} %get-tuple-element.45), channel_id=1, source_target_pairs={{0,8},{8,0},{16,24},{24,16},{1,9},{9,1},{17,25},{25,17},{2,10},{10... | collective-permute-start | bytes 208904 | tf_op jit(solution)/shard_map/ppermute | solution.py:823
  38.2 3.2 %collective-permute-start.6 = (f32[16,8,128]{2,1,0:T(8,128)S(1)}, f32[16,8,128]{2,1,0:T(8,128)S(1)}, u32[]{:S(2)}, u32[]{:S(2)}) collective-permute-start(f32[16,8,128]{2,1,0:T(8,128)S(1)} %get-tuple-element.47), channel_id=1, source_target_pairs={{0,1},{1,0},{2,3},{3,2},{4,5},{5,4},{6,7},{7,6},{8,9},{9,8},{10,11... | collective-permute-start | bytes 196616 | tf_op jit(solution)/shard_map/ppermute | solution.py:823
